TPU v7x, 32 devices: a whole 2x2x4 slice. The times are simulated.
32 devices in a mesh: batch: 4 (over x, core), patch: 8 (over z, y).
Axes of the slice: x: 2, y: 2, z: 4, core: 2. Of those that a mesh axis runs over, the one named last changes fastest.
Arguments:
- latent: bfloat16 [64, 64, 1280], P(('batch', 'patch')), parts along dimension 0, may hold values from -100 to 100
- conv_weight: bfloat16 [3, 3, 1280, 1280], P(None, None, 'patch'), may hold values from -0.25 to 0.25
- channel_bias: float32 [1280], P('patch'), may hold values from -6 to 6
- w_query: bfloat16 [1280, 1280], P('patch'), may hold values from -0.5 to 0.5
- w_key: bfloat16 [1280, 1280], P('patch'), may hold values from -0.5 to 0.5
- w_value: bfloat16 [1280, 1280], P('patch'), may hold values from -0.15625 to 0.15625
- w_out: bfloat16 [1280, 1280], P('patch'), may hold values from -0.15625 to 0.15625
Outputs:
- output: bfloat16 [64, 64, 1280], P(('batch', 'patch')), parts along dimension 0
There are 4 independent parts, one for each index of `batch`. A program takes and returns all parts, laid end to end along the dimension named above; an argument that names none is the same for every part. Nothing has to cross between parts.
All inputs are finite; a program needn't handle non-finite values.
Results may differ from a plain program's by a relative error of at most 0.015.
Values may be sent and summed in bfloat16 or wider, within the bound.
No kernel may reach another device: no remote copies, remote signals or barrier semaphores. Data moves between devices by JAX's collectives and lax.ppermute only.
A program may use at most 128 MiB of HBM per device.

v0:
```python
import jax
import jax.numpy as jnp
from jax import lax
from jax.sharding import PartitionSpec as P

C = 1280
HEADS = 20
HEAD_DIM = 64
GROUPS = 32


epsilon = 1e-05


def contract(left, right):
    return lax.dot_general(
        left, right, (((1,), (1,)), ((), ())), preferred_element_type=jnp.float32
    )


def group_norm(values, entries):
    grouped = values.reshape(-1, GROUPS, C // GROUPS)
    centre = lax.psum(jnp.sum(grouped, axis=(0, 2)), "patch") / entries
    deviation = grouped - centre[None, :, None]
    spread = lax.psum(jnp.sum(jnp.square(deviation), axis=(0, 2)), "patch") / entries
    normalized = (grouped - centre[None, :, None]) * lax.rsqrt(spread + epsilon)[None, :, None]
    return normalized.reshape(values.shape)


def convolve(padded, kernel, row_count, columns):
    running = jnp.zeros((row_count * columns, kernel.shape[2]), jnp.float32)
    for row_shift in range(3):
        for col_shift in range(3):
            window = padded[
                row_shift : row_shift + row_count, col_shift : col_shift + columns, :
            ].reshape(-1, C)
            running = running + contract(window, kernel[row_shift, col_shift])
    return running


def attend(queries, key_all, value_all):
    query_heads = queries.reshape(-1, HEADS, HEAD_DIM).transpose(1, 0, 2)
    key_heads = key_all.reshape(-1, HEADS, HEAD_DIM).transpose(1, 0, 2)
    value_heads = value_all.reshape(-1, HEADS, HEAD_DIM).transpose(1, 0, 2)

    def one_head(triple):
        query_one, key_one, value_one = triple
        scores = jnp.dot(query_one, key_one.T, preferred_element_type=jnp.float32) * HEAD_DIM ** (
            -0.5
        )
        row_peak = jnp.max(scores, axis=1, keepdims=True)
        unnormalized = jnp.exp(scores - row_peak)
        row_total = jnp.sum(unnormalized, axis=1, keepdims=True)
        mixture = jnp.dot(
            unnormalized.astype(jnp.bfloat16), value_one, preferred_element_type=jnp.float32
        )
        return mixture / row_total

    heads_out = lax.map(one_head, (query_heads, key_heads, value_heads))
    return heads_out.transpose(1, 0, 2).reshape(-1, C).astype(jnp.bfloat16)


def on_device(latent, conv_weight, channel_bias, w_query, w_key, w_value, w_out):
    rows_local, columns, channels = latent.shape
    devices = lax.axis_size("patch")
    entries = rows_local * devices * columns * (channels // GROUPS)
    inputs = latent.astype(jnp.float32)
    activated = jax.nn.silu(group_norm(inputs, entries)).astype(jnp.bfloat16)
    whole_image = lax.all_gather(activated, "patch", axis=0, tiled=True)
    all_rows = whole_image.shape[0]
    padded = jnp.pad(whole_image, ((1, 1), (1, 1), (0, 0)))
    convolved = convolve(padded, conv_weight, all_rows, columns) + channel_bias
    convolved = convolved.reshape(all_rows, columns, -1)
    returned = lax.all_to_all(
        convolved.astype(jnp.bfloat16), "patch", split_axis=0, concat_axis=2, tiled=True
    ).astype(convolved.dtype)
    hidden = (inputs + returned).astype(jnp.bfloat16)
    hidden = lax.optimization_barrier(hidden)
    residual = hidden.astype(jnp.float32).reshape(-1, channels)
    normed = group_norm(residual, entries).astype(jnp.bfloat16)
    full_query, full_key, full_value = (
        lax.all_gather(w_query, "patch", axis=0, tiled=True),
        lax.all_gather(w_key, "patch", axis=0, tiled=True),
        lax.all_gather(w_value, "patch", axis=0, tiled=True),
    )
    queries = contract(normed, full_query).astype(jnp.bfloat16)
    key_local = contract(normed, full_key).astype(jnp.bfloat16)
    value_local = contract(normed, full_value).astype(jnp.bfloat16)
    key_all, value_all = (
        lax.all_gather(key_local, "patch", axis=0, tiled=True),
        lax.all_gather(value_local, "patch", axis=0, tiled=True),
    )
    attended = attend(queries, key_all, value_all)
    projected = contract(attended, lax.all_gather(w_out, "patch", axis=0, tiled=True))
    output = (residual + projected).astype(jnp.bfloat16)
    return output.reshape(rows_local, columns, channels)


def solution(mesh):
    return jax.shard_map(
        on_device,
        mesh=mesh,
        in_specs=(
            P(("batch", "patch"), None, None),
            P(None, None, "patch", None),
            P("patch"),
            P("patch", None),
            P("patch", None),
            P("patch", None),
            P("patch", None),
        ),
        out_specs=P(("batch", "patch"), None, None),
        check_vma=False,
    )
```

profile of v0, /device:TPU:0, one launch (start us, length us, event | category | flops | bytes accessed | tf_op | source)
XLA Modules:
  0.0 487.3 jit_solution(1819898840598745351)
XLA Ops:
  7.8 23.1 %psum.28 = f32[32]{0:T(128)S(1)} all-reduce(f32[32]{0:T(128)S(1)} %reduce_sum.59), channel_id=1, replica_groups=mesh['batch'=4,'patch'=8] {'patch'}, use_global_device_ids=true, to_apply=%region_2.0 | all-reduce | flops 32 | bytes 256 | tf_op jit(solution)/shard_map/psum | solution.py:23
  32.3 17.1 %psum.29 = f32[32]{0:T(128)S(1)} all-reduce(f32[32]{0:T(128)S(1)} %reduce_sum.62), channel_id=1, replica_groups=mesh['batch'=4,'patch'=8] {'patch'}, use_global_device_ids=true, to_apply=%region_5.6 | all-reduce | flops 32 | bytes 256 | tf_op jit(solution)/shard_map/psum | solution.py:25
  49.7 1.9 fusion.24
  53.7 51.4 %all-gather.8.cloned.1.call-done = bf16[16,64,1280]{2,1,0:T(8,128)(2,1)} async-done(((bf16[2,64,1280]{2,1,0:T(8,128)(2,1)}), bf16[16,64,1280]{2,1,0:T(8,128)(2,1)}) %all-gather.8.cloned.1.call-update) | async-done | bytes 2621456 | tf_op jit(solution)/shard_map/all_gather | solution.py:69
  105.1 15.5 %pad_slice_fusion = (bf16[16,64,1280]{2,1,0:T(8,128)(2,1)}, bf16[16,64,1280]{2,1,0:T(8,128)(2,1)}, bf16[16,64,1280]{2,1,0:T(8,128)(2,1)}, bf16[16,64,1280]{2,1,0...) fusion(bf16[16,64,1280]{2,1,0:T(8,128)(2,1)} %all-gather.8.clon, ...), kind=kLoop, calls=%fused_computation.16 | loop fusion | bytes 23592960 | tf_op jit(solution)/shard_map/slice | solution.py:34
  120.6 2.9 fusion.37
  123.6 2.1 convolution_add_fusion.8
  136.0 32.7 %all_to_all.4 = bf16[16,64,160]{2,1,0:T(8,128)(2,1)S(1)} all-to-all(bf16[16,64,160]{2,1,0:T(8,128)(2,1)S(1)} %bitcast.123), channel_id=1, replica_groups=mesh['batch'=4,'patch'=8] {'patch'}, dimensions={0} | all-to-all | bytes 655360 | tf_op jit(solution)/shard_map/all_to_all | solution.py:74
  169.8 19.3 %psum.30 = f32[32]{0:T(128)S(1)} all-reduce(f32[32]{0:T(128)S(1)} %reduce_sum.81), channel_id=1, replica_groups=mesh['batch'=4,'patch'=8] {'patch'}, use_global_device_ids=true, to_apply=%region_8.9 | all-reduce | flops 32 | bytes 256 | tf_op jit(solution)/shard_map/psum | solution.py:23
  189.6 17.4 %psum.31 = f32[32]{0:T(128)S(1)} all-reduce(f32[32]{0:T(128)S(1)} %reduce_sum.84), channel_id=1, replica_groups=mesh['batch'=4,'patch'=8] {'patch'}, use_global_device_ids=true, to_apply=%region_11.12 | all-reduce | flops 32 | bytes 256 | tf_op jit(solution)/shard_map/psum | solution.py:25
  207.2 4.2 convolution_convert_fusion.1
  211.5 29.0 %all-gather.16.cloned.1.call-done = bf16[1280,1280]{1,0:T(8,128)(2,1)} async-done(((bf16[160,1280]{1,0:T(8,128)(2,1)}), bf16[1280,1280]{1,0:T(8,128)(2,1)}) %all-gather.16.cloned.1.call-update) | async-done | bytes 3276816 | tf_op jit(solution)/shard_map/all_gather | solution.py:84
  240.5 3.8 convolution_convert_fusion
  245.1 58.0 %all-gather.10.cloned.1.call-done = bf16[1280,1280]{1,0:T(8,128)(2,1)} async-done(((bf16[160,1280]{1,0:T(8,128)(2,1)}), bf16[1280,1280]{1,0:T(8,128)(2,1)}) %all-gather.10.cloned.1.call-update) | async-done | bytes 3276816 | tf_op jit(solution)/shard_map/all_gather | solution.py:82
  303.1 3.1 convolution_convert_fusion.2
  306.5 52.0 %all-gather.14.cloned.1.call-done = bf16[1024,1280]{1,0:T(8,128)(2,1)} async-done(((bf16[128,1280]{1,0:T(8,128)(2,1)}), bf16[1024,1280]{1,0:T(8,128)(2,1)}) %all-gather.14.cloned.1.call-update) | async-done | bytes 2621456 | tf_op jit(solution)/shard_map/all_gather | solution.py:90
  358.4 3.0 copy.30
  361.4 52.3 %all-gather.18.cloned.1.call-done = bf16[1024,1280]{1,0:T(8,128)(2,1)} async-done(((bf16[128,1280]{1,0:T(8,128)(2,1)}), bf16[1024,1280]{1,0:T(8,128)(2,1)}) %all-gather.18.cloned.1.call-update) | async-done | bytes 2621456 | tf_op jit(solution)/shard_map/all_gather | solution.py:91
  413.7 4.4 copy.31
  418.2 47.5 %while.10 = (s32[]{:T(128)}, bf16[20,128,64]{1,2,0:T(8,128)(2,1)}, bf16[20,128,64]{1,2,0:T(8,128)(2,1)S(1)}, bf16[20,1024,64]{1,2,0:T(8,128)(2,1)S(1)}, bf16[20,1024,64]{1,2,0:T(8,128)(2,1)}, /*index=5*/s32[]{:T(128)}) while((s32[]{:T(128)}, bf16[20,128,64]{1,2,0:T(8,128)(2,1)}, bf16[20,128,64]{1,2,0:T(8,128)(2,1)S(1)}, ...), condition=%wide.region_15.16_spmd, body=%wide.region_12.15_spmd.sunk | while | flops 34348800 | bytes 1888837 | solution.py:59
  418.7 1.8 fusion.75
  421.1 1.8 fusion.75
  435.3 1.8 fusion.75
  437.7 1.8 fusion.75
  449.6 1.8 fusion.75
  452.0 1.8 fusion.75
  454.3 1.8 fusion.75
  456.7 1.8 fusion.75
  461.5 1.8 fusion.75
  463.8 1.8 fusion.75
  465.6 10.9 %all-gather.20.cloned.1.call-done = bf16[1280,1280]{1,0:T(8,128)(2,1)} async-done(((bf16[160,1280]{1,0:T(8,128)(2,1)}), bf16[1280,1280]{1,0:T(8,128)(2,1)}) %all-gather.20.cloned.1.call-update) | async-done | bytes 3276816 | tf_op jit(solution)/shard_map/all_gather | solution.py:94
  476.5 4.0 fusion.14
  (119 shorter events, 47.3 us)
Async XLA Ops:
  6.5 98.6 %all-gather.8.cloned.1.call-start = ((), (), s32[]{:S(2)}) async-start(), calls=%async_computation.1 | async-start | bytes 2949120 | tf_op jit(solution)/shard_map/all_gather | solution.py:69
  51.6 155.7 %all-gather.12.cloned.1.call-start = ((), (), s32[]{:S(2)}) async-start(), calls=%async_computation.3 | async-start | bytes 3686400 | tf_op jit(solution)/shard_map/all_gather | solution.py:83
  52.3 188.2 %all-gather.16.cloned.1.call-start = ((), (), s32[]{:S(2)}) async-start(), calls=%async_computation.5 | async-start | bytes 3686400 | tf_op jit(solution)/shard_map/all_gather | solution.py:84
  53.1 250.1 %all-gather.10.cloned.1.call-start = ((), (), s32[]{:S(2)}) async-start(), calls=%async_computation.2 | async-start | bytes 3686400 | tf_op jit(solution)/shard_map/all_gather | solution.py:82
  53.6 304.8 %all-gather.14.cloned.1.call-start = ((), (), s32[]{:S(2)}) async-start(), calls=%async_computation.4 | async-start | bytes 2949120 | tf_op jit(solution)/shard_map/all_gather | solution.py:90
  120.6 3.0 copy-start.3
  123.6 2.2 copy-start.2
  123.6 3.0 copy-start.5
  126.6 1.8 copy-start.1
  128.3 1.7 copy-start
  133.1 1.7 copy-start.6
  133.1 1.7 copy-start.7
  135.8 33.7 %copy-start.4 = (bf16[2,64,1280]{2,1,0:T(8,128)(2,1)S(1)}, bf16[2,64,1280]{2,1,0:T(8,128)(2,1)}, u32[]{:S(2)}) copy-start(bf16[2,64,1280]{2,1,0:T(8,128)(2,1)} %param.9) | copy-start | bytes 983044
  211.5 202.2 %all-gather.18.cloned.1.call-start = ((), (), s32[]{:S(2)}) async-start(), calls=%async_computation.6 | async-start | bytes 2949120 | tf_op jit(solution)/shard_map/all_gather | solution.py:91
  244.3 232.2 %all-gather.20.cloned.1.call-start = ((), (), s32[]{:S(2)}) async-start(), calls=%async_computation.7 | async-start | bytes 3686400 | tf_op jit(solution)/shard_map/all_gather | solution.py:94
Sparse Core Ops, SparseCore 0:
  51.7 53.3 all-gather.7
  107.3 69.7 all-gather.11
  179.3 61.1 all-gather.15
  242.5 60.5 all-gather.9
  305.1 53.2 all-gather.13
  360.4 53.2 all-gather.17
  415.9 60.5 all-gather.19
where the time goes:
time: 488 us; the launch traced here: 487 us
  waiting for transfers between devices  256 us (52%)
  blocking collectives  110 us (23%)
  matrix products  69.9 us (14%)
  local copies, waits for them, and re-layouts  28.1 us (6%)
  between operations  13.7 us (3%)
  other arithmetic  9.48 us (2%)
    all_gather x1, waiting for transfers between devices, on_device(): lax.all_gather(w_query, 'patch', axis=0, tiled=True)  58 us
    all_gather x1, waiting for transfers between devices, on_device(): lax.all_gather(value_local, 'patch', axis=0, tiled=True)  52.3 us
    all_gather x1, waiting for transfers between devices, on_device(): lax.all_gather(key_local, 'patch', axis=0, tiled=True)  52 us
    all_gather x1, waiting for transfers between devices, on_device(): whole_image = lax.all_gather(activated, 'patch', axis=0, tiled=True)  51.4 us
    psum x2, blocking collectives, group_norm(): centre = lax.psum(jnp.sum(grouped, axis=(0, 2)), 'patch') / entries  42.4 us
    dot_general x20, matrix products, one_head(): jnp.dot(unnormalized.astype(jnp.bfloat16), value_one, preferred_element_t...  36.1 us
    psum x2, blocking collectives, group_norm(): lax.psum(jnp.sum(jnp.square(deviation), axis=(0, 2)), 'patch') / entries  34.5 us
    all_to_all x1, blocking collectives, on_device(): lax.all_to_all(convolved.astype(jnp.bfloat16), 'patch', split_axis=0, con...  32.7 us
  transfers between devices with their start and end apart: 7, of which 6 were waited for; matrix products, arithmetic and copies ran while one was open for 20% of the time, Pallas kernels for 0%

commit v1 on v0

v1 whole, which is shorter than its diff:
```python
import functools

import jax
import jax.numpy as jnp
from jax import lax
from jax.experimental import pallas as pl
from jax.experimental.pallas import tpu as pltpu
from jax.sharding import PartitionSpec as P

C = 1280
HEADS = 20
HEAD_DIM = 64
GROUPS = 32
SPAN = C // GROUPS
OUTER = 4
SET_HEADS = HEADS // OUTER
SET_CHANNELS = SET_HEADS * HEAD_DIM
SHARED = SET_HEADS // 2
EPSILON = 1e-05
VMEM_LIMIT = 48 * 1024 * 1024

f32 = jnp.float32
bf16 = jnp.bfloat16

NT = (((1,), (1,)), ((), ()))
NN = (((1,), (0,)), ((), ()))


def dot(left, right, dims=NN, precision=None):
    return lax.dot_general(left, right, dims, preferred_element_type=f32, precision=precision)


def exact(left, right, dims=NN):
    return dot(left, right, dims, lax.Precision.HIGHEST)


def conv_kernel(n, columns, me_ref, *refs):
    pieces = refs[:n]
    kernel_ref, bias_ref, normed_ref = refs[n : n + 3]
    hidden_refs = refs[n + 3 : 2 * n + 3]
    act_ref, kept_ref, hidden_ref = refs[2 * n + 3 :]
    block = pieces[0].shape[0]
    positions = block * n
    own = normed_ref.shape[0]
    inner = n // OUTER
    me = me_ref[0]
    entries = float(positions * SPAN)

    def source(index):
        return gather_source(me, index, inner)

    chunk = 16
    steps = block // chunk

    def add(step, total):
        for piece in pieces:
            total = total + piece[pl.ds(step * chunk, chunk), :].astype(f32)
        return total

    member = (
        lax.broadcasted_iota(jnp.int32, (C, 128), 0) // SPAN
        == lax.broadcasted_iota(jnp.int32, (C, 128), 1)
    ).astype(f32)

    def group_mean(total):
        summed = jnp.sum(total, axis=0, keepdims=True)
        per_group = exact(jnp.broadcast_to(summed, (8, C)), member) / entries
        return exact(per_group, member, NT)[0:1, :]

    zero = jnp.zeros((chunk, C), f32)
    centre = group_mean(lax.fori_loop(0, steps, add, zero))

    def add_square(step, total):
        for piece in pieces:
            away = piece[pl.ds(step * chunk, chunk), :].astype(f32) - centre
            total = total + away * away
        return total

    spread = group_mean(lax.fori_loop(0, steps, add_square, zero))
    half_scale = 0.5 * lax.rsqrt(spread + EPSILON)

    act_ref[0:columns, :] = jnp.zeros((columns, C), bf16)
    act_ref[positions + columns :, :] = jnp.zeros((columns, C), bf16)
    starts = [pl.multiple_of(source(index) * block, block) for index in range(n)]

    def activate(step, carry):
        for start, piece in zip(starts, pieces):
            half = (piece[pl.ds(step * chunk, chunk), :].astype(f32) - centre) * half_scale
            value = half + half * jnp.tanh(half)
            row = pl.multiple_of(columns + start + step * chunk, chunk)
            act_ref[pl.ds(row, chunk), :] = value.astype(bf16)
        return carry

    lax.fori_loop(0, steps, activate, 0)

    choose = (
        lax.broadcasted_iota(jnp.int32, (own, C), 0) + me * own
        == lax.broadcasted_iota(jnp.int32, (own, C), 1)
    ).astype(bf16)
    for start, piece in zip(starts, pieces):
        kept_ref[:, pl.ds(start, block)] = dot(choose, piece[...], NT)

    wide = 256
    column = lax.broadcasted_iota(jnp.int32, (own, wide), 1) % columns
    bias = bias_ref[...]
    for at in range(0, positions, wide):
        taps = dot(kernel_ref[0], act_ref[at : at + wide, :], NT)
        for shift in (1, 2):
            low = at + shift * columns
            taps = taps + dot(kernel_ref[shift], act_ref[low : low + wide, :], NT)
        before = jnp.where(column > 0, pltpu.roll(taps[0:own], 1, 1), 0.0)
        after = jnp.where(column < columns - 1, pltpu.roll(taps[2 * own :], wide - 1, 1), 0.0)
        convolved = taps[own : 2 * own] + before + after
        hidden = kept_ref[:, at : at + wide] + convolved + bias
        hidden_ref[:, at : at + wide] = hidden.astype(bf16).astype(f32)

    for shift, target in enumerate(hidden_refs):
        start = pl.multiple_of(lax.rem(me + shift, n) * block, block)
        target[...] = hidden_ref[:, pl.ds(start, block)].astype(bf16)

    for low in range(0, own, SPAN):
        group = hidden_ref[low : low + SPAN, :]
        mean = jnp.sum(jnp.sum(group, axis=0, keepdims=True), axis=1, keepdims=True) / entries
        away = group - mean
        square = away * away
        var = jnp.sum(jnp.sum(square, axis=0, keepdims=True), axis=1, keepdims=True) / entries
        hidden_ref[low : low + SPAN, :] = away * lax.rsqrt(var + EPSILON)
    normed_ref[...] = hidden_ref[...].astype(bf16)


def attention_kernel(n, me_ref, *refs):
    pieces = refs[:n]
    weight_ref = refs[n]
    outs = refs[n + 1 : 2 * n + 1]
    normed_ref, query_ref, key_ref, value_ref, sems = refs[2 * n + 1 :]
    own, positions = pieces[0].shape
    inner = n // OUTER
    block = positions // n
    full = (SET_HEADS - 1) // inner * HEAD_DIM
    rows = full + HEAD_DIM
    me = me_ref[0]

    copies = []
    for index, piece in enumerate(pieces):
        row = pl.multiple_of(gather_source(me, index, inner) * own, own)
        copy = pltpu.make_async_copy(piece, normed_ref.at[pl.ds(row, own), :], sems.at[index])
        copy.start()
        copies.append(copy)
    for copy in copies:
        copy.wait()

    wide = 256
    for at in range(0, positions, wide):
        made = dot(weight_ref[...], normed_ref[:, at : at + wide])
        query = made[0:rows].astype(bf16).astype(f32) * HEAD_DIM ** (-0.5)
        query_ref[:, at : at + wide] = query.astype(bf16)
        key_ref[at : at + wide, :] = made[rows : 2 * rows].T.astype(bf16)
        value_ref[:, at : at + wide] = made[2 * rows :].astype(bf16)

    def attend(head, shifts):
        low = head * HEAD_DIM
        starts = [pl.multiple_of(lax.rem(me + shift, n) * block, block) for shift in shifts]
        query = jnp.concatenate(
            [query_ref[low : low + HEAD_DIM, pl.ds(start, block)] for start in starts], axis=1
        )
        scores = dot(key_ref[:, low : low + HEAD_DIM], query)
        peak = jnp.max(scores, axis=0, keepdims=True)
        unnormalized = jnp.exp(scores - peak)
        total = jnp.sum(unnormalized, axis=0, keepdims=True)
        mixture = dot(value_ref[low : low + HEAD_DIM, :], unnormalized.astype(bf16))
        attended = (mixture / total).astype(bf16)
        for place, shift in enumerate(shifts):
            outs[shift][low : low + HEAD_DIM, :] = attended[:, place * block : (place + 1) * block]

    for head in range(full // HEAD_DIM):
        for shift in range(0, n, 2):
            attend(head, (shift, shift + 1))
    shared = list(range(0, n, inner))
    for at in range(0, len(shared), 2):
        attend(full // HEAD_DIM, tuple(shared[at : at + 2]))


def output_kernel(n, me_ref, *refs):
    attended_refs = refs[:n]
    hidden_refs = refs[n : 2 * n]
    mine_ref, other_ref, out_ref = refs[2 * n : 2 * n + 3]
    attended_ref, total_ref = refs[2 * n + 3 :]
    me, half = me_ref[0], me_ref[1]
    inner = n // OUTER
    own = C // n
    heads = (SET_HEADS - 1) // inner
    full = heads * HEAD_DIM
    for shift in range(n):
        origin = lax.rem(me + n - shift, n)
        member = lax.rem(origin, inner)
        base = lax.div(origin, inner) * SET_CHANNELS
        first = member * heads + (member >= inner // 2).astype(jnp.int32)
        row = pl.multiple_of(base + first * HEAD_DIM, HEAD_DIM)
        attended_ref[pl.ds(row, full), :] = attended_refs[shift][0:full, :]
        if shift % inner == 0:
            row = pl.multiple_of(base + SHARED * HEAD_DIM, HEAD_DIM)
            attended_ref[pl.ds(row, HEAD_DIM), :] = attended_refs[shift][full:, :]
        row = pl.multiple_of(origin * own, own)
        total_ref[pl.ds(row, own), :] = hidden_refs[shift][...].astype(f32)
    attended = attended_ref[...]
    part = own // 2
    for weight_ref, which in ((mine_ref, half), (other_ref, 1 - half)):
        made = dot(weight_ref[...], attended)
        for origin in range(n):
            row = pl.multiple_of(origin * own + which * part, 8)
            total_ref[pl.ds(row, part), :] += made[origin * part : (origin + 1) * part]
    out_ref[...] = total_ref[...].T.astype(bf16)


def gather_source(me, index, inner):
    outer_step, inner_step = divmod(index, inner)
    outer_at = lax.rem(lax.div(me, inner) + OUTER - outer_step, OUTER)
    inner_at = lax.rem(lax.rem(me, inner) + inner - inner_step, inner)
    return outer_at * inner + inner_at


def moves(n, inner, outer_step, inner_step):
    pairs = []
    for start in range(n):
        outer_at = (start // inner + outer_step) % OUTER
        inner_at = (start % inner + inner_step) % inner
        pairs.append((start, outer_at * inner + inner_at))
    return pairs


def gather(shard, n):
    inner = n // OUTER
    pieces = []
    along = shard
    for outer_step in range(OUTER):
        if outer_step:
            along = lax.ppermute(along, "patch", moves(n, inner, 1, 0))
        across = along
        pieces.append(across)
        for _ in range(1, inner):
            across = lax.ppermute(across, "patch", moves(n, inner, 0, 1))
            pieces.append(across)
    return pieces


def exchange(blocks, n):
    received = [blocks[0]]
    for shift in range(1, n):
        pairs = [(start, (start + shift) % n) for start in range(n)]
        received.append(lax.ppermute(blocks[shift], "patch", pairs))
    return received


def head_weights(weights, me, n):
    inner = n // OUTER
    own = C // n
    heads = (SET_HEADS - 1) // inner
    member = lax.rem(me, inner)
    if inner == 2:
        rest = own - heads * HEAD_DIM
        whole = lax.dynamic_slice_in_dim(weights, member * rest, own - rest, 1)
        part = lax.dynamic_slice_in_dim(weights, (1 - member) * (own - rest), rest, 1)
        other = lax.ppermute(part, "patch", moves(n, inner, 0, 1))
        first = jnp.where(member == 0, part, other)
        second = jnp.where(member == 0, other, part)
        return jnp.concatenate([whole, first, second], axis=1)
    sets = [list(range(at, at + inner)) for at in range(0, n, inner)]
    every = lax.all_gather(weights, "patch", axis=1, tiled=True, axis_index_groups=sets)
    first = member * heads + (member >= inner // 2).astype(jnp.int32)
    whole = lax.dynamic_slice_in_dim(every, first * HEAD_DIM, heads * HEAD_DIM, 1)
    shared = every[:, SHARED * HEAD_DIM : (SHARED + 1) * HEAD_DIM]
    return jnp.concatenate([whole, shared], axis=1)


def after(values, *others):
    return lax.optimization_barrier((values, *others))[0]


def on_device(latent, conv_weight, channel_bias, w_query, w_key, w_value, w_out):
    rows_local, columns, channels = latent.shape
    n = lax.axis_size("patch")
    inner = n // OUTER
    own = channels // n
    block = rows_local * columns
    positions = block * n
    me = lax.axis_index("patch")
    half = lax.rem(lax.axis_index("batch"), 2)
    place = jnp.stack([me, half]).astype(jnp.int32)
    vmem = pl.BlockSpec(memory_space=pltpu.VMEM)
    smem = pl.BlockSpec(memory_space=pltpu.SMEM)
    anywhere = pl.BlockSpec(memory_space=pl.ANY)
    params = pltpu.CompilerParams(vmem_limit_bytes=VMEM_LIMIT)

    pieces = gather(latent.reshape(block, channels), n)

    ready = pieces[-1]
    weights = jnp.stack([w_query, w_key, w_value])
    weights, w_out = after((weights, w_out), ready)
    weights = head_weights(weights, me, n)
    rows = weights.shape[1]
    weights = weights.reshape(3 * rows, channels)
    w_mine = lax.dynamic_slice_in_dim(w_out, half * (own // 2), own // 2, 0)
    w_mine = lax.all_gather(w_mine, "patch", axis=0, tiled=True)
    swap = [(at, at ^ 1) for at in range(lax.axis_size("batch"))]
    w_other = lax.ppermute(w_mine, "batch", swap)

    made = pl.pallas_call(
        functools.partial(conv_kernel, n, columns),
        out_shape=[jax.ShapeDtypeStruct((own, positions), bf16)]
        + [jax.ShapeDtypeStruct((own, block), bf16)] * n,
        in_specs=[smem] + [vmem] * (n + 2),
        out_specs=[vmem] * (n + 1),
        scratch_shapes=[
            pltpu.VMEM((positions + 2 * columns, channels), bf16),
            pltpu.VMEM((own, positions), f32),
            pltpu.VMEM((own, positions), f32),
        ],
        compiler_params=params,
        cost_estimate=pl.CostEstimate(
            flops=2 * 9 * positions * channels * own,
            bytes_accessed=2 * (positions * channels + 9 * channels * own),
            transcendentals=positions * channels,
        ),
        name="norm_conv_norm",
    )(
        place,
        *pieces,
        conv_weight.reshape(3, 3 * own, channels),
        channel_bias.reshape(own, 1),
    )
    normed, hidden_blocks = made[0], list(made[1:])

    normed_pieces = gather(normed, n)
    hidden_blocks = after(hidden_blocks, normed_pieces[-1])
    hidden_blocks = exchange(hidden_blocks, n)

    full = rows - HEAD_DIM
    attended = pl.pallas_call(
        functools.partial(attention_kernel, n),
        out_shape=[
            jax.ShapeDtypeStruct((rows if shift % inner == 0 else full, block), bf16)
            for shift in range(n)
        ],
        in_specs=[smem] + [anywhere] * n + [vmem],
        out_specs=[vmem] * n,
        scratch_shapes=[
            pltpu.VMEM((channels, positions), bf16),
            pltpu.VMEM((rows, positions), bf16),
            pltpu.VMEM((positions, rows), bf16),
            pltpu.VMEM((rows, positions), bf16),
            pltpu.SemaphoreType.DMA((n,)),
        ],
        compiler_params=params,
        cost_estimate=pl.CostEstimate(
            flops=2 * positions * channels * 3 * rows + 4 * positions * positions * rows,
            bytes_accessed=2 * (positions * channels + 3 * rows * channels),
            transcendentals=positions * positions * rows // HEAD_DIM,
        ),
        name="attention",
    )(place, *normed_pieces, weights)
    attended = exchange(list(attended), n)

    output = pl.pallas_call(
        functools.partial(output_kernel, n),
        out_shape=jax.ShapeDtypeStruct((block, channels), bf16),
        in_specs=[smem] + [vmem] * (2 * n + 2),
        out_specs=vmem,
        scratch_shapes=[
            pltpu.VMEM((channels, block), bf16),
            pltpu.VMEM((channels, block), f32),
        ],
        compiler_params=params,
        cost_estimate=pl.CostEstimate(
            flops=2 * block * channels * channels,
            bytes_accessed=2 * channels * (channels + 3 * block),
            transcendentals=0,
        ),
        name="project",
    )(place, *attended, *hidden_blocks, w_mine, w_other)
    return output.reshape(rows_local, columns, channels)


def solution(mesh):
    return jax.shard_map(
        on_device,
        mesh=mesh,
        in_specs=(
            P(("batch", "patch"), None, None),
            P(None, None, "patch", None),
            P("patch"),
            P("patch", None),
            P("patch", None),
            P("patch", None),
            P("patch", None),
        ),
        out_specs=P(("batch", "patch"), None, None),
        check_vma=False,
    )
```

time: 488 us -> 183 us (0.38)
  waiting for transfers between devices: 256 us -> 96.9 us
  blocking collectives: 110 us -> 0 us
  matrix products: 69.9 us -> 0 us
  starting transfers between devices: 0.24 us -> 36.1 us
  Pallas kernels: 0 us -> 25.1 us
  local copies, waits for them, and re-layouts: 28.1 us -> 7.2 us
  other arithmetic: 9.48 us -> 3.68 us
    all_gather x7 -> x1, waiting for transfers between devices: 254 us -> 0.01 us  [on_device(): w_mine = lax.all_gather(w_mine, 'patch', axis=0, tiled=True)]
    ppermute x0 -> x30, waiting for transfers between devices: none -> 96.9 us  [the longest x6 50.7 us: gather(): along = lax.ppermute(along, 'patch', moves(n, inner, 1, 0))]
    psum x4 -> x0, blocking collectives: 76.9 us -> none  [the longest x2 42.4 us: group_norm(): centre = lax.psum(jnp.sum(grouped, axis=(0, 2)), 'patch') / entries]
    dot_general x53 -> x0, matrix products: 69.9 us -> none  [the longest x20 36.1 us: one_head(): jnp.dot(unnormalized.astype(jnp.bfloat16), value_one, preferred_element_t...]
    ppermute x0 -> x30, starting transfers between devices: none -> 36.1 us  [the longest x14 23.6 us: exchange(): received.append(lax.ppermute(blocks[shift], 'patch', pairs))]
    all_to_all x1 -> x0, blocking collectives: 32.7 us -> none  [on_device(): lax.all_to_all(convolved.astype(jnp.bfloat16), 'patch', split_axis=0, con...]
    pallas_call x0 -> x3, Pallas kernels: none -> 25.1 us  [the longest x1 12.5 us: on_device(): pl.pallas_call(functools.partial(conv_kernel, n, columns), out_shape=[jax...]
    slice x1 -> x0, local copies, waits for them, and re-layouts: 15.5 us -> none  [convolve(): padded[row_shift:row_shift + row_count, col_shift:col_shift + columns, :]]
  transfers between devices with their start and end apart: 7 -> 31, of which waited for: 6 -> 15; matrix products, arithmetic and copies ran while one was open for 20% -> 3% of each run, Pallas kernels for 0% -> 12%
where the time goes in v1:
time: 183 us
  waiting for transfers between devices  96.9 us (53%)
  starting transfers between devices  36.1 us (20%)
  Pallas kernels  25.1 us (14%)
  between operations  13.5 us (7%)
  local copies, waits for them, and re-layouts  7.2 us (4%)
  other arithmetic  3.68 us (2%)
    ppermute x6, waiting for transfers between devices, gather(): along = lax.ppermute(along, 'patch', moves(n, inner, 1, 0))  50.7 us
    ppermute x8, waiting for transfers between devices, gather(): across = lax.ppermute(across, 'patch', moves(n, inner, 0, 1))  37 us
    ppermute x14, starting transfers between devices, exchange(): received.append(lax.ppermute(blocks[shift], 'patch', pairs))  23.6 us
    pallas_call x1, Pallas kernels, on_device(): pl.pallas_call(functools.partial(conv_kernel, n, columns), out_shape=[jax...  12.5 us
    pallas_call x1, Pallas kernels, on_device(): pl.pallas_call(functools.partial(attention_kernel, n), out_shape=[jax.Sha...  10 us
    ppermute x8, starting transfers between devices, gather(): across = lax.ppermute(across, 'patch', moves(n, inner, 0, 1))  8.36 us
    ppermute x1, waiting for transfers between devices, head_weights(): other = lax.ppermute(part, 'patch', moves(n, inner, 0, 1))  5.53 us
    unnamed x28, local copies, waits for them, and re-layouts  4.17 us
  transfers between devices with their start and end apart: 31, of which 15 were waited for; matrix products, arithmetic and copies ran while one was open for 3% of the time, Pallas kernels for 12%

profile of v1, /device:TPU:0, one launch (start us, length us, event | category | flops | bytes accessed | tf_op | source)
XLA Modules:
  0.0 182.6 jit_solution(12560331622507722443)
XLA Ops:
  6.5 3.0 %collective-permute-start.1 = (bf16[128,1280]{1,0:T(8,128)(2,1)}, bf16[128,1280]{1,0:T(8,128)(2,1)S(1)}, u32[]{:S(2)}, u32[]{:S(2)}) collective-permute-start(bf16[128,1280]{1,0:T(8,128)(2,1)} %bitcast.11), channel_id=1, source_target_pairs={{0,2},{1,3},{2,4},{3,5},{4,6},{5,7},{6,0},{7,1},{8,10},{9,11},{10,... | collective-permute-start | bytes 983048 | tf_op jit(solution)/shard_map/ppermute | solution.py:237
  9.6 9.9 %collective-permute-done.1.refs_2_ = bf16[128,1280]{1,0:T(8,128)(2,1)S(1)} collective-permute-done((bf16[128,1280]{1,0:T(8,128)(2,1)}, bf16[128,1280]{1,0:T(8,128)(2,1)S(1)}, u32[]{:S(2)}, u32[]{:S(2)}) %collective-permute-start.1) | collective-permute-done | bytes 327712 | tf_op jit(solution)/shard_map/ppermute | solution.py:237
  19.5 10.7 %collective-permute-done.3.refs_4_ = bf16[128,1280]{1,0:T(8,128)(2,1)S(1)} collective-permute-done((bf16[128,1280]{1,0:T(8,128)(2,1)S(1)}, bf16[128,1280]{1,0:T(8,128)(2,1)S(1)}, u32[]{:S(2)}, u32[]{:S(2)}) %collective-permute-start.3) | collective-permute-done | bytes 327712 | tf_op jit(solution)/shard_map/ppermute | solution.py:237
  30.2 9.8 %collective-permute-done.5.refs_6_ = bf16[128,1280]{1,0:T(8,128)(2,1)S(1)} collective-permute-done((bf16[128,1280]{1,0:T(8,128)(2,1)S(1)}, bf16[128,1280]{1,0:T(8,128)(2,1)S(1)}, u32[]{:S(2)}, u32[]{:S(2)}) %collective-permute-start.5) | collective-permute-done | bytes 327712 | tf_op jit(solution)/shard_map/ppermute | solution.py:237
  41.0 2.5 %pad_maximum_fusion.1 = bf16[3,160,1280]{2,1,0:T(8,128)(2,1)} fusion(bf16[1,160,1280]{2,1,0:T(8,128)(2,1)} %bitcast.14, bf16[1,160,1280]{2,1,0:T(8,128)(2,1)} %bitcast.15, bf16[1,160,1280]{2,1,0:T(8,128)(2,1)} %bitcast.16), kind=kLoop, calls=%fused_computation.1 | loop fusion | flops 1228800 | bytes 2457600 | tf_op jit(solution)/shard_map/stack | solution.py:297
  43.5 3.8 %collective-permute-done.6.refs_7_ = bf16[128,1280]{1,0:T(8,128)(2,1)S(1)} collective-permute-done((bf16[128,1280]{1,0:T(8,128)(2,1)S(1)}, bf16[128,1280]{1,0:T(8,128)(2,1)S(1)}, u32[]{:S(2)}, u32[]{:S(2)}) %collective-permute-start.6) | collective-permute-done | bytes 327712 | tf_op jit(solution)/shard_map/ppermute | solution.py:241
  48.0 1.3 collective-permute-start
  50.1 1.3 collective-permute-start.4
  51.6 9.0 %collective-permute-done.refs_1_ = bf16[128,1280]{1,0:T(8,128)(2,1)S(1)} collective-permute-done((bf16[128,1280]{1,0:T(8,128)(2,1)S(1)}, bf16[128,1280]{1,0:T(8,128)(2,1)S(1)}, u32[]{:S(2)}, u32[]{:S(2)}) %collective-permute-start) | collective-permute-done | bytes 327712 | tf_op jit(solution)/shard_map/ppermute | solution.py:241
  60.6 6.2 %collective-permute-done.2.refs_3_ = bf16[128,1280]{1,0:T(8,128)(2,1)S(1)} collective-permute-done((bf16[128,1280]{1,0:T(8,128)(2,1)S(1)}, bf16[128,1280]{1,0:T(8,128)(2,1)S(1)}, u32[]{:S(2)}, u32[]{:S(2)}) %collective-permute-start.2) | collective-permute-done | bytes 327712 | tf_op jit(solution)/shard_map/ppermute | solution.py:241
  66.8 3.5 %collective-permute-done.4.refs_5_ = bf16[128,1280]{1,0:T(8,128)(2,1)S(1)} collective-permute-done((bf16[128,1280]{1,0:T(8,128)(2,1)S(1)}, bf16[128,1280]{1,0:T(8,128)(2,1)S(1)}, u32[]{:S(2)}, u32[]{:S(2)}) %collective-permute-start.4) | collective-permute-done | bytes 327712 | tf_op jit(solution)/shard_map/ppermute | solution.py:241
  72.0 12.5 %norm_conv_norm.1 = (bf16[160,1024]{1,0:T(8,128)(2,1)S(1)}, bf16[160,128]{1,0:T(8,128)(2,1)S(1)}, bf16[160,128]{1,0:T(8,128)(2,1)S(1)}, bf16[160,128]{1,0:T(8,12...) custom-call(s32[2]{0:T(128)S(1)} %pad_add_fusion.me_ref, ...), custom_call_target="tpu_custom_call" | custom-call | flops 3774873600 | bytes 6307840 | tf_op jit(solution)/shard_map/norm_conv_norm/pallas_call | solution.py:307
  87.0 12.4 %collective-permute-done.8.refs_2_ = bf16[160,1024]{1,0:T(8,128)(2,1)S(1)} collective-permute-done((bf16[160,1024]{1,0:T(8,128)(2,1)S(1)}, bf16[160,1024]{1,0:T(8,128)(2,1)S(1)}, u32[]{:S(2)}, u32[]{:S(2)}) %collective-permute-start.8) | collective-permute-done | bytes 327712 | tf_op jit(solution)/shard_map/ppermute | solution.py:237
  100.2 7.9 %collective-permute-done.10.refs_4_ = bf16[160,1024]{1,0:T(8,128)(2,1)S(1)} collective-permute-done((bf16[160,1024]{1,0:T(8,128)(2,1)S(1)}, bf16[160,1024]{1,0:T(8,128)(2,1)S(1)}, u32[]{:S(2)}, u32[]{:S(2)}) %collective-permute-start.10) | collective-permute-done | bytes 327712 | tf_op jit(solution)/shard_map/ppermute | solution.py:237
  109.1 1.1 collective-permute-start.14
  110.3 1.3 constant_dynamic-slice_fusion.2
  112.6 5.5 %collective-permute-done.14 = bf16[3,32,1280]{2,1,0:T(8,128)(2,1)S(1)} collective-permute-done((bf16[3,32,1280]{2,1,0:T(8,128)(2,1)S(1)}, bf16[3,32,1280]{2,1,0:T(8,128)(2,1)S(1)}, u32[]{:S(2)}, u32[]{:S(2)}) %collective-permute-start.14) | collective-permute-done | bytes 245792 | tf_op jit(solution)/shard_map/ppermute | solution.py:263
  121.3 3.8 %collective-permute-done.9.refs_3_ = bf16[160,1024]{1,0:T(8,128)(2,1)S(1)} collective-permute-done((bf16[160,1024]{1,0:T(8,128)(2,1)S(1)}, bf16[160,1024]{1,0:T(8,128)(2,1)S(1)}, u32[]{:S(2)}, u32[]{:S(2)}) %collective-permute-start.9) | collective-permute-done | bytes 327712 | tf_op jit(solution)/shard_map/ppermute | solution.py:241
  125.1 7.0 %collective-permute-done.11.refs_5_ = bf16[160,1024]{1,0:T(8,128)(2,1)S(1)} collective-permute-done((bf16[160,1024]{1,0:T(8,128)(2,1)S(1)}, bf16[160,1024]{1,0:T(8,128)(2,1)S(1)}, u32[]{:S(2)}, u32[]{:S(2)}) %collective-permute-start.11) | collective-permute-done | bytes 327712 | tf_op jit(solution)/shard_map/ppermute | solution.py:241
  132.1 3.6 %collective-permute-done.13.refs_7_ = bf16[160,1024]{1,0:T(8,128)(2,1)S(1)} collective-permute-done((bf16[160,1024]{1,0:T(8,128)(2,1)S(1)}, bf16[160,1024]{1,0:T(8,128)(2,1)S(1)}, u32[]{:S(2)}, u32[]{:S(2)}) %collective-permute-start.13) | collective-permute-done | bytes 327712 | tf_op jit(solution)/shard_map/ppermute | solution.py:241
  135.8 10.0 %attention.1 = (bf16[192,128]{1,0:T(8,128)(2,1)S(1)}, bf16[128,128]{1,0:T(8,128)(2,1)S(1)}, bf16[192,128]{1,0:T(8,128)(2,1)S(1)}, bf16[128,128]{1,0:T(8,128)(2,1...) custom-call(s32[2]{0:T(128)S(1)} %pad_add_fusion.me_ref, ...), custom_call_target="tpu_custom_call" | custom-call | flops 2315255808 | bytes 4096000 | tf_op jit(solution)/shard_map/attention/pallas_call | solution.py:338
  147.5 1.2 collective-permute-start.22
  148.7 3.3 %collective-permute-start.19 = (bf16[128,128]{1,0:T(8,128)(2,1)S(1)}, bf16[128,128]{1,0:T(8,128)(2,1)S(1)}, u32[]{:S(2)}, u32[]{:S(2)}) collective-permute-start(bf16[128,128]{1,0:T(8,128)(2,1)S(1)} %get-tuple-element.39), channel_id=1, source_target_pairs={{0,5},{1,6},{2,7},{3,0},{4,1},{5,2},{6,3},{7,4},{8,13},{9,14},{10,... | collective-permute-start | bytes 98312 | tf_op jit(solution)/shard_map/ppermute | solution.py:250
  152.5 1.6 collective-permute-start.21
  154.7 3.8 %collective-permute-start.24 = (bf16[160,128]{1,0:T(8,128)(2,1)S(1)}, bf16[160,128]{1,0:T(8,128)(2,1)S(1)}, u32[]{:S(2)}, u32[]{:S(2)}) collective-permute-start(bf16[160,128]{1,0:T(8,128)(2,1)S(1)} %copy-done.8), channel_id=1, source_target_pairs={{0,3},{1,4},{2,5},{3,6},{4,7},{5,0},{6,1},{7,2},{8,11},{9,12},{10,... | collective-permute-start | bytes 122888 | tf_op jit(solution)/shard_map/ppermute | solution.py:250
  158.5 1.4 collective-permute-start.25
  159.9 1.6 collective-permute-start.26
  161.5 2.2 %collective-permute-start.27 = (bf16[160,128]{1,0:T(8,128)(2,1)S(1)}, bf16[160,128]{1,0:T(8,128)(2,1)S(1)}, u32[]{:S(2)}, u32[]{:S(2)}) collective-permute-start(bf16[160,128]{1,0:T(8,128)(2,1)S(1)} %get-tuple-element.56), channel_id=1, source_target_pairs={{0,6},{1,7},{2,0},{3,1},{4,2},{5,3},{6,4},{7,5},{8,14},{9,15},{10,... | collective-permute-start | bytes 122888 | tf_op jit(solution)/shard_map/ppermute | solution.py:250
  163.9 1.9 %collective-permute-start.18 = (bf16[192,128]{1,0:T(8,128)(2,1)S(1)}, bf16[192,128]{1,0:T(8,128)(2,1)S(1)}, u32[]{:S(2)}, u32[]{:S(2)}) collective-permute-start(bf16[192,128]{1,0:T(8,128)(2,1)S(1)} %get-tuple-element.38), channel_id=1, source_target_pairs={{0,4},{1,5},{2,6},{3,7},{4,0},{5,1},{6,2},{7,3},{8,12},{9,13},{10,... | collective-permute-start | bytes 147464 | tf_op jit(solution)/shard_map/ppermute | solution.py:250
  165.8 3.3 %collective-permute-start.20 = (bf16[192,128]{1,0:T(8,128)(2,1)S(1)}, bf16[192,128]{1,0:T(8,128)(2,1)S(1)}, u32[]{:S(2)}, u32[]{:S(2)}) collective-permute-start(bf16[192,128]{1,0:T(8,128)(2,1)S(1)} %get-tuple-element.40), channel_id=1, source_target_pairs={{0,6},{1,7},{2,0},{3,1},{4,2},{5,3},{6,4},{7,5},{8,14},{9,15},{10,... | collective-permute-start | bytes 147464 | tf_op jit(solution)/shard_map/ppermute | solution.py:250
  170.0 3.1 %collective-permute-done.28.refs_15_ = bf16[160,128]{1,0:T(8,128)(2,1)S(1)} collective-permute-done((bf16[160,128]{1,0:T(8,128)(2,1)S(1)}, bf16[160,128]{1,0:T(8,128)(2,1)S(1)}, u32[]{:S(2)}, u32[]{:S(2)}) %collective-permute-start.28) | collective-permute-done | bytes 40992 | tf_op jit(solution)/shard_map/ppermute | solution.py:250
  173.2 2.6 %project.1 = bf16[128,1280]{1,0:T(8,128)(2,1)} custom-call(s32[2]{0:T(128)S(1)} %pad_add_fusion.me_ref, bf16[192,128]{1,0:T(8,128)(2,1)S(1)} %get-tuple-element.34.refs_0_, bf16[128,128]{1,0:T(8,128)(2,1)S(1)} %collective-permute-done.15.refs_1_, bf16[192,128]{1,0:T(8,128)(2,1)S(1)} %collective-permute-done.16.refs_2_, ...), custom_call_target="tpu_custom_call" | custom-call | flops 419430400 | bytes 4259840 | tf_op jit(solution)/shard_map/project/pallas_call | solution.py:363
  (70 shorter events, 16.8 us)
Async XLA Ops:
  6.5 40.8 %copy-start = (bf16[160,1280]{1,0:T(8,128)(2,1)S(1)}, bf16[160,1280]{1,0:T(8,128)(2,1)}, u32[]{:S(2)}) copy-start(bf16[160,1280]{1,0:T(8,128)(2,1)} %param.13) | copy-start | bytes 1228804
  6.5 92.8 %all-gather.2.cloned.1.call-start = ((), (), s32[]{:S(2)}) async-start(), calls=%async_computation | async-start | bytes 1843200 | tf_op jit(solution)/shard_map/all_gather | solution.py:303
  6.5 13.0 %collective-permute-start.1 = (bf16[128,1280]{1,0:T(8,128)(2,1)}, bf16[128,1280]{1,0:T(8,128)(2,1)S(1)}, u32[]{:S(2)}, u32[]{:S(2)}) collective-permute-start(bf16[128,1280]{1,0:T(8,128)(2,1)} %bitcast.11), channel_id=1, source_target_pairs={{0,2},{1,3},{2,4},{3,5},{4,6},{5,7},{6,0},{7,1},{8,10},{9,11},{10,... | collective-permute-start | bytes 983048 | tf_op jit(solution)/shard_map/ppermute | solution.py:237
  19.5 10.7 %collective-permute-start.3 = (bf16[128,1280]{1,0:T(8,128)(2,1)S(1)}, bf16[128,1280]{1,0:T(8,128)(2,1)S(1)}, u32[]{:S(2)}, u32[]{:S(2)}) collective-permute-start(bf16[128,1280]{1,0:T(8,128)(2,1)S(1)} %collective-permute-done.1.refs_2_), channel_id=1, source_target_pairs={{0,2},{1,3},{2,4},{3,5},{4,6},{5,7},{6,0},{7,1},{8,10},{9,11},{10,... | collective-permute-start | bytes 983048 | tf_op jit(solution)/shard_map/ppermute | solution.py:237
  30.2 9.8 %collective-permute-start.5 = (bf16[128,1280]{1,0:T(8,128)(2,1)S(1)}, bf16[128,1280]{1,0:T(8,128)(2,1)S(1)}, u32[]{:S(2)}, u32[]{:S(2)}) collective-permute-start(bf16[128,1280]{1,0:T(8,128)(2,1)S(1)} %collective-permute-done.3.refs_4_), channel_id=1, source_target_pairs={{0,2},{1,3},{2,4},{3,5},{4,6},{5,7},{6,0},{7,1},{8,10},{9,11},{10,... | collective-permute-start | bytes 983048 | tf_op jit(solution)/shard_map/ppermute | solution.py:237
  40.0 7.3 %collective-permute-start.6 = (bf16[128,1280]{1,0:T(8,128)(2,1)S(1)}, bf16[128,1280]{1,0:T(8,128)(2,1)S(1)}, u32[]{:S(2)}, u32[]{:S(2)}) collective-permute-start(bf16[128,1280]{1,0:T(8,128)(2,1)S(1)} %collective-permute-done.5.refs_6_), channel_id=1, source_target_pairs={{0,1},{1,0},{2,3},{3,2},{4,5},{5,4},{6,7},{7,6},{8,9},{9,8},{10,11... | collective-permute-start | bytes 983048 | tf_op jit(solution)/shard_map/ppermute | solution.py:241
  48.0 12.6 %collective-permute-start = (bf16[128,1280]{1,0:T(8,128)(2,1)S(1)}, bf16[128,1280]{1,0:T(8,128)(2,1)S(1)}, u32[]{:S(2)}, u32[]{:S(2)}) collective-permute-start(bf16[128,1280]{1,0:T(8,128)(2,1)S(1)} %bitcast.12), channel_id=1, source_target_pairs={{0,1},{1,0},{2,3},{3,2},{4,5},{5,4},{6,7},{7,6},{8,9},{9,8},{10,11... | collective-permute-start | bytes 983048 | tf_op jit(solution)/shard_map/ppermute | solution.py:241
  49.4 17.4 %collective-permute-start.2 = (bf16[128,1280]{1,0:T(8,128)(2,1)S(1)}, bf16[128,1280]{1,0:T(8,128)(2,1)S(1)}, u32[]{:S(2)}, u32[]{:S(2)}) collective-permute-start(bf16[128,1280]{1,0:T(8,128)(2,1)S(1)} %collective-permute-done.1.refs_2_), channel_id=1, source_target_pairs={{0,1},{1,0},{2,3},{3,2},{4,5},{5,4},{6,7},{7,6},{8,9},{9,8},{10,11... | collective-permute-start | bytes 983048 | tf_op jit(solution)/shard_map/ppermute | solution.py:241
  50.1 20.2 %collective-permute-start.4 = (bf16[128,1280]{1,0:T(8,128)(2,1)S(1)}, bf16[128,1280]{1,0:T(8,128)(2,1)S(1)}, u32[]{:S(2)}, u32[]{:S(2)}) collective-permute-start(bf16[128,1280]{1,0:T(8,128)(2,1)S(1)} %collective-permute-done.3.refs_4_), channel_id=1, source_target_pairs={{0,1},{1,0},{2,3},{3,2},{4,5},{5,4},{6,7},{7,6},{8,9},{9,8},{10,11... | collective-permute-start | bytes 983048 | tf_op jit(solution)/shard_map/ppermute | solution.py:241
  87.0 12.4 %collective-permute-start.8 = (bf16[160,1024]{1,0:T(8,128)(2,1)S(1)}, bf16[160,1024]{1,0:T(8,128)(2,1)S(1)}, u32[]{:S(2)}, u32[]{:S(2)}) collective-permute-start(bf16[160,1024]{1,0:T(8,128)(2,1)S(1)} %get-tuple-element.32.refs_0_), channel_id=1, source_target_pairs={{0,2},{1,3},{2,4},{3,5},{4,6},{5,7},{6,0},{7,1},{8,10},{9,11},{10,... | collective-permute-start | bytes 983048 | tf_op jit(solution)/shard_map/ppermute | solution.py:237
  99.3 8.9 %collective-permute-start.10 = (bf16[160,1024]{1,0:T(8,128)(2,1)S(1)}, bf16[160,1024]{1,0:T(8,128)(2,1)S(1)}, u32[]{:S(2)}, u32[]{:S(2)}) collective-permute-start(bf16[160,1024]{1,0:T(8,128)(2,1)S(1)} %collective-permute-done.8.refs_2_), channel_id=1, source_target_pairs={{0,2},{1,3},{2,4},{3,5},{4,6},{5,7},{6,0},{7,1},{8,10},{9,11},{10,... | collective-permute-start | bytes 983048 | tf_op jit(solution)/shard_map/ppermute | solution.py:237
  99.3 73.8 %collective-permute-start.29 = (bf16[640,1280]{1,0:T(8,128)(2,1)}, bf16[640,1280]{1,0:T(8,128)(2,1)S(1)}, u32[]{:S(2)}, u32[]{:S(2)}) collective-permute-start(bf16[640,1280]{1,0:T(8,128)(2,1)} %all-gather.2.cloned.1.call-done.refs_16_), channel_id=1, source_target_pairs={{0,8},{8,0},{16,24},{24,16},{1,9},{9,1},{17,25},{25,17},{2,10},{10... | collective-permute-start | bytes 4915208 | tf_op jit(solution)/shard_map/ppermute | solution.py:305
  99.3 21.9 %collective-permute-start.7 = (bf16[160,1024]{1,0:T(8,128)(2,1)S(1)}, bf16[160,1024]{1,0:T(8,128)(2,1)S(1)}, u32[]{:S(2)}, u32[]{:S(2)}) collective-permute-start(bf16[160,1024]{1,0:T(8,128)(2,1)S(1)} %get-tuple-element.32.refs_0_), channel_id=1, source_target_pairs={{0,1},{1,0},{2,3},{3,2},{4,5},{5,4},{6,7},{7,6},{8,9},{9,8},{10,11... | collective-permute-start | bytes 983048 | tf_op jit(solution)/shard_map/ppermute | solution.py:241
  108.2 11.0 %collective-permute-start.12 = (bf16[160,1024]{1,0:T(8,128)(2,1)S(1)}, bf16[160,1024]{1,0:T(8,128)(2,1)S(1)}, u32[]{:S(2)}, u32[]{:S(2)}) collective-permute-start(bf16[160,1024]{1,0:T(8,128)(2,1)S(1)} %collective-permute-done.10.refs_4_), channel_id=1, source_target_pairs={{0,2},{1,3},{2,4},{3,5},{4,6},{5,7},{6,0},{7,1},{8,10},{9,11},{10,... | collective-permute-start | bytes 983048 | tf_op jit(solution)/shard_map/ppermute | solution.py:237
  109.1 9.0 %collective-permute-start.14 = (bf16[3,32,1280]{2,1,0:T(8,128)(2,1)S(1)}, bf16[3,32,1280]{2,1,0:T(8,128)(2,1)S(1)}, u32[]{:S(2)}, u32[]{:S(2)}) collective-permute-start(bf16[3,32,1280]{2,1,0:T(8,128)(2,1)S(1)} %constant_dynamic-slice_fusion.1), channel_id=1, source_target_pairs={{0,1},{1,0},{2,3},{3,2},{4,5},{5,4},{6,7},{7,6},{8,9},{9,8},{10,11... | collective-permute-start | bytes 737288 | tf_op jit(solution)/shard_map/ppermute | solution.py:263
  111.5 13.6 %collective-permute-start.9 = (bf16[160,1024]{1,0:T(8,128)(2,1)S(1)}, bf16[160,1024]{1,0:T(8,128)(2,1)S(1)}, u32[]{:S(2)}, u32[]{:S(2)}) collective-permute-start(bf16[160,1024]{1,0:T(8,128)(2,1)S(1)} %collective-permute-done.8.refs_2_), channel_id=1, source_target_pairs={{0,1},{1,0},{2,3},{3,2},{4,5},{5,4},{6,7},{7,6},{8,9},{9,8},{10,11... | collective-permute-start | bytes 983048 | tf_op jit(solution)/shard_map/ppermute | solution.py:241
  118.1 14.0 %collective-permute-start.11 = (bf16[160,1024]{1,0:T(8,128)(2,1)S(1)}, bf16[160,1024]{1,0:T(8,128)(2,1)S(1)}, u32[]{:S(2)}, u32[]{:S(2)}) collective-permute-start(bf16[160,1024]{1,0:T(8,128)(2,1)S(1)} %collective-permute-done.10.refs_4_), channel_id=1, source_target_pairs={{0,1},{1,0},{2,3},{3,2},{4,5},{5,4},{6,7},{7,6},{8,9},{9,8},{10,11... | collective-permute-start | bytes 983048 | tf_op jit(solution)/shard_map/ppermute | solution.py:241
  119.2 16.6 %collective-permute-start.13 = (bf16[160,1024]{1,0:T(8,128)(2,1)S(1)}, bf16[160,1024]{1,0:T(8,128)(2,1)S(1)}, u32[]{:S(2)}, u32[]{:S(2)}) collective-permute-start(bf16[160,1024]{1,0:T(8,128)(2,1)S(1)} %collective-permute-done.12.refs_6_), channel_id=1, source_target_pairs={{0,1},{1,0},{2,3},{3,2},{4,5},{5,4},{6,7},{7,6},{8,9},{9,8},{10,11... | collective-permute-start | bytes 983048 | tf_op jit(solution)/shard_map/ppermute | solution.py:241
  145.9 6.7 %collective-permute-start.15 = (bf16[128,128]{1,0:T(8,128)(2,1)S(1)}, bf16[128,128]{1,0:T(8,128)(2,1)S(1)}, u32[]{:S(2)}, u32[]{:S(2)}) collective-permute-start(bf16[128,128]{1,0:T(8,128)(2,1)S(1)} %get-tuple-element.35), channel_id=1, source_target_pairs={{0,1},{1,2},{2,3},{3,4},{4,5},{5,6},{6,7},{7,0},{8,9},{9,10},{10,1... | collective-permute-start | bytes 98312 | tf_op jit(solution)/shard_map/ppermute | solution.py:250
  146.7 7.4 %collective-permute-start.17 = (bf16[128,128]{1,0:T(8,128)(2,1)S(1)}, bf16[128,128]{1,0:T(8,128)(2,1)S(1)}, u32[]{:S(2)}, u32[]{:S(2)}) collective-permute-start(bf16[128,128]{1,0:T(8,128)(2,1)S(1)} %get-tuple-element.37), channel_id=1, source_target_pairs={{0,3},{1,4},{2,5},{3,6},{4,7},{5,0},{6,1},{7,2},{8,11},{9,12},{10,... | collective-permute-start | bytes 98312 | tf_op jit(solution)/shard_map/ppermute | solution.py:250
  147.5 12.5 %collective-permute-start.22 = (bf16[160,128]{1,0:T(8,128)(2,1)S(1)}, bf16[160,128]{1,0:T(8,128)(2,1)S(1)}, u32[]{:S(2)}, u32[]{:S(2)}) collective-permute-start(bf16[160,128]{1,0:T(8,128)(2,1)S(1)} %copy-done.12), channel_id=1, source_target_pairs={{0,1},{1,2},{2,3},{3,4},{4,5},{5,6},{6,7},{7,0},{8,9},{9,10},{10,1... | collective-permute-start | bytes 122888 | tf_op jit(solution)/shard_map/ppermute | solution.py:250
  148.7 6.0 %collective-permute-start.19 = (bf16[128,128]{1,0:T(8,128)(2,1)S(1)}, bf16[128,128]{1,0:T(8,128)(2,1)S(1)}, u32[]{:S(2)}, u32[]{:S(2)}) collective-permute-start(bf16[128,128]{1,0:T(8,128)(2,1)S(1)} %get-tuple-element.39), channel_id=1, source_target_pairs={{0,5},{1,6},{2,7},{3,0},{4,1},{5,2},{6,3},{7,4},{8,13},{9,14},{10,... | collective-permute-start | bytes 98312 | tf_op jit(solution)/shard_map/ppermute | solution.py:250
  152.5 6.0 %collective-permute-start.21 = (bf16[128,128]{1,0:T(8,128)(2,1)S(1)}, bf16[128,128]{1,0:T(8,128)(2,1)S(1)}, u32[]{:S(2)}, u32[]{:S(2)}) collective-permute-start(bf16[128,128]{1,0:T(8,128)(2,1)S(1)} %get-tuple-element.41), channel_id=1, source_target_pairs={{0,7},{1,0},{2,1},{3,2},{4,3},{5,4},{6,5},{7,6},{8,15},{9,8},{10,9... | collective-permute-start | bytes 98312 | tf_op jit(solution)/shard_map/ppermute | solution.py:250
  154.1 7.4 %collective-permute-start.23 = (bf16[160,128]{1,0:T(8,128)(2,1)S(1)}, bf16[160,128]{1,0:T(8,128)(2,1)S(1)}, u32[]{:S(2)}, u32[]{:S(2)}) collective-permute-start(bf16[160,128]{1,0:T(8,128)(2,1)S(1)} %copy-done.10), channel_id=1, source_target_pairs={{0,2},{1,3},{2,4},{3,5},{4,6},{5,7},{6,0},{7,1},{8,10},{9,11},{10,... | collective-permute-start | bytes 122888 | tf_op jit(solution)/shard_map/ppermute | solution.py:250
  154.7 9.1 %collective-permute-start.24 = (bf16[160,128]{1,0:T(8,128)(2,1)S(1)}, bf16[160,128]{1,0:T(8,128)(2,1)S(1)}, u32[]{:S(2)}, u32[]{:S(2)}) collective-permute-start(bf16[160,128]{1,0:T(8,128)(2,1)S(1)} %copy-done.8), channel_id=1, source_target_pairs={{0,3},{1,4},{2,5},{3,6},{4,7},{5,0},{6,1},{7,2},{8,11},{9,12},{10,... | collective-permute-start | bytes 122888 | tf_op jit(solution)/shard_map/ppermute | solution.py:250
  158.5 5.5 %collective-permute-start.25 = (bf16[160,128]{1,0:T(8,128)(2,1)S(1)}, bf16[160,128]{1,0:T(8,128)(2,1)S(1)}, u32[]{:S(2)}, u32[]{:S(2)}) collective-permute-start(bf16[160,128]{1,0:T(8,128)(2,1)S(1)} %copy-done.6), channel_id=1, source_target_pairs={{0,4},{1,5},{2,6},{3,7},{4,0},{5,1},{6,2},{7,3},{8,12},{9,13},{10,... | collective-permute-start | bytes 122888 | tf_op jit(solution)/shard_map/ppermute | solution.py:250
  159.9 5.9 %collective-permute-start.26 = (bf16[160,128]{1,0:T(8,128)(2,1)S(1)}, bf16[160,128]{1,0:T(8,128)(2,1)S(1)}, u32[]{:S(2)}, u32[]{:S(2)}) collective-permute-start(bf16[160,128]{1,0:T(8,128)(2,1)S(1)} %get-tuple-element.55), channel_id=1, source_target_pairs={{0,5},{1,6},{2,7},{3,0},{4,1},{5,2},{6,3},{7,4},{8,13},{9,14},{10,... | collective-permute-start | bytes 122888 | tf_op jit(solution)/shard_map/ppermute | solution.py:250
  161.5 7.6 %collective-permute-start.27 = (bf16[160,128]{1,0:T(8,128)(2,1)S(1)}, bf16[160,128]{1,0:T(8,128)(2,1)S(1)}, u32[]{:S(2)}, u32[]{:S(2)}) collective-permute-start(bf16[160,128]{1,0:T(8,128)(2,1)S(1)} %get-tuple-element.56), channel_id=1, source_target_pairs={{0,6},{1,7},{2,0},{3,1},{4,2},{5,3},{6,4},{7,5},{8,14},{9,15},{10,... | collective-permute-start | bytes 122888 | tf_op jit(solution)/shard_map/ppermute | solution.py:250
  163.7 9.4 %collective-permute-start.16 = (bf16[192,128]{1,0:T(8,128)(2,1)S(1)}, bf16[192,128]{1,0:T(8,128)(2,1)S(1)}, u32[]{:S(2)}, u32[]{:S(2)}) collective-permute-start(bf16[192,128]{1,0:T(8,128)(2,1)S(1)} %get-tuple-element.36), channel_id=1, source_target_pairs={{0,2},{1,3},{2,4},{3,5},{4,6},{5,7},{6,0},{7,1},{8,10},{9,11},{10,... | collective-permute-start | bytes 147464 | tf_op jit(solution)/shard_map/ppermute | solution.py:250
  163.9 9.2 %collective-permute-start.18 = (bf16[192,128]{1,0:T(8,128)(2,1)S(1)}, bf16[192,128]{1,0:T(8,128)(2,1)S(1)}, u32[]{:S(2)}, u32[]{:S(2)}) collective-permute-start(bf16[192,128]{1,0:T(8,128)(2,1)S(1)} %get-tuple-element.38), channel_id=1, source_target_pairs={{0,4},{1,5},{2,6},{3,7},{4,0},{5,1},{6,2},{7,3},{8,12},{9,13},{10,... | collective-permute-start | bytes 147464 | tf_op jit(solution)/shard_map/ppermute | solution.py:250
  165.8 7.3 %collective-permute-start.20 = (bf16[192,128]{1,0:T(8,128)(2,1)S(1)}, bf16[192,128]{1,0:T(8,128)(2,1)S(1)}, u32[]{:S(2)}, u32[]{:S(2)}) collective-permute-start(bf16[192,128]{1,0:T(8,128)(2,1)S(1)} %get-tuple-element.40), channel_id=1, source_target_pairs={{0,6},{1,7},{2,0},{3,1},{4,2},{5,3},{6,4},{7,5},{8,14},{9,15},{10,... | collective-permute-start | bytes 147464 | tf_op jit(solution)/shard_map/ppermute | solution.py:250
  169.1 4.0 %collective-permute-start.28 = (bf16[160,128]{1,0:T(8,128)(2,1)S(1)}, bf16[160,128]{1,0:T(8,128)(2,1)S(1)}, u32[]{:S(2)}, u32[]{:S(2)}) collective-permute-start(bf16[160,128]{1,0:T(8,128)(2,1)S(1)} %get-tuple-element.57), channel_id=1, source_target_pairs={{0,7},{1,0},{2,1},{3,2},{4,3},{5,4},{6,5},{7,6},{8,15},{9,8},{10,9... | collective-permute-start | bytes 122888 | tf_op jit(solution)/shard_map/ppermute | solution.py:250
  (13 other events, 130.5 us)
Sparse Core Ops, SparseCore 0:
  48.1 48.9 all-gather.1

commit v2 on v1

v2 whole, which is shorter than its diff:
```python
import functools

import jax
import jax.numpy as jnp
from jax import lax
from jax.experimental import pallas as pl
from jax.experimental.pallas import tpu as pltpu
from jax.sharding import PartitionSpec as P

C = 1280
HEADS = 20
HEAD_DIM = 64
GROUPS = 32
SPAN = C // GROUPS
OUTER = 4
SET_HEADS = HEADS // OUTER
SET_CHANNELS = SET_HEADS * HEAD_DIM
FIXED = 4
EPSILON = 1e-05
VMEM_LIMIT = 48 * 1024 * 1024

f32 = jnp.float32
bf16 = jnp.bfloat16

NT = (((1,), (1,)), ((), ()))
NN = (((1,), (0,)), ((), ()))


def dot(left, right, dims=NN, precision=None):
    return lax.dot_general(left, right, dims, preferred_element_type=f32, precision=precision)


def exact(left, right, dims=NN):
    return dot(left, right, dims, lax.Precision.HIGHEST)


def conv_kernel(columns, place_ref, *refs):
    count = len(refs) - 6
    pieces = refs[:count]
    kernel_ref, bias_ref = refs[count : count + 2]
    out_refs = refs[count + 2 : count + 4]
    act_ref, kept_ref = refs[count + 4 :]
    block = pieces[0].shape[0]
    positions = block * count
    own = out_refs[0].shape[0]
    me = place_ref[0]
    entries = float(positions * SPAN)
    chunk = 16
    steps = block // chunk
    starts = [
        pl.multiple_of(place_ref[FIXED + index] * (2 * block) + (index % 2) * block, block)
        for index in range(count)
    ]

    def add(step, total):
        for piece in pieces:
            total = total + piece[pl.ds(step * chunk, chunk), :].astype(f32)
        return total

    member = (
        lax.broadcasted_iota(jnp.int32, (C, 128), 0) // SPAN
        == lax.broadcasted_iota(jnp.int32, (C, 128), 1)
    ).astype(f32)

    def group_mean(total):
        summed = jnp.sum(total, axis=0, keepdims=True)
        per_group = exact(jnp.broadcast_to(summed, (8, C)), member) / entries
        return exact(per_group, member, NT)[0:1, :]

    zero = jnp.zeros((chunk, C), f32)
    centre = group_mean(lax.fori_loop(0, steps, add, zero))

    def add_square(step, total):
        for piece in pieces:
            away = piece[pl.ds(step * chunk, chunk), :].astype(f32) - centre
            total = total + away * away
        return total

    spread = group_mean(lax.fori_loop(0, steps, add_square, zero))
    half_scale = 0.5 * lax.rsqrt(spread + EPSILON)

    act_ref[0:columns, :] = jnp.zeros((columns, C), bf16)
    act_ref[positions + columns :, :] = jnp.zeros((columns, C), bf16)

    def activate(step, carry):
        for start, piece in zip(starts, pieces):
            half = (piece[pl.ds(step * chunk, chunk), :].astype(f32) - centre) * half_scale
            value = half + half * jnp.tanh(half)
            row = pl.multiple_of(columns + start + step * chunk, chunk)
            act_ref[pl.ds(row, chunk), :] = value.astype(bf16)
        return carry

    lax.fori_loop(0, steps, activate, 0)

    choose = (
        lax.broadcasted_iota(jnp.int32, (own, C), 0) + me * own
        == lax.broadcasted_iota(jnp.int32, (own, C), 1)
    ).astype(bf16)
    for index in range(0, count, 2):
        pair = jnp.concatenate([pieces[index][...], pieces[index + 1][...]], axis=0)
        start = pl.multiple_of(starts[index], 2 * block)
        kept_ref[:, pl.ds(start, 2 * block)] = dot(choose, pair, NT)

    wide = 256
    column = lax.broadcasted_iota(jnp.int32, (own, wide), 1) % columns
    bias = bias_ref[...]
    for at in range(0, positions, wide):
        taps = dot(kernel_ref[0], act_ref[at : at + wide, :], NT)
        for shift in (1, 2):
            low = at + shift * columns
            taps = taps + dot(kernel_ref[shift], act_ref[low : low + wide, :], NT)
        before = jnp.where(column > 0, pltpu.roll(taps[0:own], 1, 1), 0.0)
        after_ = jnp.where(column < columns - 1, pltpu.roll(taps[2 * own :], wide - 1, 1), 0.0)
        convolved = taps[own : 2 * own] + before + after_
        hidden = kept_ref[:, at : at + wide] + convolved + bias
        which, low = divmod(at, positions // 2)
        out_refs[which][:, low : low + wide] = hidden.astype(bf16)


def attention_kernel(inner, place_ref, *refs):
    count = len(refs) - 8 - OUTER
    pieces = refs[:count]
    weight_ref = refs[count]
    outs = refs[count + 1 : count + 1 + OUTER]
    kept_ref = refs[count + 1 + OUTER]
    hidden_ref, normed_ref, query_ref, key_ref, value_ref, sems = refs[count + 2 + OUTER :]
    own, part = pieces[0].shape
    n = count // 2
    positions = 2 * part
    block = positions // n
    me, outer_at, inner_at = place_ref[0], place_ref[1], place_ref[2]
    entries = float(positions * SPAN)

    copies = []
    for index, piece in enumerate(pieces):
        row = pl.multiple_of(place_ref[FIXED + index] * own, own)
        low = (index % 2) * part
        target = hidden_ref.at[pl.ds(row, own), low : low + part]
        copy = pltpu.make_async_copy(piece, target, sems.at[index])
        copy.start()
        copies.append(copy)
    for copy in copies:
        copy.wait()

    kept_ref[...] = hidden_ref[:, pl.ds(pl.multiple_of(me * block, block), block)]
    for at in range(0, C, 2 * SPAN):
        pair = hidden_ref[at : at + 2 * SPAN, :].astype(f32)
        scaled = []
        for low in (0, SPAN):
            group = pair[low : low + SPAN]
            mean = jnp.sum(jnp.sum(group, axis=0, keepdims=True), axis=1, keepdims=True) / entries
            away = group - mean
            square = jnp.sum(away * away, axis=0, keepdims=True)
            var = jnp.sum(square, axis=1, keepdims=True) / entries
            scaled.append(away * lax.rsqrt(var + EPSILON))
        normed_ref[at : at + 2 * SPAN, :] = jnp.concatenate(scaled, axis=0).astype(bf16)

    wide = 256
    for at in range(0, positions, wide):
        made = dot(weight_ref[SET_CHANNELS:, :], normed_ref[:, at : at + wide])
        for head in range(SET_HEADS):
            low = head * HEAD_DIM
            key_ref[head, at : at + wide, :] = made[low : low + HEAD_DIM].T.astype(bf16)
        value_ref[:, at : at + wide] = made[SET_CHANNELS:].astype(bf16)

    for at in range(0, OUTER, 2):
        normed = []
        for step in (at, at + 1):
            target = lax.rem(outer_at + step, OUTER) * inner + inner_at
            normed.append(normed_ref[:, pl.ds(pl.multiple_of(target * block, block), block)])
        made = dot(weight_ref[:SET_CHANNELS, :], jnp.concatenate(normed, axis=1))
        scaled = made.astype(bf16).astype(f32) * HEAD_DIM ** (-0.5)
        query_ref[:, at * block : (at + 2) * block] = scaled.astype(bf16)

    for at in range(0, OUTER, 2):
        for head in range(SET_HEADS):
            low = head * HEAD_DIM
            query = query_ref[low : low + HEAD_DIM, at * block : (at + 2) * block]
            scores = dot(key_ref[head], query)
            peak = jnp.max(scores, axis=0, keepdims=True)
            unnormalized = jnp.exp(scores - peak)
            total = jnp.sum(unnormalized, axis=0, keepdims=True)
            mixture = dot(value_ref[low : low + HEAD_DIM, :], unnormalized.astype(bf16))
            attended = (mixture / total).astype(bf16)
            outs[at][low : low + HEAD_DIM, :] = attended[:, :block]
            outs[at + 1][low : low + HEAD_DIM, :] = attended[:, block:]


def output_kernel(n, splits, place_ref, *refs):
    attended_refs = refs[:OUTER]
    hidden_ref = refs[OUTER]
    weight_refs = refs[OUTER + 1 : OUTER + 1 + splits]
    out_ref, attended_ref, total_ref = refs[OUTER + 1 + splits :]
    outer_at, mine = place_ref[1], place_ref[3]
    for step in range(OUTER):
        origin = lax.rem(outer_at + OUTER - step, OUTER)
        row = pl.multiple_of(origin * SET_CHANNELS, SET_CHANNELS)
        attended_ref[pl.ds(row, SET_CHANNELS), :] = attended_refs[step][...]
    total_ref[...] = hidden_ref[...].astype(f32)
    attended = attended_ref[...]
    own = C // n
    part = own // splits
    for step, weight_ref in enumerate(weight_refs):
        which = jnp.bitwise_xor(mine, step)
        made = dot(weight_ref[...], attended)
        for origin in range(n):
            row = pl.multiple_of(origin * own + which * part, 8)
            total_ref[pl.ds(row, part), :] += made[origin * part : (origin + 1) * part]
    out_ref[...] = total_ref[...].T.astype(bf16)


def ring_of(n):
    inner = n // OUTER
    path = [(0, 0)]
    for outer_at in range(OUTER):
        across = range(1, inner) if outer_at % 2 == 0 else range(inner - 1, 0, -1)
        path += [(outer_at, inner_at) for inner_at in across]
    path += [(outer_at, 0) for outer_at in range(OUTER - 1, 0, -1)]
    return [outer_at * inner + inner_at for outer_at, inner_at in path]


def pieces_of(n):
    far = n // 2
    return [0] + [away for step in range(1, far) for away in (-step, step)] + [far]


def sources_of(n):
    ring = ring_of(n)
    table = []
    for device in range(n):
        at = ring.index(device)
        table.append([ring[(at + away) % n] for away in pieces_of(n) for _ in (0, 1)])
    return table


def gather(halves, n):
    ring = ring_of(n)
    forward = [(ring[at], ring[(at + 1) % n]) for at in range(n)]
    backward = [(target, start) for start, target in forward]
    far = n // 2
    found = {(0, 0): halves[0], (1, 0): halves[1]}
    for step in range(1, far + 1):
        for half in (0, 1):
            for sign, pairs in ((-1, forward), (1, backward)):
                if step == far and (half == 0) != (sign == -1):
                    continue
                found[half, sign * step] = lax.ppermute(
                    found[half, sign * (step - 1)], "patch", pairs
                )
    found[0, far] = found[0, -far]
    return [found[half, away] for away in pieces_of(n) for half in (0, 1)]


def swap_weights(weights, core, n, ready):
    if n // OUTER != 2:
        return None
    rows = weights.reshape(-1, C)
    part = rows.shape[0] // 2
    own_half = after(lax.dynamic_slice_in_dim(rows, core * part, part, 0), *ready)
    return lax.ppermute(own_half, "patch", [(at, at ^ 1) for at in range(n)])


def set_weights(weights, first, inner_at, core, n, ready):
    inner = n // OUTER
    if inner == 2:
        first = after(first, ready)
        cores = [(at, at ^ 1) for at in range(lax.axis_size("batch"))]
        second = lax.ppermute(first, "batch", cores)
        low = jnp.where(core == 0, first, second)
        high = jnp.where(core == 0, second, first)
        other = jnp.concatenate([low, high], axis=0).reshape(weights.shape)
        return jnp.concatenate(
            [jnp.where(inner_at == 0, weights, other), jnp.where(inner_at == 0, other, weights)],
            axis=1,
        )
    sets = [list(range(at, at + inner)) for at in range(0, n, inner)]
    return lax.all_gather(weights, "patch", axis=1, tiled=True, axis_index_groups=sets)


def output_weights(w_out, mine, splits, ready):
    part = w_out.shape[0] // splits
    shard = after(lax.dynamic_slice_in_dim(w_out, mine * part, part, 0), *ready)
    parts = [lax.all_gather(shard, "patch", axis=0, tiled=True)]
    batch = lax.axis_size("batch")
    step = splits // 2
    while step:
        swap = [(at, at ^ step) for at in range(batch)]
        parts = parts + [lax.ppermute(one, "batch", swap) for one in parts]
        step //= 2
    order = [0]
    step = splits // 2
    while step:
        order = order + [one ^ step for one in order]
        step //= 2
    return [parts[order.index(at)] for at in range(splits)]


def after(value, *ready):
    anywhere = pl.BlockSpec(memory_space=pl.ANY)
    return pl.pallas_call(
        lambda *refs: None,
        out_shape=jax.ShapeDtypeStruct(value.shape, value.dtype),
        in_specs=[anywhere] * (1 + len(ready)),
        out_specs=anywhere,
        input_output_aliases={0: 0},
        name="after",
    )(value, *ready)


def on_device(latent, conv_weight, channel_bias, w_query, w_key, w_value, w_out):
    rows_local, columns, channels = latent.shape
    n = lax.axis_size("patch")
    inner = n // OUTER
    own = channels // n
    block = rows_local * columns
    positions = block * n
    splits = 4 if own % 32 == 0 else 2
    me = lax.axis_index("patch")
    batch_at = lax.axis_index("batch")
    inner_at = lax.rem(me, inner)
    mine = lax.rem(batch_at, splits)
    fixed = jnp.stack([me, lax.div(me, inner), inner_at, mine]).astype(jnp.int32)
    sources = jnp.asarray(sources_of(n), jnp.int32)
    place = jnp.concatenate([fixed, lax.dynamic_index_in_dim(sources, me, 0, keepdims=False)])
    vmem = pl.BlockSpec(memory_space=pltpu.VMEM)
    smem = pl.BlockSpec(memory_space=pltpu.SMEM)
    anywhere = pl.BlockSpec(memory_space=pl.ANY)
    params = pltpu.CompilerParams(vmem_limit_bytes=VMEM_LIMIT)

    whole = latent.reshape(block, channels)
    pieces = gather((whole[: block // 2], whole[block // 2 :]), n)

    weights = jnp.stack([w_query, w_key, w_value])
    core = lax.rem(batch_at, 2)
    first = swap_weights(weights, core, n, pieces[-5:])
    out_parts = output_weights(w_out, mine, splits, pieces[-5:])

    hidden = pl.pallas_call(
        functools.partial(conv_kernel, columns),
        out_shape=[jax.ShapeDtypeStruct((own, positions // 2), bf16)] * 2,
        in_specs=[smem] + [vmem] * (2 * n + 2),
        out_specs=[vmem] * 2,
        scratch_shapes=[
            pltpu.VMEM((positions + 2 * columns, channels), bf16),
            pltpu.VMEM((own, positions), f32),
        ],
        compiler_params=params,
        cost_estimate=pl.CostEstimate(
            flops=2 * 9 * positions * channels * own,
            bytes_accessed=2 * (positions * channels + 9 * channels * own),
            transcendentals=positions * channels,
        ),
        name="norm_conv",
    )(
        place,
        *pieces,
        conv_weight.reshape(3, 3 * own, channels),
        channel_bias.reshape(own, 1),
    )

    hidden_pieces = gather(tuple(hidden), n)
    weights = set_weights(weights, first, inner_at, core, n, hidden_pieces[4])
    weights = weights.reshape(3 * SET_CHANNELS, channels)

    *attended, kept = pl.pallas_call(
        functools.partial(attention_kernel, inner),
        out_shape=[jax.ShapeDtypeStruct((SET_CHANNELS, block), bf16)] * OUTER
        + [jax.ShapeDtypeStruct((channels, block), bf16)],
        in_specs=[smem] + [anywhere] * (2 * n) + [vmem],
        out_specs=[vmem] * (OUTER + 1),
        scratch_shapes=[
            pltpu.VMEM((channels, positions), bf16),
            pltpu.VMEM((channels, positions), bf16),
            pltpu.VMEM((SET_CHANNELS, OUTER * block), bf16),
            pltpu.VMEM((SET_HEADS, positions, HEAD_DIM), bf16),
            pltpu.VMEM((SET_CHANNELS, positions), bf16),
            pltpu.SemaphoreType.DMA((2 * n,)),
        ],
        compiler_params=params,
        cost_estimate=pl.CostEstimate(
            flops=2 * positions * channels * 3 * SET_CHANNELS
            + 4 * positions * OUTER * block * SET_CHANNELS,
            bytes_accessed=2 * (positions * channels + 3 * SET_CHANNELS * channels),
            transcendentals=positions * OUTER * block * SET_HEADS,
        ),
        name="attention",
    )(place, *hidden_pieces, weights)

    received = [attended[0]]
    for step in range(1, OUTER):
        pairs = [(at, (at + step * inner) % n) for at in range(n)]
        received.append(lax.ppermute(attended[step], "patch", pairs))

    output = pl.pallas_call(
        functools.partial(output_kernel, n, splits),
        out_shape=jax.ShapeDtypeStruct((block, channels), bf16),
        in_specs=[smem] + [vmem] * (OUTER + 1 + splits),
        out_specs=vmem,
        scratch_shapes=[
            pltpu.VMEM((channels, block), bf16),
            pltpu.VMEM((channels, block), f32),
        ],
        compiler_params=params,
        cost_estimate=pl.CostEstimate(
            flops=2 * block * channels * channels,
            bytes_accessed=2 * channels * (channels + 3 * block),
            transcendentals=0,
        ),
        name="project",
    )(place, *received, kept, *out_parts)
    return output.reshape(rows_local, columns, channels)


def solution(mesh):
    return jax.shard_map(
        on_device,
        mesh=mesh,
        in_specs=(
            P(("batch", "patch"), None, None),
            P(None, None, "patch", None),
            P("patch"),
            P("patch", None),
            P("patch", None),
            P("patch", None),
            P("patch", None),
        ),
        out_specs=P(("batch", "patch"), None, None),
        check_vma=False,
    )
```

time: 183 us -> 143 us (0.78)
  waiting for transfers between devices: 96.9 us -> 32.2 us
  blocking collectives: 0 us -> 35.2 us
  between operations: 13.5 us -> 0.2 us
  local copies, waits for them, and re-layouts: 7.2 us -> 10.1 us
    ppermute x30 -> x36, waiting for transfers between devices: 96.9 us -> 32.2 us  [the longest x28 24.6 us: gather(): lax.ppermute(found[half, sign * (step - 1)], 'patch', pairs)]
    all_gather x0 -> x1, blocking collectives: none -> 35.2 us  [output_weights(): parts = [lax.all_gather(shard, 'patch', axis=0, tiled=True)]]
    unnamed x28 -> x32, local copies, waits for them, and re-layouts: 4.17 us -> 5.94 us
    pallas_call x3 -> x6, Pallas kernels: 25.1 us -> 26.4 us  [the longest x1 12 us: on_device(): pl.pallas_call(functools.partial(conv_kernel, columns), out_shape=[jax.Sh...]
    ppermute x30 -> x36, starting transfers between devices: 36.1 us -> 35.1 us  [the longest x28 28.7 us: gather(): lax.ppermute(found[half, sign * (step - 1)], 'patch', pairs)]
  transfers between devices with their start and end apart: 31 -> 36, of which waited for: 15 -> 16; matrix products, arithmetic and copies ran while one was open for 3% -> 4% of each run, Pallas kernels for 12% -> 17%
where the time goes in v2:
time: 143 us; the launch traced here: 142 us
  blocking collectives  35.2 us (25%)
  starting transfers between devices  35.1 us (25%)
  waiting for transfers between devices  32.2 us (23%)
  Pallas kernels  26.4 us (18%)
  local copies, waits for them, and re-layouts  10.1 us (7%)
  other arithmetic  3.06 us (2%)
    all_gather x1, blocking collectives, output_weights(): parts = [lax.all_gather(shard, 'patch', axis=0, tiled=True)]  35.2 us
    ppermute x28, starting transfers between devices, gather(): lax.ppermute(found[half, sign * (step - 1)], 'patch', pairs)  28.7 us
    ppermute x28, waiting for transfers between devices, gather(): lax.ppermute(found[half, sign * (step - 1)], 'patch', pairs)  24.6 us
    pallas_call x1, Pallas kernels, on_device(): pl.pallas_call(functools.partial(conv_kernel, columns), out_shape=[jax.Sh...  12 us
    pallas_call x1, Pallas kernels, on_device(): pl.pallas_call(functools.partial(attention_kernel, inner), out_shape=[jax...  11.9 us
    unnamed x32, local copies, waits for them, and re-layouts  5.94 us
    ppermute x3, waiting for transfers between devices, on_device(): received.append(lax.ppermute(attended[step], 'patch', pairs))  4.74 us
    ppermute x3, starting transfers between devices, on_device(): received.append(lax.ppermute(attended[step], 'patch', pairs))  3.88 us
  transfers between devices with their start and end apart: 36, of which 16 were waited for; matrix products, arithmetic and copies ran while one was open for 4% of the time, Pallas kernels for 17%

profile of v2, /device:TPU:0, one launch (start us, length us, event | category | flops | bytes accessed | tf_op | source)
XLA Modules:
  0.0 142.2 jit_solution(8105487918249173665)
XLA Ops:
  1.1 3.1 %collective-permute-start.3 = (bf16[64,1280]{1,0:T(8,128)(2,1)S(1)}, bf16[64,1280]{1,0:T(8,128)(2,1)S(1)}, u32[]{:S(2)}, u32[]{:S(2)}) collective-permute-start(bf16[64,1280]{1,0:T(8,128)(2,1)S(1)} %get-tuple-element.23.refs_1_), channel_id=1, source_target_pairs={{1,0},{3,1},{5,3},{7,5},{6,7},{4,6},{2,4},{0,2},{9,8},{11,9},{13,1... | collective-permute-start | bytes 491528 | tf_op jit(solution)/shard_map/ppermute | solution.py:247
  4.2 2.0 %collective-permute-start.2 = (bf16[64,1280]{1,0:T(8,128)(2,1)S(1)}, bf16[64,1280]{1,0:T(8,128)(2,1)S(1)}, u32[]{:S(2)}, u32[]{:S(2)}) collective-permute-start(bf16[64,1280]{1,0:T(8,128)(2,1)S(1)} %get-tuple-element.24.refs_0_), channel_id=1, source_target_pairs={{1,0},{3,1},{5,3},{7,5},{6,7},{4,6},{2,4},{0,2},{9,8},{11,9},{13,1... | collective-permute-start | bytes 491528 | tf_op jit(solution)/shard_map/ppermute | solution.py:247
  6.2 2.9 %collective-permute-done.3.refs_5_ = bf16[64,1280]{1,0:T(8,128)(2,1)S(1)} collective-permute-done((bf16[64,1280]{1,0:T(8,128)(2,1)S(1)}, bf16[64,1280]{1,0:T(8,128)(2,1)S(1)}, u32[]{:S(2)}, u32[]{:S(2)}) %collective-permute-start.3) | collective-permute-done | bytes 163872 | tf_op jit(solution)/shard_map/ppermute | solution.py:247
  9.1 2.1 %collective-permute-start.7 = (bf16[64,1280]{1,0:T(8,128)(2,1)S(1)}, bf16[64,1280]{1,0:T(8,128)(2,1)S(1)}, u32[]{:S(2)}, u32[]{:S(2)}) collective-permute-start(bf16[64,1280]{1,0:T(8,128)(2,1)S(1)} %collective-permute-done.3.refs_5_), channel_id=1, source_target_pairs={{1,0},{3,1},{5,3},{7,5},{6,7},{4,6},{2,4},{0,2},{9,8},{11,9},{13,1... | collective-permute-start | bytes 491528 | tf_op jit(solution)/shard_map/ppermute | solution.py:247
  12.6 2.1 %collective-permute-start.6 = (bf16[64,1280]{1,0:T(8,128)(2,1)S(1)}, bf16[64,1280]{1,0:T(8,128)(2,1)S(1)}, u32[]{:S(2)}, u32[]{:S(2)}) collective-permute-start(bf16[64,1280]{1,0:T(8,128)(2,1)S(1)} %collective-permute-done.2.refs_4_), channel_id=1, source_target_pairs={{1,0},{3,1},{5,3},{7,5},{6,7},{4,6},{2,4},{0,2},{9,8},{11,9},{13,1... | collective-permute-start | bytes 491528 | tf_op jit(solution)/shard_map/ppermute | solution.py:247
  14.8 1.5 %collective-permute-done.7.refs_9_ = bf16[64,1280]{1,0:T(8,128)(2,1)S(1)} collective-permute-done((bf16[64,1280]{1,0:T(8,128)(2,1)S(1)}, bf16[64,1280]{1,0:T(8,128)(2,1)S(1)}, u32[]{:S(2)}, u32[]{:S(2)}) %collective-permute-start.7) | collective-permute-done | bytes 163872 | tf_op jit(solution)/shard_map/ppermute | solution.py:247
  16.3 2.1 %collective-permute-start.11 = (bf16[64,1280]{1,0:T(8,128)(2,1)S(1)}, bf16[64,1280]{1,0:T(8,128)(2,1)S(1)}, u32[]{:S(2)}, u32[]{:S(2)}) collective-permute-start(bf16[64,1280]{1,0:T(8,128)(2,1)S(1)} %collective-permute-done.7.refs_9_), channel_id=1, source_target_pairs={{1,0},{3,1},{5,3},{7,5},{6,7},{4,6},{2,4},{0,2},{9,8},{11,9},{13,1... | collective-permute-start | bytes 491528 | tf_op jit(solution)/shard_map/ppermute | solution.py:247
  19.8 2.1 %collective-permute-start.10 = (bf16[64,1280]{1,0:T(8,128)(2,1)S(1)}, bf16[64,1280]{1,0:T(8,128)(2,1)S(1)}, u32[]{:S(2)}, u32[]{:S(2)}) collective-permute-start(bf16[64,1280]{1,0:T(8,128)(2,1)S(1)} %collective-permute-done.6.refs_8_), channel_id=1, source_target_pairs={{1,0},{3,1},{5,3},{7,5},{6,7},{4,6},{2,4},{0,2},{9,8},{11,9},{13,1... | collective-permute-start | bytes 491528 | tf_op jit(solution)/shard_map/ppermute | solution.py:247
  21.9 1.5 %collective-permute-done.11.refs_13_.refs_3_ = bf16[64,1280]{1,0:T(8,128)(2,1)S(1)} collective-permute-done((bf16[64,1280]{1,0:T(8,128)(2,1)S(1)}, bf16[64,1280]{1,0:T(8,128)(2,1)S(1)}, u32[]{:S(2)}, u32[]{:S(2)}) %collective-permute-start.11) | collective-permute-done | bytes 163872 | tf_op jit(solution)/shard_map/ppermute | solution.py:247
  23.4 2.1 %collective-permute-start.13 = (bf16[64,1280]{1,0:T(8,128)(2,1)S(1)}, bf16[64,1280]{1,0:T(8,128)(2,1)S(1)}, u32[]{:S(2)}, u32[]{:S(2)}) collective-permute-start(bf16[64,1280]{1,0:T(8,128)(2,1)S(1)} %collective-permute-done.11.refs_13_.refs_3_), channel_id=1, source_target_pairs={{1,0},{3,1},{5,3},{7,5},{6,7},{4,6},{2,4},{0,2},{9,8},{11,9},{13,1... | collective-permute-start | bytes 491528 | tf_op jit(solution)/shard_map/ppermute | solution.py:247
  26.9 2.1 %collective-permute-done.9.refs_11_.refs_1_ = bf16[64,1280]{1,0:T(8,128)(2,1)S(1)} collective-permute-done((bf16[64,1280]{1,0:T(8,128)(2,1)S(1)}, bf16[64,1280]{1,0:T(8,128)(2,1)S(1)}, u32[]{:S(2)}, u32[]{:S(2)}) %collective-permute-start.9) | collective-permute-done | bytes 163872 | tf_op jit(solution)/shard_map/ppermute | solution.py:247
  29.4 1.5 %collective-permute-done.12.refs_14_.refs_4_ = bf16[64,1280]{1,0:T(8,128)(2,1)S(1)} collective-permute-done((bf16[64,1280]{1,0:T(8,128)(2,1)S(1)}, bf16[64,1280]{1,0:T(8,128)(2,1)S(1)}, u32[]{:S(2)}, u32[]{:S(2)}) %collective-permute-start.12) | collective-permute-done | bytes 163872 | tf_op jit(solution)/shard_map/ppermute | solution.py:247
  37.8 12.0 %norm_conv.1 = (bf16[160,512]{1,0:T(8,128)(2,1)S(1)}, bf16[160,512]{1,0:T(8,128)(2,1)S(1)}) custom-call(s32[20]{0:T(128)S(1)} %concatenate.9.place_ref, bf16[64,1280]{1,0:T(8,128)(2,1)S(1)} %get-tuple-element.24.refs_0_, bf16[64,1280]{1,0:T(8,128)(2,1)S(1)} %get-tuple-element.23.refs_1_, bf16[64,1280]{1,0:T(8,128)(2,1)S(1)} %collective-permute-done.refs_2_, ...), custom_call_target="tpu_custom_call" | custom-call | flops 3774873600 | bytes 6307840 | tf_op jit(solution)/shard_map/norm_conv/pallas_call | solution.py:338
  49.8 1.6 %collective-permute-start.16 = (bf16[160,512]{1,0:T(8,128)(2,1)S(1)}, bf16[160,512]{1,0:T(8,128)(2,1)S(1)}, u32[]{:S(2)}, u32[]{:S(2)}) collective-permute-start(bf16[160,512]{1,0:T(8,128)(2,1)S(1)} %get-tuple-element.12.refs_0_), channel_id=1, source_target_pairs={{1,0},{3,1},{5,3},{7,5},{6,7},{4,6},{2,4},{0,2},{9,8},{11,9},{13,1... | collective-permute-start | bytes 491528 | tf_op jit(solution)/shard_map/ppermute | solution.py:247
  51.4 3.7 %collective-permute-done.16.refs_1_.refs_4_ = bf16[160,512]{1,0:T(8,128)(2,1)S(1)} collective-permute-done((bf16[160,512]{1,0:T(8,128)(2,1)S(1)}, bf16[160,512]{1,0:T(8,128)(2,1)S(1)}, u32[]{:S(2)}, u32[]{:S(2)}) %collective-permute-start.16) | collective-permute-done | bytes 163872 | tf_op jit(solution)/shard_map/ppermute | solution.py:247
  59.7 35.2 %all_gather.3.refs_5_ = bf16[320,1280]{1,0:T(8,128)(2,1)S(1)} all-gather(bf16[40,1280]{1,0:T(8,128)(2,1)} %after.5), channel_id=1, replica_groups=mesh['batch'=4,'patch'=8] {'patch'}, dimensions={0}, use_global_device_ids=true | all-gather | bytes 921600 | tf_op jit(solution)/shard_map/all_gather | solution.py:283
  94.9 1.6 %collective-permute-start.34 = (bf16[320,1280]{1,0:T(8,128)(2,1)S(1)}, bf16[320,1280]{1,0:T(8,128)(2,1)S(1)}, u32[]{:S(2)}, u32[]{:S(2)}) collective-permute-start(bf16[320,1280]{1,0:T(8,128)(2,1)S(1)} %all_gather.3.refs_5_), channel_id=1, source_target_pairs={{0,16},{8,24},{16,0},{24,8},{1,17},{9,25},{17,1},{25,9},{2,18},{10... | collective-permute-start | bytes 2457608 | tf_op jit(solution)/shard_map/ppermute | solution.py:288
  96.5 2.0 %collective-permute-start.18 = (bf16[160,512]{1,0:T(8,128)(2,1)S(1)}, bf16[160,512]{1,0:T(8,128)(2,1)S(1)}, u32[]{:S(2)}, u32[]{:S(2)}) collective-permute-start(bf16[160,512]{1,0:T(8,128)(2,1)S(1)} %collective-permute-done.14.refs_2_), channel_id=1, source_target_pairs={{0,1},{1,3},{3,5},{5,7},{7,6},{6,4},{4,2},{2,0},{8,9},{9,11},{11,1... | collective-permute-start | bytes 491528 | tf_op jit(solution)/shard_map/ppermute | solution.py:247
  98.6 2.0 %collective-permute-start.19 = (bf16[160,512]{1,0:T(8,128)(2,1)S(1)}, bf16[160,512]{1,0:T(8,128)(2,1)S(1)}, u32[]{:S(2)}, u32[]{:S(2)}) collective-permute-start(bf16[160,512]{1,0:T(8,128)(2,1)S(1)} %collective-permute-done.15.refs_3_), channel_id=1, source_target_pairs={{0,1},{1,3},{3,5},{5,7},{7,6},{6,4},{4,2},{2,0},{8,9},{9,11},{11,1... | collective-permute-start | bytes 491528 | tf_op jit(solution)/shard_map/ppermute | solution.py:247
  102.0 1.8 %collective-permute-done.21.refs_9_ = bf16[160,512]{1,0:T(8,128)(2,1)S(1)} collective-permute-done((bf16[160,512]{1,0:T(8,128)(2,1)S(1)}, bf16[160,512]{1,0:T(8,128)(2,1)S(1)}, u32[]{:S(2)}, u32[]{:S(2)}) %collective-permute-start.21) | collective-permute-done | bytes 163872 | tf_op jit(solution)/shard_map/ppermute | solution.py:247
  103.9 2.0 %collective-permute-start.25 = (bf16[160,512]{1,0:T(8,128)(2,1)S(1)}, bf16[160,512]{1,0:T(8,128)(2,1)S(1)}, u32[]{:S(2)}, u32[]{:S(2)}) collective-permute-start(bf16[160,512]{1,0:T(8,128)(2,1)S(1)} %collective-permute-done.21.refs_9_), channel_id=1, source_target_pairs={{1,0},{3,1},{5,3},{7,5},{6,7},{4,6},{2,4},{0,2},{9,8},{11,9},{13,1... | collective-permute-start | bytes 491528 | tf_op jit(solution)/shard_map/ppermute | solution.py:247
  105.9 2.8 %collective-permute-done.34.refs_7_ = bf16[320,1280]{1,0:T(8,128)(2,1)S(1)} collective-permute-done((bf16[320,1280]{1,0:T(8,128)(2,1)S(1)}, bf16[320,1280]{1,0:T(8,128)(2,1)S(1)}, u32[]{:S(2)}, u32[]{:S(2)}) %collective-permute-start.34) | collective-permute-done | bytes 819232 | tf_op jit(solution)/shard_map/ppermute | solution.py:288
  109.0 1.4 collective-permute-done.22.refs_10_
  110.4 1.9 %collective-permute-start.26 = (bf16[160,512]{1,0:T(8,128)(2,1)S(1)}, bf16[160,512]{1,0:T(8,128)(2,1)S(1)}, u32[]{:S(2)}, u32[]{:S(2)}) collective-permute-start(bf16[160,512]{1,0:T(8,128)(2,1)S(1)} %collective-permute-done.22.refs_10_), channel_id=1, source_target_pairs={{0,1},{1,3},{3,5},{5,7},{7,6},{6,4},{4,2},{2,0},{8,9},{9,11},{11,1... | collective-permute-start | bytes 491528 | tf_op jit(solution)/shard_map/ppermute | solution.py:247
  112.7 4.2 %collective-permute-done.24.refs_12_ = bf16[160,512]{1,0:T(8,128)(2,1)S(1)} collective-permute-done((bf16[160,512]{1,0:T(8,128)(2,1)S(1)}, bf16[160,512]{1,0:T(8,128)(2,1)S(1)}, u32[]{:S(2)}, u32[]{:S(2)}) %collective-permute-start.24) | collective-permute-done | bytes 163872 | tf_op jit(solution)/shard_map/ppermute | solution.py:247
  116.9 2.3 %collective-permute-done.27.refs_15_ = bf16[160,512]{1,0:T(8,128)(2,1)S(1)} collective-permute-done((bf16[160,512]{1,0:T(8,128)(2,1)S(1)}, bf16[160,512]{1,0:T(8,128)(2,1)S(1)}, u32[]{:S(2)}, u32[]{:S(2)}) %collective-permute-start.27) | collective-permute-done | bytes 163872 | tf_op jit(solution)/shard_map/ppermute | solution.py:247
  119.2 11.9 %attention.1 = (bf16[320,128]{1,0:T(8,128)(2,1)S(1)}, bf16[320,128]{1,0:T(8,128)(2,1)S(1)}, bf16[320,128]{1,0:T(8,128)(2,1)S(1)}, bf16[320,128]{1,0:T(8,128)(2,1)S(1)}, bf16[1280,128]{1,0:T(8,128)(2,1)S(1)}) custom-call(s32[20]{0:T(128)S(1)} %concatenate.9.place_ref, bf16[160,512]{1,0:T(8,128)(2,1)S(1)} %get-tuple-element.12.refs_0_, ...), custom_call_target="tpu_custom_call" | custom-call | flops 3187671040 | bytes 5079040 | tf_op jit(solution)/shard_map/attention/pallas_call | solution.py:365
  131.4 1.5 %collective-permute-start.31 = (bf16[320,128]{1,0:T(8,128)(2,1)S(1)}, bf16[320,128]{1,0:T(8,128)(2,1)S(1)}, u32[]{:S(2)}, u32[]{:S(2)}) collective-permute-start(bf16[320,128]{1,0:T(8,128)(2,1)S(1)} %get-tuple-element.16), channel_id=1, source_target_pairs={{0,4},{1,5},{2,6},{3,7},{4,0},{5,1},{6,2},{7,3},{8,12},{9,13},{10,... | collective-permute-start | bytes 245768 | tf_op jit(solution)/shard_map/ppermute | solution.py:392
  132.8 2.1 %collective-permute-start.32 = (bf16[320,128]{1,0:T(8,128)(2,1)S(1)}, bf16[320,128]{1,0:T(8,128)(2,1)S(1)}, u32[]{:S(2)}, u32[]{:S(2)}) collective-permute-start(bf16[320,128]{1,0:T(8,128)(2,1)S(1)} %get-tuple-element.17), channel_id=1, source_target_pairs={{0,6},{1,7},{2,0},{3,1},{4,2},{5,3},{6,4},{7,5},{8,14},{9,15},{10,... | collective-permute-start | bytes 245768 | tf_op jit(solution)/shard_map/ppermute | solution.py:392
  135.0 3.0 %collective-permute-done.30.refs_1_ = bf16[320,128]{1,0:T(8,128)(2,1)S(1)} collective-permute-done((bf16[320,128]{1,0:T(8,128)(2,1)S(1)}, bf16[320,128]{1,0:T(8,128)(2,1)S(1)}, u32[]{:S(2)}, u32[]{:S(2)}) %collective-permute-start.30) | collective-permute-done | bytes 81952 | tf_op jit(solution)/shard_map/ppermute | solution.py:392
  137.9 1.8 %collective-permute-done.31.refs_2_ = bf16[320,128]{1,0:T(8,128)(2,1)S(1)} collective-permute-done((bf16[320,128]{1,0:T(8,128)(2,1)S(1)}, bf16[320,128]{1,0:T(8,128)(2,1)S(1)}, u32[]{:S(2)}, u32[]{:S(2)}) %collective-permute-start.31) | collective-permute-done | bytes 81952 | tf_op jit(solution)/shard_map/ppermute | solution.py:392
  139.7 2.5 %project.1 = bf16[128,1280]{1,0:T(8,128)(2,1)} custom-call(s32[20]{0:T(128)S(1)} %concatenate.9.place_ref, bf16[320,128]{1,0:T(8,128)(2,1)S(1)} %get-tuple-element.14.refs_0_, bf16[320,128]{1,0:T(8,128)(2,1)S(1)} %collective-permute-done.30.refs_1_, bf16[320,128]{1,0:T(8,128)(2,1)S(1)} %collective-permute-done.31.refs_2_, ...), custom_call_target="tpu_custom_call" | custom-call | flops 419430400 | bytes 4259840 | tf_op jit(solution)/shard_map/project/pallas_call | solution.py:394
  (90 shorter events, 19.6 us)
Async XLA Ops:
  1.1 8.0 %collective-permute-start.3 = (bf16[64,1280]{1,0:T(8,128)(2,1)S(1)}, bf16[64,1280]{1,0:T(8,128)(2,1)S(1)}, u32[]{:S(2)}, u32[]{:S(2)}) collective-permute-start(bf16[64,1280]{1,0:T(8,128)(2,1)S(1)} %get-tuple-element.23.refs_1_), channel_id=1, source_target_pairs={{1,0},{3,1},{5,3},{7,5},{6,7},{4,6},{2,4},{0,2},{9,8},{11,9},{13,1... | collective-permute-start | bytes 491528 | tf_op jit(solution)/shard_map/ppermute | solution.py:247
  4.2 7.1 %collective-permute-start = (bf16[64,1280]{1,0:T(8,128)(2,1)S(1)}, bf16[64,1280]{1,0:T(8,128)(2,1)S(1)}, u32[]{:S(2)}, u32[]{:S(2)}) collective-permute-start(bf16[64,1280]{1,0:T(8,128)(2,1)S(1)} %get-tuple-element.24.refs_0_), channel_id=1, source_target_pairs={{0,1},{1,3},{3,5},{5,7},{7,6},{6,4},{4,2},{2,0},{8,9},{9,11},{11,1... | collective-permute-start | bytes 491528 | tf_op jit(solution)/shard_map/ppermute | solution.py:247
  4.2 8.5 %collective-permute-start.2 = (bf16[64,1280]{1,0:T(8,128)(2,1)S(1)}, bf16[64,1280]{1,0:T(8,128)(2,1)S(1)}, u32[]{:S(2)}, u32[]{:S(2)}) collective-permute-start(bf16[64,1280]{1,0:T(8,128)(2,1)S(1)} %get-tuple-element.24.refs_0_), channel_id=1, source_target_pairs={{1,0},{3,1},{5,3},{7,5},{6,7},{4,6},{2,4},{0,2},{9,8},{11,9},{13,1... | collective-permute-start | bytes 491528 | tf_op jit(solution)/shard_map/ppermute | solution.py:247
  6.2 8.6 %collective-permute-start.1 = (bf16[64,1280]{1,0:T(8,128)(2,1)S(1)}, bf16[64,1280]{1,0:T(8,128)(2,1)S(1)}, u32[]{:S(2)}, u32[]{:S(2)}) collective-permute-start(bf16[64,1280]{1,0:T(8,128)(2,1)S(1)} %get-tuple-element.23.refs_1_), channel_id=1, source_target_pairs={{0,1},{1,3},{3,5},{5,7},{7,6},{6,4},{4,2},{2,0},{8,9},{9,11},{11,1... | collective-permute-start | bytes 491528 | tf_op jit(solution)/shard_map/ppermute | solution.py:247
  9.1 7.2 %collective-permute-start.7 = (bf16[64,1280]{1,0:T(8,128)(2,1)S(1)}, bf16[64,1280]{1,0:T(8,128)(2,1)S(1)}, u32[]{:S(2)}, u32[]{:S(2)}) collective-permute-start(bf16[64,1280]{1,0:T(8,128)(2,1)S(1)} %collective-permute-done.3.refs_5_), channel_id=1, source_target_pairs={{1,0},{3,1},{5,3},{7,5},{6,7},{4,6},{2,4},{0,2},{9,8},{11,9},{13,1... | collective-permute-start | bytes 491528 | tf_op jit(solution)/shard_map/ppermute | solution.py:247
  11.3 7.1 %collective-permute-start.4 = (bf16[64,1280]{1,0:T(8,128)(2,1)S(1)}, bf16[64,1280]{1,0:T(8,128)(2,1)S(1)}, u32[]{:S(2)}, u32[]{:S(2)}) collective-permute-start(bf16[64,1280]{1,0:T(8,128)(2,1)S(1)} %collective-permute-done.refs_2_), channel_id=1, source_target_pairs={{0,1},{1,3},{3,5},{5,7},{7,6},{6,4},{4,2},{2,0},{8,9},{9,11},{11,1... | collective-permute-start | bytes 491528 | tf_op jit(solution)/shard_map/ppermute | solution.py:247
  12.6 7.2 %collective-permute-start.6 = (bf16[64,1280]{1,0:T(8,128)(2,1)S(1)}, bf16[64,1280]{1,0:T(8,128)(2,1)S(1)}, u32[]{:S(2)}, u32[]{:S(2)}) collective-permute-start(bf16[64,1280]{1,0:T(8,128)(2,1)S(1)} %collective-permute-done.2.refs_4_), channel_id=1, source_target_pairs={{1,0},{3,1},{5,3},{7,5},{6,7},{4,6},{2,4},{0,2},{9,8},{11,9},{13,1... | collective-permute-start | bytes 491528 | tf_op jit(solution)/shard_map/ppermute | solution.py:247
  14.8 7.1 %collective-permute-start.5 = (bf16[64,1280]{1,0:T(8,128)(2,1)S(1)}, bf16[64,1280]{1,0:T(8,128)(2,1)S(1)}, u32[]{:S(2)}, u32[]{:S(2)}) collective-permute-start(bf16[64,1280]{1,0:T(8,128)(2,1)S(1)} %collective-permute-done.1.refs_3_), channel_id=1, source_target_pairs={{0,1},{1,3},{3,5},{5,7},{7,6},{6,4},{4,2},{2,0},{8,9},{9,11},{11,1... | collective-permute-start | bytes 491528 | tf_op jit(solution)/shard_map/ppermute | solution.py:247
  16.3 7.1 %collective-permute-start.11 = (bf16[64,1280]{1,0:T(8,128)(2,1)S(1)}, bf16[64,1280]{1,0:T(8,128)(2,1)S(1)}, u32[]{:S(2)}, u32[]{:S(2)}) collective-permute-start(bf16[64,1280]{1,0:T(8,128)(2,1)S(1)} %collective-permute-done.7.refs_9_), channel_id=1, source_target_pairs={{1,0},{3,1},{5,3},{7,5},{6,7},{4,6},{2,4},{0,2},{9,8},{11,9},{13,1... | collective-permute-start | bytes 491528 | tf_op jit(solution)/shard_map/ppermute | solution.py:247
  18.4 7.1 %collective-permute-start.8 = (bf16[64,1280]{1,0:T(8,128)(2,1)S(1)}, bf16[64,1280]{1,0:T(8,128)(2,1)S(1)}, u32[]{:S(2)}, u32[]{:S(2)}) collective-permute-start(bf16[64,1280]{1,0:T(8,128)(2,1)S(1)} %collective-permute-done.4.refs_6_), channel_id=1, source_target_pairs={{0,1},{1,3},{3,5},{5,7},{7,6},{6,4},{4,2},{2,0},{8,9},{9,11},{11,1... | collective-permute-start | bytes 491528 | tf_op jit(solution)/shard_map/ppermute | solution.py:247
  19.8 7.1 %collective-permute-start.10 = (bf16[64,1280]{1,0:T(8,128)(2,1)S(1)}, bf16[64,1280]{1,0:T(8,128)(2,1)S(1)}, u32[]{:S(2)}, u32[]{:S(2)}) collective-permute-start(bf16[64,1280]{1,0:T(8,128)(2,1)S(1)} %collective-permute-done.6.refs_8_), channel_id=1, source_target_pairs={{1,0},{3,1},{5,3},{7,5},{6,7},{4,6},{2,4},{0,2},{9,8},{11,9},{13,1... | collective-permute-start | bytes 491528 | tf_op jit(solution)/shard_map/ppermute | solution.py:247
  21.9 7.1 %collective-permute-start.9 = (bf16[64,1280]{1,0:T(8,128)(2,1)S(1)}, bf16[64,1280]{1,0:T(8,128)(2,1)S(1)}, u32[]{:S(2)}, u32[]{:S(2)}) collective-permute-start(bf16[64,1280]{1,0:T(8,128)(2,1)S(1)} %collective-permute-done.5.refs_7_), channel_id=1, source_target_pairs={{0,1},{1,3},{3,5},{5,7},{7,6},{6,4},{4,2},{2,0},{8,9},{9,11},{11,1... | collective-permute-start | bytes 491528 | tf_op jit(solution)/shard_map/ppermute | solution.py:247
  23.4 5.9 %collective-permute-start.13 = (bf16[64,1280]{1,0:T(8,128)(2,1)S(1)}, bf16[64,1280]{1,0:T(8,128)(2,1)S(1)}, u32[]{:S(2)}, u32[]{:S(2)}) collective-permute-start(bf16[64,1280]{1,0:T(8,128)(2,1)S(1)} %collective-permute-done.11.refs_13_.refs_3_), channel_id=1, source_target_pairs={{1,0},{3,1},{5,3},{7,5},{6,7},{4,6},{2,4},{0,2},{9,8},{11,9},{13,1... | collective-permute-start | bytes 491528 | tf_op jit(solution)/shard_map/ppermute | solution.py:247
  31.6 23.6 %collective-permute-start.28 = (bf16[240,1280]{1,0:T(8,128)(2,1)}, bf16[240,1280]{1,0:T(8,128)(2,1)}, u32[]{:S(2)}, u32[]{:S(2)}) collective-permute-start(bf16[240,1280]{1,0:T(8,128)(2,1)} %after.3), channel_id=1, source_target_pairs={{0,1},{1,0},{2,3},{3,2},{4,5},{5,4},{6,7},{7,6},{8,9},{9,8},{10,11... | collective-permute-start | bytes 1843208 | tf_op jit(solution)/shard_map/ppermute | solution.py:260
  55.8 42.7 %collective-permute-start.29 = (bf16[240,1280]{1,0:T(8,128)(2,1)}, bf16[240,1280]{1,0:T(8,128)(2,1)S(1)}, u32[]{:S(2)}, u32[]{:S(2)}) collective-permute-start(bf16[240,1280]{1,0:T(8,128)(2,1)} %after.4), channel_id=1, source_target_pairs={{0,8},{8,0},{16,24},{24,16},{1,9},{9,1},{17,25},{25,17},{2,10},{10... | collective-permute-start | bytes 1843208 | tf_op jit(solution)/shard_map/ppermute | solution.py:268
  56.5 40.0 %collective-permute-start.14 = (bf16[160,512]{1,0:T(8,128)(2,1)S(1)}, bf16[160,512]{1,0:T(8,128)(2,1)S(1)}, u32[]{:S(2)}, u32[]{:S(2)}) collective-permute-start(bf16[160,512]{1,0:T(8,128)(2,1)S(1)} %get-tuple-element.12.refs_0_), channel_id=1, source_target_pairs={{0,1},{1,3},{3,5},{5,7},{7,6},{6,4},{4,2},{2,0},{8,9},{9,11},{11,1... | collective-permute-start | bytes 491528 | tf_op jit(solution)/shard_map/ppermute | solution.py:247
  57.6 38.8 %collective-permute-start.17 = (bf16[160,512]{1,0:T(8,128)(2,1)S(1)}, bf16[160,512]{1,0:T(8,128)(2,1)S(1)}, u32[]{:S(2)}, u32[]{:S(2)}) collective-permute-start(bf16[160,512]{1,0:T(8,128)(2,1)S(1)} %get-tuple-element.13.refs_1_), channel_id=1, source_target_pairs={{1,0},{3,1},{5,3},{7,5},{6,7},{4,6},{2,4},{0,2},{9,8},{11,9},{13,1... | collective-permute-start | bytes 491528 | tf_op jit(solution)/shard_map/ppermute | solution.py:247
  58.5 40.0 %collective-permute-start.15 = (bf16[160,512]{1,0:T(8,128)(2,1)S(1)}, bf16[160,512]{1,0:T(8,128)(2,1)S(1)}, u32[]{:S(2)}, u32[]{:S(2)}) collective-permute-start(bf16[160,512]{1,0:T(8,128)(2,1)S(1)} %get-tuple-element.13.refs_1_), channel_id=1, source_target_pairs={{0,1},{1,3},{3,5},{5,7},{7,6},{6,4},{4,2},{2,0},{8,9},{9,11},{11,1... | collective-permute-start | bytes 491528 | tf_op jit(solution)/shard_map/ppermute | solution.py:247
  94.9 13.9 %collective-permute-start.34 = (bf16[320,1280]{1,0:T(8,128)(2,1)S(1)}, bf16[320,1280]{1,0:T(8,128)(2,1)S(1)}, u32[]{:S(2)}, u32[]{:S(2)}) collective-permute-start(bf16[320,1280]{1,0:T(8,128)(2,1)S(1)} %all_gather.3.refs_5_), channel_id=1, source_target_pairs={{0,16},{8,24},{16,0},{24,8},{1,17},{9,25},{17,1},{25,9},{2,18},{10... | collective-permute-start | bytes 2457608 | tf_op jit(solution)/shard_map/ppermute | solution.py:288
  96.5 9.4 %collective-permute-start.20 = (bf16[160,512]{1,0:T(8,128)(2,1)S(1)}, bf16[160,512]{1,0:T(8,128)(2,1)S(1)}, u32[]{:S(2)}, u32[]{:S(2)}) collective-permute-start(bf16[160,512]{1,0:T(8,128)(2,1)S(1)} %copy-done.12), channel_id=1, source_target_pairs={{1,0},{3,1},{5,3},{7,5},{6,7},{4,6},{2,4},{0,2},{9,8},{11,9},{13,1... | collective-permute-start | bytes 491528 | tf_op jit(solution)/shard_map/ppermute | solution.py:247
  96.5 5.4 %collective-permute-start.18 = (bf16[160,512]{1,0:T(8,128)(2,1)S(1)}, bf16[160,512]{1,0:T(8,128)(2,1)S(1)}, u32[]{:S(2)}, u32[]{:S(2)}) collective-permute-start(bf16[160,512]{1,0:T(8,128)(2,1)S(1)} %collective-permute-done.14.refs_2_), channel_id=1, source_target_pairs={{0,1},{1,3},{3,5},{5,7},{7,6},{6,4},{4,2},{2,0},{8,9},{9,11},{11,1... | collective-permute-start | bytes 491528 | tf_op jit(solution)/shard_map/ppermute | solution.py:247
  101.9 33.1 %collective-permute-start.33 = (bf16[320,1280]{1,0:T(8,128)(2,1)S(1)}, bf16[320,1280]{1,0:T(8,128)(2,1)S(1)}, u32[]{:S(2)}, u32[]{:S(2)}) collective-permute-start(bf16[320,1280]{1,0:T(8,128)(2,1)S(1)} %all_gather.3.refs_5_), channel_id=1, source_target_pairs={{0,8},{8,0},{16,24},{24,16},{1,9},{9,1},{17,25},{25,17},{2,10},{10... | collective-permute-start | bytes 2457608 | tf_op jit(solution)/shard_map/ppermute | solution.py:288
  103.8 6.5 %collective-permute-start.22 = (bf16[160,512]{1,0:T(8,128)(2,1)S(1)}, bf16[160,512]{1,0:T(8,128)(2,1)S(1)}, u32[]{:S(2)}, u32[]{:S(2)}) collective-permute-start(bf16[160,512]{1,0:T(8,128)(2,1)S(1)} %collective-permute-done.18.refs_6_), channel_id=1, source_target_pairs={{0,1},{1,3},{3,5},{5,7},{7,6},{6,4},{4,2},{2,0},{8,9},{9,11},{11,1... | collective-permute-start | bytes 491528 | tf_op jit(solution)/shard_map/ppermute | solution.py:247
  103.9 6.5 %collective-permute-start.25 = (bf16[160,512]{1,0:T(8,128)(2,1)S(1)}, bf16[160,512]{1,0:T(8,128)(2,1)S(1)}, u32[]{:S(2)}, u32[]{:S(2)}) collective-permute-start(bf16[160,512]{1,0:T(8,128)(2,1)S(1)} %collective-permute-done.21.refs_9_), channel_id=1, source_target_pairs={{1,0},{3,1},{5,3},{7,5},{6,7},{4,6},{2,4},{0,2},{9,8},{11,9},{13,1... | collective-permute-start | bytes 491528 | tf_op jit(solution)/shard_map/ppermute | solution.py:247
  105.9 6.5 %collective-permute-start.23 = (bf16[160,512]{1,0:T(8,128)(2,1)S(1)}, bf16[160,512]{1,0:T(8,128)(2,1)S(1)}, u32[]{:S(2)}, u32[]{:S(2)}) collective-permute-start(bf16[160,512]{1,0:T(8,128)(2,1)S(1)} %collective-permute-done.19.refs_7_), channel_id=1, source_target_pairs={{0,1},{1,3},{3,5},{5,7},{7,6},{6,4},{4,2},{2,0},{8,9},{9,11},{11,1... | collective-permute-start | bytes 491528 | tf_op jit(solution)/shard_map/ppermute | solution.py:247
  108.7 31.0 %collective-permute-start.35 = (bf16[320,1280]{1,0:T(8,128)(2,1)S(1)}, bf16[320,1280]{1,0:T(8,128)(2,1)S(1)}, u32[]{:S(2)}, u32[]{:S(2)}) collective-permute-start(bf16[320,1280]{1,0:T(8,128)(2,1)S(1)} %collective-permute-done.34.refs_7_), channel_id=1, source_target_pairs={{0,8},{8,0},{16,24},{24,16},{1,9},{9,1},{17,25},{25,17},{2,10},{10... | collective-permute-start | bytes 2457608 | tf_op jit(solution)/shard_map/ppermute | solution.py:288
  110.4 6.6 %collective-permute-start.24 = (bf16[160,512]{1,0:T(8,128)(2,1)S(1)}, bf16[160,512]{1,0:T(8,128)(2,1)S(1)}, u32[]{:S(2)}, u32[]{:S(2)}) collective-permute-start(bf16[160,512]{1,0:T(8,128)(2,1)S(1)} %collective-permute-done.20.refs_8_), channel_id=1, source_target_pairs={{1,0},{3,1},{5,3},{7,5},{6,7},{4,6},{2,4},{0,2},{9,8},{11,9},{13,1... | collective-permute-start | bytes 491528 | tf_op jit(solution)/shard_map/ppermute | solution.py:247
  110.4 6.5 %collective-permute-start.26 = (bf16[160,512]{1,0:T(8,128)(2,1)S(1)}, bf16[160,512]{1,0:T(8,128)(2,1)S(1)}, u32[]{:S(2)}, u32[]{:S(2)}) collective-permute-start(bf16[160,512]{1,0:T(8,128)(2,1)S(1)} %collective-permute-done.22.refs_10_), channel_id=1, source_target_pairs={{0,1},{1,3},{3,5},{5,7},{7,6},{6,4},{4,2},{2,0},{8,9},{9,11},{11,1... | collective-permute-start | bytes 491528 | tf_op jit(solution)/shard_map/ppermute | solution.py:247
  112.4 6.8 %collective-permute-start.27 = (bf16[160,512]{1,0:T(8,128)(2,1)S(1)}, bf16[160,512]{1,0:T(8,128)(2,1)S(1)}, u32[]{:S(2)}, u32[]{:S(2)}) collective-permute-start(bf16[160,512]{1,0:T(8,128)(2,1)S(1)} %collective-permute-done.25.refs_13_), channel_id=1, source_target_pairs={{1,0},{3,1},{5,3},{7,5},{6,7},{4,6},{2,4},{0,2},{9,8},{11,9},{13,1... | collective-permute-start | bytes 491528 | tf_op jit(solution)/shard_map/ppermute | solution.py:247
  131.1 6.9 %collective-permute-start.30 = (bf16[320,128]{1,0:T(8,128)(2,1)S(1)}, bf16[320,128]{1,0:T(8,128)(2,1)S(1)}, u32[]{:S(2)}, u32[]{:S(2)}) collective-permute-start(bf16[320,128]{1,0:T(8,128)(2,1)S(1)} %get-tuple-element.15), channel_id=1, source_target_pairs={{0,2},{1,3},{2,4},{3,5},{4,6},{5,7},{6,0},{7,1},{8,10},{9,11},{10,... | collective-permute-start | bytes 245768 | tf_op jit(solution)/shard_map/ppermute | solution.py:392
  131.4 8.3 %collective-permute-start.31 = (bf16[320,128]{1,0:T(8,128)(2,1)S(1)}, bf16[320,128]{1,0:T(8,128)(2,1)S(1)}, u32[]{:S(2)}, u32[]{:S(2)}) collective-permute-start(bf16[320,128]{1,0:T(8,128)(2,1)S(1)} %get-tuple-element.16), channel_id=1, source_target_pairs={{0,4},{1,5},{2,6},{3,7},{4,0},{5,1},{6,2},{7,3},{8,12},{9,13},{10,... | collective-permute-start | bytes 245768 | tf_op jit(solution)/shard_map/ppermute | solution.py:392
  132.8 6.9 %collective-permute-start.32 = (bf16[320,128]{1,0:T(8,128)(2,1)S(1)}, bf16[320,128]{1,0:T(8,128)(2,1)S(1)}, u32[]{:S(2)}, u32[]{:S(2)}) collective-permute-start(bf16[320,128]{1,0:T(8,128)(2,1)S(1)} %get-tuple-element.17), channel_id=1, source_target_pairs={{0,6},{1,7},{2,0},{3,1},{4,2},{5,3},{6,4},{7,5},{8,14},{9,15},{10,... | collective-permute-start | bytes 245768 | tf_op jit(solution)/shard_map/ppermute | solution.py:392
  (20 other events, 159.3 us)

commit v3 on v2

--- a/solution.py
+++ b/solution.py
@@ -15,7 +15,8 @@
 OUTER = 4
 SET_HEADS = HEADS // OUTER
 SET_CHANNELS = SET_HEADS * HEAD_DIM
-FIXED = 4
+FIXED = 5
+GRANULE = 32
 EPSILON = 1e-05
 VMEM_LIMIT = 48 * 1024 * 1024
 
@@ -35,11 +36,13 @@
 
 
 def conv_kernel(columns, place_ref, *refs):
-    count = len(refs) - 6
+    count = len(refs) - 8
     pieces = refs[:count]
-    kernel_ref, bias_ref = refs[count : count + 2]
+    source_ref, bias_ref = refs[count : count + 2]
     out_refs = refs[count + 2 : count + 4]
-    act_ref, kept_ref = refs[count + 4 :]
+    act_ref, kept_ref, kernel_ref, sem = refs[count + 4 :]
+    load = pltpu.make_async_copy(source_ref, kernel_ref, sem)
+    load.start()
     block = pieces[0].shape[0]
     positions = block * count
     own = out_refs[0].shape[0]
@@ -101,6 +104,7 @@
         start = pl.multiple_of(starts[index], 2 * block)
         kept_ref[:, pl.ds(start, 2 * block)] = dot(choose, pair, NT)
 
+    load.wait()
     wide = 256
     column = lax.broadcasted_iota(jnp.int32, (own, wide), 1) % columns
     bias = bias_ref[...]
@@ -117,13 +121,11 @@
         out_refs[which][:, low : low + wide] = hidden.astype(bf16)
 
 
-def attention_kernel(inner, place_ref, *refs):
-    count = len(refs) - 8 - OUTER
+def attention_kernel(count, inner, place_ref, *refs):
     pieces = refs[:count]
-    weight_ref = refs[count]
-    outs = refs[count + 1 : count + 1 + OUTER]
-    kept_ref = refs[count + 1 + OUTER]
-    hidden_ref, normed_ref, query_ref, key_ref, value_ref, sems = refs[count + 2 + OUTER :]
+    parts = refs[count : -8 - OUTER]
+    outs = refs[-8 - OUTER : -8]
+    kept_ref, hidden_ref, normed_ref, weight_ref, query_ref, key_ref, value_ref, sems = refs[-8:]
     own, part = pieces[0].shape
     n = count // 2
     positions = 2 * part
@@ -139,6 +141,30 @@
         copy = pltpu.make_async_copy(piece, target, sems.at[index])
         copy.start()
         copies.append(copy)
+    loads = []
+
+    def load(source, row):
+        loads.append(pltpu.make_async_copy(source, weight_ref.at[pl.ds(row, source.shape[0]), :], sems.at[count]))
+        loads[-1].start()
+
+    if inner == 2:
+        for kind in range(3):
+            row = kind * SET_CHANNELS + inner_at * own
+            load(parts[kind], pl.multiple_of(row, GRANULE))
+        quarters = quarter_starts(3 * own)
+        for step, part_ref in enumerate(parts[3:]):
+            which = jnp.bitwise_xor(place_ref[4], step)
+            first = jnp.int32(quarters[0])
+            for at in range(1, 4):
+                first = jnp.where(which == at, quarters[at], first)
+            for at in range(part_ref.shape[0] // GRANULE):
+                granule = first + at
+                kind = lax.div(granule, own // GRANULE)
+                row = kind * SET_CHANNELS + (1 - inner_at) * own
+                row = row + lax.rem(granule, own // GRANULE) * GRANULE
+                load(part_ref.at[at * GRANULE : (at + 1) * GRANULE, :], pl.multiple_of(row, GRANULE))
+    else:
+        load(parts[0], 0)
     for copy in copies:
         copy.wait()
 
@@ -155,6 +181,8 @@
             scaled.append(away * lax.rsqrt(var + EPSILON))
         normed_ref[at : at + 2 * SPAN, :] = jnp.concatenate(scaled, axis=0).astype(bf16)
 
+    for copy in loads:
+        copy.wait()
     wide = 256
     for at in range(0, positions, wide):
         made = dot(weight_ref[SET_CHANNELS:, :], normed_ref[:, at : at + wide])
@@ -186,12 +214,12 @@
             outs[at + 1][low : low + HEAD_DIM, :] = attended[:, block:]
 
 
-def output_kernel(n, splits, place_ref, *refs):
+def output_kernel(n, place_ref, *refs):
     attended_refs = refs[:OUTER]
     hidden_ref = refs[OUTER]
-    weight_refs = refs[OUTER + 1 : OUTER + 1 + splits]
-    out_ref, attended_ref, total_ref = refs[OUTER + 1 + splits :]
-    outer_at, mine = place_ref[1], place_ref[3]
+    weight_refs = refs[OUTER + 1 : OUTER + 3]
+    out_ref, attended_ref, total_ref = refs[OUTER + 3 :]
+    outer_at, core = place_ref[1], place_ref[3]
     for step in range(OUTER):
         origin = lax.rem(outer_at + OUTER - step, OUTER)
         row = pl.multiple_of(origin * SET_CHANNELS, SET_CHANNELS)
@@ -199,9 +227,8 @@
     total_ref[...] = hidden_ref[...].astype(f32)
     attended = attended_ref[...]
     own = C // n
-    part = own // splits
-    for step, weight_ref in enumerate(weight_refs):
-        which = jnp.bitwise_xor(mine, step)
+    part = own // 2
+    for which, weight_ref in zip((core, 1 - core), weight_refs):
         made = dot(weight_ref[...], attended)
         for origin in range(n):
             row = pl.multiple_of(origin * own + which * part, 8)
@@ -251,58 +278,47 @@
     return [found[half, away] for away in pieces_of(n) for half in (0, 1)]
 
 
-def swap_weights(weights, core, n, ready):
-    if n // OUTER != 2:
-        return None
-    rows = weights.reshape(-1, C)
-    part = rows.shape[0] // 2
-    own_half = after(lax.dynamic_slice_in_dim(rows, core * part, part, 0), *ready)
-    return lax.ppermute(own_half, "patch", [(at, at ^ 1) for at in range(n)])
-
-
-def set_weights(weights, first, inner_at, core, n, ready):
-    inner = n // OUTER
-    if inner == 2:
-        first = after(first, ready)
-        cores = [(at, at ^ 1) for at in range(lax.axis_size("batch"))]
-        second = lax.ppermute(first, "batch", cores)
-        low = jnp.where(core == 0, first, second)
-        high = jnp.where(core == 0, second, first)
-        other = jnp.concatenate([low, high], axis=0).reshape(weights.shape)
-        return jnp.concatenate(
-            [jnp.where(inner_at == 0, weights, other), jnp.where(inner_at == 0, other, weights)],
-            axis=1,
-        )
-    sets = [list(range(at, at + inner)) for at in range(0, n, inner)]
-    return lax.all_gather(weights, "patch", axis=1, tiled=True, axis_index_groups=sets)
-
-
-def output_weights(w_out, mine, splits, ready):
-    part = w_out.shape[0] // splits
-    shard = after(lax.dynamic_slice_in_dim(w_out, mine * part, part, 0), *ready)
-    parts = [lax.all_gather(shard, "patch", axis=0, tiled=True)]
+def swap_weights(weights, core, side, n, ready):
+    rows = jnp.concatenate(weights, axis=0)
+    quarters = jnp.asarray(quarter_starts(rows.shape[0]), jnp.int32)
+    start = lax.dynamic_index_in_dim(quarters, 2 * core + side, 0, keepdims=False) * GRANULE
+    own_part = after(lax.dynamic_slice_in_dim(rows, start, quarter_rows(rows.shape[0]), 0), *ready)
+    return lax.ppermute(own_part, "patch", [(at, at ^ 1) for at in range(n)])
+
+
+def spread_weights(first, ready):
     batch = lax.axis_size("batch")
-    step = splits // 2
-    while step:
-        swap = [(at, at ^ step) for at in range(batch)]
-        parts = parts + [lax.ppermute(one, "batch", swap) for one in parts]
-        step //= 2
-    order = [0]
-    step = splits // 2
-    while step:
-        order = order + [one ^ step for one in order]
-        step //= 2
-    return [parts[order.index(at)] for at in range(splits)]
+    across, cores = ([(at, at ^ bit) for at in range(batch)] for bit in (2, 1))
+    first = after(first, *ready)
+    second = lax.ppermute(first, "batch", across)
+    return [first, second] + [lax.ppermute(one, "batch", cores) for one in (first, second)]
+
+
+def quarter_rows(rows):
+    return -(-rows // (4 * GRANULE)) * GRANULE
+
+
+def quarter_starts(rows):
+    part = quarter_rows(rows)
+    return [min(at * part, rows - part) // GRANULE for at in range(4)]
+
+
+def output_weights(w_out, core, ready):
+    part = w_out.shape[0] // 2
+    shard = after(lax.dynamic_slice_in_dim(w_out, core * part, part, 0), *ready)
+    return lax.all_gather(shard, "patch", axis=0, tiled=True)
 
 
 def after(value, *ready):
     anywhere = pl.BlockSpec(memory_space=pl.ANY)
+    vmem = pl.BlockSpec(memory_space=pltpu.VMEM)
     return pl.pallas_call(
         lambda *refs: None,
         out_shape=jax.ShapeDtypeStruct(value.shape, value.dtype),
-        in_specs=[anywhere] * (1 + len(ready)),
+        in_specs=[anywhere] + [vmem] * len(ready),
         out_specs=anywhere,
         input_output_aliases={0: 0},
+        cost_estimate=pl.CostEstimate(flops=0, bytes_accessed=0, transcendentals=0),
         name="after",
     )(value, *ready)
 
@@ -314,12 +330,13 @@
     own = channels // n
     block = rows_local * columns
     positions = block * n
-    splits = 4 if own % 32 == 0 else 2
     me = lax.axis_index("patch")
     batch_at = lax.axis_index("batch")
     inner_at = lax.rem(me, inner)
-    mine = lax.rem(batch_at, splits)
-    fixed = jnp.stack([me, lax.div(me, inner), inner_at, mine]).astype(jnp.int32)
+    core = lax.rem(batch_at, 2)
+    side = lax.rem(lax.div(batch_at, 2), 2)
+    fixed = jnp.stack([me, lax.div(me, inner), inner_at, core, 2 * core + side])
+    fixed = fixed.astype(jnp.int32)
     sources = jnp.asarray(sources_of(n), jnp.int32)
     place = jnp.concatenate([fixed, lax.dynamic_index_in_dim(sources, me, 0, keepdims=False)])
     vmem = pl.BlockSpec(memory_space=pltpu.VMEM)
@@ -330,19 +347,25 @@
     whole = latent.reshape(block, channels)
     pieces = gather((whole[: block // 2], whole[block // 2 :]), n)
 
-    weights = jnp.stack([w_query, w_key, w_value])
-    core = lax.rem(batch_at, 2)
-    first = swap_weights(weights, core, n, pieces[-5:])
-    out_parts = output_weights(w_out, mine, splits, pieces[-5:])
+    if inner == 2:
+        first = swap_weights((w_query, w_key, w_value), core, side, n, pieces[-5:])
+    else:
+        sets = [list(range(at, at + inner)) for at in range(0, n, inner)]
+        weights = jnp.stack([w_query, w_key, w_value])
+        weights = lax.all_gather(weights, "patch", axis=1, tiled=True, axis_index_groups=sets)
+        weights = [weights.reshape(3 * SET_CHANNELS, channels)]
+    out_half = output_weights(w_out, core, pieces[-5:])
 
     hidden = pl.pallas_call(
         functools.partial(conv_kernel, columns),
         out_shape=[jax.ShapeDtypeStruct((own, positions // 2), bf16)] * 2,
-        in_specs=[smem] + [vmem] * (2 * n + 2),
+        in_specs=[smem] + [vmem] * (2 * n) + [anywhere, vmem],
         out_specs=[vmem] * 2,
         scratch_shapes=[
             pltpu.VMEM((positions + 2 * columns, channels), bf16),
             pltpu.VMEM((own, positions), f32),
+            pltpu.VMEM((3, 3 * own, channels), bf16),
+            pltpu.SemaphoreType.DMA,
         ],
         compiler_params=params,
         cost_estimate=pl.CostEstimate(
@@ -359,22 +382,26 @@
     )
 
     hidden_pieces = gather(tuple(hidden), n)
-    weights = set_weights(weights, first, inner_at, core, n, hidden_pieces[4])
-    weights = weights.reshape(3 * SET_CHANNELS, channels)
+    if inner == 2:
+        weights = [w_query, w_key, w_value] + spread_weights(first, hidden[:1])
+    out_half = after(out_half, *hidden_pieces[-5:], *weights[3:])
+    cores = [(at, at ^ 1) for at in range(lax.axis_size("batch"))]
+    out_other = lax.ppermute(out_half, "batch", cores)
 
     *attended, kept = pl.pallas_call(
-        functools.partial(attention_kernel, inner),
+        functools.partial(attention_kernel, 2 * n, inner),
         out_shape=[jax.ShapeDtypeStruct((SET_CHANNELS, block), bf16)] * OUTER
         + [jax.ShapeDtypeStruct((channels, block), bf16)],
-        in_specs=[smem] + [anywhere] * (2 * n) + [vmem],
+        in_specs=[smem] + [anywhere] * (2 * n + len(weights)),
         out_specs=[vmem] * (OUTER + 1),
         scratch_shapes=[
             pltpu.VMEM((channels, positions), bf16),
             pltpu.VMEM((channels, positions), bf16),
+            pltpu.VMEM((3 * SET_CHANNELS, channels), bf16),
             pltpu.VMEM((SET_CHANNELS, OUTER * block), bf16),
             pltpu.VMEM((SET_HEADS, positions, HEAD_DIM), bf16),
             pltpu.VMEM((SET_CHANNELS, positions), bf16),
-            pltpu.SemaphoreType.DMA((2 * n,)),
+            pltpu.SemaphoreType.DMA((2 * n + 1,)),
         ],
         compiler_params=params,
         cost_estimate=pl.CostEstimate(
@@ -384,7 +411,7 @@
             transcendentals=positions * OUTER * block * SET_HEADS,
         ),
         name="attention",
-    )(place, *hidden_pieces, weights)
+    )(place, *hidden_pieces, *weights)
 
     received = [attended[0]]
     for step in range(1, OUTER):
@@ -392,9 +419,9 @@
         received.append(lax.ppermute(attended[step], "patch", pairs))
 
     output = pl.pallas_call(
-        functools.partial(output_kernel, n, splits),
+        functools.partial(output_kernel, n),
         out_shape=jax.ShapeDtypeStruct((block, channels), bf16),
-        in_specs=[smem] + [vmem] * (OUTER + 1 + splits),
+        in_specs=[smem] + [vmem] * (OUTER + 3),
         out_specs=vmem,
         scratch_shapes=[
             pltpu.VMEM((channels, block), bf16),
@@ -407,7 +434,7 @@
             transcendentals=0,
         ),
         name="project",
-    )(place, *received, kept, *out_parts)
+    )(place, *received, kept, out_half, out_other)
     return output.reshape(rows_local, columns, channels)
 
 

time: 143 us -> 163 us (1.14)
  blocking collectives: 35.2 us -> 0 us
  local copies, waits for them, and re-layouts: 10.1 us -> 40.1 us
  between operations: 0.2 us -> 14.3 us
  Pallas kernels: 26.4 us -> 34 us
  waiting for transfers between devices: 32.2 us -> 37.6 us
  other arithmetic: 3.06 us -> 1.11 us
    all_gather x1 -> x0, blocking collectives: 35.2 us -> none  [output_weights(): parts = [lax.all_gather(shard, 'patch', axis=0, tiled=True)]]
    unnamed x32 -> x142, local copies, waits for them, and re-layouts: 5.94 us -> 36.8 us
    ppermute x28, waiting for transfers between devices: 24.6 us -> 31.9 us  [gather(): lax.ppermute(found[half, sign * (step - 1)], 'patch', pairs)]
    pallas_call x3 -> x4, Pallas kernels: 0.01 us -> 4.97 us  [after(): pl.pallas_call(lambda *refs: None, out_shape=jax.ShapeDtypeStruct(value.s...]
    pallas_call x2, Pallas kernels: 14.4 us -> 17.4 us  [the longest x1 14.9 us: on_device(): pl.pallas_call(functools.partial(attention_kernel, 2 * n, inner), out_sha...]
    ppermute x5, waiting for transfers between devices: 2.81 us -> 0.01 us  [the longest x2 0.01 us: spread_weights(): lax.ppermute(one, 'batch', cores)]
  transfers between devices with their start and end apart: 36 -> 37, of which waited for: 16 -> 19; matrix products, arithmetic and copies ran while one was open for 4% -> 2% of each run, Pallas kernels for 17% -> 18%
where the time goes in v3:
time: 163 us; the launch traced here: 162 us
  local copies, waits for them, and re-layouts  40.1 us (25%)
  waiting for transfers between devices  37.6 us (23%)
  starting transfers between devices  35.2 us (22%)
  Pallas kernels  34 us (21%)
  between operations  14.3 us (9%)
    unnamed x142, local copies, waits for them, and re-layouts  36.8 us
    ppermute x28, waiting for transfers between devices, gather(): lax.ppermute(found[half, sign * (step - 1)], 'patch', pairs)  31.9 us
    ppermute x28, starting transfers between devices, gather(): lax.ppermute(found[half, sign * (step - 1)], 'patch', pairs)  27.1 us
    pallas_call x1, Pallas kernels, on_device(): pl.pallas_call(functools.partial(attention_kernel, 2 * n, inner), out_sha...  14.9 us
    pallas_call x1, Pallas kernels, on_device(): pl.pallas_call(functools.partial(conv_kernel, columns), out_shape=[jax.Sh...  11.7 us
    ppermute x3, waiting for transfers between devices, on_device(): received.append(lax.ppermute(attended[step], 'patch', pairs))  5.71 us
    pallas_call x4, Pallas kernels, after(): pl.pallas_call(lambda *refs: None, out_shape=jax.ShapeDtypeStruct(value.s...  4.97 us
    ppermute x3, starting transfers between devices, on_device(): received.append(lax.ppermute(attended[step], 'patch', pairs))  4.45 us
  transfers between devices with their start and end apart: 37, of which 19 were waited for; matrix products, arithmetic and copies ran while one was open for 2% of the time, Pallas kernels for 18%

profile of v3, /device:TPU:0, one launch (start us, length us, event | category | flops | bytes accessed | tf_op | source)
XLA Modules:
  0.0 162.5 jit_solution(7234307827312257593)
XLA Ops:
  7.7 3.0 %collective-permute-start = (bf16[64,1280]{1,0:T(8,128)(2,1)S(1)}, bf16[64,1280]{1,0:T(8,128)(2,1)S(1)}, u32[]{:S(2)}, u32[]{:S(2)}) collective-permute-start(bf16[64,1280]{1,0:T(8,128)(2,1)S(1)} %get-tuple-element.20.refs_0_), channel_id=1, source_target_pairs={{0,1},{1,3},{3,5},{5,7},{7,6},{6,4},{4,2},{2,0},{8,9},{9,11},{11,1... | collective-permute-start | bytes 491528 | tf_op jit(solution)/shard_map/ppermute | solution.py:274
  10.9 1.9 %collective-permute-start.1 = (bf16[64,1280]{1,0:T(8,128)(2,1)S(1)}, bf16[64,1280]{1,0:T(8,128)(2,1)S(1)}, u32[]{:S(2)}, u32[]{:S(2)}) collective-permute-start(bf16[64,1280]{1,0:T(8,128)(2,1)S(1)} %get-tuple-element.19.refs_1_), channel_id=1, source_target_pairs={{0,1},{1,3},{3,5},{5,7},{7,6},{6,4},{4,2},{2,0},{8,9},{9,11},{11,1... | collective-permute-start | bytes 491528 | tf_op jit(solution)/shard_map/ppermute | solution.py:274
  12.9 2.9 %collective-permute-done.refs_2_ = bf16[64,1280]{1,0:T(8,128)(2,1)S(1)} collective-permute-done((bf16[64,1280]{1,0:T(8,128)(2,1)S(1)}, bf16[64,1280]{1,0:T(8,128)(2,1)S(1)}, u32[]{:S(2)}, u32[]{:S(2)}) %collective-permute-start) | collective-permute-done | bytes 163872 | tf_op jit(solution)/shard_map/ppermute | solution.py:274
  15.8 2.0 %collective-permute-start.4 = (bf16[64,1280]{1,0:T(8,128)(2,1)S(1)}, bf16[64,1280]{1,0:T(8,128)(2,1)S(1)}, u32[]{:S(2)}, u32[]{:S(2)}) collective-permute-start(bf16[64,1280]{1,0:T(8,128)(2,1)S(1)} %collective-permute-done.refs_2_), channel_id=1, source_target_pairs={{0,1},{1,3},{3,5},{5,7},{7,6},{6,4},{4,2},{2,0},{8,9},{9,11},{11,1... | collective-permute-start | bytes 491528 | tf_op jit(solution)/shard_map/ppermute | solution.py:274
  19.4 2.0 %collective-permute-start.5 = (bf16[64,1280]{1,0:T(8,128)(2,1)S(1)}, bf16[64,1280]{1,0:T(8,128)(2,1)S(1)}, u32[]{:S(2)}, u32[]{:S(2)}) collective-permute-start(bf16[64,1280]{1,0:T(8,128)(2,1)S(1)} %collective-permute-done.1.refs_3_), channel_id=1, source_target_pairs={{0,1},{1,3},{3,5},{5,7},{7,6},{6,4},{4,2},{2,0},{8,9},{9,11},{11,1... | collective-permute-start | bytes 491528 | tf_op jit(solution)/shard_map/ppermute | solution.py:274
  23.0 2.0 %collective-permute-start.8 = (bf16[64,1280]{1,0:T(8,128)(2,1)S(1)}, bf16[64,1280]{1,0:T(8,128)(2,1)}, u32[]{:S(2)}, u32[]{:S(2)}) collective-permute-start(bf16[64,1280]{1,0:T(8,128)(2,1)S(1)} %collective-permute-done.4.refs_6_), channel_id=1, source_target_pairs={{0,1},{1,3},{3,5},{5,7},{7,6},{6,4},{4,2},{2,0},{8,9},{9,11},{11,1... | collective-permute-start | bytes 491528 | tf_op jit(solution)/shard_map/ppermute | solution.py:274
  26.5 2.0 %collective-permute-start.9 = (bf16[64,1280]{1,0:T(8,128)(2,1)S(1)}, bf16[64,1280]{1,0:T(8,128)(2,1)S(1)}, u32[]{:S(2)}, u32[]{:S(2)}) collective-permute-start(bf16[64,1280]{1,0:T(8,128)(2,1)S(1)} %collective-permute-done.5.refs_7_), channel_id=1, source_target_pairs={{0,1},{1,3},{3,5},{5,7},{7,6},{6,4},{4,2},{2,0},{8,9},{9,11},{11,1... | collective-permute-start | bytes 491528 | tf_op jit(solution)/shard_map/ppermute | solution.py:274
  30.3 2.0 %collective-permute-start.12 = (bf16[64,1280]{1,0:T(8,128)(2,1)}, bf16[64,1280]{1,0:T(8,128)(2,1)S(1)}, u32[]{:S(2)}, u32[]{:S(2)}) collective-permute-start(bf16[64,1280]{1,0:T(8,128)(2,1)} %collective-permute-done.8.refs_10_), channel_id=1, source_target_pairs={{0,1},{1,3},{3,5},{5,7},{7,6},{6,4},{4,2},{2,0},{8,9},{9,11},{11,1... | collective-permute-start | bytes 491528 | tf_op jit(solution)/shard_map/ppermute | solution.py:274
  33.7 2.4 %collective-permute-done.10.refs_12_.refs_2_ = bf16[64,1280]{1,0:T(8,128)(2,1)S(1)} collective-permute-done((bf16[64,1280]{1,0:T(8,128)(2,1)S(1)}, bf16[64,1280]{1,0:T(8,128)(2,1)S(1)}, u32[]{:S(2)}, u32[]{:S(2)}) %collective-permute-start.10) | collective-permute-done | bytes 163872 | tf_op jit(solution)/shard_map/ppermute | solution.py:274
  36.1 1.9 %collective-permute-done.13.refs_15_.refs_5_ = bf16[64,1280]{1,0:T(8,128)(2,1)S(1)} collective-permute-done((bf16[64,1280]{1,0:T(8,128)(2,1)S(1)}, bf16[64,1280]{1,0:T(8,128)(2,1)S(1)}, u32[]{:S(2)}, u32[]{:S(2)}) %collective-permute-start.13) | collective-permute-done | bytes 163872 | tf_op jit(solution)/shard_map/ppermute | solution.py:274
  43.3 1.2 after.4
  44.5 1.6 collective-permute-start.28
  53.5 11.7 %norm_conv.1 = (bf16[160,512]{1,0:T(8,128)(2,1)S(1)}, bf16[160,512]{1,0:T(8,128)(2,1)}) custom-call(s32[21]{0:T(128)S(1)} %concatenate.6.place_ref, bf16[64,1280]{1,0:T(8,128)(2,1)S(1)} %get-tuple-element.20.refs_0_, bf16[64,1280]{1,0:T(8,128)(2,1)S(1)} %get-tuple-element.19.refs_1_, bf16[64,1280]{1,0:T(8,128)(2,1)S(1)} %copy-done.36, ...), custom_call_target="tpu_custom_call" | custom-call | flops 3774873600 | bytes 6307840 | tf_op jit(solution)/shard_map/norm_conv/pallas_call | solution.py:359
  67.7 1.6 collective-permute-start.16
  70.9 1.5 collective-permute-start.29
  72.4 5.3 %collective-permute-done.14.refs_2_ = bf16[160,512]{1,0:T(8,128)(2,1)S(1)} collective-permute-done((bf16[160,512]{1,0:T(8,128)(2,1)S(1)}, bf16[160,512]{1,0:T(8,128)(2,1)S(1)}, u32[]{:S(2)}, u32[]{:S(2)}) %collective-permute-start.14) | collective-permute-done | bytes 163872 | tf_op jit(solution)/shard_map/ppermute | solution.py:274
  78.4 7.2 %collective-permute-done.15.refs_3_ = bf16[160,512]{1,0:T(8,128)(2,1)S(1)} collective-permute-done((bf16[160,512]{1,0:T(8,128)(2,1)}, bf16[160,512]{1,0:T(8,128)(2,1)S(1)}, u32[]{:S(2)}, u32[]{:S(2)}) %collective-permute-start.15) | collective-permute-done | bytes 163872 | tf_op jit(solution)/shard_map/ppermute | solution.py:274
  86.3 2.0 %collective-permute-start.21 = (bf16[160,512]{1,0:T(8,128)(2,1)S(1)}, bf16[160,512]{1,0:T(8,128)(2,1)S(1)}, u32[]{:S(2)}, u32[]{:S(2)}) collective-permute-start(bf16[160,512]{1,0:T(8,128)(2,1)S(1)} %collective-permute-done.17.refs_5_), channel_id=1, source_target_pairs={{1,0},{3,1},{5,3},{7,5},{6,7},{4,6},{2,4},{0,2},{9,8},{11,9},{13,1... | collective-permute-start | bytes 491528 | tf_op jit(solution)/shard_map/ppermute | solution.py:274
  89.8 1.9 %collective-permute-done.18.refs_6_ = bf16[160,512]{1,0:T(8,128)(2,1)S(1)} collective-permute-done((bf16[160,512]{1,0:T(8,128)(2,1)S(1)}, bf16[160,512]{1,0:T(8,128)(2,1)S(1)}, u32[]{:S(2)}, u32[]{:S(2)}) %collective-permute-start.18) | collective-permute-done | bytes 163872 | tf_op jit(solution)/shard_map/ppermute | solution.py:274
  92.4 3.0 %collective-permute-done.19.refs_7_ = bf16[160,512]{1,0:T(8,128)(2,1)S(1)} collective-permute-done((bf16[160,512]{1,0:T(8,128)(2,1)S(1)}, bf16[160,512]{1,0:T(8,128)(2,1)S(1)}, u32[]{:S(2)}, u32[]{:S(2)}) %collective-permute-start.19) | collective-permute-done | bytes 163872 | tf_op jit(solution)/shard_map/ppermute | solution.py:274
  96.2 2.0 %collective-permute-start.25 = (bf16[160,512]{1,0:T(8,128)(2,1)S(1)}, bf16[160,512]{1,0:T(8,128)(2,1)S(1)}, u32[]{:S(2)}, u32[]{:S(2)}) collective-permute-start(bf16[160,512]{1,0:T(8,128)(2,1)S(1)} %collective-permute-done.21.refs_9_), channel_id=1, source_target_pairs={{1,0},{3,1},{5,3},{7,5},{6,7},{4,6},{2,4},{0,2},{9,8},{11,9},{13,1... | collective-permute-start | bytes 491528 | tf_op jit(solution)/shard_map/ppermute | solution.py:274
  100.8 1.3 collective-permute-start.26
  102.7 1.7 %collective-permute-start.27 = (bf16[160,512]{1,0:T(8,128)(2,1)S(1)}, bf16[160,512]{1,0:T(8,128)(2,1)S(1)}, u32[]{:S(2)}, u32[]{:S(2)}) collective-permute-start(bf16[160,512]{1,0:T(8,128)(2,1)S(1)} %collective-permute-done.25.refs_13_.refs_3_), channel_id=1, source_target_pairs={{1,0},{3,1},{5,3},{7,5},{6,7},{4,6},{2,4},{0,2},{9,8},{11,9},{13,1... | collective-permute-start | bytes 491528 | tf_op jit(solution)/shard_map/ppermute | solution.py:274
  104.4 1.8 %collective-permute-done.24.refs_12_.refs_2_ = bf16[160,512]{1,0:T(8,128)(2,1)S(1)} collective-permute-done((bf16[160,512]{1,0:T(8,128)(2,1)S(1)}, bf16[160,512]{1,0:T(8,128)(2,1)S(1)}, u32[]{:S(2)}, u32[]{:S(2)}) %collective-permute-start.24) | collective-permute-done | bytes 163872 | tf_op jit(solution)/shard_map/ppermute | solution.py:274
  106.5 2.6 %collective-permute-done.27.refs_15_.refs_5_ = bf16[160,512]{1,0:T(8,128)(2,1)S(1)} collective-permute-done((bf16[160,512]{1,0:T(8,128)(2,1)S(1)}, bf16[160,512]{1,0:T(8,128)(2,1)S(1)}, u32[]{:S(2)}, u32[]{:S(2)}) %collective-permute-start.27) | collective-permute-done | bytes 163872 | tf_op jit(solution)/shard_map/ppermute | solution.py:274
  110.6 1.6 after.7.refs_5_
  128.1 14.9 %attention.1 = (bf16[320,128]{1,0:T(8,128)(2,1)S(1)}, bf16[320,128]{1,0:T(8,128)(2,1)S(1)}, bf16[320,128]{1,0:T(8,128)(2,1)S(1)}, bf16[320,128]{1,0:T(8,128)(2,1)S(1)}, bf16[1280,128]{1,0:T(8,128)(2,1)S(1)}) custom-call(s32[21]{0:T(128)S(1)} %concatenate.6.place_ref, bf16[160,512]{1,0:T(8,128)(2,1)S(1)} %copy-done.24, ...), custom_call_target="tpu_custom_call" | custom-call | flops 3187671040 | bytes 5079040 | tf_op jit(solution)/shard_map/attention/pallas_call | solution.py:391
  142.9 1.5 collective-permute-start.32
  144.6 2.8 %collective-permute-start.34 = (bf16[320,128]{1,0:T(8,128)(2,1)S(1)}, bf16[320,128]{1,0:T(8,128)(2,1)S(1)}, u32[]{:S(2)}, u32[]{:S(2)}) collective-permute-start(bf16[320,128]{1,0:T(8,128)(2,1)S(1)} %get-tuple-element.17), channel_id=1, source_target_pairs={{0,6},{1,7},{2,0},{3,1},{4,2},{5,3},{6,4},{7,5},{8,14},{9,15},{10,... | collective-permute-start | bytes 245768 | tf_op jit(solution)/shard_map/ppermute | solution.py:419
  147.4 2.8 %collective-permute-done.32.refs_1_ = bf16[320,128]{1,0:T(8,128)(2,1)S(1)} collective-permute-done((bf16[320,128]{1,0:T(8,128)(2,1)S(1)}, bf16[320,128]{1,0:T(8,128)(2,1)S(1)}, u32[]{:S(2)}, u32[]{:S(2)}) %collective-permute-start.32) | collective-permute-done | bytes 81952 | tf_op jit(solution)/shard_map/ppermute | solution.py:419
  150.2 2.9 %collective-permute-done.33.refs_2_ = bf16[320,128]{1,0:T(8,128)(2,1)S(1)} collective-permute-done((bf16[320,128]{1,0:T(8,128)(2,1)S(1)}, bf16[320,128]{1,0:T(8,128)(2,1)S(1)}, u32[]{:S(2)}, u32[]{:S(2)}) %collective-permute-start.33) | collective-permute-done | bytes 81952 | tf_op jit(solution)/shard_map/ppermute | solution.py:419
  153.1 2.5 %project.1 = bf16[128,1280]{1,0:T(8,128)(2,1)} custom-call(s32[21]{0:T(128)S(1)} %concatenate.6.place_ref, bf16[320,128]{1,0:T(8,128)(2,1)S(1)} %get-tuple-element.14.refs_0_, bf16[320,128]{1,0:T(8,128)(2,1)S(1)} %collective-permute-done.32.refs_1_, bf16[320,128]{1,0:T(8,128)(2,1)S(1)} %collective-permute-done.33.refs_2_, ...), custom_call_target="tpu_custom_call" | custom-call | flops 419430400 | bytes 4259840 | tf_op jit(solution)/shard_map/project/pallas_call | solution.py:421
  (199 shorter events, 50.6 us)
Async XLA Ops:
  6.6 103.2 %all-gather.2.cloned.1.call-start = ((), (), s32[]{:S(2)}) async-start(), calls=%async_computation | async-start | bytes 1843200 | tf_op jit(solution)/shard_map/all_gather | solution.py:309
  7.7 8.1 %collective-permute-start = (bf16[64,1280]{1,0:T(8,128)(2,1)S(1)}, bf16[64,1280]{1,0:T(8,128)(2,1)S(1)}, u32[]{:S(2)}, u32[]{:S(2)}) collective-permute-start(bf16[64,1280]{1,0:T(8,128)(2,1)S(1)} %get-tuple-element.20.refs_0_), channel_id=1, source_target_pairs={{0,1},{1,3},{3,5},{5,7},{7,6},{6,4},{4,2},{2,0},{8,9},{9,11},{11,1... | collective-permute-start | bytes 491528 | tf_op jit(solution)/shard_map/ppermute | solution.py:274
  10.8 7.8 %collective-permute-start.3 = (bf16[64,1280]{1,0:T(8,128)(2,1)S(1)}, bf16[64,1280]{1,0:T(8,128)(2,1)S(1)}, u32[]{:S(2)}, u32[]{:S(2)}) collective-permute-start(bf16[64,1280]{1,0:T(8,128)(2,1)S(1)} %get-tuple-element.19.refs_1_), channel_id=1, source_target_pairs={{1,0},{3,1},{5,3},{7,5},{6,7},{4,6},{2,4},{0,2},{9,8},{11,9},{13,1... | collective-permute-start | bytes 491528 | tf_op jit(solution)/shard_map/ppermute | solution.py:274
  10.9 8.5 %collective-permute-start.1 = (bf16[64,1280]{1,0:T(8,128)(2,1)S(1)}, bf16[64,1280]{1,0:T(8,128)(2,1)S(1)}, u32[]{:S(2)}, u32[]{:S(2)}) collective-permute-start(bf16[64,1280]{1,0:T(8,128)(2,1)S(1)} %get-tuple-element.19.refs_1_), channel_id=1, source_target_pairs={{0,1},{1,3},{3,5},{5,7},{7,6},{6,4},{4,2},{2,0},{8,9},{9,11},{11,1... | collective-permute-start | bytes 491528 | tf_op jit(solution)/shard_map/ppermute | solution.py:274
  12.8 8.6 %collective-permute-start.2 = (bf16[64,1280]{1,0:T(8,128)(2,1)S(1)}, bf16[64,1280]{1,0:T(8,128)(2,1)S(1)}, u32[]{:S(2)}, u32[]{:S(2)}) collective-permute-start(bf16[64,1280]{1,0:T(8,128)(2,1)S(1)} %get-tuple-element.20.refs_0_), channel_id=1, source_target_pairs={{1,0},{3,1},{5,3},{7,5},{6,7},{4,6},{2,4},{0,2},{9,8},{11,9},{13,1... | collective-permute-start | bytes 491528 | tf_op jit(solution)/shard_map/ppermute | solution.py:274
  15.8 7.2 %collective-permute-start.4 = (bf16[64,1280]{1,0:T(8,128)(2,1)S(1)}, bf16[64,1280]{1,0:T(8,128)(2,1)S(1)}, u32[]{:S(2)}, u32[]{:S(2)}) collective-permute-start(bf16[64,1280]{1,0:T(8,128)(2,1)S(1)} %collective-permute-done.refs_2_), channel_id=1, source_target_pairs={{0,1},{1,3},{3,5},{5,7},{7,6},{6,4},{4,2},{2,0},{8,9},{9,11},{11,1... | collective-permute-start | bytes 491528 | tf_op jit(solution)/shard_map/ppermute | solution.py:274
  18.5 7.1 %collective-permute-start.7 = (bf16[64,1280]{1,0:T(8,128)(2,1)S(1)}, bf16[64,1280]{1,0:T(8,128)(2,1)S(1)}, u32[]{:S(2)}, u32[]{:S(2)}) collective-permute-start(bf16[64,1280]{1,0:T(8,128)(2,1)S(1)} %collective-permute-done.3.refs_5_), channel_id=1, source_target_pairs={{1,0},{3,1},{5,3},{7,5},{6,7},{4,6},{2,4},{0,2},{9,8},{11,9},{13,1... | collective-permute-start | bytes 491528 | tf_op jit(solution)/shard_map/ppermute | solution.py:274
  19.4 7.2 %collective-permute-start.5 = (bf16[64,1280]{1,0:T(8,128)(2,1)S(1)}, bf16[64,1280]{1,0:T(8,128)(2,1)S(1)}, u32[]{:S(2)}, u32[]{:S(2)}) collective-permute-start(bf16[64,1280]{1,0:T(8,128)(2,1)S(1)} %collective-permute-done.1.refs_3_), channel_id=1, source_target_pairs={{0,1},{1,3},{3,5},{5,7},{7,6},{6,4},{4,2},{2,0},{8,9},{9,11},{11,1... | collective-permute-start | bytes 491528 | tf_op jit(solution)/shard_map/ppermute | solution.py:274
  21.4 7.8 %collective-permute-start.6 = (bf16[64,1280]{1,0:T(8,128)(2,1)S(1)}, bf16[64,1280]{1,0:T(8,128)(2,1)S(1)}, u32[]{:S(2)}, u32[]{:S(2)}) collective-permute-start(bf16[64,1280]{1,0:T(8,128)(2,1)S(1)} %collective-permute-done.2.refs_4_), channel_id=1, source_target_pairs={{1,0},{3,1},{5,3},{7,5},{6,7},{4,6},{2,4},{0,2},{9,8},{11,9},{13,1... | collective-permute-start | bytes 491528 | tf_op jit(solution)/shard_map/ppermute | solution.py:274
  23.0 7.2 %collective-permute-start.8 = (bf16[64,1280]{1,0:T(8,128)(2,1)S(1)}, bf16[64,1280]{1,0:T(8,128)(2,1)}, u32[]{:S(2)}, u32[]{:S(2)}) collective-permute-start(bf16[64,1280]{1,0:T(8,128)(2,1)S(1)} %collective-permute-done.4.refs_6_), channel_id=1, source_target_pairs={{0,1},{1,3},{3,5},{5,7},{7,6},{6,4},{4,2},{2,0},{8,9},{9,11},{11,1... | collective-permute-start | bytes 491528 | tf_op jit(solution)/shard_map/ppermute | solution.py:274
  25.6 7.1 %collective-permute-start.11 = (bf16[64,1280]{1,0:T(8,128)(2,1)S(1)}, bf16[64,1280]{1,0:T(8,128)(2,1)S(1)}, u32[]{:S(2)}, u32[]{:S(2)}) collective-permute-start(bf16[64,1280]{1,0:T(8,128)(2,1)S(1)} %collective-permute-done.7.refs_9_), channel_id=1, source_target_pairs={{1,0},{3,1},{5,3},{7,5},{6,7},{4,6},{2,4},{0,2},{9,8},{11,9},{13,1... | collective-permute-start | bytes 491528 | tf_op jit(solution)/shard_map/ppermute | solution.py:274
  26.5 7.1 %collective-permute-start.9 = (bf16[64,1280]{1,0:T(8,128)(2,1)S(1)}, bf16[64,1280]{1,0:T(8,128)(2,1)S(1)}, u32[]{:S(2)}, u32[]{:S(2)}) collective-permute-start(bf16[64,1280]{1,0:T(8,128)(2,1)S(1)} %collective-permute-done.5.refs_7_), channel_id=1, source_target_pairs={{0,1},{1,3},{3,5},{5,7},{7,6},{6,4},{4,2},{2,0},{8,9},{9,11},{11,1... | collective-permute-start | bytes 491528 | tf_op jit(solution)/shard_map/ppermute | solution.py:274
  29.2 6.9 %collective-permute-start.10 = (bf16[64,1280]{1,0:T(8,128)(2,1)S(1)}, bf16[64,1280]{1,0:T(8,128)(2,1)S(1)}, u32[]{:S(2)}, u32[]{:S(2)}) collective-permute-start(bf16[64,1280]{1,0:T(8,128)(2,1)S(1)} %collective-permute-done.6.refs_8_), channel_id=1, source_target_pairs={{1,0},{3,1},{5,3},{7,5},{6,7},{4,6},{2,4},{0,2},{9,8},{11,9},{13,1... | collective-permute-start | bytes 491528 | tf_op jit(solution)/shard_map/ppermute | solution.py:274
  44.5 24.8 %collective-permute-start.28 = (bf16[128,1280]{1,0:T(8,128)(2,1)}, bf16[128,1280]{1,0:T(8,128)(2,1)S(1)}, u32[]{:S(2)}, u32[]{:S(2)}) collective-permute-start(bf16[128,1280]{1,0:T(8,128)(2,1)} %after.4), channel_id=1, source_target_pairs={{0,1},{1,0},{2,3},{3,2},{4,5},{5,4},{6,7},{7,6},{8,9},{9,8},{10,11... | collective-permute-start | bytes 983048 | tf_op jit(solution)/shard_map/ppermute | solution.py:286
  65.2 12.6 %collective-permute-start.14 = (bf16[160,512]{1,0:T(8,128)(2,1)S(1)}, bf16[160,512]{1,0:T(8,128)(2,1)S(1)}, u32[]{:S(2)}, u32[]{:S(2)}) collective-permute-start(bf16[160,512]{1,0:T(8,128)(2,1)S(1)} %get-tuple-element.12.refs_1_.refs_0_), channel_id=1, source_target_pairs={{0,1},{1,3},{3,5},{5,7},{7,6},{6,4},{4,2},{2,0},{8,9},{9,11},{11,1... | collective-permute-start | bytes 491528 | tf_op jit(solution)/shard_map/ppermute | solution.py:274
  65.7 20.0 %collective-permute-start.15 = (bf16[160,512]{1,0:T(8,128)(2,1)}, bf16[160,512]{1,0:T(8,128)(2,1)S(1)}, u32[]{:S(2)}, u32[]{:S(2)}) collective-permute-start(bf16[160,512]{1,0:T(8,128)(2,1)} %get-tuple-element.13.refs_1_), channel_id=1, source_target_pairs={{0,1},{1,3},{3,5},{5,7},{7,6},{6,4},{4,2},{2,0},{8,9},{9,11},{11,1... | collective-permute-start | bytes 491528 | tf_op jit(solution)/shard_map/ppermute | solution.py:274
  66.8 19.5 %collective-permute-start.17 = (bf16[160,512]{1,0:T(8,128)(2,1)}, bf16[160,512]{1,0:T(8,128)(2,1)S(1)}, u32[]{:S(2)}, u32[]{:S(2)}) collective-permute-start(bf16[160,512]{1,0:T(8,128)(2,1)} %get-tuple-element.13.refs_1_), channel_id=1, source_target_pairs={{1,0},{3,1},{5,3},{7,5},{6,7},{4,6},{2,4},{0,2},{9,8},{11,9},{13,1... | collective-permute-start | bytes 491528 | tf_op jit(solution)/shard_map/ppermute | solution.py:274
  67.7 21.3 %collective-permute-start.16 = (bf16[160,512]{1,0:T(8,128)(2,1)S(1)}, bf16[160,512]{1,0:T(8,128)(2,1)S(1)}, u32[]{:S(2)}, u32[]{:S(2)}) collective-permute-start(bf16[160,512]{1,0:T(8,128)(2,1)S(1)} %get-tuple-element.12.refs_1_.refs_0_), channel_id=1, source_target_pairs={{1,0},{3,1},{5,3},{7,5},{6,7},{4,6},{2,4},{0,2},{9,8},{11,9},{13,1... | collective-permute-start | bytes 491528 | tf_op jit(solution)/shard_map/ppermute | solution.py:274
  70.9 27.9 %collective-permute-start.29 = (bf16[128,1280]{1,0:T(8,128)(2,1)}, bf16[128,1280]{1,0:T(8,128)(2,1)S(1)}, u32[]{:S(2)}, u32[]{:S(2)}) collective-permute-start(bf16[128,1280]{1,0:T(8,128)(2,1)} %after.5.refs_19_.refs_6_), channel_id=1, source_target_pairs={{0,16},{8,24},{16,0},{24,8},{1,17},{9,25},{17,1},{25,9},{2,18},{10... | collective-permute-start | bytes 983048 | tf_op jit(solution)/shard_map/ppermute | solution.py:293
  77.8 13.9 %collective-permute-start.18 = (bf16[160,512]{1,0:T(8,128)(2,1)S(1)}, bf16[160,512]{1,0:T(8,128)(2,1)S(1)}, u32[]{:S(2)}, u32[]{:S(2)}) collective-permute-start(bf16[160,512]{1,0:T(8,128)(2,1)S(1)} %collective-permute-done.14.refs_2_), channel_id=1, source_target_pairs={{0,1},{1,3},{3,5},{5,7},{7,6},{6,4},{4,2},{2,0},{8,9},{9,11},{11,1... | collective-permute-start | bytes 491528 | tf_op jit(solution)/shard_map/ppermute | solution.py:274
  85.7 9.8 %collective-permute-start.19 = (bf16[160,512]{1,0:T(8,128)(2,1)S(1)}, bf16[160,512]{1,0:T(8,128)(2,1)S(1)}, u32[]{:S(2)}, u32[]{:S(2)}) collective-permute-start(bf16[160,512]{1,0:T(8,128)(2,1)S(1)} %collective-permute-done.15.refs_3_), channel_id=1, source_target_pairs={{0,1},{1,3},{3,5},{5,7},{7,6},{6,4},{4,2},{2,0},{8,9},{9,11},{11,1... | collective-permute-start | bytes 491528 | tf_op jit(solution)/shard_map/ppermute | solution.py:274
  86.3 9.8 %collective-permute-start.21 = (bf16[160,512]{1,0:T(8,128)(2,1)S(1)}, bf16[160,512]{1,0:T(8,128)(2,1)S(1)}, u32[]{:S(2)}, u32[]{:S(2)}) collective-permute-start(bf16[160,512]{1,0:T(8,128)(2,1)S(1)} %collective-permute-done.17.refs_5_), channel_id=1, source_target_pairs={{1,0},{3,1},{5,3},{7,5},{6,7},{4,6},{2,4},{0,2},{9,8},{11,9},{13,1... | collective-permute-start | bytes 491528 | tf_op jit(solution)/shard_map/ppermute | solution.py:274
  89.0 9.8 %collective-permute-start.20 = (bf16[160,512]{1,0:T(8,128)(2,1)S(1)}, bf16[160,512]{1,0:T(8,128)(2,1)S(1)}, u32[]{:S(2)}, u32[]{:S(2)}) collective-permute-start(bf16[160,512]{1,0:T(8,128)(2,1)S(1)} %collective-permute-done.16.refs_4_), channel_id=1, source_target_pairs={{1,0},{3,1},{5,3},{7,5},{6,7},{4,6},{2,4},{0,2},{9,8},{11,9},{13,1... | collective-permute-start | bytes 491528 | tf_op jit(solution)/shard_map/ppermute | solution.py:274
  91.7 7.7 %collective-permute-start.22 = (bf16[160,512]{1,0:T(8,128)(2,1)S(1)}, bf16[160,512]{1,0:T(8,128)(2,1)S(1)}, u32[]{:S(2)}, u32[]{:S(2)}) collective-permute-start(bf16[160,512]{1,0:T(8,128)(2,1)S(1)} %collective-permute-done.18.refs_6_), channel_id=1, source_target_pairs={{0,1},{1,3},{3,5},{5,7},{7,6},{6,4},{4,2},{2,0},{8,9},{9,11},{11,1... | collective-permute-start | bytes 491528 | tf_op jit(solution)/shard_map/ppermute | solution.py:274
  96.2 6.6 %collective-permute-start.25 = (bf16[160,512]{1,0:T(8,128)(2,1)S(1)}, bf16[160,512]{1,0:T(8,128)(2,1)S(1)}, u32[]{:S(2)}, u32[]{:S(2)}) collective-permute-start(bf16[160,512]{1,0:T(8,128)(2,1)S(1)} %collective-permute-done.21.refs_9_), channel_id=1, source_target_pairs={{1,0},{3,1},{5,3},{7,5},{6,7},{4,6},{2,4},{0,2},{9,8},{11,9},{13,1... | collective-permute-start | bytes 491528 | tf_op jit(solution)/shard_map/ppermute | solution.py:274
  98.9 10.2 %collective-permute-start.30 = (bf16[128,1280]{1,0:T(8,128)(2,1)}, bf16[128,1280]{1,0:T(8,128)(2,1)S(1)}, u32[]{:S(2)}, u32[]{:S(2)}) collective-permute-start(bf16[128,1280]{1,0:T(8,128)(2,1)} %after.5.refs_19_.refs_6_), channel_id=1, source_target_pairs={{0,8},{8,0},{16,24},{24,16},{1,9},{9,1},{17,25},{25,17},{2,10},{10... | collective-permute-start | bytes 983048 | tf_op jit(solution)/shard_map/ppermute | solution.py:294
  98.9 10.9 %collective-permute-start.31 = (bf16[128,1280]{1,0:T(8,128)(2,1)S(1)}, bf16[128,1280]{1,0:T(8,128)(2,1)S(1)}, u32[]{:S(2)}, u32[]{:S(2)}) collective-permute-start(bf16[128,1280]{1,0:T(8,128)(2,1)S(1)} %collective-permute-done.29.refs_20_.refs_7_), channel_id=1, source_target_pairs={{0,8},{8,0},{16,24},{24,16},{1,9},{9,1},{17,25},{25,17},{2,10},{10... | collective-permute-start | bytes 983048 | tf_op jit(solution)/shard_map/ppermute | solution.py:294
  99.4 6.8 %collective-permute-start.24 = (bf16[160,512]{1,0:T(8,128)(2,1)S(1)}, bf16[160,512]{1,0:T(8,128)(2,1)S(1)}, u32[]{:S(2)}, u32[]{:S(2)}) collective-permute-start(bf16[160,512]{1,0:T(8,128)(2,1)S(1)} %collective-permute-done.20.refs_8_), channel_id=1, source_target_pairs={{1,0},{3,1},{5,3},{7,5},{6,7},{4,6},{2,4},{0,2},{9,8},{11,9},{13,1... | collective-permute-start | bytes 491528 | tf_op jit(solution)/shard_map/ppermute | solution.py:274
  112.2 40.9 %collective-permute-start.35 = (bf16[640,1280]{1,0:T(8,128)(2,1)}, bf16[640,1280]{1,0:T(8,128)(2,1)S(1)}, u32[]{:S(2)}, u32[]{:S(2)}) collective-permute-start(bf16[640,1280]{1,0:T(8,128)(2,1)} %after.7.refs_5_), channel_id=1, source_target_pairs={{0,8},{8,0},{16,24},{24,16},{1,9},{9,1},{17,25},{25,17},{2,10},{10... | collective-permute-start | bytes 4915208 | tf_op jit(solution)/shard_map/ppermute | solution.py:389
  142.9 7.2 %collective-permute-start.32 = (bf16[320,128]{1,0:T(8,128)(2,1)S(1)}, bf16[320,128]{1,0:T(8,128)(2,1)S(1)}, u32[]{:S(2)}, u32[]{:S(2)}) collective-permute-start(bf16[320,128]{1,0:T(8,128)(2,1)S(1)} %get-tuple-element.15), channel_id=1, source_target_pairs={{0,2},{1,3},{2,4},{3,5},{4,6},{5,7},{6,0},{7,1},{8,10},{9,11},{10,... | collective-permute-start | bytes 245768 | tf_op jit(solution)/shard_map/ppermute | solution.py:419
  144.5 8.6 %collective-permute-start.33 = (bf16[320,128]{1,0:T(8,128)(2,1)S(1)}, bf16[320,128]{1,0:T(8,128)(2,1)S(1)}, u32[]{:S(2)}, u32[]{:S(2)}) collective-permute-start(bf16[320,128]{1,0:T(8,128)(2,1)S(1)} %get-tuple-element.16), channel_id=1, source_target_pairs={{0,4},{1,5},{2,6},{3,7},{4,0},{5,1},{6,2},{7,3},{8,12},{9,13},{10,... | collective-permute-start | bytes 245768 | tf_op jit(solution)/shard_map/ppermute | solution.py:419
  144.6 8.5 %collective-permute-start.34 = (bf16[320,128]{1,0:T(8,128)(2,1)S(1)}, bf16[320,128]{1,0:T(8,128)(2,1)S(1)}, u32[]{:S(2)}, u32[]{:S(2)}) collective-permute-start(bf16[320,128]{1,0:T(8,128)(2,1)S(1)} %get-tuple-element.17), channel_id=1, source_target_pairs={{0,6},{1,7},{2,0},{3,1},{4,2},{5,3},{6,4},{7,5},{8,14},{9,15},{10,... | collective-permute-start | bytes 245768 | tf_op jit(solution)/shard_map/ppermute | solution.py:419
  (76 other events, 494.2 us)
Sparse Core Ops, SparseCore 0:
  40.1 52.9 all-gather.1

commit v4 on v3

--- a/solution.py
+++ b/solution.py
@@ -15,10 +15,11 @@
 OUTER = 4
 SET_HEADS = HEADS // OUTER
 SET_CHANNELS = SET_HEADS * HEAD_DIM
-FIXED = 5
+QUAD = 4
+HANDED = (0, 1, 2, 3)
 GRANULE = 32
 EPSILON = 1e-05
-VMEM_LIMIT = 48 * 1024 * 1024
+MEBI = 1024 * 1024
 
 f32 = jnp.float32
 bf16 = jnp.bfloat16
@@ -35,7 +36,7 @@
     return dot(left, right, dims, lax.Precision.HIGHEST)
 
 
-def conv_kernel(columns, place_ref, *refs):
+def conv_kernel(columns, sources_ref, *refs):
     count = len(refs) - 8
     pieces = refs[:count]
     source_ref, bias_ref = refs[count : count + 2]
@@ -46,12 +47,12 @@
     block = pieces[0].shape[0]
     positions = block * count
     own = out_refs[0].shape[0]
-    me = place_ref[0]
+    me = lax.axis_index("patch")
     entries = float(positions * SPAN)
     chunk = 16
     steps = block // chunk
     starts = [
-        pl.multiple_of(place_ref[FIXED + index] * (2 * block) + (index % 2) * block, block)
+        pl.multiple_of(sources_ref[me * count + index] * (2 * block) + (index % 2) * block, block)
         for index in range(count)
     ]
 
@@ -107,7 +108,13 @@
     load.wait()
     wide = 256
     column = lax.broadcasted_iota(jnp.int32, (own, wide), 1) % columns
-    bias = bias_ref[...]
+    square = (own, own)
+    bias = jnp.where(
+        lax.broadcasted_iota(jnp.int32, square, 0) == lax.broadcasted_iota(jnp.int32, square, 1),
+        bias_ref[...],
+        0.0,
+    )
+    bias = jnp.sum(bias, axis=1, keepdims=True)
     for at in range(0, positions, wide):
         taps = dot(kernel_ref[0], act_ref[at : at + wide, :], NT)
         for shift in (1, 2):
@@ -121,7 +128,7 @@
         out_refs[which][:, low : low + wide] = hidden.astype(bf16)
 
 
-def attention_kernel(count, inner, place_ref, *refs):
+def attention_kernel(count, inner, sources_ref, *refs):
     pieces = refs[:count]
     parts = refs[count : -8 - OUTER]
     outs = refs[-8 - OUTER : -8]
@@ -130,41 +137,38 @@
     n = count // 2
     positions = 2 * part
     block = positions // n
-    me, outer_at, inner_at = place_ref[0], place_ref[1], place_ref[2]
+    me = lax.axis_index("patch")
+    outer_at, inner_at = lax.div(me, inner), lax.rem(me, inner)
     entries = float(positions * SPAN)
 
     copies = []
     for index, piece in enumerate(pieces):
-        row = pl.multiple_of(place_ref[FIXED + index] * own, own)
+        row = pl.multiple_of(sources_ref[me * count + index] * own, own)
         low = (index % 2) * part
         target = hidden_ref.at[pl.ds(row, own), low : low + part]
-        copy = pltpu.make_async_copy(piece, target, sems.at[index])
-        copy.start()
-        copies.append(copy)
+        copies.append(pltpu.make_async_copy(piece, target, sems.at[index]))
     loads = []
 
     def load(source, row):
-        loads.append(pltpu.make_async_copy(source, weight_ref.at[pl.ds(row, source.shape[0]), :], sems.at[count]))
-        loads[-1].start()
+        target = weight_ref.at[pl.ds(row, source.shape[0]), :]
+        loads.append(pltpu.make_async_copy(source, target, sems.at[count + len(loads)]))
 
     if inner == 2:
         for kind in range(3):
             row = kind * SET_CHANNELS + inner_at * own
-            load(parts[kind], pl.multiple_of(row, GRANULE))
-        quarters = quarter_starts(3 * own)
-        for step, part_ref in enumerate(parts[3:]):
-            which = jnp.bitwise_xor(place_ref[4], step)
-            first = jnp.int32(quarters[0])
-            for at in range(1, 4):
-                first = jnp.where(which == at, quarters[at], first)
+            load(parts[kind], pl.multiple_of(row, own))
+        mine = quad_place()
+        for step, part_ref in zip(HANDED, parts[3 : 3 + QUAD]):
+            first = quarter_start(jnp.bitwise_xor(mine, step), own)
             for at in range(part_ref.shape[0] // GRANULE):
-                granule = first + at
-                kind = lax.div(granule, own // GRANULE)
-                row = kind * SET_CHANNELS + (1 - inner_at) * own
-                row = row + lax.rem(granule, own // GRANULE) * GRANULE
-                load(part_ref.at[at * GRANULE : (at + 1) * GRANULE, :], pl.multiple_of(row, GRANULE))
+                kind, low = granule_at(first + at, own)
+                row = kind * SET_CHANNELS + (1 - inner_at) * own + low
+                source = part_ref.at[at * GRANULE : (at + 1) * GRANULE, :]
+                load(source, pl.multiple_of(row, GRANULE))
     else:
         load(parts[0], 0)
+    for copy in copies + loads:
+        copy.start()
     for copy in copies:
         copy.wait()
 
@@ -214,19 +218,20 @@
             outs[at + 1][low : low + HEAD_DIM, :] = attended[:, block:]
 
 
-def output_kernel(n, place_ref, *refs):
+def output_kernel(n, *refs):
     attended_refs = refs[:OUTER]
     hidden_ref = refs[OUTER]
-    weight_refs = refs[OUTER + 1 : OUTER + 3]
-    out_ref, attended_ref, total_ref = refs[OUTER + 3 :]
-    outer_at, core = place_ref[1], place_ref[3]
+    weight_refs = refs[OUTER + 1 : -3]
+    out_ref, attended_ref, total_ref = refs[-3:]
+    own = C // n
+    outer_at = lax.div(lax.axis_index("patch"), n // OUTER)
     for step in range(OUTER):
         origin = lax.rem(outer_at + OUTER - step, OUTER)
         row = pl.multiple_of(origin * SET_CHANNELS, SET_CHANNELS)
         attended_ref[pl.ds(row, SET_CHANNELS), :] = attended_refs[step][...]
+    attended = attended_ref[...]
     total_ref[...] = hidden_ref[...].astype(f32)
-    attended = attended_ref[...]
-    own = C // n
+    core = lax.rem(lax.axis_index("batch"), 2)
     part = own // 2
     for which, weight_ref in zip((core, 1 - core), weight_refs):
         made = dot(weight_ref[...], attended)
@@ -234,6 +239,52 @@
             row = pl.multiple_of(origin * own + which * part, 8)
             total_ref[pl.ds(row, part), :] += made[origin * part : (origin + 1) * part]
     out_ref[...] = total_ref[...].T.astype(bf16)
+
+
+def pick_kernel(*refs):
+    weight_refs = refs[:3]
+    source_ref, quarter_ref, half_ref, sems = refs[3:]
+    own = source_ref.shape[0]
+    half = half_ref.shape[0]
+    row = pl.multiple_of(lax.rem(lax.axis_index("batch"), 2) * half, half)
+    copy = pltpu.make_async_copy(source_ref.at[pl.ds(row, half), :], half_ref, sems.at[0])
+    copy.start()
+    count = quarter_ref.shape[0] // GRANULE
+    first = quarter_start(quad_place(), own)
+
+    def each(act):
+        for at in range(count):
+            kind, low = granule_at(first + at, own)
+            rows = pl.ds(pl.multiple_of(low, GRANULE), GRANULE)
+            target = quarter_ref.at[at * GRANULE : (at + 1) * GRANULE, :]
+            for which, weight_ref in enumerate(weight_refs):
+
+                @pl.when(kind == which)
+                def _(weight_ref=weight_ref):
+                    act(pltpu.make_async_copy(weight_ref.at[rows, :], target, sems.at[1 + at]))
+
+    each(lambda one: one.start())
+    each(lambda one: one.wait())
+    copy.wait()
+
+
+def quad_place():
+    at = lax.rem(lax.axis_index("batch"), QUAD)
+    return 2 * lax.rem(at, 2) + lax.div(at, 2)
+
+
+def quarter_rows(own):
+    return -(-3 * own // (QUAD * GRANULE)) * GRANULE
+
+
+def quarter_start(place, own):
+    part = quarter_rows(own) // GRANULE
+    return jnp.minimum(place * part, 3 * own // GRANULE - part)
+
+
+def granule_at(granule, own):
+    count = own // GRANULE
+    return lax.div(granule, count), lax.rem(granule, count) * GRANULE
 
 
 def ring_of(n):
@@ -260,7 +311,7 @@
     return table
 
 
-def gather(halves, n):
+def gather(halves, n, beside=()):
     ring = ring_of(n)
     forward = [(ring[at], ring[(at + 1) % n]) for at in range(n)]
     backward = [(target, start) for start, target in forward]
@@ -274,53 +325,58 @@
                 found[half, sign * step] = lax.ppermute(
                     found[half, sign * (step - 1)], "patch", pairs
                 )
+        if step == 1 and beside:
+            (found[0, -1],) = after([found[0, -1]], beside)
     found[0, far] = found[0, -far]
     return [found[half, away] for away in pieces_of(n) for half in (0, 1)]
 
 
-def swap_weights(weights, core, side, n, ready):
-    rows = jnp.concatenate(weights, axis=0)
-    quarters = jnp.asarray(quarter_starts(rows.shape[0]), jnp.int32)
-    start = lax.dynamic_index_in_dim(quarters, 2 * core + side, 0, keepdims=False) * GRANULE
-    own_part = after(lax.dynamic_slice_in_dim(rows, start, quarter_rows(rows.shape[0]), 0), *ready)
-    return lax.ppermute(own_part, "patch", [(at, at ^ 1) for at in range(n)])
-
-
-def spread_weights(first, ready):
+def pick(weights):
+    hbm = pl.BlockSpec(memory_space=pltpu.HBM)
+    anywhere = pl.BlockSpec(memory_space=pl.ANY)
+    own = weights[0].shape[0]
+    shapes = [(quarter_rows(own), C), (own // 2, C)]
+    return pl.pallas_call(
+        pick_kernel,
+        out_shape=[jax.ShapeDtypeStruct(shape, bf16) for shape in shapes],
+        in_specs=[hbm] * len(weights),
+        out_specs=[anywhere] * len(shapes),
+        scratch_shapes=[pltpu.SemaphoreType.DMA((1 + quarter_rows(own) // GRANULE,))],
+        compiler_params=pltpu.CompilerParams(vmem_limit_bytes=MEBI),
+        cost_estimate=pl.CostEstimate(flops=0, bytes_accessed=0, transcendentals=0),
+        name="pick",
+    )(*weights)
+
+
+def hand_on(block):
     batch = lax.axis_size("batch")
     across, cores = ([(at, at ^ bit) for at in range(batch)] for bit in (2, 1))
-    first = after(first, *ready)
-    second = lax.ppermute(first, "batch", across)
-    return [first, second] + [lax.ppermute(one, "batch", cores) for one in (first, second)]
-
-
-def quarter_rows(rows):
-    return -(-rows // (4 * GRANULE)) * GRANULE
-
-
-def quarter_starts(rows):
-    part = quarter_rows(rows)
-    return [min(at * part, rows - part) // GRANULE for at in range(4)]
-
-
-def output_weights(w_out, core, ready):
-    part = w_out.shape[0] // 2
-    shard = after(lax.dynamic_slice_in_dim(w_out, core * part, part, 0), *ready)
-    return lax.all_gather(shard, "patch", axis=0, tiled=True)
-
-
-def after(value, *ready):
+    blocks = [block, lax.ppermute(block, "batch", across)]
+    return blocks + [lax.ppermute(one, "batch", cores) for one in blocks]
+
+
+def moves(n, outer_step, inner_step):
+    inner = n // OUTER
+    pairs = []
+    for start in range(n):
+        outer_at = (start // inner + outer_step) % OUTER
+        inner_at = (start % inner + inner_step) % inner
+        pairs.append((start, outer_at * inner + inner_at))
+    return pairs
+
+
+def after(values, ready):
     anywhere = pl.BlockSpec(memory_space=pl.ANY)
-    vmem = pl.BlockSpec(memory_space=pltpu.VMEM)
     return pl.pallas_call(
         lambda *refs: None,
-        out_shape=jax.ShapeDtypeStruct(value.shape, value.dtype),
-        in_specs=[anywhere] + [vmem] * len(ready),
-        out_specs=anywhere,
-        input_output_aliases={0: 0},
+        out_shape=[jax.ShapeDtypeStruct(value.shape, value.dtype) for value in values],
+        in_specs=[anywhere] * (len(values) + len(ready)),
+        out_specs=[anywhere] * len(values),
+        input_output_aliases={at: at for at in range(len(values))},
+        compiler_params=pltpu.CompilerParams(vmem_limit_bytes=MEBI),
         cost_estimate=pl.CostEstimate(flops=0, bytes_accessed=0, transcendentals=0),
         name="after",
-    )(value, *ready)
+    )(*values, *ready)
 
 
 def on_device(latent, conv_weight, channel_bias, w_query, w_key, w_value, w_out):
@@ -330,31 +386,27 @@
     own = channels // n
     block = rows_local * columns
     positions = block * n
-    me = lax.axis_index("patch")
-    batch_at = lax.axis_index("batch")
-    inner_at = lax.rem(me, inner)
-    core = lax.rem(batch_at, 2)
-    side = lax.rem(lax.div(batch_at, 2), 2)
-    fixed = jnp.stack([me, lax.div(me, inner), inner_at, core, 2 * core + side])
-    fixed = fixed.astype(jnp.int32)
-    sources = jnp.asarray(sources_of(n), jnp.int32)
-    place = jnp.concatenate([fixed, lax.dynamic_index_in_dim(sources, me, 0, keepdims=False)])
+    sources = jnp.asarray(sources_of(n), jnp.int32).reshape(-1)
     vmem = pl.BlockSpec(memory_space=pltpu.VMEM)
     smem = pl.BlockSpec(memory_space=pltpu.SMEM)
     anywhere = pl.BlockSpec(memory_space=pl.ANY)
-    params = pltpu.CompilerParams(vmem_limit_bytes=VMEM_LIMIT)
 
     whole = latent.reshape(block, channels)
-    pieces = gather((whole[: block // 2], whole[block // 2 :]), n)
-
+    halves = whole[: block // 2], whole[block // 2 :]
     if inner == 2:
-        first = swap_weights((w_query, w_key, w_value), core, side, n, pieces[-5:])
+        quarter, out_half = pick((w_query, w_key, w_value, w_out))
+        pieces = gather(halves, n, [quarter, out_half])
+        quarter, out_half = after([quarter, out_half], pieces[-5:])
+        quarter = lax.ppermute(quarter, "patch", moves(n, 0, 1))
     else:
+        pieces = gather(halves, n)
         sets = [list(range(at, at + inner)) for at in range(0, n, inner)]
         weights = jnp.stack([w_query, w_key, w_value])
         weights = lax.all_gather(weights, "patch", axis=1, tiled=True, axis_index_groups=sets)
         weights = [weights.reshape(3 * SET_CHANNELS, channels)]
-    out_half = output_weights(w_out, core, pieces[-5:])
+        core = lax.rem(lax.axis_index("batch"), 2)
+        out_half = lax.dynamic_slice_in_dim(w_out, core * (own // 2), own // 2, 0)
+    out_half = lax.all_gather(out_half, "patch", axis=0, tiled=True)
 
     hidden = pl.pallas_call(
         functools.partial(conv_kernel, columns),
@@ -367,7 +419,7 @@
             pltpu.VMEM((3, 3 * own, channels), bf16),
             pltpu.SemaphoreType.DMA,
         ],
-        compiler_params=params,
+        compiler_params=pltpu.CompilerParams(vmem_limit_bytes=20 * MEBI),
         cost_estimate=pl.CostEstimate(
             flops=2 * 9 * positions * channels * own,
             bytes_accessed=2 * (positions * channels + 9 * channels * own),
@@ -375,18 +427,18 @@
         ),
         name="norm_conv",
     )(
-        place,
+        sources,
         *pieces,
         conv_weight.reshape(3, 3 * own, channels),
-        channel_bias.reshape(own, 1),
+        channel_bias.reshape(1, own),
     )
 
     hidden_pieces = gather(tuple(hidden), n)
     if inner == 2:
-        weights = [w_query, w_key, w_value] + spread_weights(first, hidden[:1])
-    out_half = after(out_half, *hidden_pieces[-5:], *weights[3:])
+        weights = [w_query, w_key, w_value] + hand_on(after([quarter], hidden[:1])[0])
+    (out_half,) = after([out_half], hidden_pieces[-5:] + weights[3:])
     cores = [(at, at ^ 1) for at in range(lax.axis_size("batch"))]
-    out_other = lax.ppermute(out_half, "batch", cores)
+    out_weights = [out_half, lax.ppermute(out_half, "batch", cores)]
 
     *attended, kept = pl.pallas_call(
         functools.partial(attention_kernel, 2 * n, inner),
@@ -401,9 +453,9 @@
             pltpu.VMEM((SET_CHANNELS, OUTER * block), bf16),
             pltpu.VMEM((SET_HEADS, positions, HEAD_DIM), bf16),
             pltpu.VMEM((SET_CHANNELS, positions), bf16),
-            pltpu.SemaphoreType.DMA((2 * n + 1,)),
+            pltpu.SemaphoreType.DMA((2 * n + 3 + QUAD * quarter_rows(own) // GRANULE,)),
         ],
-        compiler_params=params,
+        compiler_params=pltpu.CompilerParams(vmem_limit_bytes=28 * MEBI),
         cost_estimate=pl.CostEstimate(
             flops=2 * positions * channels * 3 * SET_CHANNELS
             + 4 * positions * OUTER * block * SET_CHANNELS,
@@ -411,7 +463,7 @@
             transcendentals=positions * OUTER * block * SET_HEADS,
         ),
         name="attention",
-    )(place, *hidden_pieces, *weights)
+    )(sources, *hidden_pieces, *weights)
 
     received = [attended[0]]
     for step in range(1, OUTER):
@@ -421,20 +473,20 @@
     output = pl.pallas_call(
         functools.partial(output_kernel, n),
         out_shape=jax.ShapeDtypeStruct((block, channels), bf16),
-        in_specs=[smem] + [vmem] * (OUTER + 3),
+        in_specs=[vmem] * (OUTER + 1 + len(out_weights)),
         out_specs=vmem,
         scratch_shapes=[
             pltpu.VMEM((channels, block), bf16),
             pltpu.VMEM((channels, block), f32),
         ],
-        compiler_params=params,
+        compiler_params=pltpu.CompilerParams(vmem_limit_bytes=12 * MEBI),
         cost_estimate=pl.CostEstimate(
             flops=2 * block * channels * channels,
             bytes_accessed=2 * channels * (channels + 3 * block),
             transcendentals=0,
         ),
         name="project",
-    )(place, *received, kept, out_half, out_other)
+    )(*received, kept, *out_weights)
     return output.reshape(rows_local, columns, channels)
 
 

time: 163 us -> 136 us (0.83)
  local copies, waits for them, and re-layouts: 40.1 us -> 14.3 us
  waiting for transfers between devices: 37.6 us -> 42.7 us
  Pallas kernels: 34 us -> 30.4 us
    unnamed x142 -> x60, local copies, waits for them, and re-layouts: 36.8 us -> 13.3 us
    ppermute x28, waiting for transfers between devices: 31.9 us -> 37.7 us  [gather(): lax.ppermute(found[half, sign * (step - 1)], 'patch', pairs)]
    pallas_call x4 -> x5, Pallas kernels: 4.97 us -> 0.73 us  [the longest x1 0.72 us: pick(): pl.pallas_call(pick_kernel, out_shape=[jax.ShapeDtypeStruct(shape, bf16)...]
  transfers between devices with their start and end apart: 37 -> 37, of which waited for: 19 -> 16; matrix products, arithmetic and copies ran while one was open for 2% -> 0% of each run, Pallas kernels for 18% -> 20%
where the time goes in v4:
time: 136 us
  waiting for transfers between devices  42.7 us (31%)
  starting transfers between devices  35 us (26%)
  Pallas kernels  30.4 us (22%)
  local copies, waits for them, and re-layouts  14.3 us (11%)
  between operations  13.6 us (10%)
    ppermute x28, waiting for transfers between devices, gather(): lax.ppermute(found[half, sign * (step - 1)], 'patch', pairs)  37.7 us
    ppermute x28, starting transfers between devices, gather(): lax.ppermute(found[half, sign * (step - 1)], 'patch', pairs)  27.6 us
    pallas_call x1, Pallas kernels, on_device(): pl.pallas_call(functools.partial(attention_kernel, 2 * n, inner), out_sha...  15.3 us
    unnamed x60, local copies, waits for them, and re-layouts  13.3 us
    pallas_call x1, Pallas kernels, on_device(): pl.pallas_call(functools.partial(conv_kernel, columns), out_shape=[jax.Sh...  10.9 us
    ppermute x3, waiting for transfers between devices, on_device(): received.append(lax.ppermute(attended[step], 'patch', pairs))  4.93 us
    ppermute x3, starting transfers between devices, on_device(): received.append(lax.ppermute(attended[step], 'patch', pairs))  4.55 us
    pallas_call x1, Pallas kernels, on_device(): pl.pallas_call(functools.partial(output_kernel, n), out_shape=jax.ShapeDt...  3.46 us
  transfers between devices with their start and end apart: 37, of which 16 were waited for; matrix products, arithmetic and copies ran while one was open for 0% of the time, Pallas kernels for 20%

profile of v4, /device:TPU:0, one launch (start us, length us, event | category | flops | bytes accessed | tf_op | source)
XLA Modules:
  0.0 136.0 jit_solution(13324311382876779594)
XLA Ops:
  7.6 3.0 %collective-permute-start = (bf16[64,1280]{1,0:T(8,128)(2,1)S(1)}, bf16[64,1280]{1,0:T(8,128)(2,1)S(1)}, u32[]{:S(2)}, u32[]{:S(2)}) collective-permute-start(bf16[64,1280]{1,0:T(8,128)(2,1)S(1)} %get-tuple-element.28.refs_0_), channel_id=1, source_target_pairs={{0,1},{1,3},{3,5},{5,7},{7,6},{6,4},{4,2},{2,0},{8,9},{9,11},{11,1... | collective-permute-start | bytes 491528 | tf_op jit(solution)/shard_map/ppermute | solution.py:325
  10.7 1.9 %collective-permute-start.1 = (bf16[64,1280]{1,0:T(8,128)(2,1)S(1)}, bf16[64,1280]{1,0:T(8,128)(2,1)S(1)}, u32[]{:S(2)}, u32[]{:S(2)}) collective-permute-start(bf16[64,1280]{1,0:T(8,128)(2,1)S(1)} %get-tuple-element.27.refs_1_), channel_id=1, source_target_pairs={{0,1},{1,3},{3,5},{5,7},{7,6},{6,4},{4,2},{2,0},{8,9},{9,11},{11,1... | collective-permute-start | bytes 491528 | tf_op jit(solution)/shard_map/ppermute | solution.py:325
  17.5 1.9 %collective-permute-start.4 = (bf16[64,1280]{1,0:T(8,128)(2,1)S(1)}, bf16[64,1280]{1,0:T(8,128)(2,1)S(1)}, u32[]{:S(2)}, u32[]{:S(2)}) collective-permute-start(bf16[64,1280]{1,0:T(8,128)(2,1)S(1)} %after.4.refs_2_), channel_id=1, source_target_pairs={{0,1},{1,3},{3,5},{5,7},{7,6},{6,4},{4,2},{2,0},{8,9},{9,11},{11,1... | collective-permute-start | bytes 491528 | tf_op jit(solution)/shard_map/ppermute | solution.py:325
  19.6 1.9 %collective-permute-start.5 = (bf16[64,1280]{1,0:T(8,128)(2,1)S(1)}, bf16[64,1280]{1,0:T(8,128)(2,1)S(1)}, u32[]{:S(2)}, u32[]{:S(2)}) collective-permute-start(bf16[64,1280]{1,0:T(8,128)(2,1)S(1)} %collective-permute-done.1.refs_3_), channel_id=1, source_target_pairs={{0,1},{1,3},{3,5},{5,7},{7,6},{6,4},{4,2},{2,0},{8,9},{9,11},{11,1... | collective-permute-start | bytes 491528 | tf_op jit(solution)/shard_map/ppermute | solution.py:325
  21.6 3.1 %collective-permute-done.4.refs_6_ = bf16[64,1280]{1,0:T(8,128)(2,1)S(1)} collective-permute-done((bf16[64,1280]{1,0:T(8,128)(2,1)S(1)}, bf16[64,1280]{1,0:T(8,128)(2,1)S(1)}, u32[]{:S(2)}, u32[]{:S(2)}) %collective-permute-start.4) | collective-permute-done | bytes 163872 | tf_op jit(solution)/shard_map/ppermute | solution.py:325
  24.7 1.9 %collective-permute-start.8 = (bf16[64,1280]{1,0:T(8,128)(2,1)S(1)}, bf16[64,1280]{1,0:T(8,128)(2,1)S(1)}, u32[]{:S(2)}, u32[]{:S(2)}) collective-permute-start(bf16[64,1280]{1,0:T(8,128)(2,1)S(1)} %collective-permute-done.4.refs_6_), channel_id=1, source_target_pairs={{0,1},{1,3},{3,5},{5,7},{7,6},{6,4},{4,2},{2,0},{8,9},{9,11},{11,1... | collective-permute-start | bytes 491528 | tf_op jit(solution)/shard_map/ppermute | solution.py:325
  26.7 1.5 %collective-permute-done.5.refs_7_ = bf16[64,1280]{1,0:T(8,128)(2,1)S(1)} collective-permute-done((bf16[64,1280]{1,0:T(8,128)(2,1)S(1)}, bf16[64,1280]{1,0:T(8,128)(2,1)S(1)}, u32[]{:S(2)}, u32[]{:S(2)}) %collective-permute-start.5) | collective-permute-done | bytes 163872 | tf_op jit(solution)/shard_map/ppermute | solution.py:325
  28.2 1.9 %collective-permute-start.9 = (bf16[64,1280]{1,0:T(8,128)(2,1)S(1)}, bf16[64,1280]{1,0:T(8,128)(2,1)S(1)}, u32[]{:S(2)}, u32[]{:S(2)}) collective-permute-start(bf16[64,1280]{1,0:T(8,128)(2,1)S(1)} %collective-permute-done.5.refs_7_), channel_id=1, source_target_pairs={{0,1},{1,3},{3,5},{5,7},{7,6},{6,4},{4,2},{2,0},{8,9},{9,11},{11,1... | collective-permute-start | bytes 491528 | tf_op jit(solution)/shard_map/ppermute | solution.py:325
  30.2 1.6 %collective-permute-done.8.refs_10_ = bf16[64,1280]{1,0:T(8,128)(2,1)S(1)} collective-permute-done((bf16[64,1280]{1,0:T(8,128)(2,1)S(1)}, bf16[64,1280]{1,0:T(8,128)(2,1)S(1)}, u32[]{:S(2)}, u32[]{:S(2)}) %collective-permute-start.8) | collective-permute-done | bytes 163872 | tf_op jit(solution)/shard_map/ppermute | solution.py:325
  31.8 1.9 %collective-permute-start.12 = (bf16[64,1280]{1,0:T(8,128)(2,1)S(1)}, bf16[64,1280]{1,0:T(8,128)(2,1)S(1)}, u32[]{:S(2)}, u32[]{:S(2)}) collective-permute-start(bf16[64,1280]{1,0:T(8,128)(2,1)S(1)} %collective-permute-done.8.refs_10_), channel_id=1, source_target_pairs={{0,1},{1,3},{3,5},{5,7},{7,6},{6,4},{4,2},{2,0},{8,9},{9,11},{11,1... | collective-permute-start | bytes 491528 | tf_op jit(solution)/shard_map/ppermute | solution.py:325
  37.2 2.8 %collective-permute-done.13.refs_15_.refs_6_ = bf16[64,1280]{1,0:T(8,128)(2,1)S(1)} collective-permute-done((bf16[64,1280]{1,0:T(8,128)(2,1)S(1)}, bf16[64,1280]{1,0:T(8,128)(2,1)S(1)}, u32[]{:S(2)}, u32[]{:S(2)}) %collective-permute-start.13) | collective-permute-done | bytes 163872 | tf_op jit(solution)/shard_map/ppermute | solution.py:325
  40.7 2.0 %copy-done.7 = bf16[3,3,160,1280]{3,2,1,0:T(8,128)(2,1)S(1)} copy-done((bf16[3,3,160,1280]{3,2,1,0:T(8,128)(2,1)S(1)}, bf16[3,3,160,1280]{3,2,1,0:T(8,128)(2,1)}, u32[]{:S(2)}) %copy-start.7) | copy-done | bytes 3686424
  42.8 10.9 %norm_conv.1 = (bf16[160,512]{1,0:T(8,128)(2,1)S(1)}, bf16[160,512]{1,0:T(8,128)(2,1)S(1)}) custom-call(s32[128]{0:T(128)S(1)} %copy-done.29, bf16[64,1280]{1,0:T(8,128)(2,1)S(1)} %get-tuple-element.28.refs_0_, bf16[64,1280]{1,0:T(8,128)(2,1)S(1)} %get-tuple-element.27.refs_1_, bf16[64,1280]{1,0:T(8,128)(2,1)S(1)} %after.4.refs_2_, ...), custom_call_target="tpu_custom_call" | custom-call | flops 3774873600 | bytes 6307840 | tf_op jit(solution)/shard_map/norm_conv/pallas_call | solution.py:411
  53.7 1.5 %collective-permute-start.14 = (bf16[160,512]{1,0:T(8,128)(2,1)S(1)}, bf16[160,512]{1,0:T(8,128)(2,1)S(1)}, u32[]{:S(2)}, u32[]{:S(2)}) collective-permute-start(bf16[160,512]{1,0:T(8,128)(2,1)S(1)} %get-tuple-element.18.refs_1_.refs_0_), channel_id=1, source_target_pairs={{0,1},{1,3},{3,5},{5,7},{7,6},{6,4},{4,2},{2,0},{8,9},{9,11},{11,1... | collective-permute-start | bytes 491528 | tf_op jit(solution)/shard_map/ppermute | solution.py:325
  55.4 1.8 %collective-permute-start.17 = (bf16[160,512]{1,0:T(8,128)(2,1)S(1)}, bf16[160,512]{1,0:T(8,128)(2,1)S(1)}, u32[]{:S(2)}, u32[]{:S(2)}) collective-permute-start(bf16[160,512]{1,0:T(8,128)(2,1)S(1)} %get-tuple-element.19.refs_1_), channel_id=1, source_target_pairs={{1,0},{3,1},{5,3},{7,5},{6,7},{4,6},{2,4},{0,2},{9,8},{11,9},{13,1... | collective-permute-start | bytes 491528 | tf_op jit(solution)/shard_map/ppermute | solution.py:325
  57.8 1.6 %collective-permute-start.29 = (bf16[128,1280]{1,0:T(8,128)(2,1)S(1)}, bf16[128,1280]{1,0:T(8,128)(2,1)S(1)}, u32[]{:S(2)}, u32[]{:S(2)}) collective-permute-start(bf16[128,1280]{1,0:T(8,128)(2,1)S(1)} %after.6.refs_19_.refs_6_), channel_id=1, source_target_pairs={{0,16},{8,24},{16,0},{24,8},{1,17},{9,25},{17,1},{25,9},{2,18},{10... | collective-permute-start | bytes 983048 | tf_op jit(solution)/shard_map/ppermute | solution.py:354
  59.4 4.1 %collective-permute-done.14.refs_2_ = bf16[160,512]{1,0:T(8,128)(2,1)S(1)} collective-permute-done((bf16[160,512]{1,0:T(8,128)(2,1)S(1)}, bf16[160,512]{1,0:T(8,128)(2,1)S(1)}, u32[]{:S(2)}, u32[]{:S(2)}) %collective-permute-start.14) | collective-permute-done | bytes 163872 | tf_op jit(solution)/shard_map/ppermute | solution.py:325
  64.1 3.0 %collective-permute-done.15.refs_3_ = bf16[160,512]{1,0:T(8,128)(2,1)S(1)} collective-permute-done((bf16[160,512]{1,0:T(8,128)(2,1)S(1)}, bf16[160,512]{1,0:T(8,128)(2,1)S(1)}, u32[]{:S(2)}, u32[]{:S(2)}) %collective-permute-start.15) | collective-permute-done | bytes 163872 | tf_op jit(solution)/shard_map/ppermute | solution.py:325
  67.8 2.0 %collective-permute-start.21 = (bf16[160,512]{1,0:T(8,128)(2,1)S(1)}, bf16[160,512]{1,0:T(8,128)(2,1)S(1)}, u32[]{:S(2)}, u32[]{:S(2)}) collective-permute-start(bf16[160,512]{1,0:T(8,128)(2,1)S(1)} %collective-permute-done.17.refs_5_), channel_id=1, source_target_pairs={{1,0},{3,1},{5,3},{7,5},{6,7},{4,6},{2,4},{0,2},{9,8},{11,9},{13,1... | collective-permute-start | bytes 491528 | tf_op jit(solution)/shard_map/ppermute | solution.py:325
  70.5 1.4 %collective-permute-start.20 = (bf16[160,512]{1,0:T(8,128)(2,1)S(1)}, bf16[160,512]{1,0:T(8,128)(2,1)S(1)}, u32[]{:S(2)}, u32[]{:S(2)}) collective-permute-start(bf16[160,512]{1,0:T(8,128)(2,1)S(1)} %collective-permute-done.16.refs_4_), channel_id=1, source_target_pairs={{1,0},{3,1},{5,3},{7,5},{6,7},{4,6},{2,4},{0,2},{9,8},{11,9},{13,1... | collective-permute-start | bytes 491528 | tf_op jit(solution)/shard_map/ppermute | solution.py:325
  73.8 6.9 %collective-permute-done.19.refs_7_ = bf16[160,512]{1,0:T(8,128)(2,1)S(1)} collective-permute-done((bf16[160,512]{1,0:T(8,128)(2,1)S(1)}, bf16[160,512]{1,0:T(8,128)(2,1)S(1)}, u32[]{:S(2)}, u32[]{:S(2)}) %collective-permute-start.19) | collective-permute-done | bytes 163872 | tf_op jit(solution)/shard_map/ppermute | solution.py:325
  81.3 2.0 %collective-permute-start.25 = (bf16[160,512]{1,0:T(8,128)(2,1)S(1)}, bf16[160,512]{1,0:T(8,128)(2,1)S(1)}, u32[]{:S(2)}, u32[]{:S(2)}) collective-permute-start(bf16[160,512]{1,0:T(8,128)(2,1)S(1)} %collective-permute-done.21.refs_9_), channel_id=1, source_target_pairs={{1,0},{3,1},{5,3},{7,5},{6,7},{4,6},{2,4},{0,2},{9,8},{11,9},{13,1... | collective-permute-start | bytes 491528 | tf_op jit(solution)/shard_map/ppermute | solution.py:325
  84.5 2.8 %collective-permute-done.22.refs_10_ = bf16[160,512]{1,0:T(8,128)(2,1)S(1)} collective-permute-done((bf16[160,512]{1,0:T(8,128)(2,1)S(1)}, bf16[160,512]{1,0:T(8,128)(2,1)S(1)}, u32[]{:S(2)}, u32[]{:S(2)}) %collective-permute-start.22) | collective-permute-done | bytes 163872 | tf_op jit(solution)/shard_map/ppermute | solution.py:325
  88.0 5.3 %collective-permute-done.23.refs_11_.refs_1_ = bf16[160,512]{1,0:T(8,128)(2,1)S(1)} collective-permute-done((bf16[160,512]{1,0:T(8,128)(2,1)S(1)}, bf16[160,512]{1,0:T(8,128)(2,1)S(1)}, u32[]{:S(2)}, u32[]{:S(2)}) %collective-permute-start.23) | collective-permute-done | bytes 163872 | tf_op jit(solution)/shard_map/ppermute | solution.py:325
  94.0 2.0 %collective-permute-start.27 = (bf16[160,512]{1,0:T(8,128)(2,1)S(1)}, bf16[160,512]{1,0:T(8,128)(2,1)S(1)}, u32[]{:S(2)}, u32[]{:S(2)}) collective-permute-start(bf16[160,512]{1,0:T(8,128)(2,1)S(1)} %collective-permute-done.25.refs_13_.refs_3_), channel_id=1, source_target_pairs={{1,0},{3,1},{5,3},{7,5},{6,7},{4,6},{2,4},{0,2},{9,8},{11,9},{13,1... | collective-permute-start | bytes 491528 | tf_op jit(solution)/shard_map/ppermute | solution.py:325
  96.0 2.6 %collective-permute-done.26.refs_14_.refs_4_ = bf16[160,512]{1,0:T(8,128)(2,1)S(1)} collective-permute-done((bf16[160,512]{1,0:T(8,128)(2,1)S(1)}, bf16[160,512]{1,0:T(8,128)(2,1)S(1)}, u32[]{:S(2)}, u32[]{:S(2)}) %collective-permute-start.26) | collective-permute-done | bytes 163872 | tf_op jit(solution)/shard_map/ppermute | solution.py:325
  100.9 15.3 %attention.1 = (bf16[320,128]{1,0:T(8,128)(2,1)S(1)}, bf16[320,128]{1,0:T(8,128)(2,1)S(1)}, bf16[320,128]{1,0:T(8,128)(2,1)S(1)}, bf16[320,128]{1,0:T(8,128)(2,1)S(1)}, bf16[1280,128]{1,0:T(8,128)(2,1)S(1)}) custom-call(s32[128]{0:T(128)S(1)} %copy-done.29, bf16[160,512]{1,0:T(8,128)(2,1)S(1)} %get-tuple-element.18.refs_1_.refs_0_, ...), custom_call_target="tpu_custom_call" | custom-call | flops 3187671040 | bytes 5079040 | tf_op jit(solution)/shard_map/attention/pallas_call | solution.py:443
  116.2 2.1 %collective-permute-start.32 = (bf16[320,128]{1,0:T(8,128)(2,1)S(1)}, bf16[320,128]{1,0:T(8,128)(2,1)S(1)}, u32[]{:S(2)}, u32[]{:S(2)}) collective-permute-start(bf16[320,128]{1,0:T(8,128)(2,1)S(1)} %get-tuple-element.22), channel_id=1, source_target_pairs={{0,2},{1,3},{2,4},{3,5},{4,6},{5,7},{6,0},{7,1},{8,10},{9,11},{10,... | collective-permute-start | bytes 245768 | tf_op jit(solution)/shard_map/ppermute | solution.py:471
  118.3 2.4 %collective-permute-start.34 = (bf16[320,128]{1,0:T(8,128)(2,1)S(1)}, bf16[320,128]{1,0:T(8,128)(2,1)S(1)}, u32[]{:S(2)}, u32[]{:S(2)}) collective-permute-start(bf16[320,128]{1,0:T(8,128)(2,1)S(1)} %get-tuple-element.24), channel_id=1, source_target_pairs={{0,6},{1,7},{2,0},{3,1},{4,2},{5,3},{6,4},{7,5},{8,14},{9,15},{10,... | collective-permute-start | bytes 245768 | tf_op jit(solution)/shard_map/ppermute | solution.py:471
  120.7 2.5 %collective-permute-done.32.refs_1_ = bf16[320,128]{1,0:T(8,128)(2,1)S(1)} collective-permute-done((bf16[320,128]{1,0:T(8,128)(2,1)S(1)}, bf16[320,128]{1,0:T(8,128)(2,1)S(1)}, u32[]{:S(2)}, u32[]{:S(2)}) %collective-permute-start.32) | collective-permute-done | bytes 81952 | tf_op jit(solution)/shard_map/ppermute | solution.py:471
  123.2 2.4 %collective-permute-done.33.refs_2_ = bf16[320,128]{1,0:T(8,128)(2,1)S(1)} collective-permute-done((bf16[320,128]{1,0:T(8,128)(2,1)S(1)}, bf16[320,128]{1,0:T(8,128)(2,1)S(1)}, u32[]{:S(2)}, u32[]{:S(2)}) %collective-permute-start.33) | collective-permute-done | bytes 81952 | tf_op jit(solution)/shard_map/ppermute | solution.py:471
  125.7 3.5 %project.1 = bf16[128,1280]{1,0:T(8,128)(2,1)} custom-call(bf16[320,128]{1,0:T(8,128)(2,1)S(1)} %get-tuple-element.21.refs_0_, bf16[320,128]{1,0:T(8,128)(2,1)S(1)} %collective-permute-done.32.refs_1_, bf16[320,128]{1,0:T(8,128)(2,1)S(1)} %collective-permute-done.33.refs_2_, bf16[320,128]{1,0:T(8,128)(2,1)S(1)} %collective-permute-done.34.refs_3_, ...), custom_call_target="tpu_custom_call" | custom-call | flops 419430400 | bytes 4259840 | tf_op jit(solution)/shard_map/project/pallas_call | solution.py:473
  (112 shorter events, 20.7 us)
Async XLA Ops:
  6.5 92.8 %all-gather.2.cloned.1.call-start = ((), (), s32[]{:S(2)}) async-start(), calls=%async_computation | async-start | bytes 1843200 | tf_op jit(solution)/shard_map/all_gather | solution.py:409
  7.6 9.9 %collective-permute-start = (bf16[64,1280]{1,0:T(8,128)(2,1)S(1)}, bf16[64,1280]{1,0:T(8,128)(2,1)S(1)}, u32[]{:S(2)}, u32[]{:S(2)}) collective-permute-start(bf16[64,1280]{1,0:T(8,128)(2,1)S(1)} %get-tuple-element.28.refs_0_), channel_id=1, source_target_pairs={{0,1},{1,3},{3,5},{5,7},{7,6},{6,4},{4,2},{2,0},{8,9},{9,11},{11,1... | collective-permute-start | bytes 491528 | tf_op jit(solution)/shard_map/ppermute | solution.py:325
  10.6 8.9 %collective-permute-start.3 = (bf16[64,1280]{1,0:T(8,128)(2,1)S(1)}, bf16[64,1280]{1,0:T(8,128)(2,1)S(1)}, u32[]{:S(2)}, u32[]{:S(2)}) collective-permute-start(bf16[64,1280]{1,0:T(8,128)(2,1)S(1)} %get-tuple-element.27.refs_1_), channel_id=1, source_target_pairs={{1,0},{3,1},{5,3},{7,5},{6,7},{4,6},{2,4},{0,2},{9,8},{11,9},{13,1... | collective-permute-start | bytes 491528 | tf_op jit(solution)/shard_map/ppermute | solution.py:325
  10.7 8.9 %collective-permute-start.1 = (bf16[64,1280]{1,0:T(8,128)(2,1)S(1)}, bf16[64,1280]{1,0:T(8,128)(2,1)S(1)}, u32[]{:S(2)}, u32[]{:S(2)}) collective-permute-start(bf16[64,1280]{1,0:T(8,128)(2,1)S(1)} %get-tuple-element.27.refs_1_), channel_id=1, source_target_pairs={{0,1},{1,3},{3,5},{5,7},{7,6},{6,4},{4,2},{2,0},{8,9},{9,11},{11,1... | collective-permute-start | bytes 491528 | tf_op jit(solution)/shard_map/ppermute | solution.py:325
  12.6 8.9 %collective-permute-start.2 = (bf16[64,1280]{1,0:T(8,128)(2,1)S(1)}, bf16[64,1280]{1,0:T(8,128)(2,1)S(1)}, u32[]{:S(2)}, u32[]{:S(2)}) collective-permute-start(bf16[64,1280]{1,0:T(8,128)(2,1)S(1)} %get-tuple-element.28.refs_0_), channel_id=1, source_target_pairs={{1,0},{3,1},{5,3},{7,5},{6,7},{4,6},{2,4},{0,2},{9,8},{11,9},{13,1... | collective-permute-start | bytes 491528 | tf_op jit(solution)/shard_map/ppermute | solution.py:325
  17.5 7.2 %collective-permute-start.4 = (bf16[64,1280]{1,0:T(8,128)(2,1)S(1)}, bf16[64,1280]{1,0:T(8,128)(2,1)S(1)}, u32[]{:S(2)}, u32[]{:S(2)}) collective-permute-start(bf16[64,1280]{1,0:T(8,128)(2,1)S(1)} %after.4.refs_2_), channel_id=1, source_target_pairs={{0,1},{1,3},{3,5},{5,7},{7,6},{6,4},{4,2},{2,0},{8,9},{9,11},{11,1... | collective-permute-start | bytes 491528 | tf_op jit(solution)/shard_map/ppermute | solution.py:325
  19.4 7.1 %collective-permute-start.7 = (bf16[64,1280]{1,0:T(8,128)(2,1)S(1)}, bf16[64,1280]{1,0:T(8,128)(2,1)S(1)}, u32[]{:S(2)}, u32[]{:S(2)}) collective-permute-start(bf16[64,1280]{1,0:T(8,128)(2,1)S(1)} %collective-permute-done.3.refs_5_), channel_id=1, source_target_pairs={{1,0},{3,1},{5,3},{7,5},{6,7},{4,6},{2,4},{0,2},{9,8},{11,9},{13,1... | collective-permute-start | bytes 491528 | tf_op jit(solution)/shard_map/ppermute | solution.py:325
  19.6 8.6 %collective-permute-start.5 = (bf16[64,1280]{1,0:T(8,128)(2,1)S(1)}, bf16[64,1280]{1,0:T(8,128)(2,1)S(1)}, u32[]{:S(2)}, u32[]{:S(2)}) collective-permute-start(bf16[64,1280]{1,0:T(8,128)(2,1)S(1)} %collective-permute-done.1.refs_3_), channel_id=1, source_target_pairs={{0,1},{1,3},{3,5},{5,7},{7,6},{6,4},{4,2},{2,0},{8,9},{9,11},{11,1... | collective-permute-start | bytes 491528 | tf_op jit(solution)/shard_map/ppermute | solution.py:325
  21.5 8.6 %collective-permute-start.6 = (bf16[64,1280]{1,0:T(8,128)(2,1)S(1)}, bf16[64,1280]{1,0:T(8,128)(2,1)S(1)}, u32[]{:S(2)}, u32[]{:S(2)}) collective-permute-start(bf16[64,1280]{1,0:T(8,128)(2,1)S(1)} %collective-permute-done.2.refs_4_), channel_id=1, source_target_pairs={{1,0},{3,1},{5,3},{7,5},{6,7},{4,6},{2,4},{0,2},{9,8},{11,9},{13,1... | collective-permute-start | bytes 491528 | tf_op jit(solution)/shard_map/ppermute | solution.py:325
  24.7 7.1 %collective-permute-start.8 = (bf16[64,1280]{1,0:T(8,128)(2,1)S(1)}, bf16[64,1280]{1,0:T(8,128)(2,1)S(1)}, u32[]{:S(2)}, u32[]{:S(2)}) collective-permute-start(bf16[64,1280]{1,0:T(8,128)(2,1)S(1)} %collective-permute-done.4.refs_6_), channel_id=1, source_target_pairs={{0,1},{1,3},{3,5},{5,7},{7,6},{6,4},{4,2},{2,0},{8,9},{9,11},{11,1... | collective-permute-start | bytes 491528 | tf_op jit(solution)/shard_map/ppermute | solution.py:325
  26.6 7.1 %collective-permute-start.11 = (bf16[64,1280]{1,0:T(8,128)(2,1)S(1)}, bf16[64,1280]{1,0:T(8,128)(2,1)S(1)}, u32[]{:S(2)}, u32[]{:S(2)}) collective-permute-start(bf16[64,1280]{1,0:T(8,128)(2,1)S(1)} %collective-permute-done.7.refs_9_), channel_id=1, source_target_pairs={{1,0},{3,1},{5,3},{7,5},{6,7},{4,6},{2,4},{0,2},{9,8},{11,9},{13,1... | collective-permute-start | bytes 491528 | tf_op jit(solution)/shard_map/ppermute | solution.py:325
  28.2 6.7 %collective-permute-start.9 = (bf16[64,1280]{1,0:T(8,128)(2,1)S(1)}, bf16[64,1280]{1,0:T(8,128)(2,1)S(1)}, u32[]{:S(2)}, u32[]{:S(2)}) collective-permute-start(bf16[64,1280]{1,0:T(8,128)(2,1)S(1)} %collective-permute-done.5.refs_7_), channel_id=1, source_target_pairs={{0,1},{1,3},{3,5},{5,7},{7,6},{6,4},{4,2},{2,0},{8,9},{9,11},{11,1... | collective-permute-start | bytes 491528 | tf_op jit(solution)/shard_map/ppermute | solution.py:325
  40.0 17.8 %collective-permute-start.28 = (bf16[128,1280]{1,0:T(8,128)(2,1)S(1)}, bf16[128,1280]{1,0:T(8,128)(2,1)S(1)}, u32[]{:S(2)}, u32[]{:S(2)}) collective-permute-start(bf16[128,1280]{1,0:T(8,128)(2,1)S(1)} %get-tuple-element.20), channel_id=1, source_target_pairs={{0,1},{1,0},{2,3},{3,2},{4,5},{5,4},{6,7},{7,6},{8,9},{9,8},{10,11... | collective-permute-start | bytes 983048 | tf_op jit(solution)/shard_map/ppermute | solution.py:400
  53.7 9.8 %collective-permute-start.14 = (bf16[160,512]{1,0:T(8,128)(2,1)S(1)}, bf16[160,512]{1,0:T(8,128)(2,1)S(1)}, u32[]{:S(2)}, u32[]{:S(2)}) collective-permute-start(bf16[160,512]{1,0:T(8,128)(2,1)S(1)} %get-tuple-element.18.refs_1_.refs_0_), channel_id=1, source_target_pairs={{0,1},{1,3},{3,5},{5,7},{7,6},{6,4},{4,2},{2,0},{8,9},{9,11},{11,1... | collective-permute-start | bytes 491528 | tf_op jit(solution)/shard_map/ppermute | solution.py:325
  55.1 12.0 %collective-permute-start.15 = (bf16[160,512]{1,0:T(8,128)(2,1)S(1)}, bf16[160,512]{1,0:T(8,128)(2,1)S(1)}, u32[]{:S(2)}, u32[]{:S(2)}) collective-permute-start(bf16[160,512]{1,0:T(8,128)(2,1)S(1)} %get-tuple-element.19.refs_1_), channel_id=1, source_target_pairs={{0,1},{1,3},{3,5},{5,7},{7,6},{6,4},{4,2},{2,0},{8,9},{9,11},{11,1... | collective-permute-start | bytes 491528 | tf_op jit(solution)/shard_map/ppermute | solution.py:325
  55.4 12.4 %collective-permute-start.17 = (bf16[160,512]{1,0:T(8,128)(2,1)S(1)}, bf16[160,512]{1,0:T(8,128)(2,1)S(1)}, u32[]{:S(2)}, u32[]{:S(2)}) collective-permute-start(bf16[160,512]{1,0:T(8,128)(2,1)S(1)} %get-tuple-element.19.refs_1_), channel_id=1, source_target_pairs={{1,0},{3,1},{5,3},{7,5},{6,7},{4,6},{2,4},{0,2},{9,8},{11,9},{13,1... | collective-permute-start | bytes 491528 | tf_op jit(solution)/shard_map/ppermute | solution.py:325
  57.2 13.3 %collective-permute-start.16 = (bf16[160,512]{1,0:T(8,128)(2,1)S(1)}, bf16[160,512]{1,0:T(8,128)(2,1)S(1)}, u32[]{:S(2)}, u32[]{:S(2)}) collective-permute-start(bf16[160,512]{1,0:T(8,128)(2,1)S(1)} %get-tuple-element.18.refs_1_.refs_0_), channel_id=1, source_target_pairs={{1,0},{3,1},{5,3},{7,5},{6,7},{4,6},{2,4},{0,2},{9,8},{11,9},{13,1... | collective-permute-start | bytes 491528 | tf_op jit(solution)/shard_map/ppermute | solution.py:325
  57.8 26.2 %collective-permute-start.29 = (bf16[128,1280]{1,0:T(8,128)(2,1)S(1)}, bf16[128,1280]{1,0:T(8,128)(2,1)S(1)}, u32[]{:S(2)}, u32[]{:S(2)}) collective-permute-start(bf16[128,1280]{1,0:T(8,128)(2,1)S(1)} %after.6.refs_19_.refs_6_), channel_id=1, source_target_pairs={{0,16},{8,24},{16,0},{24,8},{1,17},{9,25},{17,1},{25,9},{2,18},{10... | collective-permute-start | bytes 983048 | tf_op jit(solution)/shard_map/ppermute | solution.py:354
  63.5 9.1 %collective-permute-start.18 = (bf16[160,512]{1,0:T(8,128)(2,1)S(1)}, bf16[160,512]{1,0:T(8,128)(2,1)S(1)}, u32[]{:S(2)}, u32[]{:S(2)}) collective-permute-start(bf16[160,512]{1,0:T(8,128)(2,1)S(1)} %collective-permute-done.14.refs_2_), channel_id=1, source_target_pairs={{0,1},{1,3},{3,5},{5,7},{7,6},{6,4},{4,2},{2,0},{8,9},{9,11},{11,1... | collective-permute-start | bytes 491528 | tf_op jit(solution)/shard_map/ppermute | solution.py:325
  67.1 13.6 %collective-permute-start.19 = (bf16[160,512]{1,0:T(8,128)(2,1)S(1)}, bf16[160,512]{1,0:T(8,128)(2,1)S(1)}, u32[]{:S(2)}, u32[]{:S(2)}) collective-permute-start(bf16[160,512]{1,0:T(8,128)(2,1)S(1)} %collective-permute-done.15.refs_3_), channel_id=1, source_target_pairs={{0,1},{1,3},{3,5},{5,7},{7,6},{6,4},{4,2},{2,0},{8,9},{9,11},{11,1... | collective-permute-start | bytes 491528 | tf_op jit(solution)/shard_map/ppermute | solution.py:325
  67.8 13.5 %collective-permute-start.21 = (bf16[160,512]{1,0:T(8,128)(2,1)S(1)}, bf16[160,512]{1,0:T(8,128)(2,1)S(1)}, u32[]{:S(2)}, u32[]{:S(2)}) collective-permute-start(bf16[160,512]{1,0:T(8,128)(2,1)S(1)} %collective-permute-done.17.refs_5_), channel_id=1, source_target_pairs={{1,0},{3,1},{5,3},{7,5},{6,7},{4,6},{2,4},{0,2},{9,8},{11,9},{13,1... | collective-permute-start | bytes 491528 | tf_op jit(solution)/shard_map/ppermute | solution.py:325
  70.5 13.5 %collective-permute-start.20 = (bf16[160,512]{1,0:T(8,128)(2,1)S(1)}, bf16[160,512]{1,0:T(8,128)(2,1)S(1)}, u32[]{:S(2)}, u32[]{:S(2)}) collective-permute-start(bf16[160,512]{1,0:T(8,128)(2,1)S(1)} %collective-permute-done.16.refs_4_), channel_id=1, source_target_pairs={{1,0},{3,1},{5,3},{7,5},{6,7},{4,6},{2,4},{0,2},{9,8},{11,9},{13,1... | collective-permute-start | bytes 491528 | tf_op jit(solution)/shard_map/ppermute | solution.py:325
  72.6 14.8 %collective-permute-start.22 = (bf16[160,512]{1,0:T(8,128)(2,1)S(1)}, bf16[160,512]{1,0:T(8,128)(2,1)S(1)}, u32[]{:S(2)}, u32[]{:S(2)}) collective-permute-start(bf16[160,512]{1,0:T(8,128)(2,1)S(1)} %collective-permute-done.18.refs_6_), channel_id=1, source_target_pairs={{0,1},{1,3},{3,5},{5,7},{7,6},{6,4},{4,2},{2,0},{8,9},{9,11},{11,1... | collective-permute-start | bytes 491528 | tf_op jit(solution)/shard_map/ppermute | solution.py:325
  80.7 12.7 %collective-permute-start.23 = (bf16[160,512]{1,0:T(8,128)(2,1)S(1)}, bf16[160,512]{1,0:T(8,128)(2,1)S(1)}, u32[]{:S(2)}, u32[]{:S(2)}) collective-permute-start(bf16[160,512]{1,0:T(8,128)(2,1)S(1)} %collective-permute-done.19.refs_7_), channel_id=1, source_target_pairs={{0,1},{1,3},{3,5},{5,7},{7,6},{6,4},{4,2},{2,0},{8,9},{9,11},{11,1... | collective-permute-start | bytes 491528 | tf_op jit(solution)/shard_map/ppermute | solution.py:325
  81.3 12.7 %collective-permute-start.25 = (bf16[160,512]{1,0:T(8,128)(2,1)S(1)}, bf16[160,512]{1,0:T(8,128)(2,1)S(1)}, u32[]{:S(2)}, u32[]{:S(2)}) collective-permute-start(bf16[160,512]{1,0:T(8,128)(2,1)S(1)} %collective-permute-done.21.refs_9_), channel_id=1, source_target_pairs={{1,0},{3,1},{5,3},{7,5},{6,7},{4,6},{2,4},{0,2},{9,8},{11,9},{13,1... | collective-permute-start | bytes 491528 | tf_op jit(solution)/shard_map/ppermute | solution.py:325
  84.0 15.3 %collective-permute-start.30 = (bf16[128,1280]{1,0:T(8,128)(2,1)S(1)}, bf16[128,1280]{1,0:T(8,128)(2,1)S(1)}, u32[]{:S(2)}, u32[]{:S(2)}) collective-permute-start(bf16[128,1280]{1,0:T(8,128)(2,1)S(1)} %after.6.refs_19_.refs_6_), channel_id=1, source_target_pairs={{0,8},{8,0},{16,24},{24,16},{1,9},{9,1},{17,25},{25,17},{2,10},{10... | collective-permute-start | bytes 983048 | tf_op jit(solution)/shard_map/ppermute | solution.py:355
  84.0 15.3 %collective-permute-start.31 = (bf16[128,1280]{1,0:T(8,128)(2,1)S(1)}, bf16[128,1280]{1,0:T(8,128)(2,1)S(1)}, u32[]{:S(2)}, u32[]{:S(2)}) collective-permute-start(bf16[128,1280]{1,0:T(8,128)(2,1)S(1)} %collective-permute-done.29.refs_20_.refs_7_), channel_id=1, source_target_pairs={{0,8},{8,0},{16,24},{24,16},{1,9},{9,1},{17,25},{25,17},{2,10},{10... | collective-permute-start | bytes 983048 | tf_op jit(solution)/shard_map/ppermute | solution.py:355
  87.4 8.7 %collective-permute-start.24 = (bf16[160,512]{1,0:T(8,128)(2,1)S(1)}, bf16[160,512]{1,0:T(8,128)(2,1)S(1)}, u32[]{:S(2)}, u32[]{:S(2)}) collective-permute-start(bf16[160,512]{1,0:T(8,128)(2,1)S(1)} %collective-permute-done.20.refs_8_), channel_id=1, source_target_pairs={{1,0},{3,1},{5,3},{7,5},{6,7},{4,6},{2,4},{0,2},{9,8},{11,9},{13,1... | collective-permute-start | bytes 491528 | tf_op jit(solution)/shard_map/ppermute | solution.py:325
  99.5 26.2 %collective-permute-start.35 = (bf16[640,1280]{1,0:T(8,128)(2,1)}, bf16[640,1280]{1,0:T(8,128)(2,1)S(1)}, u32[]{:S(2)}, u32[]{:S(2)}) collective-permute-start(bf16[640,1280]{1,0:T(8,128)(2,1)} %after.7.refs_5_), channel_id=1, source_target_pairs={{0,8},{8,0},{16,24},{24,16},{1,9},{9,1},{17,25},{25,17},{2,10},{10... | collective-permute-start | bytes 4915208 | tf_op jit(solution)/shard_map/ppermute | solution.py:441
  116.2 7.0 %collective-permute-start.32 = (bf16[320,128]{1,0:T(8,128)(2,1)S(1)}, bf16[320,128]{1,0:T(8,128)(2,1)S(1)}, u32[]{:S(2)}, u32[]{:S(2)}) collective-permute-start(bf16[320,128]{1,0:T(8,128)(2,1)S(1)} %get-tuple-element.22), channel_id=1, source_target_pairs={{0,2},{1,3},{2,4},{3,5},{4,6},{5,7},{6,0},{7,1},{8,10},{9,11},{10,... | collective-permute-start | bytes 245768 | tf_op jit(solution)/shard_map/ppermute | solution.py:471
  118.3 7.4 %collective-permute-start.33 = (bf16[320,128]{1,0:T(8,128)(2,1)S(1)}, bf16[320,128]{1,0:T(8,128)(2,1)S(1)}, u32[]{:S(2)}, u32[]{:S(2)}) collective-permute-start(bf16[320,128]{1,0:T(8,128)(2,1)S(1)} %get-tuple-element.23), channel_id=1, source_target_pairs={{0,4},{1,5},{2,6},{3,7},{4,0},{5,1},{6,2},{7,3},{8,12},{9,13},{10,... | collective-permute-start | bytes 245768 | tf_op jit(solution)/shard_map/ppermute | solution.py:471
  118.3 7.4 %collective-permute-start.34 = (bf16[320,128]{1,0:T(8,128)(2,1)S(1)}, bf16[320,128]{1,0:T(8,128)(2,1)S(1)}, u32[]{:S(2)}, u32[]{:S(2)}) collective-permute-start(bf16[320,128]{1,0:T(8,128)(2,1)S(1)} %get-tuple-element.24), channel_id=1, source_target_pairs={{0,6},{1,7},{2,0},{3,1},{4,2},{5,3},{6,4},{7,5},{8,14},{9,15},{10,... | collective-permute-start | bytes 245768 | tf_op jit(solution)/shard_map/ppermute | solution.py:471
  (35 other events, 283.6 us)
Sparse Core Ops, SparseCore 0:
  40.2 54.0 all-gather.1

commit v5 on v4

--- a/solution.py
+++ b/solution.py
@@ -16,8 +16,9 @@
 SET_HEADS = HEADS // OUTER
 SET_CHANNELS = SET_HEADS * HEAD_DIM
 QUAD = 4
-HANDED = (0, 1, 2, 3)
-GRANULE = 32
+HANDED = (0, 2, 1, 3)
+FAR = ((1, 0), (2, 0), (3, 0), (2, 1))
+LAST = ((1, 1), (3, 1))
 EPSILON = 1e-05
 MEBI = 1024 * 1024
 
@@ -157,14 +158,10 @@
         for kind in range(3):
             row = kind * SET_CHANNELS + inner_at * own
             load(parts[kind], pl.multiple_of(row, own))
-        mine = quad_place()
-        for step, part_ref in zip(HANDED, parts[3 : 3 + QUAD]):
-            first = quarter_start(jnp.bitwise_xor(mine, step), own)
-            for at in range(part_ref.shape[0] // GRANULE):
-                kind, low = granule_at(first + at, own)
-                row = kind * SET_CHANNELS + (1 - inner_at) * own + low
-                source = part_ref.at[at * GRANULE : (at + 1) * GRANULE, :]
-                load(source, pl.multiple_of(row, GRANULE))
+        mine = lax.rem(lax.axis_index("batch"), QUAD)
+        for step, part_ref in zip(HANDED, parts[3:]):
+            row = jnp.bitwise_xor(mine, step) * SET_CHANNELS + (1 - inner_at) * own
+            load(part_ref, pl.multiple_of(row, own))
     else:
         load(parts[0], 0)
     for copy in copies + loads:
@@ -189,7 +186,7 @@
         copy.wait()
     wide = 256
     for at in range(0, positions, wide):
-        made = dot(weight_ref[SET_CHANNELS:, :], normed_ref[:, at : at + wide])
+        made = dot(weight_ref[SET_CHANNELS : 3 * SET_CHANNELS, :], normed_ref[:, at : at + wide])
         for head in range(SET_HEADS):
             low = head * HEAD_DIM
             key_ref[head, at : at + wide, :] = made[low : low + HEAD_DIM].T.astype(bf16)
@@ -223,68 +220,49 @@
     hidden_ref = refs[OUTER]
     weight_refs = refs[OUTER + 1 : -3]
     out_ref, attended_ref, total_ref = refs[-3:]
+    inner = n // OUTER
     own = C // n
-    outer_at = lax.div(lax.axis_index("patch"), n // OUTER)
+    me = lax.axis_index("patch")
+    outer_at, inner_at = lax.div(me, inner), lax.rem(me, inner)
     for step in range(OUTER):
         origin = lax.rem(outer_at + OUTER - step, OUTER)
         row = pl.multiple_of(origin * SET_CHANNELS, SET_CHANNELS)
         attended_ref[pl.ds(row, SET_CHANNELS), :] = attended_refs[step][...]
     attended = attended_ref[...]
+    if inner != 2:
+        total = dot(weight_refs[0][...], attended) + hidden_ref[...].astype(f32)
+        out_ref[...] = total.T.astype(bf16)
+        return
+
     total_ref[...] = hidden_ref[...].astype(f32)
-    core = lax.rem(lax.axis_index("batch"), 2)
-    part = own // 2
-    for which, weight_ref in zip((core, 1 - core), weight_refs):
-        made = dot(weight_ref[...], attended)
-        for origin in range(n):
-            row = pl.multiple_of(origin * own + which * part, 8)
-            total_ref[pl.ds(row, part), :] += made[origin * part : (origin + 1) * part]
+    mine = lax.rem(lax.axis_index("batch"), QUAD)
+    near, far = weight_refs[1 : 1 + QUAD], blocks_of(weight_refs[-4:-2], own)
+
+    def add(weight_ref, outer_step, inner_step):
+        origin = lax.rem(outer_at + OUTER - outer_step, OUTER) * inner
+        origin = origin + lax.rem(inner_at + inner_step, inner)
+        rows = pl.ds(pl.multiple_of(origin * own, own), own)
+        total_ref[rows, :] += dot(weight_ref[...], attended)
+
+    add(weight_refs[0], 0, 0)
+    for step, weight_ref in zip(HANDED, near):
+
+        @pl.when(jnp.bitwise_xor(mine, step) == QUAD - 1)
+        def _(weight_ref=weight_ref):
+            add(weight_ref, 0, 1)
+
+    for step, weight_ref in zip(HANDED, far):
+        holder = jnp.bitwise_xor(mine, step)
+        outer_step = jnp.where(holder == 0, 1, jnp.where(holder == 2, 3, 2))
+        add(weight_ref, outer_step, lax.div(holder, QUAD - 1))
+    core = lax.rem(mine, 2)
+    for which, weight_ref in zip((core, 1 - core), weight_refs[-2:]):
+        add(weight_ref, 1 + 2 * which, 1)
     out_ref[...] = total_ref[...].T.astype(bf16)
 
 
-def pick_kernel(*refs):
-    weight_refs = refs[:3]
-    source_ref, quarter_ref, half_ref, sems = refs[3:]
-    own = source_ref.shape[0]
-    half = half_ref.shape[0]
-    row = pl.multiple_of(lax.rem(lax.axis_index("batch"), 2) * half, half)
-    copy = pltpu.make_async_copy(source_ref.at[pl.ds(row, half), :], half_ref, sems.at[0])
-    copy.start()
-    count = quarter_ref.shape[0] // GRANULE
-    first = quarter_start(quad_place(), own)
-
-    def each(act):
-        for at in range(count):
-            kind, low = granule_at(first + at, own)
-            rows = pl.ds(pl.multiple_of(low, GRANULE), GRANULE)
-            target = quarter_ref.at[at * GRANULE : (at + 1) * GRANULE, :]
-            for which, weight_ref in enumerate(weight_refs):
-
-                @pl.when(kind == which)
-                def _(weight_ref=weight_ref):
-                    act(pltpu.make_async_copy(weight_ref.at[rows, :], target, sems.at[1 + at]))
-
-    each(lambda one: one.start())
-    each(lambda one: one.wait())
-    copy.wait()
-
-
-def quad_place():
-    at = lax.rem(lax.axis_index("batch"), QUAD)
-    return 2 * lax.rem(at, 2) + lax.div(at, 2)
-
-
-def quarter_rows(own):
-    return -(-3 * own // (QUAD * GRANULE)) * GRANULE
-
-
-def quarter_start(place, own):
-    part = quarter_rows(own) // GRANULE
-    return jnp.minimum(place * part, 3 * own // GRANULE - part)
-
-
-def granule_at(granule, own):
-    count = own // GRANULE
-    return lax.div(granule, count), lax.rem(granule, count) * GRANULE
+def blocks_of(refs, rows):
+    return [ref.at[at : at + rows, :] for ref in refs for at in range(0, ref.shape[0], rows)]
 
 
 def ring_of(n):
@@ -331,28 +309,18 @@
     return [found[half, away] for away in pieces_of(n) for half in (0, 1)]
 
 
-def pick(weights):
-    hbm = pl.BlockSpec(memory_space=pltpu.HBM)
-    anywhere = pl.BlockSpec(memory_space=pl.ANY)
-    own = weights[0].shape[0]
-    shapes = [(quarter_rows(own), C), (own // 2, C)]
-    return pl.pallas_call(
-        pick_kernel,
-        out_shape=[jax.ShapeDtypeStruct(shape, bf16) for shape in shapes],
-        in_specs=[hbm] * len(weights),
-        out_specs=[anywhere] * len(shapes),
-        scratch_shapes=[pltpu.SemaphoreType.DMA((1 + quarter_rows(own) // GRANULE,))],
-        compiler_params=pltpu.CompilerParams(vmem_limit_bytes=MEBI),
-        cost_estimate=pl.CostEstimate(flops=0, bytes_accessed=0, transcendentals=0),
-        name="pick",
-    )(*weights)
-
-
-def hand_on(block):
-    batch = lax.axis_size("batch")
-    across, cores = ([(at, at ^ bit) for at in range(batch)] for bit in (2, 1))
-    blocks = [block, lax.ppermute(block, "batch", across)]
-    return blocks + [lax.ppermute(one, "batch", cores) for one in blocks]
+def send(block, shifts):
+    batch, n = lax.axis_size("batch"), lax.axis_size("patch")
+    pairs = []
+    for at in range(batch):
+        for start, target in moves(n, *shifts[at % len(shifts)]):
+            pairs.append((at * n + start, at * n + target))
+    return lax.ppermute(block, ("batch", "patch"), pairs)
+
+
+def swap(block, bit):
+    pairs = [(at, at ^ bit) for at in range(lax.axis_size("batch"))]
+    return lax.ppermute(block, "batch", pairs)
 
 
 def moves(n, outer_step, inner_step):
@@ -367,7 +335,7 @@
 
 def after(values, ready):
     anywhere = pl.BlockSpec(memory_space=pl.ANY)
-    return pl.pallas_call(
+    made = pl.pallas_call(
         lambda *refs: None,
         out_shape=[jax.ShapeDtypeStruct(value.shape, value.dtype) for value in values],
         in_specs=[anywhere] * (len(values) + len(ready)),
@@ -377,6 +345,7 @@
         cost_estimate=pl.CostEstimate(flops=0, bytes_accessed=0, transcendentals=0),
         name="after",
     )(*values, *ready)
+    return list(made)
 
 
 def on_device(latent, conv_weight, channel_bias, w_query, w_key, w_value, w_out):
@@ -394,19 +363,20 @@
     whole = latent.reshape(block, channels)
     halves = whole[: block // 2], whole[block // 2 :]
     if inner == 2:
-        quarter, out_half = pick((w_query, w_key, w_value, w_out))
-        pieces = gather(halves, n, [quarter, out_half])
-        quarter, out_half = after([quarter, out_half], pieces[-5:])
-        quarter = lax.ppermute(quarter, "patch", moves(n, 0, 1))
+        place = lax.rem(lax.axis_index("batch"), QUAD)
+        chosen = jnp.where(place == 0, w_query, jnp.where(place == 1, w_key, w_value))
+        chosen = jnp.where(place == 3, w_out, chosen)
+        pieces = gather(halves, n, [chosen])
+        chosen, out_own = after([chosen, w_out], pieces[-5:])
+        near = [send(chosen, [(0, 1)])]
+        far = [send(out_own, FAR)]
     else:
         pieces = gather(halves, n)
         sets = [list(range(at, at + inner)) for at in range(0, n, inner)]
         weights = jnp.stack([w_query, w_key, w_value])
         weights = lax.all_gather(weights, "patch", axis=1, tiled=True, axis_index_groups=sets)
         weights = [weights.reshape(3 * SET_CHANNELS, channels)]
-        core = lax.rem(lax.axis_index("batch"), 2)
-        out_half = lax.dynamic_slice_in_dim(w_out, core * (own // 2), own // 2, 0)
-    out_half = lax.all_gather(out_half, "patch", axis=0, tiled=True)
+        out_weights = [lax.all_gather(w_out, "patch", axis=0, tiled=True)]
 
     hidden = pl.pallas_call(
         functools.partial(conv_kernel, columns),
@@ -435,10 +405,13 @@
 
     hidden_pieces = gather(tuple(hidden), n)
     if inner == 2:
-        weights = [w_query, w_key, w_value] + hand_on(after([quarter], hidden[:1])[0])
-    (out_half,) = after([out_half], hidden_pieces[-5:] + weights[3:])
-    cores = [(at, at ^ 1) for at in range(lax.axis_size("batch"))]
-    out_weights = [out_half, lax.ppermute(out_half, "batch", cores)]
+        *near, far = after(near + far, hidden[:1])
+        near.append(swap(near[0], 2))
+        near += [swap(one, 1) for one in near]
+        weights = [w_query, w_key, w_value] + near
+        far, out_own = after([far, out_own], hidden_pieces[-5:] + near)
+        across = swap(far, 2)
+        last = send(out_own, LAST)
 
     *attended, kept = pl.pallas_call(
         functools.partial(attention_kernel, 2 * n, inner),
@@ -449,11 +422,11 @@
         scratch_shapes=[
             pltpu.VMEM((channels, positions), bf16),
             pltpu.VMEM((channels, positions), bf16),
-            pltpu.VMEM((3 * SET_CHANNELS, channels), bf16),
+            pltpu.VMEM((QUAD * SET_CHANNELS, channels), bf16),
             pltpu.VMEM((SET_CHANNELS, OUTER * block), bf16),
             pltpu.VMEM((SET_HEADS, positions, HEAD_DIM), bf16),
             pltpu.VMEM((SET_CHANNELS, positions), bf16),
-            pltpu.SemaphoreType.DMA((2 * n + 3 + QUAD * quarter_rows(own) // GRANULE,)),
+            pltpu.SemaphoreType.DMA((2 * n + 3 + QUAD,)),
         ],
         compiler_params=pltpu.CompilerParams(vmem_limit_bytes=28 * MEBI),
         cost_estimate=pl.CostEstimate(
@@ -465,6 +438,9 @@
         name="attention",
     )(sources, *hidden_pieces, *weights)
 
+    if inner == 2:
+        far, last = after([jnp.concatenate([far, across], axis=0), last], [kept])
+        out_weights = [w_out] + near + [far, swap(far, 1), last, swap(last, 1)]
     received = [attended[0]]
     for step in range(1, OUTER):
         pairs = [(at, (at + step * inner) % n) for at in range(n)]

time: 136 us -> 111 us (0.82)
  between operations: 13.6 us -> 0.17 us
  local copies, waits for them, and re-layouts: 14.3 us -> 1.13 us
  starting transfers between devices: 35 us -> 46.9 us
  waiting for transfers between devices: 42.7 us -> 33.9 us
  Pallas kernels: 30.4 us -> 27.3 us
  other arithmetic: 0 us -> 1.41 us
    unnamed x60 -> x15, local copies, waits for them, and re-layouts: 13.3 us -> 0.06 us
    ppermute x28, waiting for transfers between devices: 37.7 us -> 28.6 us  [gather(): lax.ppermute(found[half, sign * (step - 1)], 'patch', pairs)]
    ppermute x5 -> x9, starting transfers between devices: 2.82 us -> 11.1 us  [the longest x6 6.52 us: swap(): return lax.ppermute(block, 'batch', pairs)]
    ppermute x28, starting transfers between devices: 27.6 us -> 30.8 us  [gather(): lax.ppermute(found[half, sign * (step - 1)], 'patch', pairs)]
  transfers between devices with their start and end apart: 37 -> 40, of which waited for: 16 -> 20; matrix products, arithmetic and copies ran while one was open for 0% -> 1% of each run, Pallas kernels for 20% -> 23%
where the time goes in v5:
time: 111 us
  starting transfers between devices  46.9 us (42%)
  waiting for transfers between devices  33.9 us (31%)
  Pallas kernels  27.3 us (25%)
  other arithmetic  1.41 us (1%)
  local copies, waits for them, and re-layouts  1.13 us (1%)
    ppermute x28, starting transfers between devices, gather(): lax.ppermute(found[half, sign * (step - 1)], 'patch', pairs)  30.8 us
    ppermute x28, waiting for transfers between devices, gather(): lax.ppermute(found[half, sign * (step - 1)], 'patch', pairs)  28.6 us
    pallas_call x1, Pallas kernels, on_device(): pl.pallas_call(functools.partial(attention_kernel, 2 * n, inner), out_sha...  14 us
    pallas_call x1, Pallas kernels, on_device(): pl.pallas_call(functools.partial(conv_kernel, columns), out_shape=[jax.Sh...  10.9 us
    ppermute x6, starting transfers between devices, swap(): return lax.ppermute(block, 'batch', pairs)  6.52 us
    ppermute x3, waiting for transfers between devices, on_device(): received.append(lax.ppermute(attended[step], 'patch', pairs))  5.27 us
    ppermute x3, starting transfers between devices, on_device(): received.append(lax.ppermute(attended[step], 'patch', pairs))  4.95 us
    ppermute x3, starting transfers between devices, send(): return lax.ppermute(block, ('batch', 'patch'), pairs)  4.62 us
  transfers between devices with their start and end apart: 40, of which 20 were waited for; matrix products, arithmetic and copies ran while one was open for 1% of the time, Pallas kernels for 23%

profile of v5, /device:TPU:0, one launch (start us, length us, event | category | flops | bytes accessed | tf_op | source)
XLA Modules:
  0.0 110.7 jit_solution(10194344447115219564)
XLA Ops:
  1.1 3.1 %collective-permute-start.3 = (bf16[64,1280]{1,0:T(8,128)(2,1)S(1)}, bf16[64,1280]{1,0:T(8,128)(2,1)S(1)}, u32[]{:S(2)}, u32[]{:S(2)}) collective-permute-start(bf16[64,1280]{1,0:T(8,128)(2,1)S(1)} %get-tuple-element.35.refs_1_), channel_id=1, source_target_pairs={{1,0},{3,1},{5,3},{7,5},{6,7},{4,6},{2,4},{0,2},{9,8},{11,9},{13,1... | collective-permute-start | bytes 491528 | tf_op jit(solution)/shard_map/ppermute | solution.py:303
  4.2 2.0 %collective-permute-start.2 = (bf16[64,1280]{1,0:T(8,128)(2,1)S(1)}, bf16[64,1280]{1,0:T(8,128)(2,1)S(1)}, u32[]{:S(2)}, u32[]{:S(2)}) collective-permute-start(bf16[64,1280]{1,0:T(8,128)(2,1)S(1)} %get-tuple-element.36.refs_0_), channel_id=1, source_target_pairs={{1,0},{3,1},{5,3},{7,5},{6,7},{4,6},{2,4},{0,2},{9,8},{11,9},{13,1... | collective-permute-start | bytes 491528 | tf_op jit(solution)/shard_map/ppermute | solution.py:303
  7.6 1.6 %collective-permute-done.3.refs_5_ = bf16[64,1280]{1,0:T(8,128)(2,1)S(1)} collective-permute-done((bf16[64,1280]{1,0:T(8,128)(2,1)S(1)}, bf16[64,1280]{1,0:T(8,128)(2,1)S(1)}, u32[]{:S(2)}, u32[]{:S(2)}) %collective-permute-start.3) | collective-permute-done | bytes 163872 | tf_op jit(solution)/shard_map/ppermute | solution.py:303
  9.1 2.1 %collective-permute-start.7 = (bf16[64,1280]{1,0:T(8,128)(2,1)S(1)}, bf16[64,1280]{1,0:T(8,128)(2,1)S(1)}, u32[]{:S(2)}, u32[]{:S(2)}) collective-permute-start(bf16[64,1280]{1,0:T(8,128)(2,1)S(1)} %collective-permute-done.3.refs_5_), channel_id=1, source_target_pairs={{1,0},{3,1},{5,3},{7,5},{6,7},{4,6},{2,4},{0,2},{9,8},{11,9},{13,1... | collective-permute-start | bytes 491528 | tf_op jit(solution)/shard_map/ppermute | solution.py:303
  11.2 2.1 %collective-permute-done.refs_0_ = bf16[64,1280]{1,0:T(8,128)(2,1)S(1)} collective-permute-done((bf16[64,1280]{1,0:T(8,128)(2,1)S(1)}, bf16[64,1280]{1,0:T(8,128)(2,1)S(1)}, u32[]{:S(2)}, u32[]{:S(2)}) %collective-permute-start) | collective-permute-done | bytes 163872 | tf_op jit(solution)/shard_map/ppermute | solution.py:303
  13.6 1.7 %collective-permute-start.5 = (bf16[64,1280]{1,0:T(8,128)(2,1)S(1)}, bf16[64,1280]{1,0:T(8,128)(2,1)S(1)}, u32[]{:S(2)}, u32[]{:S(2)}) collective-permute-start(bf16[64,1280]{1,0:T(8,128)(2,1)S(1)} %collective-permute-done.1.refs_3_), channel_id=1, source_target_pairs={{0,1},{1,3},{3,5},{5,7},{7,6},{6,4},{4,2},{2,0},{8,9},{9,11},{11,1... | collective-permute-start | bytes 491528 | tf_op jit(solution)/shard_map/ppermute | solution.py:303
  15.6 1.9 %collective-permute-start.11 = (bf16[64,1280]{1,0:T(8,128)(2,1)S(1)}, bf16[64,1280]{1,0:T(8,128)(2,1)S(1)}, u32[]{:S(2)}, u32[]{:S(2)}) collective-permute-start(bf16[64,1280]{1,0:T(8,128)(2,1)S(1)} %collective-permute-done.7.refs_9_), channel_id=1, source_target_pairs={{1,0},{3,1},{5,3},{7,5},{6,7},{4,6},{2,4},{0,2},{9,8},{11,9},{13,1... | collective-permute-start | bytes 491528 | tf_op jit(solution)/shard_map/ppermute | solution.py:303
  17.5 2.9 %collective-permute-done.4.refs_6_ = bf16[64,1280]{1,0:T(8,128)(2,1)S(1)} collective-permute-done((bf16[64,1280]{1,0:T(8,128)(2,1)S(1)}, bf16[64,1280]{1,0:T(8,128)(2,1)S(1)}, u32[]{:S(2)}, u32[]{:S(2)}) %collective-permute-start.4) | collective-permute-done | bytes 163872 | tf_op jit(solution)/shard_map/ppermute | solution.py:303
  20.7 3.2 %collective-permute-done.5.refs_7_ = bf16[64,1280]{1,0:T(8,128)(2,1)S(1)} collective-permute-done((bf16[64,1280]{1,0:T(8,128)(2,1)S(1)}, bf16[64,1280]{1,0:T(8,128)(2,1)S(1)}, u32[]{:S(2)}, u32[]{:S(2)}) %collective-permute-start.5) | collective-permute-done | bytes 163872 | tf_op jit(solution)/shard_map/ppermute | solution.py:303
  24.3 1.7 %collective-permute-start.10 = (bf16[64,1280]{1,0:T(8,128)(2,1)S(1)}, bf16[64,1280]{1,0:T(8,128)(2,1)S(1)}, u32[]{:S(2)}, u32[]{:S(2)}) collective-permute-start(bf16[64,1280]{1,0:T(8,128)(2,1)S(1)} %collective-permute-done.6.refs_8_), channel_id=1, source_target_pairs={{1,0},{3,1},{5,3},{7,5},{6,7},{4,6},{2,4},{0,2},{9,8},{11,9},{13,1... | collective-permute-start | bytes 491528 | tf_op jit(solution)/shard_map/ppermute | solution.py:303
  26.0 1.6 %collective-permute-start.13 = (bf16[64,1280]{1,0:T(8,128)(2,1)S(1)}, bf16[64,1280]{1,0:T(8,128)(2,1)S(1)}, u32[]{:S(2)}, u32[]{:S(2)}) collective-permute-start(bf16[64,1280]{1,0:T(8,128)(2,1)S(1)} %collective-permute-done.11.refs_13_.refs_4_), channel_id=1, source_target_pairs={{1,0},{3,1},{5,3},{7,5},{6,7},{4,6},{2,4},{0,2},{9,8},{11,9},{13,1... | collective-permute-start | bytes 491528 | tf_op jit(solution)/shard_map/ppermute | solution.py:303
  28.1 2.3 %collective-permute-done.9.refs_11_.refs_2_ = bf16[64,1280]{1,0:T(8,128)(2,1)S(1)} collective-permute-done((bf16[64,1280]{1,0:T(8,128)(2,1)S(1)}, bf16[64,1280]{1,0:T(8,128)(2,1)S(1)}, u32[]{:S(2)}, u32[]{:S(2)}) %collective-permute-start.9) | collective-permute-done | bytes 163872 | tf_op jit(solution)/shard_map/ppermute | solution.py:303
  31.3 1.6 %collective-permute-done.12.refs_14_.refs_5_ = bf16[64,1280]{1,0:T(8,128)(2,1)S(1)} collective-permute-done((bf16[64,1280]{1,0:T(8,128)(2,1)S(1)}, bf16[64,1280]{1,0:T(8,128)(2,1)S(1)}, u32[]{:S(2)}, u32[]{:S(2)}) %collective-permute-start.12) | collective-permute-done | bytes 163872 | tf_op jit(solution)/shard_map/ppermute | solution.py:303
  33.4 1.5 %collective-permute-start.29 = (bf16[160,1280]{1,0:T(8,128)(2,1)S(1)}, bf16[160,1280]{1,0:T(8,128)(2,1)S(1)}, u32[]{:S(2)}, u32[]{:S(2)}) collective-permute-start(bf16[160,1280]{1,0:T(8,128)(2,1)S(1)} %get-tuple-element.23.refs_1_), channel_id=1, source_target_pairs={{0,2},{1,3},{2,4},{3,5},{4,6},{5,7},{6,0},{7,1},{8,12},{9,13},{10,... | collective-permute-start | bytes 1228808 | tf_op jit(solution)/shard_map/ppermute | solution.py:318
  34.9 10.9 %norm_conv.1 = (bf16[160,512]{1,0:T(8,128)(2,1)S(1)}, bf16[160,512]{1,0:T(8,128)(2,1)S(1)}) custom-call(s32[128]{0:T(128)S(1)} %copy-done.6, bf16[64,1280]{1,0:T(8,128)(2,1)S(1)} %get-tuple-element.36.refs_0_, bf16[64,1280]{1,0:T(8,128)(2,1)S(1)} %get-tuple-element.35.refs_1_, bf16[64,1280]{1,0:T(8,128)(2,1)S(1)} %after.5.refs_2_, ...), custom_call_target="tpu_custom_call" | custom-call | flops 3774873600 | bytes 6307840 | tf_op jit(solution)/shard_map/norm_conv/pallas_call | solution.py:381
  45.9 3.7 %collective-permute-start.30 = (bf16[160,1280]{1,0:T(8,128)(2,1)S(1)}, bf16[160,1280]{1,0:T(8,128)(2,1)S(1)}, u32[]{:S(2)}, u32[]{:S(2)}) collective-permute-start(bf16[160,1280]{1,0:T(8,128)(2,1)S(1)} %get-tuple-element.24.refs_19_.refs_7_.refs_6_), channel_id=1, source_target_pairs={{0,16},{8,24},{16,0},{24,8},{1,17},{9,25},{17,1},{25,9},{2,18},{10... | collective-permute-start | bytes 1228808 | tf_op jit(solution)/shard_map/ppermute | solution.py:323
  49.6 2.0 %collective-permute-start.15 = (bf16[160,512]{1,0:T(8,128)(2,1)S(1)}, bf16[160,512]{1,0:T(8,128)(2,1)S(1)}, u32[]{:S(2)}, u32[]{:S(2)}) collective-permute-start(bf16[160,512]{1,0:T(8,128)(2,1)S(1)} %get-tuple-element.21.refs_1_), channel_id=1, source_target_pairs={{0,1},{1,3},{3,5},{5,7},{7,6},{6,4},{4,2},{2,0},{8,9},{9,11},{11,1... | collective-permute-start | bytes 491528 | tf_op jit(solution)/shard_map/ppermute | solution.py:303
  51.7 2.0 %collective-permute-start.14 = (bf16[160,512]{1,0:T(8,128)(2,1)S(1)}, bf16[160,512]{1,0:T(8,128)(2,1)S(1)}, u32[]{:S(2)}, u32[]{:S(2)}) collective-permute-start(bf16[160,512]{1,0:T(8,128)(2,1)S(1)} %get-tuple-element.20.refs_2_.refs_0_), channel_id=1, source_target_pairs={{0,1},{1,3},{3,5},{5,7},{7,6},{6,4},{4,2},{2,0},{8,9},{9,11},{11,1... | collective-permute-start | bytes 491528 | tf_op jit(solution)/shard_map/ppermute | solution.py:303
  53.6 2.2 %collective-permute-done.17.refs_5_ = bf16[160,512]{1,0:T(8,128)(2,1)S(1)} collective-permute-done((bf16[160,512]{1,0:T(8,128)(2,1)S(1)}, bf16[160,512]{1,0:T(8,128)(2,1)S(1)}, u32[]{:S(2)}, u32[]{:S(2)}) %collective-permute-start.17) | collective-permute-done | bytes 163872 | tf_op jit(solution)/shard_map/ppermute | solution.py:303
  57.9 1.4 %collective-permute-done.16.refs_4_ = bf16[160,512]{1,0:T(8,128)(2,1)S(1)} collective-permute-done((bf16[160,512]{1,0:T(8,128)(2,1)S(1)}, bf16[160,512]{1,0:T(8,128)(2,1)S(1)}, u32[]{:S(2)}, u32[]{:S(2)}) %collective-permute-start.16) | collective-permute-done | bytes 163872 | tf_op jit(solution)/shard_map/ppermute | solution.py:303
  64.7 1.7 %collective-permute-start.23 = (bf16[160,512]{1,0:T(8,128)(2,1)S(1)}, bf16[160,512]{1,0:T(8,128)(2,1)S(1)}, u32[]{:S(2)}, u32[]{:S(2)}) collective-permute-start(bf16[160,512]{1,0:T(8,128)(2,1)S(1)} %collective-permute-done.19.refs_7_), channel_id=1, source_target_pairs={{0,1},{1,3},{3,5},{5,7},{7,6},{6,4},{4,2},{2,0},{8,9},{9,11},{11,1... | collective-permute-start | bytes 491528 | tf_op jit(solution)/shard_map/ppermute | solution.py:303
  67.0 2.1 %collective-permute-done.25.refs_13_.refs_4_ = bf16[160,512]{1,0:T(8,128)(2,1)S(1)} collective-permute-done((bf16[160,512]{1,0:T(8,128)(2,1)S(1)}, bf16[160,512]{1,0:T(8,128)(2,1)S(1)}, u32[]{:S(2)}, u32[]{:S(2)}) %collective-permute-start.25) | collective-permute-done | bytes 163872 | tf_op jit(solution)/shard_map/ppermute | solution.py:303
  69.1 1.4 %collective-permute-start.24 = (bf16[160,512]{1,0:T(8,128)(2,1)S(1)}, bf16[160,512]{1,0:T(8,128)(2,1)S(1)}, u32[]{:S(2)}, u32[]{:S(2)}) collective-permute-start(bf16[160,512]{1,0:T(8,128)(2,1)S(1)} %collective-permute-done.20.refs_8_), channel_id=1, source_target_pairs={{1,0},{3,1},{5,3},{7,5},{6,7},{4,6},{2,4},{0,2},{9,8},{11,9},{13,1... | collective-permute-start | bytes 491528 | tf_op jit(solution)/shard_map/ppermute | solution.py:303
  74.4 1.6 %collective-permute-done.24.refs_12_.refs_3_ = bf16[160,512]{1,0:T(8,128)(2,1)S(1)} collective-permute-done((bf16[160,512]{1,0:T(8,128)(2,1)S(1)}, bf16[160,512]{1,0:T(8,128)(2,1)S(1)}, u32[]{:S(2)}, u32[]{:S(2)}) %collective-permute-start.24) | collective-permute-done | bytes 163872 | tf_op jit(solution)/shard_map/ppermute | solution.py:303
  76.0 1.8 %collective-permute-done.27.refs_15_.refs_6_ = bf16[160,512]{1,0:T(8,128)(2,1)S(1)} collective-permute-done((bf16[160,512]{1,0:T(8,128)(2,1)S(1)}, bf16[160,512]{1,0:T(8,128)(2,1)S(1)}, u32[]{:S(2)}, u32[]{:S(2)}) %collective-permute-start.27) | collective-permute-done | bytes 163872 | tf_op jit(solution)/shard_map/ppermute | solution.py:303
  79.3 2.6 %collective-permute-start.37 = (bf16[160,1280]{1,0:T(8,128)(2,1)S(1)}, bf16[160,1280]{1,0:T(8,128)(2,1)S(1)}, u32[]{:S(2)}, u32[]{:S(2)}) collective-permute-start(bf16[160,1280]{1,0:T(8,128)(2,1)S(1)} %get-tuple-element.32), channel_id=1, source_target_pairs={{0,3},{1,2},{2,5},{3,4},{4,7},{5,6},{6,1},{7,0},{8,15},{9,14},{10,... | collective-permute-start | bytes 1228808 | tf_op jit(solution)/shard_map/ppermute | solution.py:318
  81.9 14.0 %attention.1 = (bf16[320,128]{1,0:T(8,128)(2,1)S(1)}, bf16[320,128]{1,0:T(8,128)(2,1)S(1)}, bf16[320,128]{1,0:T(8,128)(2,1)S(1)}, bf16[320,128]{1,0:T(8,128)(2,1)S(1)}, bf16[1280,128]{1,0:T(8,128)(2,1)S(1)}) custom-call(s32[128]{0:T(128)S(1)} %copy-done.6, bf16[160,512]{1,0:T(8,128)(2,1)S(1)} %get-tuple-element.20.refs_2_.refs_0_, ...), custom_call_target="tpu_custom_call" | custom-call | flops 3187671040 | bytes 5079040 | tf_op jit(solution)/shard_map/attention/pallas_call | solution.py:416
  96.1 2.1 %collective-permute-start.38 = (bf16[320,1280]{1,0:T(8,128)(2,1)S(1)}, bf16[320,1280]{1,0:T(8,128)(2,1)S(1)}, u32[]{:S(2)}, u32[]{:S(2)}) collective-permute-start(bf16[320,1280]{1,0:T(8,128)(2,1)S(1)} %get-tuple-element.33.refs_10_), channel_id=1, source_target_pairs={{0,8},{8,0},{16,24},{24,16},{1,9},{9,1},{17,25},{25,17},{2,10},{10... | collective-permute-start | bytes 2457608 | tf_op jit(solution)/shard_map/ppermute | solution.py:323
  100.3 2.9 %collective-permute-start.35 = (bf16[320,128]{1,0:T(8,128)(2,1)S(1)}, bf16[320,128]{1,0:T(8,128)(2,1)S(1)}, u32[]{:S(2)}, u32[]{:S(2)}) collective-permute-start(bf16[320,128]{1,0:T(8,128)(2,1)S(1)} %get-tuple-element.28), channel_id=1, source_target_pairs={{0,6},{1,7},{2,0},{3,1},{4,2},{5,3},{6,4},{7,5},{8,14},{9,15},{10,... | collective-permute-start | bytes 245768 | tf_op jit(solution)/shard_map/ppermute | solution.py:447
  103.2 2.2 %collective-permute-done.33.refs_1_ = bf16[320,128]{1,0:T(8,128)(2,1)S(1)} collective-permute-done((bf16[320,128]{1,0:T(8,128)(2,1)S(1)}, bf16[320,128]{1,0:T(8,128)(2,1)S(1)}, u32[]{:S(2)}, u32[]{:S(2)}) %collective-permute-start.33) | collective-permute-done | bytes 81952 | tf_op jit(solution)/shard_map/ppermute | solution.py:447
  105.4 3.1 %collective-permute-done.34.refs_2_ = bf16[320,128]{1,0:T(8,128)(2,1)S(1)} collective-permute-done((bf16[320,128]{1,0:T(8,128)(2,1)S(1)}, bf16[320,128]{1,0:T(8,128)(2,1)S(1)}, u32[]{:S(2)}, u32[]{:S(2)}) %collective-permute-start.34) | collective-permute-done | bytes 81952 | tf_op jit(solution)/shard_map/ppermute | solution.py:447
  108.5 2.3 %project.1 = bf16[128,1280]{1,0:T(8,128)(2,1)} custom-call(bf16[320,128]{1,0:T(8,128)(2,1)S(1)} %get-tuple-element.25.refs_0_, bf16[320,128]{1,0:T(8,128)(2,1)S(1)} %collective-permute-done.33.refs_1_, bf16[320,128]{1,0:T(8,128)(2,1)S(1)} %collective-permute-done.34.refs_2_, bf16[320,128]{1,0:T(8,128)(2,1)S(1)} %collective-permute-done.35.refs_3_, ...), custom_call_target="tpu_custom_call" | custom-call | flops 419430400 | bytes 4259840 | tf_op jit(solution)/shard_map/project/pallas_call | solution.py:449
  (74 shorter events, 21.2 us)
Async XLA Ops:
  1.1 8.0 %collective-permute-start.3 = (bf16[64,1280]{1,0:T(8,128)(2,1)S(1)}, bf16[64,1280]{1,0:T(8,128)(2,1)S(1)}, u32[]{:S(2)}, u32[]{:S(2)}) collective-permute-start(bf16[64,1280]{1,0:T(8,128)(2,1)S(1)} %get-tuple-element.35.refs_1_), channel_id=1, source_target_pairs={{1,0},{3,1},{5,3},{7,5},{6,7},{4,6},{2,4},{0,2},{9,8},{11,9},{13,1... | collective-permute-start | bytes 491528 | tf_op jit(solution)/shard_map/ppermute | solution.py:303
  4.2 9.5 %collective-permute-start.1 = (bf16[64,1280]{1,0:T(8,128)(2,1)S(1)}, bf16[64,1280]{1,0:T(8,128)(2,1)S(1)}, u32[]{:S(2)}, u32[]{:S(2)}) collective-permute-start(bf16[64,1280]{1,0:T(8,128)(2,1)S(1)} %get-tuple-element.35.refs_1_), channel_id=1, source_target_pairs={{0,1},{1,3},{3,5},{5,7},{7,6},{6,4},{4,2},{2,0},{8,9},{9,11},{11,1... | collective-permute-start | bytes 491528 | tf_op jit(solution)/shard_map/ppermute | solution.py:303
  4.2 11.1 %collective-permute-start.2 = (bf16[64,1280]{1,0:T(8,128)(2,1)S(1)}, bf16[64,1280]{1,0:T(8,128)(2,1)S(1)}, u32[]{:S(2)}, u32[]{:S(2)}) collective-permute-start(bf16[64,1280]{1,0:T(8,128)(2,1)S(1)} %get-tuple-element.36.refs_0_), channel_id=1, source_target_pairs={{1,0},{3,1},{5,3},{7,5},{6,7},{4,6},{2,4},{0,2},{9,8},{11,9},{13,1... | collective-permute-start | bytes 491528 | tf_op jit(solution)/shard_map/ppermute | solution.py:303
  6.2 7.1 %collective-permute-start = (bf16[64,1280]{1,0:T(8,128)(2,1)S(1)}, bf16[64,1280]{1,0:T(8,128)(2,1)S(1)}, u32[]{:S(2)}, u32[]{:S(2)}) collective-permute-start(bf16[64,1280]{1,0:T(8,128)(2,1)S(1)} %get-tuple-element.36.refs_0_), channel_id=1, source_target_pairs={{0,1},{1,3},{3,5},{5,7},{7,6},{6,4},{4,2},{2,0},{8,9},{9,11},{11,1... | collective-permute-start | bytes 491528 | tf_op jit(solution)/shard_map/ppermute | solution.py:303
  9.1 6.5 %collective-permute-start.7 = (bf16[64,1280]{1,0:T(8,128)(2,1)S(1)}, bf16[64,1280]{1,0:T(8,128)(2,1)S(1)}, u32[]{:S(2)}, u32[]{:S(2)}) collective-permute-start(bf16[64,1280]{1,0:T(8,128)(2,1)S(1)} %collective-permute-done.3.refs_5_), channel_id=1, source_target_pairs={{1,0},{3,1},{5,3},{7,5},{6,7},{4,6},{2,4},{0,2},{9,8},{11,9},{13,1... | collective-permute-start | bytes 491528 | tf_op jit(solution)/shard_map/ppermute | solution.py:303
  13.3 7.1 %collective-permute-start.4 = (bf16[64,1280]{1,0:T(8,128)(2,1)S(1)}, bf16[64,1280]{1,0:T(8,128)(2,1)S(1)}, u32[]{:S(2)}, u32[]{:S(2)}) collective-permute-start(bf16[64,1280]{1,0:T(8,128)(2,1)S(1)} %after.5.refs_2_), channel_id=1, source_target_pairs={{0,1},{1,3},{3,5},{5,7},{7,6},{6,4},{4,2},{2,0},{8,9},{9,11},{11,1... | collective-permute-start | bytes 491528 | tf_op jit(solution)/shard_map/ppermute | solution.py:303
  13.6 10.4 %collective-permute-start.5 = (bf16[64,1280]{1,0:T(8,128)(2,1)S(1)}, bf16[64,1280]{1,0:T(8,128)(2,1)S(1)}, u32[]{:S(2)}, u32[]{:S(2)}) collective-permute-start(bf16[64,1280]{1,0:T(8,128)(2,1)S(1)} %collective-permute-done.1.refs_3_), channel_id=1, source_target_pairs={{0,1},{1,3},{3,5},{5,7},{7,6},{6,4},{4,2},{2,0},{8,9},{9,11},{11,1... | collective-permute-start | bytes 491528 | tf_op jit(solution)/shard_map/ppermute | solution.py:303
  15.3 9.0 %collective-permute-start.6 = (bf16[64,1280]{1,0:T(8,128)(2,1)S(1)}, bf16[64,1280]{1,0:T(8,128)(2,1)S(1)}, u32[]{:S(2)}, u32[]{:S(2)}) collective-permute-start(bf16[64,1280]{1,0:T(8,128)(2,1)S(1)} %collective-permute-done.2.refs_4_), channel_id=1, source_target_pairs={{1,0},{3,1},{5,3},{7,5},{6,7},{4,6},{2,4},{0,2},{9,8},{11,9},{13,1... | collective-permute-start | bytes 491528 | tf_op jit(solution)/shard_map/ppermute | solution.py:303
  15.6 10.4 %collective-permute-start.11 = (bf16[64,1280]{1,0:T(8,128)(2,1)S(1)}, bf16[64,1280]{1,0:T(8,128)(2,1)S(1)}, u32[]{:S(2)}, u32[]{:S(2)}) collective-permute-start(bf16[64,1280]{1,0:T(8,128)(2,1)S(1)} %collective-permute-done.7.refs_9_), channel_id=1, source_target_pairs={{1,0},{3,1},{5,3},{7,5},{6,7},{4,6},{2,4},{0,2},{9,8},{11,9},{13,1... | collective-permute-start | bytes 491528 | tf_op jit(solution)/shard_map/ppermute | solution.py:303
  20.5 7.1 %collective-permute-start.8 = (bf16[64,1280]{1,0:T(8,128)(2,1)S(1)}, bf16[64,1280]{1,0:T(8,128)(2,1)S(1)}, u32[]{:S(2)}, u32[]{:S(2)}) collective-permute-start(bf16[64,1280]{1,0:T(8,128)(2,1)S(1)} %collective-permute-done.4.refs_6_), channel_id=1, source_target_pairs={{0,1},{1,3},{3,5},{5,7},{7,6},{6,4},{4,2},{2,0},{8,9},{9,11},{11,1... | collective-permute-start | bytes 491528 | tf_op jit(solution)/shard_map/ppermute | solution.py:303
  24.0 6.4 %collective-permute-start.9 = (bf16[64,1280]{1,0:T(8,128)(2,1)S(1)}, bf16[64,1280]{1,0:T(8,128)(2,1)S(1)}, u32[]{:S(2)}, u32[]{:S(2)}) collective-permute-start(bf16[64,1280]{1,0:T(8,128)(2,1)S(1)} %collective-permute-done.5.refs_7_), channel_id=1, source_target_pairs={{0,1},{1,3},{3,5},{5,7},{7,6},{6,4},{4,2},{2,0},{8,9},{9,11},{11,1... | collective-permute-start | bytes 491528 | tf_op jit(solution)/shard_map/ppermute | solution.py:303
  32.9 12.9 %collective-permute-start.28 = (bf16[160,1280]{1,0:T(8,128)(2,1)S(1)}, bf16[160,1280]{1,0:T(8,128)(2,1)S(1)}, u32[]{:S(2)}, u32[]{:S(2)}) collective-permute-start(bf16[160,1280]{1,0:T(8,128)(2,1)S(1)} %get-tuple-element.22), channel_id=1, source_target_pairs={{0,1},{1,0},{2,3},{3,2},{4,5},{5,4},{6,7},{7,6},{8,9},{9,8},{10,11... | collective-permute-start | bytes 1228808 | tf_op jit(solution)/shard_map/ppermute | solution.py:318
  33.4 12.5 %collective-permute-start.29 = (bf16[160,1280]{1,0:T(8,128)(2,1)S(1)}, bf16[160,1280]{1,0:T(8,128)(2,1)S(1)}, u32[]{:S(2)}, u32[]{:S(2)}) collective-permute-start(bf16[160,1280]{1,0:T(8,128)(2,1)S(1)} %get-tuple-element.23.refs_1_), channel_id=1, source_target_pairs={{0,2},{1,3},{2,4},{3,5},{4,6},{5,7},{6,0},{7,1},{8,12},{9,13},{10,... | collective-permute-start | bytes 1228808 | tf_op jit(solution)/shard_map/ppermute | solution.py:318
  45.9 16.5 %collective-permute-start.30 = (bf16[160,1280]{1,0:T(8,128)(2,1)S(1)}, bf16[160,1280]{1,0:T(8,128)(2,1)S(1)}, u32[]{:S(2)}, u32[]{:S(2)}) collective-permute-start(bf16[160,1280]{1,0:T(8,128)(2,1)S(1)} %get-tuple-element.24.refs_19_.refs_7_.refs_6_), channel_id=1, source_target_pairs={{0,16},{8,24},{16,0},{24,8},{1,17},{9,25},{17,1},{25,9},{2,18},{10... | collective-permute-start | bytes 1228808 | tf_op jit(solution)/shard_map/ppermute | solution.py:323
  49.6 6.3 %collective-permute-start.17 = (bf16[160,512]{1,0:T(8,128)(2,1)S(1)}, bf16[160,512]{1,0:T(8,128)(2,1)S(1)}, u32[]{:S(2)}, u32[]{:S(2)}) collective-permute-start(bf16[160,512]{1,0:T(8,128)(2,1)S(1)} %get-tuple-element.21.refs_1_), channel_id=1, source_target_pairs={{1,0},{3,1},{5,3},{7,5},{6,7},{4,6},{2,4},{0,2},{9,8},{11,9},{13,1... | collective-permute-start | bytes 491528 | tf_op jit(solution)/shard_map/ppermute | solution.py:303
  49.6 7.1 %collective-permute-start.15 = (bf16[160,512]{1,0:T(8,128)(2,1)S(1)}, bf16[160,512]{1,0:T(8,128)(2,1)S(1)}, u32[]{:S(2)}, u32[]{:S(2)}) collective-permute-start(bf16[160,512]{1,0:T(8,128)(2,1)S(1)} %get-tuple-element.21.refs_1_), channel_id=1, source_target_pairs={{0,1},{1,3},{3,5},{5,7},{7,6},{6,4},{4,2},{2,0},{8,9},{9,11},{11,1... | collective-permute-start | bytes 491528 | tf_op jit(solution)/shard_map/ppermute | solution.py:303
  51.6 7.8 %collective-permute-start.16 = (bf16[160,512]{1,0:T(8,128)(2,1)S(1)}, bf16[160,512]{1,0:T(8,128)(2,1)S(1)}, u32[]{:S(2)}, u32[]{:S(2)}) collective-permute-start(bf16[160,512]{1,0:T(8,128)(2,1)S(1)} %get-tuple-element.20.refs_2_.refs_0_), channel_id=1, source_target_pairs={{1,0},{3,1},{5,3},{7,5},{6,7},{4,6},{2,4},{0,2},{9,8},{11,9},{13,1... | collective-permute-start | bytes 491528 | tf_op jit(solution)/shard_map/ppermute | solution.py:303
  51.7 8.6 %collective-permute-start.14 = (bf16[160,512]{1,0:T(8,128)(2,1)S(1)}, bf16[160,512]{1,0:T(8,128)(2,1)S(1)}, u32[]{:S(2)}, u32[]{:S(2)}) collective-permute-start(bf16[160,512]{1,0:T(8,128)(2,1)S(1)} %get-tuple-element.20.refs_2_.refs_0_), channel_id=1, source_target_pairs={{0,1},{1,3},{3,5},{5,7},{7,6},{6,4},{4,2},{2,0},{8,9},{9,11},{11,1... | collective-permute-start | bytes 491528 | tf_op jit(solution)/shard_map/ppermute | solution.py:303
  55.8 6.6 %collective-permute-start.21 = (bf16[160,512]{1,0:T(8,128)(2,1)S(1)}, bf16[160,512]{1,0:T(8,128)(2,1)S(1)}, u32[]{:S(2)}, u32[]{:S(2)}) collective-permute-start(bf16[160,512]{1,0:T(8,128)(2,1)S(1)} %collective-permute-done.17.refs_5_), channel_id=1, source_target_pairs={{1,0},{3,1},{5,3},{7,5},{6,7},{4,6},{2,4},{0,2},{9,8},{11,9},{13,1... | collective-permute-start | bytes 491528 | tf_op jit(solution)/shard_map/ppermute | solution.py:303
  56.7 6.4 %collective-permute-start.19 = (bf16[160,512]{1,0:T(8,128)(2,1)S(1)}, bf16[160,512]{1,0:T(8,128)(2,1)S(1)}, u32[]{:S(2)}, u32[]{:S(2)}) collective-permute-start(bf16[160,512]{1,0:T(8,128)(2,1)S(1)} %collective-permute-done.15.refs_3_), channel_id=1, source_target_pairs={{0,1},{1,3},{3,5},{5,7},{7,6},{6,4},{4,2},{2,0},{8,9},{9,11},{11,1... | collective-permute-start | bytes 491528 | tf_op jit(solution)/shard_map/ppermute | solution.py:303
  62.4 16.6 %collective-permute-start.31 = (bf16[160,1280]{1,0:T(8,128)(2,1)S(1)}, bf16[160,1280]{1,0:T(8,128)(2,1)S(1)}, u32[]{:S(2)}, u32[]{:S(2)}) collective-permute-start(bf16[160,1280]{1,0:T(8,128)(2,1)S(1)} %get-tuple-element.24.refs_19_.refs_7_.refs_6_), channel_id=1, source_target_pairs={{0,8},{8,0},{16,24},{24,16},{1,9},{9,1},{17,25},{25,17},{2,10},{10... | collective-permute-start | bytes 1228808 | tf_op jit(solution)/shard_map/ppermute | solution.py:323
  62.4 16.6 %collective-permute-start.32 = (bf16[160,1280]{1,0:T(8,128)(2,1)S(1)}, bf16[160,1280]{1,0:T(8,128)(2,1)S(1)}, u32[]{:S(2)}, u32[]{:S(2)}) collective-permute-start(bf16[160,1280]{1,0:T(8,128)(2,1)S(1)} %collective-permute-done.30.refs_20_.refs_8_.refs_7_), channel_id=1, source_target_pairs={{0,8},{8,0},{16,24},{24,16},{1,9},{9,1},{17,25},{25,17},{2,10},{10... | collective-permute-start | bytes 1228808 | tf_op jit(solution)/shard_map/ppermute | solution.py:323
  64.7 7.1 %collective-permute-start.23 = (bf16[160,512]{1,0:T(8,128)(2,1)S(1)}, bf16[160,512]{1,0:T(8,128)(2,1)S(1)}, u32[]{:S(2)}, u32[]{:S(2)}) collective-permute-start(bf16[160,512]{1,0:T(8,128)(2,1)S(1)} %collective-permute-done.19.refs_7_), channel_id=1, source_target_pairs={{0,1},{1,3},{3,5},{5,7},{7,6},{6,4},{4,2},{2,0},{8,9},{9,11},{11,1... | collective-permute-start | bytes 491528 | tf_op jit(solution)/shard_map/ppermute | solution.py:303
  66.4 7.3 %collective-permute-start.22 = (bf16[160,512]{1,0:T(8,128)(2,1)S(1)}, bf16[160,512]{1,0:T(8,128)(2,1)S(1)}, u32[]{:S(2)}, u32[]{:S(2)}) collective-permute-start(bf16[160,512]{1,0:T(8,128)(2,1)S(1)} %collective-permute-done.18.refs_6_), channel_id=1, source_target_pairs={{0,1},{1,3},{3,5},{5,7},{7,6},{6,4},{4,2},{2,0},{8,9},{9,11},{11,1... | collective-permute-start | bytes 491528 | tf_op jit(solution)/shard_map/ppermute | solution.py:303
  69.1 6.9 %collective-permute-start.24 = (bf16[160,512]{1,0:T(8,128)(2,1)S(1)}, bf16[160,512]{1,0:T(8,128)(2,1)S(1)}, u32[]{:S(2)}, u32[]{:S(2)}) collective-permute-start(bf16[160,512]{1,0:T(8,128)(2,1)S(1)} %collective-permute-done.20.refs_8_), channel_id=1, source_target_pairs={{1,0},{3,1},{5,3},{7,5},{6,7},{4,6},{2,4},{0,2},{9,8},{11,9},{13,1... | collective-permute-start | bytes 491528 | tf_op jit(solution)/shard_map/ppermute | solution.py:303
  79.1 16.9 %collective-permute-start.36 = (bf16[160,1280]{1,0:T(8,128)(2,1)S(1)}, bf16[160,1280]{1,0:T(8,128)(2,1)S(1)}, u32[]{:S(2)}, u32[]{:S(2)}) collective-permute-start(bf16[160,1280]{1,0:T(8,128)(2,1)S(1)} %get-tuple-element.31), channel_id=1, source_target_pairs={{0,16},{8,24},{16,0},{24,8},{1,17},{9,25},{17,1},{25,9},{2,18},{10... | collective-permute-start | bytes 1228808 | tf_op jit(solution)/shard_map/ppermute | solution.py:323
  79.3 16.8 %collective-permute-start.37 = (bf16[160,1280]{1,0:T(8,128)(2,1)S(1)}, bf16[160,1280]{1,0:T(8,128)(2,1)S(1)}, u32[]{:S(2)}, u32[]{:S(2)}) collective-permute-start(bf16[160,1280]{1,0:T(8,128)(2,1)S(1)} %get-tuple-element.32), channel_id=1, source_target_pairs={{0,3},{1,2},{2,5},{3,4},{4,7},{5,6},{6,1},{7,0},{8,15},{9,14},{10,... | collective-permute-start | bytes 1228808 | tf_op jit(solution)/shard_map/ppermute | solution.py:318
  96.1 12.4 %collective-permute-start.38 = (bf16[320,1280]{1,0:T(8,128)(2,1)S(1)}, bf16[320,1280]{1,0:T(8,128)(2,1)S(1)}, u32[]{:S(2)}, u32[]{:S(2)}) collective-permute-start(bf16[320,1280]{1,0:T(8,128)(2,1)S(1)} %get-tuple-element.33.refs_10_), channel_id=1, source_target_pairs={{0,8},{8,0},{16,24},{24,16},{1,9},{9,1},{17,25},{25,17},{2,10},{10... | collective-permute-start | bytes 2457608 | tf_op jit(solution)/shard_map/ppermute | solution.py:323
  98.1 10.3 %collective-permute-start.39 = (bf16[160,1280]{1,0:T(8,128)(2,1)S(1)}, bf16[160,1280]{1,0:T(8,128)(2,1)S(1)}, u32[]{:S(2)}, u32[]{:S(2)}) collective-permute-start(bf16[160,1280]{1,0:T(8,128)(2,1)S(1)} %get-tuple-element.34.refs_12_), channel_id=1, source_target_pairs={{0,8},{8,0},{16,24},{24,16},{1,9},{9,1},{17,25},{25,17},{2,10},{10... | collective-permute-start | bytes 1228808 | tf_op jit(solution)/shard_map/ppermute | solution.py:323
  98.2 7.1 %collective-permute-start.33 = (bf16[320,128]{1,0:T(8,128)(2,1)S(1)}, bf16[320,128]{1,0:T(8,128)(2,1)S(1)}, u32[]{:S(2)}, u32[]{:S(2)}) collective-permute-start(bf16[320,128]{1,0:T(8,128)(2,1)S(1)} %get-tuple-element.26), channel_id=1, source_target_pairs={{0,2},{1,3},{2,4},{3,5},{4,6},{5,7},{6,0},{7,1},{8,10},{9,11},{10,... | collective-permute-start | bytes 245768 | tf_op jit(solution)/shard_map/ppermute | solution.py:447
  99.1 9.3 %collective-permute-start.34 = (bf16[320,128]{1,0:T(8,128)(2,1)S(1)}, bf16[320,128]{1,0:T(8,128)(2,1)S(1)}, u32[]{:S(2)}, u32[]{:S(2)}) collective-permute-start(bf16[320,128]{1,0:T(8,128)(2,1)S(1)} %get-tuple-element.27), channel_id=1, source_target_pairs={{0,4},{1,5},{2,6},{3,7},{4,0},{5,1},{6,2},{7,3},{8,12},{9,13},{10,... | collective-permute-start | bytes 245768 | tf_op jit(solution)/shard_map/ppermute | solution.py:447
  100.3 8.2 %collective-permute-start.35 = (bf16[320,128]{1,0:T(8,128)(2,1)S(1)}, bf16[320,128]{1,0:T(8,128)(2,1)S(1)}, u32[]{:S(2)}, u32[]{:S(2)}) collective-permute-start(bf16[320,128]{1,0:T(8,128)(2,1)S(1)} %get-tuple-element.28), channel_id=1, source_target_pairs={{0,6},{1,7},{2,0},{3,1},{4,2},{5,3},{6,4},{7,5},{8,14},{9,15},{10,... | collective-permute-start | bytes 245768 | tf_op jit(solution)/shard_map/ppermute | solution.py:447
  (15 other events, 165.4 us)

commit v6 on v5

--- a/solution.py
+++ b/solution.py
@@ -16,9 +16,11 @@
 SET_HEADS = HEADS // OUTER
 SET_CHANNELS = SET_HEADS * HEAD_DIM
 QUAD = 4
+GRANULE = 32
 HANDED = (0, 2, 1, 3)
 FAR = ((1, 0), (2, 0), (3, 0), (2, 1))
 LAST = ((1, 1), (3, 1))
+SOONER, LATER = (1, 2), (3, 0)
 EPSILON = 1e-05
 MEBI = 1024 * 1024
 
@@ -29,22 +31,23 @@
 NN = (((1,), (0,)), ((), ()))
 
 
-def dot(left, right, dims=NN, precision=None):
-    return lax.dot_general(left, right, dims, preferred_element_type=f32, precision=precision)
-
-
-def exact(left, right, dims=NN):
-    return dot(left, right, dims, lax.Precision.HIGHEST)
+def dot(left, right, dims=NN):
+    return lax.dot_general(left, right, dims, preferred_element_type=f32)
+
+
+def exact(row, member, dims=NN):
+    high = row.astype(bf16).astype(f32)
+    middle = (row - high).astype(bf16).astype(f32)
+    parts = [high, middle, row - high - middle, jnp.zeros((13, row.shape[1]), f32)]
+    return jnp.sum(dot(jnp.concatenate(parts, axis=0).astype(bf16), member, dims), axis=0, keepdims=True)
 
 
 def conv_kernel(columns, sources_ref, *refs):
-    count = len(refs) - 8
+    count = len(refs) - 6
     pieces = refs[:count]
-    source_ref, bias_ref = refs[count : count + 2]
+    kernel_ref, bias_ref = refs[count : count + 2]
     out_refs = refs[count + 2 : count + 4]
-    act_ref, kept_ref, kernel_ref, sem = refs[count + 4 :]
-    load = pltpu.make_async_copy(source_ref, kernel_ref, sem)
-    load.start()
+    act_ref, kept_ref = refs[count + 4 :]
     block = pieces[0].shape[0]
     positions = block * count
     own = out_refs[0].shape[0]
@@ -65,12 +68,11 @@
     member = (
         lax.broadcasted_iota(jnp.int32, (C, 128), 0) // SPAN
         == lax.broadcasted_iota(jnp.int32, (C, 128), 1)
-    ).astype(f32)
+    ).astype(bf16)
 
     def group_mean(total):
         summed = jnp.sum(total, axis=0, keepdims=True)
-        per_group = exact(jnp.broadcast_to(summed, (8, C)), member) / entries
-        return exact(per_group, member, NT)[0:1, :]
+        return exact(exact(summed, member) / entries, member, NT)
 
     zero = jnp.zeros((chunk, C), f32)
     centre = group_mean(lax.fori_loop(0, steps, add, zero))
@@ -97,16 +99,18 @@
 
     lax.fori_loop(0, steps, activate, 0)
 
+    window = min(C, (own + 127) // 128 * 128 + 128)
+    base = jnp.minimum(lax.div(me * own, 128) * 128, C - window)
+    lanes = pl.ds(pl.multiple_of(base, 128), window)
     choose = (
-        lax.broadcasted_iota(jnp.int32, (own, C), 0) + me * own
-        == lax.broadcasted_iota(jnp.int32, (own, C), 1)
+        lax.broadcasted_iota(jnp.int32, (own, window), 0) + (me * own - base)
+        == lax.broadcasted_iota(jnp.int32, (own, window), 1)
     ).astype(bf16)
     for index in range(0, count, 2):
-        pair = jnp.concatenate([pieces[index][...], pieces[index + 1][...]], axis=0)
+        pair = jnp.concatenate([pieces[index][:, lanes], pieces[index + 1][:, lanes]], axis=0)
         start = pl.multiple_of(starts[index], 2 * block)
         kept_ref[:, pl.ds(start, 2 * block)] = dot(choose, pair, NT)
 
-    load.wait()
     wide = 256
     column = lax.broadcasted_iota(jnp.int32, (own, wide), 1) % columns
     square = (own, own)
@@ -131,9 +135,9 @@
 
 def attention_kernel(count, inner, sources_ref, *refs):
     pieces = refs[:count]
-    parts = refs[count : -8 - OUTER]
-    outs = refs[-8 - OUTER : -8]
-    kept_ref, hidden_ref, normed_ref, weight_ref, query_ref, key_ref, value_ref, sems = refs[-8:]
+    parts = refs[count:-9]
+    outs = refs[-9:-7]
+    kept_ref, later_ref, key_ref, value_ref, normed_ref, weight_ref, sems = refs[-7:]
     own, part = pieces[0].shape
     n = count // 2
     positions = 2 * part
@@ -141,18 +145,11 @@
     me = lax.axis_index("patch")
     outer_at, inner_at = lax.div(me, inner), lax.rem(me, inner)
     entries = float(positions * SPAN)
-
-    copies = []
-    for index, piece in enumerate(pieces):
-        row = pl.multiple_of(sources_ref[me * count + index] * own, own)
-        low = (index % 2) * part
-        target = hidden_ref.at[pl.ds(row, own), low : low + part]
-        copies.append(pltpu.make_async_copy(piece, target, sems.at[index]))
     loads = []
 
     def load(source, row):
         target = weight_ref.at[pl.ds(row, source.shape[0]), :]
-        loads.append(pltpu.make_async_copy(source, target, sems.at[count + len(loads)]))
+        loads.append(pltpu.make_async_copy(source, target, sems.at[len(loads)]))
 
     if inner == 2:
         for kind in range(3):
@@ -160,27 +157,53 @@
             load(parts[kind], pl.multiple_of(row, own))
         mine = lax.rem(lax.axis_index("batch"), QUAD)
         for step, part_ref in zip(HANDED, parts[3:]):
-            row = jnp.bitwise_xor(mine, step) * SET_CHANNELS + (1 - inner_at) * own
-            load(part_ref, pl.multiple_of(row, own))
+            place = jnp.bitwise_xor(mine, step)
+            first = quarter_start(place, own)
+            twice = QUAD * (part_ref.shape[0] // GRANULE) - 3 * own // GRANULE
+            for at in range(part_ref.shape[0] // GRANULE):
+                granule = first + at
+                kind = lax.div(granule, own // GRANULE)
+                row = kind * SET_CHANNELS + (1 - inner_at) * own
+                row = row + lax.rem(granule, own // GRANULE) * GRANULE
+                if at < twice:
+                    spare = 3 * SET_CHANNELS + at * GRANULE
+                    row = jnp.where(place == QUAD - 1, spare, row)
+                source = part_ref.at[at * GRANULE : (at + 1) * GRANULE, :]
+                load(source, pl.multiple_of(row, GRANULE))
     else:
         load(parts[0], 0)
-    for copy in copies + loads:
+    for copy in loads:
         copy.start()
-    for copy in copies:
-        copy.wait()
-
-    kept_ref[...] = hidden_ref[:, pl.ds(pl.multiple_of(me * block, block), block)]
-    for at in range(0, C, 2 * SPAN):
-        pair = hidden_ref[at : at + 2 * SPAN, :].astype(f32)
-        scaled = []
-        for low in (0, SPAN):
-            group = pair[low : low + SPAN]
-            mean = jnp.sum(jnp.sum(group, axis=0, keepdims=True), axis=1, keepdims=True) / entries
-            away = group - mean
-            square = jnp.sum(away * away, axis=0, keepdims=True)
-            var = jnp.sum(square, axis=1, keepdims=True) / entries
-            scaled.append(away * lax.rsqrt(var + EPSILON))
-        normed_ref[at : at + 2 * SPAN, :] = jnp.concatenate(scaled, axis=0).astype(bf16)
+
+    groups = [(at, low) for at in range(0, count, 2) for low in range(0, own, SPAN)]
+
+    def whole(values):
+        return jnp.sum(jnp.sum(values, axis=0, keepdims=True), axis=1, keepdims=True)
+
+    def group_of(at, low):
+        halves = []
+        for piece in pieces[at : at + 2]:
+            first = low // 16 * 16
+            rows = piece[first : -(-(low + SPAN) // 16) * 16, :].astype(f32)
+            halves.append(rows[low - first : low - first + SPAN])
+        return halves
+
+    means = [sum(whole(half) for half in group_of(*group)) / entries for group in groups]
+    scales = []
+    for mean, group in zip(means, groups):
+        square = sum(whole(jnp.square(half - mean)) for half in group_of(*group))
+        scales.append(lax.rsqrt(square / entries + EPSILON))
+    for at in range(0, count, 2):
+        row = pl.multiple_of(sources_ref[me * count + at] * own, own)
+        which = [index for index, group in enumerate(groups) if group[0] == at]
+        mean = jnp.concatenate([jnp.broadcast_to(means[index], (SPAN, 1)) for index in which], axis=0)
+        scale = jnp.concatenate([jnp.broadcast_to(scales[index], (SPAN, 1)) for index in which], axis=0)
+        for half, piece in enumerate(pieces[at : at + 2]):
+            normed = (piece[...].astype(f32) - mean) * scale
+            normed_ref[pl.ds(row, own), half * part : (half + 1) * part] = normed.astype(bf16)
+        start = pl.multiple_of(lax.rem(me, n // 2) * block, block)
+        low, high = (piece[:, pl.ds(start, block)] for piece in pieces[at : at + 2])
+        kept_ref[pl.ds(row, own), :] = jnp.where(me < n // 2, low, high)
 
     for copy in loads:
         copy.wait()
@@ -192,27 +215,34 @@
             key_ref[head, at : at + wide, :] = made[low : low + HEAD_DIM].T.astype(bf16)
         value_ref[:, at : at + wide] = made[SET_CHANNELS:].astype(bf16)
 
-    for at in range(0, OUTER, 2):
+    def queries(steps):
         normed = []
-        for step in (at, at + 1):
+        for step in steps:
             target = lax.rem(outer_at + step, OUTER) * inner + inner_at
             normed.append(normed_ref[:, pl.ds(pl.multiple_of(target * block, block), block)])
         made = dot(weight_ref[:SET_CHANNELS, :], jnp.concatenate(normed, axis=1))
-        scaled = made.astype(bf16).astype(f32) * HEAD_DIM ** (-0.5)
-        query_ref[:, at * block : (at + 2) * block] = scaled.astype(bf16)
-
-    for at in range(0, OUTER, 2):
-        for head in range(SET_HEADS):
-            low = head * HEAD_DIM
-            query = query_ref[low : low + HEAD_DIM, at * block : (at + 2) * block]
-            scores = dot(key_ref[head], query)
-            peak = jnp.max(scores, axis=0, keepdims=True)
-            unnormalized = jnp.exp(scores - peak)
-            total = jnp.sum(unnormalized, axis=0, keepdims=True)
-            mixture = dot(value_ref[low : low + HEAD_DIM, :], unnormalized.astype(bf16))
-            attended = (mixture / total).astype(bf16)
-            outs[at][low : low + HEAD_DIM, :] = attended[:, :block]
-            outs[at + 1][low : low + HEAD_DIM, :] = attended[:, block:]
+        return (made.astype(bf16).astype(f32) * HEAD_DIM ** (-0.5)).astype(bf16)
+
+    later_ref[...] = queries(LATER)
+    attend(queries(SOONER), key_ref, value_ref, outs)
+
+
+def later_kernel(query_ref, key_ref, value_ref, *outs):
+    attend(query_ref[...], key_ref, value_ref, outs)
+
+
+def attend(query, key_ref, value_ref, outs):
+    block = outs[0].shape[1]
+    for head in range(SET_HEADS):
+        low = head * HEAD_DIM
+        scores = dot(key_ref[head], query[low : low + HEAD_DIM])
+        peak = jnp.max(scores, axis=0, keepdims=True)
+        unnormalized = jnp.exp(scores - peak)
+        total = jnp.sum(unnormalized, axis=0, keepdims=True)
+        mixture = dot(value_ref[low : low + HEAD_DIM, :], unnormalized.astype(bf16))
+        attended = (mixture / total).astype(bf16)
+        for place, out in enumerate(outs):
+            out[low : low + HEAD_DIM, :] = attended[:, place * block : (place + 1) * block]
 
 
 def output_kernel(n, *refs):
@@ -236,33 +266,34 @@
 
     total_ref[...] = hidden_ref[...].astype(f32)
     mine = lax.rem(lax.axis_index("batch"), QUAD)
-    near, far = weight_refs[1 : 1 + QUAD], blocks_of(weight_refs[-4:-2], own)
-
-    def add(weight_ref, outer_step, inner_step):
+    core = lax.rem(mine, 2)
+
+    def add(weights, outer_step, inner_step, low=0):
         origin = lax.rem(outer_at + OUTER - outer_step, OUTER) * inner
         origin = origin + lax.rem(inner_at + inner_step, inner)
-        rows = pl.ds(pl.multiple_of(origin * own, own), own)
-        total_ref[rows, :] += dot(weight_ref[...], attended)
-
-    add(weight_refs[0], 0, 0)
-    for step, weight_ref in zip(HANDED, near):
-
-        @pl.when(jnp.bitwise_xor(mine, step) == QUAD - 1)
-        def _(weight_ref=weight_ref):
-            add(weight_ref, 0, 1)
-
-    for step, weight_ref in zip(HANDED, far):
-        holder = jnp.bitwise_xor(mine, step)
-        outer_step = jnp.where(holder == 0, 1, jnp.where(holder == 2, 3, 2))
-        add(weight_ref, outer_step, lax.div(holder, QUAD - 1))
-    core = lax.rem(mine, 2)
-    for which, weight_ref in zip((core, 1 - core), weight_refs[-2:]):
-        add(weight_ref, 1 + 2 * which, 1)
+        rows = pl.ds(pl.multiple_of(origin * own + low, 16), weights.shape[0])
+        total_ref[rows, :] += dot(weights, attended)
+
+    own_ref, far_ref, far_other_ref, last_ref, last_other_ref = weight_refs
+    add(own_ref[...], 0, 0)
+    for holder, ref in ((mine, far_ref), (jnp.bitwise_xor(mine, 1), far_other_ref)):
+        for step in (0, 1):
+            which = jnp.bitwise_xor(holder, 2 * step)
+            outer_step = jnp.where(which == 0, 1, jnp.where(which == 2, 3, 2))
+            add(ref[step * own : (step + 1) * own, :], outer_step, lax.div(which, QUAD - 1))
+        add(ref[2 * own :, :], 0, 1, lax.rem(holder, 2) * (own // 2))
+    add(last_ref[...], 1 + 2 * core, 1)
+    add(last_other_ref[...], 3 - 2 * core, 1)
     out_ref[...] = total_ref[...].T.astype(bf16)
 
 
-def blocks_of(refs, rows):
-    return [ref.at[at : at + rows, :] for ref in refs for at in range(0, ref.shape[0], rows)]
+def quarter_rows(own):
+    return -(-3 * own // (QUAD * GRANULE)) * GRANULE
+
+
+def quarter_start(place, own):
+    part = quarter_rows(own) // GRANULE
+    return jnp.minimum(place * part, 3 * own // GRANULE - part)
 
 
 def ring_of(n):
@@ -363,13 +394,21 @@
     whole = latent.reshape(block, channels)
     halves = whole[: block // 2], whole[block // 2 :]
     if inner == 2:
-        place = lax.rem(lax.axis_index("batch"), QUAD)
-        chosen = jnp.where(place == 0, w_query, jnp.where(place == 1, w_key, w_value))
-        chosen = jnp.where(place == 3, w_out, chosen)
+        quarter = quarter_rows(own)
+        core = lax.rem(lax.axis_index("batch"), 2)
+        start = quarter_start(lax.rem(lax.axis_index("batch"), QUAD), own) * GRANULE
+        stacked = jnp.concatenate([w_query, w_key, w_value], axis=0)
+        chosen = jnp.concatenate(
+            [
+                lax.dynamic_slice_in_dim(stacked, start, quarter, 0),
+                lax.dynamic_slice_in_dim(w_out, core * (own // 2), own // 2, 0),
+            ],
+            axis=0,
+        )
         pieces = gather(halves, n, [chosen])
         chosen, out_own = after([chosen, w_out], pieces[-5:])
-        near = [send(chosen, [(0, 1)])]
-        far = [send(out_own, FAR)]
+        chosen = send(chosen, [(0, 1)])
+        far = send(out_own, FAR)
     else:
         pieces = gather(halves, n)
         sets = [list(range(at, at + inner)) for at in range(0, n, inner)]
@@ -381,13 +420,11 @@
     hidden = pl.pallas_call(
         functools.partial(conv_kernel, columns),
         out_shape=[jax.ShapeDtypeStruct((own, positions // 2), bf16)] * 2,
-        in_specs=[smem] + [vmem] * (2 * n) + [anywhere, vmem],
+        in_specs=[smem] + [vmem] * (2 * n + 2),
         out_specs=[vmem] * 2,
         scratch_shapes=[
             pltpu.VMEM((positions + 2 * columns, channels), bf16),
             pltpu.VMEM((own, positions), f32),
-            pltpu.VMEM((3, 3 * own, channels), bf16),
-            pltpu.SemaphoreType.DMA,
         ],
         compiler_params=pltpu.CompilerParams(vmem_limit_bytes=20 * MEBI),
         cost_estimate=pl.CostEstimate(
@@ -405,7 +442,8 @@
 
     hidden_pieces = gather(tuple(hidden), n)
     if inner == 2:
-        *near, far = after(near + far, hidden[:1])
+        chosen, far = after([chosen, far], hidden[:1])
+        near = [chosen[:quarter]]
         near.append(swap(near[0], 2))
         near += [swap(one, 1) for one in near]
         weights = [w_query, w_key, w_value] + near
@@ -413,38 +451,60 @@
         across = swap(far, 2)
         last = send(out_own, LAST)
 
-    *attended, kept = pl.pallas_call(
+    pair = [jax.ShapeDtypeStruct((SET_CHANNELS, block), bf16)] * 2
+    attended = {}
+    attended[SOONER[0]], attended[SOONER[1]], kept, query, key, value = pl.pallas_call(
         functools.partial(attention_kernel, 2 * n, inner),
-        out_shape=[jax.ShapeDtypeStruct((SET_CHANNELS, block), bf16)] * OUTER
-        + [jax.ShapeDtypeStruct((channels, block), bf16)],
-        in_specs=[smem] + [anywhere] * (2 * n + len(weights)),
-        out_specs=[vmem] * (OUTER + 1),
+        out_shape=pair
+        + [
+            jax.ShapeDtypeStruct((channels, block), bf16),
+            jax.ShapeDtypeStruct((SET_CHANNELS, 2 * block), bf16),
+            jax.ShapeDtypeStruct((SET_HEADS, positions, HEAD_DIM), bf16),
+            jax.ShapeDtypeStruct((SET_CHANNELS, positions), bf16),
+        ],
+        in_specs=[smem] + [vmem] * (2 * n) + [anywhere] * len(weights),
+        out_specs=[vmem] * 6,
         scratch_shapes=[
             pltpu.VMEM((channels, positions), bf16),
-            pltpu.VMEM((channels, positions), bf16),
             pltpu.VMEM((QUAD * SET_CHANNELS, channels), bf16),
-            pltpu.VMEM((SET_CHANNELS, OUTER * block), bf16),
-            pltpu.VMEM((SET_HEADS, positions, HEAD_DIM), bf16),
-            pltpu.VMEM((SET_CHANNELS, positions), bf16),
-            pltpu.SemaphoreType.DMA((2 * n + 3 + QUAD,)),
+            pltpu.SemaphoreType.DMA((3 + QUAD * quarter_rows(own) // GRANULE,)),
         ],
         compiler_params=pltpu.CompilerParams(vmem_limit_bytes=28 * MEBI),
         cost_estimate=pl.CostEstimate(
             flops=2 * positions * channels * 3 * SET_CHANNELS
-            + 4 * positions * OUTER * block * SET_CHANNELS,
+            + 8 * positions * block * SET_CHANNELS,
             bytes_accessed=2 * (positions * channels + 3 * SET_CHANNELS * channels),
-            transcendentals=positions * OUTER * block * SET_HEADS,
+            transcendentals=positions * 2 * block * SET_HEADS,
         ),
         name="attention",
     )(sources, *hidden_pieces, *weights)
-
+    attended[LATER[0]], attended[LATER[1]] = pl.pallas_call(
+        later_kernel,
+        out_shape=pair,
+        in_specs=[vmem] * 3,
+        out_specs=[vmem] * 2,
+        compiler_params=pltpu.CompilerParams(vmem_limit_bytes=16 * MEBI),
+        cost_estimate=pl.CostEstimate(
+            flops=8 * positions * block * SET_CHANNELS,
+            bytes_accessed=8 * positions * SET_CHANNELS,
+            transcendentals=positions * 2 * block * SET_HEADS,
+        ),
+        name="later_attention",
+    )(query, key, value)
+
+    def hand_over(step):
+        pairs = [(at, (at + step * inner) % n) for at in range(n)]
+        return lax.ppermute(attended[step], "patch", pairs)
+
+    received = {step: hand_over(step) for step in SOONER}
+    first, last_step = list(received.values()), LATER[0]
+    (attended[last_step],) = after([attended[last_step]], first)
+    received[last_step] = hand_over(last_step)
+    received[0] = attended[0]
     if inner == 2:
-        far, last = after([jnp.concatenate([far, across], axis=0), last], [kept])
-        out_weights = [w_out] + near + [far, swap(far, 1), last, swap(last, 1)]
-    received = [attended[0]]
-    for step in range(1, OUTER):
-        pairs = [(at, (at + step * inner) % n) for at in range(n)]
-        received.append(lax.ppermute(attended[step], "patch", pairs))
+        far = jnp.concatenate([far, across, chosen[quarter:]], axis=0)
+        far, last = after([far, last], [attended[SOONER[0]]])
+        out_weights = [w_out, far, swap(far, 1), last, swap(last, 1)]
 
     output = pl.pallas_call(
         functools.partial(output_kernel, n),
@@ -462,7 +522,7 @@
             transcendentals=0,
         ),
         name="project",
-    )(*received, kept, *out_weights)
+    )(*[received[step] for step in range(OUTER)], kept, *out_weights)
     return output.reshape(rows_local, columns, channels)
 
 

time: 111 us -> 108 us (0.973)
  waiting for transfers between devices: 33.9 us -> 30.8 us
  starting transfers between devices: 46.9 us -> 48.7 us
  Pallas kernels: 27.3 us -> 25.5 us
    ppermute x28, waiting for transfers between devices: 28.6 us -> 23.8 us  [gather(): lax.ppermute(found[half, sign * (step - 1)], 'patch', pairs)]
    pallas_call x0 -> x1, Pallas kernels: none -> 3.36 us  [on_device(): pl.pallas_call(later_kernel, out_shape=pair, in_specs=[vmem] * 3, out_spe...]
    pallas_call x1, Pallas kernels: 10.9 us -> 8.43 us  [on_device(): pl.pallas_call(functools.partial(conv_kernel, columns), out_shape=[jax.Sh...]
    ppermute x28, starting transfers between devices: 30.8 us -> 33.2 us  [gather(): lax.ppermute(found[half, sign * (step - 1)], 'patch', pairs)]
    pallas_call x1, Pallas kernels: 14 us -> 11.7 us  [on_device(): pl.pallas_call(functools.partial(attention_kernel, 2 * n, inner), out_sha...]
    ppermute x6, starting transfers between devices: 6.52 us -> 8.59 us  [swap(): return lax.ppermute(block, 'batch', pairs)]
    ppermute x3, waiting for transfers between devices: 5.27 us -> 7.03 us  [hand_over(): return lax.ppermute(attended[step], 'patch', pairs)]
    ppermute x3, starting transfers between devices: 4.95 us -> 3.25 us  [hand_over(): return lax.ppermute(attended[step], 'patch', pairs)]
  transfers between devices with their start and end apart: 40 -> 40, of which waited for: 20 -> 13; matrix products, arithmetic and copies ran while one was open for 1% -> 1% of each run, Pallas kernels for 23% -> 22%
where the time goes in v6:
time: 108 us
  starting transfers between devices  48.7 us (45%)
  waiting for transfers between devices  30.8 us (29%)
  Pallas kernels  25.5 us (24%)
  local copies, waits for them, and re-layouts  2.13 us (2%)
    ppermute x28, starting transfers between devices, gather(): lax.ppermute(found[half, sign * (step - 1)], 'patch', pairs)  33.2 us
    ppermute x28, waiting for transfers between devices, gather(): lax.ppermute(found[half, sign * (step - 1)], 'patch', pairs)  23.8 us
    pallas_call x1, Pallas kernels, on_device(): pl.pallas_call(functools.partial(attention_kernel, 2 * n, inner), out_sha...  11.7 us
    ppermute x6, starting transfers between devices, swap(): return lax.ppermute(block, 'batch', pairs)  8.59 us
    pallas_call x1, Pallas kernels, on_device(): pl.pallas_call(functools.partial(conv_kernel, columns), out_shape=[jax.Sh...  8.43 us
    ppermute x3, waiting for transfers between devices, hand_over(): return lax.ppermute(attended[step], 'patch', pairs)  7.03 us
    ppermute x3, starting transfers between devices, send(): return lax.ppermute(block, ('batch', 'patch'), pairs)  3.75 us
    pallas_call x1, Pallas kernels, on_device(): pl.pallas_call(later_kernel, out_shape=pair, in_specs=[vmem] * 3, out_spe...  3.36 us
  transfers between devices with their start and end apart: 40, of which 13 were waited for; matrix products, arithmetic and copies ran while one was open for 1% of the time, Pallas kernels for 22%

profile of v6, /device:TPU:0, one launch (start us, length us, event | category | flops | bytes accessed | tf_op | source)
XLA Modules:
  0.0 107.8 jit_solution(3437221411801598320)
XLA Ops:
  1.1 3.1 %collective-permute-start.3 = (bf16[64,1280]{1,0:T(8,128)(2,1)S(1)}, bf16[64,1280]{1,0:T(8,128)(2,1)S(1)}, u32[]{:S(2)}, u32[]{:S(2)}) collective-permute-start(bf16[64,1280]{1,0:T(8,128)(2,1)S(1)} %get-tuple-element.41.refs_1_), channel_id=1, source_target_pairs={{1,0},{3,1},{5,3},{7,5},{6,7},{4,6},{2,4},{0,2},{9,8},{11,9},{13,1... | collective-permute-start | bytes 491528 | tf_op jit(solution)/shard_map/ppermute | solution.py:334
  4.2 2.0 %collective-permute-start.2 = (bf16[64,1280]{1,0:T(8,128)(2,1)S(1)}, bf16[64,1280]{1,0:T(8,128)(2,1)S(1)}, u32[]{:S(2)}, u32[]{:S(2)}) collective-permute-start(bf16[64,1280]{1,0:T(8,128)(2,1)S(1)} %get-tuple-element.42.refs_0_), channel_id=1, source_target_pairs={{1,0},{3,1},{5,3},{7,5},{6,7},{4,6},{2,4},{0,2},{9,8},{11,9},{13,1... | collective-permute-start | bytes 491528 | tf_op jit(solution)/shard_map/ppermute | solution.py:334
  7.6 1.6 %collective-permute-done.3.refs_5_ = bf16[64,1280]{1,0:T(8,128)(2,1)S(1)} collective-permute-done((bf16[64,1280]{1,0:T(8,128)(2,1)S(1)}, bf16[64,1280]{1,0:T(8,128)(2,1)S(1)}, u32[]{:S(2)}, u32[]{:S(2)}) %collective-permute-start.3) | collective-permute-done | bytes 163872 | tf_op jit(solution)/shard_map/ppermute | solution.py:334
  9.1 2.1 %collective-permute-start.7 = (bf16[64,1280]{1,0:T(8,128)(2,1)S(1)}, bf16[64,1280]{1,0:T(8,128)(2,1)S(1)}, u32[]{:S(2)}, u32[]{:S(2)}) collective-permute-start(bf16[64,1280]{1,0:T(8,128)(2,1)S(1)} %collective-permute-done.3.refs_5_), channel_id=1, source_target_pairs={{1,0},{3,1},{5,3},{7,5},{6,7},{4,6},{2,4},{0,2},{9,8},{11,9},{13,1... | collective-permute-start | bytes 491528 | tf_op jit(solution)/shard_map/ppermute | solution.py:334
  11.3 2.1 %collective-permute-done.refs_0_ = bf16[64,1280]{1,0:T(8,128)(2,1)S(1)} collective-permute-done((bf16[64,1280]{1,0:T(8,128)(2,1)S(1)}, bf16[64,1280]{1,0:T(8,128)(2,1)S(1)}, u32[]{:S(2)}, u32[]{:S(2)}) %collective-permute-start) | collective-permute-done | bytes 163872 | tf_op jit(solution)/shard_map/ppermute | solution.py:334
  13.6 1.7 %collective-permute-start.5 = (bf16[64,1280]{1,0:T(8,128)(2,1)S(1)}, bf16[64,1280]{1,0:T(8,128)(2,1)S(1)}, u32[]{:S(2)}, u32[]{:S(2)}) collective-permute-start(bf16[64,1280]{1,0:T(8,128)(2,1)S(1)} %collective-permute-done.1.refs_3_), channel_id=1, source_target_pairs={{0,1},{1,3},{3,5},{5,7},{7,6},{6,4},{4,2},{2,0},{8,9},{9,11},{11,1... | collective-permute-start | bytes 491528 | tf_op jit(solution)/shard_map/ppermute | solution.py:334
  15.7 1.9 %collective-permute-start.11 = (bf16[64,1280]{1,0:T(8,128)(2,1)S(1)}, bf16[64,1280]{1,0:T(8,128)(2,1)S(1)}, u32[]{:S(2)}, u32[]{:S(2)}) collective-permute-start(bf16[64,1280]{1,0:T(8,128)(2,1)S(1)} %collective-permute-done.7.refs_9_), channel_id=1, source_target_pairs={{1,0},{3,1},{5,3},{7,5},{6,7},{4,6},{2,4},{0,2},{9,8},{11,9},{13,1... | collective-permute-start | bytes 491528 | tf_op jit(solution)/shard_map/ppermute | solution.py:334
  17.5 3.0 %collective-permute-done.4.refs_6_ = bf16[64,1280]{1,0:T(8,128)(2,1)S(1)} collective-permute-done((bf16[64,1280]{1,0:T(8,128)(2,1)S(1)}, bf16[64,1280]{1,0:T(8,128)(2,1)S(1)}, u32[]{:S(2)}, u32[]{:S(2)}) %collective-permute-start.4) | collective-permute-done | bytes 163872 | tf_op jit(solution)/shard_map/ppermute | solution.py:334
  20.8 3.2 %collective-permute-done.5.refs_7_ = bf16[64,1280]{1,0:T(8,128)(2,1)S(1)} collective-permute-done((bf16[64,1280]{1,0:T(8,128)(2,1)S(1)}, bf16[64,1280]{1,0:T(8,128)(2,1)S(1)}, u32[]{:S(2)}, u32[]{:S(2)}) %collective-permute-start.5) | collective-permute-done | bytes 163872 | tf_op jit(solution)/shard_map/ppermute | solution.py:334
  24.3 1.7 %collective-permute-start.10 = (bf16[64,1280]{1,0:T(8,128)(2,1)S(1)}, bf16[64,1280]{1,0:T(8,128)(2,1)S(1)}, u32[]{:S(2)}, u32[]{:S(2)}) collective-permute-start(bf16[64,1280]{1,0:T(8,128)(2,1)S(1)} %collective-permute-done.6.refs_8_), channel_id=1, source_target_pairs={{1,0},{3,1},{5,3},{7,5},{6,7},{4,6},{2,4},{0,2},{9,8},{11,9},{13,1... | collective-permute-start | bytes 491528 | tf_op jit(solution)/shard_map/ppermute | solution.py:334
  26.0 1.6 %collective-permute-start.13 = (bf16[64,1280]{1,0:T(8,128)(2,1)S(1)}, bf16[64,1280]{1,0:T(8,128)(2,1)S(1)}, u32[]{:S(2)}, u32[]{:S(2)}) collective-permute-start(bf16[64,1280]{1,0:T(8,128)(2,1)S(1)} %collective-permute-done.11.refs_13_.refs_4_), channel_id=1, source_target_pairs={{1,0},{3,1},{5,3},{7,5},{6,7},{4,6},{2,4},{0,2},{9,8},{11,9},{13,1... | collective-permute-start | bytes 491528 | tf_op jit(solution)/shard_map/ppermute | solution.py:334
  28.1 2.3 %collective-permute-done.9.refs_11_.refs_2_ = bf16[64,1280]{1,0:T(8,128)(2,1)S(1)} collective-permute-done((bf16[64,1280]{1,0:T(8,128)(2,1)S(1)}, bf16[64,1280]{1,0:T(8,128)(2,1)S(1)}, u32[]{:S(2)}, u32[]{:S(2)}) %collective-permute-start.9) | collective-permute-done | bytes 163872 | tf_op jit(solution)/shard_map/ppermute | solution.py:334
  31.4 1.6 %collective-permute-done.12.refs_14_.refs_5_ = bf16[64,1280]{1,0:T(8,128)(2,1)S(1)} collective-permute-done((bf16[64,1280]{1,0:T(8,128)(2,1)S(1)}, bf16[64,1280]{1,0:T(8,128)(2,1)S(1)}, u32[]{:S(2)}, u32[]{:S(2)}) %collective-permute-start.12) | collective-permute-done | bytes 163872 | tf_op jit(solution)/shard_map/ppermute | solution.py:334
  34.9 8.4 %norm_conv.1 = (bf16[160,512]{1,0:T(8,128)(2,1)S(1)}, bf16[160,512]{1,0:T(8,128)(2,1)S(1)}) custom-call(s32[128]{0:T(128)S(1)} %copy-done.6, bf16[64,1280]{1,0:T(8,128)(2,1)S(1)} %get-tuple-element.42.refs_0_, bf16[64,1280]{1,0:T(8,128)(2,1)S(1)} %get-tuple-element.41.refs_1_, bf16[64,1280]{1,0:T(8,128)(2,1)S(1)} %after.6.refs_2_, ...), custom_call_target="tpu_custom_call" | custom-call | flops 3774873600 | bytes 6307840 | tf_op jit(solution)/shard_map/norm_conv/pallas_call | solution.py:420
  43.4 1.8 %collective-permute-start.17 = (bf16[160,512]{1,0:T(8,128)(2,1)S(1)}, bf16[160,512]{1,0:T(8,128)(2,1)S(1)}, u32[]{:S(2)}, u32[]{:S(2)}) collective-permute-start(bf16[160,512]{1,0:T(8,128)(2,1)S(1)} %get-tuple-element.24.refs_1_), channel_id=1, source_target_pairs={{1,0},{3,1},{5,3},{7,5},{6,7},{4,6},{2,4},{0,2},{9,8},{11,9},{13,1... | collective-permute-start | bytes 491528 | tf_op jit(solution)/shard_map/ppermute | solution.py:334
  45.4 1.8 %collective-permute-start.14 = (bf16[160,512]{1,0:T(8,128)(2,1)S(1)}, bf16[160,512]{1,0:T(8,128)(2,1)S(1)}, u32[]{:S(2)}, u32[]{:S(2)}) collective-permute-start(bf16[160,512]{1,0:T(8,128)(2,1)S(1)} %get-tuple-element.23.refs_2_.refs_0_), channel_id=1, source_target_pairs={{0,1},{1,3},{3,5},{5,7},{7,6},{6,4},{4,2},{2,0},{8,9},{9,11},{11,1... | collective-permute-start | bytes 491528 | tf_op jit(solution)/shard_map/ppermute | solution.py:334
  47.5 4.9 %collective-permute-start.30 = (bf16[128,1280]{1,0:T(8,128)(2,1)S(1)}, bf16[128,1280]{1,0:T(8,128)(2,1)S(1)}, u32[]{:S(2)}, u32[]{:S(2)}) collective-permute-start(bf16[128,1280]{1,0:T(8,128)(2,1)S(1)} %slice.22.refs_19_.refs_7_), channel_id=1, source_target_pairs={{0,16},{8,24},{16,0},{24,8},{1,17},{9,25},{17,1},{25,9},{2,18},{10... | collective-permute-start | bytes 983048 | tf_op jit(solution)/shard_map/ppermute | solution.py:354
  52.4 2.0 %collective-permute-start.19 = (bf16[160,512]{1,0:T(8,128)(2,1)S(1)}, bf16[160,512]{1,0:T(8,128)(2,1)S(1)}, u32[]{:S(2)}, u32[]{:S(2)}) collective-permute-start(bf16[160,512]{1,0:T(8,128)(2,1)S(1)} %collective-permute-done.15.refs_3_), channel_id=1, source_target_pairs={{0,1},{1,3},{3,5},{5,7},{7,6},{6,4},{4,2},{2,0},{8,9},{9,11},{11,1... | collective-permute-start | bytes 491528 | tf_op jit(solution)/shard_map/ppermute | solution.py:334
  56.5 3.1 %collective-permute-done.21.refs_9_ = bf16[160,512]{1,0:T(8,128)(2,1)S(1)} collective-permute-done((bf16[160,512]{1,0:T(8,128)(2,1)S(1)}, bf16[160,512]{1,0:T(8,128)(2,1)S(1)}, u32[]{:S(2)}, u32[]{:S(2)}) %collective-permute-start.21) | collective-permute-done | bytes 163872 | tf_op jit(solution)/shard_map/ppermute | solution.py:334
  59.6 2.0 %collective-permute-start.23 = (bf16[160,512]{1,0:T(8,128)(2,1)S(1)}, bf16[160,512]{1,0:T(8,128)(2,1)S(1)}, u32[]{:S(2)}, u32[]{:S(2)}) collective-permute-start(bf16[160,512]{1,0:T(8,128)(2,1)S(1)} %collective-permute-done.19.refs_7_), channel_id=1, source_target_pairs={{0,1},{1,3},{3,5},{5,7},{7,6},{6,4},{4,2},{2,0},{8,9},{9,11},{11,1... | collective-permute-start | bytes 491528 | tf_op jit(solution)/shard_map/ppermute | solution.py:334
  62.7 2.5 %collective-permute-start.22 = (bf16[160,512]{1,0:T(8,128)(2,1)S(1)}, bf16[160,512]{1,0:T(8,128)(2,1)S(1)}, u32[]{:S(2)}, u32[]{:S(2)}) collective-permute-start(bf16[160,512]{1,0:T(8,128)(2,1)S(1)} %collective-permute-done.18.refs_6_), channel_id=1, source_target_pairs={{0,1},{1,3},{3,5},{5,7},{7,6},{6,4},{4,2},{2,0},{8,9},{9,11},{11,1... | collective-permute-start | bytes 491528 | tf_op jit(solution)/shard_map/ppermute | solution.py:334
  66.5 2.7 %collective-permute-start.27 = (bf16[160,512]{1,0:T(8,128)(2,1)S(1)}, bf16[160,512]{1,0:T(8,128)(2,1)S(1)}, u32[]{:S(2)}, u32[]{:S(2)}) collective-permute-start(bf16[160,512]{1,0:T(8,128)(2,1)S(1)} %collective-permute-done.25.refs_13_.refs_4_), channel_id=1, source_target_pairs={{1,0},{3,1},{5,3},{7,5},{6,7},{4,6},{2,4},{0,2},{9,8},{11,9},{13,1... | collective-permute-start | bytes 491528 | tf_op jit(solution)/shard_map/ppermute | solution.py:334
  70.5 2.3 %collective-permute-done.24.refs_12_.refs_3_ = bf16[160,512]{1,0:T(8,128)(2,1)S(1)} collective-permute-done((bf16[160,512]{1,0:T(8,128)(2,1)S(1)}, bf16[160,512]{1,0:T(8,128)(2,1)S(1)}, u32[]{:S(2)}, u32[]{:S(2)}) %collective-permute-start.24) | collective-permute-done | bytes 163872 | tf_op jit(solution)/shard_map/ppermute | solution.py:334
  72.7 2.6 %collective-permute-done.27.refs_15_.refs_6_ = bf16[160,512]{1,0:T(8,128)(2,1)S(1)} collective-permute-done((bf16[160,512]{1,0:T(8,128)(2,1)S(1)}, bf16[160,512]{1,0:T(8,128)(2,1)S(1)}, u32[]{:S(2)}, u32[]{:S(2)}) %collective-permute-start.27) | collective-permute-done | bytes 163872 | tf_op jit(solution)/shard_map/ppermute | solution.py:334
  75.4 1.6 %collective-permute-start.36 = (bf16[160,1280]{1,0:T(8,128)(2,1)S(1)}, bf16[160,1280]{1,0:T(8,128)(2,1)S(1)}, u32[]{:S(2)}, u32[]{:S(2)}) collective-permute-start(bf16[160,1280]{1,0:T(8,128)(2,1)S(1)} %get-tuple-element.37), channel_id=1, source_target_pairs={{0,16},{8,24},{16,0},{24,8},{1,17},{9,25},{17,1},{25,9},{2,18},{10... | collective-permute-start | bytes 1228808 | tf_op jit(solution)/shard_map/ppermute | solution.py:354
  77.0 1.8 %collective-permute-start.37 = (bf16[160,1280]{1,0:T(8,128)(2,1)S(1)}, bf16[160,1280]{1,0:T(8,128)(2,1)S(1)}, u32[]{:S(2)}, u32[]{:S(2)}) collective-permute-start(bf16[160,1280]{1,0:T(8,128)(2,1)S(1)} %get-tuple-element.38), channel_id=1, source_target_pairs={{0,3},{1,2},{2,5},{3,4},{4,7},{5,6},{6,1},{7,0},{8,15},{9,14},{10,... | collective-permute-start | bytes 1228808 | tf_op jit(solution)/shard_map/ppermute | solution.py:349
  78.8 11.7 %attention.1 = (bf16[320,128]{1,0:T(8,128)(2,1)S(1)}, bf16[320,128]{1,0:T(8,128)(2,1)S(1)}, bf16[1280,128]{1,0:T(8,128)(2,1)S(1)}, bf16[320,256]{1,0:T(8,128)(2,...) custom-call(s32[128]{0:T(128)S(1)} %copy-done.6, ...), custom_call_target="tpu_custom_call" | custom-call | flops 2852126720 | bytes 5079040 | tf_op jit(solution)/shard_map/attention/pallas_call | solution.py:456
  92.2 2.5 %collective-permute-start.34 = (bf16[320,128]{1,0:T(8,128)(2,1)S(1)}, bf16[320,128]{1,0:T(8,128)(2,1)S(1)}, u32[]{:S(2)}, u32[]{:S(2)}) collective-permute-start(bf16[320,128]{1,0:T(8,128)(2,1)S(1)} %get-tuple-element.33), channel_id=1, source_target_pairs={{0,4},{1,5},{2,6},{3,7},{4,0},{5,1},{6,2},{7,3},{8,12},{9,13},{10,... | collective-permute-start | bytes 245768 | tf_op jit(solution)/shard_map/ppermute | solution.py:497
  94.8 3.4 %later_attention.1 = (bf16[320,128]{1,0:T(8,128)(2,1)S(1)}, bf16[320,128]{1,0:T(8,128)(2,1)S(1)}) custom-call(bf16[320,256]{1,0:T(8,128)(2,1)S(1)} %get-tuple-element.28.query_ref, bf16[5,1024,64]{2,1,0:T(8,128)(2,1)S(1)} %get-tuple-element.29.key_ref, bf16[320,1024]{1,0:T(8,128)(2,1)S(1)} %get-tuple-element.30.value_ref), custom_call_target="tpu_custom_call" | custom-call | flops 335544320 | bytes 2621440 | tf_op jit(solution)/shard_map/later_attention/pallas_call | solution.py:481
  98.1 3.3 %collective-permute-done.34.refs_2_ = bf16[320,128]{1,0:T(8,128)(2,1)S(1)} collective-permute-done((bf16[320,128]{1,0:T(8,128)(2,1)S(1)}, bf16[320,128]{1,0:T(8,128)(2,1)S(1)}, u32[]{:S(2)}, u32[]{:S(2)}) %collective-permute-start.34) | collective-permute-done | bytes 81952 | tf_op jit(solution)/shard_map/ppermute | solution.py:497
  102.1 3.8 %collective-permute-done.35.refs_3_ = bf16[320,128]{1,0:T(8,128)(2,1)S(1)} collective-permute-done((bf16[320,128]{1,0:T(8,128)(2,1)S(1)}, bf16[320,128]{1,0:T(8,128)(2,1)S(1)}, u32[]{:S(2)}, u32[]{:S(2)}) %collective-permute-start.35) | collective-permute-done | bytes 81952 | tf_op jit(solution)/shard_map/ppermute | solution.py:497
  105.8 2.0 %project.1 = bf16[128,1280]{1,0:T(8,128)(2,1)} custom-call(bf16[320,128]{1,0:T(8,128)(2,1)S(1)} %get-tuple-element.31.refs_0_, bf16[320,128]{1,0:T(8,128)(2,1)S(1)} %collective-permute-done.33.refs_1_, bf16[320,128]{1,0:T(8,128)(2,1)S(1)} %collective-permute-done.34.refs_2_, bf16[320,128]{1,0:T(8,128)(2,1)S(1)} %collective-permute-done.35.refs_3_, ...), custom_call_target="tpu_custom_call" | custom-call | flops 419430400 | bytes 4259840 | tf_op jit(solution)/shard_map/project/pallas_call | solution.py:509
  (80 shorter events, 15.6 us)
Async XLA Ops:
  1.1 8.0 %collective-permute-start.3 = (bf16[64,1280]{1,0:T(8,128)(2,1)S(1)}, bf16[64,1280]{1,0:T(8,128)(2,1)S(1)}, u32[]{:S(2)}, u32[]{:S(2)}) collective-permute-start(bf16[64,1280]{1,0:T(8,128)(2,1)S(1)} %get-tuple-element.41.refs_1_), channel_id=1, source_target_pairs={{1,0},{3,1},{5,3},{7,5},{6,7},{4,6},{2,4},{0,2},{9,8},{11,9},{13,1... | collective-permute-start | bytes 491528 | tf_op jit(solution)/shard_map/ppermute | solution.py:334
  4.2 9.5 %collective-permute-start.1 = (bf16[64,1280]{1,0:T(8,128)(2,1)S(1)}, bf16[64,1280]{1,0:T(8,128)(2,1)S(1)}, u32[]{:S(2)}, u32[]{:S(2)}) collective-permute-start(bf16[64,1280]{1,0:T(8,128)(2,1)S(1)} %get-tuple-element.41.refs_1_), channel_id=1, source_target_pairs={{0,1},{1,3},{3,5},{5,7},{7,6},{6,4},{4,2},{2,0},{8,9},{9,11},{11,1... | collective-permute-start | bytes 491528 | tf_op jit(solution)/shard_map/ppermute | solution.py:334
  4.2 11.1 %collective-permute-start.2 = (bf16[64,1280]{1,0:T(8,128)(2,1)S(1)}, bf16[64,1280]{1,0:T(8,128)(2,1)S(1)}, u32[]{:S(2)}, u32[]{:S(2)}) collective-permute-start(bf16[64,1280]{1,0:T(8,128)(2,1)S(1)} %get-tuple-element.42.refs_0_), channel_id=1, source_target_pairs={{1,0},{3,1},{5,3},{7,5},{6,7},{4,6},{2,4},{0,2},{9,8},{11,9},{13,1... | collective-permute-start | bytes 491528 | tf_op jit(solution)/shard_map/ppermute | solution.py:334
  6.2 7.1 %collective-permute-start = (bf16[64,1280]{1,0:T(8,128)(2,1)S(1)}, bf16[64,1280]{1,0:T(8,128)(2,1)S(1)}, u32[]{:S(2)}, u32[]{:S(2)}) collective-permute-start(bf16[64,1280]{1,0:T(8,128)(2,1)S(1)} %get-tuple-element.42.refs_0_), channel_id=1, source_target_pairs={{0,1},{1,3},{3,5},{5,7},{7,6},{6,4},{4,2},{2,0},{8,9},{9,11},{11,1... | collective-permute-start | bytes 491528 | tf_op jit(solution)/shard_map/ppermute | solution.py:334
  13.4 7.1 %collective-permute-start.4 = (bf16[64,1280]{1,0:T(8,128)(2,1)S(1)}, bf16[64,1280]{1,0:T(8,128)(2,1)S(1)}, u32[]{:S(2)}, u32[]{:S(2)}) collective-permute-start(bf16[64,1280]{1,0:T(8,128)(2,1)S(1)} %after.6.refs_2_), channel_id=1, source_target_pairs={{0,1},{1,3},{3,5},{5,7},{7,6},{6,4},{4,2},{2,0},{8,9},{9,11},{11,1... | collective-permute-start | bytes 491528 | tf_op jit(solution)/shard_map/ppermute | solution.py:334
  13.6 10.4 %collective-permute-start.5 = (bf16[64,1280]{1,0:T(8,128)(2,1)S(1)}, bf16[64,1280]{1,0:T(8,128)(2,1)S(1)}, u32[]{:S(2)}, u32[]{:S(2)}) collective-permute-start(bf16[64,1280]{1,0:T(8,128)(2,1)S(1)} %collective-permute-done.1.refs_3_), channel_id=1, source_target_pairs={{0,1},{1,3},{3,5},{5,7},{7,6},{6,4},{4,2},{2,0},{8,9},{9,11},{11,1... | collective-permute-start | bytes 491528 | tf_op jit(solution)/shard_map/ppermute | solution.py:334
  15.3 9.0 %collective-permute-start.6 = (bf16[64,1280]{1,0:T(8,128)(2,1)S(1)}, bf16[64,1280]{1,0:T(8,128)(2,1)S(1)}, u32[]{:S(2)}, u32[]{:S(2)}) collective-permute-start(bf16[64,1280]{1,0:T(8,128)(2,1)S(1)} %collective-permute-done.2.refs_4_), channel_id=1, source_target_pairs={{1,0},{3,1},{5,3},{7,5},{6,7},{4,6},{2,4},{0,2},{9,8},{11,9},{13,1... | collective-permute-start | bytes 491528 | tf_op jit(solution)/shard_map/ppermute | solution.py:334
  15.7 10.4 %collective-permute-start.11 = (bf16[64,1280]{1,0:T(8,128)(2,1)S(1)}, bf16[64,1280]{1,0:T(8,128)(2,1)S(1)}, u32[]{:S(2)}, u32[]{:S(2)}) collective-permute-start(bf16[64,1280]{1,0:T(8,128)(2,1)S(1)} %collective-permute-done.7.refs_9_), channel_id=1, source_target_pairs={{1,0},{3,1},{5,3},{7,5},{6,7},{4,6},{2,4},{0,2},{9,8},{11,9},{13,1... | collective-permute-start | bytes 491528 | tf_op jit(solution)/shard_map/ppermute | solution.py:334
  20.5 7.1 %collective-permute-start.8 = (bf16[64,1280]{1,0:T(8,128)(2,1)S(1)}, bf16[64,1280]{1,0:T(8,128)(2,1)S(1)}, u32[]{:S(2)}, u32[]{:S(2)}) collective-permute-start(bf16[64,1280]{1,0:T(8,128)(2,1)S(1)} %collective-permute-done.4.refs_6_), channel_id=1, source_target_pairs={{0,1},{1,3},{3,5},{5,7},{7,6},{6,4},{4,2},{2,0},{8,9},{9,11},{11,1... | collective-permute-start | bytes 491528 | tf_op jit(solution)/shard_map/ppermute | solution.py:334
  32.9 14.5 %collective-permute-start.28 = (bf16[208,1280]{1,0:T(8,128)(2,1)S(1)}, bf16[208,1280]{1,0:T(8,128)(2,1)S(1)}, u32[]{:S(2)}, u32[]{:S(2)}) collective-permute-start(bf16[208,1280]{1,0:T(8,128)(2,1)S(1)} %get-tuple-element.25), channel_id=1, source_target_pairs={{0,1},{1,0},{2,3},{3,2},{4,5},{5,4},{6,7},{7,6},{8,9},{9,8},{10,11... | collective-permute-start | bytes 1597448 | tf_op jit(solution)/shard_map/ppermute | solution.py:349
  33.4 13.8 %collective-permute-start.29 = (bf16[160,1280]{1,0:T(8,128)(2,1)S(1)}, bf16[160,1280]{1,0:T(8,128)(2,1)S(1)}, u32[]{:S(2)}, u32[]{:S(2)}) collective-permute-start(bf16[160,1280]{1,0:T(8,128)(2,1)S(1)} %get-tuple-element.26.refs_1_), channel_id=1, source_target_pairs={{0,2},{1,3},{2,4},{3,5},{4,6},{5,7},{6,0},{7,1},{8,12},{9,13},{10,... | collective-permute-start | bytes 1228808 | tf_op jit(solution)/shard_map/ppermute | solution.py:349
  43.4 9.1 %collective-permute-start.17 = (bf16[160,512]{1,0:T(8,128)(2,1)S(1)}, bf16[160,512]{1,0:T(8,128)(2,1)S(1)}, u32[]{:S(2)}, u32[]{:S(2)}) collective-permute-start(bf16[160,512]{1,0:T(8,128)(2,1)S(1)} %get-tuple-element.24.refs_1_), channel_id=1, source_target_pairs={{1,0},{3,1},{5,3},{7,5},{6,7},{4,6},{2,4},{0,2},{9,8},{11,9},{13,1... | collective-permute-start | bytes 491528 | tf_op jit(solution)/shard_map/ppermute | solution.py:334
  45.2 7.3 %collective-permute-start.15 = (bf16[160,512]{1,0:T(8,128)(2,1)S(1)}, bf16[160,512]{1,0:T(8,128)(2,1)S(1)}, u32[]{:S(2)}, u32[]{:S(2)}) collective-permute-start(bf16[160,512]{1,0:T(8,128)(2,1)S(1)} %get-tuple-element.24.refs_1_), channel_id=1, source_target_pairs={{0,1},{1,3},{3,5},{5,7},{7,6},{6,4},{4,2},{2,0},{8,9},{9,11},{11,1... | collective-permute-start | bytes 491528 | tf_op jit(solution)/shard_map/ppermute | solution.py:334
  45.4 9.1 %collective-permute-start.14 = (bf16[160,512]{1,0:T(8,128)(2,1)S(1)}, bf16[160,512]{1,0:T(8,128)(2,1)S(1)}, u32[]{:S(2)}, u32[]{:S(2)}) collective-permute-start(bf16[160,512]{1,0:T(8,128)(2,1)S(1)} %get-tuple-element.23.refs_2_.refs_0_), channel_id=1, source_target_pairs={{0,1},{1,3},{3,5},{5,7},{7,6},{6,4},{4,2},{2,0},{8,9},{9,11},{11,1... | collective-permute-start | bytes 491528 | tf_op jit(solution)/shard_map/ppermute | solution.py:334
  47.3 8.0 %collective-permute-start.16 = (bf16[160,512]{1,0:T(8,128)(2,1)S(1)}, bf16[160,512]{1,0:T(8,128)(2,1)S(1)}, u32[]{:S(2)}, u32[]{:S(2)}) collective-permute-start(bf16[160,512]{1,0:T(8,128)(2,1)S(1)} %get-tuple-element.23.refs_2_.refs_0_), channel_id=1, source_target_pairs={{1,0},{3,1},{5,3},{7,5},{6,7},{4,6},{2,4},{0,2},{9,8},{11,9},{13,1... | collective-permute-start | bytes 491528 | tf_op jit(solution)/shard_map/ppermute | solution.py:334
  47.5 17.6 %collective-permute-start.30 = (bf16[128,1280]{1,0:T(8,128)(2,1)S(1)}, bf16[128,1280]{1,0:T(8,128)(2,1)S(1)}, u32[]{:S(2)}, u32[]{:S(2)}) collective-permute-start(bf16[128,1280]{1,0:T(8,128)(2,1)S(1)} %slice.22.refs_19_.refs_7_), channel_id=1, source_target_pairs={{0,16},{8,24},{16,0},{24,8},{1,17},{9,25},{17,1},{25,9},{2,18},{10... | collective-permute-start | bytes 983048 | tf_op jit(solution)/shard_map/ppermute | solution.py:354
  52.4 7.2 %collective-permute-start.21 = (bf16[160,512]{1,0:T(8,128)(2,1)S(1)}, bf16[160,512]{1,0:T(8,128)(2,1)S(1)}, u32[]{:S(2)}, u32[]{:S(2)}) collective-permute-start(bf16[160,512]{1,0:T(8,128)(2,1)S(1)} %collective-permute-done.17.refs_5_), channel_id=1, source_target_pairs={{1,0},{3,1},{5,3},{7,5},{6,7},{4,6},{2,4},{0,2},{9,8},{11,9},{13,1... | collective-permute-start | bytes 491528 | tf_op jit(solution)/shard_map/ppermute | solution.py:334
  52.4 7.2 %collective-permute-start.19 = (bf16[160,512]{1,0:T(8,128)(2,1)S(1)}, bf16[160,512]{1,0:T(8,128)(2,1)S(1)}, u32[]{:S(2)}, u32[]{:S(2)}) collective-permute-start(bf16[160,512]{1,0:T(8,128)(2,1)S(1)} %collective-permute-done.15.refs_3_), channel_id=1, source_target_pairs={{0,1},{1,3},{3,5},{5,7},{7,6},{6,4},{4,2},{2,0},{8,9},{9,11},{11,1... | collective-permute-start | bytes 491528 | tf_op jit(solution)/shard_map/ppermute | solution.py:334
  54.5 8.2 %collective-permute-start.18 = (bf16[160,512]{1,0:T(8,128)(2,1)S(1)}, bf16[160,512]{1,0:T(8,128)(2,1)S(1)}, u32[]{:S(2)}, u32[]{:S(2)}) collective-permute-start(bf16[160,512]{1,0:T(8,128)(2,1)S(1)} %collective-permute-done.14.refs_2_), channel_id=1, source_target_pairs={{0,1},{1,3},{3,5},{5,7},{7,6},{6,4},{4,2},{2,0},{8,9},{9,11},{11,1... | collective-permute-start | bytes 491528 | tf_op jit(solution)/shard_map/ppermute | solution.py:334
  55.3 9.9 %collective-permute-start.20 = (bf16[160,512]{1,0:T(8,128)(2,1)S(1)}, bf16[160,512]{1,0:T(8,128)(2,1)S(1)}, u32[]{:S(2)}, u32[]{:S(2)}) collective-permute-start(bf16[160,512]{1,0:T(8,128)(2,1)S(1)} %collective-permute-done.16.refs_4_), channel_id=1, source_target_pairs={{1,0},{3,1},{5,3},{7,5},{6,7},{4,6},{2,4},{0,2},{9,8},{11,9},{13,1... | collective-permute-start | bytes 491528 | tf_op jit(solution)/shard_map/ppermute | solution.py:334
  59.6 6.9 %collective-permute-start.23 = (bf16[160,512]{1,0:T(8,128)(2,1)S(1)}, bf16[160,512]{1,0:T(8,128)(2,1)S(1)}, u32[]{:S(2)}, u32[]{:S(2)}) collective-permute-start(bf16[160,512]{1,0:T(8,128)(2,1)S(1)} %collective-permute-done.19.refs_7_), channel_id=1, source_target_pairs={{0,1},{1,3},{3,5},{5,7},{7,6},{6,4},{4,2},{2,0},{8,9},{9,11},{11,1... | collective-permute-start | bytes 491528 | tf_op jit(solution)/shard_map/ppermute | solution.py:334
  62.7 6.6 %collective-permute-start.22 = (bf16[160,512]{1,0:T(8,128)(2,1)S(1)}, bf16[160,512]{1,0:T(8,128)(2,1)S(1)}, u32[]{:S(2)}, u32[]{:S(2)}) collective-permute-start(bf16[160,512]{1,0:T(8,128)(2,1)S(1)} %collective-permute-done.18.refs_6_), channel_id=1, source_target_pairs={{0,1},{1,3},{3,5},{5,7},{7,6},{6,4},{4,2},{2,0},{8,9},{9,11},{11,1... | collective-permute-start | bytes 491528 | tf_op jit(solution)/shard_map/ppermute | solution.py:334
  65.1 10.2 %collective-permute-start.31 = (bf16[128,1280]{1,0:T(8,128)(2,1)S(1)}, bf16[128,1280]{1,0:T(8,128)(2,1)S(1)}, u32[]{:S(2)}, u32[]{:S(2)}) collective-permute-start(bf16[128,1280]{1,0:T(8,128)(2,1)S(1)} %slice.22.refs_19_.refs_7_), channel_id=1, source_target_pairs={{0,8},{8,0},{16,24},{24,16},{1,9},{9,1},{17,25},{25,17},{2,10},{10... | collective-permute-start | bytes 983048 | tf_op jit(solution)/shard_map/ppermute | solution.py:354
  65.1 10.2 %collective-permute-start.32 = (bf16[128,1280]{1,0:T(8,128)(2,1)S(1)}, bf16[128,1280]{1,0:T(8,128)(2,1)S(1)}, u32[]{:S(2)}, u32[]{:S(2)}) collective-permute-start(bf16[128,1280]{1,0:T(8,128)(2,1)S(1)} %collective-permute-done.30.refs_20_.refs_8_), channel_id=1, source_target_pairs={{0,8},{8,0},{16,24},{24,16},{1,9},{9,1},{17,25},{25,17},{2,10},{10... | collective-permute-start | bytes 983048 | tf_op jit(solution)/shard_map/ppermute | solution.py:354
  65.7 7.1 %collective-permute-start.24 = (bf16[160,512]{1,0:T(8,128)(2,1)S(1)}, bf16[160,512]{1,0:T(8,128)(2,1)S(1)}, u32[]{:S(2)}, u32[]{:S(2)}) collective-permute-start(bf16[160,512]{1,0:T(8,128)(2,1)S(1)} %collective-permute-done.20.refs_8_), channel_id=1, source_target_pairs={{1,0},{3,1},{5,3},{7,5},{6,7},{4,6},{2,4},{0,2},{9,8},{11,9},{13,1... | collective-permute-start | bytes 491528 | tf_op jit(solution)/shard_map/ppermute | solution.py:334
  66.5 8.8 %collective-permute-start.27 = (bf16[160,512]{1,0:T(8,128)(2,1)S(1)}, bf16[160,512]{1,0:T(8,128)(2,1)S(1)}, u32[]{:S(2)}, u32[]{:S(2)}) collective-permute-start(bf16[160,512]{1,0:T(8,128)(2,1)S(1)} %collective-permute-done.25.refs_13_.refs_4_), channel_id=1, source_target_pairs={{1,0},{3,1},{5,3},{7,5},{6,7},{4,6},{2,4},{0,2},{9,8},{11,9},{13,1... | collective-permute-start | bytes 491528 | tf_op jit(solution)/shard_map/ppermute | solution.py:334
  75.4 15.2 %collective-permute-start.36 = (bf16[160,1280]{1,0:T(8,128)(2,1)S(1)}, bf16[160,1280]{1,0:T(8,128)(2,1)S(1)}, u32[]{:S(2)}, u32[]{:S(2)}) collective-permute-start(bf16[160,1280]{1,0:T(8,128)(2,1)S(1)} %get-tuple-element.37), channel_id=1, source_target_pairs={{0,16},{8,24},{16,0},{24,8},{1,17},{9,25},{17,1},{25,9},{2,18},{10... | collective-permute-start | bytes 1228808 | tf_op jit(solution)/shard_map/ppermute | solution.py:354
  77.0 13.6 %collective-permute-start.37 = (bf16[160,1280]{1,0:T(8,128)(2,1)S(1)}, bf16[160,1280]{1,0:T(8,128)(2,1)S(1)}, u32[]{:S(2)}, u32[]{:S(2)}) collective-permute-start(bf16[160,1280]{1,0:T(8,128)(2,1)S(1)} %get-tuple-element.38), channel_id=1, source_target_pairs={{0,3},{1,2},{2,5},{3,4},{4,7},{5,6},{6,1},{7,0},{8,15},{9,14},{10,... | collective-permute-start | bytes 1228808 | tf_op jit(solution)/shard_map/ppermute | solution.py:349
  90.7 15.2 %collective-permute-start.38 = (bf16[400,1280]{1,0:T(8,128)(2,1)S(1)}, bf16[400,1280]{1,0:T(8,128)(2,1)S(1)}, u32[]{:S(2)}, u32[]{:S(2)}) collective-permute-start(bf16[400,1280]{1,0:T(8,128)(2,1)S(1)} %get-tuple-element.39.refs_6_), channel_id=1, source_target_pairs={{0,8},{8,0},{16,24},{24,16},{1,9},{9,1},{17,25},{25,17},{2,10},{10... | collective-permute-start | bytes 3072008 | tf_op jit(solution)/shard_map/ppermute | solution.py:354
  92.1 13.7 %collective-permute-start.39 = (bf16[160,1280]{1,0:T(8,128)(2,1)S(1)}, bf16[160,1280]{1,0:T(8,128)(2,1)S(1)}, u32[]{:S(2)}, u32[]{:S(2)}) collective-permute-start(bf16[160,1280]{1,0:T(8,128)(2,1)S(1)} %get-tuple-element.40.refs_8_), channel_id=1, source_target_pairs={{0,8},{8,0},{16,24},{24,16},{1,9},{9,1},{17,25},{25,17},{2,10},{10... | collective-permute-start | bytes 1228808 | tf_op jit(solution)/shard_map/ppermute | solution.py:354
  92.2 9.2 %collective-permute-start.34 = (bf16[320,128]{1,0:T(8,128)(2,1)S(1)}, bf16[320,128]{1,0:T(8,128)(2,1)S(1)}, u32[]{:S(2)}, u32[]{:S(2)}) collective-permute-start(bf16[320,128]{1,0:T(8,128)(2,1)S(1)} %get-tuple-element.33), channel_id=1, source_target_pairs={{0,4},{1,5},{2,6},{3,7},{4,0},{5,1},{6,2},{7,3},{8,12},{9,13},{10,... | collective-permute-start | bytes 245768 | tf_op jit(solution)/shard_map/ppermute | solution.py:497
  94.6 6.7 %collective-permute-start.33 = (bf16[320,128]{1,0:T(8,128)(2,1)S(1)}, bf16[320,128]{1,0:T(8,128)(2,1)S(1)}, u32[]{:S(2)}, u32[]{:S(2)}) collective-permute-start(bf16[320,128]{1,0:T(8,128)(2,1)S(1)} %get-tuple-element.32.refs_2_), channel_id=1, source_target_pairs={{0,2},{1,3},{2,4},{3,5},{4,6},{5,7},{6,0},{7,1},{8,10},{9,11},{10,... | collective-permute-start | bytes 245768 | tf_op jit(solution)/shard_map/ppermute | solution.py:497
  (15 other events, 155.2 us)

commit v7 on v6

--- a/solution.py
+++ b/solution.py
@@ -20,8 +20,10 @@
 HANDED = (0, 2, 1, 3)
 FAR = ((1, 0), (2, 0), (3, 0), (2, 1))
 LAST = ((1, 1), (3, 1))
-SOONER, LATER = (1, 2), (3, 0)
+SOONER = tuple(range(1, OUTER))
+WIDE = 256
 EPSILON = 1e-05
+CHUNK = 16
 MEBI = 1024 * 1024
 
 f32 = jnp.float32
@@ -42,48 +44,71 @@
     return jnp.sum(dot(jnp.concatenate(parts, axis=0).astype(bf16), member, dims), axis=0, keepdims=True)
 
 
+def stats_kernel(*refs):
+    pieces, out_ref = refs[:-1], refs[-1]
+    block = pieces[0].shape[0]
+    steps = block // CHUNK
+
+    def add(step, total):
+        for piece in pieces[:2]:
+            total = total + folded(piece[pl.ds(step * CHUNK, CHUNK), :].astype(f32))
+        return total
+
+    zero = jnp.zeros((8, C), f32)
+    pivot = jnp.sum(lax.fori_loop(0, steps, add, zero), axis=0, keepdims=True) / (2 * block)
+    first, second = add_moments(pieces, pivot, zero, zero)
+    out_ref[0:8, :] = jnp.broadcast_to(pivot, (8, C))
+    out_ref[8:16, :] = first
+    out_ref[16:24, :] = second
+
+
+def folded(rows):
+    return rows[:8] + rows[8:]
+
+
+def add_moments(pieces, pivot, first, second):
+    def add(step, sums):
+        first, second = sums
+        for piece in pieces:
+            away = piece[pl.ds(step * CHUNK, CHUNK), :].astype(f32) - pivot
+            first = first + folded(away)
+            second = second + folded(away * away)
+        return first, second
+
+    return lax.fori_loop(0, pieces[0].shape[0] // CHUNK, add, (first, second))
+
+
 def conv_kernel(columns, sources_ref, *refs):
-    count = len(refs) - 6
+    count = len(refs) - 7
     pieces = refs[:count]
-    kernel_ref, bias_ref = refs[count : count + 2]
-    out_refs = refs[count + 2 : count + 4]
-    act_ref, kept_ref = refs[count + 4 :]
+    stats_ref, kernel_ref, bias_ref = refs[count : count + 3]
+    out_refs = refs[count + 3 : count + 5]
+    act_ref, kept_ref = refs[count + 5 :]
     block = pieces[0].shape[0]
     positions = block * count
     own = out_refs[0].shape[0]
     me = lax.axis_index("patch")
-    entries = float(positions * SPAN)
-    chunk = 16
-    steps = block // chunk
+    steps = block // CHUNK
     starts = [
         pl.multiple_of(sources_ref[me * count + index] * (2 * block) + (index % 2) * block, block)
         for index in range(count)
     ]
 
-    def add(step, total):
-        for piece in pieces:
-            total = total + piece[pl.ds(step * chunk, chunk), :].astype(f32)
-        return total
-
     member = (
         lax.broadcasted_iota(jnp.int32, (C, 128), 0) // SPAN
         == lax.broadcasted_iota(jnp.int32, (C, 128), 1)
     ).astype(bf16)
 
-    def group_mean(total):
-        summed = jnp.sum(total, axis=0, keepdims=True)
-        return exact(exact(summed, member) / entries, member, NT)
-
-    zero = jnp.zeros((chunk, C), f32)
-    centre = group_mean(lax.fori_loop(0, steps, add, zero))
-
-    def add_square(step, total):
-        for piece in pieces:
-            away = piece[pl.ds(step * chunk, chunk), :].astype(f32) - centre
-            total = total + away * away
-        return total
-
-    spread = group_mean(lax.fori_loop(0, steps, add_square, zero))
+    def group_mean(per_channel):
+        return exact(exact(per_channel, member) / SPAN, member, NT)
+
+    pivot = stats_ref[0:1, :]
+    first, second = add_moments(pieces[-2:], pivot, stats_ref[8:16, :], stats_ref[16:24, :])
+    above = jnp.sum(first, axis=0, keepdims=True) / positions
+    within = jnp.sum(second, axis=0, keepdims=True) / positions - above * above
+    mean = pivot + above
+    centre = group_mean(mean)
+    spread = group_mean(within + (mean - centre) * (mean - centre))
     half_scale = 0.5 * lax.rsqrt(spread + EPSILON)
 
     act_ref[0:columns, :] = jnp.zeros((columns, C), bf16)
@@ -91,15 +116,15 @@
 
     def activate(step, carry):
         for start, piece in zip(starts, pieces):
-            half = (piece[pl.ds(step * chunk, chunk), :].astype(f32) - centre) * half_scale
+            half = (piece[pl.ds(step * CHUNK, CHUNK), :].astype(f32) - centre) * half_scale
             value = half + half * jnp.tanh(half)
-            row = pl.multiple_of(columns + start + step * chunk, chunk)
-            act_ref[pl.ds(row, chunk), :] = value.astype(bf16)
+            row = pl.multiple_of(columns + start + step * CHUNK, CHUNK)
+            act_ref[pl.ds(row, CHUNK), :] = value.astype(bf16)
         return carry
 
     lax.fori_loop(0, steps, activate, 0)
 
-    window = min(C, (own + 127) // 128 * 128 + 128)
+    window = window_of(own)
     base = jnp.minimum(lax.div(me * own, 128) * 128, C - window)
     lanes = pl.ds(pl.multiple_of(base, 128), window)
     choose = (
@@ -111,7 +136,7 @@
         start = pl.multiple_of(starts[index], 2 * block)
         kept_ref[:, pl.ds(start, 2 * block)] = dot(choose, pair, NT)
 
-    wide = 256
+    wide = WIDE
     column = lax.broadcasted_iota(jnp.int32, (own, wide), 1) % columns
     square = (own, own)
     bias = jnp.where(
@@ -133,113 +158,140 @@
         out_refs[which][:, low : low + wide] = hidden.astype(bf16)
 
 
+def window_of(own):
+    return min(C, (own + 127) // 128 * 128 + 128)
+
+
+def norm_pair(pair):
+    own = pair[0].shape[0]
+    entries = float(2 * pair[0].shape[1] * SPAN)
+
+    def whole(values):
+        return jnp.sum(jnp.sum(values, axis=0, keepdims=True), axis=1, keepdims=True)
+
+    def group_at(low):
+        first, last = low // 16 * 16, -(-(low + SPAN) // 16) * 16
+        return [ref[first:last, :].astype(f32)[low - first : low - first + SPAN] for ref in pair]
+
+    lows = range(0, own, SPAN)
+    means = [sum(whole(half) for half in group_at(low)) / entries for low in lows]
+    squares = [
+        sum(whole(jnp.square(half - mean)) for half in group_at(low))
+        for low, mean in zip(lows, means)
+    ]
+    scales = [lax.rsqrt(square / entries + EPSILON) for square in squares]
+    mean = jnp.concatenate([jnp.broadcast_to(one, (SPAN, 1)) for one in means], axis=0)
+    scale = jnp.concatenate([jnp.broadcast_to(one, (SPAN, 1)) for one in scales], axis=0)
+    return [((ref[...].astype(f32) - mean) * scale).astype(bf16) for ref in pair]
+
+
+def own_lanes(pair, me, n):
+    block = 2 * pair[0].shape[1] // n
+    start = pl.multiple_of(lax.rem(me, n // 2) * block, block)
+    low, high = (ref[:, pl.ds(start, block)] for ref in pair)
+    return jnp.where(me < n // 2, low, high)
+
+
+def project_kernel(count, sources_ref, *refs):
+    pieces = refs[: count - 2]
+    weight_refs = refs[count - 2 : -3]
+    sums_ref, kept_ref, normed_ref = refs[-3:]
+    own, part = pieces[0].shape
+    me = lax.axis_index("patch")
+    for at in range(0, count - 2, 2):
+        pair = pieces[at : at + 2]
+        rows = pl.ds(pl.multiple_of(sources_ref[me * count + at] * own, own), own)
+        for half, normed in enumerate(norm_pair(pair)):
+            normed_ref[rows, half * part : (half + 1) * part] = normed
+        kept_ref[rows, :] = own_lanes(pair, me, count // 2)
+    missing = pl.multiple_of(sources_ref[me * count + count - 2] * own, own)
+    normed_ref[pl.ds(missing, own), :] = jnp.zeros((own, 2 * part), bf16)
+    weights = jnp.concatenate([ref[...] for ref in weight_refs], axis=0)
+    for at in range(0, 2 * part, WIDE):
+        sums_ref[:, at : at + WIDE] = dot(weights, normed_ref[:, at : at + WIDE])
+
+
 def attention_kernel(count, inner, sources_ref, *refs):
-    pieces = refs[:count]
-    parts = refs[count:-9]
-    outs = refs[-9:-7]
-    kept_ref, later_ref, key_ref, value_ref, normed_ref, weight_ref, sems = refs[-7:]
-    own, part = pieces[0].shape
+    pair = refs[:2]
+    weight_refs = refs[2:-9]
+    sums_ref, some_ref = refs[-9:-7]
+    outs = refs[-7:-4]
+    kept_ref, made_ref, key_ref, last_ref = refs[-4:]
+    own, part = pair[0].shape
     n = count // 2
-    positions = 2 * part
-    block = positions // n
     me = lax.axis_index("patch")
     outer_at, inner_at = lax.div(me, inner), lax.rem(me, inner)
-    entries = float(positions * SPAN)
-    loads = []
-
-    def load(source, row):
-        target = weight_ref.at[pl.ds(row, source.shape[0]), :]
-        loads.append(pltpu.make_async_copy(source, target, sems.at[len(loads)]))
-
-    if inner == 2:
-        for kind in range(3):
-            row = kind * SET_CHANNELS + inner_at * own
-            load(parts[kind], pl.multiple_of(row, own))
-        mine = lax.rem(lax.axis_index("batch"), QUAD)
-        for step, part_ref in zip(HANDED, parts[3:]):
-            place = jnp.bitwise_xor(mine, step)
-            first = quarter_start(place, own)
-            twice = QUAD * (part_ref.shape[0] // GRANULE) - 3 * own // GRANULE
-            for at in range(part_ref.shape[0] // GRANULE):
-                granule = first + at
-                kind = lax.div(granule, own // GRANULE)
-                row = kind * SET_CHANNELS + (1 - inner_at) * own
-                row = row + lax.rem(granule, own // GRANULE) * GRANULE
-                if at < twice:
-                    spare = 3 * SET_CHANNELS + at * GRANULE
-                    row = jnp.where(place == QUAD - 1, spare, row)
-                source = part_ref.at[at * GRANULE : (at + 1) * GRANULE, :]
-                load(source, pl.multiple_of(row, GRANULE))
-    else:
-        load(parts[0], 0)
-    for copy in loads:
-        copy.start()
-
-    groups = [(at, low) for at in range(0, count, 2) for low in range(0, own, SPAN)]
-
-    def whole(values):
-        return jnp.sum(jnp.sum(values, axis=0, keepdims=True), axis=1, keepdims=True)
-
-    def group_of(at, low):
-        halves = []
-        for piece in pieces[at : at + 2]:
-            first = low // 16 * 16
-            rows = piece[first : -(-(low + SPAN) // 16) * 16, :].astype(f32)
-            halves.append(rows[low - first : low - first + SPAN])
-        return halves
-
-    means = [sum(whole(half) for half in group_of(*group)) / entries for group in groups]
-    scales = []
-    for mean, group in zip(means, groups):
-        square = sum(whole(jnp.square(half - mean)) for half in group_of(*group))
-        scales.append(lax.rsqrt(square / entries + EPSILON))
-    for at in range(0, count, 2):
-        row = pl.multiple_of(sources_ref[me * count + at] * own, own)
-        which = [index for index, group in enumerate(groups) if group[0] == at]
-        mean = jnp.concatenate([jnp.broadcast_to(means[index], (SPAN, 1)) for index in which], axis=0)
-        scale = jnp.concatenate([jnp.broadcast_to(scales[index], (SPAN, 1)) for index in which], axis=0)
-        for half, piece in enumerate(pieces[at : at + 2]):
-            normed = (piece[...].astype(f32) - mean) * scale
-            normed_ref[pl.ds(row, own), half * part : (half + 1) * part] = normed.astype(bf16)
-        start = pl.multiple_of(lax.rem(me, n // 2) * block, block)
-        low, high = (piece[:, pl.ds(start, block)] for piece in pieces[at : at + 2])
-        kept_ref[pl.ds(row, own), :] = jnp.where(me < n // 2, low, high)
-
-    for copy in loads:
-        copy.wait()
-    wide = 256
-    for at in range(0, positions, wide):
-        made = dot(weight_ref[SET_CHANNELS : 3 * SET_CHANNELS, :], normed_ref[:, at : at + wide])
+    source = sources_ref[me * count + count - 2]
+    row = pl.multiple_of(source * own, own)
+    kept_ref[...] = some_ref[...]
+    kept_ref[pl.ds(row, own), :] = own_lanes(pair, me, n)
+
+    window = last_ref.shape[0]
+    base = jnp.minimum(lax.div(source * own, 128) * 128, C - window)
+    lanes = pl.ds(pl.multiple_of(base, 128), window)
+    last_ref[...] = jnp.zeros_like(last_ref)
+    within = pl.ds(pl.multiple_of(source * own - base, 16), own)
+    for half, normed in enumerate(norm_pair(pair)):
+        last_ref[within, half * part : (half + 1) * part] = normed
+    weights = jnp.concatenate([ref[:, lanes] for ref in weight_refs], axis=0)
+    places = rows_of(weight_refs, own, inner, inner_at)
+    for at in range(0, 2 * part, WIDE):
+        made = dot(weights, last_ref[:, at : at + WIDE]) + sums_ref[:, at : at + WIDE]
+        made = made.astype(bf16)
+        for low, size, target in places:
+            made_ref[pl.ds(target, size), at : at + WIDE] = made[low : low + size]
+
+    for at in range(0, 2 * part, WIDE):
         for head in range(SET_HEADS):
-            low = head * HEAD_DIM
-            key_ref[head, at : at + wide, :] = made[low : low + HEAD_DIM].T.astype(bf16)
-        value_ref[:, at : at + wide] = made[SET_CHANNELS:].astype(bf16)
-
-    def queries(steps):
-        normed = []
-        for step in steps:
-            target = lax.rem(outer_at + step, OUTER) * inner + inner_at
-            normed.append(normed_ref[:, pl.ds(pl.multiple_of(target * block, block), block)])
-        made = dot(weight_ref[:SET_CHANNELS, :], jnp.concatenate(normed, axis=1))
-        return (made.astype(bf16).astype(f32) * HEAD_DIM ** (-0.5)).astype(bf16)
-
-    later_ref[...] = queries(LATER)
-    attend(queries(SOONER), key_ref, value_ref, outs)
-
-
-def later_kernel(query_ref, key_ref, value_ref, *outs):
-    attend(query_ref[...], key_ref, value_ref, outs)
-
-
-def attend(query, key_ref, value_ref, outs):
+            low = SET_CHANNELS + head * HEAD_DIM
+            key = made_ref[low : low + HEAD_DIM, at : at + WIDE].astype(f32)
+            key_ref[head, at : at + WIDE, :] = key.T.astype(bf16)
+
+    targets = [lax.rem(outer_at + step, OUTER) * inner + inner_at for step in SOONER]
+    attend(targets, made_ref, key_ref, outs)
+
+
+def rows_of(weight_refs, own, inner, inner_at):
+    if inner != 2:
+        return [(0, weight_refs[0].shape[0], 0)]
+    places = []
+    for kind in range(3):
+        place = kind * SET_CHANNELS + inner_at * own
+        places.append((kind * own, own, pl.multiple_of(place, own)))
+    mine = lax.rem(lax.axis_index("batch"), QUAD)
+    size = weight_refs[3].shape[0]
+    twice = QUAD * (size // GRANULE) - 3 * own // GRANULE
+    for order, step in enumerate(HANDED):
+        which = jnp.bitwise_xor(mine, step)
+        first = quarter_start(which, own)
+        for at in range(size // GRANULE):
+            granule = first + at
+            place = lax.div(granule, own // GRANULE) * SET_CHANNELS + (1 - inner_at) * own
+            place = place + lax.rem(granule, own // GRANULE) * GRANULE
+            if at < twice:
+                place = jnp.where(which == QUAD - 1, 3 * SET_CHANNELS + at * GRANULE, place)
+            low = 3 * own + order * size + at * GRANULE
+            places.append((low, GRANULE, pl.multiple_of(place, GRANULE)))
+    return places
+
+
+def later_kernel(made_ref, key_ref, out_ref):
+    attend([lax.axis_index("patch")], made_ref, key_ref, [out_ref])
+
+
+def attend(targets, made_ref, key_ref, outs):
     block = outs[0].shape[1]
+    starts = [pl.multiple_of(target * block, block) for target in targets]
     for head in range(SET_HEADS):
         low = head * HEAD_DIM
-        scores = dot(key_ref[head], query[low : low + HEAD_DIM])
+        query = [made_ref[low : low + HEAD_DIM, pl.ds(start, block)] for start in starts]
+        query = jnp.concatenate(query, axis=1).astype(f32) * HEAD_DIM ** (-0.5)
+        scores = dot(key_ref[head], query.astype(bf16))
         peak = jnp.max(scores, axis=0, keepdims=True)
         unnormalized = jnp.exp(scores - peak)
         total = jnp.sum(unnormalized, axis=0, keepdims=True)
-        mixture = dot(value_ref[low : low + HEAD_DIM, :], unnormalized.astype(bf16))
+        value = made_ref[2 * SET_CHANNELS + low : 2 * SET_CHANNELS + low + HEAD_DIM, :]
+        mixture = dot(value, unnormalized.astype(bf16))
         attended = (mixture / total).astype(bf16)
         for place, out in enumerate(outs):
             out[low : low + HEAD_DIM, :] = attended[:, place * block : (place + 1) * block]
@@ -393,24 +445,36 @@
 
     whole = latent.reshape(block, channels)
     halves = whole[: block // 2], whole[block // 2 :]
+    chosen = []
     if inner == 2:
         quarter = quarter_rows(own)
         core = lax.rem(lax.axis_index("batch"), 2)
         start = quarter_start(lax.rem(lax.axis_index("batch"), QUAD), own) * GRANULE
         stacked = jnp.concatenate([w_query, w_key, w_value], axis=0)
-        chosen = jnp.concatenate(
-            [
-                lax.dynamic_slice_in_dim(stacked, start, quarter, 0),
-                lax.dynamic_slice_in_dim(w_out, core * (own // 2), own // 2, 0),
-            ],
-            axis=0,
-        )
-        pieces = gather(halves, n, [chosen])
-        chosen, out_own = after([chosen, w_out], pieces[-5:])
+        chosen = [
+            lax.dynamic_slice_in_dim(stacked, start, quarter, 0),
+            lax.dynamic_slice_in_dim(w_out, core * (own // 2), own // 2, 0),
+        ]
+        chosen = [jnp.concatenate(chosen, axis=0)]
+    pieces = gather(halves, n, chosen)
+    stats = pl.pallas_call(
+        stats_kernel,
+        out_shape=jax.ShapeDtypeStruct((24, channels), f32),
+        in_specs=[vmem] * (2 * n - 2),
+        out_specs=vmem,
+        compiler_params=pltpu.CompilerParams(vmem_limit_bytes=2 * MEBI),
+        cost_estimate=pl.CostEstimate(
+            flops=6 * positions * channels,
+            bytes_accessed=2 * positions * channels,
+            transcendentals=0,
+        ),
+        name="stats",
+    )(*pieces[:-2])
+    if inner == 2:
+        chosen, out_own = after(chosen + [w_out], pieces[-5:] + [stats])
         chosen = send(chosen, [(0, 1)])
         far = send(out_own, FAR)
     else:
-        pieces = gather(halves, n)
         sets = [list(range(at, at + inner)) for at in range(0, n, inner)]
         weights = jnp.stack([w_query, w_key, w_value])
         weights = lax.all_gather(weights, "patch", axis=1, tiled=True, axis_index_groups=sets)
@@ -420,7 +484,7 @@
     hidden = pl.pallas_call(
         functools.partial(conv_kernel, columns),
         out_shape=[jax.ShapeDtypeStruct((own, positions // 2), bf16)] * 2,
-        in_specs=[smem] + [vmem] * (2 * n + 2),
+        in_specs=[smem] + [vmem] * (2 * n + 3),
         out_specs=[vmem] * 2,
         scratch_shapes=[
             pltpu.VMEM((positions + 2 * columns, channels), bf16),
@@ -436,74 +500,82 @@
     )(
         sources,
         *pieces,
+        stats,
         conv_weight.reshape(3, 3 * own, channels),
         channel_bias.reshape(1, own),
     )
 
     hidden_pieces = gather(tuple(hidden), n)
     if inner == 2:
-        chosen, far = after([chosen, far], hidden[:1])
+        (chosen,) = after([chosen], hidden[:1])
         near = [chosen[:quarter]]
         near.append(swap(near[0], 2))
+        near[0], far = after([near[0], far], near[1:])
         near += [swap(one, 1) for one in near]
         weights = [w_query, w_key, w_value] + near
-        far, out_own = after([far, out_own], hidden_pieces[-5:] + near)
+    made_rows = sum(weight.shape[0] for weight in weights)
+    sums, some = pl.pallas_call(
+        functools.partial(project_kernel, 2 * n),
+        out_shape=[
+            jax.ShapeDtypeStruct((made_rows, positions), f32),
+            jax.ShapeDtypeStruct((channels, block), bf16),
+        ],
+        in_specs=[smem] + [vmem] * (2 * n - 2 + len(weights)),
+        out_specs=[vmem] * 2,
+        scratch_shapes=[pltpu.VMEM((channels, positions), bf16)],
+        compiler_params=pltpu.CompilerParams(vmem_limit_bytes=20 * MEBI),
+        cost_estimate=pl.CostEstimate(
+            flops=2 * positions * channels * made_rows,
+            bytes_accessed=2 * (positions * channels + made_rows * channels),
+            transcendentals=0,
+        ),
+        name="norm_project",
+    )(sources, *hidden_pieces[:-2], *weights)
+    if inner == 2:
+        far, out_own = after([far, out_own], hidden_pieces[-5:] + [sums])
         across = swap(far, 2)
         last = send(out_own, LAST)
-
-    pair = [jax.ShapeDtypeStruct((SET_CHANNELS, block), bf16)] * 2
-    attended = {}
-    attended[SOONER[0]], attended[SOONER[1]], kept, query, key, value = pl.pallas_call(
+    one_block = jax.ShapeDtypeStruct((SET_CHANNELS, block), bf16)
+    *sent, kept, made, key = pl.pallas_call(
         functools.partial(attention_kernel, 2 * n, inner),
-        out_shape=pair
+        out_shape=[one_block] * len(SOONER)
         + [
             jax.ShapeDtypeStruct((channels, block), bf16),
-            jax.ShapeDtypeStruct((SET_CHANNELS, 2 * block), bf16),
+            jax.ShapeDtypeStruct((made_rows, positions), bf16),
             jax.ShapeDtypeStruct((SET_HEADS, positions, HEAD_DIM), bf16),
-            jax.ShapeDtypeStruct((SET_CHANNELS, positions), bf16),
         ],
-        in_specs=[smem] + [vmem] * (2 * n) + [anywhere] * len(weights),
-        out_specs=[vmem] * 6,
-        scratch_shapes=[
-            pltpu.VMEM((channels, positions), bf16),
-            pltpu.VMEM((QUAD * SET_CHANNELS, channels), bf16),
-            pltpu.SemaphoreType.DMA((3 + QUAD * quarter_rows(own) // GRANULE,)),
-        ],
+        in_specs=[smem] + [vmem] * (4 + len(weights)),
+        out_specs=[vmem] * (3 + len(SOONER)),
+        scratch_shapes=[pltpu.VMEM((window_of(own), positions), bf16)],
         compiler_params=pltpu.CompilerParams(vmem_limit_bytes=28 * MEBI),
         cost_estimate=pl.CostEstimate(
-            flops=2 * positions * channels * 3 * SET_CHANNELS
-            + 8 * positions * block * SET_CHANNELS,
-            bytes_accessed=2 * (positions * channels + 3 * SET_CHANNELS * channels),
-            transcendentals=positions * 2 * block * SET_HEADS,
+            flops=2 * positions * window_of(own) * made_rows
+            + 12 * positions * block * SET_CHANNELS,
+            bytes_accessed=6 * made_rows * positions,
+            transcendentals=positions * 3 * block * SET_HEADS,
         ),
         name="attention",
-    )(sources, *hidden_pieces, *weights)
-    attended[LATER[0]], attended[LATER[1]] = pl.pallas_call(
+    )(sources, *hidden_pieces[-2:], *weights, sums, some)
+    received = [None]
+    for step, sent_block in zip(SOONER, sent):
+        pairs = [(at, (at + step * inner) % n) for at in range(n)]
+        received.append(lax.ppermute(sent_block, "patch", pairs))
+    received[0] = pl.pallas_call(
         later_kernel,
-        out_shape=pair,
-        in_specs=[vmem] * 3,
-        out_specs=[vmem] * 2,
+        out_shape=one_block,
+        in_specs=[vmem] * 2,
+        out_specs=vmem,
         compiler_params=pltpu.CompilerParams(vmem_limit_bytes=16 * MEBI),
         cost_estimate=pl.CostEstimate(
-            flops=8 * positions * block * SET_CHANNELS,
+            flops=4 * positions * block * SET_CHANNELS,
             bytes_accessed=8 * positions * SET_CHANNELS,
-            transcendentals=positions * 2 * block * SET_HEADS,
+            transcendentals=positions * block * SET_HEADS,
         ),
-        name="later_attention",
-    )(query, key, value)
-
-    def hand_over(step):
-        pairs = [(at, (at + step * inner) % n) for at in range(n)]
-        return lax.ppermute(attended[step], "patch", pairs)
-
-    received = {step: hand_over(step) for step in SOONER}
-    first, last_step = list(received.values()), LATER[0]
-    (attended[last_step],) = after([attended[last_step]], first)
-    received[last_step] = hand_over(last_step)
-    received[0] = attended[0]
+        name="own_attention",
+    )(made, key)
     if inner == 2:
         far = jnp.concatenate([far, across, chosen[quarter:]], axis=0)
-        far, last = after([far, last], [attended[SOONER[0]]])
+        far, last = after([far, last], sent[:1])
         out_weights = [w_out, far, swap(far, 1), last, swap(last, 1)]
 
     output = pl.pallas_call(
@@ -522,7 +594,7 @@
             transcendentals=0,
         ),
         name="project",
-    )(*[received[step] for step in range(OUTER)], kept, *out_weights)
+    )(*received, kept, *out_weights)
     return output.reshape(rows_local, columns, channels)
 
 

time: 108 us -> 106 us (0.981)
  waiting for transfers between devices: 30.8 us -> 26.2 us
  starting transfers between devices: 48.7 us -> 51.9 us
  Pallas kernels: 25.5 us -> 24.3 us
    pallas_call x1, Pallas kernels: 11.7 us -> 6.17 us  [on_device(): pl.pallas_call(functools.partial(attention_kernel, 2 * n, inner), out_sha...]
    pallas_call x1 -> x3, Pallas kernels: 3.36 us -> 8.64 us  [the longest x1 5.69 us: on_device(): pl.pallas_call(functools.partial(project_kernel, 2 * n), out_shape=[jax.S...]
    ppermute x3, waiting for transfers between devices: 7.03 us -> 3.52 us  [on_device(): received.append(lax.ppermute(sent_block, 'patch', pairs))]
    ppermute x28, waiting for transfers between devices: 23.8 us -> 21.1 us  [gather(): lax.ppermute(found[half, sign * (step - 1)], 'patch', pairs)]
    ppermute x3, waiting for transfers between devices: 0.01 us -> 1.5 us  [send(): return lax.ppermute(block, ('batch', 'patch'), pairs)]
    ppermute x3, starting transfers between devices: 3.75 us -> 5.18 us  [send(): return lax.ppermute(block, ('batch', 'patch'), pairs)]
  transfers between devices with their start and end apart: 40 -> 40, of which waited for: 13 -> 17; matrix products, arithmetic and copies ran while one was open for 1% -> 2% of each run, Pallas kernels for 22% -> 21%
where the time goes in v7:
time: 106 us
  starting transfers between devices  51.9 us (49%)
  waiting for transfers between devices  26.2 us (25%)
  Pallas kernels  24.3 us (23%)
  local copies, waits for them, and re-layouts  2.07 us (2%)
  other arithmetic  1.34 us (1%)
    ppermute x28, starting transfers between devices, gather(): lax.ppermute(found[half, sign * (step - 1)], 'patch', pairs)  33.1 us
    ppermute x28, waiting for transfers between devices, gather(): lax.ppermute(found[half, sign * (step - 1)], 'patch', pairs)  21.1 us
    ppermute x6, starting transfers between devices, swap(): return lax.ppermute(block, 'batch', pairs)  9.58 us
    pallas_call x1, Pallas kernels, on_device(): pl.pallas_call(functools.partial(conv_kernel, columns), out_shape=[jax.Sh...  7.49 us
    pallas_call x1, Pallas kernels, on_device(): pl.pallas_call(functools.partial(attention_kernel, 2 * n, inner), out_sha...  6.17 us
    pallas_call x1, Pallas kernels, on_device(): pl.pallas_call(functools.partial(project_kernel, 2 * n), out_shape=[jax.S...  5.69 us
    ppermute x3, starting transfers between devices, send(): return lax.ppermute(block, ('batch', 'patch'), pairs)  5.18 us
    ppermute x3, starting transfers between devices, on_device(): received.append(lax.ppermute(sent_block, 'patch', pairs))  4 us
  transfers between devices with their start and end apart: 40, of which 17 were waited for; matrix products, arithmetic and copies ran while one was open for 2% of the time, Pallas kernels for 21%

profile of v7, /device:TPU:0, one launch (start us, length us, event | category | flops | bytes accessed | tf_op | source)
XLA Modules:
  0.0 106.0 jit_solution(17305175410128195336)
XLA Ops:
  1.0 3.1 %collective-permute-start.3 = (bf16[64,1280]{1,0:T(8,128)(2,1)S(1)}, bf16[64,1280]{1,0:T(8,128)(2,1)S(1)}, u32[]{:S(2)}, u32[]{:S(2)}) collective-permute-start(bf16[64,1280]{1,0:T(8,128)(2,1)S(1)} %get-tuple-element.41.refs_1_), channel_id=1, source_target_pairs={{1,0},{3,1},{5,3},{7,5},{6,7},{4,6},{2,4},{0,2},{9,8},{11,9},{13,1... | collective-permute-start | bytes 491528 | tf_op jit(solution)/shard_map/ppermute | solution.py:386
  4.1 2.0 %collective-permute-start.2 = (bf16[64,1280]{1,0:T(8,128)(2,1)S(1)}, bf16[64,1280]{1,0:T(8,128)(2,1)S(1)}, u32[]{:S(2)}, u32[]{:S(2)}) collective-permute-start(bf16[64,1280]{1,0:T(8,128)(2,1)S(1)} %get-tuple-element.42.refs_0_), channel_id=1, source_target_pairs={{1,0},{3,1},{5,3},{7,5},{6,7},{4,6},{2,4},{0,2},{9,8},{11,9},{13,1... | collective-permute-start | bytes 491528 | tf_op jit(solution)/shard_map/ppermute | solution.py:386
  9.1 2.1 %collective-permute-start.7 = (bf16[64,1280]{1,0:T(8,128)(2,1)S(1)}, bf16[64,1280]{1,0:T(8,128)(2,1)S(1)}, u32[]{:S(2)}, u32[]{:S(2)}) collective-permute-start(bf16[64,1280]{1,0:T(8,128)(2,1)S(1)} %collective-permute-done.3.refs_5_), channel_id=1, source_target_pairs={{1,0},{3,1},{5,3},{7,5},{6,7},{4,6},{2,4},{0,2},{9,8},{11,9},{13,1... | collective-permute-start | bytes 491528 | tf_op jit(solution)/shard_map/ppermute | solution.py:386
  11.2 2.1 %collective-permute-done.refs_0_ = bf16[64,1280]{1,0:T(8,128)(2,1)S(1)} collective-permute-done((bf16[64,1280]{1,0:T(8,128)(2,1)S(1)}, bf16[64,1280]{1,0:T(8,128)(2,1)S(1)}, u32[]{:S(2)}, u32[]{:S(2)}) %collective-permute-start) | collective-permute-done | bytes 163872 | tf_op jit(solution)/shard_map/ppermute | solution.py:386
  13.6 1.7 %collective-permute-start.5 = (bf16[64,1280]{1,0:T(8,128)(2,1)S(1)}, bf16[64,1280]{1,0:T(8,128)(2,1)S(1)}, u32[]{:S(2)}, u32[]{:S(2)}) collective-permute-start(bf16[64,1280]{1,0:T(8,128)(2,1)S(1)} %collective-permute-done.1.refs_3_), channel_id=1, source_target_pairs={{0,1},{1,3},{3,5},{5,7},{7,6},{6,4},{4,2},{2,0},{8,9},{9,11},{11,1... | collective-permute-start | bytes 491528 | tf_op jit(solution)/shard_map/ppermute | solution.py:386
  15.6 1.9 %collective-permute-start.11 = (bf16[64,1280]{1,0:T(8,128)(2,1)S(1)}, bf16[64,1280]{1,0:T(8,128)(2,1)S(1)}, u32[]{:S(2)}, u32[]{:S(2)}) collective-permute-start(bf16[64,1280]{1,0:T(8,128)(2,1)S(1)} %collective-permute-done.7.refs_9_), channel_id=1, source_target_pairs={{1,0},{3,1},{5,3},{7,5},{6,7},{4,6},{2,4},{0,2},{9,8},{11,9},{13,1... | collective-permute-start | bytes 491528 | tf_op jit(solution)/shard_map/ppermute | solution.py:386
  17.5 2.9 %collective-permute-done.4.refs_6_ = bf16[64,1280]{1,0:T(8,128)(2,1)S(1)} collective-permute-done((bf16[64,1280]{1,0:T(8,128)(2,1)S(1)}, bf16[64,1280]{1,0:T(8,128)(2,1)S(1)}, u32[]{:S(2)}, u32[]{:S(2)}) %collective-permute-start.4) | collective-permute-done | bytes 163872 | tf_op jit(solution)/shard_map/ppermute | solution.py:386
  20.7 3.2 %collective-permute-done.5.refs_7_ = bf16[64,1280]{1,0:T(8,128)(2,1)S(1)} collective-permute-done((bf16[64,1280]{1,0:T(8,128)(2,1)S(1)}, bf16[64,1280]{1,0:T(8,128)(2,1)S(1)}, u32[]{:S(2)}, u32[]{:S(2)}) %collective-permute-start.5) | collective-permute-done | bytes 163872 | tf_op jit(solution)/shard_map/ppermute | solution.py:386
  24.2 1.7 %collective-permute-start.10 = (bf16[64,1280]{1,0:T(8,128)(2,1)S(1)}, bf16[64,1280]{1,0:T(8,128)(2,1)S(1)}, u32[]{:S(2)}, u32[]{:S(2)}) collective-permute-start(bf16[64,1280]{1,0:T(8,128)(2,1)S(1)} %collective-permute-done.6.refs_8_), channel_id=1, source_target_pairs={{1,0},{3,1},{5,3},{7,5},{6,7},{4,6},{2,4},{0,2},{9,8},{11,9},{13,1... | collective-permute-start | bytes 491528 | tf_op jit(solution)/shard_map/ppermute | solution.py:386
  26.0 1.6 %collective-permute-start.13 = (bf16[64,1280]{1,0:T(8,128)(2,1)S(1)}, bf16[64,1280]{1,0:T(8,128)(2,1)S(1)}, u32[]{:S(2)}, u32[]{:S(2)}) collective-permute-start(bf16[64,1280]{1,0:T(8,128)(2,1)S(1)} %collective-permute-done.11.refs_13_.refs_4_), channel_id=1, source_target_pairs={{1,0},{3,1},{5,3},{7,5},{6,7},{4,6},{2,4},{0,2},{9,8},{11,9},{13,1... | collective-permute-start | bytes 491528 | tf_op jit(solution)/shard_map/ppermute | solution.py:386
  28.1 2.3 %collective-permute-done.9.refs_11_.refs_2_ = bf16[64,1280]{1,0:T(8,128)(2,1)S(1)} collective-permute-done((bf16[64,1280]{1,0:T(8,128)(2,1)S(1)}, bf16[64,1280]{1,0:T(8,128)(2,1)S(1)}, u32[]{:S(2)}, u32[]{:S(2)}) %collective-permute-start.9) | collective-permute-done | bytes 163872 | tf_op jit(solution)/shard_map/ppermute | solution.py:386
  31.3 1.5 %collective-permute-done.12.refs_14_.refs_5_ = bf16[64,1280]{1,0:T(8,128)(2,1)S(1)} collective-permute-done((bf16[64,1280]{1,0:T(8,128)(2,1)S(1)}, bf16[64,1280]{1,0:T(8,128)(2,1)S(1)}, u32[]{:S(2)}, u32[]{:S(2)}) %collective-permute-start.12) | collective-permute-done | bytes 163872 | tf_op jit(solution)/shard_map/ppermute | solution.py:386
  33.4 1.5 %collective-permute-start.23 = (bf16[160,1280]{1,0:T(8,128)(2,1)S(1)}, bf16[160,1280]{1,0:T(8,128)(2,1)S(1)}, u32[]{:S(2)}, u32[]{:S(2)}) collective-permute-start(bf16[160,1280]{1,0:T(8,128)(2,1)S(1)} %get-tuple-element.26.refs_1_), channel_id=1, source_target_pairs={{0,2},{1,3},{2,4},{3,5},{4,6},{5,7},{6,0},{7,1},{8,12},{9,13},{10,... | collective-permute-start | bytes 1228808 | tf_op jit(solution)/shard_map/ppermute | solution.py:401
  34.9 7.5 %norm_conv.1 = (bf16[160,512]{1,0:T(8,128)(2,1)S(1)}, bf16[160,512]{1,0:T(8,128)(2,1)S(1)}) custom-call(s32[128]{0:T(128)S(1)} %copy-done.4, bf16[64,1280]{1,0:T(8,128)(2,1)S(1)} %get-tuple-element.42.refs_0_, bf16[64,1280]{1,0:T(8,128)(2,1)S(1)} %get-tuple-element.41.refs_1_, bf16[64,1280]{1,0:T(8,128)(2,1)S(1)} %after.6.refs_2_, ...), custom_call_target="tpu_custom_call" | custom-call | flops 3774873600 | bytes 6307840 | tf_op jit(solution)/shard_map/norm_conv/pallas_call | solution.py:484
  42.4 1.7 %collective-permute-start.27 = (bf16[160,512]{1,0:T(8,128)(2,1)S(1)}, bf16[160,512]{1,0:T(8,128)(2,1)S(1)}, u32[]{:S(2)}, u32[]{:S(2)}) collective-permute-start(bf16[160,512]{1,0:T(8,128)(2,1)S(1)} %get-tuple-element.24.refs_1_), channel_id=1, source_target_pairs={{0,1},{1,3},{3,5},{5,7},{7,6},{6,4},{4,2},{2,0},{8,9},{9,11},{11,1... | collective-permute-start | bytes 491528 | tf_op jit(solution)/shard_map/ppermute | solution.py:386
  44.5 8.3 %collective-permute-start.24 = (bf16[128,1280]{1,0:T(8,128)(2,1)S(1)}, bf16[128,1280]{1,0:T(8,128)(2,1)S(1)}, u32[]{:S(2)}, u32[]{:S(2)}) collective-permute-start(bf16[128,1280]{1,0:T(8,128)(2,1)S(1)} %slice.24.refs_0_), channel_id=1, source_target_pairs={{0,16},{8,24},{16,0},{24,8},{1,17},{9,25},{17,1},{25,9},{2,18},{10... | collective-permute-start | bytes 983048 | tf_op jit(solution)/shard_map/ppermute | solution.py:406
  52.8 2.0 %collective-permute-start.14 = (bf16[160,512]{1,0:T(8,128)(2,1)S(1)}, bf16[160,512]{1,0:T(8,128)(2,1)S(1)}, u32[]{:S(2)}, u32[]{:S(2)}) collective-permute-start(bf16[160,512]{1,0:T(8,128)(2,1)S(1)} %get-tuple-element.23.refs_1_.refs_0_), channel_id=1, source_target_pairs={{0,1},{1,3},{3,5},{5,7},{7,6},{6,4},{4,2},{2,0},{8,9},{9,11},{11,1... | collective-permute-start | bytes 491528 | tf_op jit(solution)/shard_map/ppermute | solution.py:386
  54.9 4.0 %collective-permute-done.28.refs_4_ = bf16[160,512]{1,0:T(8,128)(2,1)S(1)} collective-permute-done((bf16[160,512]{1,0:T(8,128)(2,1)S(1)}, bf16[160,512]{1,0:T(8,128)(2,1)S(1)}, u32[]{:S(2)}, u32[]{:S(2)}) %collective-permute-start.28) | collective-permute-done | bytes 163872 | tf_op jit(solution)/shard_map/ppermute | solution.py:386
  61.2 2.5 %collective-permute-start.15 = (bf16[160,512]{1,0:T(8,128)(2,1)S(1)}, bf16[160,512]{1,0:T(8,128)(2,1)S(1)}, u32[]{:S(2)}, u32[]{:S(2)}) collective-permute-start(bf16[160,512]{1,0:T(8,128)(2,1)S(1)} %collective-permute-done.14.refs_2_), channel_id=1, source_target_pairs={{0,1},{1,3},{3,5},{5,7},{7,6},{6,4},{4,2},{2,0},{8,9},{9,11},{11,1... | collective-permute-start | bytes 491528 | tf_op jit(solution)/shard_map/ppermute | solution.py:386
  64.3 1.6 %collective-permute-done.30.refs_8_ = bf16[160,512]{1,0:T(8,128)(2,1)S(1)} collective-permute-done((bf16[160,512]{1,0:T(8,128)(2,1)S(1)}, bf16[160,512]{1,0:T(8,128)(2,1)S(1)}, u32[]{:S(2)}, u32[]{:S(2)}) %collective-permute-start.30) | collective-permute-done | bytes 163872 | tf_op jit(solution)/shard_map/ppermute | solution.py:386
  67.1 2.0 %collective-permute-start.16 = (bf16[160,512]{1,0:T(8,128)(2,1)S(1)}, bf16[160,512]{1,0:T(8,128)(2,1)S(1)}, u32[]{:S(2)}, u32[]{:S(2)}) collective-permute-start(bf16[160,512]{1,0:T(8,128)(2,1)S(1)} %collective-permute-done.15.refs_6_), channel_id=1, source_target_pairs={{0,1},{1,3},{3,5},{5,7},{7,6},{6,4},{4,2},{2,0},{8,9},{9,11},{11,1... | collective-permute-start | bytes 491528 | tf_op jit(solution)/shard_map/ppermute | solution.py:386
  70.0 3.8 %collective-permute-start.32 = (bf16[160,512]{1,0:T(8,128)(2,1)S(1)}, bf16[160,512]{1,0:T(8,128)(2,1)S(1)}, u32[]{:S(2)}, u32[]{:S(2)}) collective-permute-start(bf16[160,512]{1,0:T(8,128)(2,1)S(1)} %collective-permute-done.30.refs_8_), channel_id=1, source_target_pairs={{1,0},{3,1},{5,3},{7,5},{6,7},{4,6},{2,4},{0,2},{9,8},{11,9},{13,1... | collective-permute-start | bytes 491528 | tf_op jit(solution)/shard_map/ppermute | solution.py:386
  73.8 2.1 %collective-permute-start.21 = (bf16[160,512]{1,0:T(8,128)(2,1)S(1)}, bf16[160,512]{1,0:T(8,128)(2,1)S(1)}, u32[]{:S(2)}, u32[]{:S(2)}) collective-permute-start(bf16[160,512]{1,0:T(8,128)(2,1)S(1)} %collective-permute-done.20.refs_13_.refs_4_), channel_id=1, source_target_pairs={{1,0},{3,1},{5,3},{7,5},{6,7},{4,6},{2,4},{0,2},{9,8},{11,9},{13,1... | collective-permute-start | bytes 491528 | tf_op jit(solution)/shard_map/ppermute | solution.py:386
  76.7 5.7 %norm_project.1 = (f32[992,1024]{1,0:T(8,128)S(1)}, bf16[1280,128]{1,0:T(8,128)(2,1)S(1)}) custom-call(s32[128]{0:T(128)S(1)} %copy-done.4, bf16[160,512]{1,0:T(8,128)(2,1)S(1)} %get-tuple-element.23.refs_1_.refs_0_, bf16[160,512]{1,0:T(8,128)(2,1)S(1)} %get-tuple-element.24.refs_1_, bf16[160,512]{1,0:T(8,128)(2,1)S(1)} %collective-permute-done.14.refs_2_, ...), custom_call_target="tpu_custom_call" | custom-call | flops 2600468480 | bytes 5160960 | tf_op jit(solution)/shard_map/norm_project/pallas_call | solution.py:517
  83.0 3.2 %collective-permute-start.37 = (bf16[160,1280]{1,0:T(8,128)(2,1)S(1)}, bf16[160,1280]{1,0:T(8,128)(2,1)S(1)}, u32[]{:S(2)}, u32[]{:S(2)}) collective-permute-start(bf16[160,1280]{1,0:T(8,128)(2,1)S(1)} %get-tuple-element.38), channel_id=1, source_target_pairs={{0,3},{1,2},{2,5},{3,4},{4,7},{5,6},{6,1},{7,0},{8,15},{9,14},{10,... | collective-permute-start | bytes 1228808 | tf_op jit(solution)/shard_map/ppermute | solution.py:401
  86.3 6.2 %attention.1 = (bf16[320,128]{1,0:T(8,128)(2,1)S(1)}, bf16[320,128]{1,0:T(8,128)(2,1)S(1)}, bf16[320,128]{1,0:T(8,128)(2,1)S(1)}, bf16[1280,128]{1,0:T(8,128)(2,...) custom-call(s32[128]{0:T(128)S(1)} %copy-done.4, ...), custom_call_target="tpu_custom_call" | custom-call | flops 1283457024 | bytes 6094848 | tf_op jit(solution)/shard_map/attention/pallas_call | solution.py:539
  92.5 1.5 %collective-permute-done.37.refs_1_ = bf16[160,1280]{1,0:T(8,128)(2,1)S(1)} collective-permute-done((bf16[160,1280]{1,0:T(8,128)(2,1)S(1)}, bf16[160,1280]{1,0:T(8,128)(2,1)S(1)}, u32[]{:S(2)}, u32[]{:S(2)}) %collective-permute-start.37) | collective-permute-done | bytes 409632 | tf_op jit(solution)/shard_map/ppermute | solution.py:401
  94.5 2.0 %collective-permute-start.34 = (bf16[320,128]{1,0:T(8,128)(2,1)S(1)}, bf16[320,128]{1,0:T(8,128)(2,1)S(1)}, u32[]{:S(2)}, u32[]{:S(2)}) collective-permute-start(bf16[320,128]{1,0:T(8,128)(2,1)S(1)} %get-tuple-element.33), channel_id=1, source_target_pairs={{0,4},{1,5},{2,6},{3,7},{4,0},{5,1},{6,2},{7,3},{8,12},{9,13},{10,... | collective-permute-start | bytes 245768 | tf_op jit(solution)/shard_map/ppermute | solution.py:562
  98.5 2.0 %own_attention.1.refs_0_ = bf16[320,128]{1,0:T(8,128)(2,1)S(1)} custom-call(bf16[992,1024]{1,0:T(8,128)(2,1)S(1)} %get-tuple-element.30.made_ref, bf16[5,1024,64]{2,1,0:T(8,128)(2,1)S(1)} %get-tuple-element.31.key_ref), custom_call_target="tpu_custom_call" | custom-call | flops 167772160 | bytes 2621440 | tf_op jit(solution)/shard_map/own_attention/pallas_call | solution.py:563
  100.5 1.6 %collective-permute-done.34.refs_2_ = bf16[320,128]{1,0:T(8,128)(2,1)S(1)} collective-permute-done((bf16[320,128]{1,0:T(8,128)(2,1)S(1)}, bf16[320,128]{1,0:T(8,128)(2,1)S(1)}, u32[]{:S(2)}, u32[]{:S(2)}) %collective-permute-start.34) | collective-permute-done | bytes 81952 | tf_op jit(solution)/shard_map/ppermute | solution.py:562
  102.5 1.6 %collective-permute-done.33.refs_1_ = bf16[320,128]{1,0:T(8,128)(2,1)S(1)} collective-permute-done((bf16[320,128]{1,0:T(8,128)(2,1)S(1)}, bf16[320,128]{1,0:T(8,128)(2,1)S(1)}, u32[]{:S(2)}, u32[]{:S(2)}) %collective-permute-start.33) | collective-permute-done | bytes 81952 | tf_op jit(solution)/shard_map/ppermute | solution.py:562
  104.0 2.0 %project.1 = bf16[128,1280]{1,0:T(8,128)(2,1)} custom-call(bf16[320,128]{1,0:T(8,128)(2,1)S(1)} %own_attention.1.refs_0_, bf16[320,128]{1,0:T(8,128)(2,1)S(1)} %collective-permute-done.33.refs_1_, bf16[320,128]{1,0:T(8,128)(2,1)S(1)} %collective-permute-done.34.refs_2_, bf16[320,128]{1,0:T(8,128)(2,1)S(1)} %collective-permute-done.35.refs_3_, ...), custom_call_target="tpu_custom_call" | custom-call | flops 419430400 | bytes 4259840 | tf_op jit(solution)/shard_map/project/pallas_call | solution.py:581
  (82 shorter events, 17.1 us)
Async XLA Ops:
  1.0 8.0 %collective-permute-start.3 = (bf16[64,1280]{1,0:T(8,128)(2,1)S(1)}, bf16[64,1280]{1,0:T(8,128)(2,1)S(1)}, u32[]{:S(2)}, u32[]{:S(2)}) collective-permute-start(bf16[64,1280]{1,0:T(8,128)(2,1)S(1)} %get-tuple-element.41.refs_1_), channel_id=1, source_target_pairs={{1,0},{3,1},{5,3},{7,5},{6,7},{4,6},{2,4},{0,2},{9,8},{11,9},{13,1... | collective-permute-start | bytes 491528 | tf_op jit(solution)/shard_map/ppermute | solution.py:386
  4.1 9.5 %collective-permute-start.1 = (bf16[64,1280]{1,0:T(8,128)(2,1)S(1)}, bf16[64,1280]{1,0:T(8,128)(2,1)S(1)}, u32[]{:S(2)}, u32[]{:S(2)}) collective-permute-start(bf16[64,1280]{1,0:T(8,128)(2,1)S(1)} %get-tuple-element.41.refs_1_), channel_id=1, source_target_pairs={{0,1},{1,3},{3,5},{5,7},{7,6},{6,4},{4,2},{2,0},{8,9},{9,11},{11,1... | collective-permute-start | bytes 491528 | tf_op jit(solution)/shard_map/ppermute | solution.py:386
  4.1 11.1 %collective-permute-start.2 = (bf16[64,1280]{1,0:T(8,128)(2,1)S(1)}, bf16[64,1280]{1,0:T(8,128)(2,1)S(1)}, u32[]{:S(2)}, u32[]{:S(2)}) collective-permute-start(bf16[64,1280]{1,0:T(8,128)(2,1)S(1)} %get-tuple-element.42.refs_0_), channel_id=1, source_target_pairs={{1,0},{3,1},{5,3},{7,5},{6,7},{4,6},{2,4},{0,2},{9,8},{11,9},{13,1... | collective-permute-start | bytes 491528 | tf_op jit(solution)/shard_map/ppermute | solution.py:386
  6.1 7.1 %collective-permute-start = (bf16[64,1280]{1,0:T(8,128)(2,1)S(1)}, bf16[64,1280]{1,0:T(8,128)(2,1)S(1)}, u32[]{:S(2)}, u32[]{:S(2)}) collective-permute-start(bf16[64,1280]{1,0:T(8,128)(2,1)S(1)} %get-tuple-element.42.refs_0_), channel_id=1, source_target_pairs={{0,1},{1,3},{3,5},{5,7},{7,6},{6,4},{4,2},{2,0},{8,9},{9,11},{11,1... | collective-permute-start | bytes 491528 | tf_op jit(solution)/shard_map/ppermute | solution.py:386
  9.1 6.5 %collective-permute-start.7 = (bf16[64,1280]{1,0:T(8,128)(2,1)S(1)}, bf16[64,1280]{1,0:T(8,128)(2,1)S(1)}, u32[]{:S(2)}, u32[]{:S(2)}) collective-permute-start(bf16[64,1280]{1,0:T(8,128)(2,1)S(1)} %collective-permute-done.3.refs_5_), channel_id=1, source_target_pairs={{1,0},{3,1},{5,3},{7,5},{6,7},{4,6},{2,4},{0,2},{9,8},{11,9},{13,1... | collective-permute-start | bytes 491528 | tf_op jit(solution)/shard_map/ppermute | solution.py:386
  13.3 7.1 %collective-permute-start.4 = (bf16[64,1280]{1,0:T(8,128)(2,1)S(1)}, bf16[64,1280]{1,0:T(8,128)(2,1)S(1)}, u32[]{:S(2)}, u32[]{:S(2)}) collective-permute-start(bf16[64,1280]{1,0:T(8,128)(2,1)S(1)} %after.6.refs_2_), channel_id=1, source_target_pairs={{0,1},{1,3},{3,5},{5,7},{7,6},{6,4},{4,2},{2,0},{8,9},{9,11},{11,1... | collective-permute-start | bytes 491528 | tf_op jit(solution)/shard_map/ppermute | solution.py:386
  13.6 10.4 %collective-permute-start.5 = (bf16[64,1280]{1,0:T(8,128)(2,1)S(1)}, bf16[64,1280]{1,0:T(8,128)(2,1)S(1)}, u32[]{:S(2)}, u32[]{:S(2)}) collective-permute-start(bf16[64,1280]{1,0:T(8,128)(2,1)S(1)} %collective-permute-done.1.refs_3_), channel_id=1, source_target_pairs={{0,1},{1,3},{3,5},{5,7},{7,6},{6,4},{4,2},{2,0},{8,9},{9,11},{11,1... | collective-permute-start | bytes 491528 | tf_op jit(solution)/shard_map/ppermute | solution.py:386
  15.3 9.0 %collective-permute-start.6 = (bf16[64,1280]{1,0:T(8,128)(2,1)S(1)}, bf16[64,1280]{1,0:T(8,128)(2,1)S(1)}, u32[]{:S(2)}, u32[]{:S(2)}) collective-permute-start(bf16[64,1280]{1,0:T(8,128)(2,1)S(1)} %collective-permute-done.2.refs_4_), channel_id=1, source_target_pairs={{1,0},{3,1},{5,3},{7,5},{6,7},{4,6},{2,4},{0,2},{9,8},{11,9},{13,1... | collective-permute-start | bytes 491528 | tf_op jit(solution)/shard_map/ppermute | solution.py:386
  15.6 10.4 %collective-permute-start.11 = (bf16[64,1280]{1,0:T(8,128)(2,1)S(1)}, bf16[64,1280]{1,0:T(8,128)(2,1)S(1)}, u32[]{:S(2)}, u32[]{:S(2)}) collective-permute-start(bf16[64,1280]{1,0:T(8,128)(2,1)S(1)} %collective-permute-done.7.refs_9_), channel_id=1, source_target_pairs={{1,0},{3,1},{5,3},{7,5},{6,7},{4,6},{2,4},{0,2},{9,8},{11,9},{13,1... | collective-permute-start | bytes 491528 | tf_op jit(solution)/shard_map/ppermute | solution.py:386
  20.4 7.1 %collective-permute-start.8 = (bf16[64,1280]{1,0:T(8,128)(2,1)S(1)}, bf16[64,1280]{1,0:T(8,128)(2,1)S(1)}, u32[]{:S(2)}, u32[]{:S(2)}) collective-permute-start(bf16[64,1280]{1,0:T(8,128)(2,1)S(1)} %collective-permute-done.4.refs_6_), channel_id=1, source_target_pairs={{0,1},{1,3},{3,5},{5,7},{7,6},{6,4},{4,2},{2,0},{8,9},{9,11},{11,1... | collective-permute-start | bytes 491528 | tf_op jit(solution)/shard_map/ppermute | solution.py:386
  23.9 6.4 %collective-permute-start.9 = (bf16[64,1280]{1,0:T(8,128)(2,1)S(1)}, bf16[64,1280]{1,0:T(8,128)(2,1)S(1)}, u32[]{:S(2)}, u32[]{:S(2)}) collective-permute-start(bf16[64,1280]{1,0:T(8,128)(2,1)S(1)} %collective-permute-done.5.refs_7_), channel_id=1, source_target_pairs={{0,1},{1,3},{3,5},{5,7},{7,6},{6,4},{4,2},{2,0},{8,9},{9,11},{11,1... | collective-permute-start | bytes 491528 | tf_op jit(solution)/shard_map/ppermute | solution.py:386
  32.9 11.6 %collective-permute-start.22 = (bf16[208,1280]{1,0:T(8,128)(2,1)S(1)}, bf16[208,1280]{1,0:T(8,128)(2,1)S(1)}, u32[]{:S(2)}, u32[]{:S(2)}) collective-permute-start(bf16[208,1280]{1,0:T(8,128)(2,1)S(1)} %get-tuple-element.25), channel_id=1, source_target_pairs={{0,1},{1,0},{2,3},{3,2},{4,5},{5,4},{6,7},{7,6},{8,9},{9,8},{10,11... | collective-permute-start | bytes 1597448 | tf_op jit(solution)/shard_map/ppermute | solution.py:401
  33.4 30.3 %collective-permute-start.23 = (bf16[160,1280]{1,0:T(8,128)(2,1)S(1)}, bf16[160,1280]{1,0:T(8,128)(2,1)S(1)}, u32[]{:S(2)}, u32[]{:S(2)}) collective-permute-start(bf16[160,1280]{1,0:T(8,128)(2,1)S(1)} %get-tuple-element.26.refs_1_), channel_id=1, source_target_pairs={{0,2},{1,3},{2,4},{3,5},{4,6},{5,7},{6,0},{7,1},{8,12},{9,13},{10,... | collective-permute-start | bytes 1228808 | tf_op jit(solution)/shard_map/ppermute | solution.py:401
  42.4 10.4 %collective-permute-start.27 = (bf16[160,512]{1,0:T(8,128)(2,1)S(1)}, bf16[160,512]{1,0:T(8,128)(2,1)S(1)}, u32[]{:S(2)}, u32[]{:S(2)}) collective-permute-start(bf16[160,512]{1,0:T(8,128)(2,1)S(1)} %get-tuple-element.24.refs_1_), channel_id=1, source_target_pairs={{0,1},{1,3},{3,5},{5,7},{7,6},{6,4},{4,2},{2,0},{8,9},{9,11},{11,1... | collective-permute-start | bytes 491528 | tf_op jit(solution)/shard_map/ppermute | solution.py:386
  44.1 10.7 %collective-permute-start.18 = (bf16[160,512]{1,0:T(8,128)(2,1)S(1)}, bf16[160,512]{1,0:T(8,128)(2,1)S(1)}, u32[]{:S(2)}, u32[]{:S(2)}) collective-permute-start(bf16[160,512]{1,0:T(8,128)(2,1)S(1)} %get-tuple-element.24.refs_1_), channel_id=1, source_target_pairs={{1,0},{3,1},{5,3},{7,5},{6,7},{4,6},{2,4},{0,2},{9,8},{11,9},{13,1... | collective-permute-start | bytes 491528 | tf_op jit(solution)/shard_map/ppermute | solution.py:386
  44.5 19.2 %collective-permute-start.24 = (bf16[128,1280]{1,0:T(8,128)(2,1)S(1)}, bf16[128,1280]{1,0:T(8,128)(2,1)S(1)}, u32[]{:S(2)}, u32[]{:S(2)}) collective-permute-start(bf16[128,1280]{1,0:T(8,128)(2,1)S(1)} %slice.24.refs_0_), channel_id=1, source_target_pairs={{0,16},{8,24},{16,0},{24,8},{1,17},{9,25},{17,1},{25,9},{2,18},{10... | collective-permute-start | bytes 983048 | tf_op jit(solution)/shard_map/ppermute | solution.py:406
  52.8 7.0 %collective-permute-start.14 = (bf16[160,512]{1,0:T(8,128)(2,1)S(1)}, bf16[160,512]{1,0:T(8,128)(2,1)S(1)}, u32[]{:S(2)}, u32[]{:S(2)}) collective-permute-start(bf16[160,512]{1,0:T(8,128)(2,1)S(1)} %get-tuple-element.23.refs_1_.refs_0_), channel_id=1, source_target_pairs={{0,1},{1,3},{3,5},{5,7},{7,6},{6,4},{4,2},{2,0},{8,9},{9,11},{11,1... | collective-permute-start | bytes 491528 | tf_op jit(solution)/shard_map/ppermute | solution.py:386
  54.8 6.4 %collective-permute-start.29 = (bf16[160,512]{1,0:T(8,128)(2,1)S(1)}, bf16[160,512]{1,0:T(8,128)(2,1)S(1)}, u32[]{:S(2)}, u32[]{:S(2)}) collective-permute-start(bf16[160,512]{1,0:T(8,128)(2,1)S(1)} %collective-permute-done.27.refs_3_), channel_id=1, source_target_pairs={{0,1},{1,3},{3,5},{5,7},{7,6},{6,4},{4,2},{2,0},{8,9},{9,11},{11,1... | collective-permute-start | bytes 491528 | tf_op jit(solution)/shard_map/ppermute | solution.py:386
  63.7 6.3 %collective-permute-start.31 = (bf16[160,512]{1,0:T(8,128)(2,1)S(1)}, bf16[160,512]{1,0:T(8,128)(2,1)S(1)}, u32[]{:S(2)}, u32[]{:S(2)}) collective-permute-start(bf16[160,512]{1,0:T(8,128)(2,1)S(1)} %collective-permute-done.29.refs_7_), channel_id=1, source_target_pairs={{0,1},{1,3},{3,5},{5,7},{7,6},{6,4},{4,2},{2,0},{8,9},{9,11},{11,1... | collective-permute-start | bytes 491528 | tf_op jit(solution)/shard_map/ppermute | solution.py:386
  63.7 12.9 %collective-permute-start.25 = (bf16[128,1280]{1,0:T(8,128)(2,1)S(1)}, bf16[128,1280]{1,0:T(8,128)(2,1)S(1)}, u32[]{:S(2)}, u32[]{:S(2)}) collective-permute-start(bf16[128,1280]{1,0:T(8,128)(2,1)S(1)} %get-tuple-element.27.refs_17_.refs_5_), channel_id=1, source_target_pairs={{0,8},{8,0},{16,24},{24,16},{1,9},{9,1},{17,25},{25,17},{2,10},{10... | collective-permute-start | bytes 983048 | tf_op jit(solution)/shard_map/ppermute | solution.py:406
  64.2 12.5 %collective-permute-start.26 = (bf16[128,1280]{1,0:T(8,128)(2,1)S(1)}, bf16[128,1280]{1,0:T(8,128)(2,1)S(1)}, u32[]{:S(2)}, u32[]{:S(2)}) collective-permute-start(bf16[128,1280]{1,0:T(8,128)(2,1)S(1)} %collective-permute-done.24.refs_2_.refs_18_.refs_6_), channel_id=1, source_target_pairs={{0,8},{8,0},{16,24},{24,16},{1,9},{9,1},{17,25},{25,17},{2,10},{10... | collective-permute-start | bytes 983048 | tf_op jit(solution)/shard_map/ppermute | solution.py:406
  65.9 7.9 %collective-permute-start.20 = (bf16[160,512]{1,0:T(8,128)(2,1)S(1)}, bf16[160,512]{1,0:T(8,128)(2,1)S(1)}, u32[]{:S(2)}, u32[]{:S(2)}) collective-permute-start(bf16[160,512]{1,0:T(8,128)(2,1)S(1)} %collective-permute-done.19.refs_9_), channel_id=1, source_target_pairs={{1,0},{3,1},{5,3},{7,5},{6,7},{4,6},{2,4},{0,2},{9,8},{11,9},{13,1... | collective-permute-start | bytes 491528 | tf_op jit(solution)/shard_map/ppermute | solution.py:386
  67.1 8.9 %collective-permute-start.16 = (bf16[160,512]{1,0:T(8,128)(2,1)S(1)}, bf16[160,512]{1,0:T(8,128)(2,1)S(1)}, u32[]{:S(2)}, u32[]{:S(2)}) collective-permute-start(bf16[160,512]{1,0:T(8,128)(2,1)S(1)} %collective-permute-done.15.refs_6_), channel_id=1, source_target_pairs={{0,1},{1,3},{3,5},{5,7},{7,6},{6,4},{4,2},{2,0},{8,9},{9,11},{11,1... | collective-permute-start | bytes 491528 | tf_op jit(solution)/shard_map/ppermute | solution.py:386
  70.0 6.7 %collective-permute-start.32 = (bf16[160,512]{1,0:T(8,128)(2,1)S(1)}, bf16[160,512]{1,0:T(8,128)(2,1)S(1)}, u32[]{:S(2)}, u32[]{:S(2)}) collective-permute-start(bf16[160,512]{1,0:T(8,128)(2,1)S(1)} %collective-permute-done.30.refs_8_), channel_id=1, source_target_pairs={{1,0},{3,1},{5,3},{7,5},{6,7},{4,6},{2,4},{0,2},{9,8},{11,9},{13,1... | collective-permute-start | bytes 491528 | tf_op jit(solution)/shard_map/ppermute | solution.py:386
  73.8 8.6 %collective-permute-start.21 = (bf16[160,512]{1,0:T(8,128)(2,1)S(1)}, bf16[160,512]{1,0:T(8,128)(2,1)S(1)}, u32[]{:S(2)}, u32[]{:S(2)}) collective-permute-start(bf16[160,512]{1,0:T(8,128)(2,1)S(1)} %collective-permute-done.20.refs_13_.refs_4_), channel_id=1, source_target_pairs={{1,0},{3,1},{5,3},{7,5},{6,7},{4,6},{2,4},{0,2},{9,8},{11,9},{13,1... | collective-permute-start | bytes 491528 | tf_op jit(solution)/shard_map/ppermute | solution.py:386
  75.9 6.5 %collective-permute-start.17 = (bf16[160,512]{1,0:T(8,128)(2,1)S(1)}, bf16[160,512]{1,0:T(8,128)(2,1)S(1)}, u32[]{:S(2)}, u32[]{:S(2)}) collective-permute-start(bf16[160,512]{1,0:T(8,128)(2,1)S(1)} %collective-permute-done.16.refs_10_), channel_id=1, source_target_pairs={{0,1},{1,3},{3,5},{5,7},{7,6},{6,4},{4,2},{2,0},{8,9},{9,11},{11,1... | collective-permute-start | bytes 491528 | tf_op jit(solution)/shard_map/ppermute | solution.py:386
  82.4 10.0 %collective-permute-start.36 = (bf16[160,1280]{1,0:T(8,128)(2,1)S(1)}, bf16[160,1280]{1,0:T(8,128)(2,1)S(1)}, u32[]{:S(2)}, u32[]{:S(2)}) collective-permute-start(bf16[160,1280]{1,0:T(8,128)(2,1)S(1)} %get-tuple-element.37), channel_id=1, source_target_pairs={{0,16},{8,24},{16,0},{24,8},{1,17},{9,25},{17,1},{25,9},{2,18},{10... | collective-permute-start | bytes 1228808 | tf_op jit(solution)/shard_map/ppermute | solution.py:406
  83.0 11.0 %collective-permute-start.37 = (bf16[160,1280]{1,0:T(8,128)(2,1)S(1)}, bf16[160,1280]{1,0:T(8,128)(2,1)S(1)}, u32[]{:S(2)}, u32[]{:S(2)}) collective-permute-start(bf16[160,1280]{1,0:T(8,128)(2,1)S(1)} %get-tuple-element.38), channel_id=1, source_target_pairs={{0,3},{1,2},{2,5},{3,4},{4,7},{5,6},{6,1},{7,0},{8,15},{9,14},{10,... | collective-permute-start | bytes 1228808 | tf_op jit(solution)/shard_map/ppermute | solution.py:401
  94.0 10.0 %collective-permute-start.38 = (bf16[400,1280]{1,0:T(8,128)(2,1)S(1)}, bf16[400,1280]{1,0:T(8,128)(2,1)S(1)}, u32[]{:S(2)}, u32[]{:S(2)}) collective-permute-start(bf16[400,1280]{1,0:T(8,128)(2,1)S(1)} %get-tuple-element.39.refs_6_), channel_id=1, source_target_pairs={{0,8},{8,0},{16,24},{24,16},{1,9},{9,1},{17,25},{25,17},{2,10},{10... | collective-permute-start | bytes 3072008 | tf_op jit(solution)/shard_map/ppermute | solution.py:406
  94.0 10.0 %collective-permute-start.39 = (bf16[160,1280]{1,0:T(8,128)(2,1)S(1)}, bf16[160,1280]{1,0:T(8,128)(2,1)S(1)}, u32[]{:S(2)}, u32[]{:S(2)}) collective-permute-start(bf16[160,1280]{1,0:T(8,128)(2,1)S(1)} %get-tuple-element.40.refs_8_), channel_id=1, source_target_pairs={{0,8},{8,0},{16,24},{24,16},{1,9},{9,1},{17,25},{25,17},{2,10},{10... | collective-permute-start | bytes 1228808 | tf_op jit(solution)/shard_map/ppermute | solution.py:406
  94.5 7.6 %collective-permute-start.34 = (bf16[320,128]{1,0:T(8,128)(2,1)S(1)}, bf16[320,128]{1,0:T(8,128)(2,1)S(1)}, u32[]{:S(2)}, u32[]{:S(2)}) collective-permute-start(bf16[320,128]{1,0:T(8,128)(2,1)S(1)} %get-tuple-element.33), channel_id=1, source_target_pairs={{0,4},{1,5},{2,6},{3,7},{4,0},{5,1},{6,2},{7,3},{8,12},{9,13},{10,... | collective-permute-start | bytes 245768 | tf_op jit(solution)/shard_map/ppermute | solution.py:562
  97.7 6.3 %collective-permute-start.33 = (bf16[320,128]{1,0:T(8,128)(2,1)S(1)}, bf16[320,128]{1,0:T(8,128)(2,1)S(1)}, u32[]{:S(2)}, u32[]{:S(2)}) collective-permute-start(bf16[320,128]{1,0:T(8,128)(2,1)S(1)} %get-tuple-element.32.refs_2_), channel_id=1, source_target_pairs={{0,2},{1,3},{2,4},{3,5},{4,6},{5,7},{6,0},{7,1},{8,10},{9,11},{10,... | collective-permute-start | bytes 245768 | tf_op jit(solution)/shard_map/ppermute | solution.py:562
  (15 other events, 196.5 us)

commit v8 on v7

--- a/solution.py
+++ b/solution.py
@@ -471,7 +471,7 @@
         name="stats",
     )(*pieces[:-2])
     if inner == 2:
-        chosen, out_own = after(chosen + [w_out], pieces[-5:] + [stats])
+        chosen, out_own = after(chosen + [w_out], pieces[-6:-2])
         chosen = send(chosen, [(0, 1)])
         far = send(out_own, FAR)
     else:
@@ -532,7 +532,7 @@
         name="norm_project",
     )(sources, *hidden_pieces[:-2], *weights)
     if inner == 2:
-        far, out_own = after([far, out_own], hidden_pieces[-5:] + [sums])
+        far, out_own = after([far, out_own], hidden_pieces[-6:-2])
         across = swap(far, 2)
         last = send(out_own, LAST)
     one_block = jax.ShapeDtypeStruct((SET_CHANNELS, block), bf16)

time: 106 us -> 106 us (level)
  starting transfers between devices: 51.9 us -> 49 us
  waiting for transfers between devices: 26.2 us -> 28.4 us
    ppermute x6, starting transfers between devices: 9.58 us -> 1.15 us  [swap(): return lax.ppermute(block, 'batch', pairs)]
    ppermute x28, starting transfers between devices: 33.1 us -> 38.6 us  [gather(): lax.ppermute(found[half, sign * (step - 1)], 'patch', pairs)]
    ppermute x28, waiting for transfers between devices: 21.1 us -> 24.5 us  [gather(): lax.ppermute(found[half, sign * (step - 1)], 'patch', pairs)]
    ppermute x3, waiting for transfers between devices: 1.5 us -> 0.01 us  [send(): return lax.ppermute(block, ('batch', 'patch'), pairs)]
  transfers between devices with their start and end apart: 40 -> 40, of which waited for: 17 -> 15; matrix products, arithmetic and copies ran while one was open for 2% -> 2% of each run, Pallas kernels for 21% -> 21%
where the time goes in v8:
time: 106 us; the launch traced here: 105 us
  starting transfers between devices  49 us (46%)
  waiting for transfers between devices  28.4 us (27%)
  Pallas kernels  24.2 us (23%)
  local copies, waits for them, and re-layouts  2.06 us (2%)
  other arithmetic  1.34 us (1%)
    ppermute x28, starting transfers between devices, gather(): lax.ppermute(found[half, sign * (step - 1)], 'patch', pairs)  38.6 us
    ppermute x28, waiting for transfers between devices, gather(): lax.ppermute(found[half, sign * (step - 1)], 'patch', pairs)  24.5 us
    pallas_call x1, Pallas kernels, on_device(): pl.pallas_call(functools.partial(conv_kernel, columns), out_shape=[jax.Sh...  7.47 us
    pallas_call x1, Pallas kernels, on_device(): pl.pallas_call(functools.partial(attention_kernel, 2 * n, inner), out_sha...  6.17 us
    ppermute x3, starting transfers between devices, send(): return lax.ppermute(block, ('batch', 'patch'), pairs)  5.89 us
    pallas_call x1, Pallas kernels, on_device(): pl.pallas_call(functools.partial(project_kernel, 2 * n), out_shape=[jax.S...  5.7 us
    ppermute x3, waiting for transfers between devices, on_device(): received.append(lax.ppermute(sent_block, 'patch', pairs))  3.91 us
    ppermute x3, starting transfers between devices, on_device(): received.append(lax.ppermute(sent_block, 'patch', pairs))  3.41 us
  transfers between devices with their start and end apart: 40, of which 15 were waited for; matrix products, arithmetic and copies ran while one was open for 2% of the time, Pallas kernels for 21%

profile of v8, /device:TPU:0, one launch (start us, length us, event | category | flops | bytes accessed | tf_op | source)
XLA Modules:
  0.0 105.3 jit_solution(14327036273062170986)
XLA Ops:
  1.0 3.1 %collective-permute-start.3 = (bf16[64,1280]{1,0:T(8,128)(2,1)S(1)}, bf16[64,1280]{1,0:T(8,128)(2,1)S(1)}, u32[]{:S(2)}, u32[]{:S(2)}) collective-permute-start(bf16[64,1280]{1,0:T(8,128)(2,1)S(1)} %get-tuple-element.41.refs_1_), channel_id=1, source_target_pairs={{1,0},{3,1},{5,3},{7,5},{6,7},{4,6},{2,4},{0,2},{9,8},{11,9},{13,1... | collective-permute-start | bytes 491528 | tf_op jit(solution)/shard_map/ppermute | solution.py:386
  4.1 2.0 %collective-permute-start.2 = (bf16[64,1280]{1,0:T(8,128)(2,1)S(1)}, bf16[64,1280]{1,0:T(8,128)(2,1)S(1)}, u32[]{:S(2)}, u32[]{:S(2)}) collective-permute-start(bf16[64,1280]{1,0:T(8,128)(2,1)S(1)} %get-tuple-element.42.refs_0_), channel_id=1, source_target_pairs={{1,0},{3,1},{5,3},{7,5},{6,7},{4,6},{2,4},{0,2},{9,8},{11,9},{13,1... | collective-permute-start | bytes 491528 | tf_op jit(solution)/shard_map/ppermute | solution.py:386
  9.1 2.1 %collective-permute-start.7 = (bf16[64,1280]{1,0:T(8,128)(2,1)S(1)}, bf16[64,1280]{1,0:T(8,128)(2,1)S(1)}, u32[]{:S(2)}, u32[]{:S(2)}) collective-permute-start(bf16[64,1280]{1,0:T(8,128)(2,1)S(1)} %collective-permute-done.3.refs_5_), channel_id=1, source_target_pairs={{1,0},{3,1},{5,3},{7,5},{6,7},{4,6},{2,4},{0,2},{9,8},{11,9},{13,1... | collective-permute-start | bytes 491528 | tf_op jit(solution)/shard_map/ppermute | solution.py:386
  11.2 2.1 %collective-permute-done.refs_0_ = bf16[64,1280]{1,0:T(8,128)(2,1)S(1)} collective-permute-done((bf16[64,1280]{1,0:T(8,128)(2,1)S(1)}, bf16[64,1280]{1,0:T(8,128)(2,1)S(1)}, u32[]{:S(2)}, u32[]{:S(2)}) %collective-permute-start) | collective-permute-done | bytes 163872 | tf_op jit(solution)/shard_map/ppermute | solution.py:386
  13.6 1.7 %collective-permute-start.5 = (bf16[64,1280]{1,0:T(8,128)(2,1)S(1)}, bf16[64,1280]{1,0:T(8,128)(2,1)S(1)}, u32[]{:S(2)}, u32[]{:S(2)}) collective-permute-start(bf16[64,1280]{1,0:T(8,128)(2,1)S(1)} %collective-permute-done.1.refs_3_), channel_id=1, source_target_pairs={{0,1},{1,3},{3,5},{5,7},{7,6},{6,4},{4,2},{2,0},{8,9},{9,11},{11,1... | collective-permute-start | bytes 491528 | tf_op jit(solution)/shard_map/ppermute | solution.py:386
  15.6 1.9 %collective-permute-start.11 = (bf16[64,1280]{1,0:T(8,128)(2,1)S(1)}, bf16[64,1280]{1,0:T(8,128)(2,1)S(1)}, u32[]{:S(2)}, u32[]{:S(2)}) collective-permute-start(bf16[64,1280]{1,0:T(8,128)(2,1)S(1)} %collective-permute-done.7.refs_9_), channel_id=1, source_target_pairs={{1,0},{3,1},{5,3},{7,5},{6,7},{4,6},{2,4},{0,2},{9,8},{11,9},{13,1... | collective-permute-start | bytes 491528 | tf_op jit(solution)/shard_map/ppermute | solution.py:386
  17.5 2.9 %collective-permute-done.4.refs_6_ = bf16[64,1280]{1,0:T(8,128)(2,1)S(1)} collective-permute-done((bf16[64,1280]{1,0:T(8,128)(2,1)S(1)}, bf16[64,1280]{1,0:T(8,128)(2,1)S(1)}, u32[]{:S(2)}, u32[]{:S(2)}) %collective-permute-start.4) | collective-permute-done | bytes 163872 | tf_op jit(solution)/shard_map/ppermute | solution.py:386
  20.7 3.2 %collective-permute-done.5.refs_7_ = bf16[64,1280]{1,0:T(8,128)(2,1)S(1)} collective-permute-done((bf16[64,1280]{1,0:T(8,128)(2,1)S(1)}, bf16[64,1280]{1,0:T(8,128)(2,1)S(1)}, u32[]{:S(2)}, u32[]{:S(2)}) %collective-permute-start.5) | collective-permute-done | bytes 163872 | tf_op jit(solution)/shard_map/ppermute | solution.py:386
  24.2 1.7 %collective-permute-start.10 = (bf16[64,1280]{1,0:T(8,128)(2,1)S(1)}, bf16[64,1280]{1,0:T(8,128)(2,1)S(1)}, u32[]{:S(2)}, u32[]{:S(2)}) collective-permute-start(bf16[64,1280]{1,0:T(8,128)(2,1)S(1)} %collective-permute-done.6.refs_8_), channel_id=1, source_target_pairs={{1,0},{3,1},{5,3},{7,5},{6,7},{4,6},{2,4},{0,2},{9,8},{11,9},{13,1... | collective-permute-start | bytes 491528 | tf_op jit(solution)/shard_map/ppermute | solution.py:386
  26.0 1.6 %collective-permute-start.13 = (bf16[64,1280]{1,0:T(8,128)(2,1)S(1)}, bf16[64,1280]{1,0:T(8,128)(2,1)S(1)}, u32[]{:S(2)}, u32[]{:S(2)}) collective-permute-start(bf16[64,1280]{1,0:T(8,128)(2,1)S(1)} %collective-permute-done.11.refs_13_.refs_5_), channel_id=1, source_target_pairs={{1,0},{3,1},{5,3},{7,5},{6,7},{4,6},{2,4},{0,2},{9,8},{11,9},{13,1... | collective-permute-start | bytes 491528 | tf_op jit(solution)/shard_map/ppermute | solution.py:386
  28.1 2.3 %collective-permute-done.9.refs_11_.refs_3_ = bf16[64,1280]{1,0:T(8,128)(2,1)S(1)} collective-permute-done((bf16[64,1280]{1,0:T(8,128)(2,1)S(1)}, bf16[64,1280]{1,0:T(8,128)(2,1)S(1)}, u32[]{:S(2)}, u32[]{:S(2)}) %collective-permute-start.9) | collective-permute-done | bytes 163872 | tf_op jit(solution)/shard_map/ppermute | solution.py:386
  31.4 2.9 %collective-permute-start.23 = (bf16[160,1280]{1,0:T(8,128)(2,1)S(1)}, bf16[160,1280]{1,0:T(8,128)(2,1)S(1)}, u32[]{:S(2)}, u32[]{:S(2)}) collective-permute-start(bf16[160,1280]{1,0:T(8,128)(2,1)S(1)} %get-tuple-element.26.refs_1_), channel_id=1, source_target_pairs={{0,2},{1,3},{2,4},{3,5},{4,6},{5,7},{6,0},{7,1},{8,12},{9,13},{10,... | collective-permute-start | bytes 1228808 | tf_op jit(solution)/shard_map/ppermute | solution.py:401
  35.3 7.5 %norm_conv.1 = (bf16[160,512]{1,0:T(8,128)(2,1)S(1)}, bf16[160,512]{1,0:T(8,128)(2,1)S(1)}) custom-call(s32[128]{0:T(128)S(1)} %copy-done.4, bf16[64,1280]{1,0:T(8,128)(2,1)S(1)} %get-tuple-element.42.refs_0_, bf16[64,1280]{1,0:T(8,128)(2,1)S(1)} %get-tuple-element.41.refs_1_, bf16[64,1280]{1,0:T(8,128)(2,1)S(1)} %after.6.refs_2_, ...), custom_call_target="tpu_custom_call" | custom-call | flops 3774873600 | bytes 6307840 | tf_op jit(solution)/shard_map/norm_conv/pallas_call | solution.py:484
  43.7 8.8 %collective-permute-start.18 = (bf16[160,512]{1,0:T(8,128)(2,1)S(1)}, bf16[160,512]{1,0:T(8,128)(2,1)S(1)}, u32[]{:S(2)}, u32[]{:S(2)}) collective-permute-start(bf16[160,512]{1,0:T(8,128)(2,1)S(1)} %get-tuple-element.24.refs_1_), channel_id=1, source_target_pairs={{1,0},{3,1},{5,3},{7,5},{6,7},{4,6},{2,4},{0,2},{9,8},{11,9},{13,1... | collective-permute-start | bytes 491528 | tf_op jit(solution)/shard_map/ppermute | solution.py:386
  52.7 2.0 %collective-permute-start.28 = (bf16[160,512]{1,0:T(8,128)(2,1)S(1)}, bf16[160,512]{1,0:T(8,128)(2,1)S(1)}, u32[]{:S(2)}, u32[]{:S(2)}) collective-permute-start(bf16[160,512]{1,0:T(8,128)(2,1)S(1)} %get-tuple-element.23.refs_1_.refs_0_), channel_id=1, source_target_pairs={{1,0},{3,1},{5,3},{7,5},{6,7},{4,6},{2,4},{0,2},{9,8},{11,9},{13,1... | collective-permute-start | bytes 491528 | tf_op jit(solution)/shard_map/ppermute | solution.py:386
  54.7 2.0 %collective-permute-done.27.refs_3_ = bf16[160,512]{1,0:T(8,128)(2,1)S(1)} collective-permute-done((bf16[160,512]{1,0:T(8,128)(2,1)S(1)}, bf16[160,512]{1,0:T(8,128)(2,1)S(1)}, u32[]{:S(2)}, u32[]{:S(2)}) %collective-permute-start.27) | collective-permute-done | bytes 163872 | tf_op jit(solution)/shard_map/ppermute | solution.py:386
  58.0 2.5 %collective-permute-start.29 = (bf16[160,512]{1,0:T(8,128)(2,1)S(1)}, bf16[160,512]{1,0:T(8,128)(2,1)S(1)}, u32[]{:S(2)}, u32[]{:S(2)}) collective-permute-start(bf16[160,512]{1,0:T(8,128)(2,1)S(1)} %collective-permute-done.27.refs_3_), channel_id=1, source_target_pairs={{0,1},{1,3},{3,5},{5,7},{7,6},{6,4},{4,2},{2,0},{8,9},{9,11},{11,1... | collective-permute-start | bytes 491528 | tf_op jit(solution)/shard_map/ppermute | solution.py:386
  60.5 2.2 %collective-permute-done.14.refs_2_ = bf16[160,512]{1,0:T(8,128)(2,1)S(1)} collective-permute-done((bf16[160,512]{1,0:T(8,128)(2,1)S(1)}, bf16[160,512]{1,0:T(8,128)(2,1)S(1)}, u32[]{:S(2)}, u32[]{:S(2)}) %collective-permute-start.14) | collective-permute-done | bytes 163872 | tf_op jit(solution)/shard_map/ppermute | solution.py:386
  62.7 2.0 %collective-permute-start.30 = (bf16[160,512]{1,0:T(8,128)(2,1)S(1)}, bf16[160,512]{1,0:T(8,128)(2,1)S(1)}, u32[]{:S(2)}, u32[]{:S(2)}) collective-permute-start(bf16[160,512]{1,0:T(8,128)(2,1)S(1)} %collective-permute-done.28.refs_4_), channel_id=1, source_target_pairs={{1,0},{3,1},{5,3},{7,5},{6,7},{4,6},{2,4},{0,2},{9,8},{11,9},{13,1... | collective-permute-start | bytes 491528 | tf_op jit(solution)/shard_map/ppermute | solution.py:386
  66.4 1.7 %collective-permute-done.30.refs_8_ = bf16[160,512]{1,0:T(8,128)(2,1)S(1)} collective-permute-done((bf16[160,512]{1,0:T(8,128)(2,1)S(1)}, bf16[160,512]{1,0:T(8,128)(2,1)S(1)}, u32[]{:S(2)}, u32[]{:S(2)}) %collective-permute-start.30) | collective-permute-done | bytes 163872 | tf_op jit(solution)/shard_map/ppermute | solution.py:386
  68.0 2.0 %collective-permute-start.20 = (bf16[160,512]{1,0:T(8,128)(2,1)S(1)}, bf16[160,512]{1,0:T(8,128)(2,1)S(1)}, u32[]{:S(2)}, u32[]{:S(2)}) collective-permute-start(bf16[160,512]{1,0:T(8,128)(2,1)S(1)} %collective-permute-done.19.refs_9_), channel_id=1, source_target_pairs={{1,0},{3,1},{5,3},{7,5},{6,7},{4,6},{2,4},{0,2},{9,8},{11,9},{13,1... | collective-permute-start | bytes 491528 | tf_op jit(solution)/shard_map/ppermute | solution.py:386
  70.1 2.0 %collective-permute-done.31.refs_11_.refs_3_ = bf16[160,512]{1,0:T(8,128)(2,1)S(1)} collective-permute-done((bf16[160,512]{1,0:T(8,128)(2,1)S(1)}, bf16[160,512]{1,0:T(8,128)(2,1)S(1)}, u32[]{:S(2)}, u32[]{:S(2)}) %collective-permute-start.31) | collective-permute-done | bytes 163872 | tf_op jit(solution)/shard_map/ppermute | solution.py:386
  72.1 2.4 %collective-permute-done.20.refs_13_.refs_5_ = bf16[160,512]{1,0:T(8,128)(2,1)S(1)} collective-permute-done((bf16[160,512]{1,0:T(8,128)(2,1)S(1)}, bf16[160,512]{1,0:T(8,128)(2,1)S(1)}, u32[]{:S(2)}, u32[]{:S(2)}) %collective-permute-start.20) | collective-permute-done | bytes 163872 | tf_op jit(solution)/shard_map/ppermute | solution.py:386
  74.6 1.8 %collective-permute-done.32.refs_12_.refs_4_ = bf16[160,512]{1,0:T(8,128)(2,1)S(1)} collective-permute-done((bf16[160,512]{1,0:T(8,128)(2,1)S(1)}, bf16[160,512]{1,0:T(8,128)(2,1)S(1)}, u32[]{:S(2)}, u32[]{:S(2)}) %collective-permute-start.32) | collective-permute-done | bytes 163872 | tf_op jit(solution)/shard_map/ppermute | solution.py:386
  78.1 1.5 %collective-permute-start.17 = (bf16[160,512]{1,0:T(8,128)(2,1)S(1)}, bf16[160,512]{1,0:T(8,128)(2,1)S(1)}, u32[]{:S(2)}, u32[]{:S(2)}) collective-permute-start(bf16[160,512]{1,0:T(8,128)(2,1)S(1)} %collective-permute-done.16.refs_10_.refs_2_), channel_id=1, source_target_pairs={{0,1},{1,3},{3,5},{5,7},{7,6},{6,4},{4,2},{2,0},{8,9},{9,11},{11,1... | collective-permute-start | bytes 491528 | tf_op jit(solution)/shard_map/ppermute | solution.py:386
  79.5 2.0 %collective-permute-start.37 = (bf16[160,1280]{1,0:T(8,128)(2,1)S(1)}, bf16[160,1280]{1,0:T(8,128)(2,1)S(1)}, u32[]{:S(2)}, u32[]{:S(2)}) collective-permute-start(bf16[160,1280]{1,0:T(8,128)(2,1)S(1)} %get-tuple-element.38), channel_id=1, source_target_pairs={{0,3},{1,2},{2,5},{3,4},{4,7},{5,6},{6,1},{7,0},{8,15},{9,14},{10,... | collective-permute-start | bytes 1228808 | tf_op jit(solution)/shard_map/ppermute | solution.py:401
  81.5 5.7 %norm_project.1 = (f32[992,1024]{1,0:T(8,128)S(1)}, bf16[1280,128]{1,0:T(8,128)(2,1)S(1)}) custom-call(s32[128]{0:T(128)S(1)} %copy-done.4, bf16[160,512]{1,0:T(8,128)(2,1)S(1)} %get-tuple-element.23.refs_1_.refs_0_, bf16[160,512]{1,0:T(8,128)(2,1)S(1)} %get-tuple-element.24.refs_1_, bf16[160,512]{1,0:T(8,128)(2,1)S(1)} %collective-permute-done.14.refs_2_, ...), custom_call_target="tpu_custom_call" | custom-call | flops 2600468480 | bytes 5160960 | tf_op jit(solution)/shard_map/norm_project/pallas_call | solution.py:517
  87.2 6.2 %attention.1 = (bf16[320,128]{1,0:T(8,128)(2,1)S(1)}, bf16[320,128]{1,0:T(8,128)(2,1)S(1)}, bf16[320,128]{1,0:T(8,128)(2,1)S(1)}, bf16[1280,128]{1,0:T(8,128)(2,...) custom-call(s32[128]{0:T(128)S(1)} %copy-done.4, ...), custom_call_target="tpu_custom_call" | custom-call | flops 1283457024 | bytes 6094848 | tf_op jit(solution)/shard_map/attention/pallas_call | solution.py:539
  95.5 1.6 %collective-permute-start.35 = (bf16[320,128]{1,0:T(8,128)(2,1)S(1)}, bf16[320,128]{1,0:T(8,128)(2,1)S(1)}, u32[]{:S(2)}, u32[]{:S(2)}) collective-permute-start(bf16[320,128]{1,0:T(8,128)(2,1)S(1)} %get-tuple-element.34), channel_id=1, source_target_pairs={{0,6},{1,7},{2,0},{3,1},{4,2},{5,3},{6,4},{7,5},{8,14},{9,15},{10,... | collective-permute-start | bytes 245768 | tf_op jit(solution)/shard_map/ppermute | solution.py:562
  97.5 1.9 %own_attention.1.refs_0_ = bf16[320,128]{1,0:T(8,128)(2,1)S(1)} custom-call(bf16[992,1024]{1,0:T(8,128)(2,1)S(1)} %get-tuple-element.30.made_ref, bf16[5,1024,64]{2,1,0:T(8,128)(2,1)S(1)} %get-tuple-element.31.key_ref), custom_call_target="tpu_custom_call" | custom-call | flops 167772160 | bytes 2621440 | tf_op jit(solution)/shard_map/own_attention/pallas_call | solution.py:563
  99.5 2.1 %collective-permute-done.34.refs_2_ = bf16[320,128]{1,0:T(8,128)(2,1)S(1)} collective-permute-done((bf16[320,128]{1,0:T(8,128)(2,1)S(1)}, bf16[320,128]{1,0:T(8,128)(2,1)S(1)}, u32[]{:S(2)}, u32[]{:S(2)}) %collective-permute-start.34) | collective-permute-done | bytes 81952 | tf_op jit(solution)/shard_map/ppermute | solution.py:562
  103.4 2.0 %project.1 = bf16[128,1280]{1,0:T(8,128)(2,1)} custom-call(bf16[320,128]{1,0:T(8,128)(2,1)S(1)} %own_attention.1.refs_0_, bf16[320,128]{1,0:T(8,128)(2,1)S(1)} %collective-permute-done.33.refs_1_, bf16[320,128]{1,0:T(8,128)(2,1)S(1)} %collective-permute-done.34.refs_2_, bf16[320,128]{1,0:T(8,128)(2,1)S(1)} %collective-permute-done.35.refs_3_, ...), custom_call_target="tpu_custom_call" | custom-call | flops 419430400 | bytes 4259840 | tf_op jit(solution)/shard_map/project/pallas_call | solution.py:581
  (82 shorter events, 17.8 us)
Async XLA Ops:
  1.0 8.0 %collective-permute-start.3 = (bf16[64,1280]{1,0:T(8,128)(2,1)S(1)}, bf16[64,1280]{1,0:T(8,128)(2,1)S(1)}, u32[]{:S(2)}, u32[]{:S(2)}) collective-permute-start(bf16[64,1280]{1,0:T(8,128)(2,1)S(1)} %get-tuple-element.41.refs_1_), channel_id=1, source_target_pairs={{1,0},{3,1},{5,3},{7,5},{6,7},{4,6},{2,4},{0,2},{9,8},{11,9},{13,1... | collective-permute-start | bytes 491528 | tf_op jit(solution)/shard_map/ppermute | solution.py:386
  4.1 9.5 %collective-permute-start.1 = (bf16[64,1280]{1,0:T(8,128)(2,1)S(1)}, bf16[64,1280]{1,0:T(8,128)(2,1)S(1)}, u32[]{:S(2)}, u32[]{:S(2)}) collective-permute-start(bf16[64,1280]{1,0:T(8,128)(2,1)S(1)} %get-tuple-element.41.refs_1_), channel_id=1, source_target_pairs={{0,1},{1,3},{3,5},{5,7},{7,6},{6,4},{4,2},{2,0},{8,9},{9,11},{11,1... | collective-permute-start | bytes 491528 | tf_op jit(solution)/shard_map/ppermute | solution.py:386
  4.1 11.1 %collective-permute-start.2 = (bf16[64,1280]{1,0:T(8,128)(2,1)S(1)}, bf16[64,1280]{1,0:T(8,128)(2,1)S(1)}, u32[]{:S(2)}, u32[]{:S(2)}) collective-permute-start(bf16[64,1280]{1,0:T(8,128)(2,1)S(1)} %get-tuple-element.42.refs_0_), channel_id=1, source_target_pairs={{1,0},{3,1},{5,3},{7,5},{6,7},{4,6},{2,4},{0,2},{9,8},{11,9},{13,1... | collective-permute-start | bytes 491528 | tf_op jit(solution)/shard_map/ppermute | solution.py:386
  6.1 7.1 %collective-permute-start = (bf16[64,1280]{1,0:T(8,128)(2,1)S(1)}, bf16[64,1280]{1,0:T(8,128)(2,1)S(1)}, u32[]{:S(2)}, u32[]{:S(2)}) collective-permute-start(bf16[64,1280]{1,0:T(8,128)(2,1)S(1)} %get-tuple-element.42.refs_0_), channel_id=1, source_target_pairs={{0,1},{1,3},{3,5},{5,7},{7,6},{6,4},{4,2},{2,0},{8,9},{9,11},{11,1... | collective-permute-start | bytes 491528 | tf_op jit(solution)/shard_map/ppermute | solution.py:386
  9.1 6.5 %collective-permute-start.7 = (bf16[64,1280]{1,0:T(8,128)(2,1)S(1)}, bf16[64,1280]{1,0:T(8,128)(2,1)S(1)}, u32[]{:S(2)}, u32[]{:S(2)}) collective-permute-start(bf16[64,1280]{1,0:T(8,128)(2,1)S(1)} %collective-permute-done.3.refs_5_), channel_id=1, source_target_pairs={{1,0},{3,1},{5,3},{7,5},{6,7},{4,6},{2,4},{0,2},{9,8},{11,9},{13,1... | collective-permute-start | bytes 491528 | tf_op jit(solution)/shard_map/ppermute | solution.py:386
  13.3 7.1 %collective-permute-start.4 = (bf16[64,1280]{1,0:T(8,128)(2,1)S(1)}, bf16[64,1280]{1,0:T(8,128)(2,1)S(1)}, u32[]{:S(2)}, u32[]{:S(2)}) collective-permute-start(bf16[64,1280]{1,0:T(8,128)(2,1)S(1)} %after.6.refs_2_), channel_id=1, source_target_pairs={{0,1},{1,3},{3,5},{5,7},{7,6},{6,4},{4,2},{2,0},{8,9},{9,11},{11,1... | collective-permute-start | bytes 491528 | tf_op jit(solution)/shard_map/ppermute | solution.py:386
  13.6 10.4 %collective-permute-start.5 = (bf16[64,1280]{1,0:T(8,128)(2,1)S(1)}, bf16[64,1280]{1,0:T(8,128)(2,1)S(1)}, u32[]{:S(2)}, u32[]{:S(2)}) collective-permute-start(bf16[64,1280]{1,0:T(8,128)(2,1)S(1)} %collective-permute-done.1.refs_3_), channel_id=1, source_target_pairs={{0,1},{1,3},{3,5},{5,7},{7,6},{6,4},{4,2},{2,0},{8,9},{9,11},{11,1... | collective-permute-start | bytes 491528 | tf_op jit(solution)/shard_map/ppermute | solution.py:386
  15.3 9.0 %collective-permute-start.6 = (bf16[64,1280]{1,0:T(8,128)(2,1)S(1)}, bf16[64,1280]{1,0:T(8,128)(2,1)S(1)}, u32[]{:S(2)}, u32[]{:S(2)}) collective-permute-start(bf16[64,1280]{1,0:T(8,128)(2,1)S(1)} %collective-permute-done.2.refs_4_), channel_id=1, source_target_pairs={{1,0},{3,1},{5,3},{7,5},{6,7},{4,6},{2,4},{0,2},{9,8},{11,9},{13,1... | collective-permute-start | bytes 491528 | tf_op jit(solution)/shard_map/ppermute | solution.py:386
  15.6 10.4 %collective-permute-start.11 = (bf16[64,1280]{1,0:T(8,128)(2,1)S(1)}, bf16[64,1280]{1,0:T(8,128)(2,1)S(1)}, u32[]{:S(2)}, u32[]{:S(2)}) collective-permute-start(bf16[64,1280]{1,0:T(8,128)(2,1)S(1)} %collective-permute-done.7.refs_9_), channel_id=1, source_target_pairs={{1,0},{3,1},{5,3},{7,5},{6,7},{4,6},{2,4},{0,2},{9,8},{11,9},{13,1... | collective-permute-start | bytes 491528 | tf_op jit(solution)/shard_map/ppermute | solution.py:386
  20.4 7.1 %collective-permute-start.8 = (bf16[64,1280]{1,0:T(8,128)(2,1)S(1)}, bf16[64,1280]{1,0:T(8,128)(2,1)S(1)}, u32[]{:S(2)}, u32[]{:S(2)}) collective-permute-start(bf16[64,1280]{1,0:T(8,128)(2,1)S(1)} %collective-permute-done.4.refs_6_), channel_id=1, source_target_pairs={{0,1},{1,3},{3,5},{5,7},{7,6},{6,4},{4,2},{2,0},{8,9},{9,11},{11,1... | collective-permute-start | bytes 491528 | tf_op jit(solution)/shard_map/ppermute | solution.py:386
  23.9 6.4 %collective-permute-start.9 = (bf16[64,1280]{1,0:T(8,128)(2,1)S(1)}, bf16[64,1280]{1,0:T(8,128)(2,1)S(1)}, u32[]{:S(2)}, u32[]{:S(2)}) collective-permute-start(bf16[64,1280]{1,0:T(8,128)(2,1)S(1)} %collective-permute-done.5.refs_7_), channel_id=1, source_target_pairs={{0,1},{1,3},{3,5},{5,7},{7,6},{6,4},{4,2},{2,0},{8,9},{9,11},{11,1... | collective-permute-start | bytes 491528 | tf_op jit(solution)/shard_map/ppermute | solution.py:386
  26.0 9.3 %collective-permute-start.13 = (bf16[64,1280]{1,0:T(8,128)(2,1)S(1)}, bf16[64,1280]{1,0:T(8,128)(2,1)S(1)}, u32[]{:S(2)}, u32[]{:S(2)}) collective-permute-start(bf16[64,1280]{1,0:T(8,128)(2,1)S(1)} %collective-permute-done.11.refs_13_.refs_5_), channel_id=1, source_target_pairs={{1,0},{3,1},{5,3},{7,5},{6,7},{4,6},{2,4},{0,2},{9,8},{11,9},{13,1... | collective-permute-start | bytes 491528 | tf_op jit(solution)/shard_map/ppermute | solution.py:386
  27.6 7.7 %collective-permute-start.12 = (bf16[64,1280]{1,0:T(8,128)(2,1)S(1)}, bf16[64,1280]{1,0:T(8,128)(2,1)S(1)}, u32[]{:S(2)}, u32[]{:S(2)}) collective-permute-start(bf16[64,1280]{1,0:T(8,128)(2,1)S(1)} %collective-permute-done.8.refs_10_.refs_2_), channel_id=1, source_target_pairs={{0,1},{1,3},{3,5},{5,7},{7,6},{6,4},{4,2},{2,0},{8,9},{9,11},{11,1... | collective-permute-start | bytes 491528 | tf_op jit(solution)/shard_map/ppermute | solution.py:386
  30.3 22.3 %collective-permute-start.22 = (bf16[208,1280]{1,0:T(8,128)(2,1)S(1)}, bf16[208,1280]{1,0:T(8,128)(2,1)S(1)}, u32[]{:S(2)}, u32[]{:S(2)}) collective-permute-start(bf16[208,1280]{1,0:T(8,128)(2,1)S(1)} %get-tuple-element.25), channel_id=1, source_target_pairs={{0,1},{1,0},{2,3},{3,2},{4,5},{5,4},{6,7},{7,6},{8,9},{9,8},{10,11... | collective-permute-start | bytes 1597448 | tf_op jit(solution)/shard_map/ppermute | solution.py:401
  31.4 33.4 %collective-permute-start.23 = (bf16[160,1280]{1,0:T(8,128)(2,1)S(1)}, bf16[160,1280]{1,0:T(8,128)(2,1)S(1)}, u32[]{:S(2)}, u32[]{:S(2)}) collective-permute-start(bf16[160,1280]{1,0:T(8,128)(2,1)S(1)} %get-tuple-element.26.refs_1_), channel_id=1, source_target_pairs={{0,2},{1,3},{2,4},{3,5},{4,6},{5,7},{6,0},{7,1},{8,12},{9,13},{10,... | collective-permute-start | bytes 1228808 | tf_op jit(solution)/shard_map/ppermute | solution.py:401
  42.8 13.9 %collective-permute-start.27 = (bf16[160,512]{1,0:T(8,128)(2,1)S(1)}, bf16[160,512]{1,0:T(8,128)(2,1)S(1)}, u32[]{:S(2)}, u32[]{:S(2)}) collective-permute-start(bf16[160,512]{1,0:T(8,128)(2,1)S(1)} %get-tuple-element.24.refs_1_), channel_id=1, source_target_pairs={{0,1},{1,3},{3,5},{5,7},{7,6},{6,4},{4,2},{2,0},{8,9},{9,11},{11,1... | collective-permute-start | bytes 491528 | tf_op jit(solution)/shard_map/ppermute | solution.py:386
  43.7 14.3 %collective-permute-start.18 = (bf16[160,512]{1,0:T(8,128)(2,1)S(1)}, bf16[160,512]{1,0:T(8,128)(2,1)S(1)}, u32[]{:S(2)}, u32[]{:S(2)}) collective-permute-start(bf16[160,512]{1,0:T(8,128)(2,1)S(1)} %get-tuple-element.24.refs_1_), channel_id=1, source_target_pairs={{1,0},{3,1},{5,3},{7,5},{6,7},{4,6},{2,4},{0,2},{9,8},{11,9},{13,1... | collective-permute-start | bytes 491528 | tf_op jit(solution)/shard_map/ppermute | solution.py:386
  52.6 13.2 %collective-permute-start.24 = (bf16[128,1280]{1,0:T(8,128)(2,1)S(1)}, bf16[128,1280]{1,0:T(8,128)(2,1)S(1)}, u32[]{:S(2)}, u32[]{:S(2)}) collective-permute-start(bf16[128,1280]{1,0:T(8,128)(2,1)S(1)} %slice.24.refs_0_), channel_id=1, source_target_pairs={{0,16},{8,24},{16,0},{24,8},{1,17},{9,25},{17,1},{25,9},{2,18},{10... | collective-permute-start | bytes 983048 | tf_op jit(solution)/shard_map/ppermute | solution.py:406
  52.7 7.8 %collective-permute-start.28 = (bf16[160,512]{1,0:T(8,128)(2,1)S(1)}, bf16[160,512]{1,0:T(8,128)(2,1)S(1)}, u32[]{:S(2)}, u32[]{:S(2)}) collective-permute-start(bf16[160,512]{1,0:T(8,128)(2,1)S(1)} %get-tuple-element.23.refs_1_.refs_0_), channel_id=1, source_target_pairs={{1,0},{3,1},{5,3},{7,5},{6,7},{4,6},{2,4},{0,2},{9,8},{11,9},{13,1... | collective-permute-start | bytes 491528 | tf_op jit(solution)/shard_map/ppermute | solution.py:386
  58.0 6.7 %collective-permute-start.29 = (bf16[160,512]{1,0:T(8,128)(2,1)S(1)}, bf16[160,512]{1,0:T(8,128)(2,1)S(1)}, u32[]{:S(2)}, u32[]{:S(2)}) collective-permute-start(bf16[160,512]{1,0:T(8,128)(2,1)S(1)} %collective-permute-done.27.refs_3_), channel_id=1, source_target_pairs={{0,1},{1,3},{3,5},{5,7},{7,6},{6,4},{4,2},{2,0},{8,9},{9,11},{11,1... | collective-permute-start | bytes 491528 | tf_op jit(solution)/shard_map/ppermute | solution.py:386
  64.7 7.4 %collective-permute-start.31 = (bf16[160,512]{1,0:T(8,128)(2,1)S(1)}, bf16[160,512]{1,0:T(8,128)(2,1)S(1)}, u32[]{:S(2)}, u32[]{:S(2)}) collective-permute-start(bf16[160,512]{1,0:T(8,128)(2,1)S(1)} %collective-permute-done.29.refs_7_), channel_id=1, source_target_pairs={{0,1},{1,3},{3,5},{5,7},{7,6},{6,4},{4,2},{2,0},{8,9},{9,11},{11,1... | collective-permute-start | bytes 491528 | tf_op jit(solution)/shard_map/ppermute | solution.py:386
  65.8 13.7 %collective-permute-start.25 = (bf16[128,1280]{1,0:T(8,128)(2,1)S(1)}, bf16[128,1280]{1,0:T(8,128)(2,1)S(1)}, u32[]{:S(2)}, u32[]{:S(2)}) collective-permute-start(bf16[128,1280]{1,0:T(8,128)(2,1)S(1)} %get-tuple-element.27.refs_17_.refs_5_), channel_id=1, source_target_pairs={{0,8},{8,0},{16,24},{24,16},{1,9},{9,1},{17,25},{25,17},{2,10},{10... | collective-permute-start | bytes 983048 | tf_op jit(solution)/shard_map/ppermute | solution.py:406
  65.8 15.7 %collective-permute-start.26 = (bf16[128,1280]{1,0:T(8,128)(2,1)S(1)}, bf16[128,1280]{1,0:T(8,128)(2,1)S(1)}, u32[]{:S(2)}, u32[]{:S(2)}) collective-permute-start(bf16[128,1280]{1,0:T(8,128)(2,1)S(1)} %collective-permute-done.24.refs_2_.refs_18_.refs_6_), channel_id=1, source_target_pairs={{0,8},{8,0},{16,24},{24,16},{1,9},{9,1},{17,25},{25,17},{2,10},{10... | collective-permute-start | bytes 983048 | tf_op jit(solution)/shard_map/ppermute | solution.py:406
  68.0 6.5 %collective-permute-start.20 = (bf16[160,512]{1,0:T(8,128)(2,1)S(1)}, bf16[160,512]{1,0:T(8,128)(2,1)S(1)}, u32[]{:S(2)}, u32[]{:S(2)}) collective-permute-start(bf16[160,512]{1,0:T(8,128)(2,1)S(1)} %collective-permute-done.19.refs_9_), channel_id=1, source_target_pairs={{1,0},{3,1},{5,3},{7,5},{6,7},{4,6},{2,4},{0,2},{9,8},{11,9},{13,1... | collective-permute-start | bytes 491528 | tf_op jit(solution)/shard_map/ppermute | solution.py:386
  77.4 16.0 %collective-permute-start.36 = (bf16[160,1280]{1,0:T(8,128)(2,1)S(1)}, bf16[160,1280]{1,0:T(8,128)(2,1)S(1)}, u32[]{:S(2)}, u32[]{:S(2)}) collective-permute-start(bf16[160,1280]{1,0:T(8,128)(2,1)S(1)} %get-tuple-element.37), channel_id=1, source_target_pairs={{0,16},{8,24},{16,0},{24,8},{1,17},{9,25},{17,1},{25,9},{2,18},{10... | collective-permute-start | bytes 1228808 | tf_op jit(solution)/shard_map/ppermute | solution.py:406
  77.5 9.8 %collective-permute-start.21 = (bf16[160,512]{1,0:T(8,128)(2,1)S(1)}, bf16[160,512]{1,0:T(8,128)(2,1)S(1)}, u32[]{:S(2)}, u32[]{:S(2)}) collective-permute-start(bf16[160,512]{1,0:T(8,128)(2,1)S(1)} %collective-permute-done.20.refs_13_.refs_5_), channel_id=1, source_target_pairs={{1,0},{3,1},{5,3},{7,5},{6,7},{4,6},{2,4},{0,2},{9,8},{11,9},{13,1... | collective-permute-start | bytes 491528 | tf_op jit(solution)/shard_map/ppermute | solution.py:386
  78.1 9.2 %collective-permute-start.17 = (bf16[160,512]{1,0:T(8,128)(2,1)S(1)}, bf16[160,512]{1,0:T(8,128)(2,1)S(1)}, u32[]{:S(2)}, u32[]{:S(2)}) collective-permute-start(bf16[160,512]{1,0:T(8,128)(2,1)S(1)} %collective-permute-done.16.refs_10_.refs_2_), channel_id=1, source_target_pairs={{0,1},{1,3},{3,5},{5,7},{7,6},{6,4},{4,2},{2,0},{8,9},{9,11},{11,1... | collective-permute-start | bytes 491528 | tf_op jit(solution)/shard_map/ppermute | solution.py:386
  79.5 14.0 %collective-permute-start.37 = (bf16[160,1280]{1,0:T(8,128)(2,1)S(1)}, bf16[160,1280]{1,0:T(8,128)(2,1)S(1)}, u32[]{:S(2)}, u32[]{:S(2)}) collective-permute-start(bf16[160,1280]{1,0:T(8,128)(2,1)S(1)} %get-tuple-element.38), channel_id=1, source_target_pairs={{0,3},{1,2},{2,5},{3,4},{4,7},{5,6},{6,1},{7,0},{8,15},{9,14},{10,... | collective-permute-start | bytes 1228808 | tf_op jit(solution)/shard_map/ppermute | solution.py:401
  93.5 9.9 %collective-permute-start.38 = (bf16[400,1280]{1,0:T(8,128)(2,1)S(1)}, bf16[400,1280]{1,0:T(8,128)(2,1)S(1)}, u32[]{:S(2)}, u32[]{:S(2)}) collective-permute-start(bf16[400,1280]{1,0:T(8,128)(2,1)S(1)} %get-tuple-element.39.refs_6_), channel_id=1, source_target_pairs={{0,8},{8,0},{16,24},{24,16},{1,9},{9,1},{17,25},{25,17},{2,10},{10... | collective-permute-start | bytes 3072008 | tf_op jit(solution)/shard_map/ppermute | solution.py:406
  93.6 9.8 %collective-permute-start.39 = (bf16[160,1280]{1,0:T(8,128)(2,1)S(1)}, bf16[160,1280]{1,0:T(8,128)(2,1)S(1)}, u32[]{:S(2)}, u32[]{:S(2)}) collective-permute-start(bf16[160,1280]{1,0:T(8,128)(2,1)S(1)} %get-tuple-element.40.refs_8_), channel_id=1, source_target_pairs={{0,8},{8,0},{16,24},{24,16},{1,9},{9,1},{17,25},{25,17},{2,10},{10... | collective-permute-start | bytes 1228808 | tf_op jit(solution)/shard_map/ppermute | solution.py:406
  94.1 7.5 %collective-permute-start.34 = (bf16[320,128]{1,0:T(8,128)(2,1)S(1)}, bf16[320,128]{1,0:T(8,128)(2,1)S(1)}, u32[]{:S(2)}, u32[]{:S(2)}) collective-permute-start(bf16[320,128]{1,0:T(8,128)(2,1)S(1)} %get-tuple-element.33), channel_id=1, source_target_pairs={{0,4},{1,5},{2,6},{3,7},{4,0},{5,1},{6,2},{7,3},{8,12},{9,13},{10,... | collective-permute-start | bytes 245768 | tf_op jit(solution)/shard_map/ppermute | solution.py:562
  95.5 6.9 %collective-permute-start.35 = (bf16[320,128]{1,0:T(8,128)(2,1)S(1)}, bf16[320,128]{1,0:T(8,128)(2,1)S(1)}, u32[]{:S(2)}, u32[]{:S(2)}) collective-permute-start(bf16[320,128]{1,0:T(8,128)(2,1)S(1)} %get-tuple-element.34), channel_id=1, source_target_pairs={{0,6},{1,7},{2,0},{3,1},{4,2},{5,3},{6,4},{7,5},{8,14},{9,15},{10,... | collective-permute-start | bytes 245768 | tf_op jit(solution)/shard_map/ppermute | solution.py:562
  (15 other events, 181.4 us)

commit v9 on v8

--- a/solution.py
+++ b/solution.py
@@ -457,6 +457,8 @@
         ]
         chosen = [jnp.concatenate(chosen, axis=0)]
     pieces = gather(halves, n, chosen)
+    if inner == 2:
+        far = send(w_out, FAR)
     stats = pl.pallas_call(
         stats_kernel,
         out_shape=jax.ShapeDtypeStruct((24, channels), f32),
@@ -471,9 +473,9 @@
         name="stats",
     )(*pieces[:-2])
     if inner == 2:
-        chosen, out_own = after(chosen + [w_out], pieces[-6:-2])
+        chosen, far = after(chosen + [far], pieces[-6:-2])
         chosen = send(chosen, [(0, 1)])
-        far = send(out_own, FAR)
+        across = swap(far, 2)
     else:
         sets = [list(range(at, at + inner)) for at in range(0, n, inner)]
         weights = jnp.stack([w_query, w_key, w_value])
@@ -507,10 +509,9 @@
 
     hidden_pieces = gather(tuple(hidden), n)
     if inner == 2:
-        (chosen,) = after([chosen], hidden[:1])
+        chosen, across = after([chosen, across], hidden[:1])
         near = [chosen[:quarter]]
         near.append(swap(near[0], 2))
-        near[0], far = after([near[0], far], near[1:])
         near += [swap(one, 1) for one in near]
         weights = [w_query, w_key, w_value] + near
     made_rows = sum(weight.shape[0] for weight in weights)
@@ -532,8 +533,9 @@
         name="norm_project",
     )(sources, *hidden_pieces[:-2], *weights)
     if inner == 2:
-        far, out_own = after([far, out_own], hidden_pieces[-6:-2])
-        across = swap(far, 2)
+        far = jnp.concatenate([far, across, chosen[quarter:]], axis=0)
+        far, out_own = after([far, w_out], hidden_pieces[-6:-2])
+        far = [far, swap(far, 1)]
         last = send(out_own, LAST)
     one_block = jax.ShapeDtypeStruct((SET_CHANNELS, block), bf16)
     *sent, kept, made, key = pl.pallas_call(
@@ -574,9 +576,8 @@
         name="own_attention",
     )(made, key)
     if inner == 2:
-        far = jnp.concatenate([far, across, chosen[quarter:]], axis=0)
-        far, last = after([far, last], sent[:1])
-        out_weights = [w_out, far, swap(far, 1), last, swap(last, 1)]
+        (last,) = after([last], sent[:1])
+        out_weights = [w_out] + far + [last, swap(last, 1)]
 
     output = pl.pallas_call(
         functools.partial(output_kernel, n),

time: 106 us -> 115 us (1.085)
  waiting for transfers between devices: 28.4 us -> 35.4 us
  starting transfers between devices: 49 us -> 51.6 us
    ppermute x28, waiting for transfers between devices: 24.5 us -> 32.5 us  [gather(): lax.ppermute(found[half, sign * (step - 1)], 'patch', pairs)]
    ppermute x6, starting transfers between devices: 1.15 us -> 5.65 us  [swap(): return lax.ppermute(block, 'batch', pairs)]
    ppermute x3, starting transfers between devices: 5.89 us -> 3.53 us  [send(): return lax.ppermute(block, ('batch', 'patch'), pairs)]
    ppermute x3, starting transfers between devices: 3.41 us -> 5.35 us  [on_device(): received.append(lax.ppermute(sent_block, 'patch', pairs))]
    ppermute x28, starting transfers between devices: 38.6 us -> 37 us  [gather(): lax.ppermute(found[half, sign * (step - 1)], 'patch', pairs)]
  transfers between devices with their start and end apart: 40 -> 40, of which waited for: 15 -> 18; matrix products, arithmetic and copies ran while one was open for 2% -> 2% of each run, Pallas kernels for 21% -> 19%
where the time goes in v9:
time: 115 us
  starting transfers between devices  51.6 us (45%)
  waiting for transfers between devices  35.4 us (31%)
  Pallas kernels  24.3 us (21%)
  local copies, waits for them, and re-layouts  2.05 us (2%)
  other arithmetic  1.35 us (1%)
    ppermute x28, starting transfers between devices, gather(): lax.ppermute(found[half, sign * (step - 1)], 'patch', pairs)  37 us
    ppermute x28, waiting for transfers between devices, gather(): lax.ppermute(found[half, sign * (step - 1)], 'patch', pairs)  32.5 us
    pallas_call x1, Pallas kernels, on_device(): pl.pallas_call(functools.partial(conv_kernel, columns), out_shape=[jax.Sh...  7.48 us
    pallas_call x1, Pallas kernels, on_device(): pl.pallas_call(functools.partial(attention_kernel, 2 * n, inner), out_sha...  6.16 us
    pallas_call x1, Pallas kernels, on_device(): pl.pallas_call(functools.partial(project_kernel, 2 * n), out_shape=[jax.S...  5.72 us
    ppermute x6, starting transfers between devices, swap(): return lax.ppermute(block, 'batch', pairs)  5.65 us
    ppermute x3, starting transfers between devices, on_device(): received.append(lax.ppermute(sent_block, 'patch', pairs))  5.35 us
    ppermute x3, starting transfers between devices, send(): return lax.ppermute(block, ('batch', 'patch'), pairs)  3.53 us
  transfers between devices with their start and end apart: 40, of which 18 were waited for; matrix products, arithmetic and copies ran while one was open for 2% of the time, Pallas kernels for 19%

profile of v9, /device:TPU:0, one launch (start us, length us, event | category | flops | bytes accessed | tf_op | source)
XLA Modules:
  0.0 114.8 jit_solution(5141165043709966706)
XLA Ops:
  1.0 3.0 %collective-permute-start = (bf16[64,1280]{1,0:T(8,128)(2,1)S(1)}, bf16[64,1280]{1,0:T(8,128)(2,1)S(1)}, u32[]{:S(2)}, u32[]{:S(2)}) collective-permute-start(bf16[64,1280]{1,0:T(8,128)(2,1)S(1)} %get-tuple-element.38.refs_0_), channel_id=1, source_target_pairs={{0,1},{1,3},{3,5},{5,7},{7,6},{6,4},{4,2},{2,0},{8,9},{9,11},{11,1... | collective-permute-start | bytes 491528 | tf_op jit(solution)/shard_map/ppermute | solution.py:386
  4.2 2.0 %collective-permute-start.3 = (bf16[64,1280]{1,0:T(8,128)(2,1)S(1)}, bf16[64,1280]{1,0:T(8,128)(2,1)S(1)}, u32[]{:S(2)}, u32[]{:S(2)}) collective-permute-start(bf16[64,1280]{1,0:T(8,128)(2,1)S(1)} %get-tuple-element.37.refs_1_), channel_id=1, source_target_pairs={{1,0},{3,1},{5,3},{7,5},{6,7},{4,6},{2,4},{0,2},{9,8},{11,9},{13,1... | collective-permute-start | bytes 491528 | tf_op jit(solution)/shard_map/ppermute | solution.py:386
  8.8 2.4 %collective-permute-start.4 = (bf16[64,1280]{1,0:T(8,128)(2,1)S(1)}, bf16[64,1280]{1,0:T(8,128)(2,1)S(1)}, u32[]{:S(2)}, u32[]{:S(2)}) collective-permute-start(bf16[64,1280]{1,0:T(8,128)(2,1)S(1)} %after.5.refs_2_), channel_id=1, source_target_pairs={{0,1},{1,3},{3,5},{5,7},{7,6},{6,4},{4,2},{2,0},{8,9},{9,11},{11,1... | collective-permute-start | bytes 491528 | tf_op jit(solution)/shard_map/ppermute | solution.py:386
  11.2 2.0 %collective-permute-done.3.refs_5_ = bf16[64,1280]{1,0:T(8,128)(2,1)S(1)} collective-permute-done((bf16[64,1280]{1,0:T(8,128)(2,1)S(1)}, bf16[64,1280]{1,0:T(8,128)(2,1)S(1)}, u32[]{:S(2)}, u32[]{:S(2)}) %collective-permute-start.3) | collective-permute-done | bytes 163872 | tf_op jit(solution)/shard_map/ppermute | solution.py:386
  13.6 1.7 %collective-permute-start.22 = (bf16[160,1280]{1,0:T(8,128)(2,1)S(1)}, bf16[160,1280]{1,0:T(8,128)(2,1)S(1)}, u32[]{:S(2)}, u32[]{:S(2)}) collective-permute-start(bf16[160,1280]{1,0:T(8,128)(2,1)S(1)} %copy-done), channel_id=1, source_target_pairs={{0,2},{1,3},{2,4},{3,5},{4,6},{5,7},{6,0},{7,1},{8,12},{9,13},{10,... | collective-permute-start | bytes 1228808 | tf_op jit(solution)/shard_map/ppermute | solution.py:401
  15.3 1.6 %collective-permute-start.6 = (bf16[64,1280]{1,0:T(8,128)(2,1)S(1)}, bf16[64,1280]{1,0:T(8,128)(2,1)S(1)}, u32[]{:S(2)}, u32[]{:S(2)}) collective-permute-start(bf16[64,1280]{1,0:T(8,128)(2,1)S(1)} %collective-permute-done.2.refs_4_), channel_id=1, source_target_pairs={{1,0},{3,1},{5,3},{7,5},{6,7},{4,6},{2,4},{0,2},{9,8},{11,9},{13,1... | collective-permute-start | bytes 491528 | tf_op jit(solution)/shard_map/ppermute | solution.py:386
  17.3 1.5 %collective-permute-start.8 = (bf16[64,1280]{1,0:T(8,128)(2,1)S(1)}, bf16[64,1280]{1,0:T(8,128)(2,1)S(1)}, u32[]{:S(2)}, u32[]{:S(2)}) collective-permute-start(bf16[64,1280]{1,0:T(8,128)(2,1)S(1)} %collective-permute-done.4.refs_6_), channel_id=1, source_target_pairs={{0,1},{1,3},{3,5},{5,7},{7,6},{6,4},{4,2},{2,0},{8,9},{9,11},{11,1... | collective-permute-start | bytes 491528 | tf_op jit(solution)/shard_map/ppermute | solution.py:386
  20.1 2.8 %collective-permute-start.11 = (bf16[64,1280]{1,0:T(8,128)(2,1)S(1)}, bf16[64,1280]{1,0:T(8,128)(2,1)S(1)}, u32[]{:S(2)}, u32[]{:S(2)}) collective-permute-start(bf16[64,1280]{1,0:T(8,128)(2,1)S(1)} %collective-permute-done.7.refs_9_), channel_id=1, source_target_pairs={{1,0},{3,1},{5,3},{7,5},{6,7},{4,6},{2,4},{0,2},{9,8},{11,9},{13,1... | collective-permute-start | bytes 491528 | tf_op jit(solution)/shard_map/ppermute | solution.py:386
  22.9 7.5 %collective-permute-done.6.refs_8_ = bf16[64,1280]{1,0:T(8,128)(2,1)S(1)} collective-permute-done((bf16[64,1280]{1,0:T(8,128)(2,1)S(1)}, bf16[64,1280]{1,0:T(8,128)(2,1)S(1)}, u32[]{:S(2)}, u32[]{:S(2)}) %collective-permute-start.6) | collective-permute-done | bytes 163872 | tf_op jit(solution)/shard_map/ppermute | solution.py:386
  30.4 6.1 %collective-permute-start.10 = (bf16[64,1280]{1,0:T(8,128)(2,1)S(1)}, bf16[64,1280]{1,0:T(8,128)(2,1)S(1)}, u32[]{:S(2)}, u32[]{:S(2)}) collective-permute-start(bf16[64,1280]{1,0:T(8,128)(2,1)S(1)} %collective-permute-done.6.refs_8_), channel_id=1, source_target_pairs={{1,0},{3,1},{5,3},{7,5},{6,7},{4,6},{2,4},{0,2},{9,8},{11,9},{13,1... | collective-permute-start | bytes 491528 | tf_op jit(solution)/shard_map/ppermute | solution.py:386
  36.6 3.4 %collective-permute-start.13 = (bf16[64,1280]{1,0:T(8,128)(2,1)S(1)}, bf16[64,1280]{1,0:T(8,128)(2,1)S(1)}, u32[]{:S(2)}, u32[]{:S(2)}) collective-permute-start(bf16[64,1280]{1,0:T(8,128)(2,1)S(1)} %collective-permute-done.11.refs_13_.refs_5_), channel_id=1, source_target_pairs={{1,0},{3,1},{5,3},{7,5},{6,7},{4,6},{2,4},{0,2},{9,8},{11,9},{13,1... | collective-permute-start | bytes 491528 | tf_op jit(solution)/shard_map/ppermute | solution.py:386
  40.0 2.3 %collective-permute-done.9.refs_11_.refs_3_ = bf16[64,1280]{1,0:T(8,128)(2,1)S(1)} collective-permute-done((bf16[64,1280]{1,0:T(8,128)(2,1)S(1)}, bf16[64,1280]{1,0:T(8,128)(2,1)S(1)}, u32[]{:S(2)}, u32[]{:S(2)}) %collective-permute-start.9) | collective-permute-done | bytes 163872 | tf_op jit(solution)/shard_map/ppermute | solution.py:386
  42.3 3.5 %collective-permute-start.24 = (bf16[160,1280]{1,0:T(8,128)(2,1)S(1)}, bf16[160,1280]{1,0:T(8,128)(2,1)S(1)}, u32[]{:S(2)}, u32[]{:S(2)}) collective-permute-start(bf16[160,1280]{1,0:T(8,128)(2,1)S(1)} %get-tuple-element.24), channel_id=1, source_target_pairs={{0,16},{8,24},{16,0},{24,8},{1,17},{9,25},{17,1},{25,9},{2,18},{10... | collective-permute-start | bytes 1228808 | tf_op jit(solution)/shard_map/ppermute | solution.py:406
  46.9 7.5 %norm_conv.1 = (bf16[160,512]{1,0:T(8,128)(2,1)S(1)}, bf16[160,512]{1,0:T(8,128)(2,1)S(1)}) custom-call(s32[128]{0:T(128)S(1)} %copy-done.4, bf16[64,1280]{1,0:T(8,128)(2,1)S(1)} %get-tuple-element.38.refs_0_, bf16[64,1280]{1,0:T(8,128)(2,1)S(1)} %get-tuple-element.37.refs_1_, bf16[64,1280]{1,0:T(8,128)(2,1)S(1)} %after.5.refs_2_, ...), custom_call_target="tpu_custom_call" | custom-call | flops 3774873600 | bytes 6307840 | tf_op jit(solution)/shard_map/norm_conv/pallas_call | solution.py:486
  54.5 2.3 %collective-permute-start.18 = (bf16[160,512]{1,0:T(8,128)(2,1)S(1)}, bf16[160,512]{1,0:T(8,128)(2,1)S(1)}, u32[]{:S(2)}, u32[]{:S(2)}) collective-permute-start(bf16[160,512]{1,0:T(8,128)(2,1)S(1)} %get-tuple-element.22.refs_1_), channel_id=1, source_target_pairs={{1,0},{3,1},{5,3},{7,5},{6,7},{4,6},{2,4},{0,2},{9,8},{11,9},{13,1... | collective-permute-start | bytes 491528 | tf_op jit(solution)/shard_map/ppermute | solution.py:386
  56.7 4.2 %collective-permute-done.14.refs_2_ = bf16[160,512]{1,0:T(8,128)(2,1)S(1)} collective-permute-done((bf16[160,512]{1,0:T(8,128)(2,1)S(1)}, bf16[160,512]{1,0:T(8,128)(2,1)S(1)}, u32[]{:S(2)}, u32[]{:S(2)}) %collective-permute-start.14) | collective-permute-done | bytes 163872 | tf_op jit(solution)/shard_map/ppermute | solution.py:386
  61.0 1.7 %collective-permute-start.29 = (bf16[160,512]{1,0:T(8,128)(2,1)S(1)}, bf16[160,512]{1,0:T(8,128)(2,1)S(1)}, u32[]{:S(2)}, u32[]{:S(2)}) collective-permute-start(bf16[160,512]{1,0:T(8,128)(2,1)S(1)} %get-tuple-element.21.refs_2_.refs_0_), channel_id=1, source_target_pairs={{1,0},{3,1},{5,3},{7,5},{6,7},{4,6},{2,4},{0,2},{9,8},{11,9},{13,1... | collective-permute-start | bytes 491528 | tf_op jit(solution)/shard_map/ppermute | solution.py:386
  63.0 1.4 %collective-permute-start.25 = (bf16[128,1280]{1,0:T(8,128)(2,1)S(1)}, bf16[128,1280]{1,0:T(8,128)(2,1)S(1)}, u32[]{:S(2)}, u32[]{:S(2)}) collective-permute-start(bf16[128,1280]{1,0:T(8,128)(2,1)S(1)} %slice.22.refs_17_.refs_5_), channel_id=1, source_target_pairs={{0,16},{8,24},{16,0},{24,8},{1,17},{9,25},{17,1},{25,9},{2,18},{10... | collective-permute-start | bytes 983048 | tf_op jit(solution)/shard_map/ppermute | solution.py:406
  64.5 1.4 %collective-permute-start.19 = (bf16[160,512]{1,0:T(8,128)(2,1)S(1)}, bf16[160,512]{1,0:T(8,128)(2,1)S(1)}, u32[]{:S(2)}, u32[]{:S(2)}) collective-permute-start(bf16[160,512]{1,0:T(8,128)(2,1)S(1)} %collective-permute-done.18.refs_5_), channel_id=1, source_target_pairs={{1,0},{3,1},{5,3},{7,5},{6,7},{4,6},{2,4},{0,2},{9,8},{11,9},{13,1... | collective-permute-start | bytes 491528 | tf_op jit(solution)/shard_map/ppermute | solution.py:386
  67.6 1.6 %collective-permute-start.31 = (bf16[160,512]{1,0:T(8,128)(2,1)S(1)}, bf16[160,512]{1,0:T(8,128)(2,1)S(1)}, u32[]{:S(2)}, u32[]{:S(2)}) collective-permute-start(bf16[160,512]{1,0:T(8,128)(2,1)S(1)} %collective-permute-done.29.refs_4_), channel_id=1, source_target_pairs={{1,0},{3,1},{5,3},{7,5},{6,7},{4,6},{2,4},{0,2},{9,8},{11,9},{13,1... | collective-permute-start | bytes 491528 | tf_op jit(solution)/shard_map/ppermute | solution.py:386
  77.2 1.3 %collective-permute-done.32.refs_11_.refs_3_ = bf16[160,512]{1,0:T(8,128)(2,1)S(1)} collective-permute-done((bf16[160,512]{1,0:T(8,128)(2,1)S(1)}, bf16[160,512]{1,0:T(8,128)(2,1)S(1)}, u32[]{:S(2)}, u32[]{:S(2)}) %collective-permute-start.32) | collective-permute-done | bytes 163872 | tf_op jit(solution)/shard_map/ppermute | solution.py:386
  78.5 1.5 %collective-permute-done.33.refs_12_.refs_4_ = bf16[160,512]{1,0:T(8,128)(2,1)S(1)} collective-permute-done((bf16[160,512]{1,0:T(8,128)(2,1)S(1)}, bf16[160,512]{1,0:T(8,128)(2,1)S(1)}, u32[]{:S(2)}, u32[]{:S(2)}) %collective-permute-start.33) | collective-permute-done | bytes 163872 | tf_op jit(solution)/shard_map/ppermute | solution.py:386
  80.1 1.8 %collective-permute-start.38 = (bf16[160,1280]{1,0:T(8,128)(2,1)S(1)}, bf16[160,1280]{1,0:T(8,128)(2,1)S(1)}, u32[]{:S(2)}, u32[]{:S(2)}) collective-permute-start(bf16[160,1280]{1,0:T(8,128)(2,1)S(1)} %get-tuple-element.36), channel_id=1, source_target_pairs={{0,3},{1,2},{2,5},{3,4},{4,7},{5,6},{6,1},{7,0},{8,15},{9,14},{10,... | collective-permute-start | bytes 1228808 | tf_op jit(solution)/shard_map/ppermute | solution.py:401
  84.0 5.7 %norm_project.1 = (f32[992,1024]{1,0:T(8,128)S(1)}, bf16[1280,128]{1,0:T(8,128)(2,1)S(1)}) custom-call(s32[128]{0:T(128)S(1)} %copy-done.4, bf16[160,512]{1,0:T(8,128)(2,1)S(1)} %get-tuple-element.21.refs_2_.refs_0_, bf16[160,512]{1,0:T(8,128)(2,1)S(1)} %get-tuple-element.22.refs_1_, bf16[160,512]{1,0:T(8,128)(2,1)S(1)} %collective-permute-done.14.refs_2_, ...), custom_call_target="tpu_custom_call" | custom-call | flops 2600468480 | bytes 5160960 | tf_op jit(solution)/shard_map/norm_project/pallas_call | solution.py:518
  89.7 5.7 %collective-permute-done.17.refs_0_ = bf16[160,512]{1,0:T(8,128)(2,1)S(1)} collective-permute-done((bf16[160,512]{1,0:T(8,128)(2,1)S(1)}, bf16[160,512]{1,0:T(8,128)(2,1)S(1)}, u32[]{:S(2)}, u32[]{:S(2)}) %collective-permute-start.17) | collective-permute-done | bytes 163872 | tf_op jit(solution)/shard_map/ppermute | solution.py:386
  96.3 6.2 %attention.1 = (bf16[320,128]{1,0:T(8,128)(2,1)S(1)}, bf16[320,128]{1,0:T(8,128)(2,1)S(1)}, bf16[320,128]{1,0:T(8,128)(2,1)S(1)}, bf16[1280,128]{1,0:T(8,128)(2,...) custom-call(s32[128]{0:T(128)S(1)} %copy-done.4, ...), custom_call_target="tpu_custom_call" | custom-call | flops 1283457024 | bytes 6094848 | tf_op jit(solution)/shard_map/attention/pallas_call | solution.py:541
  102.7 1.4 %collective-permute-start.34 = (bf16[320,128]{1,0:T(8,128)(2,1)S(1)}, bf16[320,128]{1,0:T(8,128)(2,1)S(1)}, u32[]{:S(2)}, u32[]{:S(2)}) collective-permute-start(bf16[320,128]{1,0:T(8,128)(2,1)S(1)} %get-tuple-element.30.refs_1_), channel_id=1, source_target_pairs={{0,2},{1,3},{2,4},{3,5},{4,6},{5,7},{6,0},{7,1},{8,10},{9,11},{10,... | collective-permute-start | bytes 245768 | tf_op jit(solution)/shard_map/ppermute | solution.py:564
  104.1 2.4 %collective-permute-start.35 = (bf16[320,128]{1,0:T(8,128)(2,1)S(1)}, bf16[320,128]{1,0:T(8,128)(2,1)S(1)}, u32[]{:S(2)}, u32[]{:S(2)}) collective-permute-start(bf16[320,128]{1,0:T(8,128)(2,1)S(1)} %get-tuple-element.31), channel_id=1, source_target_pairs={{0,4},{1,5},{2,6},{3,7},{4,0},{5,1},{6,2},{7,3},{8,12},{9,13},{10,... | collective-permute-start | bytes 245768 | tf_op jit(solution)/shard_map/ppermute | solution.py:564
  106.5 1.5 %collective-permute-start.36 = (bf16[320,128]{1,0:T(8,128)(2,1)S(1)}, bf16[320,128]{1,0:T(8,128)(2,1)S(1)}, u32[]{:S(2)}, u32[]{:S(2)}) collective-permute-start(bf16[320,128]{1,0:T(8,128)(2,1)S(1)} %get-tuple-element.32), channel_id=1, source_target_pairs={{0,6},{1,7},{2,0},{3,1},{4,2},{5,3},{6,4},{7,5},{8,14},{9,15},{10,... | collective-permute-start | bytes 245768 | tf_op jit(solution)/shard_map/ppermute | solution.py:564
  108.1 2.0 %own_attention.1.refs_0_ = bf16[320,128]{1,0:T(8,128)(2,1)S(1)} custom-call(bf16[992,1024]{1,0:T(8,128)(2,1)S(1)} %get-tuple-element.28.made_ref, bf16[5,1024,64]{2,1,0:T(8,128)(2,1)S(1)} %get-tuple-element.29.key_ref), custom_call_target="tpu_custom_call" | custom-call | flops 167772160 | bytes 2621440 | tf_op jit(solution)/shard_map/own_attention/pallas_call | solution.py:565
  110.0 2.8 %collective-permute-done.35.refs_2_ = bf16[320,128]{1,0:T(8,128)(2,1)S(1)} collective-permute-done((bf16[320,128]{1,0:T(8,128)(2,1)S(1)}, bf16[320,128]{1,0:T(8,128)(2,1)S(1)}, u32[]{:S(2)}, u32[]{:S(2)}) %collective-permute-start.35) | collective-permute-done | bytes 81952 | tf_op jit(solution)/shard_map/ppermute | solution.py:564
  112.8 2.0 %project.1 = bf16[128,1280]{1,0:T(8,128)(2,1)} custom-call(bf16[320,128]{1,0:T(8,128)(2,1)S(1)} %own_attention.1.refs_0_, bf16[320,128]{1,0:T(8,128)(2,1)S(1)} %collective-permute-done.34.refs_1_, bf16[320,128]{1,0:T(8,128)(2,1)S(1)} %collective-permute-done.35.refs_2_, bf16[320,128]{1,0:T(8,128)(2,1)S(1)} %collective-permute-done.36.refs_3_, ...), custom_call_target="tpu_custom_call" | custom-call | flops 419430400 | bytes 4259840 | tf_op jit(solution)/shard_map/project/pallas_call | solution.py:582
  (81 shorter events, 20.4 us)
Async XLA Ops:
  1.0 7.8 %collective-permute-start = (bf16[64,1280]{1,0:T(8,128)(2,1)S(1)}, bf16[64,1280]{1,0:T(8,128)(2,1)S(1)}, u32[]{:S(2)}, u32[]{:S(2)}) collective-permute-start(bf16[64,1280]{1,0:T(8,128)(2,1)S(1)} %get-tuple-element.38.refs_0_), channel_id=1, source_target_pairs={{0,1},{1,3},{3,5},{5,7},{7,6},{6,4},{4,2},{2,0},{8,9},{9,11},{11,1... | collective-permute-start | bytes 491528 | tf_op jit(solution)/shard_map/ppermute | solution.py:386
  4.1 11.3 %collective-permute-start.2 = (bf16[64,1280]{1,0:T(8,128)(2,1)S(1)}, bf16[64,1280]{1,0:T(8,128)(2,1)S(1)}, u32[]{:S(2)}, u32[]{:S(2)}) collective-permute-start(bf16[64,1280]{1,0:T(8,128)(2,1)S(1)} %get-tuple-element.38.refs_0_), channel_id=1, source_target_pairs={{1,0},{3,1},{5,3},{7,5},{6,7},{4,6},{2,4},{0,2},{9,8},{11,9},{13,1... | collective-permute-start | bytes 491528 | tf_op jit(solution)/shard_map/ppermute | solution.py:386
  4.2 9.0 %collective-permute-start.3 = (bf16[64,1280]{1,0:T(8,128)(2,1)S(1)}, bf16[64,1280]{1,0:T(8,128)(2,1)S(1)}, u32[]{:S(2)}, u32[]{:S(2)}) collective-permute-start(bf16[64,1280]{1,0:T(8,128)(2,1)S(1)} %get-tuple-element.37.refs_1_), channel_id=1, source_target_pairs={{1,0},{3,1},{5,3},{7,5},{6,7},{4,6},{2,4},{0,2},{9,8},{11,9},{13,1... | collective-permute-start | bytes 491528 | tf_op jit(solution)/shard_map/ppermute | solution.py:386
  6.1 10.8 %collective-permute-start.1 = (bf16[64,1280]{1,0:T(8,128)(2,1)S(1)}, bf16[64,1280]{1,0:T(8,128)(2,1)S(1)}, u32[]{:S(2)}, u32[]{:S(2)}) collective-permute-start(bf16[64,1280]{1,0:T(8,128)(2,1)S(1)} %get-tuple-element.37.refs_1_), channel_id=1, source_target_pairs={{0,1},{1,3},{3,5},{5,7},{7,6},{6,4},{4,2},{2,0},{8,9},{9,11},{11,1... | collective-permute-start | bytes 491528 | tf_op jit(solution)/shard_map/ppermute | solution.py:386
  8.8 8.5 %collective-permute-start.4 = (bf16[64,1280]{1,0:T(8,128)(2,1)S(1)}, bf16[64,1280]{1,0:T(8,128)(2,1)S(1)}, u32[]{:S(2)}, u32[]{:S(2)}) collective-permute-start(bf16[64,1280]{1,0:T(8,128)(2,1)S(1)} %after.5.refs_2_), channel_id=1, source_target_pairs={{0,1},{1,3},{3,5},{5,7},{7,6},{6,4},{4,2},{2,0},{8,9},{9,11},{11,1... | collective-permute-start | bytes 491528 | tf_op jit(solution)/shard_map/ppermute | solution.py:386
  13.2 6.9 %collective-permute-start.7 = (bf16[64,1280]{1,0:T(8,128)(2,1)S(1)}, bf16[64,1280]{1,0:T(8,128)(2,1)S(1)}, u32[]{:S(2)}, u32[]{:S(2)}) collective-permute-start(bf16[64,1280]{1,0:T(8,128)(2,1)S(1)} %collective-permute-done.3.refs_5_), channel_id=1, source_target_pairs={{1,0},{3,1},{5,3},{7,5},{6,7},{4,6},{2,4},{0,2},{9,8},{11,9},{13,1... | collective-permute-start | bytes 491528 | tf_op jit(solution)/shard_map/ppermute | solution.py:386
  13.6 26.4 %collective-permute-start.22 = (bf16[160,1280]{1,0:T(8,128)(2,1)S(1)}, bf16[160,1280]{1,0:T(8,128)(2,1)S(1)}, u32[]{:S(2)}, u32[]{:S(2)}) collective-permute-start(bf16[160,1280]{1,0:T(8,128)(2,1)S(1)} %copy-done), channel_id=1, source_target_pairs={{0,2},{1,3},{2,4},{3,5},{4,6},{5,7},{6,0},{7,1},{8,12},{9,13},{10,... | collective-permute-start | bytes 1228808 | tf_op jit(solution)/shard_map/ppermute | solution.py:401
  15.3 15.1 %collective-permute-start.6 = (bf16[64,1280]{1,0:T(8,128)(2,1)S(1)}, bf16[64,1280]{1,0:T(8,128)(2,1)S(1)}, u32[]{:S(2)}, u32[]{:S(2)}) collective-permute-start(bf16[64,1280]{1,0:T(8,128)(2,1)S(1)} %collective-permute-done.2.refs_4_), channel_id=1, source_target_pairs={{1,0},{3,1},{5,3},{7,5},{6,7},{4,6},{2,4},{0,2},{9,8},{11,9},{13,1... | collective-permute-start | bytes 491528 | tf_op jit(solution)/shard_map/ppermute | solution.py:386
  16.9 19.6 %collective-permute-start.5 = (bf16[64,1280]{1,0:T(8,128)(2,1)S(1)}, bf16[64,1280]{1,0:T(8,128)(2,1)S(1)}, u32[]{:S(2)}, u32[]{:S(2)}) collective-permute-start(bf16[64,1280]{1,0:T(8,128)(2,1)S(1)} %collective-permute-done.1.refs_3_), channel_id=1, source_target_pairs={{0,1},{1,3},{3,5},{5,7},{7,6},{6,4},{4,2},{2,0},{8,9},{9,11},{11,1... | collective-permute-start | bytes 491528 | tf_op jit(solution)/shard_map/ppermute | solution.py:386
  17.3 19.2 %collective-permute-start.8 = (bf16[64,1280]{1,0:T(8,128)(2,1)S(1)}, bf16[64,1280]{1,0:T(8,128)(2,1)S(1)}, u32[]{:S(2)}, u32[]{:S(2)}) collective-permute-start(bf16[64,1280]{1,0:T(8,128)(2,1)S(1)} %collective-permute-done.4.refs_6_), channel_id=1, source_target_pairs={{0,1},{1,3},{3,5},{5,7},{7,6},{6,4},{4,2},{2,0},{8,9},{9,11},{11,1... | collective-permute-start | bytes 491528 | tf_op jit(solution)/shard_map/ppermute | solution.py:386
  20.1 16.5 %collective-permute-start.11 = (bf16[64,1280]{1,0:T(8,128)(2,1)S(1)}, bf16[64,1280]{1,0:T(8,128)(2,1)S(1)}, u32[]{:S(2)}, u32[]{:S(2)}) collective-permute-start(bf16[64,1280]{1,0:T(8,128)(2,1)S(1)} %collective-permute-done.7.refs_9_), channel_id=1, source_target_pairs={{1,0},{3,1},{5,3},{7,5},{6,7},{4,6},{2,4},{0,2},{9,8},{11,9},{13,1... | collective-permute-start | bytes 491528 | tf_op jit(solution)/shard_map/ppermute | solution.py:386
  30.4 9.6 %collective-permute-start.10 = (bf16[64,1280]{1,0:T(8,128)(2,1)S(1)}, bf16[64,1280]{1,0:T(8,128)(2,1)S(1)}, u32[]{:S(2)}, u32[]{:S(2)}) collective-permute-start(bf16[64,1280]{1,0:T(8,128)(2,1)S(1)} %collective-permute-done.6.refs_8_), channel_id=1, source_target_pairs={{1,0},{3,1},{5,3},{7,5},{6,7},{4,6},{2,4},{0,2},{9,8},{11,9},{13,1... | collective-permute-start | bytes 491528 | tf_op jit(solution)/shard_map/ppermute | solution.py:386
  36.5 10.3 %collective-permute-start.12 = (bf16[64,1280]{1,0:T(8,128)(2,1)S(1)}, bf16[64,1280]{1,0:T(8,128)(2,1)S(1)}, u32[]{:S(2)}, u32[]{:S(2)}) collective-permute-start(bf16[64,1280]{1,0:T(8,128)(2,1)S(1)} %collective-permute-done.8.refs_10_.refs_2_), channel_id=1, source_target_pairs={{0,1},{1,3},{3,5},{5,7},{7,6},{6,4},{4,2},{2,0},{8,9},{9,11},{11,1... | collective-permute-start | bytes 491528 | tf_op jit(solution)/shard_map/ppermute | solution.py:386
  36.6 10.2 %collective-permute-start.13 = (bf16[64,1280]{1,0:T(8,128)(2,1)S(1)}, bf16[64,1280]{1,0:T(8,128)(2,1)S(1)}, u32[]{:S(2)}, u32[]{:S(2)}) collective-permute-start(bf16[64,1280]{1,0:T(8,128)(2,1)S(1)} %collective-permute-done.11.refs_13_.refs_5_), channel_id=1, source_target_pairs={{1,0},{3,1},{5,3},{7,5},{6,7},{4,6},{2,4},{0,2},{9,8},{11,9},{13,1... | collective-permute-start | bytes 491528 | tf_op jit(solution)/shard_map/ppermute | solution.py:386
  42.3 20.7 %collective-permute-start.23 = (bf16[208,1280]{1,0:T(8,128)(2,1)S(1)}, bf16[208,1280]{1,0:T(8,128)(2,1)S(1)}, u32[]{:S(2)}, u32[]{:S(2)}) collective-permute-start(bf16[208,1280]{1,0:T(8,128)(2,1)S(1)} %get-tuple-element.23), channel_id=1, source_target_pairs={{0,1},{1,0},{2,3},{3,2},{4,5},{5,4},{6,7},{7,6},{8,9},{9,8},{10,11... | collective-permute-start | bytes 1597448 | tf_op jit(solution)/shard_map/ppermute | solution.py:401
  42.3 20.4 %collective-permute-start.24 = (bf16[160,1280]{1,0:T(8,128)(2,1)S(1)}, bf16[160,1280]{1,0:T(8,128)(2,1)S(1)}, u32[]{:S(2)}, u32[]{:S(2)}) collective-permute-start(bf16[160,1280]{1,0:T(8,128)(2,1)S(1)} %get-tuple-element.24), channel_id=1, source_target_pairs={{0,16},{8,24},{16,0},{24,8},{1,17},{9,25},{17,1},{25,9},{2,18},{10... | collective-permute-start | bytes 1228808 | tf_op jit(solution)/shard_map/ppermute | solution.py:406
  54.5 10.0 %collective-permute-start.18 = (bf16[160,512]{1,0:T(8,128)(2,1)S(1)}, bf16[160,512]{1,0:T(8,128)(2,1)S(1)}, u32[]{:S(2)}, u32[]{:S(2)}) collective-permute-start(bf16[160,512]{1,0:T(8,128)(2,1)S(1)} %get-tuple-element.22.refs_1_), channel_id=1, source_target_pairs={{1,0},{3,1},{5,3},{7,5},{6,7},{4,6},{2,4},{0,2},{9,8},{11,9},{13,1... | collective-permute-start | bytes 491528 | tf_op jit(solution)/shard_map/ppermute | solution.py:386
  56.7 9.1 %collective-permute-start.28 = (bf16[160,512]{1,0:T(8,128)(2,1)S(1)}, bf16[160,512]{1,0:T(8,128)(2,1)S(1)}, u32[]{:S(2)}, u32[]{:S(2)}) collective-permute-start(bf16[160,512]{1,0:T(8,128)(2,1)S(1)} %get-tuple-element.22.refs_1_), channel_id=1, source_target_pairs={{0,1},{1,3},{3,5},{5,7},{7,6},{6,4},{4,2},{2,0},{8,9},{9,11},{11,1... | collective-permute-start | bytes 491528 | tf_op jit(solution)/shard_map/ppermute | solution.py:386
  61.0 6.7 %collective-permute-start.29 = (bf16[160,512]{1,0:T(8,128)(2,1)S(1)}, bf16[160,512]{1,0:T(8,128)(2,1)S(1)}, u32[]{:S(2)}, u32[]{:S(2)}) collective-permute-start(bf16[160,512]{1,0:T(8,128)(2,1)S(1)} %get-tuple-element.21.refs_2_.refs_0_), channel_id=1, source_target_pairs={{1,0},{3,1},{5,3},{7,5},{6,7},{4,6},{2,4},{0,2},{9,8},{11,9},{13,1... | collective-permute-start | bytes 491528 | tf_op jit(solution)/shard_map/ppermute | solution.py:386
  62.7 7.0 %collective-permute-start.15 = (bf16[160,512]{1,0:T(8,128)(2,1)S(1)}, bf16[160,512]{1,0:T(8,128)(2,1)S(1)}, u32[]{:S(2)}, u32[]{:S(2)}) collective-permute-start(bf16[160,512]{1,0:T(8,128)(2,1)S(1)} %collective-permute-done.14.refs_2_), channel_id=1, source_target_pairs={{0,1},{1,3},{3,5},{5,7},{7,6},{6,4},{4,2},{2,0},{8,9},{9,11},{11,1... | collective-permute-start | bytes 491528 | tf_op jit(solution)/shard_map/ppermute | solution.py:386
  63.0 13.3 %collective-permute-start.25 = (bf16[128,1280]{1,0:T(8,128)(2,1)S(1)}, bf16[128,1280]{1,0:T(8,128)(2,1)S(1)}, u32[]{:S(2)}, u32[]{:S(2)}) collective-permute-start(bf16[128,1280]{1,0:T(8,128)(2,1)S(1)} %slice.22.refs_17_.refs_5_), channel_id=1, source_target_pairs={{0,16},{8,24},{16,0},{24,8},{1,17},{9,25},{17,1},{25,9},{2,18},{10... | collective-permute-start | bytes 983048 | tf_op jit(solution)/shard_map/ppermute | solution.py:406
  64.5 6.7 %collective-permute-start.19 = (bf16[160,512]{1,0:T(8,128)(2,1)S(1)}, bf16[160,512]{1,0:T(8,128)(2,1)S(1)}, u32[]{:S(2)}, u32[]{:S(2)}) collective-permute-start(bf16[160,512]{1,0:T(8,128)(2,1)S(1)} %collective-permute-done.18.refs_5_), channel_id=1, source_target_pairs={{1,0},{3,1},{5,3},{7,5},{6,7},{4,6},{2,4},{0,2},{9,8},{11,9},{13,1... | collective-permute-start | bytes 491528 | tf_op jit(solution)/shard_map/ppermute | solution.py:386
  65.8 7.4 %collective-permute-start.30 = (bf16[160,512]{1,0:T(8,128)(2,1)S(1)}, bf16[160,512]{1,0:T(8,128)(2,1)S(1)}, u32[]{:S(2)}, u32[]{:S(2)}) collective-permute-start(bf16[160,512]{1,0:T(8,128)(2,1)S(1)} %collective-permute-done.28.refs_3_), channel_id=1, source_target_pairs={{0,1},{1,3},{3,5},{5,7},{7,6},{6,4},{4,2},{2,0},{8,9},{9,11},{11,1... | collective-permute-start | bytes 491528 | tf_op jit(solution)/shard_map/ppermute | solution.py:386
  67.6 7.1 %collective-permute-start.31 = (bf16[160,512]{1,0:T(8,128)(2,1)S(1)}, bf16[160,512]{1,0:T(8,128)(2,1)S(1)}, u32[]{:S(2)}, u32[]{:S(2)}) collective-permute-start(bf16[160,512]{1,0:T(8,128)(2,1)S(1)} %collective-permute-done.29.refs_4_), channel_id=1, source_target_pairs={{1,0},{3,1},{5,3},{7,5},{6,7},{4,6},{2,4},{0,2},{9,8},{11,9},{13,1... | collective-permute-start | bytes 491528 | tf_op jit(solution)/shard_map/ppermute | solution.py:386
  76.3 7.6 %collective-permute-start.27 = (bf16[128,1280]{1,0:T(8,128)(2,1)S(1)}, bf16[128,1280]{1,0:T(8,128)(2,1)S(1)}, u32[]{:S(2)}, u32[]{:S(2)}) collective-permute-start(bf16[128,1280]{1,0:T(8,128)(2,1)S(1)} %collective-permute-done.25.refs_18_.refs_6_), channel_id=1, source_target_pairs={{0,8},{8,0},{16,24},{24,16},{1,9},{9,1},{17,25},{25,17},{2,10},{10... | collective-permute-start | bytes 983048 | tf_op jit(solution)/shard_map/ppermute | solution.py:406
  80.1 32.8 %collective-permute-start.37 = (bf16[400,1280]{1,0:T(8,128)(2,1)S(1)}, bf16[400,1280]{1,0:T(8,128)(2,1)S(1)}, u32[]{:S(2)}, u32[]{:S(2)}) collective-permute-start(bf16[400,1280]{1,0:T(8,128)(2,1)S(1)} %get-tuple-element.35.refs_6_), channel_id=1, source_target_pairs={{0,8},{8,0},{16,24},{24,16},{1,9},{9,1},{17,25},{25,17},{2,10},{10... | collective-permute-start | bytes 3072008 | tf_op jit(solution)/shard_map/ppermute | solution.py:406
  80.1 22.4 %collective-permute-start.38 = (bf16[160,1280]{1,0:T(8,128)(2,1)S(1)}, bf16[160,1280]{1,0:T(8,128)(2,1)S(1)}, u32[]{:S(2)}, u32[]{:S(2)}) collective-permute-start(bf16[160,1280]{1,0:T(8,128)(2,1)S(1)} %get-tuple-element.36), channel_id=1, source_target_pairs={{0,3},{1,2},{2,5},{3,4},{4,7},{5,6},{6,1},{7,0},{8,15},{9,14},{10,... | collective-permute-start | bytes 1228808 | tf_op jit(solution)/shard_map/ppermute | solution.py:401
  81.9 13.5 %collective-permute-start.17 = (bf16[160,512]{1,0:T(8,128)(2,1)S(1)}, bf16[160,512]{1,0:T(8,128)(2,1)S(1)}, u32[]{:S(2)}, u32[]{:S(2)}) collective-permute-start(bf16[160,512]{1,0:T(8,128)(2,1)S(1)} %collective-permute-done.16.refs_10_.refs_2_), channel_id=1, source_target_pairs={{0,1},{1,3},{3,5},{5,7},{7,6},{6,4},{4,2},{2,0},{8,9},{9,11},{11,1... | collective-permute-start | bytes 491528 | tf_op jit(solution)/shard_map/ppermute | solution.py:386
  82.8 13.5 %collective-permute-start.21 = (bf16[160,512]{1,0:T(8,128)(2,1)S(1)}, bf16[160,512]{1,0:T(8,128)(2,1)S(1)}, u32[]{:S(2)}, u32[]{:S(2)}) collective-permute-start(bf16[160,512]{1,0:T(8,128)(2,1)S(1)} %collective-permute-done.20.refs_13_.refs_5_), channel_id=1, source_target_pairs={{1,0},{3,1},{5,3},{7,5},{6,7},{4,6},{2,4},{0,2},{9,8},{11,9},{13,1... | collective-permute-start | bytes 491528 | tf_op jit(solution)/shard_map/ppermute | solution.py:386
  102.5 10.3 %collective-permute-start.39 = (bf16[160,1280]{1,0:T(8,128)(2,1)S(1)}, bf16[160,1280]{1,0:T(8,128)(2,1)S(1)}, u32[]{:S(2)}, u32[]{:S(2)}) collective-permute-start(bf16[160,1280]{1,0:T(8,128)(2,1)S(1)} %after.9.refs_8_), channel_id=1, source_target_pairs={{0,8},{8,0},{16,24},{24,16},{1,9},{9,1},{17,25},{25,17},{2,10},{10... | collective-permute-start | bytes 1228808 | tf_op jit(solution)/shard_map/ppermute | solution.py:406
  102.7 7.3 %collective-permute-start.34 = (bf16[320,128]{1,0:T(8,128)(2,1)S(1)}, bf16[320,128]{1,0:T(8,128)(2,1)S(1)}, u32[]{:S(2)}, u32[]{:S(2)}) collective-permute-start(bf16[320,128]{1,0:T(8,128)(2,1)S(1)} %get-tuple-element.30.refs_1_), channel_id=1, source_target_pairs={{0,2},{1,3},{2,4},{3,5},{4,6},{5,7},{6,0},{7,1},{8,10},{9,11},{10,... | collective-permute-start | bytes 245768 | tf_op jit(solution)/shard_map/ppermute | solution.py:564
  104.1 8.7 %collective-permute-start.35 = (bf16[320,128]{1,0:T(8,128)(2,1)S(1)}, bf16[320,128]{1,0:T(8,128)(2,1)S(1)}, u32[]{:S(2)}, u32[]{:S(2)}) collective-permute-start(bf16[320,128]{1,0:T(8,128)(2,1)S(1)} %get-tuple-element.31), channel_id=1, source_target_pairs={{0,4},{1,5},{2,6},{3,7},{4,0},{5,1},{6,2},{7,3},{8,12},{9,13},{10,... | collective-permute-start | bytes 245768 | tf_op jit(solution)/shard_map/ppermute | solution.py:564
  (15 other events, 196.6 us)

commit v10 on v8

--- a/solution.py
+++ b/solution.py
@@ -18,8 +18,7 @@
 QUAD = 4
 GRANULE = 32
 HANDED = (0, 2, 1, 3)
-FAR = ((1, 0), (2, 0), (3, 0), (2, 1))
-LAST = ((1, 1), (3, 1))
+FAR = ((1, 0), (3, 0), (2, 0), (0, 1))
 SOONER = tuple(range(1, OUTER))
 WIDE = 256
 EPSILON = 1e-05
@@ -326,16 +325,28 @@
         rows = pl.ds(pl.multiple_of(origin * own + low, 16), weights.shape[0])
         total_ref[rows, :] += dot(weights, attended)
 
-    own_ref, far_ref, far_other_ref, last_ref, last_other_ref = weight_refs
+    own_ref, far_ref, across_ref, other_ref, mine_ref, others_ref = weight_refs
+    side = lax.div(mine, 2)
     add(own_ref[...], 0, 0)
-    for holder, ref in ((mine, far_ref), (jnp.bitwise_xor(mine, 1), far_other_ref)):
-        for step in (0, 1):
-            which = jnp.bitwise_xor(holder, 2 * step)
-            outer_step = jnp.where(which == 0, 1, jnp.where(which == 2, 3, 2))
-            add(ref[step * own : (step + 1) * own, :], outer_step, lax.div(which, QUAD - 1))
-        add(ref[2 * own :, :], 0, 1, lax.rem(holder, 2) * (own // 2))
-    add(last_ref[...], 1 + 2 * core, 1)
-    add(last_other_ref[...], 3 - 2 * core, 1)
+    far = [far_ref[...], across_ref[...], other_ref[:own, :], other_ref[own:, :]]
+    for step, weights in zip(HANDED, far):
+        which = jnp.bitwise_xor(mine, step)
+        outer_step = jnp.where(which == 0, 1, jnp.where(which == 1, 3, jnp.where(which == 2, 2, 0)))
+        add(weights, outer_step, lax.div(which, QUAD - 1))
+
+    def add_relayed(two_ref, one_ref):
+        add(two_ref[:own, :], 1 + side, 1)
+        add(two_ref[own:, :], 2 - side, 1)
+        add(one_ref[:own, :], 3, 1)
+
+    @pl.when(core == 0)
+    def _():
+        add_relayed(mine_ref, others_ref)
+
+    @pl.when(core == 1)
+    def _():
+        add_relayed(others_ref, mine_ref)
+
     out_ref[...] = total_ref[...].T.astype(bf16)
 
 
@@ -396,7 +407,8 @@
     batch, n = lax.axis_size("batch"), lax.axis_size("patch")
     pairs = []
     for at in range(batch):
-        for start, target in moves(n, *shifts[at % len(shifts)]):
+        shift = shifts[at % len(shifts)]
+        for start, target in moves(n, *shift) if shift else ():
             pairs.append((at * n + start, at * n + target))
     return lax.ppermute(block, ("batch", "patch"), pairs)
 
@@ -448,14 +460,9 @@
     chosen = []
     if inner == 2:
         quarter = quarter_rows(own)
-        core = lax.rem(lax.axis_index("batch"), 2)
         start = quarter_start(lax.rem(lax.axis_index("batch"), QUAD), own) * GRANULE
         stacked = jnp.concatenate([w_query, w_key, w_value], axis=0)
-        chosen = [
-            lax.dynamic_slice_in_dim(stacked, start, quarter, 0),
-            lax.dynamic_slice_in_dim(w_out, core * (own // 2), own // 2, 0),
-        ]
-        chosen = [jnp.concatenate(chosen, axis=0)]
+        chosen = [lax.dynamic_slice_in_dim(stacked, start, quarter, 0)]
     pieces = gather(halves, n, chosen)
     stats = pl.pallas_call(
         stats_kernel,
@@ -507,12 +514,12 @@
 
     hidden_pieces = gather(tuple(hidden), n)
     if inner == 2:
-        (chosen,) = after([chosen], hidden[:1])
-        near = [chosen[:quarter]]
+        near = after([chosen], hidden[:1])
         near.append(swap(near[0], 2))
-        near[0], far = after([near[0], far], near[1:])
         near += [swap(one, 1) for one in near]
         weights = [w_query, w_key, w_value] + near
+        far = [far, swap(far, 2)]
+
     made_rows = sum(weight.shape[0] for weight in weights)
     sums, some = pl.pallas_call(
         functools.partial(project_kernel, 2 * n),
@@ -532,9 +539,11 @@
         name="norm_project",
     )(sources, *hidden_pieces[:-2], *weights)
     if inner == 2:
-        far, out_own = after([far, out_own], hidden_pieces[-6:-2])
-        across = swap(far, 2)
-        last = send(out_own, LAST)
+        far = after(far, hidden_pieces[-6:-2])
+        place = lax.rem(lax.axis_index("batch"), QUAD)
+        relayed = [send(jnp.where(place == QUAD - 1, far[1], far[0]), [(0, 1)])]
+        relayed.append(send(far[1], [(0, 1), None]))
+        far.append(swap(jnp.concatenate(far, axis=0), 1))
     one_block = jax.ShapeDtypeStruct((SET_CHANNELS, block), bf16)
     *sent, kept, made, key = pl.pallas_call(
         functools.partial(attention_kernel, 2 * n, inner),
@@ -574,9 +583,8 @@
         name="own_attention",
     )(made, key)
     if inner == 2:
-        far = jnp.concatenate([far, across, chosen[quarter:]], axis=0)
-        far, last = after([far, last], sent[:1])
-        out_weights = [w_out, far, swap(far, 1), last, swap(last, 1)]
+        (relayed,) = after([jnp.concatenate(relayed, axis=0)], sent[:1])
+        out_weights = [w_out] + far + [relayed, swap(relayed, 1)]
 
     output = pl.pallas_call(
         functools.partial(output_kernel, n),

time: 106 us -> 110 us (1.038)
  waiting for transfers between devices: 28.4 us -> 34.4 us
  starting transfers between devices: 49 us -> 46.7 us
    ppermute x28, starting transfers between devices: 38.6 us -> 30.4 us  [gather(): lax.ppermute(found[half, sign * (step - 1)], 'patch', pairs)]
    ppermute x28, waiting for transfers between devices: 24.5 us -> 30.1 us  [gather(): lax.ppermute(found[half, sign * (step - 1)], 'patch', pairs)]
    ppermute x6, starting transfers between devices: 1.15 us -> 5.12 us  [swap(): return lax.ppermute(block, 'batch', pairs)]
    ppermute x3 -> x4, starting transfers between devices: 5.89 us -> 7.28 us  [send(): return lax.ppermute(block, ('batch', 'patch'), pairs)]
  transfers between devices with their start and end apart: 40 -> 41, of which waited for: 15 -> 17; matrix products, arithmetic and copies ran while one was open for 2% -> 1% of each run, Pallas kernels for 21% -> 21%
where the time goes in v10:
time: 110 us; the launch traced here: 109 us
  starting transfers between devices  46.7 us (42%)
  waiting for transfers between devices  34.4 us (31%)
  Pallas kernels  25 us (23%)
  local copies, waits for them, and re-layouts  1.8 us (2%)
  other arithmetic  1.38 us (1%)
    ppermute x28, starting transfers between devices, gather(): lax.ppermute(found[half, sign * (step - 1)], 'patch', pairs)  30.4 us
    ppermute x28, waiting for transfers between devices, gather(): lax.ppermute(found[half, sign * (step - 1)], 'patch', pairs)  30.1 us
    pallas_call x1, Pallas kernels, on_device(): pl.pallas_call(functools.partial(conv_kernel, columns), out_shape=[jax.Sh...  7.48 us
    ppermute x4, starting transfers between devices, send(): return lax.ppermute(block, ('batch', 'patch'), pairs)  7.28 us
    pallas_call x1, Pallas kernels, on_device(): pl.pallas_call(functools.partial(project_kernel, 2 * n), out_shape=[jax.S...  6.26 us
    pallas_call x1, Pallas kernels, on_device(): pl.pallas_call(functools.partial(attention_kernel, 2 * n, inner), out_sha...  6.15 us
    ppermute x6, starting transfers between devices, swap(): return lax.ppermute(block, 'batch', pairs)  5.12 us
    ppermute x3, waiting for transfers between devices, on_device(): received.append(lax.ppermute(sent_block, 'patch', pairs))  4.24 us
  transfers between devices with their start and end apart: 41, of which 17 were waited for; matrix products, arithmetic and copies ran while one was open for 1% of the time, Pallas kernels for 21%

profile of v10, /device:TPU:0, one launch (start us, length us, event | category | flops | bytes accessed | tf_op | source)
XLA Modules:
  0.0 109.5 jit_solution(7606556960420057129)
XLA Ops:
  1.1 3.0 %collective-permute-start = (bf16[64,1280]{1,0:T(8,128)(2,1)S(1)}, bf16[64,1280]{1,0:T(8,128)(2,1)S(1)}, u32[]{:S(2)}, u32[]{:S(2)}) collective-permute-start(bf16[64,1280]{1,0:T(8,128)(2,1)S(1)} %get-tuple-element.34.refs_0_), channel_id=1, source_target_pairs={{0,1},{1,3},{3,5},{5,7},{7,6},{6,4},{4,2},{2,0},{8,9},{9,11},{11,1... | collective-permute-start | bytes 491528 | tf_op jit(solution)/shard_map/ppermute | solution.py:397
  4.2 1.9 %collective-permute-start.1 = (bf16[64,1280]{1,0:T(8,128)(2,1)S(1)}, bf16[64,1280]{1,0:T(8,128)(2,1)S(1)}, u32[]{:S(2)}, u32[]{:S(2)}) collective-permute-start(bf16[64,1280]{1,0:T(8,128)(2,1)S(1)} %get-tuple-element.33.refs_1_), channel_id=1, source_target_pairs={{0,1},{1,3},{3,5},{5,7},{7,6},{6,4},{4,2},{2,0},{8,9},{9,11},{11,1... | collective-permute-start | bytes 491528 | tf_op jit(solution)/shard_map/ppermute | solution.py:397
  7.5 1.7 %collective-permute-done.refs_0_ = bf16[64,1280]{1,0:T(8,128)(2,1)S(1)} collective-permute-done((bf16[64,1280]{1,0:T(8,128)(2,1)S(1)}, bf16[64,1280]{1,0:T(8,128)(2,1)S(1)}, u32[]{:S(2)}, u32[]{:S(2)}) %collective-permute-start) | collective-permute-done | bytes 163872 | tf_op jit(solution)/shard_map/ppermute | solution.py:397
  9.2 2.0 %collective-permute-start.4 = (bf16[64,1280]{1,0:T(8,128)(2,1)S(1)}, bf16[64,1280]{1,0:T(8,128)(2,1)S(1)}, u32[]{:S(2)}, u32[]{:S(2)}) collective-permute-start(bf16[64,1280]{1,0:T(8,128)(2,1)S(1)} %after.5.refs_2_), channel_id=1, source_target_pairs={{0,1},{1,3},{3,5},{5,7},{7,6},{6,4},{4,2},{2,0},{8,9},{9,11},{11,1... | collective-permute-start | bytes 491528 | tf_op jit(solution)/shard_map/ppermute | solution.py:397
  11.2 2.1 %collective-permute-done.3.refs_5_ = bf16[64,1280]{1,0:T(8,128)(2,1)S(1)} collective-permute-done((bf16[64,1280]{1,0:T(8,128)(2,1)S(1)}, bf16[64,1280]{1,0:T(8,128)(2,1)S(1)}, u32[]{:S(2)}, u32[]{:S(2)}) %collective-permute-start.3) | collective-permute-done | bytes 163872 | tf_op jit(solution)/shard_map/ppermute | solution.py:397
  13.7 1.6 %collective-permute-start.5 = (bf16[64,1280]{1,0:T(8,128)(2,1)S(1)}, bf16[64,1280]{1,0:T(8,128)(2,1)S(1)}, u32[]{:S(2)}, u32[]{:S(2)}) collective-permute-start(bf16[64,1280]{1,0:T(8,128)(2,1)S(1)} %collective-permute-done.1.refs_3_), channel_id=1, source_target_pairs={{0,1},{1,3},{3,5},{5,7},{7,6},{6,4},{4,2},{2,0},{8,9},{9,11},{11,1... | collective-permute-start | bytes 491528 | tf_op jit(solution)/shard_map/ppermute | solution.py:397
  15.7 2.1 %collective-permute-start.8 = (bf16[64,1280]{1,0:T(8,128)(2,1)S(1)}, bf16[64,1280]{1,0:T(8,128)(2,1)S(1)}, u32[]{:S(2)}, u32[]{:S(2)}) collective-permute-start(bf16[64,1280]{1,0:T(8,128)(2,1)S(1)} %collective-permute-done.4.refs_6_), channel_id=1, source_target_pairs={{0,1},{1,3},{3,5},{5,7},{7,6},{6,4},{4,2},{2,0},{8,9},{9,11},{11,1... | collective-permute-start | bytes 491528 | tf_op jit(solution)/shard_map/ppermute | solution.py:397
  17.8 2.6 %collective-permute-done.7.refs_9_ = bf16[64,1280]{1,0:T(8,128)(2,1)S(1)} collective-permute-done((bf16[64,1280]{1,0:T(8,128)(2,1)S(1)}, bf16[64,1280]{1,0:T(8,128)(2,1)S(1)}, u32[]{:S(2)}, u32[]{:S(2)}) %collective-permute-start.7) | collective-permute-done | bytes 163872 | tf_op jit(solution)/shard_map/ppermute | solution.py:397
  20.8 1.6 %collective-permute-start.9 = (bf16[64,1280]{1,0:T(8,128)(2,1)S(1)}, bf16[64,1280]{1,0:T(8,128)(2,1)S(1)}, u32[]{:S(2)}, u32[]{:S(2)}) collective-permute-start(bf16[64,1280]{1,0:T(8,128)(2,1)S(1)} %collective-permute-done.5.refs_7_), channel_id=1, source_target_pairs={{0,1},{1,3},{3,5},{5,7},{7,6},{6,4},{4,2},{2,0},{8,9},{9,11},{11,1... | collective-permute-start | bytes 491528 | tf_op jit(solution)/shard_map/ppermute | solution.py:397
  22.4 1.5 %collective-permute-done.6.refs_8_ = bf16[64,1280]{1,0:T(8,128)(2,1)S(1)} collective-permute-done((bf16[64,1280]{1,0:T(8,128)(2,1)S(1)}, bf16[64,1280]{1,0:T(8,128)(2,1)S(1)}, u32[]{:S(2)}, u32[]{:S(2)}) %collective-permute-start.6) | collective-permute-done | bytes 163872 | tf_op jit(solution)/shard_map/ppermute | solution.py:397
  24.3 1.6 %collective-permute-start.12 = (bf16[64,1280]{1,0:T(8,128)(2,1)S(1)}, bf16[64,1280]{1,0:T(8,128)(2,1)S(1)}, u32[]{:S(2)}, u32[]{:S(2)}) collective-permute-start(bf16[64,1280]{1,0:T(8,128)(2,1)S(1)} %collective-permute-done.8.refs_10_.refs_2_), channel_id=1, source_target_pairs={{0,1},{1,3},{3,5},{5,7},{7,6},{6,4},{4,2},{2,0},{8,9},{9,11},{11,1... | collective-permute-start | bytes 491528 | tf_op jit(solution)/shard_map/ppermute | solution.py:397
  25.9 1.6 %collective-permute-done.11.refs_13_.refs_5_ = bf16[64,1280]{1,0:T(8,128)(2,1)S(1)} collective-permute-done((bf16[64,1280]{1,0:T(8,128)(2,1)S(1)}, bf16[64,1280]{1,0:T(8,128)(2,1)S(1)}, u32[]{:S(2)}, u32[]{:S(2)}) %collective-permute-start.11) | collective-permute-done | bytes 163872 | tf_op jit(solution)/shard_map/ppermute | solution.py:397
  28.0 3.0 %collective-permute-done.10.refs_12_.refs_4_ = bf16[64,1280]{1,0:T(8,128)(2,1)S(1)} collective-permute-done((bf16[64,1280]{1,0:T(8,128)(2,1)S(1)}, bf16[64,1280]{1,0:T(8,128)(2,1)S(1)}, u32[]{:S(2)}, u32[]{:S(2)}) %collective-permute-start.10) | collective-permute-done | bytes 163872 | tf_op jit(solution)/shard_map/ppermute | solution.py:397
  31.1 1.6 %collective-permute-start.22 = (bf16[128,1280]{1,0:T(8,128)(2,1)S(1)}, bf16[128,1280]{1,0:T(8,128)(2,1)S(1)}, u32[]{:S(2)}, u32[]{:S(2)}) collective-permute-start(bf16[128,1280]{1,0:T(8,128)(2,1)S(1)} %get-tuple-element.21), channel_id=1, source_target_pairs={{0,1},{1,0},{2,3},{3,2},{4,5},{5,4},{6,7},{7,6},{8,9},{9,8},{10,11... | collective-permute-start | bytes 983048 | tf_op jit(solution)/shard_map/ppermute | solution.py:413
  32.6 1.6 %collective-permute-start.35 = (bf16[160,1280]{1,0:T(8,128)(2,1)S(1)}, bf16[160,1280]{1,0:T(8,128)(2,1)S(1)}, u32[]{:S(2)}, u32[]{:S(2)}) collective-permute-start(bf16[160,1280]{1,0:T(8,128)(2,1)S(1)} %get-tuple-element.30), channel_id=1, source_target_pairs={{0,2},{1,3},{2,4},{3,5},{4,6},{5,7},{6,0},{7,1},{8,14},{9,15},{10,... | collective-permute-start | bytes 1228808 | tf_op jit(solution)/shard_map/ppermute | solution.py:413
  35.3 7.5 %norm_conv.1 = (bf16[160,512]{1,0:T(8,128)(2,1)S(1)}, bf16[160,512]{1,0:T(8,128)(2,1)S(1)}) custom-call(s32[128]{0:T(128)S(1)} %copy-done.4, bf16[64,1280]{1,0:T(8,128)(2,1)S(1)} %get-tuple-element.34.refs_0_, bf16[64,1280]{1,0:T(8,128)(2,1)S(1)} %get-tuple-element.33.refs_1_, bf16[64,1280]{1,0:T(8,128)(2,1)S(1)} %after.5.refs_2_, ...), custom_call_target="tpu_custom_call" | custom-call | flops 3774873600 | bytes 6307840 | tf_op jit(solution)/shard_map/norm_conv/pallas_call | solution.py:491
  45.8 3.6 %collective-permute-done.14.refs_2_ = bf16[160,512]{1,0:T(8,128)(2,1)S(1)} collective-permute-done((bf16[160,512]{1,0:T(8,128)(2,1)S(1)}, bf16[160,512]{1,0:T(8,128)(2,1)S(1)}, u32[]{:S(2)}, u32[]{:S(2)}) %collective-permute-start.14) | collective-permute-done | bytes 163872 | tf_op jit(solution)/shard_map/ppermute | solution.py:397
  49.5 1.4 %collective-permute-start.27 = (bf16[160,512]{1,0:T(8,128)(2,1)S(1)}, bf16[160,512]{1,0:T(8,128)(2,1)S(1)}, u32[]{:S(2)}, u32[]{:S(2)}) collective-permute-start(bf16[160,512]{1,0:T(8,128)(2,1)S(1)} %get-tuple-element.19.refs_1_.refs_0_), channel_id=1, source_target_pairs={{1,0},{3,1},{5,3},{7,5},{6,7},{4,6},{2,4},{0,2},{9,8},{11,9},{13,1... | collective-permute-start | bytes 491528 | tf_op jit(solution)/shard_map/ppermute | solution.py:397
  50.9 1.5 %collective-permute-start.15 = (bf16[160,512]{1,0:T(8,128)(2,1)S(1)}, bf16[160,512]{1,0:T(8,128)(2,1)S(1)}, u32[]{:S(2)}, u32[]{:S(2)}) collective-permute-start(bf16[160,512]{1,0:T(8,128)(2,1)S(1)} %collective-permute-done.14.refs_2_), channel_id=1, source_target_pairs={{0,1},{1,3},{3,5},{5,7},{7,6},{6,4},{4,2},{2,0},{8,9},{9,11},{11,1... | collective-permute-start | bytes 491528 | tf_op jit(solution)/shard_map/ppermute | solution.py:397
  52.9 3.0 %collective-permute-start.36 = (bf16[160,1280]{1,0:T(8,128)(2,1)S(1)}, bf16[160,1280]{1,0:T(8,128)(2,1)S(1)}, u32[]{:S(2)}, u32[]{:S(2)}) collective-permute-start(bf16[160,1280]{1,0:T(8,128)(2,1)S(1)} %collective-permute-done.35.refs_0_), channel_id=1, source_target_pairs={{0,16},{8,24},{16,0},{24,8},{1,17},{9,25},{17,1},{25,9},{2,18},{10... | collective-permute-start | bytes 1228808 | tf_op jit(solution)/shard_map/ppermute | solution.py:418
  56.2 2.1 %collective-permute-start.23 = (bf16[128,1280]{1,0:T(8,128)(2,1)S(1)}, bf16[128,1280]{1,0:T(8,128)(2,1)S(1)}, u32[]{:S(2)}, u32[]{:S(2)}) collective-permute-start(bf16[128,1280]{1,0:T(8,128)(2,1)S(1)} %after.7.refs_17_.refs_5_), channel_id=1, source_target_pairs={{0,16},{8,24},{16,0},{24,8},{1,17},{9,25},{17,1},{25,9},{2,18},{10... | collective-permute-start | bytes 983048 | tf_op jit(solution)/shard_map/ppermute | solution.py:418
  58.2 2.5 %collective-permute-start.29 = (bf16[160,512]{1,0:T(8,128)(2,1)S(1)}, bf16[160,512]{1,0:T(8,128)(2,1)}, u32[]{:S(2)}, u32[]{:S(2)}) collective-permute-start(bf16[160,512]{1,0:T(8,128)(2,1)S(1)} %collective-permute-done.27.refs_4_), channel_id=1, source_target_pairs={{1,0},{3,1},{5,3},{7,5},{6,7},{4,6},{2,4},{0,2},{9,8},{11,9},{13,1... | collective-permute-start | bytes 491528 | tf_op jit(solution)/shard_map/ppermute | solution.py:397
  70.2 1.4 %collective-permute-done.31.refs_12_.refs_4_ = bf16[160,512]{1,0:T(8,128)(2,1)S(1)} collective-permute-done((bf16[160,512]{1,0:T(8,128)(2,1)}, bf16[160,512]{1,0:T(8,128)(2,1)S(1)}, u32[]{:S(2)}, u32[]{:S(2)}) %collective-permute-start.31) | collective-permute-done | bytes 163872 | tf_op jit(solution)/shard_map/ppermute | solution.py:397
  71.6 3.3 %collective-permute-start.39 = (bf16[160,1280]{1,0:T(8,128)(2,1)S(1)}, bf16[160,1280]{1,0:T(8,128)(2,1)S(1)}, u32[]{:S(2)}, u32[]{:S(2)}) collective-permute-start(bf16[160,1280]{1,0:T(8,128)(2,1)S(1)} %get-tuple-element.32.refs_7_), channel_id=1, source_target_pairs={{0,1},{1,0},{2,3},{3,2},{4,5},{5,4},{6,7},{7,6},{16,17},{17,16},{1... | collective-permute-start | bytes 1228808 | tf_op jit(solution)/shard_map/ppermute | solution.py:413
  77.0 6.3 %norm_project.1 = (f32[992,1024]{1,0:T(8,128)S(1)}, bf16[1280,128]{1,0:T(8,128)(2,1)S(1)}) custom-call(s32[128]{0:T(128)S(1)} %copy-done.4, bf16[160,512]{1,0:T(8,128)(2,1)S(1)} %get-tuple-element.19.refs_1_.refs_0_, bf16[160,512]{1,0:T(8,128)(2,1)S(1)} %get-tuple-element.20.refs_1_, bf16[160,512]{1,0:T(8,128)(2,1)S(1)} %collective-permute-done.14.refs_2_, ...), custom_call_target="tpu_custom_call" | custom-call | flops 2600468480 | bytes 5160960 | tf_op jit(solution)/shard_map/norm_project/pallas_call | solution.py:524
  83.3 7.7 %collective-permute-done.21.refs_1_ = bf16[160,512]{1,0:T(8,128)(2,1)S(1)} collective-permute-done((bf16[160,512]{1,0:T(8,128)(2,1)S(1)}, bf16[160,512]{1,0:T(8,128)(2,1)S(1)}, u32[]{:S(2)}, u32[]{:S(2)}) %collective-permute-start.21) | collective-permute-done | bytes 163872 | tf_op jit(solution)/shard_map/ppermute | solution.py:397
  90.9 6.2 %attention.1 = (bf16[320,128]{1,0:T(8,128)(2,1)S(1)}, bf16[320,128]{1,0:T(8,128)(2,1)S(1)}, bf16[320,128]{1,0:T(8,128)(2,1)S(1)}, bf16[1280,128]{1,0:T(8,128)(2,...) custom-call(s32[128]{0:T(128)S(1)} %copy-done.4, ...), custom_call_target="tpu_custom_call" | custom-call | flops 1283457024 | bytes 6094848 | tf_op jit(solution)/shard_map/attention/pallas_call | solution.py:548
  97.3 3.3 %collective-permute-start.33 = (bf16[320,128]{1,0:T(8,128)(2,1)S(1)}, bf16[320,128]{1,0:T(8,128)(2,1)S(1)}, u32[]{:S(2)}, u32[]{:S(2)}) collective-permute-start(bf16[320,128]{1,0:T(8,128)(2,1)S(1)} %get-tuple-element.27), channel_id=1, source_target_pairs={{0,4},{1,5},{2,6},{3,7},{4,0},{5,1},{6,2},{7,3},{8,12},{9,13},{10,... | collective-permute-start | bytes 245768 | tf_op jit(solution)/shard_map/ppermute | solution.py:571
  101.2 1.9 %own_attention.1.refs_0_ = bf16[320,128]{1,0:T(8,128)(2,1)S(1)} custom-call(bf16[992,1024]{1,0:T(8,128)(2,1)S(1)} %get-tuple-element.24.made_ref, bf16[5,1024,64]{2,1,0:T(8,128)(2,1)S(1)} %get-tuple-element.25.key_ref), custom_call_target="tpu_custom_call" | custom-call | flops 167772160 | bytes 2621440 | tf_op jit(solution)/shard_map/own_attention/pallas_call | solution.py:572
  103.1 1.4 %collective-permute-done.32.refs_1_ = bf16[320,128]{1,0:T(8,128)(2,1)S(1)} collective-permute-done((bf16[320,128]{1,0:T(8,128)(2,1)S(1)}, bf16[320,128]{1,0:T(8,128)(2,1)S(1)}, u32[]{:S(2)}, u32[]{:S(2)}) %collective-permute-start.32) | collective-permute-done | bytes 81952 | tf_op jit(solution)/shard_map/ppermute | solution.py:571
  104.5 2.9 %collective-permute-done.33.refs_2_ = bf16[320,128]{1,0:T(8,128)(2,1)S(1)} collective-permute-done((bf16[320,128]{1,0:T(8,128)(2,1)S(1)}, bf16[320,128]{1,0:T(8,128)(2,1)S(1)}, u32[]{:S(2)}, u32[]{:S(2)}) %collective-permute-start.33) | collective-permute-done | bytes 81952 | tf_op jit(solution)/shard_map/ppermute | solution.py:571
  107.4 2.1 %project.1 = bf16[128,1280]{1,0:T(8,128)(2,1)} custom-call(bf16[320,128]{1,0:T(8,128)(2,1)S(1)} %own_attention.1.refs_0_, bf16[320,128]{1,0:T(8,128)(2,1)S(1)} %collective-permute-done.32.refs_1_, bf16[320,128]{1,0:T(8,128)(2,1)S(1)} %collective-permute-done.33.refs_2_, bf16[320,128]{1,0:T(8,128)(2,1)S(1)} %collective-permute-done.34.refs_3_, ...), custom_call_target="tpu_custom_call" | custom-call | flops 419430400 | bytes 4259840 | tf_op jit(solution)/shard_map/project/pallas_call | solution.py:589
  (85 shorter events, 21.7 us)
Async XLA Ops:
  1.1 8.1 %collective-permute-start = (bf16[64,1280]{1,0:T(8,128)(2,1)S(1)}, bf16[64,1280]{1,0:T(8,128)(2,1)S(1)}, u32[]{:S(2)}, u32[]{:S(2)}) collective-permute-start(bf16[64,1280]{1,0:T(8,128)(2,1)S(1)} %get-tuple-element.34.refs_0_), channel_id=1, source_target_pairs={{0,1},{1,3},{3,5},{5,7},{7,6},{6,4},{4,2},{2,0},{8,9},{9,11},{11,1... | collective-permute-start | bytes 491528 | tf_op jit(solution)/shard_map/ppermute | solution.py:397
  4.1 11.2 %collective-permute-start.2 = (bf16[64,1280]{1,0:T(8,128)(2,1)S(1)}, bf16[64,1280]{1,0:T(8,128)(2,1)S(1)}, u32[]{:S(2)}, u32[]{:S(2)}) collective-permute-start(bf16[64,1280]{1,0:T(8,128)(2,1)S(1)} %get-tuple-element.34.refs_0_), channel_id=1, source_target_pairs={{1,0},{3,1},{5,3},{7,5},{6,7},{4,6},{2,4},{0,2},{9,8},{11,9},{13,1... | collective-permute-start | bytes 491528 | tf_op jit(solution)/shard_map/ppermute | solution.py:397
  4.2 9.5 %collective-permute-start.1 = (bf16[64,1280]{1,0:T(8,128)(2,1)S(1)}, bf16[64,1280]{1,0:T(8,128)(2,1)S(1)}, u32[]{:S(2)}, u32[]{:S(2)}) collective-permute-start(bf16[64,1280]{1,0:T(8,128)(2,1)S(1)} %get-tuple-element.33.refs_1_), channel_id=1, source_target_pairs={{0,1},{1,3},{3,5},{5,7},{7,6},{6,4},{4,2},{2,0},{8,9},{9,11},{11,1... | collective-permute-start | bytes 491528 | tf_op jit(solution)/shard_map/ppermute | solution.py:397
  6.1 7.1 %collective-permute-start.3 = (bf16[64,1280]{1,0:T(8,128)(2,1)S(1)}, bf16[64,1280]{1,0:T(8,128)(2,1)S(1)}, u32[]{:S(2)}, u32[]{:S(2)}) collective-permute-start(bf16[64,1280]{1,0:T(8,128)(2,1)S(1)} %get-tuple-element.33.refs_1_), channel_id=1, source_target_pairs={{1,0},{3,1},{5,3},{7,5},{6,7},{4,6},{2,4},{0,2},{9,8},{11,9},{13,1... | collective-permute-start | bytes 491528 | tf_op jit(solution)/shard_map/ppermute | solution.py:397
  13.3 7.1 %collective-permute-start.7 = (bf16[64,1280]{1,0:T(8,128)(2,1)S(1)}, bf16[64,1280]{1,0:T(8,128)(2,1)S(1)}, u32[]{:S(2)}, u32[]{:S(2)}) collective-permute-start(bf16[64,1280]{1,0:T(8,128)(2,1)S(1)} %collective-permute-done.3.refs_5_), channel_id=1, source_target_pairs={{1,0},{3,1},{5,3},{7,5},{6,7},{4,6},{2,4},{0,2},{9,8},{11,9},{13,1... | collective-permute-start | bytes 491528 | tf_op jit(solution)/shard_map/ppermute | solution.py:397
  13.7 7.1 %collective-permute-start.5 = (bf16[64,1280]{1,0:T(8,128)(2,1)S(1)}, bf16[64,1280]{1,0:T(8,128)(2,1)S(1)}, u32[]{:S(2)}, u32[]{:S(2)}) collective-permute-start(bf16[64,1280]{1,0:T(8,128)(2,1)S(1)} %collective-permute-done.1.refs_3_), channel_id=1, source_target_pairs={{0,1},{1,3},{3,5},{5,7},{7,6},{6,4},{4,2},{2,0},{8,9},{9,11},{11,1... | collective-permute-start | bytes 491528 | tf_op jit(solution)/shard_map/ppermute | solution.py:397
  15.3 8.6 %collective-permute-start.6 = (bf16[64,1280]{1,0:T(8,128)(2,1)S(1)}, bf16[64,1280]{1,0:T(8,128)(2,1)S(1)}, u32[]{:S(2)}, u32[]{:S(2)}) collective-permute-start(bf16[64,1280]{1,0:T(8,128)(2,1)S(1)} %collective-permute-done.2.refs_4_), channel_id=1, source_target_pairs={{1,0},{3,1},{5,3},{7,5},{6,7},{4,6},{2,4},{0,2},{9,8},{11,9},{13,1... | collective-permute-start | bytes 491528 | tf_op jit(solution)/shard_map/ppermute | solution.py:397
  15.7 8.6 %collective-permute-start.8 = (bf16[64,1280]{1,0:T(8,128)(2,1)S(1)}, bf16[64,1280]{1,0:T(8,128)(2,1)S(1)}, u32[]{:S(2)}, u32[]{:S(2)}) collective-permute-start(bf16[64,1280]{1,0:T(8,128)(2,1)S(1)} %collective-permute-done.4.refs_6_), channel_id=1, source_target_pairs={{0,1},{1,3},{3,5},{5,7},{7,6},{6,4},{4,2},{2,0},{8,9},{9,11},{11,1... | collective-permute-start | bytes 491528 | tf_op jit(solution)/shard_map/ppermute | solution.py:397
  20.4 7.1 %collective-permute-start.11 = (bf16[64,1280]{1,0:T(8,128)(2,1)S(1)}, bf16[64,1280]{1,0:T(8,128)(2,1)S(1)}, u32[]{:S(2)}, u32[]{:S(2)}) collective-permute-start(bf16[64,1280]{1,0:T(8,128)(2,1)S(1)} %collective-permute-done.7.refs_9_), channel_id=1, source_target_pairs={{1,0},{3,1},{5,3},{7,5},{6,7},{4,6},{2,4},{0,2},{9,8},{11,9},{13,1... | collective-permute-start | bytes 491528 | tf_op jit(solution)/shard_map/ppermute | solution.py:397
  20.8 7.2 %collective-permute-start.9 = (bf16[64,1280]{1,0:T(8,128)(2,1)S(1)}, bf16[64,1280]{1,0:T(8,128)(2,1)S(1)}, u32[]{:S(2)}, u32[]{:S(2)}) collective-permute-start(bf16[64,1280]{1,0:T(8,128)(2,1)S(1)} %collective-permute-done.5.refs_7_), channel_id=1, source_target_pairs={{0,1},{1,3},{3,5},{5,7},{7,6},{6,4},{4,2},{2,0},{8,9},{9,11},{11,1... | collective-permute-start | bytes 491528 | tf_op jit(solution)/shard_map/ppermute | solution.py:397
  23.9 7.1 %collective-permute-start.10 = (bf16[64,1280]{1,0:T(8,128)(2,1)S(1)}, bf16[64,1280]{1,0:T(8,128)(2,1)S(1)}, u32[]{:S(2)}, u32[]{:S(2)}) collective-permute-start(bf16[64,1280]{1,0:T(8,128)(2,1)S(1)} %collective-permute-done.6.refs_8_), channel_id=1, source_target_pairs={{1,0},{3,1},{5,3},{7,5},{6,7},{4,6},{2,4},{0,2},{9,8},{11,9},{13,1... | collective-permute-start | bytes 491528 | tf_op jit(solution)/shard_map/ppermute | solution.py:397
  24.3 10.9 %collective-permute-start.12 = (bf16[64,1280]{1,0:T(8,128)(2,1)S(1)}, bf16[64,1280]{1,0:T(8,128)(2,1)S(1)}, u32[]{:S(2)}, u32[]{:S(2)}) collective-permute-start(bf16[64,1280]{1,0:T(8,128)(2,1)S(1)} %collective-permute-done.8.refs_10_.refs_2_), channel_id=1, source_target_pairs={{0,1},{1,3},{3,5},{5,7},{7,6},{6,4},{4,2},{2,0},{8,9},{9,11},{11,1... | collective-permute-start | bytes 491528 | tf_op jit(solution)/shard_map/ppermute | solution.py:397
  27.5 7.7 %collective-permute-start.13 = (bf16[64,1280]{1,0:T(8,128)(2,1)S(1)}, bf16[64,1280]{1,0:T(8,128)(2,1)S(1)}, u32[]{:S(2)}, u32[]{:S(2)}) collective-permute-start(bf16[64,1280]{1,0:T(8,128)(2,1)S(1)} %collective-permute-done.11.refs_13_.refs_5_), channel_id=1, source_target_pairs={{1,0},{3,1},{5,3},{7,5},{6,7},{4,6},{2,4},{0,2},{9,8},{11,9},{13,1... | collective-permute-start | bytes 491528 | tf_op jit(solution)/shard_map/ppermute | solution.py:397
  31.1 21.4 %collective-permute-start.22 = (bf16[128,1280]{1,0:T(8,128)(2,1)S(1)}, bf16[128,1280]{1,0:T(8,128)(2,1)S(1)}, u32[]{:S(2)}, u32[]{:S(2)}) collective-permute-start(bf16[128,1280]{1,0:T(8,128)(2,1)S(1)} %get-tuple-element.21), channel_id=1, source_target_pairs={{0,1},{1,0},{2,3},{3,2},{4,5},{5,4},{6,7},{7,6},{8,9},{9,8},{10,11... | collective-permute-start | bytes 983048 | tf_op jit(solution)/shard_map/ppermute | solution.py:413
  32.6 20.3 %collective-permute-start.35 = (bf16[160,1280]{1,0:T(8,128)(2,1)S(1)}, bf16[160,1280]{1,0:T(8,128)(2,1)S(1)}, u32[]{:S(2)}, u32[]{:S(2)}) collective-permute-start(bf16[160,1280]{1,0:T(8,128)(2,1)S(1)} %get-tuple-element.30), channel_id=1, source_target_pairs={{0,2},{1,3},{2,4},{3,5},{4,6},{5,7},{6,0},{7,1},{8,14},{9,15},{10,... | collective-permute-start | bytes 1228808 | tf_op jit(solution)/shard_map/ppermute | solution.py:413
  43.8 7.1 %collective-permute-start.18 = (bf16[160,512]{1,0:T(8,128)(2,1)S(1)}, bf16[160,512]{1,0:T(8,128)(2,1)S(1)}, u32[]{:S(2)}, u32[]{:S(2)}) collective-permute-start(bf16[160,512]{1,0:T(8,128)(2,1)S(1)} %get-tuple-element.20.refs_1_), channel_id=1, source_target_pairs={{1,0},{3,1},{5,3},{7,5},{6,7},{4,6},{2,4},{0,2},{9,8},{11,9},{13,1... | collective-permute-start | bytes 491528 | tf_op jit(solution)/shard_map/ppermute | solution.py:397
  44.8 11.1 %collective-permute-start.26 = (bf16[160,512]{1,0:T(8,128)(2,1)S(1)}, bf16[160,512]{1,0:T(8,128)(2,1)S(1)}, u32[]{:S(2)}, u32[]{:S(2)}) collective-permute-start(bf16[160,512]{1,0:T(8,128)(2,1)S(1)} %get-tuple-element.20.refs_1_), channel_id=1, source_target_pairs={{0,1},{1,3},{3,5},{5,7},{7,6},{6,4},{4,2},{2,0},{8,9},{9,11},{11,1... | collective-permute-start | bytes 491528 | tf_op jit(solution)/shard_map/ppermute | solution.py:397
  50.9 7.3 %collective-permute-start.15 = (bf16[160,512]{1,0:T(8,128)(2,1)S(1)}, bf16[160,512]{1,0:T(8,128)(2,1)S(1)}, u32[]{:S(2)}, u32[]{:S(2)}) collective-permute-start(bf16[160,512]{1,0:T(8,128)(2,1)S(1)} %collective-permute-done.14.refs_2_), channel_id=1, source_target_pairs={{0,1},{1,3},{3,5},{5,7},{7,6},{6,4},{4,2},{2,0},{8,9},{9,11},{11,1... | collective-permute-start | bytes 491528 | tf_op jit(solution)/shard_map/ppermute | solution.py:397
  52.4 8.3 %collective-permute-start.19 = (bf16[160,512]{1,0:T(8,128)(2,1)S(1)}, bf16[160,512]{1,0:T(8,128)(2,1)}, u32[]{:S(2)}, u32[]{:S(2)}) collective-permute-start(bf16[160,512]{1,0:T(8,128)(2,1)S(1)} %collective-permute-done.18.refs_5_), channel_id=1, source_target_pairs={{1,0},{3,1},{5,3},{7,5},{6,7},{4,6},{2,4},{0,2},{9,8},{11,9},{13,1... | collective-permute-start | bytes 491528 | tf_op jit(solution)/shard_map/ppermute | solution.py:397
  52.9 18.6 %collective-permute-start.36 = (bf16[160,1280]{1,0:T(8,128)(2,1)S(1)}, bf16[160,1280]{1,0:T(8,128)(2,1)S(1)}, u32[]{:S(2)}, u32[]{:S(2)}) collective-permute-start(bf16[160,1280]{1,0:T(8,128)(2,1)S(1)} %collective-permute-done.35.refs_0_), channel_id=1, source_target_pairs={{0,16},{8,24},{16,0},{24,8},{1,17},{9,25},{17,1},{25,9},{2,18},{10... | collective-permute-start | bytes 1228808 | tf_op jit(solution)/shard_map/ppermute | solution.py:418
  56.2 11.6 %collective-permute-start.23 = (bf16[128,1280]{1,0:T(8,128)(2,1)S(1)}, bf16[128,1280]{1,0:T(8,128)(2,1)S(1)}, u32[]{:S(2)}, u32[]{:S(2)}) collective-permute-start(bf16[128,1280]{1,0:T(8,128)(2,1)S(1)} %after.7.refs_17_.refs_5_), channel_id=1, source_target_pairs={{0,16},{8,24},{16,0},{24,8},{1,17},{9,25},{17,1},{25,9},{2,18},{10... | collective-permute-start | bytes 983048 | tf_op jit(solution)/shard_map/ppermute | solution.py:418
  67.8 8.1 %collective-permute-start.24 = (bf16[128,1280]{1,0:T(8,128)(2,1)S(1)}, bf16[128,1280]{1,0:T(8,128)(2,1)S(1)}, u32[]{:S(2)}, u32[]{:S(2)}) collective-permute-start(bf16[128,1280]{1,0:T(8,128)(2,1)S(1)} %after.7.refs_17_.refs_5_), channel_id=1, source_target_pairs={{0,8},{8,0},{16,24},{24,16},{1,9},{9,1},{17,25},{25,17},{2,10},{10... | collective-permute-start | bytes 983048 | tf_op jit(solution)/shard_map/ppermute | solution.py:418
  67.8 15.5 %collective-permute-start.17 = (bf16[160,512]{1,0:T(8,128)(2,1)S(1)}, bf16[160,512]{1,0:T(8,128)(2,1)S(1)}, u32[]{:S(2)}, u32[]{:S(2)}) collective-permute-start(bf16[160,512]{1,0:T(8,128)(2,1)S(1)} %collective-permute-done.16.refs_10_.refs_2_), channel_id=1, source_target_pairs={{0,1},{1,3},{3,5},{5,7},{7,6},{6,4},{4,2},{2,0},{8,9},{9,11},{11,1... | collective-permute-start | bytes 491528 | tf_op jit(solution)/shard_map/ppermute | solution.py:397
  70.2 6.8 %collective-permute-start.25 = (bf16[128,1280]{1,0:T(8,128)(2,1)S(1)}, bf16[128,1280]{1,0:T(8,128)(2,1)S(1)}, u32[]{:S(2)}, u32[]{:S(2)}) collective-permute-start(bf16[128,1280]{1,0:T(8,128)(2,1)S(1)} %collective-permute-done.23.refs_18_.refs_6_), channel_id=1, source_target_pairs={{0,8},{8,0},{16,24},{24,16},{1,9},{9,1},{17,25},{25,17},{2,10},{10... | collective-permute-start | bytes 983048 | tf_op jit(solution)/shard_map/ppermute | solution.py:418
  71.6 25.5 %collective-permute-start.39 = (bf16[160,1280]{1,0:T(8,128)(2,1)S(1)}, bf16[160,1280]{1,0:T(8,128)(2,1)S(1)}, u32[]{:S(2)}, u32[]{:S(2)}) collective-permute-start(bf16[160,1280]{1,0:T(8,128)(2,1)S(1)} %get-tuple-element.32.refs_7_), channel_id=1, source_target_pairs={{0,1},{1,0},{2,3},{3,2},{4,5},{5,4},{6,7},{7,6},{16,17},{17,16},{1... | collective-permute-start | bytes 1228808 | tf_op jit(solution)/shard_map/ppermute | solution.py:413
  75.0 22.1 %collective-permute-start.38 = (bf16[160,1280]{1,0:T(8,128)(2,1)S(1)}, bf16[160,1280]{1,0:T(8,128)(2,1)S(1)}, u32[]{:S(2)}, u32[]{:S(2)}) collective-permute-start(bf16[160,1280]{1,0:T(8,128)(2,1)S(1)} %broadcast_select_fusion), channel_id=1, source_target_pairs={{0,1},{1,0},{2,3},{3,2},{4,5},{5,4},{6,7},{7,6},{8,9},{9,8},{10,11... | collective-permute-start | bytes 1228808 | tf_op jit(solution)/shard_map/ppermute | solution.py:413
  75.9 15.1 %collective-permute-start.21 = (bf16[160,512]{1,0:T(8,128)(2,1)S(1)}, bf16[160,512]{1,0:T(8,128)(2,1)S(1)}, u32[]{:S(2)}, u32[]{:S(2)}) collective-permute-start(bf16[160,512]{1,0:T(8,128)(2,1)S(1)} %collective-permute-done.20.refs_13_.refs_5_), channel_id=1, source_target_pairs={{1,0},{3,1},{5,3},{7,5},{6,7},{4,6},{2,4},{0,2},{9,8},{11,9},{13,1... | collective-permute-start | bytes 491528 | tf_op jit(solution)/shard_map/ppermute | solution.py:397
  77.0 30.4 %collective-permute-start.37 = (bf16[320,1280]{1,0:T(8,128)(2,1)S(1)}, bf16[320,1280]{1,0:T(8,128)(2,1)S(1)}, u32[]{:S(2)}, u32[]{:S(2)}) collective-permute-start(bf16[320,1280]{1,0:T(8,128)(2,1)S(1)} %pad_maximum_fusion), channel_id=1, source_target_pairs={{0,8},{8,0},{16,24},{24,16},{1,9},{9,1},{17,25},{25,17},{2,10},{10... | collective-permute-start | bytes 2457608 | tf_op jit(solution)/shard_map/ppermute | solution.py:418
  97.2 10.2 %collective-permute-start.40 = (bf16[320,1280]{1,0:T(8,128)(2,1)S(1)}, bf16[320,1280]{1,0:T(8,128)(2,1)S(1)}, u32[]{:S(2)}, u32[]{:S(2)}) collective-permute-start(bf16[320,1280]{1,0:T(8,128)(2,1)S(1)} %after.9.refs_9_), channel_id=1, source_target_pairs={{0,8},{8,0},{16,24},{24,16},{1,9},{9,1},{17,25},{25,17},{2,10},{10... | collective-permute-start | bytes 2457608 | tf_op jit(solution)/shard_map/ppermute | solution.py:418
  97.3 7.2 %collective-permute-start.32 = (bf16[320,128]{1,0:T(8,128)(2,1)S(1)}, bf16[320,128]{1,0:T(8,128)(2,1)S(1)}, u32[]{:S(2)}, u32[]{:S(2)}) collective-permute-start(bf16[320,128]{1,0:T(8,128)(2,1)S(1)} %get-tuple-element.26.refs_1_), channel_id=1, source_target_pairs={{0,2},{1,3},{2,4},{3,5},{4,6},{5,7},{6,0},{7,1},{8,10},{9,11},{10,... | collective-permute-start | bytes 245768 | tf_op jit(solution)/shard_map/ppermute | solution.py:571
  97.3 10.0 %collective-permute-start.33 = (bf16[320,128]{1,0:T(8,128)(2,1)S(1)}, bf16[320,128]{1,0:T(8,128)(2,1)S(1)}, u32[]{:S(2)}, u32[]{:S(2)}) collective-permute-start(bf16[320,128]{1,0:T(8,128)(2,1)S(1)} %get-tuple-element.27), channel_id=1, source_target_pairs={{0,4},{1,5},{2,6},{3,7},{4,0},{5,1},{6,2},{7,3},{8,12},{9,13},{10,... | collective-permute-start | bytes 245768 | tf_op jit(solution)/shard_map/ppermute | solution.py:571
  100.6 6.7 %collective-permute-start.34 = (bf16[320,128]{1,0:T(8,128)(2,1)S(1)}, bf16[320,128]{1,0:T(8,128)(2,1)S(1)}, u32[]{:S(2)}, u32[]{:S(2)}) collective-permute-start(bf16[320,128]{1,0:T(8,128)(2,1)S(1)} %get-tuple-element.28), channel_id=1, source_target_pairs={{0,6},{1,7},{2,0},{3,1},{4,2},{5,3},{6,4},{7,5},{8,14},{9,15},{10,... | collective-permute-start | bytes 245768 | tf_op jit(solution)/shard_map/ppermute | solution.py:571
  (18 other events, 126.5 us)

commit v11 on v10

--- a/solution.py
+++ b/solution.py
@@ -16,7 +16,6 @@
 SET_HEADS = HEADS // OUTER
 SET_CHANNELS = SET_HEADS * HEAD_DIM
 QUAD = 4
-GRANULE = 32
 HANDED = (0, 2, 1, 3)
 FAR = ((1, 0), (3, 0), (2, 0), (0, 1))
 SOONER = tuple(range(1, OUTER))
@@ -257,20 +256,14 @@
     for kind in range(3):
         place = kind * SET_CHANNELS + inner_at * own
         places.append((kind * own, own, pl.multiple_of(place, own)))
-    mine = lax.rem(lax.axis_index("batch"), QUAD)
-    size = weight_refs[3].shape[0]
-    twice = QUAD * (size // GRANULE) - 3 * own // GRANULE
-    for order, step in enumerate(HANDED):
-        which = jnp.bitwise_xor(mine, step)
-        first = quarter_start(which, own)
-        for at in range(size // GRANULE):
-            granule = first + at
-            place = lax.div(granule, own // GRANULE) * SET_CHANNELS + (1 - inner_at) * own
-            place = place + lax.rem(granule, own // GRANULE) * GRANULE
-            if at < twice:
-                place = jnp.where(which == QUAD - 1, 3 * SET_CHANNELS + at * GRANULE, place)
-            low = 3 * own + order * size + at * GRANULE
-            places.append((low, GRANULE, pl.multiple_of(place, GRANULE)))
+    core = lax.rem(lax.axis_index("batch"), 2)
+    size = own // 2
+    for order in range(2):
+        half = core if order == 0 else 1 - core
+        for at in range(3):
+            part = 3 * half + at
+            place = lax.div(part, 2) * SET_CHANNELS + (1 - inner_at) * own + lax.rem(part, 2) * size
+            places.append((3 * own + (3 * order + at) * size, size, pl.multiple_of(place, 16)))
     return places
 
 
@@ -350,15 +343,6 @@
     out_ref[...] = total_ref[...].T.astype(bf16)
 
 
-def quarter_rows(own):
-    return -(-3 * own // (QUAD * GRANULE)) * GRANULE
-
-
-def quarter_start(place, own):
-    part = quarter_rows(own) // GRANULE
-    return jnp.minimum(place * part, 3 * own // GRANULE - part)
-
-
 def ring_of(n):
     inner = n // OUTER
     path = [(0, 0)]
@@ -459,10 +443,9 @@
     halves = whole[: block // 2], whole[block // 2 :]
     chosen = []
     if inner == 2:
-        quarter = quarter_rows(own)
-        start = quarter_start(lax.rem(lax.axis_index("batch"), QUAD), own) * GRANULE
+        core = lax.rem(lax.axis_index("batch"), 2)
         stacked = jnp.concatenate([w_query, w_key, w_value], axis=0)
-        chosen = [lax.dynamic_slice_in_dim(stacked, start, quarter, 0)]
+        chosen = [lax.dynamic_slice_in_dim(stacked, core * (3 * own // 2), 3 * own // 2, 0)]
     pieces = gather(halves, n, chosen)
     stats = pl.pallas_call(
         stats_kernel,
@@ -514,9 +497,9 @@
 
     hidden_pieces = gather(tuple(hidden), n)
     if inner == 2:
-        near = after([chosen], hidden[:1])
-        near.append(swap(near[0], 2))
-        near += [swap(one, 1) for one in near]
+        chosen, far = after([chosen, far], hidden_pieces[2:4])
+        near = [chosen]
+        near.append(swap(near[0], 1))
         weights = [w_query, w_key, w_value] + near
         far = [far, swap(far, 2)]
 

time: 110 us -> 104 us (0.945)
  waiting for transfers between devices: 34.4 us -> 25.3 us
  starting transfers between devices: 46.7 us -> 50.5 us
    ppermute x28, waiting for transfers between devices: 30.1 us -> 21.7 us  [gather(): lax.ppermute(found[half, sign * (step - 1)], 'patch', pairs)]
    ppermute x28, starting transfers between devices: 30.4 us -> 32.9 us  [gather(): lax.ppermute(found[half, sign * (step - 1)], 'patch', pairs)]
    ppermute x3, starting transfers between devices: 3.87 us -> 5.46 us  [on_device(): received.append(lax.ppermute(sent_block, 'patch', pairs))]
    ppermute x3, waiting for transfers between devices: 4.24 us -> 2.85 us  [on_device(): received.append(lax.ppermute(sent_block, 'patch', pairs))]
    ppermute x6 -> x4, starting transfers between devices: 5.12 us -> 4.66 us  [swap(): return lax.ppermute(block, 'batch', pairs)]
  transfers between devices with their start and end apart: 41 -> 39, of which waited for: 17 -> 13; matrix products, arithmetic and copies ran while one was open for 1% -> 2% of each run, Pallas kernels for 21% -> 22%
where the time goes in v11:
time: 104 us
  starting transfers between devices  50.5 us (49%)
  waiting for transfers between devices  25.3 us (24%)
  Pallas kernels  24.9 us (24%)
  other arithmetic  1.72 us (2%)
  local copies, waits for them, and re-layouts  1.13 us (1%)
    ppermute x28, starting transfers between devices, gather(): lax.ppermute(found[half, sign * (step - 1)], 'patch', pairs)  32.9 us
    ppermute x28, waiting for transfers between devices, gather(): lax.ppermute(found[half, sign * (step - 1)], 'patch', pairs)  21.7 us
    pallas_call x1, Pallas kernels, on_device(): pl.pallas_call(functools.partial(conv_kernel, columns), out_shape=[jax.Sh...  7.48 us
    ppermute x4, starting transfers between devices, send(): return lax.ppermute(block, ('batch', 'patch'), pairs)  7.46 us
    pallas_call x1, Pallas kernels, on_device(): pl.pallas_call(functools.partial(project_kernel, 2 * n), out_shape=[jax.S...  6.24 us
    pallas_call x1, Pallas kernels, on_device(): pl.pallas_call(functools.partial(attention_kernel, 2 * n, inner), out_sha...  6.13 us
    ppermute x3, starting transfers between devices, on_device(): received.append(lax.ppermute(sent_block, 'patch', pairs))  5.46 us
    ppermute x4, starting transfers between devices, swap(): return lax.ppermute(block, 'batch', pairs)  4.66 us
  transfers between devices with their start and end apart: 39, of which 13 were waited for; matrix products, arithmetic and copies ran while one was open for 2% of the time, Pallas kernels for 22%

profile of v11, /device:TPU:0, one launch (start us, length us, event | category | flops | bytes accessed | tf_op | source)
XLA Modules:
  0.0 103.8 jit_solution(518705611394003523)
XLA Ops:
  1.1 3.0 %collective-permute-start = (bf16[64,1280]{1,0:T(8,128)(2,1)S(1)}, bf16[64,1280]{1,0:T(8,128)(2,1)S(1)}, u32[]{:S(2)}, u32[]{:S(2)}) collective-permute-start(bf16[64,1280]{1,0:T(8,128)(2,1)S(1)} %get-tuple-element.38.refs_0_), channel_id=1, source_target_pairs={{0,1},{1,3},{3,5},{5,7},{7,6},{6,4},{4,2},{2,0},{8,9},{9,11},{11,1... | collective-permute-start | bytes 491528 | tf_op jit(solution)/shard_map/ppermute | solution.py:381
  4.2 1.9 %collective-permute-start.1 = (bf16[64,1280]{1,0:T(8,128)(2,1)S(1)}, bf16[64,1280]{1,0:T(8,128)(2,1)S(1)}, u32[]{:S(2)}, u32[]{:S(2)}) collective-permute-start(bf16[64,1280]{1,0:T(8,128)(2,1)S(1)} %get-tuple-element.37.refs_1_), channel_id=1, source_target_pairs={{0,1},{1,3},{3,5},{5,7},{7,6},{6,4},{4,2},{2,0},{8,9},{9,11},{11,1... | collective-permute-start | bytes 491528 | tf_op jit(solution)/shard_map/ppermute | solution.py:381
  9.2 2.0 %collective-permute-start.4 = (bf16[64,1280]{1,0:T(8,128)(2,1)S(1)}, bf16[64,1280]{1,0:T(8,128)(2,1)S(1)}, u32[]{:S(2)}, u32[]{:S(2)}) collective-permute-start(bf16[64,1280]{1,0:T(8,128)(2,1)S(1)} %after.5.refs_2_), channel_id=1, source_target_pairs={{0,1},{1,3},{3,5},{5,7},{7,6},{6,4},{4,2},{2,0},{8,9},{9,11},{11,1... | collective-permute-start | bytes 491528 | tf_op jit(solution)/shard_map/ppermute | solution.py:381
  11.2 2.1 %collective-permute-done.3.refs_5_ = bf16[64,1280]{1,0:T(8,128)(2,1)S(1)} collective-permute-done((bf16[64,1280]{1,0:T(8,128)(2,1)S(1)}, bf16[64,1280]{1,0:T(8,128)(2,1)S(1)}, u32[]{:S(2)}, u32[]{:S(2)}) %collective-permute-start.3) | collective-permute-done | bytes 163872 | tf_op jit(solution)/shard_map/ppermute | solution.py:381
  13.7 1.6 %collective-permute-start.5 = (bf16[64,1280]{1,0:T(8,128)(2,1)S(1)}, bf16[64,1280]{1,0:T(8,128)(2,1)S(1)}, u32[]{:S(2)}, u32[]{:S(2)}) collective-permute-start(bf16[64,1280]{1,0:T(8,128)(2,1)S(1)} %collective-permute-done.1.refs_3_), channel_id=1, source_target_pairs={{0,1},{1,3},{3,5},{5,7},{7,6},{6,4},{4,2},{2,0},{8,9},{9,11},{11,1... | collective-permute-start | bytes 491528 | tf_op jit(solution)/shard_map/ppermute | solution.py:381
  15.7 2.1 %collective-permute-start.8 = (bf16[64,1280]{1,0:T(8,128)(2,1)S(1)}, bf16[64,1280]{1,0:T(8,128)(2,1)S(1)}, u32[]{:S(2)}, u32[]{:S(2)}) collective-permute-start(bf16[64,1280]{1,0:T(8,128)(2,1)S(1)} %collective-permute-done.4.refs_6_), channel_id=1, source_target_pairs={{0,1},{1,3},{3,5},{5,7},{7,6},{6,4},{4,2},{2,0},{8,9},{9,11},{11,1... | collective-permute-start | bytes 491528 | tf_op jit(solution)/shard_map/ppermute | solution.py:381
  17.8 2.6 %collective-permute-done.7.refs_9_ = bf16[64,1280]{1,0:T(8,128)(2,1)S(1)} collective-permute-done((bf16[64,1280]{1,0:T(8,128)(2,1)S(1)}, bf16[64,1280]{1,0:T(8,128)(2,1)S(1)}, u32[]{:S(2)}, u32[]{:S(2)}) %collective-permute-start.7) | collective-permute-done | bytes 163872 | tf_op jit(solution)/shard_map/ppermute | solution.py:381
  20.8 1.6 %collective-permute-start.9 = (bf16[64,1280]{1,0:T(8,128)(2,1)S(1)}, bf16[64,1280]{1,0:T(8,128)(2,1)S(1)}, u32[]{:S(2)}, u32[]{:S(2)}) collective-permute-start(bf16[64,1280]{1,0:T(8,128)(2,1)S(1)} %collective-permute-done.5.refs_7_), channel_id=1, source_target_pairs={{0,1},{1,3},{3,5},{5,7},{7,6},{6,4},{4,2},{2,0},{8,9},{9,11},{11,1... | collective-permute-start | bytes 491528 | tf_op jit(solution)/shard_map/ppermute | solution.py:381
  24.3 1.6 %collective-permute-start.12 = (bf16[64,1280]{1,0:T(8,128)(2,1)S(1)}, bf16[64,1280]{1,0:T(8,128)(2,1)S(1)}, u32[]{:S(2)}, u32[]{:S(2)}) collective-permute-start(bf16[64,1280]{1,0:T(8,128)(2,1)S(1)} %collective-permute-done.8.refs_10_.refs_2_), channel_id=1, source_target_pairs={{0,1},{1,3},{3,5},{5,7},{7,6},{6,4},{4,2},{2,0},{8,9},{9,11},{11,1... | collective-permute-start | bytes 491528 | tf_op jit(solution)/shard_map/ppermute | solution.py:381
  25.9 1.6 %collective-permute-done.11.refs_13_.refs_5_ = bf16[64,1280]{1,0:T(8,128)(2,1)S(1)} collective-permute-done((bf16[64,1280]{1,0:T(8,128)(2,1)S(1)}, bf16[64,1280]{1,0:T(8,128)(2,1)S(1)}, u32[]{:S(2)}, u32[]{:S(2)}) %collective-permute-start.11) | collective-permute-done | bytes 163872 | tf_op jit(solution)/shard_map/ppermute | solution.py:381
  28.0 3.0 %collective-permute-done.10.refs_12_.refs_4_ = bf16[64,1280]{1,0:T(8,128)(2,1)S(1)} collective-permute-done((bf16[64,1280]{1,0:T(8,128)(2,1)S(1)}, bf16[64,1280]{1,0:T(8,128)(2,1)S(1)}, u32[]{:S(2)}, u32[]{:S(2)}) %collective-permute-start.10) | collective-permute-done | bytes 163872 | tf_op jit(solution)/shard_map/ppermute | solution.py:381
  32.6 1.6 %collective-permute-start.23 = (bf16[160,1280]{1,0:T(8,128)(2,1)S(1)}, bf16[160,1280]{1,0:T(8,128)(2,1)S(1)}, u32[]{:S(2)}, u32[]{:S(2)}) collective-permute-start(bf16[160,1280]{1,0:T(8,128)(2,1)S(1)} %get-tuple-element.24), channel_id=1, source_target_pairs={{0,2},{1,3},{2,4},{3,5},{4,6},{5,7},{6,0},{7,1},{8,14},{9,15},{10,... | collective-permute-start | bytes 1228808 | tf_op jit(solution)/shard_map/ppermute | solution.py:397
  35.3 7.5 %norm_conv.1 = (bf16[160,512]{1,0:T(8,128)(2,1)S(1)}, bf16[160,512]{1,0:T(8,128)(2,1)S(1)}) custom-call(s32[128]{0:T(128)S(1)} %copy-done.4, bf16[64,1280]{1,0:T(8,128)(2,1)S(1)} %get-tuple-element.38.refs_0_, bf16[64,1280]{1,0:T(8,128)(2,1)S(1)} %get-tuple-element.37.refs_1_, bf16[64,1280]{1,0:T(8,128)(2,1)S(1)} %after.5.refs_2_, ...), custom_call_target="tpu_custom_call" | custom-call | flops 3774873600 | bytes 6307840 | tf_op jit(solution)/shard_map/norm_conv/pallas_call | solution.py:474
  43.8 1.6 %collective-permute-start.24 = (bf16[160,512]{1,0:T(8,128)(2,1)S(1)}, bf16[160,512]{1,0:T(8,128)(2,1)S(1)}, u32[]{:S(2)}, u32[]{:S(2)}) collective-permute-start(bf16[160,512]{1,0:T(8,128)(2,1)S(1)} %get-tuple-element.22.refs_1_), channel_id=1, source_target_pairs={{0,1},{1,3},{3,5},{5,7},{7,6},{6,4},{4,2},{2,0},{8,9},{9,11},{11,1... | collective-permute-start | bytes 491528 | tf_op jit(solution)/shard_map/ppermute | solution.py:381
  45.8 2.3 %collective-permute-done.14.refs_2_ = bf16[160,512]{1,0:T(8,128)(2,1)S(1)} collective-permute-done((bf16[160,512]{1,0:T(8,128)(2,1)S(1)}, bf16[160,512]{1,0:T(8,128)(2,1)S(1)}, u32[]{:S(2)}, u32[]{:S(2)}) %collective-permute-start.14) | collective-permute-done | bytes 163872 | tf_op jit(solution)/shard_map/ppermute | solution.py:381
  48.1 2.1 %collective-permute-start.26 = (bf16[160,512]{1,0:T(8,128)(2,1)S(1)}, bf16[160,512]{1,0:T(8,128)(2,1)S(1)}, u32[]{:S(2)}, u32[]{:S(2)}) collective-permute-start(bf16[160,512]{1,0:T(8,128)(2,1)S(1)} %get-tuple-element.21.refs_0_), channel_id=1, source_target_pairs={{1,0},{3,1},{5,3},{7,5},{6,7},{4,6},{2,4},{0,2},{9,8},{11,9},{13,1... | collective-permute-start | bytes 491528 | tf_op jit(solution)/shard_map/ppermute | solution.py:381
  50.2 4.5 %collective-permute-start.34 = (bf16[160,1280]{1,0:T(8,128)(2,1)S(1)}, bf16[160,1280]{1,0:T(8,128)(2,1)S(1)}, u32[]{:S(2)}, u32[]{:S(2)}) collective-permute-start(bf16[160,1280]{1,0:T(8,128)(2,1)S(1)} %get-tuple-element.34.refs_0_), channel_id=1, source_target_pairs={{0,16},{8,24},{16,0},{24,8},{1,17},{9,25},{17,1},{25,9},{2,18},{10... | collective-permute-start | bytes 1228808 | tf_op jit(solution)/shard_map/ppermute | solution.py:402
  54.7 2.5 %collective-permute-start.15 = (bf16[160,512]{1,0:T(8,128)(2,1)S(1)}, bf16[160,512]{1,0:T(8,128)(2,1)}, u32[]{:S(2)}, u32[]{:S(2)}) collective-permute-start(bf16[160,512]{1,0:T(8,128)(2,1)S(1)} %collective-permute-done.14.refs_2_), channel_id=1, source_target_pairs={{0,1},{1,3},{3,5},{5,7},{7,6},{6,4},{4,2},{2,0},{8,9},{9,11},{11,1... | collective-permute-start | bytes 491528 | tf_op jit(solution)/shard_map/ppermute | solution.py:381
  57.3 2.0 %collective-permute-start.27 = (bf16[160,512]{1,0:T(8,128)(2,1)S(1)}, bf16[160,512]{1,0:T(8,128)(2,1)}, u32[]{:S(2)}, u32[]{:S(2)}) collective-permute-start(bf16[160,512]{1,0:T(8,128)(2,1)S(1)} %collective-permute-done.24.refs_3_), channel_id=1, source_target_pairs={{0,1},{1,3},{3,5},{5,7},{7,6},{6,4},{4,2},{2,0},{8,9},{9,11},{11,1... | collective-permute-start | bytes 491528 | tf_op jit(solution)/shard_map/ppermute | solution.py:381
  59.3 2.6 %collective-permute-done.15.refs_6_ = bf16[160,512]{1,0:T(8,128)(2,1)} collective-permute-done((bf16[160,512]{1,0:T(8,128)(2,1)S(1)}, bf16[160,512]{1,0:T(8,128)(2,1)}, u32[]{:S(2)}, u32[]{:S(2)}) %collective-permute-start.15) | collective-permute-done | bytes 163872 | tf_op jit(solution)/shard_map/ppermute | solution.py:381
  61.9 2.5 %collective-permute-start.16 = (bf16[160,512]{1,0:T(8,128)(2,1)}, bf16[160,512]{1,0:T(8,128)(2,1)S(1)}, u32[]{:S(2)}, u32[]{:S(2)}) collective-permute-start(bf16[160,512]{1,0:T(8,128)(2,1)} %collective-permute-done.15.refs_6_), channel_id=1, source_target_pairs={{0,1},{1,3},{3,5},{5,7},{7,6},{6,4},{4,2},{2,0},{8,9},{9,11},{11,1... | collective-permute-start | bytes 491528 | tf_op jit(solution)/shard_map/ppermute | solution.py:381
  65.4 2.5 %collective-permute-start.29 = (bf16[160,512]{1,0:T(8,128)(2,1)}, bf16[160,512]{1,0:T(8,128)(2,1)S(1)}, u32[]{:S(2)}, u32[]{:S(2)}) collective-permute-start(bf16[160,512]{1,0:T(8,128)(2,1)} %collective-permute-done.27.refs_7_), channel_id=1, source_target_pairs={{0,1},{1,3},{3,5},{5,7},{7,6},{6,4},{4,2},{2,0},{8,9},{9,11},{11,1... | collective-permute-start | bytes 491528 | tf_op jit(solution)/shard_map/ppermute | solution.py:381
  69.4 2.2 %collective-permute-done.20.refs_13_.refs_5_ = bf16[160,512]{1,0:T(8,128)(2,1)S(1)} collective-permute-done((bf16[160,512]{1,0:T(8,128)(2,1)}, bf16[160,512]{1,0:T(8,128)(2,1)S(1)}, u32[]{:S(2)}, u32[]{:S(2)}) %collective-permute-start.20) | collective-permute-done | bytes 163872 | tf_op jit(solution)/shard_map/ppermute | solution.py:381
  71.8 1.8 %collective-permute-start.21 = (bf16[160,512]{1,0:T(8,128)(2,1)S(1)}, bf16[160,512]{1,0:T(8,128)(2,1)S(1)}, u32[]{:S(2)}, u32[]{:S(2)}) collective-permute-start(bf16[160,512]{1,0:T(8,128)(2,1)S(1)} %collective-permute-done.20.refs_13_.refs_5_), channel_id=1, source_target_pairs={{1,0},{3,1},{5,3},{7,5},{6,7},{4,6},{2,4},{0,2},{9,8},{11,9},{13,1... | collective-permute-start | bytes 491528 | tf_op jit(solution)/shard_map/ppermute | solution.py:381
  73.6 2.5 %collective-permute-start.37 = (bf16[160,1280]{1,0:T(8,128)(2,1)S(1)}, bf16[160,1280]{1,0:T(8,128)(2,1)S(1)}, u32[]{:S(2)}, u32[]{:S(2)}) collective-permute-start(bf16[160,1280]{1,0:T(8,128)(2,1)S(1)} %get-tuple-element.36.refs_7_), channel_id=1, source_target_pairs={{0,1},{1,0},{2,3},{3,2},{4,5},{5,4},{6,7},{7,6},{16,17},{17,16},{1... | collective-permute-start | bytes 1228808 | tf_op jit(solution)/shard_map/ppermute | solution.py:397
  76.2 1.8 %collective-permute-start.36 = (bf16[160,1280]{1,0:T(8,128)(2,1)S(1)}, bf16[160,1280]{1,0:T(8,128)(2,1)S(1)}, u32[]{:S(2)}, u32[]{:S(2)}) collective-permute-start(bf16[160,1280]{1,0:T(8,128)(2,1)S(1)} %broadcast_select_fusion), channel_id=1, source_target_pairs={{0,1},{1,0},{2,3},{3,2},{4,5},{5,4},{6,7},{7,6},{8,9},{9,8},{10,11... | collective-permute-start | bytes 1228808 | tf_op jit(solution)/shard_map/ppermute | solution.py:397
  78.2 6.2 %norm_project.1 = (f32[960,1024]{1,0:T(8,128)S(1)}, bf16[1280,128]{1,0:T(8,128)(2,1)S(1)}) custom-call(s32[128]{0:T(128)S(1)} %copy-done.4, bf16[160,512]{1,0:T(8,128)(2,1)S(1)} %get-tuple-element.21.refs_0_, bf16[160,512]{1,0:T(8,128)(2,1)S(1)} %get-tuple-element.22.refs_1_, bf16[160,512]{1,0:T(8,128)(2,1)S(1)} %collective-permute-done.14.refs_2_, ...), custom_call_target="tpu_custom_call" | custom-call | flops 2516582400 | bytes 5079040 | tf_op jit(solution)/shard_map/norm_project/pallas_call | solution.py:507
  84.4 6.1 %attention.1 = (bf16[320,128]{1,0:T(8,128)(2,1)S(1)}, bf16[320,128]{1,0:T(8,128)(2,1)S(1)}, bf16[320,128]{1,0:T(8,128)(2,1)S(1)}, bf16[1280,128]{1,0:T(8,128)(2,...) custom-call(s32[128]{0:T(128)S(1)} %copy-done.4, ...), custom_call_target="tpu_custom_call" | custom-call | flops 1258291200 | bytes 5898240 | tf_op jit(solution)/shard_map/attention/pallas_call | solution.py:531
  94.0 2.9 %collective-permute-start.33 = (bf16[320,128]{1,0:T(8,128)(2,1)S(1)}, bf16[320,128]{1,0:T(8,128)(2,1)S(1)}, u32[]{:S(2)}, u32[]{:S(2)}) collective-permute-start(bf16[320,128]{1,0:T(8,128)(2,1)S(1)} %get-tuple-element.32), channel_id=1, source_target_pairs={{0,6},{1,7},{2,0},{3,1},{4,2},{5,3},{6,4},{7,5},{8,14},{9,15},{10,... | collective-permute-start | bytes 245768 | tf_op jit(solution)/shard_map/ppermute | solution.py:554
  96.9 1.9 %own_attention.1.refs_0_ = bf16[320,128]{1,0:T(8,128)(2,1)S(1)} custom-call(bf16[960,1024]{1,0:T(8,128)(2,1)S(1)} %get-tuple-element.28.made_ref, bf16[5,1024,64]{2,1,0:T(8,128)(2,1)S(1)} %get-tuple-element.29.key_ref), custom_call_target="tpu_custom_call" | custom-call | flops 167772160 | bytes 2621440 | tf_op jit(solution)/shard_map/own_attention/pallas_call | solution.py:555
  98.9 2.8 %collective-permute-done.32.refs_2_ = bf16[320,128]{1,0:T(8,128)(2,1)S(1)} collective-permute-done((bf16[320,128]{1,0:T(8,128)(2,1)S(1)}, bf16[320,128]{1,0:T(8,128)(2,1)S(1)}, u32[]{:S(2)}, u32[]{:S(2)}) %collective-permute-start.32) | collective-permute-done | bytes 81952 | tf_op jit(solution)/shard_map/ppermute | solution.py:554
  101.7 2.1 %project.1 = bf16[128,1280]{1,0:T(8,128)(2,1)} custom-call(bf16[320,128]{1,0:T(8,128)(2,1)S(1)} %own_attention.1.refs_0_, bf16[320,128]{1,0:T(8,128)(2,1)S(1)} %collective-permute-done.31.refs_1_, bf16[320,128]{1,0:T(8,128)(2,1)S(1)} %collective-permute-done.32.refs_2_, bf16[320,128]{1,0:T(8,128)(2,1)S(1)} %collective-permute-done.33.refs_3_, ...), custom_call_target="tpu_custom_call" | custom-call | flops 419430400 | bytes 4259840 | tf_op jit(solution)/shard_map/project/pallas_call | solution.py:572
  (77 shorter events, 18.2 us)
Async XLA Ops:
  1.1 8.1 %collective-permute-start = (bf16[64,1280]{1,0:T(8,128)(2,1)S(1)}, bf16[64,1280]{1,0:T(8,128)(2,1)S(1)}, u32[]{:S(2)}, u32[]{:S(2)}) collective-permute-start(bf16[64,1280]{1,0:T(8,128)(2,1)S(1)} %get-tuple-element.38.refs_0_), channel_id=1, source_target_pairs={{0,1},{1,3},{3,5},{5,7},{7,6},{6,4},{4,2},{2,0},{8,9},{9,11},{11,1... | collective-permute-start | bytes 491528 | tf_op jit(solution)/shard_map/ppermute | solution.py:381
  4.1 11.2 %collective-permute-start.2 = (bf16[64,1280]{1,0:T(8,128)(2,1)S(1)}, bf16[64,1280]{1,0:T(8,128)(2,1)S(1)}, u32[]{:S(2)}, u32[]{:S(2)}) collective-permute-start(bf16[64,1280]{1,0:T(8,128)(2,1)S(1)} %get-tuple-element.38.refs_0_), channel_id=1, source_target_pairs={{1,0},{3,1},{5,3},{7,5},{6,7},{4,6},{2,4},{0,2},{9,8},{11,9},{13,1... | collective-permute-start | bytes 491528 | tf_op jit(solution)/shard_map/ppermute | solution.py:381
  4.2 9.5 %collective-permute-start.1 = (bf16[64,1280]{1,0:T(8,128)(2,1)S(1)}, bf16[64,1280]{1,0:T(8,128)(2,1)S(1)}, u32[]{:S(2)}, u32[]{:S(2)}) collective-permute-start(bf16[64,1280]{1,0:T(8,128)(2,1)S(1)} %get-tuple-element.37.refs_1_), channel_id=1, source_target_pairs={{0,1},{1,3},{3,5},{5,7},{7,6},{6,4},{4,2},{2,0},{8,9},{9,11},{11,1... | collective-permute-start | bytes 491528 | tf_op jit(solution)/shard_map/ppermute | solution.py:381
  6.1 7.1 %collective-permute-start.3 = (bf16[64,1280]{1,0:T(8,128)(2,1)S(1)}, bf16[64,1280]{1,0:T(8,128)(2,1)S(1)}, u32[]{:S(2)}, u32[]{:S(2)}) collective-permute-start(bf16[64,1280]{1,0:T(8,128)(2,1)S(1)} %get-tuple-element.37.refs_1_), channel_id=1, source_target_pairs={{1,0},{3,1},{5,3},{7,5},{6,7},{4,6},{2,4},{0,2},{9,8},{11,9},{13,1... | collective-permute-start | bytes 491528 | tf_op jit(solution)/shard_map/ppermute | solution.py:381
  13.7 7.1 %collective-permute-start.5 = (bf16[64,1280]{1,0:T(8,128)(2,1)S(1)}, bf16[64,1280]{1,0:T(8,128)(2,1)S(1)}, u32[]{:S(2)}, u32[]{:S(2)}) collective-permute-start(bf16[64,1280]{1,0:T(8,128)(2,1)S(1)} %collective-permute-done.1.refs_3_), channel_id=1, source_target_pairs={{0,1},{1,3},{3,5},{5,7},{7,6},{6,4},{4,2},{2,0},{8,9},{9,11},{11,1... | collective-permute-start | bytes 491528 | tf_op jit(solution)/shard_map/ppermute | solution.py:381
  15.3 8.6 %collective-permute-start.6 = (bf16[64,1280]{1,0:T(8,128)(2,1)S(1)}, bf16[64,1280]{1,0:T(8,128)(2,1)S(1)}, u32[]{:S(2)}, u32[]{:S(2)}) collective-permute-start(bf16[64,1280]{1,0:T(8,128)(2,1)S(1)} %collective-permute-done.2.refs_4_), channel_id=1, source_target_pairs={{1,0},{3,1},{5,3},{7,5},{6,7},{4,6},{2,4},{0,2},{9,8},{11,9},{13,1... | collective-permute-start | bytes 491528 | tf_op jit(solution)/shard_map/ppermute | solution.py:381
  15.7 8.6 %collective-permute-start.8 = (bf16[64,1280]{1,0:T(8,128)(2,1)S(1)}, bf16[64,1280]{1,0:T(8,128)(2,1)S(1)}, u32[]{:S(2)}, u32[]{:S(2)}) collective-permute-start(bf16[64,1280]{1,0:T(8,128)(2,1)S(1)} %collective-permute-done.4.refs_6_), channel_id=1, source_target_pairs={{0,1},{1,3},{3,5},{5,7},{7,6},{6,4},{4,2},{2,0},{8,9},{9,11},{11,1... | collective-permute-start | bytes 491528 | tf_op jit(solution)/shard_map/ppermute | solution.py:381
  20.4 7.1 %collective-permute-start.11 = (bf16[64,1280]{1,0:T(8,128)(2,1)S(1)}, bf16[64,1280]{1,0:T(8,128)(2,1)S(1)}, u32[]{:S(2)}, u32[]{:S(2)}) collective-permute-start(bf16[64,1280]{1,0:T(8,128)(2,1)S(1)} %collective-permute-done.7.refs_9_), channel_id=1, source_target_pairs={{1,0},{3,1},{5,3},{7,5},{6,7},{4,6},{2,4},{0,2},{9,8},{11,9},{13,1... | collective-permute-start | bytes 491528 | tf_op jit(solution)/shard_map/ppermute | solution.py:381
  20.8 7.2 %collective-permute-start.9 = (bf16[64,1280]{1,0:T(8,128)(2,1)S(1)}, bf16[64,1280]{1,0:T(8,128)(2,1)S(1)}, u32[]{:S(2)}, u32[]{:S(2)}) collective-permute-start(bf16[64,1280]{1,0:T(8,128)(2,1)S(1)} %collective-permute-done.5.refs_7_), channel_id=1, source_target_pairs={{0,1},{1,3},{3,5},{5,7},{7,6},{6,4},{4,2},{2,0},{8,9},{9,11},{11,1... | collective-permute-start | bytes 491528 | tf_op jit(solution)/shard_map/ppermute | solution.py:381
  23.9 7.1 %collective-permute-start.10 = (bf16[64,1280]{1,0:T(8,128)(2,1)S(1)}, bf16[64,1280]{1,0:T(8,128)(2,1)S(1)}, u32[]{:S(2)}, u32[]{:S(2)}) collective-permute-start(bf16[64,1280]{1,0:T(8,128)(2,1)S(1)} %collective-permute-done.6.refs_8_), channel_id=1, source_target_pairs={{1,0},{3,1},{5,3},{7,5},{6,7},{4,6},{2,4},{0,2},{9,8},{11,9},{13,1... | collective-permute-start | bytes 491528 | tf_op jit(solution)/shard_map/ppermute | solution.py:381
  24.3 10.9 %collective-permute-start.12 = (bf16[64,1280]{1,0:T(8,128)(2,1)S(1)}, bf16[64,1280]{1,0:T(8,128)(2,1)S(1)}, u32[]{:S(2)}, u32[]{:S(2)}) collective-permute-start(bf16[64,1280]{1,0:T(8,128)(2,1)S(1)} %collective-permute-done.8.refs_10_.refs_2_), channel_id=1, source_target_pairs={{0,1},{1,3},{3,5},{5,7},{7,6},{6,4},{4,2},{2,0},{8,9},{9,11},{11,1... | collective-permute-start | bytes 491528 | tf_op jit(solution)/shard_map/ppermute | solution.py:381
  27.5 7.7 %collective-permute-start.13 = (bf16[64,1280]{1,0:T(8,128)(2,1)S(1)}, bf16[64,1280]{1,0:T(8,128)(2,1)S(1)}, u32[]{:S(2)}, u32[]{:S(2)}) collective-permute-start(bf16[64,1280]{1,0:T(8,128)(2,1)S(1)} %collective-permute-done.11.refs_13_.refs_5_), channel_id=1, source_target_pairs={{1,0},{3,1},{5,3},{7,5},{6,7},{4,6},{2,4},{0,2},{9,8},{11,9},{13,1... | collective-permute-start | bytes 491528 | tf_op jit(solution)/shard_map/ppermute | solution.py:381
  31.1 19.1 %collective-permute-start.22 = (bf16[240,1280]{1,0:T(8,128)(2,1)S(1)}, bf16[240,1280]{1,0:T(8,128)(2,1)S(1)}, u32[]{:S(2)}, u32[]{:S(2)}) collective-permute-start(bf16[240,1280]{1,0:T(8,128)(2,1)S(1)} %get-tuple-element.23), channel_id=1, source_target_pairs={{0,1},{1,0},{2,3},{3,2},{4,5},{5,4},{6,7},{7,6},{8,9},{9,8},{10,11... | collective-permute-start | bytes 1843208 | tf_op jit(solution)/shard_map/ppermute | solution.py:397
  32.6 17.6 %collective-permute-start.23 = (bf16[160,1280]{1,0:T(8,128)(2,1)S(1)}, bf16[160,1280]{1,0:T(8,128)(2,1)S(1)}, u32[]{:S(2)}, u32[]{:S(2)}) collective-permute-start(bf16[160,1280]{1,0:T(8,128)(2,1)S(1)} %get-tuple-element.24), channel_id=1, source_target_pairs={{0,2},{1,3},{2,4},{3,5},{4,6},{5,7},{6,0},{7,1},{8,14},{9,15},{10,... | collective-permute-start | bytes 1228808 | tf_op jit(solution)/shard_map/ppermute | solution.py:397
  45.4 11.9 %collective-permute-start.18 = (bf16[160,512]{1,0:T(8,128)(2,1)S(1)}, bf16[160,512]{1,0:T(8,128)(2,1)S(1)}, u32[]{:S(2)}, u32[]{:S(2)}) collective-permute-start(bf16[160,512]{1,0:T(8,128)(2,1)S(1)} %get-tuple-element.22.refs_1_), channel_id=1, source_target_pairs={{1,0},{3,1},{5,3},{7,5},{6,7},{4,6},{2,4},{0,2},{9,8},{11,9},{13,1... | collective-permute-start | bytes 491528 | tf_op jit(solution)/shard_map/ppermute | solution.py:381
  48.1 11.2 %collective-permute-start.26 = (bf16[160,512]{1,0:T(8,128)(2,1)S(1)}, bf16[160,512]{1,0:T(8,128)(2,1)S(1)}, u32[]{:S(2)}, u32[]{:S(2)}) collective-permute-start(bf16[160,512]{1,0:T(8,128)(2,1)S(1)} %get-tuple-element.21.refs_0_), channel_id=1, source_target_pairs={{1,0},{3,1},{5,3},{7,5},{6,7},{4,6},{2,4},{0,2},{9,8},{11,9},{13,1... | collective-permute-start | bytes 491528 | tf_op jit(solution)/shard_map/ppermute | solution.py:381
  50.2 23.4 %collective-permute-start.34 = (bf16[160,1280]{1,0:T(8,128)(2,1)S(1)}, bf16[160,1280]{1,0:T(8,128)(2,1)S(1)}, u32[]{:S(2)}, u32[]{:S(2)}) collective-permute-start(bf16[160,1280]{1,0:T(8,128)(2,1)S(1)} %get-tuple-element.34.refs_0_), channel_id=1, source_target_pairs={{0,16},{8,24},{16,0},{24,8},{1,17},{9,25},{17,1},{25,9},{2,18},{10... | collective-permute-start | bytes 1228808 | tf_op jit(solution)/shard_map/ppermute | solution.py:402
  54.7 7.2 %collective-permute-start.15 = (bf16[160,512]{1,0:T(8,128)(2,1)S(1)}, bf16[160,512]{1,0:T(8,128)(2,1)}, u32[]{:S(2)}, u32[]{:S(2)}) collective-permute-start(bf16[160,512]{1,0:T(8,128)(2,1)S(1)} %collective-permute-done.14.refs_2_), channel_id=1, source_target_pairs={{0,1},{1,3},{3,5},{5,7},{7,6},{6,4},{4,2},{2,0},{8,9},{9,11},{11,1... | collective-permute-start | bytes 491528 | tf_op jit(solution)/shard_map/ppermute | solution.py:381
  57.3 7.2 %collective-permute-start.19 = (bf16[160,512]{1,0:T(8,128)(2,1)S(1)}, bf16[160,512]{1,0:T(8,128)(2,1)}, u32[]{:S(2)}, u32[]{:S(2)}) collective-permute-start(bf16[160,512]{1,0:T(8,128)(2,1)S(1)} %collective-permute-done.18.refs_5_), channel_id=1, source_target_pairs={{1,0},{3,1},{5,3},{7,5},{6,7},{4,6},{2,4},{0,2},{9,8},{11,9},{13,1... | collective-permute-start | bytes 491528 | tf_op jit(solution)/shard_map/ppermute | solution.py:381
  57.3 8.1 %collective-permute-start.27 = (bf16[160,512]{1,0:T(8,128)(2,1)S(1)}, bf16[160,512]{1,0:T(8,128)(2,1)}, u32[]{:S(2)}, u32[]{:S(2)}) collective-permute-start(bf16[160,512]{1,0:T(8,128)(2,1)S(1)} %collective-permute-done.24.refs_3_), channel_id=1, source_target_pairs={{0,1},{1,3},{3,5},{5,7},{7,6},{6,4},{4,2},{2,0},{8,9},{9,11},{11,1... | collective-permute-start | bytes 491528 | tf_op jit(solution)/shard_map/ppermute | solution.py:381
  59.3 8.7 %collective-permute-start.28 = (bf16[160,512]{1,0:T(8,128)(2,1)S(1)}, bf16[160,512]{1,0:T(8,128)(2,1)}, u32[]{:S(2)}, u32[]{:S(2)}) collective-permute-start(bf16[160,512]{1,0:T(8,128)(2,1)S(1)} %collective-permute-done.26.refs_4_), channel_id=1, source_target_pairs={{1,0},{3,1},{5,3},{7,5},{6,7},{4,6},{2,4},{0,2},{9,8},{11,9},{13,1... | collective-permute-start | bytes 491528 | tf_op jit(solution)/shard_map/ppermute | solution.py:381
  61.9 7.5 %collective-permute-start.16 = (bf16[160,512]{1,0:T(8,128)(2,1)}, bf16[160,512]{1,0:T(8,128)(2,1)S(1)}, u32[]{:S(2)}, u32[]{:S(2)}) collective-permute-start(bf16[160,512]{1,0:T(8,128)(2,1)} %collective-permute-done.15.refs_6_), channel_id=1, source_target_pairs={{0,1},{1,3},{3,5},{5,7},{7,6},{6,4},{4,2},{2,0},{8,9},{9,11},{11,1... | collective-permute-start | bytes 491528 | tf_op jit(solution)/shard_map/ppermute | solution.py:381
  69.4 8.7 %collective-permute-start.25 = (bf16[240,1280]{1,0:T(8,128)(2,1)S(1)}, bf16[240,1280]{1,0:T(8,128)(2,1)S(1)}, u32[]{:S(2)}, u32[]{:S(2)}) collective-permute-start(bf16[240,1280]{1,0:T(8,128)(2,1)S(1)} %get-tuple-element.25.refs_17_.refs_5_), channel_id=1, source_target_pairs={{0,8},{8,0},{16,24},{24,16},{1,9},{9,1},{17,25},{25,17},{2,10},{10... | collective-permute-start | bytes 1843208 | tf_op jit(solution)/shard_map/ppermute | solution.py:402
  71.6 12.9 %collective-permute-start.17 = (bf16[160,512]{1,0:T(8,128)(2,1)S(1)}, bf16[160,512]{1,0:T(8,128)(2,1)S(1)}, u32[]{:S(2)}, u32[]{:S(2)}) collective-permute-start(bf16[160,512]{1,0:T(8,128)(2,1)S(1)} %collective-permute-done.16.refs_10_.refs_2_), channel_id=1, source_target_pairs={{0,1},{1,3},{3,5},{5,7},{7,6},{6,4},{4,2},{2,0},{8,9},{9,11},{11,1... | collective-permute-start | bytes 491528 | tf_op jit(solution)/shard_map/ppermute | solution.py:381
  71.8 12.6 %collective-permute-start.21 = (bf16[160,512]{1,0:T(8,128)(2,1)S(1)}, bf16[160,512]{1,0:T(8,128)(2,1)S(1)}, u32[]{:S(2)}, u32[]{:S(2)}) collective-permute-start(bf16[160,512]{1,0:T(8,128)(2,1)S(1)} %collective-permute-done.20.refs_13_.refs_5_), channel_id=1, source_target_pairs={{1,0},{3,1},{5,3},{7,5},{6,7},{4,6},{2,4},{0,2},{9,8},{11,9},{13,1... | collective-permute-start | bytes 491528 | tf_op jit(solution)/shard_map/ppermute | solution.py:381
  73.6 17.0 %collective-permute-start.37 = (bf16[160,1280]{1,0:T(8,128)(2,1)S(1)}, bf16[160,1280]{1,0:T(8,128)(2,1)S(1)}, u32[]{:S(2)}, u32[]{:S(2)}) collective-permute-start(bf16[160,1280]{1,0:T(8,128)(2,1)S(1)} %get-tuple-element.36.refs_7_), channel_id=1, source_target_pairs={{0,1},{1,0},{2,3},{3,2},{4,5},{5,4},{6,7},{7,6},{16,17},{17,16},{1... | collective-permute-start | bytes 1228808 | tf_op jit(solution)/shard_map/ppermute | solution.py:397
  76.2 15.1 %collective-permute-start.36 = (bf16[160,1280]{1,0:T(8,128)(2,1)S(1)}, bf16[160,1280]{1,0:T(8,128)(2,1)S(1)}, u32[]{:S(2)}, u32[]{:S(2)}) collective-permute-start(bf16[160,1280]{1,0:T(8,128)(2,1)S(1)} %broadcast_select_fusion), channel_id=1, source_target_pairs={{0,1},{1,0},{2,3},{3,2},{4,5},{5,4},{6,7},{7,6},{8,9},{9,8},{10,11... | collective-permute-start | bytes 1228808 | tf_op jit(solution)/shard_map/ppermute | solution.py:397
  78.1 23.6 %collective-permute-start.35 = (bf16[320,1280]{1,0:T(8,128)(2,1)S(1)}, bf16[320,1280]{1,0:T(8,128)(2,1)S(1)}, u32[]{:S(2)}, u32[]{:S(2)}) collective-permute-start(bf16[320,1280]{1,0:T(8,128)(2,1)S(1)} %pad_maximum_fusion), channel_id=1, source_target_pairs={{0,8},{8,0},{16,24},{24,16},{1,9},{9,1},{17,25},{25,17},{2,10},{10... | collective-permute-start | bytes 2457608 | tf_op jit(solution)/shard_map/ppermute | solution.py:402
  91.4 10.4 %collective-permute-start.38 = (bf16[320,1280]{1,0:T(8,128)(2,1)S(1)}, bf16[320,1280]{1,0:T(8,128)(2,1)S(1)}, u32[]{:S(2)}, u32[]{:S(2)}) collective-permute-start(bf16[320,1280]{1,0:T(8,128)(2,1)S(1)} %after.9.refs_9_), channel_id=1, source_target_pairs={{0,8},{8,0},{16,24},{24,16},{1,9},{9,1},{17,25},{25,17},{2,10},{10... | collective-permute-start | bytes 2457608 | tf_op jit(solution)/shard_map/ppermute | solution.py:402
  91.4 7.4 %collective-permute-start.31 = (bf16[320,128]{1,0:T(8,128)(2,1)S(1)}, bf16[320,128]{1,0:T(8,128)(2,1)S(1)}, u32[]{:S(2)}, u32[]{:S(2)}) collective-permute-start(bf16[320,128]{1,0:T(8,128)(2,1)S(1)} %get-tuple-element.30.refs_1_), channel_id=1, source_target_pairs={{0,2},{1,3},{2,4},{3,5},{4,6},{5,7},{6,0},{7,1},{8,10},{9,11},{10,... | collective-permute-start | bytes 245768 | tf_op jit(solution)/shard_map/ppermute | solution.py:554
  92.8 8.9 %collective-permute-start.32 = (bf16[320,128]{1,0:T(8,128)(2,1)S(1)}, bf16[320,128]{1,0:T(8,128)(2,1)S(1)}, u32[]{:S(2)}, u32[]{:S(2)}) collective-permute-start(bf16[320,128]{1,0:T(8,128)(2,1)S(1)} %get-tuple-element.31), channel_id=1, source_target_pairs={{0,4},{1,5},{2,6},{3,7},{4,0},{5,1},{6,2},{7,3},{8,12},{9,13},{10,... | collective-permute-start | bytes 245768 | tf_op jit(solution)/shard_map/ppermute | solution.py:554
  94.0 7.7 %collective-permute-start.33 = (bf16[320,128]{1,0:T(8,128)(2,1)S(1)}, bf16[320,128]{1,0:T(8,128)(2,1)S(1)}, u32[]{:S(2)}, u32[]{:S(2)}) collective-permute-start(bf16[320,128]{1,0:T(8,128)(2,1)S(1)} %get-tuple-element.32), channel_id=1, source_target_pairs={{0,6},{1,7},{2,0},{3,1},{4,2},{5,3},{6,4},{7,5},{8,14},{9,15},{10,... | collective-permute-start | bytes 245768 | tf_op jit(solution)/shard_map/ppermute | solution.py:554
  (14 other events, 107.9 us)

commit v12 on v11

--- a/solution.py
+++ b/solution.py
@@ -21,6 +21,7 @@
 SOONER = tuple(range(1, OUTER))
 WIDE = 256
 EPSILON = 1e-05
+LATE = 6
 CHUNK = 16
 MEBI = 1024 * 1024
 
@@ -77,14 +78,13 @@
 
 
 def conv_kernel(columns, sources_ref, *refs):
-    count = len(refs) - 7
+    count = len(refs) - 6
     pieces = refs[:count]
     stats_ref, kernel_ref, bias_ref = refs[count : count + 3]
-    out_refs = refs[count + 3 : count + 5]
-    act_ref, kept_ref = refs[count + 5 :]
+    out_ref, act_ref, kept_ref = refs[count + 3 :]
     block = pieces[0].shape[0]
     positions = block * count
-    own = out_refs[0].shape[0]
+    own = out_ref.shape[0]
     me = lax.axis_index("patch")
     steps = block // CHUNK
     starts = [
@@ -101,7 +101,7 @@
         return exact(exact(per_channel, member) / SPAN, member, NT)
 
     pivot = stats_ref[0:1, :]
-    first, second = add_moments(pieces[-2:], pivot, stats_ref[8:16, :], stats_ref[16:24, :])
+    first, second = add_moments(pieces[-LATE:], pivot, stats_ref[8:16, :], stats_ref[16:24, :])
     above = jnp.sum(first, axis=0, keepdims=True) / positions
     within = jnp.sum(second, axis=0, keepdims=True) / positions - above * above
     mean = pivot + above
@@ -134,8 +134,16 @@
         start = pl.multiple_of(starts[index], 2 * block)
         kept_ref[:, pl.ds(start, 2 * block)] = dot(choose, pair, NT)
 
-    wide = WIDE
-    column = lax.broadcasted_iota(jnp.int32, (own, wide), 1) % columns
+    convolve(columns, 0, act_ref, kept_ref, kernel_ref, bias_ref, out_ref)
+
+
+def second_conv_kernel(columns, act_ref, kept_ref, kernel_ref, bias_ref, out_ref):
+    convolve(columns, out_ref.shape[1], act_ref, kept_ref, kernel_ref, bias_ref, out_ref)
+
+
+def convolve(columns, start, act_ref, kept_ref, kernel_ref, bias_ref, out_ref):
+    own = out_ref.shape[0]
+    column = lax.broadcasted_iota(jnp.int32, (own, WIDE), 1) % columns
     square = (own, own)
     bias = jnp.where(
         lax.broadcasted_iota(jnp.int32, square, 0) == lax.broadcasted_iota(jnp.int32, square, 1),
@@ -143,17 +151,17 @@
         0.0,
     )
     bias = jnp.sum(bias, axis=1, keepdims=True)
-    for at in range(0, positions, wide):
-        taps = dot(kernel_ref[0], act_ref[at : at + wide, :], NT)
+    for low in range(0, out_ref.shape[1], WIDE):
+        at = start + low
+        taps = dot(kernel_ref[0], act_ref[at : at + WIDE, :], NT)
         for shift in (1, 2):
-            low = at + shift * columns
-            taps = taps + dot(kernel_ref[shift], act_ref[low : low + wide, :], NT)
+            first = at + shift * columns
+            taps = taps + dot(kernel_ref[shift], act_ref[first : first + WIDE, :], NT)
         before = jnp.where(column > 0, pltpu.roll(taps[0:own], 1, 1), 0.0)
-        after_ = jnp.where(column < columns - 1, pltpu.roll(taps[2 * own :], wide - 1, 1), 0.0)
+        after_ = jnp.where(column < columns - 1, pltpu.roll(taps[2 * own :], WIDE - 1, 1), 0.0)
         convolved = taps[own : 2 * own] + before + after_
-        hidden = kept_ref[:, at : at + wide] + convolved + bias
-        which, low = divmod(at, positions // 2)
-        out_refs[which][:, low : low + wide] = hidden.astype(bf16)
+        hidden = kept_ref[:, at : at + WIDE] + convolved + bias
+        out_ref[:, low : low + WIDE] = hidden.astype(bf16)
 
 
 def window_of(own):
@@ -190,15 +198,33 @@
     return jnp.where(me < n // 2, low, high)
 
 
+def early_kernel(n, *refs):
+    pieces, outs = refs[:-2], refs[-2:]
+    me = lax.axis_index("patch")
+    own, part = pieces[0].shape
+    for at in range(0, len(pieces), 2):
+        pair = pieces[at : at + 2]
+        rows = slice(at // 2 * own, (at // 2 + 1) * own)
+        for half, normed in enumerate(norm_pair(pair)):
+            outs[0][rows, half * part : (half + 1) * part] = normed
+        outs[1][rows, :] = own_lanes(pair, me, n)
+
+
 def project_kernel(count, sources_ref, *refs):
-    pieces = refs[: count - 2]
-    weight_refs = refs[count - 2 : -3]
+    early_ref, some_ref = refs[:2]
+    pieces = refs[2:LATE]
+    weight_refs = refs[LATE:-3]
     sums_ref, kept_ref, normed_ref = refs[-3:]
     own, part = pieces[0].shape
     me = lax.axis_index("patch")
     for at in range(0, count - 2, 2):
-        pair = pieces[at : at + 2]
         rows = pl.ds(pl.multiple_of(sources_ref[me * count + at] * own, own), own)
+        if at < count - LATE:
+            there = slice(at // 2 * own, (at // 2 + 1) * own)
+            normed_ref[rows, :] = early_ref[there, :]
+            kept_ref[rows, :] = some_ref[there, :]
+            continue
+        pair = pieces[at - count + LATE :][:2]
         for half, normed in enumerate(norm_pair(pair)):
             normed_ref[rows, half * part : (half + 1) * part] = normed
         kept_ref[rows, :] = own_lanes(pair, me, count // 2)
@@ -367,7 +393,7 @@
     return table
 
 
-def gather(halves, n, beside=()):
+def gather(halves, n, beside):
     ring = ring_of(n)
     forward = [(ring[at], ring[(at + 1) % n]) for at in range(n)]
     backward = [(target, start) for start, target in forward]
@@ -381,10 +407,16 @@
                 found[half, sign * step] = lax.ppermute(
                     found[half, sign * (step - 1)], "patch", pairs
                 )
-        if step == 1 and beside:
-            (found[0, -1],) = after([found[0, -1]], beside)
+        others = beside(step, found)
+        if others:
+            (found[0, -step],) = after([found[0, -step]], others)
     found[0, far] = found[0, -far]
-    return [found[half, away] for away in pieces_of(n) for half in (0, 1)]
+    return in_order(found, n)
+
+
+def in_order(found, n):
+    places = [(half, away) for away in pieces_of(n) for half in (0, 1)]
+    return [found[place] for place in places if place in found]
 
 
 def send(block, shifts):
@@ -446,20 +478,33 @@
         core = lax.rem(lax.axis_index("batch"), 2)
         stacked = jnp.concatenate([w_query, w_key, w_value], axis=0)
         chosen = [lax.dynamic_slice_in_dim(stacked, core * (3 * own // 2), 3 * own // 2, 0)]
-    pieces = gather(halves, n, chosen)
-    stats = pl.pallas_call(
-        stats_kernel,
-        out_shape=jax.ShapeDtypeStruct((24, channels), f32),
-        in_specs=[vmem] * (2 * n - 2),
-        out_specs=vmem,
-        compiler_params=pltpu.CompilerParams(vmem_limit_bytes=2 * MEBI),
-        cost_estimate=pl.CostEstimate(
-            flops=6 * positions * channels,
-            bytes_accessed=2 * positions * channels,
-            transcendentals=0,
-        ),
-        name="stats",
-    )(*pieces[:-2])
+    far_step = n // 2
+    made_beside = []
+
+    def beside_first(step, found):
+        if step == 1:
+            return chosen
+        if step != far_step - 1:
+            return []
+        made_beside.append(
+            pl.pallas_call(
+                stats_kernel,
+                out_shape=jax.ShapeDtypeStruct((24, channels), f32),
+                in_specs=[vmem] * (2 * n - LATE),
+                out_specs=vmem,
+                compiler_params=pltpu.CompilerParams(vmem_limit_bytes=2 * MEBI),
+                cost_estimate=pl.CostEstimate(
+                    flops=6 * positions * channels,
+                    bytes_accessed=2 * positions * channels,
+                    transcendentals=0,
+                ),
+                name="stats",
+            )(*in_order(found, n)[: 2 * n - LATE])
+        )
+        return made_beside[-1:]
+
+    pieces = gather(halves, n, beside_first)
+    stats = made_beside[0]
     if inner == 2:
         chosen, out_own = after(chosen + [w_out], pieces[-6:-2])
         chosen = send(chosen, [(0, 1)])
@@ -471,31 +516,62 @@
         weights = [weights.reshape(3 * SET_CHANNELS, channels)]
         out_weights = [lax.all_gather(w_out, "patch", axis=0, tiled=True)]
 
-    hidden = pl.pallas_call(
+    kernel = conv_weight.reshape(3, 3 * own, channels)
+    bias = channel_bias.reshape(1, own)
+    half_hidden = jax.ShapeDtypeStruct((own, positions // 2), bf16)
+    flops = 9 * positions * channels * own
+    first_hidden, act, residual = pl.pallas_call(
         functools.partial(conv_kernel, columns),
-        out_shape=[jax.ShapeDtypeStruct((own, positions // 2), bf16)] * 2,
+        out_shape=[
+            half_hidden,
+            jax.ShapeDtypeStruct((positions + 2 * columns, channels), bf16),
+            jax.ShapeDtypeStruct((own, positions), f32),
+        ],
         in_specs=[smem] + [vmem] * (2 * n + 3),
-        out_specs=[vmem] * 2,
-        scratch_shapes=[
-            pltpu.VMEM((positions + 2 * columns, channels), bf16),
-            pltpu.VMEM((own, positions), f32),
-        ],
+        out_specs=[vmem] * 3,
         compiler_params=pltpu.CompilerParams(vmem_limit_bytes=20 * MEBI),
         cost_estimate=pl.CostEstimate(
-            flops=2 * 9 * positions * channels * own,
+            flops=flops,
             bytes_accessed=2 * (positions * channels + 9 * channels * own),
             transcendentals=positions * channels,
         ),
         name="norm_conv",
-    )(
-        sources,
-        *pieces,
-        stats,
-        conv_weight.reshape(3, 3 * own, channels),
-        channel_bias.reshape(1, own),
-    )
-
-    hidden_pieces = gather(tuple(hidden), n)
+    )(sources, *pieces, stats, kernel, bias)
+    second_hidden = pl.pallas_call(
+        functools.partial(second_conv_kernel, columns),
+        out_shape=half_hidden,
+        in_specs=[vmem] * 4,
+        out_specs=vmem,
+        compiler_params=pltpu.CompilerParams(vmem_limit_bytes=16 * MEBI),
+        cost_estimate=pl.CostEstimate(flops=flops, bytes_accessed=flops // 1000, transcendentals=0),
+        name="second_conv",
+    )(act, residual, kernel, bias)
+
+    def beside_second(step, found):
+        if step != far_step - 1:
+            return []
+        count = n - LATE // 2
+        made_beside.append(
+            pl.pallas_call(
+                functools.partial(early_kernel, n),
+                out_shape=[
+                    jax.ShapeDtypeStruct((count * own, positions), bf16),
+                    jax.ShapeDtypeStruct((count * own, block), bf16),
+                ],
+                in_specs=[vmem] * (2 * count),
+                out_specs=[vmem] * 2,
+                compiler_params=pltpu.CompilerParams(vmem_limit_bytes=8 * MEBI),
+                cost_estimate=pl.CostEstimate(
+                    flops=8 * positions * channels,
+                    bytes_accessed=4 * positions * channels,
+                    transcendentals=0,
+                ),
+                name="early_norm",
+            )(*in_order(found, n)[: 2 * count])
+        )
+        return made_beside[-1][:1]
+
+    hidden_pieces = gather((first_hidden, second_hidden), n, beside_second)
     if inner == 2:
         chosen, far = after([chosen, far], hidden_pieces[2:4])
         near = [chosen]
@@ -510,7 +586,7 @@
             jax.ShapeDtypeStruct((made_rows, positions), f32),
             jax.ShapeDtypeStruct((channels, block), bf16),
         ],
-        in_specs=[smem] + [vmem] * (2 * n - 2 + len(weights)),
+        in_specs=[smem] + [vmem] * (LATE + len(weights)),
         out_specs=[vmem] * 2,
         scratch_shapes=[pltpu.VMEM((channels, positions), bf16)],
         compiler_params=pltpu.CompilerParams(vmem_limit_bytes=20 * MEBI),
@@ -520,7 +596,7 @@
             transcendentals=0,
         ),
         name="norm_project",
-    )(sources, *hidden_pieces[:-2], *weights)
+    )(sources, *made_beside[-1], *hidden_pieces[-LATE:-2], *weights)
     if inner == 2:
         far = after(far, hidden_pieces[-6:-2])
         place = lax.rem(lax.axis_index("batch"), QUAD)

time: 104 us -> 104 us (level)
  starting transfers between devices: 50.5 us -> 48.4 us
  waiting for transfers between devices: 25.3 us -> 26.6 us
  Pallas kernels: 24.9 us -> 26.1 us
    pallas_call x2 -> x4, Pallas kernels: 8.47 us -> 11.2 us  [the longest x1 5.78 us: on_device(): pl.pallas_call(functools.partial(conv_kernel, columns), out_shape=[half_h...]
    ppermute x3, starting transfers between devices: 5.46 us -> 3.87 us  [on_device(): received.append(lax.ppermute(sent_block, 'patch', pairs))]
    pallas_call x1, Pallas kernels: 6.24 us -> 4.68 us  [on_device(): pl.pallas_call(functools.partial(project_kernel, 2 * n), out_shape=[jax.S...]
    ppermute x4, waiting for transfers between devices: 0.71 us -> 2.19 us  [send(): return lax.ppermute(block, ('batch', 'patch'), pairs)]
    ppermute x28, waiting for transfers between devices: 21.7 us -> 20.4 us  [gather(): lax.ppermute(found[half, sign * (step - 1)], 'patch', pairs)]
    ppermute x3, waiting for transfers between devices: 2.85 us -> 3.98 us  [on_device(): received.append(lax.ppermute(sent_block, 'patch', pairs))]
  transfers between devices with their start and end apart: 39 -> 39, of which waited for: 13 -> 16; matrix products, arithmetic and copies ran while one was open for 2% -> 2% of each run, Pallas kernels for 22% -> 23%
where the time goes in v12:
time: 104 us
  starting transfers between devices  48.4 us (47%)
  waiting for transfers between devices  26.6 us (26%)
  Pallas kernels  26.1 us (25%)
  other arithmetic  1.72 us (2%)
  local copies, waits for them, and re-layouts  1.08 us (1%)
    ppermute x28, starting transfers between devices, gather(): lax.ppermute(found[half, sign * (step - 1)], 'patch', pairs)  31.9 us
    ppermute x28, waiting for transfers between devices, gather(): lax.ppermute(found[half, sign * (step - 1)], 'patch', pairs)  20.4 us
    ppermute x4, starting transfers between devices, send(): return lax.ppermute(block, ('batch', 'patch'), pairs)  7.46 us
    pallas_call x1, Pallas kernels, on_device(): pl.pallas_call(functools.partial(attention_kernel, 2 * n, inner), out_sha...  6.14 us
    pallas_call x1, Pallas kernels, on_device(): pl.pallas_call(functools.partial(conv_kernel, columns), out_shape=[half_h...  5.78 us
    ppermute x4, starting transfers between devices, swap(): return lax.ppermute(block, 'batch', pairs)  5.13 us
    pallas_call x1, Pallas kernels, on_device(): pl.pallas_call(functools.partial(project_kernel, 2 * n), out_shape=[jax.S...  4.68 us
    ppermute x3, waiting for transfers between devices, on_device(): received.append(lax.ppermute(sent_block, 'patch', pairs))  3.98 us
  transfers between devices with their start and end apart: 39, of which 16 were waited for; matrix products, arithmetic and copies ran while one was open for 2% of the time, Pallas kernels for 23%

profile of v12, /device:TPU:0, one launch (start us, length us, event | category | flops | bytes accessed | tf_op | source)
XLA Modules:
  0.0 104.2 jit_solution(1465858898179306528)
XLA Ops:
  1.0 3.0 %collective-permute-start = (bf16[64,1280]{1,0:T(8,128)(2,1)S(1)}, bf16[64,1280]{1,0:T(8,128)(2,1)S(1)}, u32[]{:S(2)}, u32[]{:S(2)}) collective-permute-start(bf16[64,1280]{1,0:T(8,128)(2,1)S(1)} %get-tuple-element.44.refs_0_), channel_id=1, source_target_pairs={{0,1},{1,3},{3,5},{5,7},{7,6},{6,4},{4,2},{2,0},{8,9},{9,11},{11,1... | collective-permute-start | bytes 491528 | tf_op jit(solution)/shard_map/ppermute | solution.py:407
  4.2 1.9 %collective-permute-start.1 = (bf16[64,1280]{1,0:T(8,128)(2,1)S(1)}, bf16[64,1280]{1,0:T(8,128)(2,1)S(1)}, u32[]{:S(2)}, u32[]{:S(2)}) collective-permute-start(bf16[64,1280]{1,0:T(8,128)(2,1)S(1)} %get-tuple-element.43.refs_1_), channel_id=1, source_target_pairs={{0,1},{1,3},{3,5},{5,7},{7,6},{6,4},{4,2},{2,0},{8,9},{9,11},{11,1... | collective-permute-start | bytes 491528 | tf_op jit(solution)/shard_map/ppermute | solution.py:407
  9.1 2.0 %collective-permute-start.4 = (bf16[64,1280]{1,0:T(8,128)(2,1)S(1)}, bf16[64,1280]{1,0:T(8,128)(2,1)S(1)}, u32[]{:S(2)}, u32[]{:S(2)}) collective-permute-start(bf16[64,1280]{1,0:T(8,128)(2,1)S(1)} %after.7.refs_2_), channel_id=1, source_target_pairs={{0,1},{1,3},{3,5},{5,7},{7,6},{6,4},{4,2},{2,0},{8,9},{9,11},{11,1... | collective-permute-start | bytes 491528 | tf_op jit(solution)/shard_map/ppermute | solution.py:407
  11.1 2.1 %collective-permute-done.3.refs_5_ = bf16[64,1280]{1,0:T(8,128)(2,1)S(1)} collective-permute-done((bf16[64,1280]{1,0:T(8,128)(2,1)S(1)}, bf16[64,1280]{1,0:T(8,128)(2,1)S(1)}, u32[]{:S(2)}, u32[]{:S(2)}) %collective-permute-start.3) | collective-permute-done | bytes 163872 | tf_op jit(solution)/shard_map/ppermute | solution.py:407
  13.6 1.6 %collective-permute-start.5 = (bf16[64,1280]{1,0:T(8,128)(2,1)S(1)}, bf16[64,1280]{1,0:T(8,128)(2,1)S(1)}, u32[]{:S(2)}, u32[]{:S(2)}) collective-permute-start(bf16[64,1280]{1,0:T(8,128)(2,1)S(1)} %collective-permute-done.1.refs_3_), channel_id=1, source_target_pairs={{0,1},{1,3},{3,5},{5,7},{7,6},{6,4},{4,2},{2,0},{8,9},{9,11},{11,1... | collective-permute-start | bytes 491528 | tf_op jit(solution)/shard_map/ppermute | solution.py:407
  15.7 2.1 %collective-permute-start.8 = (bf16[64,1280]{1,0:T(8,128)(2,1)S(1)}, bf16[64,1280]{1,0:T(8,128)(2,1)S(1)}, u32[]{:S(2)}, u32[]{:S(2)}) collective-permute-start(bf16[64,1280]{1,0:T(8,128)(2,1)S(1)} %collective-permute-done.4.refs_6_), channel_id=1, source_target_pairs={{0,1},{1,3},{3,5},{5,7},{7,6},{6,4},{4,2},{2,0},{8,9},{9,11},{11,1... | collective-permute-start | bytes 491528 | tf_op jit(solution)/shard_map/ppermute | solution.py:407
  17.7 2.6 %collective-permute-done.7.refs_9_ = bf16[64,1280]{1,0:T(8,128)(2,1)S(1)} collective-permute-done((bf16[64,1280]{1,0:T(8,128)(2,1)S(1)}, bf16[64,1280]{1,0:T(8,128)(2,1)S(1)}, u32[]{:S(2)}, u32[]{:S(2)}) %collective-permute-start.7) | collective-permute-done | bytes 163872 | tf_op jit(solution)/shard_map/ppermute | solution.py:407
  20.8 1.6 %collective-permute-start.9 = (bf16[64,1280]{1,0:T(8,128)(2,1)S(1)}, bf16[64,1280]{1,0:T(8,128)(2,1)S(1)}, u32[]{:S(2)}, u32[]{:S(2)}) collective-permute-start(bf16[64,1280]{1,0:T(8,128)(2,1)S(1)} %collective-permute-done.5.refs_7_), channel_id=1, source_target_pairs={{0,1},{1,3},{3,5},{5,7},{7,6},{6,4},{4,2},{2,0},{8,9},{9,11},{11,1... | collective-permute-start | bytes 491528 | tf_op jit(solution)/shard_map/ppermute | solution.py:407
  25.1 1.7 %collective-permute-start.12 = (bf16[64,1280]{1,0:T(8,128)(2,1)S(1)}, bf16[64,1280]{1,0:T(8,128)(2,1)S(1)}, u32[]{:S(2)}, u32[]{:S(2)}) collective-permute-start(bf16[64,1280]{1,0:T(8,128)(2,1)S(1)} %after.8.refs_10_.refs_2_), channel_id=1, source_target_pairs={{0,1},{1,3},{3,5},{5,7},{7,6},{6,4},{4,2},{2,0},{8,9},{9,11},{11,1... | collective-permute-start | bytes 491528 | tf_op jit(solution)/shard_map/ppermute | solution.py:407
  27.9 3.1 %collective-permute-done.10.refs_12_.refs_4_ = bf16[64,1280]{1,0:T(8,128)(2,1)S(1)} collective-permute-done((bf16[64,1280]{1,0:T(8,128)(2,1)S(1)}, bf16[64,1280]{1,0:T(8,128)(2,1)S(1)}, u32[]{:S(2)}, u32[]{:S(2)}) %collective-permute-start.10) | collective-permute-done | bytes 163872 | tf_op jit(solution)/shard_map/ppermute | solution.py:407
  34.6 5.8 %norm_conv.1 = (bf16[160,512]{1,0:T(8,128)(2,1)S(1)}, bf16[1152,1280]{1,0:T(8,128)(2,1)S(1)}, f32[160,1024]{1,0:T(8,128)S(1)}) custom-call(s32[128]{0:T(128)S(1)} %copy-done.6, bf16[64,1280]{1,0:T(8,128)(2,1)S(1)} %get-tuple-element.44.refs_0_, bf16[64,1280]{1,0:T(8,128)(2,1)S(1)} %get-tuple-element.43.refs_1_, bf16[64,1280]{1,0:T(8,128)(2,1)S(1)} %after.7.refs_2_, ...), custom_call_target="tpu_custom_call" | custom-call | flops 1887436800 | bytes 6307840 | tf_op jit(solution)/shard_map/norm_conv/pallas_call | solution.py:523
  40.4 1.6 %collective-permute-start.14 = (bf16[160,512]{1,0:T(8,128)(2,1)S(1)}, bf16[160,512]{1,0:T(8,128)(2,1)S(1)}, u32[]{:S(2)}, u32[]{:S(2)}) collective-permute-start(bf16[160,512]{1,0:T(8,128)(2,1)S(1)} %get-tuple-element.24.refs_0_), channel_id=1, source_target_pairs={{0,1},{1,3},{3,5},{5,7},{7,6},{6,4},{4,2},{2,0},{8,9},{9,11},{11,1... | collective-permute-start | bytes 491528 | tf_op jit(solution)/shard_map/ppermute | solution.py:407
  42.0 2.2 %second_conv.1.refs_1_ = bf16[160,512]{1,0:T(8,128)(2,1)S(1)} custom-call(bf16[1152,1280]{1,0:T(8,128)(2,1)S(1)} %get-tuple-element.25.act_ref, f32[160,1024]{1,0:T(8,128)S(1)} %get-tuple-element.26.kept_ref, bf16[3,480,1280]{2,1,0:T(8,128)(2,1)S(1)} %bitcast.8, f32[1,160]{1,0:T(1,128)S(1)} %bitcast.10), custom_call_target="tpu_custom_call" | custom-call | flops 1887436800 | bytes 1887436 | tf_op jit(solution)/shard_map/second_conv/pallas_call | solution.py:540
  44.3 1.6 %collective-permute-start.17 = (bf16[160,512]{1,0:T(8,128)(2,1)S(1)}, bf16[160,512]{1,0:T(8,128)(2,1)S(1)}, u32[]{:S(2)}, u32[]{:S(2)}) collective-permute-start(bf16[160,512]{1,0:T(8,128)(2,1)S(1)} %second_conv.1.refs_1_), channel_id=1, source_target_pairs={{0,1},{1,3},{3,5},{5,7},{7,6},{6,4},{4,2},{2,0},{8,9},{9,11},{11,1... | collective-permute-start | bytes 491528 | tf_op jit(solution)/shard_map/ppermute | solution.py:407
  46.3 1.6 %collective-permute-done.14.refs_2_ = bf16[160,512]{1,0:T(8,128)(2,1)S(1)} collective-permute-done((bf16[160,512]{1,0:T(8,128)(2,1)S(1)}, bf16[160,512]{1,0:T(8,128)(2,1)S(1)}, u32[]{:S(2)}, u32[]{:S(2)}) %collective-permute-start.14) | collective-permute-done | bytes 163872 | tf_op jit(solution)/shard_map/ppermute | solution.py:407
  49.7 4.9 %collective-permute-start.34 = (bf16[160,1280]{1,0:T(8,128)(2,1)S(1)}, bf16[160,1280]{1,0:T(8,128)(2,1)S(1)}, u32[]{:S(2)}, u32[]{:S(2)}) collective-permute-start(bf16[160,1280]{1,0:T(8,128)(2,1)S(1)} %get-tuple-element.40.refs_0_), channel_id=1, source_target_pairs={{0,16},{8,24},{16,0},{24,8},{1,17},{9,25},{17,1},{25,9},{2,18},{10... | collective-permute-start | bytes 1228808 | tf_op jit(solution)/shard_map/ppermute | solution.py:434
  54.7 2.5 %collective-permute-start.15 = (bf16[160,512]{1,0:T(8,128)(2,1)S(1)}, bf16[160,512]{1,0:T(8,128)(2,1)}, u32[]{:S(2)}, u32[]{:S(2)}) collective-permute-start(bf16[160,512]{1,0:T(8,128)(2,1)S(1)} %collective-permute-done.14.refs_2_), channel_id=1, source_target_pairs={{0,1},{1,3},{3,5},{5,7},{7,6},{6,4},{4,2},{2,0},{8,9},{9,11},{11,1... | collective-permute-start | bytes 491528 | tf_op jit(solution)/shard_map/ppermute | solution.py:407
  57.2 2.0 %collective-permute-start.20 = (bf16[160,512]{1,0:T(8,128)(2,1)S(1)}, bf16[160,512]{1,0:T(8,128)(2,1)S(1)}, u32[]{:S(2)}, u32[]{:S(2)}) collective-permute-start(bf16[160,512]{1,0:T(8,128)(2,1)S(1)} %collective-permute-done.17.refs_3_), channel_id=1, source_target_pairs={{0,1},{1,3},{3,5},{5,7},{7,6},{6,4},{4,2},{2,0},{8,9},{9,11},{11,1... | collective-permute-start | bytes 491528 | tf_op jit(solution)/shard_map/ppermute | solution.py:407
  59.2 2.6 %collective-permute-done.15.refs_6_ = bf16[160,512]{1,0:T(8,128)(2,1)} collective-permute-done((bf16[160,512]{1,0:T(8,128)(2,1)S(1)}, bf16[160,512]{1,0:T(8,128)(2,1)}, u32[]{:S(2)}, u32[]{:S(2)}) %collective-permute-start.15) | collective-permute-done | bytes 163872 | tf_op jit(solution)/shard_map/ppermute | solution.py:407
  61.8 2.5 %collective-permute-start.16 = (bf16[160,512]{1,0:T(8,128)(2,1)}, bf16[160,512]{1,0:T(8,128)(2,1)S(1)}, u32[]{:S(2)}, u32[]{:S(2)}) collective-permute-start(bf16[160,512]{1,0:T(8,128)(2,1)} %collective-permute-done.15.refs_6_), channel_id=1, source_target_pairs={{0,1},{1,3},{3,5},{5,7},{7,6},{6,4},{4,2},{2,0},{8,9},{9,11},{11,1... | collective-permute-start | bytes 491528 | tf_op jit(solution)/shard_map/ppermute | solution.py:407
  65.3 2.5 %collective-permute-start.29 = (bf16[160,512]{1,0:T(8,128)(2,1)S(1)}, bf16[160,512]{1,0:T(8,128)(2,1)}, u32[]{:S(2)}, u32[]{:S(2)}) collective-permute-start(bf16[160,512]{1,0:T(8,128)(2,1)S(1)} %collective-permute-done.20.refs_7_), channel_id=1, source_target_pairs={{0,1},{1,3},{3,5},{5,7},{7,6},{6,4},{4,2},{2,0},{8,9},{9,11},{11,1... | collective-permute-start | bytes 491528 | tf_op jit(solution)/shard_map/ppermute | solution.py:407
  67.8 2.5 %early_norm.1 = (bf16[800,1024]{1,0:T(8,128)(2,1)S(1)}, bf16[800,128]{1,0:T(8,128)(2,1)S(1)}) custom-call(bf16[160,512]{1,0:T(8,128)(2,1)S(1)} %get-tuple-element.24.refs_0_, bf16[160,512]{1,0:T(8,128)(2,1)S(1)} %second_conv.1.refs_1_, bf16[160,512]{1,0:T(8,128)(2,1)S(1)} %collective-permute-done.14.refs_2_, ...), custom_call_target="tpu_custom_call" | custom-call | flops 10485760 | bytes 5242880 | tf_op jit(solution)/shard_map/early_norm/pallas_call | solution.py:555
  74.5 2.5 %collective-permute-start.37 = (bf16[160,1280]{1,0:T(8,128)(2,1)S(1)}, bf16[160,1280]{1,0:T(8,128)(2,1)S(1)}, u32[]{:S(2)}, u32[]{:S(2)}) collective-permute-start(bf16[160,1280]{1,0:T(8,128)(2,1)S(1)} %get-tuple-element.42.refs_7_), channel_id=1, source_target_pairs={{0,1},{1,0},{2,3},{3,2},{4,5},{5,4},{6,7},{7,6},{16,17},{17,16},{1... | collective-permute-start | bytes 1228808 | tf_op jit(solution)/shard_map/ppermute | solution.py:429
  77.1 1.8 %collective-permute-start.36 = (bf16[160,1280]{1,0:T(8,128)(2,1)S(1)}, bf16[160,1280]{1,0:T(8,128)(2,1)S(1)}, u32[]{:S(2)}, u32[]{:S(2)}) collective-permute-start(bf16[160,1280]{1,0:T(8,128)(2,1)S(1)} %broadcast_select_fusion), channel_id=1, source_target_pairs={{0,1},{1,0},{2,3},{3,2},{4,5},{5,4},{6,7},{7,6},{8,9},{9,8},{10,11... | collective-permute-start | bytes 1228808 | tf_op jit(solution)/shard_map/ppermute | solution.py:429
  79.0 4.7 %norm_project.1 = (f32[960,1024]{1,0:T(8,128)S(1)}, bf16[1280,128]{1,0:T(8,128)(2,1)S(1)}) custom-call(s32[128]{0:T(128)S(1)} %copy-done.6, bf16[800,1024]{1,0:T(8,128)(2,1)S(1)} %get-tuple-element.27.refs_1_.refs_0_, bf16[800,128]{1,0:T(8,128)(2,1)S(1)} %get-tuple-element.31.refs_1_, bf16[160,512]{1,0:T(8,128)(2,1)S(1)} %after.9.refs_2_, ...), custom_call_target="tpu_custom_call" | custom-call | flops 2516582400 | bytes 5079040 | tf_op jit(solution)/shard_map/norm_project/pallas_call | solution.py:583
  83.8 6.1 %attention.1 = (bf16[320,128]{1,0:T(8,128)(2,1)S(1)}, bf16[320,128]{1,0:T(8,128)(2,1)S(1)}, bf16[320,128]{1,0:T(8,128)(2,1)S(1)}, bf16[1280,128]{1,0:T(8,128)(2,...) custom-call(s32[128]{0:T(128)S(1)} %copy-done.6, ...), custom_call_target="tpu_custom_call" | custom-call | flops 1258291200 | bytes 5898240 | tf_op jit(solution)/shard_map/attention/pallas_call | solution.py:607
  89.9 2.2 %collective-permute-done.36 = bf16[160,1280]{1,0:T(8,128)(2,1)S(1)} collective-permute-done((bf16[160,1280]{1,0:T(8,128)(2,1)S(1)}, bf16[160,1280]{1,0:T(8,128)(2,1)S(1)}, u32[]{:S(2)}, u32[]{:S(2)}) %collective-permute-start.36) | collective-permute-done | bytes 409632 | tf_op jit(solution)/shard_map/ppermute | solution.py:429
  92.3 1.9 %collective-permute-start.32 = (bf16[320,128]{1,0:T(8,128)(2,1)S(1)}, bf16[320,128]{1,0:T(8,128)(2,1)S(1)}, u32[]{:S(2)}, u32[]{:S(2)}) collective-permute-start(bf16[320,128]{1,0:T(8,128)(2,1)S(1)} %get-tuple-element.37), channel_id=1, source_target_pairs={{0,4},{1,5},{2,6},{3,7},{4,0},{5,1},{6,2},{7,3},{8,12},{9,13},{10,... | collective-permute-start | bytes 245768 | tf_op jit(solution)/shard_map/ppermute | solution.py:630
  94.2 1.9 %collective-permute-start.33 = (bf16[320,128]{1,0:T(8,128)(2,1)S(1)}, bf16[320,128]{1,0:T(8,128)(2,1)S(1)}, u32[]{:S(2)}, u32[]{:S(2)}) collective-permute-start(bf16[320,128]{1,0:T(8,128)(2,1)S(1)} %get-tuple-element.38), channel_id=1, source_target_pairs={{0,6},{1,7},{2,0},{3,1},{4,2},{5,3},{6,4},{7,5},{8,14},{9,15},{10,... | collective-permute-start | bytes 245768 | tf_op jit(solution)/shard_map/ppermute | solution.py:630
  96.1 1.9 %own_attention.1.refs_0_ = bf16[320,128]{1,0:T(8,128)(2,1)S(1)} custom-call(bf16[960,1024]{1,0:T(8,128)(2,1)S(1)} %get-tuple-element.34.made_ref, bf16[5,1024,64]{2,1,0:T(8,128)(2,1)S(1)} %get-tuple-element.35.key_ref), custom_call_target="tpu_custom_call" | custom-call | flops 167772160 | bytes 2621440 | tf_op jit(solution)/shard_map/own_attention/pallas_call | solution.py:631
  99.4 2.6 %collective-permute-done.32.refs_2_ = bf16[320,128]{1,0:T(8,128)(2,1)S(1)} collective-permute-done((bf16[320,128]{1,0:T(8,128)(2,1)S(1)}, bf16[320,128]{1,0:T(8,128)(2,1)S(1)}, u32[]{:S(2)}, u32[]{:S(2)}) %collective-permute-start.32) | collective-permute-done | bytes 81952 | tf_op jit(solution)/shard_map/ppermute | solution.py:630
  102.1 2.1 %project.1 = bf16[128,1280]{1,0:T(8,128)(2,1)} custom-call(bf16[320,128]{1,0:T(8,128)(2,1)S(1)} %own_attention.1.refs_0_, bf16[320,128]{1,0:T(8,128)(2,1)S(1)} %collective-permute-done.31.refs_1_, bf16[320,128]{1,0:T(8,128)(2,1)S(1)} %collective-permute-done.32.refs_2_, bf16[320,128]{1,0:T(8,128)(2,1)S(1)} %collective-permute-done.33.refs_3_, ...), custom_call_target="tpu_custom_call" | custom-call | flops 419430400 | bytes 4259840 | tf_op jit(solution)/shard_map/project/pallas_call | solution.py:648
  (81 shorter events, 22.0 us)
Async XLA Ops:
  1.0 8.1 %collective-permute-start = (bf16[64,1280]{1,0:T(8,128)(2,1)S(1)}, bf16[64,1280]{1,0:T(8,128)(2,1)S(1)}, u32[]{:S(2)}, u32[]{:S(2)}) collective-permute-start(bf16[64,1280]{1,0:T(8,128)(2,1)S(1)} %get-tuple-element.44.refs_0_), channel_id=1, source_target_pairs={{0,1},{1,3},{3,5},{5,7},{7,6},{6,4},{4,2},{2,0},{8,9},{9,11},{11,1... | collective-permute-start | bytes 491528 | tf_op jit(solution)/shard_map/ppermute | solution.py:407
  4.0 11.2 %collective-permute-start.2 = (bf16[64,1280]{1,0:T(8,128)(2,1)S(1)}, bf16[64,1280]{1,0:T(8,128)(2,1)S(1)}, u32[]{:S(2)}, u32[]{:S(2)}) collective-permute-start(bf16[64,1280]{1,0:T(8,128)(2,1)S(1)} %get-tuple-element.44.refs_0_), channel_id=1, source_target_pairs={{1,0},{3,1},{5,3},{7,5},{6,7},{4,6},{2,4},{0,2},{9,8},{11,9},{13,1... | collective-permute-start | bytes 491528 | tf_op jit(solution)/shard_map/ppermute | solution.py:407
  4.2 9.5 %collective-permute-start.1 = (bf16[64,1280]{1,0:T(8,128)(2,1)S(1)}, bf16[64,1280]{1,0:T(8,128)(2,1)S(1)}, u32[]{:S(2)}, u32[]{:S(2)}) collective-permute-start(bf16[64,1280]{1,0:T(8,128)(2,1)S(1)} %get-tuple-element.43.refs_1_), channel_id=1, source_target_pairs={{0,1},{1,3},{3,5},{5,7},{7,6},{6,4},{4,2},{2,0},{8,9},{9,11},{11,1... | collective-permute-start | bytes 491528 | tf_op jit(solution)/shard_map/ppermute | solution.py:407
  6.1 7.1 %collective-permute-start.3 = (bf16[64,1280]{1,0:T(8,128)(2,1)S(1)}, bf16[64,1280]{1,0:T(8,128)(2,1)S(1)}, u32[]{:S(2)}, u32[]{:S(2)}) collective-permute-start(bf16[64,1280]{1,0:T(8,128)(2,1)S(1)} %get-tuple-element.43.refs_1_), channel_id=1, source_target_pairs={{1,0},{3,1},{5,3},{7,5},{6,7},{4,6},{2,4},{0,2},{9,8},{11,9},{13,1... | collective-permute-start | bytes 491528 | tf_op jit(solution)/shard_map/ppermute | solution.py:407
  13.6 7.1 %collective-permute-start.5 = (bf16[64,1280]{1,0:T(8,128)(2,1)S(1)}, bf16[64,1280]{1,0:T(8,128)(2,1)S(1)}, u32[]{:S(2)}, u32[]{:S(2)}) collective-permute-start(bf16[64,1280]{1,0:T(8,128)(2,1)S(1)} %collective-permute-done.1.refs_3_), channel_id=1, source_target_pairs={{0,1},{1,3},{3,5},{5,7},{7,6},{6,4},{4,2},{2,0},{8,9},{9,11},{11,1... | collective-permute-start | bytes 491528 | tf_op jit(solution)/shard_map/ppermute | solution.py:407
  15.2 8.6 %collective-permute-start.6 = (bf16[64,1280]{1,0:T(8,128)(2,1)S(1)}, bf16[64,1280]{1,0:T(8,128)(2,1)S(1)}, u32[]{:S(2)}, u32[]{:S(2)}) collective-permute-start(bf16[64,1280]{1,0:T(8,128)(2,1)S(1)} %collective-permute-done.2.refs_4_), channel_id=1, source_target_pairs={{1,0},{3,1},{5,3},{7,5},{6,7},{4,6},{2,4},{0,2},{9,8},{11,9},{13,1... | collective-permute-start | bytes 491528 | tf_op jit(solution)/shard_map/ppermute | solution.py:407
  15.7 9.4 %collective-permute-start.8 = (bf16[64,1280]{1,0:T(8,128)(2,1)S(1)}, bf16[64,1280]{1,0:T(8,128)(2,1)S(1)}, u32[]{:S(2)}, u32[]{:S(2)}) collective-permute-start(bf16[64,1280]{1,0:T(8,128)(2,1)S(1)} %collective-permute-done.4.refs_6_), channel_id=1, source_target_pairs={{0,1},{1,3},{3,5},{5,7},{7,6},{6,4},{4,2},{2,0},{8,9},{9,11},{11,1... | collective-permute-start | bytes 491528 | tf_op jit(solution)/shard_map/ppermute | solution.py:407
  20.8 7.2 %collective-permute-start.9 = (bf16[64,1280]{1,0:T(8,128)(2,1)S(1)}, bf16[64,1280]{1,0:T(8,128)(2,1)S(1)}, u32[]{:S(2)}, u32[]{:S(2)}) collective-permute-start(bf16[64,1280]{1,0:T(8,128)(2,1)S(1)} %collective-permute-done.5.refs_7_), channel_id=1, source_target_pairs={{0,1},{1,3},{3,5},{5,7},{7,6},{6,4},{4,2},{2,0},{8,9},{9,11},{11,1... | collective-permute-start | bytes 491528 | tf_op jit(solution)/shard_map/ppermute | solution.py:407
  25.1 9.1 %collective-permute-start.12 = (bf16[64,1280]{1,0:T(8,128)(2,1)S(1)}, bf16[64,1280]{1,0:T(8,128)(2,1)S(1)}, u32[]{:S(2)}, u32[]{:S(2)}) collective-permute-start(bf16[64,1280]{1,0:T(8,128)(2,1)S(1)} %after.8.refs_10_.refs_2_), channel_id=1, source_target_pairs={{0,1},{1,3},{3,5},{5,7},{7,6},{6,4},{4,2},{2,0},{8,9},{9,11},{11,1... | collective-permute-start | bytes 491528 | tf_op jit(solution)/shard_map/ppermute | solution.py:407
  31.0 18.7 %collective-permute-start.26 = (bf16[240,1280]{1,0:T(8,128)(2,1)S(1)}, bf16[240,1280]{1,0:T(8,128)(2,1)S(1)}, u32[]{:S(2)}, u32[]{:S(2)}) collective-permute-start(bf16[240,1280]{1,0:T(8,128)(2,1)S(1)} %get-tuple-element.28), channel_id=1, source_target_pairs={{0,1},{1,0},{2,3},{3,2},{4,5},{5,4},{6,7},{7,6},{8,9},{9,8},{10,11... | collective-permute-start | bytes 1843208 | tf_op jit(solution)/shard_map/ppermute | solution.py:429
  32.6 17.2 %collective-permute-start.27 = (bf16[160,1280]{1,0:T(8,128)(2,1)S(1)}, bf16[160,1280]{1,0:T(8,128)(2,1)S(1)}, u32[]{:S(2)}, u32[]{:S(2)}) collective-permute-start(bf16[160,1280]{1,0:T(8,128)(2,1)S(1)} %get-tuple-element.29), channel_id=1, source_target_pairs={{0,2},{1,3},{2,4},{3,5},{4,6},{5,7},{6,0},{7,1},{8,14},{9,15},{10,... | collective-permute-start | bytes 1228808 | tf_op jit(solution)/shard_map/ppermute | solution.py:429
  40.4 7.6 %collective-permute-start.14 = (bf16[160,512]{1,0:T(8,128)(2,1)S(1)}, bf16[160,512]{1,0:T(8,128)(2,1)S(1)}, u32[]{:S(2)}, u32[]{:S(2)}) collective-permute-start(bf16[160,512]{1,0:T(8,128)(2,1)S(1)} %get-tuple-element.24.refs_0_), channel_id=1, source_target_pairs={{0,1},{1,3},{3,5},{5,7},{7,6},{6,4},{4,2},{2,0},{8,9},{9,11},{11,1... | collective-permute-start | bytes 491528 | tf_op jit(solution)/shard_map/ppermute | solution.py:407
  45.9 11.3 %collective-permute-start.19 = (bf16[160,512]{1,0:T(8,128)(2,1)S(1)}, bf16[160,512]{1,0:T(8,128)(2,1)S(1)}, u32[]{:S(2)}, u32[]{:S(2)}) collective-permute-start(bf16[160,512]{1,0:T(8,128)(2,1)S(1)} %second_conv.1.refs_1_), channel_id=1, source_target_pairs={{1,0},{3,1},{5,3},{7,5},{6,7},{4,6},{2,4},{0,2},{9,8},{11,9},{13,1... | collective-permute-start | bytes 491528 | tf_op jit(solution)/shard_map/ppermute | solution.py:407
  48.0 11.3 %collective-permute-start.18 = (bf16[160,512]{1,0:T(8,128)(2,1)S(1)}, bf16[160,512]{1,0:T(8,128)(2,1)S(1)}, u32[]{:S(2)}, u32[]{:S(2)}) collective-permute-start(bf16[160,512]{1,0:T(8,128)(2,1)S(1)} %get-tuple-element.24.refs_0_), channel_id=1, source_target_pairs={{1,0},{3,1},{5,3},{7,5},{6,7},{4,6},{2,4},{0,2},{9,8},{11,9},{13,1... | collective-permute-start | bytes 491528 | tf_op jit(solution)/shard_map/ppermute | solution.py:407
  49.7 24.7 %collective-permute-start.34 = (bf16[160,1280]{1,0:T(8,128)(2,1)S(1)}, bf16[160,1280]{1,0:T(8,128)(2,1)S(1)}, u32[]{:S(2)}, u32[]{:S(2)}) collective-permute-start(bf16[160,1280]{1,0:T(8,128)(2,1)S(1)} %get-tuple-element.40.refs_0_), channel_id=1, source_target_pairs={{0,16},{8,24},{16,0},{24,8},{1,17},{9,25},{17,1},{25,9},{2,18},{10... | collective-permute-start | bytes 1228808 | tf_op jit(solution)/shard_map/ppermute | solution.py:434
  54.7 7.2 %collective-permute-start.15 = (bf16[160,512]{1,0:T(8,128)(2,1)S(1)}, bf16[160,512]{1,0:T(8,128)(2,1)}, u32[]{:S(2)}, u32[]{:S(2)}) collective-permute-start(bf16[160,512]{1,0:T(8,128)(2,1)S(1)} %collective-permute-done.14.refs_2_), channel_id=1, source_target_pairs={{0,1},{1,3},{3,5},{5,7},{7,6},{6,4},{4,2},{2,0},{8,9},{9,11},{11,1... | collective-permute-start | bytes 491528 | tf_op jit(solution)/shard_map/ppermute | solution.py:407
  57.2 7.2 %collective-permute-start.22 = (bf16[160,512]{1,0:T(8,128)(2,1)S(1)}, bf16[160,512]{1,0:T(8,128)(2,1)S(1)}, u32[]{:S(2)}, u32[]{:S(2)}) collective-permute-start(bf16[160,512]{1,0:T(8,128)(2,1)S(1)} %collective-permute-done.19.refs_5_), channel_id=1, source_target_pairs={{1,0},{3,1},{5,3},{7,5},{6,7},{4,6},{2,4},{0,2},{9,8},{11,9},{13,1... | collective-permute-start | bytes 491528 | tf_op jit(solution)/shard_map/ppermute | solution.py:407
  57.2 8.1 %collective-permute-start.20 = (bf16[160,512]{1,0:T(8,128)(2,1)S(1)}, bf16[160,512]{1,0:T(8,128)(2,1)S(1)}, u32[]{:S(2)}, u32[]{:S(2)}) collective-permute-start(bf16[160,512]{1,0:T(8,128)(2,1)S(1)} %collective-permute-done.17.refs_3_), channel_id=1, source_target_pairs={{0,1},{1,3},{3,5},{5,7},{7,6},{6,4},{4,2},{2,0},{8,9},{9,11},{11,1... | collective-permute-start | bytes 491528 | tf_op jit(solution)/shard_map/ppermute | solution.py:407
  59.2 8.6 %collective-permute-start.21 = (bf16[160,512]{1,0:T(8,128)(2,1)S(1)}, bf16[160,512]{1,0:T(8,128)(2,1)S(1)}, u32[]{:S(2)}, u32[]{:S(2)}) collective-permute-start(bf16[160,512]{1,0:T(8,128)(2,1)S(1)} %collective-permute-done.18.refs_4_), channel_id=1, source_target_pairs={{1,0},{3,1},{5,3},{7,5},{6,7},{4,6},{2,4},{0,2},{9,8},{11,9},{13,1... | collective-permute-start | bytes 491528 | tf_op jit(solution)/shard_map/ppermute | solution.py:407
  61.8 8.4 %collective-permute-start.16 = (bf16[160,512]{1,0:T(8,128)(2,1)}, bf16[160,512]{1,0:T(8,128)(2,1)S(1)}, u32[]{:S(2)}, u32[]{:S(2)}) collective-permute-start(bf16[160,512]{1,0:T(8,128)(2,1)} %collective-permute-done.15.refs_6_), channel_id=1, source_target_pairs={{0,1},{1,3},{3,5},{5,7},{7,6},{6,4},{4,2},{2,0},{8,9},{9,11},{11,1... | collective-permute-start | bytes 491528 | tf_op jit(solution)/shard_map/ppermute | solution.py:407
  64.4 7.2 %collective-permute-start.24 = (bf16[160,512]{1,0:T(8,128)(2,1)S(1)}, bf16[160,512]{1,0:T(8,128)(2,1)}, u32[]{:S(2)}, u32[]{:S(2)}) collective-permute-start(bf16[160,512]{1,0:T(8,128)(2,1)S(1)} %collective-permute-done.22.refs_9_), channel_id=1, source_target_pairs={{1,0},{3,1},{5,3},{7,5},{6,7},{4,6},{2,4},{0,2},{9,8},{11,9},{13,1... | collective-permute-start | bytes 491528 | tf_op jit(solution)/shard_map/ppermute | solution.py:407
  65.3 7.1 %collective-permute-start.29 = (bf16[160,512]{1,0:T(8,128)(2,1)S(1)}, bf16[160,512]{1,0:T(8,128)(2,1)}, u32[]{:S(2)}, u32[]{:S(2)}) collective-permute-start(bf16[160,512]{1,0:T(8,128)(2,1)S(1)} %collective-permute-done.20.refs_7_), channel_id=1, source_target_pairs={{0,1},{1,3},{3,5},{5,7},{7,6},{6,4},{4,2},{2,0},{8,9},{9,11},{11,1... | collective-permute-start | bytes 491528 | tf_op jit(solution)/shard_map/ppermute | solution.py:407
  70.3 8.7 %collective-permute-start.28 = (bf16[240,1280]{1,0:T(8,128)(2,1)S(1)}, bf16[240,1280]{1,0:T(8,128)(2,1)S(1)}, u32[]{:S(2)}, u32[]{:S(2)}) collective-permute-start(bf16[240,1280]{1,0:T(8,128)(2,1)S(1)} %get-tuple-element.30.refs_9_.refs_5_), channel_id=1, source_target_pairs={{0,8},{8,0},{16,24},{24,16},{1,9},{9,1},{17,25},{25,17},{2,10},{10... | collective-permute-start | bytes 1843208 | tf_op jit(solution)/shard_map/ppermute | solution.py:434
  71.6 12.1 %collective-permute-start.23 = (bf16[160,512]{1,0:T(8,128)(2,1)S(1)}, bf16[160,512]{1,0:T(8,128)(2,1)S(1)}, u32[]{:S(2)}, u32[]{:S(2)}) collective-permute-start(bf16[160,512]{1,0:T(8,128)(2,1)S(1)} %after.9.refs_2_), channel_id=1, source_target_pairs={{0,1},{1,3},{3,5},{5,7},{7,6},{6,4},{4,2},{2,0},{8,9},{9,11},{11,1... | collective-permute-start | bytes 491528 | tf_op jit(solution)/shard_map/ppermute | solution.py:407
  72.4 11.3 %collective-permute-start.25 = (bf16[160,512]{1,0:T(8,128)(2,1)}, bf16[160,512]{1,0:T(8,128)(2,1)S(1)}, u32[]{:S(2)}, u32[]{:S(2)}) collective-permute-start(bf16[160,512]{1,0:T(8,128)(2,1)} %collective-permute-done.24.refs_5_), channel_id=1, source_target_pairs={{1,0},{3,1},{5,3},{7,5},{6,7},{4,6},{2,4},{0,2},{9,8},{11,9},{13,1... | collective-permute-start | bytes 491528 | tf_op jit(solution)/shard_map/ppermute | solution.py:407
  74.5 15.4 %collective-permute-start.37 = (bf16[160,1280]{1,0:T(8,128)(2,1)S(1)}, bf16[160,1280]{1,0:T(8,128)(2,1)S(1)}, u32[]{:S(2)}, u32[]{:S(2)}) collective-permute-start(bf16[160,1280]{1,0:T(8,128)(2,1)S(1)} %get-tuple-element.42.refs_7_), channel_id=1, source_target_pairs={{0,1},{1,0},{2,3},{3,2},{4,5},{5,4},{6,7},{7,6},{16,17},{17,16},{1... | collective-permute-start | bytes 1228808 | tf_op jit(solution)/shard_map/ppermute | solution.py:429
  77.1 15.0 %collective-permute-start.36 = (bf16[160,1280]{1,0:T(8,128)(2,1)S(1)}, bf16[160,1280]{1,0:T(8,128)(2,1)S(1)}, u32[]{:S(2)}, u32[]{:S(2)}) collective-permute-start(bf16[160,1280]{1,0:T(8,128)(2,1)S(1)} %broadcast_select_fusion), channel_id=1, source_target_pairs={{0,1},{1,0},{2,3},{3,2},{4,5},{5,4},{6,7},{7,6},{8,9},{9,8},{10,11... | collective-permute-start | bytes 1228808 | tf_op jit(solution)/shard_map/ppermute | solution.py:429
  78.9 23.1 %collective-permute-start.35 = (bf16[320,1280]{1,0:T(8,128)(2,1)S(1)}, bf16[320,1280]{1,0:T(8,128)(2,1)S(1)}, u32[]{:S(2)}, u32[]{:S(2)}) collective-permute-start(bf16[320,1280]{1,0:T(8,128)(2,1)S(1)} %pad_maximum_fusion), channel_id=1, source_target_pairs={{0,8},{8,0},{16,24},{24,16},{1,9},{9,1},{17,25},{25,17},{2,10},{10... | collective-permute-start | bytes 2457608 | tf_op jit(solution)/shard_map/ppermute | solution.py:434
  92.2 9.9 %collective-permute-start.38 = (bf16[320,1280]{1,0:T(8,128)(2,1)S(1)}, bf16[320,1280]{1,0:T(8,128)(2,1)S(1)}, u32[]{:S(2)}, u32[]{:S(2)}) collective-permute-start(bf16[320,1280]{1,0:T(8,128)(2,1)S(1)} %after.13.refs_9_), channel_id=1, source_target_pairs={{0,8},{8,0},{16,24},{24,16},{1,9},{9,1},{17,25},{25,17},{2,10},{10... | collective-permute-start | bytes 2457608 | tf_op jit(solution)/shard_map/ppermute | solution.py:434
  92.2 7.2 %collective-permute-start.31 = (bf16[320,128]{1,0:T(8,128)(2,1)S(1)}, bf16[320,128]{1,0:T(8,128)(2,1)S(1)}, u32[]{:S(2)}, u32[]{:S(2)}) collective-permute-start(bf16[320,128]{1,0:T(8,128)(2,1)S(1)} %get-tuple-element.36.refs_1_), channel_id=1, source_target_pairs={{0,2},{1,3},{2,4},{3,5},{4,6},{5,7},{6,0},{7,1},{8,10},{9,11},{10,... | collective-permute-start | bytes 245768 | tf_op jit(solution)/shard_map/ppermute | solution.py:630
  92.3 9.8 %collective-permute-start.32 = (bf16[320,128]{1,0:T(8,128)(2,1)S(1)}, bf16[320,128]{1,0:T(8,128)(2,1)S(1)}, u32[]{:S(2)}, u32[]{:S(2)}) collective-permute-start(bf16[320,128]{1,0:T(8,128)(2,1)S(1)} %get-tuple-element.37), channel_id=1, source_target_pairs={{0,4},{1,5},{2,6},{3,7},{4,0},{5,1},{6,2},{7,3},{8,12},{9,13},{10,... | collective-permute-start | bytes 245768 | tf_op jit(solution)/shard_map/ppermute | solution.py:630
  94.2 7.9 %collective-permute-start.33 = (bf16[320,128]{1,0:T(8,128)(2,1)S(1)}, bf16[320,128]{1,0:T(8,128)(2,1)S(1)}, u32[]{:S(2)}, u32[]{:S(2)}) collective-permute-start(bf16[320,128]{1,0:T(8,128)(2,1)S(1)} %get-tuple-element.38), channel_id=1, source_target_pairs={{0,6},{1,7},{2,0},{3,1},{4,2},{5,3},{6,4},{7,5},{8,14},{9,15},{10,... | collective-permute-start | bytes 245768 | tf_op jit(solution)/shard_map/ppermute | solution.py:630
  (14 other events, 110.6 us)

commit v13 on v12

--- a/solution.py
+++ b/solution.py
@@ -573,7 +573,7 @@
 
     hidden_pieces = gather((first_hidden, second_hidden), n, beside_second)
     if inner == 2:
-        chosen, far = after([chosen, far], hidden_pieces[2:4])
+        chosen, far = after([chosen, far], hidden_pieces[6:10])
         near = [chosen]
         near.append(swap(near[0], 1))
         weights = [w_query, w_key, w_value] + near

time: 104 us -> 109 us (1.048)
  waiting for transfers between devices: 26.6 us -> 31.2 us
    ppermute x28, waiting for transfers between devices: 20.4 us -> 25.1 us  [gather(): lax.ppermute(found[half, sign * (step - 1)], 'patch', pairs)]
  transfers between devices with their start and end apart: 39 -> 39, of which waited for: 16 -> 19; matrix products, arithmetic and copies ran while one was open for 2% -> 2% of each run, Pallas kernels for 23% -> 21%
where the time goes in v13:
time: 109 us
  starting transfers between devices  48.7 us (45%)
  waiting for transfers between devices  31.2 us (29%)
  Pallas kernels  25.2 us (23%)
  local copies, waits for them, and re-layouts  2 us (2%)
  other arithmetic  1.72 us (2%)
    ppermute x28, starting transfers between devices, gather(): lax.ppermute(found[half, sign * (step - 1)], 'patch', pairs)  32 us
    ppermute x28, waiting for transfers between devices, gather(): lax.ppermute(found[half, sign * (step - 1)], 'patch', pairs)  25.1 us
    ppermute x4, starting transfers between devices, send(): return lax.ppermute(block, ('batch', 'patch'), pairs)  7.46 us
    pallas_call x1, Pallas kernels, on_device(): pl.pallas_call(functools.partial(attention_kernel, 2 * n, inner), out_sha...  6.14 us
    pallas_call x1, Pallas kernels, on_device(): pl.pallas_call(functools.partial(conv_kernel, columns), out_shape=[half_h...  5.78 us
    ppermute x4, starting transfers between devices, swap(): return lax.ppermute(block, 'batch', pairs)  5.44 us
    pallas_call x1, Pallas kernels, on_device(): pl.pallas_call(functools.partial(project_kernel, 2 * n), out_shape=[jax.S...  4.68 us
    ppermute x3, waiting for transfers between devices, on_device(): received.append(lax.ppermute(sent_block, 'patch', pairs))  3.98 us
  transfers between devices with their start and end apart: 39, of which 19 were waited for; matrix products, arithmetic and copies ran while one was open for 2% of the time, Pallas kernels for 21%

profile of v13, /device:TPU:0, one launch (start us, length us, event | category | flops | bytes accessed | tf_op | source)
XLA Modules:
  0.0 109.1 jit_solution(8927384860295833310)
XLA Ops:
  1.0 3.0 %collective-permute-start = (bf16[64,1280]{1,0:T(8,128)(2,1)S(1)}, bf16[64,1280]{1,0:T(8,128)(2,1)S(1)}, u32[]{:S(2)}, u32[]{:S(2)}) collective-permute-start(bf16[64,1280]{1,0:T(8,128)(2,1)S(1)} %get-tuple-element.44.refs_0_), channel_id=1, source_target_pairs={{0,1},{1,3},{3,5},{5,7},{7,6},{6,4},{4,2},{2,0},{8,9},{9,11},{11,1... | collective-permute-start | bytes 491528 | tf_op jit(solution)/shard_map/ppermute | solution.py:407
  4.2 1.9 %collective-permute-start.1 = (bf16[64,1280]{1,0:T(8,128)(2,1)S(1)}, bf16[64,1280]{1,0:T(8,128)(2,1)S(1)}, u32[]{:S(2)}, u32[]{:S(2)}) collective-permute-start(bf16[64,1280]{1,0:T(8,128)(2,1)S(1)} %get-tuple-element.43.refs_1_), channel_id=1, source_target_pairs={{0,1},{1,3},{3,5},{5,7},{7,6},{6,4},{4,2},{2,0},{8,9},{9,11},{11,1... | collective-permute-start | bytes 491528 | tf_op jit(solution)/shard_map/ppermute | solution.py:407
  9.1 2.0 %collective-permute-start.4 = (bf16[64,1280]{1,0:T(8,128)(2,1)S(1)}, bf16[64,1280]{1,0:T(8,128)(2,1)S(1)}, u32[]{:S(2)}, u32[]{:S(2)}) collective-permute-start(bf16[64,1280]{1,0:T(8,128)(2,1)S(1)} %after.7.refs_2_), channel_id=1, source_target_pairs={{0,1},{1,3},{3,5},{5,7},{7,6},{6,4},{4,2},{2,0},{8,9},{9,11},{11,1... | collective-permute-start | bytes 491528 | tf_op jit(solution)/shard_map/ppermute | solution.py:407
  11.1 2.1 %collective-permute-done.3.refs_5_ = bf16[64,1280]{1,0:T(8,128)(2,1)S(1)} collective-permute-done((bf16[64,1280]{1,0:T(8,128)(2,1)S(1)}, bf16[64,1280]{1,0:T(8,128)(2,1)S(1)}, u32[]{:S(2)}, u32[]{:S(2)}) %collective-permute-start.3) | collective-permute-done | bytes 163872 | tf_op jit(solution)/shard_map/ppermute | solution.py:407
  15.7 2.1 %collective-permute-start.8 = (bf16[64,1280]{1,0:T(8,128)(2,1)S(1)}, bf16[64,1280]{1,0:T(8,128)(2,1)S(1)}, u32[]{:S(2)}, u32[]{:S(2)}) collective-permute-start(bf16[64,1280]{1,0:T(8,128)(2,1)S(1)} %collective-permute-done.4.refs_6_), channel_id=1, source_target_pairs={{0,1},{1,3},{3,5},{5,7},{7,6},{6,4},{4,2},{2,0},{8,9},{9,11},{11,1... | collective-permute-start | bytes 491528 | tf_op jit(solution)/shard_map/ppermute | solution.py:407
  17.7 2.6 %collective-permute-done.7.refs_9_ = bf16[64,1280]{1,0:T(8,128)(2,1)S(1)} collective-permute-done((bf16[64,1280]{1,0:T(8,128)(2,1)S(1)}, bf16[64,1280]{1,0:T(8,128)(2,1)S(1)}, u32[]{:S(2)}, u32[]{:S(2)}) %collective-permute-start.7) | collective-permute-done | bytes 163872 | tf_op jit(solution)/shard_map/ppermute | solution.py:407
  25.1 1.7 %collective-permute-start.12 = (bf16[64,1280]{1,0:T(8,128)(2,1)S(1)}, bf16[64,1280]{1,0:T(8,128)(2,1)S(1)}, u32[]{:S(2)}, u32[]{:S(2)}) collective-permute-start(bf16[64,1280]{1,0:T(8,128)(2,1)S(1)} %after.8.refs_10_.refs_2_), channel_id=1, source_target_pairs={{0,1},{1,3},{3,5},{5,7},{7,6},{6,4},{4,2},{2,0},{8,9},{9,11},{11,1... | collective-permute-start | bytes 491528 | tf_op jit(solution)/shard_map/ppermute | solution.py:407
  27.9 3.1 %collective-permute-done.10.refs_12_.refs_4_ = bf16[64,1280]{1,0:T(8,128)(2,1)S(1)} collective-permute-done((bf16[64,1280]{1,0:T(8,128)(2,1)S(1)}, bf16[64,1280]{1,0:T(8,128)(2,1)S(1)}, u32[]{:S(2)}, u32[]{:S(2)}) %collective-permute-start.10) | collective-permute-done | bytes 163872 | tf_op jit(solution)/shard_map/ppermute | solution.py:407
  34.6 5.8 %norm_conv.1 = (bf16[160,512]{1,0:T(8,128)(2,1)S(1)}, bf16[1152,1280]{1,0:T(8,128)(2,1)S(1)}, f32[160,1024]{1,0:T(8,128)S(1)}) custom-call(s32[128]{0:T(128)S(1)} %copy-done.8, bf16[64,1280]{1,0:T(8,128)(2,1)S(1)} %get-tuple-element.44.refs_0_, bf16[64,1280]{1,0:T(8,128)(2,1)S(1)} %get-tuple-element.43.refs_1_, bf16[64,1280]{1,0:T(8,128)(2,1)S(1)} %after.7.refs_2_, ...), custom_call_target="tpu_custom_call" | custom-call | flops 1887436800 | bytes 6307840 | tf_op jit(solution)/shard_map/norm_conv/pallas_call | solution.py:523
  40.4 1.6 %collective-permute-start.14 = (bf16[160,512]{1,0:T(8,128)(2,1)S(1)}, bf16[160,512]{1,0:T(8,128)(2,1)S(1)}, u32[]{:S(2)}, u32[]{:S(2)}) collective-permute-start(bf16[160,512]{1,0:T(8,128)(2,1)S(1)} %get-tuple-element.24.refs_0_), channel_id=1, source_target_pairs={{0,1},{1,3},{3,5},{5,7},{7,6},{6,4},{4,2},{2,0},{8,9},{9,11},{11,1... | collective-permute-start | bytes 491528 | tf_op jit(solution)/shard_map/ppermute | solution.py:407
  42.0 2.2 %second_conv.1.refs_1_ = bf16[160,512]{1,0:T(8,128)(2,1)S(1)} custom-call(bf16[1152,1280]{1,0:T(8,128)(2,1)S(1)} %get-tuple-element.25.act_ref, f32[160,1024]{1,0:T(8,128)S(1)} %get-tuple-element.26.kept_ref, bf16[3,480,1280]{2,1,0:T(8,128)(2,1)S(1)} %bitcast.8, f32[1,160]{1,0:T(1,128)S(1)} %bitcast.10), custom_call_target="tpu_custom_call" | custom-call | flops 1887436800 | bytes 1887436 | tf_op jit(solution)/shard_map/second_conv/pallas_call | solution.py:540
  46.3 1.6 %collective-permute-done.14.refs_2_ = bf16[160,512]{1,0:T(8,128)(2,1)S(1)} collective-permute-done((bf16[160,512]{1,0:T(8,128)(2,1)S(1)}, bf16[160,512]{1,0:T(8,128)(2,1)S(1)}, u32[]{:S(2)}, u32[]{:S(2)}) %collective-permute-start.14) | collective-permute-done | bytes 163872 | tf_op jit(solution)/shard_map/ppermute | solution.py:407
  48.4 2.7 %collective-permute-done.17.refs_3_ = bf16[160,512]{1,0:T(8,128)(2,1)S(1)} collective-permute-done((bf16[160,512]{1,0:T(8,128)(2,1)S(1)}, bf16[160,512]{1,0:T(8,128)(2,1)S(1)}, u32[]{:S(2)}, u32[]{:S(2)}) %collective-permute-start.17) | collective-permute-done | bytes 163872 | tf_op jit(solution)/shard_map/ppermute | solution.py:407
  51.1 2.5 %collective-permute-start.15 = (bf16[160,512]{1,0:T(8,128)(2,1)S(1)}, bf16[160,512]{1,0:T(8,128)(2,1)S(1)}, u32[]{:S(2)}, u32[]{:S(2)}) collective-permute-start(bf16[160,512]{1,0:T(8,128)(2,1)S(1)} %collective-permute-done.14.refs_2_), channel_id=1, source_target_pairs={{0,1},{1,3},{3,5},{5,7},{7,6},{6,4},{4,2},{2,0},{8,9},{9,11},{11,1... | collective-permute-start | bytes 491528 | tf_op jit(solution)/shard_map/ppermute | solution.py:407
  55.7 1.9 %collective-permute-start.22 = (bf16[160,512]{1,0:T(8,128)(2,1)S(1)}, bf16[160,512]{1,0:T(8,128)(2,1)S(1)}, u32[]{:S(2)}, u32[]{:S(2)}) collective-permute-start(bf16[160,512]{1,0:T(8,128)(2,1)S(1)} %collective-permute-done.19.refs_5_), channel_id=1, source_target_pairs={{1,0},{3,1},{5,3},{7,5},{6,7},{4,6},{2,4},{0,2},{9,8},{11,9},{13,1... | collective-permute-start | bytes 491528 | tf_op jit(solution)/shard_map/ppermute | solution.py:407
  58.9 2.0 %collective-permute-done.21.refs_8_.refs_4_ = bf16[160,512]{1,0:T(8,128)(2,1)S(1)} collective-permute-done((bf16[160,512]{1,0:T(8,128)(2,1)S(1)}, bf16[160,512]{1,0:T(8,128)(2,1)S(1)}, u32[]{:S(2)}, u32[]{:S(2)}) %collective-permute-start.21) | collective-permute-done | bytes 163872 | tf_op jit(solution)/shard_map/ppermute | solution.py:407
  60.9 1.8 %collective-permute-done.22.refs_9_.refs_5_ = bf16[160,512]{1,0:T(8,128)(2,1)S(1)} collective-permute-done((bf16[160,512]{1,0:T(8,128)(2,1)S(1)}, bf16[160,512]{1,0:T(8,128)(2,1)S(1)}, u32[]{:S(2)}, u32[]{:S(2)}) %collective-permute-start.22) | collective-permute-done | bytes 163872 | tf_op jit(solution)/shard_map/ppermute | solution.py:407
  62.7 5.3 %collective-permute-start.34 = (bf16[160,1280]{1,0:T(8,128)(2,1)S(1)}, bf16[160,1280]{1,0:T(8,128)(2,1)S(1)}, u32[]{:S(2)}, u32[]{:S(2)}) collective-permute-start(bf16[160,1280]{1,0:T(8,128)(2,1)S(1)} %get-tuple-element.40.refs_0_), channel_id=1, source_target_pairs={{0,16},{8,24},{16,0},{24,8},{1,17},{9,25},{17,1},{25,9},{2,18},{10... | collective-permute-start | bytes 1228808 | tf_op jit(solution)/shard_map/ppermute | solution.py:434
  68.0 2.2 %collective-permute-start.16 = (bf16[160,512]{1,0:T(8,128)(2,1)S(1)}, bf16[160,512]{1,0:T(8,128)(2,1)S(1)}, u32[]{:S(2)}, u32[]{:S(2)}) collective-permute-start(bf16[160,512]{1,0:T(8,128)(2,1)S(1)} %collective-permute-done.15.refs_6_.refs_2_), channel_id=1, source_target_pairs={{0,1},{1,3},{3,5},{5,7},{7,6},{6,4},{4,2},{2,0},{8,9},{9,11},{11,1... | collective-permute-start | bytes 491528 | tf_op jit(solution)/shard_map/ppermute | solution.py:407
  70.1 2.0 %collective-permute-start.29 = (bf16[160,512]{1,0:T(8,128)(2,1)S(1)}, bf16[160,512]{1,0:T(8,128)(2,1)}, u32[]{:S(2)}, u32[]{:S(2)}) collective-permute-start(bf16[160,512]{1,0:T(8,128)(2,1)S(1)} %collective-permute-done.20.refs_7_.refs_3_), channel_id=1, source_target_pairs={{0,1},{1,3},{3,5},{5,7},{7,6},{6,4},{4,2},{2,0},{8,9},{9,11},{11,1... | collective-permute-start | bytes 491528 | tf_op jit(solution)/shard_map/ppermute | solution.py:407
  75.0 2.3 %collective-permute-done.24.refs_5_ = bf16[160,512]{1,0:T(8,128)(2,1)} collective-permute-done((bf16[160,512]{1,0:T(8,128)(2,1)S(1)}, bf16[160,512]{1,0:T(8,128)(2,1)}, u32[]{:S(2)}, u32[]{:S(2)}) %collective-permute-start.24) | collective-permute-done | bytes 163872 | tf_op jit(solution)/shard_map/ppermute | solution.py:407
  77.5 1.9 %collective-permute-start.25 = (bf16[160,512]{1,0:T(8,128)(2,1)}, bf16[160,512]{1,0:T(8,128)(2,1)S(1)}, u32[]{:S(2)}, u32[]{:S(2)}) collective-permute-start(bf16[160,512]{1,0:T(8,128)(2,1)} %collective-permute-done.24.refs_5_), channel_id=1, source_target_pairs={{1,0},{3,1},{5,3},{7,5},{6,7},{4,6},{2,4},{0,2},{9,8},{11,9},{13,1... | collective-permute-start | bytes 491528 | tf_op jit(solution)/shard_map/ppermute | solution.py:407
  79.5 2.6 %collective-permute-start.37 = (bf16[160,1280]{1,0:T(8,128)(2,1)S(1)}, bf16[160,1280]{1,0:T(8,128)(2,1)S(1)}, u32[]{:S(2)}, u32[]{:S(2)}) collective-permute-start(bf16[160,1280]{1,0:T(8,128)(2,1)S(1)} %get-tuple-element.42.refs_7_), channel_id=1, source_target_pairs={{0,1},{1,0},{2,3},{3,2},{4,5},{5,4},{6,7},{7,6},{16,17},{17,16},{1... | collective-permute-start | bytes 1228808 | tf_op jit(solution)/shard_map/ppermute | solution.py:429
  82.1 1.7 %collective-permute-start.36 = (bf16[160,1280]{1,0:T(8,128)(2,1)S(1)}, bf16[160,1280]{1,0:T(8,128)(2,1)S(1)}, u32[]{:S(2)}, u32[]{:S(2)}) collective-permute-start(bf16[160,1280]{1,0:T(8,128)(2,1)S(1)} %broadcast_select_fusion), channel_id=1, source_target_pairs={{0,1},{1,0},{2,3},{3,2},{4,5},{5,4},{6,7},{7,6},{8,9},{9,8},{10,11... | collective-permute-start | bytes 1228808 | tf_op jit(solution)/shard_map/ppermute | solution.py:429
  84.0 4.7 %norm_project.1 = (f32[960,1024]{1,0:T(8,128)S(1)}, bf16[1280,128]{1,0:T(8,128)(2,1)S(1)}) custom-call(s32[128]{0:T(128)S(1)} %copy-done.8, bf16[800,1024]{1,0:T(8,128)(2,1)S(1)} %get-tuple-element.27.refs_1_.refs_0_, bf16[800,128]{1,0:T(8,128)(2,1)S(1)} %get-tuple-element.31.refs_1_, bf16[160,512]{1,0:T(8,128)(2,1)S(1)} %after.9.refs_2_, ...), custom_call_target="tpu_custom_call" | custom-call | flops 2516582400 | bytes 5079040 | tf_op jit(solution)/shard_map/norm_project/pallas_call | solution.py:583
  88.7 6.1 %attention.1 = (bf16[320,128]{1,0:T(8,128)(2,1)S(1)}, bf16[320,128]{1,0:T(8,128)(2,1)S(1)}, bf16[320,128]{1,0:T(8,128)(2,1)S(1)}, bf16[1280,128]{1,0:T(8,128)(2,...) custom-call(s32[128]{0:T(128)S(1)} %copy-done.8, ...), custom_call_target="tpu_custom_call" | custom-call | flops 1258291200 | bytes 5898240 | tf_op jit(solution)/shard_map/attention/pallas_call | solution.py:607
  94.9 2.1 %collective-permute-done.36 = bf16[160,1280]{1,0:T(8,128)(2,1)S(1)} collective-permute-done((bf16[160,1280]{1,0:T(8,128)(2,1)S(1)}, bf16[160,1280]{1,0:T(8,128)(2,1)S(1)}, u32[]{:S(2)}, u32[]{:S(2)}) %collective-permute-start.36) | collective-permute-done | bytes 409632 | tf_op jit(solution)/shard_map/ppermute | solution.py:429
  97.2 1.9 %collective-permute-start.32 = (bf16[320,128]{1,0:T(8,128)(2,1)S(1)}, bf16[320,128]{1,0:T(8,128)(2,1)S(1)}, u32[]{:S(2)}, u32[]{:S(2)}) collective-permute-start(bf16[320,128]{1,0:T(8,128)(2,1)S(1)} %get-tuple-element.37), channel_id=1, source_target_pairs={{0,4},{1,5},{2,6},{3,7},{4,0},{5,1},{6,2},{7,3},{8,12},{9,13},{10,... | collective-permute-start | bytes 245768 | tf_op jit(solution)/shard_map/ppermute | solution.py:630
  99.1 1.9 %collective-permute-start.33 = (bf16[320,128]{1,0:T(8,128)(2,1)S(1)}, bf16[320,128]{1,0:T(8,128)(2,1)S(1)}, u32[]{:S(2)}, u32[]{:S(2)}) collective-permute-start(bf16[320,128]{1,0:T(8,128)(2,1)S(1)} %get-tuple-element.38), channel_id=1, source_target_pairs={{0,6},{1,7},{2,0},{3,1},{4,2},{5,3},{6,4},{7,5},{8,14},{9,15},{10,... | collective-permute-start | bytes 245768 | tf_op jit(solution)/shard_map/ppermute | solution.py:630
  101.0 2.0 %own_attention.1.refs_0_ = bf16[320,128]{1,0:T(8,128)(2,1)S(1)} custom-call(bf16[960,1024]{1,0:T(8,128)(2,1)S(1)} %get-tuple-element.34.made_ref, bf16[5,1024,64]{2,1,0:T(8,128)(2,1)S(1)} %get-tuple-element.35.key_ref), custom_call_target="tpu_custom_call" | custom-call | flops 167772160 | bytes 2621440 | tf_op jit(solution)/shard_map/own_attention/pallas_call | solution.py:631
  104.3 2.6 %collective-permute-done.32.refs_2_ = bf16[320,128]{1,0:T(8,128)(2,1)S(1)} collective-permute-done((bf16[320,128]{1,0:T(8,128)(2,1)S(1)}, bf16[320,128]{1,0:T(8,128)(2,1)S(1)}, u32[]{:S(2)}, u32[]{:S(2)}) %collective-permute-start.32) | collective-permute-done | bytes 81952 | tf_op jit(solution)/shard_map/ppermute | solution.py:630
  107.0 2.1 %project.1 = bf16[128,1280]{1,0:T(8,128)(2,1)} custom-call(bf16[320,128]{1,0:T(8,128)(2,1)S(1)} %own_attention.1.refs_0_, bf16[320,128]{1,0:T(8,128)(2,1)S(1)} %collective-permute-done.31.refs_1_, bf16[320,128]{1,0:T(8,128)(2,1)S(1)} %collective-permute-done.32.refs_2_, bf16[320,128]{1,0:T(8,128)(2,1)S(1)} %collective-permute-done.33.refs_3_, ...), custom_call_target="tpu_custom_call" | custom-call | flops 419430400 | bytes 4259840 | tf_op jit(solution)/shard_map/project/pallas_call | solution.py:648
  (85 shorter events, 26.9 us)
Async XLA Ops:
  1.0 8.1 %collective-permute-start = (bf16[64,1280]{1,0:T(8,128)(2,1)S(1)}, bf16[64,1280]{1,0:T(8,128)(2,1)S(1)}, u32[]{:S(2)}, u32[]{:S(2)}) collective-permute-start(bf16[64,1280]{1,0:T(8,128)(2,1)S(1)} %get-tuple-element.44.refs_0_), channel_id=1, source_target_pairs={{0,1},{1,3},{3,5},{5,7},{7,6},{6,4},{4,2},{2,0},{8,9},{9,11},{11,1... | collective-permute-start | bytes 491528 | tf_op jit(solution)/shard_map/ppermute | solution.py:407
  4.0 11.2 %collective-permute-start.2 = (bf16[64,1280]{1,0:T(8,128)(2,1)S(1)}, bf16[64,1280]{1,0:T(8,128)(2,1)S(1)}, u32[]{:S(2)}, u32[]{:S(2)}) collective-permute-start(bf16[64,1280]{1,0:T(8,128)(2,1)S(1)} %get-tuple-element.44.refs_0_), channel_id=1, source_target_pairs={{1,0},{3,1},{5,3},{7,5},{6,7},{4,6},{2,4},{0,2},{9,8},{11,9},{13,1... | collective-permute-start | bytes 491528 | tf_op jit(solution)/shard_map/ppermute | solution.py:407
  4.2 9.5 %collective-permute-start.1 = (bf16[64,1280]{1,0:T(8,128)(2,1)S(1)}, bf16[64,1280]{1,0:T(8,128)(2,1)S(1)}, u32[]{:S(2)}, u32[]{:S(2)}) collective-permute-start(bf16[64,1280]{1,0:T(8,128)(2,1)S(1)} %get-tuple-element.43.refs_1_), channel_id=1, source_target_pairs={{0,1},{1,3},{3,5},{5,7},{7,6},{6,4},{4,2},{2,0},{8,9},{9,11},{11,1... | collective-permute-start | bytes 491528 | tf_op jit(solution)/shard_map/ppermute | solution.py:407
  6.1 7.1 %collective-permute-start.3 = (bf16[64,1280]{1,0:T(8,128)(2,1)S(1)}, bf16[64,1280]{1,0:T(8,128)(2,1)S(1)}, u32[]{:S(2)}, u32[]{:S(2)}) collective-permute-start(bf16[64,1280]{1,0:T(8,128)(2,1)S(1)} %get-tuple-element.43.refs_1_), channel_id=1, source_target_pairs={{1,0},{3,1},{5,3},{7,5},{6,7},{4,6},{2,4},{0,2},{9,8},{11,9},{13,1... | collective-permute-start | bytes 491528 | tf_op jit(solution)/shard_map/ppermute | solution.py:407
  13.2 7.1 %collective-permute-start.7 = (bf16[64,1280]{1,0:T(8,128)(2,1)S(1)}, bf16[64,1280]{1,0:T(8,128)(2,1)S(1)}, u32[]{:S(2)}, u32[]{:S(2)}) collective-permute-start(bf16[64,1280]{1,0:T(8,128)(2,1)S(1)} %collective-permute-done.3.refs_5_), channel_id=1, source_target_pairs={{1,0},{3,1},{5,3},{7,5},{6,7},{4,6},{2,4},{0,2},{9,8},{11,9},{13,1... | collective-permute-start | bytes 491528 | tf_op jit(solution)/shard_map/ppermute | solution.py:407
  13.6 7.1 %collective-permute-start.5 = (bf16[64,1280]{1,0:T(8,128)(2,1)S(1)}, bf16[64,1280]{1,0:T(8,128)(2,1)S(1)}, u32[]{:S(2)}, u32[]{:S(2)}) collective-permute-start(bf16[64,1280]{1,0:T(8,128)(2,1)S(1)} %collective-permute-done.1.refs_3_), channel_id=1, source_target_pairs={{0,1},{1,3},{3,5},{5,7},{7,6},{6,4},{4,2},{2,0},{8,9},{9,11},{11,1... | collective-permute-start | bytes 491528 | tf_op jit(solution)/shard_map/ppermute | solution.py:407
  15.2 8.6 %collective-permute-start.6 = (bf16[64,1280]{1,0:T(8,128)(2,1)S(1)}, bf16[64,1280]{1,0:T(8,128)(2,1)S(1)}, u32[]{:S(2)}, u32[]{:S(2)}) collective-permute-start(bf16[64,1280]{1,0:T(8,128)(2,1)S(1)} %collective-permute-done.2.refs_4_), channel_id=1, source_target_pairs={{1,0},{3,1},{5,3},{7,5},{6,7},{4,6},{2,4},{0,2},{9,8},{11,9},{13,1... | collective-permute-start | bytes 491528 | tf_op jit(solution)/shard_map/ppermute | solution.py:407
  15.7 9.4 %collective-permute-start.8 = (bf16[64,1280]{1,0:T(8,128)(2,1)S(1)}, bf16[64,1280]{1,0:T(8,128)(2,1)S(1)}, u32[]{:S(2)}, u32[]{:S(2)}) collective-permute-start(bf16[64,1280]{1,0:T(8,128)(2,1)S(1)} %collective-permute-done.4.refs_6_), channel_id=1, source_target_pairs={{0,1},{1,3},{3,5},{5,7},{7,6},{6,4},{4,2},{2,0},{8,9},{9,11},{11,1... | collective-permute-start | bytes 491528 | tf_op jit(solution)/shard_map/ppermute | solution.py:407
  20.3 7.1 %collective-permute-start.11 = (bf16[64,1280]{1,0:T(8,128)(2,1)S(1)}, bf16[64,1280]{1,0:T(8,128)(2,1)S(1)}, u32[]{:S(2)}, u32[]{:S(2)}) collective-permute-start(bf16[64,1280]{1,0:T(8,128)(2,1)S(1)} %collective-permute-done.7.refs_9_), channel_id=1, source_target_pairs={{1,0},{3,1},{5,3},{7,5},{6,7},{4,6},{2,4},{0,2},{9,8},{11,9},{13,1... | collective-permute-start | bytes 491528 | tf_op jit(solution)/shard_map/ppermute | solution.py:407
  20.8 7.2 %collective-permute-start.9 = (bf16[64,1280]{1,0:T(8,128)(2,1)S(1)}, bf16[64,1280]{1,0:T(8,128)(2,1)S(1)}, u32[]{:S(2)}, u32[]{:S(2)}) collective-permute-start(bf16[64,1280]{1,0:T(8,128)(2,1)S(1)} %collective-permute-done.5.refs_7_), channel_id=1, source_target_pairs={{0,1},{1,3},{3,5},{5,7},{7,6},{6,4},{4,2},{2,0},{8,9},{9,11},{11,1... | collective-permute-start | bytes 491528 | tf_op jit(solution)/shard_map/ppermute | solution.py:407
  23.9 7.1 %collective-permute-start.10 = (bf16[64,1280]{1,0:T(8,128)(2,1)S(1)}, bf16[64,1280]{1,0:T(8,128)(2,1)S(1)}, u32[]{:S(2)}, u32[]{:S(2)}) collective-permute-start(bf16[64,1280]{1,0:T(8,128)(2,1)S(1)} %collective-permute-done.6.refs_8_), channel_id=1, source_target_pairs={{1,0},{3,1},{5,3},{7,5},{6,7},{4,6},{2,4},{0,2},{9,8},{11,9},{13,1... | collective-permute-start | bytes 491528 | tf_op jit(solution)/shard_map/ppermute | solution.py:407
  25.1 9.1 %collective-permute-start.12 = (bf16[64,1280]{1,0:T(8,128)(2,1)S(1)}, bf16[64,1280]{1,0:T(8,128)(2,1)S(1)}, u32[]{:S(2)}, u32[]{:S(2)}) collective-permute-start(bf16[64,1280]{1,0:T(8,128)(2,1)S(1)} %after.8.refs_10_.refs_2_), channel_id=1, source_target_pairs={{0,1},{1,3},{3,5},{5,7},{7,6},{6,4},{4,2},{2,0},{8,9},{9,11},{11,1... | collective-permute-start | bytes 491528 | tf_op jit(solution)/shard_map/ppermute | solution.py:407
  27.5 7.1 %collective-permute-start.13 = (bf16[64,1280]{1,0:T(8,128)(2,1)S(1)}, bf16[64,1280]{1,0:T(8,128)(2,1)S(1)}, u32[]{:S(2)}, u32[]{:S(2)}) collective-permute-start(bf16[64,1280]{1,0:T(8,128)(2,1)S(1)} %collective-permute-done.11.refs_13_.refs_5_), channel_id=1, source_target_pairs={{1,0},{3,1},{5,3},{7,5},{6,7},{4,6},{2,4},{0,2},{9,8},{11,9},{13,1... | collective-permute-start | bytes 491528 | tf_op jit(solution)/shard_map/ppermute | solution.py:407
  31.0 31.7 %collective-permute-start.26 = (bf16[240,1280]{1,0:T(8,128)(2,1)S(1)}, bf16[240,1280]{1,0:T(8,128)(2,1)S(1)}, u32[]{:S(2)}, u32[]{:S(2)}) collective-permute-start(bf16[240,1280]{1,0:T(8,128)(2,1)S(1)} %get-tuple-element.28), channel_id=1, source_target_pairs={{0,1},{1,0},{2,3},{3,2},{4,5},{5,4},{6,7},{7,6},{8,9},{9,8},{10,11... | collective-permute-start | bytes 1843208 | tf_op jit(solution)/shard_map/ppermute | solution.py:429
  32.6 23.1 %collective-permute-start.27 = (bf16[160,1280]{1,0:T(8,128)(2,1)S(1)}, bf16[160,1280]{1,0:T(8,128)(2,1)S(1)}, u32[]{:S(2)}, u32[]{:S(2)}) collective-permute-start(bf16[160,1280]{1,0:T(8,128)(2,1)S(1)} %get-tuple-element.29), channel_id=1, source_target_pairs={{0,2},{1,3},{2,4},{3,5},{4,6},{5,7},{6,0},{7,1},{8,14},{9,15},{10,... | collective-permute-start | bytes 1228808 | tf_op jit(solution)/shard_map/ppermute | solution.py:429
  40.4 7.6 %collective-permute-start.14 = (bf16[160,512]{1,0:T(8,128)(2,1)S(1)}, bf16[160,512]{1,0:T(8,128)(2,1)S(1)}, u32[]{:S(2)}, u32[]{:S(2)}) collective-permute-start(bf16[160,512]{1,0:T(8,128)(2,1)S(1)} %get-tuple-element.24.refs_0_), channel_id=1, source_target_pairs={{0,1},{1,3},{3,5},{5,7},{7,6},{6,4},{4,2},{2,0},{8,9},{9,11},{11,1... | collective-permute-start | bytes 491528 | tf_op jit(solution)/shard_map/ppermute | solution.py:407
  45.9 7.7 %collective-permute-start.18 = (bf16[160,512]{1,0:T(8,128)(2,1)S(1)}, bf16[160,512]{1,0:T(8,128)(2,1)S(1)}, u32[]{:S(2)}, u32[]{:S(2)}) collective-permute-start(bf16[160,512]{1,0:T(8,128)(2,1)S(1)} %get-tuple-element.24.refs_0_), channel_id=1, source_target_pairs={{1,0},{3,1},{5,3},{7,5},{6,7},{4,6},{2,4},{0,2},{9,8},{11,9},{13,1... | collective-permute-start | bytes 491528 | tf_op jit(solution)/shard_map/ppermute | solution.py:407
  48.0 7.5 %collective-permute-start.19 = (bf16[160,512]{1,0:T(8,128)(2,1)S(1)}, bf16[160,512]{1,0:T(8,128)(2,1)S(1)}, u32[]{:S(2)}, u32[]{:S(2)}) collective-permute-start(bf16[160,512]{1,0:T(8,128)(2,1)S(1)} %second_conv.1.refs_1_), channel_id=1, source_target_pairs={{1,0},{3,1},{5,3},{7,5},{6,7},{4,6},{2,4},{0,2},{9,8},{11,9},{13,1... | collective-permute-start | bytes 491528 | tf_op jit(solution)/shard_map/ppermute | solution.py:407
  62.7 16.8 %collective-permute-start.34 = (bf16[160,1280]{1,0:T(8,128)(2,1)S(1)}, bf16[160,1280]{1,0:T(8,128)(2,1)S(1)}, u32[]{:S(2)}, u32[]{:S(2)}) collective-permute-start(bf16[160,1280]{1,0:T(8,128)(2,1)S(1)} %get-tuple-element.40.refs_0_), channel_id=1, source_target_pairs={{0,16},{8,24},{16,0},{24,8},{1,17},{9,25},{17,1},{25,9},{2,18},{10... | collective-permute-start | bytes 1228808 | tf_op jit(solution)/shard_map/ppermute | solution.py:434
  70.1 7.2 %collective-permute-start.24 = (bf16[160,512]{1,0:T(8,128)(2,1)S(1)}, bf16[160,512]{1,0:T(8,128)(2,1)}, u32[]{:S(2)}, u32[]{:S(2)}) collective-permute-start(bf16[160,512]{1,0:T(8,128)(2,1)S(1)} %collective-permute-done.22.refs_9_.refs_5_), channel_id=1, source_target_pairs={{1,0},{3,1},{5,3},{7,5},{6,7},{4,6},{2,4},{0,2},{9,8},{11,9},{13,1... | collective-permute-start | bytes 491528 | tf_op jit(solution)/shard_map/ppermute | solution.py:407
  70.1 7.4 %collective-permute-start.29 = (bf16[160,512]{1,0:T(8,128)(2,1)S(1)}, bf16[160,512]{1,0:T(8,128)(2,1)}, u32[]{:S(2)}, u32[]{:S(2)}) collective-permute-start(bf16[160,512]{1,0:T(8,128)(2,1)S(1)} %collective-permute-done.20.refs_7_.refs_3_), channel_id=1, source_target_pairs={{0,1},{1,3},{3,5},{5,7},{7,6},{6,4},{4,2},{2,0},{8,9},{9,11},{11,1... | collective-permute-start | bytes 491528 | tf_op jit(solution)/shard_map/ppermute | solution.py:407
  72.2 7.2 %collective-permute-start.30 = (bf16[160,512]{1,0:T(8,128)(2,1)S(1)}, bf16[160,512]{1,0:T(8,128)(2,1)}, u32[]{:S(2)}, u32[]{:S(2)}) collective-permute-start(bf16[160,512]{1,0:T(8,128)(2,1)S(1)} %collective-permute-done.21.refs_8_.refs_4_), channel_id=1, source_target_pairs={{1,0},{3,1},{5,3},{7,5},{6,7},{4,6},{2,4},{0,2},{9,8},{11,9},{13,1... | collective-permute-start | bytes 491528 | tf_op jit(solution)/shard_map/ppermute | solution.py:407
  75.0 8.8 %collective-permute-start.28 = (bf16[240,1280]{1,0:T(8,128)(2,1)S(1)}, bf16[240,1280]{1,0:T(8,128)(2,1)S(1)}, u32[]{:S(2)}, u32[]{:S(2)}) collective-permute-start(bf16[240,1280]{1,0:T(8,128)(2,1)S(1)} %get-tuple-element.30.refs_9_.refs_5_), channel_id=1, source_target_pairs={{0,8},{8,0},{16,24},{24,16},{1,9},{9,1},{17,25},{25,17},{2,10},{10... | collective-permute-start | bytes 1843208 | tf_op jit(solution)/shard_map/ppermute | solution.py:434
  77.4 11.3 %collective-permute-start.23 = (bf16[160,512]{1,0:T(8,128)(2,1)S(1)}, bf16[160,512]{1,0:T(8,128)(2,1)S(1)}, u32[]{:S(2)}, u32[]{:S(2)}) collective-permute-start(bf16[160,512]{1,0:T(8,128)(2,1)S(1)} %after.9.refs_2_), channel_id=1, source_target_pairs={{0,1},{1,3},{3,5},{5,7},{7,6},{6,4},{4,2},{2,0},{8,9},{9,11},{11,1... | collective-permute-start | bytes 491528 | tf_op jit(solution)/shard_map/ppermute | solution.py:407
  77.5 11.2 %collective-permute-start.25 = (bf16[160,512]{1,0:T(8,128)(2,1)}, bf16[160,512]{1,0:T(8,128)(2,1)S(1)}, u32[]{:S(2)}, u32[]{:S(2)}) collective-permute-start(bf16[160,512]{1,0:T(8,128)(2,1)} %collective-permute-done.24.refs_5_), channel_id=1, source_target_pairs={{1,0},{3,1},{5,3},{7,5},{6,7},{4,6},{2,4},{0,2},{9,8},{11,9},{13,1... | collective-permute-start | bytes 491528 | tf_op jit(solution)/shard_map/ppermute | solution.py:407
  79.5 15.4 %collective-permute-start.37 = (bf16[160,1280]{1,0:T(8,128)(2,1)S(1)}, bf16[160,1280]{1,0:T(8,128)(2,1)S(1)}, u32[]{:S(2)}, u32[]{:S(2)}) collective-permute-start(bf16[160,1280]{1,0:T(8,128)(2,1)S(1)} %get-tuple-element.42.refs_7_), channel_id=1, source_target_pairs={{0,1},{1,0},{2,3},{3,2},{4,5},{5,4},{6,7},{7,6},{16,17},{17,16},{1... | collective-permute-start | bytes 1228808 | tf_op jit(solution)/shard_map/ppermute | solution.py:429
  82.1 14.9 %collective-permute-start.36 = (bf16[160,1280]{1,0:T(8,128)(2,1)S(1)}, bf16[160,1280]{1,0:T(8,128)(2,1)S(1)}, u32[]{:S(2)}, u32[]{:S(2)}) collective-permute-start(bf16[160,1280]{1,0:T(8,128)(2,1)S(1)} %broadcast_select_fusion), channel_id=1, source_target_pairs={{0,1},{1,0},{2,3},{3,2},{4,5},{5,4},{6,7},{7,6},{8,9},{9,8},{10,11... | collective-permute-start | bytes 1228808 | tf_op jit(solution)/shard_map/ppermute | solution.py:429
  83.9 23.1 %collective-permute-start.35 = (bf16[320,1280]{1,0:T(8,128)(2,1)S(1)}, bf16[320,1280]{1,0:T(8,128)(2,1)S(1)}, u32[]{:S(2)}, u32[]{:S(2)}) collective-permute-start(bf16[320,1280]{1,0:T(8,128)(2,1)S(1)} %pad_maximum_fusion), channel_id=1, source_target_pairs={{0,8},{8,0},{16,24},{24,16},{1,9},{9,1},{17,25},{25,17},{2,10},{10... | collective-permute-start | bytes 2457608 | tf_op jit(solution)/shard_map/ppermute | solution.py:434
  97.1 9.9 %collective-permute-start.38 = (bf16[320,1280]{1,0:T(8,128)(2,1)S(1)}, bf16[320,1280]{1,0:T(8,128)(2,1)S(1)}, u32[]{:S(2)}, u32[]{:S(2)}) collective-permute-start(bf16[320,1280]{1,0:T(8,128)(2,1)S(1)} %after.13.refs_9_), channel_id=1, source_target_pairs={{0,8},{8,0},{16,24},{24,16},{1,9},{9,1},{17,25},{25,17},{2,10},{10... | collective-permute-start | bytes 2457608 | tf_op jit(solution)/shard_map/ppermute | solution.py:434
  97.1 7.2 %collective-permute-start.31 = (bf16[320,128]{1,0:T(8,128)(2,1)S(1)}, bf16[320,128]{1,0:T(8,128)(2,1)S(1)}, u32[]{:S(2)}, u32[]{:S(2)}) collective-permute-start(bf16[320,128]{1,0:T(8,128)(2,1)S(1)} %get-tuple-element.36.refs_1_), channel_id=1, source_target_pairs={{0,2},{1,3},{2,4},{3,5},{4,6},{5,7},{6,0},{7,1},{8,10},{9,11},{10,... | collective-permute-start | bytes 245768 | tf_op jit(solution)/shard_map/ppermute | solution.py:630
  97.2 9.8 %collective-permute-start.32 = (bf16[320,128]{1,0:T(8,128)(2,1)S(1)}, bf16[320,128]{1,0:T(8,128)(2,1)S(1)}, u32[]{:S(2)}, u32[]{:S(2)}) collective-permute-start(bf16[320,128]{1,0:T(8,128)(2,1)S(1)} %get-tuple-element.37), channel_id=1, source_target_pairs={{0,4},{1,5},{2,6},{3,7},{4,0},{5,1},{6,2},{7,3},{8,12},{9,13},{10,... | collective-permute-start | bytes 245768 | tf_op jit(solution)/shard_map/ppermute | solution.py:630
  99.1 7.8 %collective-permute-start.33 = (bf16[320,128]{1,0:T(8,128)(2,1)S(1)}, bf16[320,128]{1,0:T(8,128)(2,1)S(1)}, u32[]{:S(2)}, u32[]{:S(2)}) collective-permute-start(bf16[320,128]{1,0:T(8,128)(2,1)S(1)} %get-tuple-element.38), channel_id=1, source_target_pairs={{0,6},{1,7},{2,0},{3,1},{4,2},{5,3},{6,4},{7,5},{8,14},{9,15},{10,... | collective-permute-start | bytes 245768 | tf_op jit(solution)/shard_map/ppermute | solution.py:630
  (16 other events, 116.2 us)

commit v14 on v12

--- a/solution.py
+++ b/solution.py
@@ -506,7 +506,8 @@
     pieces = gather(halves, n, beside_first)
     stats = made_beside[0]
     if inner == 2:
-        chosen, out_own = after(chosen + [w_out], pieces[-6:-2])
+        (chosen,) = after(chosen, pieces[6:10])
+        (out_own,) = after([w_out], pieces[-6:-2])
         chosen = send(chosen, [(0, 1)])
         far = send(out_own, FAR)
     else:

time: 104 us -> 104 us (level)
  starting transfers between devices: 48.4 us -> 45.8 us
  waiting for transfers between devices: 26.6 us -> 28.5 us
    ppermute x28, waiting for transfers between devices: 20.4 us -> 22.7 us  [gather(): lax.ppermute(found[half, sign * (step - 1)], 'patch', pairs)]
    ppermute x4, starting transfers between devices: 5.13 us -> 3.22 us  [swap(): return lax.ppermute(block, 'batch', pairs)]
    ppermute x4, starting transfers between devices: 7.46 us -> 5.94 us  [send(): return lax.ppermute(block, ('batch', 'patch'), pairs)]
  transfers between devices with their start and end apart: 39 -> 39, of which waited for: 16 -> 19; matrix products, arithmetic and copies ran while one was open for 2% -> 2% of each run, Pallas kernels for 23% -> 23%
where the time goes in v14:
time: 104 us; the launch traced here: 103 us
  starting transfers between devices  45.8 us (44%)
  waiting for transfers between devices  28.5 us (27%)
  Pallas kernels  26.1 us (25%)
  other arithmetic  1.72 us (2%)
  local copies, waits for them, and re-layouts  1.07 us (1%)
    ppermute x28, starting transfers between devices, gather(): lax.ppermute(found[half, sign * (step - 1)], 'patch', pairs)  32.1 us
    ppermute x28, waiting for transfers between devices, gather(): lax.ppermute(found[half, sign * (step - 1)], 'patch', pairs)  22.7 us
    pallas_call x1, Pallas kernels, on_device(): pl.pallas_call(functools.partial(attention_kernel, 2 * n, inner), out_sha...  6.14 us
    ppermute x4, starting transfers between devices, send(): return lax.ppermute(block, ('batch', 'patch'), pairs)  5.94 us
    pallas_call x1, Pallas kernels, on_device(): pl.pallas_call(functools.partial(conv_kernel, columns), out_shape=[half_h...  5.8 us
    pallas_call x1, Pallas kernels, on_device(): pl.pallas_call(functools.partial(project_kernel, 2 * n), out_shape=[jax.S...  4.68 us
    ppermute x3, starting transfers between devices, on_device(): received.append(lax.ppermute(sent_block, 'patch', pairs))  4.53 us
    ppermute x3, waiting for transfers between devices, on_device(): received.append(lax.ppermute(sent_block, 'patch', pairs))  3.5 us
  transfers between devices with their start and end apart: 39, of which 19 were waited for; matrix products, arithmetic and copies ran while one was open for 2% of the time, Pallas kernels for 23%

profile of v14, /device:TPU:0, one launch (start us, length us, event | category | flops | bytes accessed | tf_op | source)
XLA Modules:
  0.0 103.4 jit_solution(10131202702286023246)
XLA Ops:
  1.0 3.0 %collective-permute-start = (bf16[64,1280]{1,0:T(8,128)(2,1)S(1)}, bf16[64,1280]{1,0:T(8,128)(2,1)S(1)}, u32[]{:S(2)}, u32[]{:S(2)}) collective-permute-start(bf16[64,1280]{1,0:T(8,128)(2,1)S(1)} %get-tuple-element.40.refs_0_), channel_id=1, source_target_pairs={{0,1},{1,3},{3,5},{5,7},{7,6},{6,4},{4,2},{2,0},{8,9},{9,11},{11,1... | collective-permute-start | bytes 491528 | tf_op jit(solution)/shard_map/ppermute | solution.py:407
  4.2 1.9 %collective-permute-start.1 = (bf16[64,1280]{1,0:T(8,128)(2,1)S(1)}, bf16[64,1280]{1,0:T(8,128)(2,1)S(1)}, u32[]{:S(2)}, u32[]{:S(2)}) collective-permute-start(bf16[64,1280]{1,0:T(8,128)(2,1)S(1)} %get-tuple-element.39.refs_1_), channel_id=1, source_target_pairs={{0,1},{1,3},{3,5},{5,7},{7,6},{6,4},{4,2},{2,0},{8,9},{9,11},{11,1... | collective-permute-start | bytes 491528 | tf_op jit(solution)/shard_map/ppermute | solution.py:407
  9.1 2.0 %collective-permute-start.4 = (bf16[64,1280]{1,0:T(8,128)(2,1)S(1)}, bf16[64,1280]{1,0:T(8,128)(2,1)S(1)}, u32[]{:S(2)}, u32[]{:S(2)}) collective-permute-start(bf16[64,1280]{1,0:T(8,128)(2,1)S(1)} %after.8.refs_2_), channel_id=1, source_target_pairs={{0,1},{1,3},{3,5},{5,7},{7,6},{6,4},{4,2},{2,0},{8,9},{9,11},{11,1... | collective-permute-start | bytes 491528 | tf_op jit(solution)/shard_map/ppermute | solution.py:407
  11.1 2.1 %collective-permute-done.3.refs_5_ = bf16[64,1280]{1,0:T(8,128)(2,1)S(1)} collective-permute-done((bf16[64,1280]{1,0:T(8,128)(2,1)S(1)}, bf16[64,1280]{1,0:T(8,128)(2,1)S(1)}, u32[]{:S(2)}, u32[]{:S(2)}) %collective-permute-start.3) | collective-permute-done | bytes 163872 | tf_op jit(solution)/shard_map/ppermute | solution.py:407
  13.6 1.6 %collective-permute-start.5 = (bf16[64,1280]{1,0:T(8,128)(2,1)S(1)}, bf16[64,1280]{1,0:T(8,128)(2,1)S(1)}, u32[]{:S(2)}, u32[]{:S(2)}) collective-permute-start(bf16[64,1280]{1,0:T(8,128)(2,1)S(1)} %collective-permute-done.1.refs_3_), channel_id=1, source_target_pairs={{0,1},{1,3},{3,5},{5,7},{7,6},{6,4},{4,2},{2,0},{8,9},{9,11},{11,1... | collective-permute-start | bytes 491528 | tf_op jit(solution)/shard_map/ppermute | solution.py:407
  15.7 2.1 %collective-permute-start.8 = (bf16[64,1280]{1,0:T(8,128)(2,1)S(1)}, bf16[64,1280]{1,0:T(8,128)(2,1)S(1)}, u32[]{:S(2)}, u32[]{:S(2)}) collective-permute-start(bf16[64,1280]{1,0:T(8,128)(2,1)S(1)} %collective-permute-done.4.refs_6_.refs_1_), channel_id=1, source_target_pairs={{0,1},{1,3},{3,5},{5,7},{7,6},{6,4},{4,2},{2,0},{8,9},{9,11},{11,1... | collective-permute-start | bytes 491528 | tf_op jit(solution)/shard_map/ppermute | solution.py:407
  17.7 2.6 %collective-permute-done.7.refs_9_.refs_4_ = bf16[64,1280]{1,0:T(8,128)(2,1)S(1)} collective-permute-done((bf16[64,1280]{1,0:T(8,128)(2,1)S(1)}, bf16[64,1280]{1,0:T(8,128)(2,1)S(1)}, u32[]{:S(2)}, u32[]{:S(2)}) %collective-permute-start.7) | collective-permute-done | bytes 163872 | tf_op jit(solution)/shard_map/ppermute | solution.py:407
  25.1 1.7 %collective-permute-start.12 = (bf16[64,1280]{1,0:T(8,128)(2,1)S(1)}, bf16[64,1280]{1,0:T(8,128)(2,1)S(1)}, u32[]{:S(2)}, u32[]{:S(2)}) collective-permute-start(bf16[64,1280]{1,0:T(8,128)(2,1)S(1)} %after.9.refs_10_.refs_1_), channel_id=1, source_target_pairs={{0,1},{1,3},{3,5},{5,7},{7,6},{6,4},{4,2},{2,0},{8,9},{9,11},{11,1... | collective-permute-start | bytes 491528 | tf_op jit(solution)/shard_map/ppermute | solution.py:407
  27.9 1.6 %collective-permute-start.26 = (bf16[240,1280]{1,0:T(8,128)(2,1)S(1)}, bf16[240,1280]{1,0:T(8,128)(2,1)S(1)}, u32[]{:S(2)}, u32[]{:S(2)}) collective-permute-start(bf16[240,1280]{1,0:T(8,128)(2,1)S(1)} %after.11), channel_id=1, source_target_pairs={{0,1},{1,0},{2,3},{3,2},{4,5},{5,4},{6,7},{7,6},{8,9},{9,8},{10,11... | collective-permute-start | bytes 1843208 | tf_op jit(solution)/shard_map/ppermute | solution.py:429
  29.6 2.2 %collective-permute-done.10.refs_12_.refs_3_ = bf16[64,1280]{1,0:T(8,128)(2,1)S(1)} collective-permute-done((bf16[64,1280]{1,0:T(8,128)(2,1)S(1)}, bf16[64,1280]{1,0:T(8,128)(2,1)S(1)}, u32[]{:S(2)}, u32[]{:S(2)}) %collective-permute-start.10) | collective-permute-done | bytes 163872 | tf_op jit(solution)/shard_map/ppermute | solution.py:407
  32.2 3.1 %collective-permute-done.13.refs_15_ = bf16[64,1280]{1,0:T(8,128)(2,1)S(1)} collective-permute-done((bf16[64,1280]{1,0:T(8,128)(2,1)S(1)}, bf16[64,1280]{1,0:T(8,128)(2,1)S(1)}, u32[]{:S(2)}, u32[]{:S(2)}) %collective-permute-start.13) | collective-permute-done | bytes 163872 | tf_op jit(solution)/shard_map/ppermute | solution.py:407
  35.3 5.8 %norm_conv.1 = (bf16[160,512]{1,0:T(8,128)(2,1)S(1)}, bf16[1152,1280]{1,0:T(8,128)(2,1)S(1)}, f32[160,1024]{1,0:T(8,128)S(1)}) custom-call(s32[128]{0:T(128)S(1)} %copy-done.6, bf16[64,1280]{1,0:T(8,128)(2,1)S(1)} %get-tuple-element.40.refs_0_, bf16[64,1280]{1,0:T(8,128)(2,1)S(1)} %get-tuple-element.39.refs_1_, bf16[64,1280]{1,0:T(8,128)(2,1)S(1)} %after.8.refs_2_, ...), custom_call_target="tpu_custom_call" | custom-call | flops 1887436800 | bytes 6307840 | tf_op jit(solution)/shard_map/norm_conv/pallas_call | solution.py:524
  42.7 2.2 %second_conv.1.refs_1_ = bf16[160,512]{1,0:T(8,128)(2,1)S(1)} custom-call(bf16[1152,1280]{1,0:T(8,128)(2,1)S(1)} %get-tuple-element.23.act_ref, f32[160,1024]{1,0:T(8,128)S(1)} %get-tuple-element.24.kept_ref, bf16[3,480,1280]{2,1,0:T(8,128)(2,1)S(1)} %bitcast.8, f32[1,160]{1,0:T(1,128)S(1)} %bitcast.10), custom_call_target="tpu_custom_call" | custom-call | flops 1887436800 | bytes 1887436 | tf_op jit(solution)/shard_map/second_conv/pallas_call | solution.py:541
  45.0 1.6 %collective-permute-start.17 = (bf16[160,512]{1,0:T(8,128)(2,1)S(1)}, bf16[160,512]{1,0:T(8,128)(2,1)S(1)}, u32[]{:S(2)}, u32[]{:S(2)}) collective-permute-start(bf16[160,512]{1,0:T(8,128)(2,1)S(1)} %second_conv.1.refs_1_), channel_id=1, source_target_pairs={{0,1},{1,3},{3,5},{5,7},{7,6},{6,4},{4,2},{2,0},{8,9},{9,11},{11,1... | collective-permute-start | bytes 491528 | tf_op jit(solution)/shard_map/ppermute | solution.py:407
  47.5 2.8 %collective-permute-done.17.refs_3_ = bf16[160,512]{1,0:T(8,128)(2,1)S(1)} collective-permute-done((bf16[160,512]{1,0:T(8,128)(2,1)S(1)}, bf16[160,512]{1,0:T(8,128)(2,1)S(1)}, u32[]{:S(2)}, u32[]{:S(2)}) %collective-permute-start.17) | collective-permute-done | bytes 163872 | tf_op jit(solution)/shard_map/ppermute | solution.py:407
  50.3 2.8 %collective-permute-start.34 = (bf16[160,1280]{1,0:T(8,128)(2,1)S(1)}, bf16[160,1280]{1,0:T(8,128)(2,1)S(1)}, u32[]{:S(2)}, u32[]{:S(2)}) collective-permute-start(bf16[160,1280]{1,0:T(8,128)(2,1)S(1)} %get-tuple-element.36.refs_0_), channel_id=1, source_target_pairs={{0,16},{8,24},{16,0},{24,8},{1,17},{9,25},{17,1},{25,9},{2,18},{10... | collective-permute-start | bytes 1228808 | tf_op jit(solution)/shard_map/ppermute | solution.py:434
  53.1 2.5 %collective-permute-start.15 = (bf16[160,512]{1,0:T(8,128)(2,1)S(1)}, bf16[160,512]{1,0:T(8,128)(2,1)}, u32[]{:S(2)}, u32[]{:S(2)}) collective-permute-start(bf16[160,512]{1,0:T(8,128)(2,1)S(1)} %collective-permute-done.14.refs_2_), channel_id=1, source_target_pairs={{0,1},{1,3},{3,5},{5,7},{7,6},{6,4},{4,2},{2,0},{8,9},{9,11},{11,1... | collective-permute-start | bytes 491528 | tf_op jit(solution)/shard_map/ppermute | solution.py:407
  55.7 2.0 %collective-permute-start.20 = (bf16[160,512]{1,0:T(8,128)(2,1)S(1)}, bf16[160,512]{1,0:T(8,128)(2,1)S(1)}, u32[]{:S(2)}, u32[]{:S(2)}) collective-permute-start(bf16[160,512]{1,0:T(8,128)(2,1)S(1)} %collective-permute-done.17.refs_3_), channel_id=1, source_target_pairs={{0,1},{1,3},{3,5},{5,7},{7,6},{6,4},{4,2},{2,0},{8,9},{9,11},{11,1... | collective-permute-start | bytes 491528 | tf_op jit(solution)/shard_map/ppermute | solution.py:407
  57.7 2.3 %collective-permute-done.15.refs_6_ = bf16[160,512]{1,0:T(8,128)(2,1)} collective-permute-done((bf16[160,512]{1,0:T(8,128)(2,1)S(1)}, bf16[160,512]{1,0:T(8,128)(2,1)}, u32[]{:S(2)}, u32[]{:S(2)}) %collective-permute-start.15) | collective-permute-done | bytes 163872 | tf_op jit(solution)/shard_map/ppermute | solution.py:407
  60.0 2.5 %collective-permute-start.16 = (bf16[160,512]{1,0:T(8,128)(2,1)}, bf16[160,512]{1,0:T(8,128)(2,1)S(1)}, u32[]{:S(2)}, u32[]{:S(2)}) collective-permute-start(bf16[160,512]{1,0:T(8,128)(2,1)} %collective-permute-done.15.refs_6_), channel_id=1, source_target_pairs={{0,1},{1,3},{3,5},{5,7},{7,6},{6,4},{4,2},{2,0},{8,9},{9,11},{11,1... | collective-permute-start | bytes 491528 | tf_op jit(solution)/shard_map/ppermute | solution.py:407
  63.4 2.5 %collective-permute-start.29 = (bf16[160,512]{1,0:T(8,128)(2,1)S(1)}, bf16[160,512]{1,0:T(8,128)(2,1)}, u32[]{:S(2)}, u32[]{:S(2)}) collective-permute-start(bf16[160,512]{1,0:T(8,128)(2,1)S(1)} %collective-permute-done.20.refs_7_), channel_id=1, source_target_pairs={{0,1},{1,3},{3,5},{5,7},{7,6},{6,4},{4,2},{2,0},{8,9},{9,11},{11,1... | collective-permute-start | bytes 491528 | tf_op jit(solution)/shard_map/ppermute | solution.py:407
  66.1 2.5 %early_norm.1 = (bf16[800,1024]{1,0:T(8,128)(2,1)S(1)}, bf16[800,128]{1,0:T(8,128)(2,1)S(1)}) custom-call(bf16[160,512]{1,0:T(8,128)(2,1)S(1)} %get-tuple-element.22.refs_0_, bf16[160,512]{1,0:T(8,128)(2,1)S(1)} %second_conv.1.refs_1_, bf16[160,512]{1,0:T(8,128)(2,1)S(1)} %collective-permute-done.14.refs_2_, ...), custom_call_target="tpu_custom_call" | custom-call | flops 10485760 | bytes 5242880 | tf_op jit(solution)/shard_map/early_norm/pallas_call | solution.py:556
  73.4 2.3 %collective-permute-start.37 = (bf16[160,1280]{1,0:T(8,128)(2,1)S(1)}, bf16[160,1280]{1,0:T(8,128)(2,1)S(1)}, u32[]{:S(2)}, u32[]{:S(2)}) collective-permute-start(bf16[160,1280]{1,0:T(8,128)(2,1)S(1)} %get-tuple-element.38.refs_7_), channel_id=1, source_target_pairs={{0,1},{1,0},{2,3},{3,2},{4,5},{5,4},{6,7},{7,6},{16,17},{17,16},{1... | collective-permute-start | bytes 1228808 | tf_op jit(solution)/shard_map/ppermute | solution.py:429
  75.7 2.1 %collective-permute-start.36 = (bf16[160,1280]{1,0:T(8,128)(2,1)S(1)}, bf16[160,1280]{1,0:T(8,128)(2,1)S(1)}, u32[]{:S(2)}, u32[]{:S(2)}) collective-permute-start(bf16[160,1280]{1,0:T(8,128)(2,1)S(1)} %broadcast_select_fusion), channel_id=1, source_target_pairs={{0,1},{1,0},{2,3},{3,2},{4,5},{5,4},{6,7},{7,6},{8,9},{9,8},{10,11... | collective-permute-start | bytes 1228808 | tf_op jit(solution)/shard_map/ppermute | solution.py:429
  77.9 4.7 %norm_project.1 = (f32[960,1024]{1,0:T(8,128)S(1)}, bf16[1280,128]{1,0:T(8,128)(2,1)S(1)}) custom-call(s32[128]{0:T(128)S(1)} %copy-done.6, bf16[800,1024]{1,0:T(8,128)(2,1)S(1)} %get-tuple-element.25.refs_1_.refs_0_, bf16[800,128]{1,0:T(8,128)(2,1)S(1)} %get-tuple-element.27.refs_1_, bf16[160,512]{1,0:T(8,128)(2,1)S(1)} %after.10.refs_2_, ...), custom_call_target="tpu_custom_call" | custom-call | flops 2516582400 | bytes 5079040 | tf_op jit(solution)/shard_map/norm_project/pallas_call | solution.py:584
  82.6 6.1 %attention.1 = (bf16[320,128]{1,0:T(8,128)(2,1)S(1)}, bf16[320,128]{1,0:T(8,128)(2,1)S(1)}, bf16[320,128]{1,0:T(8,128)(2,1)S(1)}, bf16[1280,128]{1,0:T(8,128)(2,...) custom-call(s32[128]{0:T(128)S(1)} %copy-done.6, ...), custom_call_target="tpu_custom_call" | custom-call | flops 1258291200 | bytes 5898240 | tf_op jit(solution)/shard_map/attention/pallas_call | solution.py:608
  88.8 2.3 %collective-permute-done.36 = bf16[160,1280]{1,0:T(8,128)(2,1)S(1)} collective-permute-done((bf16[160,1280]{1,0:T(8,128)(2,1)S(1)}, bf16[160,1280]{1,0:T(8,128)(2,1)S(1)}, u32[]{:S(2)}, u32[]{:S(2)}) %collective-permute-start.36) | collective-permute-done | bytes 409632 | tf_op jit(solution)/shard_map/ppermute | solution.py:429
  91.5 2.0 %collective-permute-start.32 = (bf16[320,128]{1,0:T(8,128)(2,1)S(1)}, bf16[320,128]{1,0:T(8,128)(2,1)S(1)}, u32[]{:S(2)}, u32[]{:S(2)}) collective-permute-start(bf16[320,128]{1,0:T(8,128)(2,1)S(1)} %get-tuple-element.33), channel_id=1, source_target_pairs={{0,4},{1,5},{2,6},{3,7},{4,0},{5,1},{6,2},{7,3},{8,12},{9,13},{10,... | collective-permute-start | bytes 245768 | tf_op jit(solution)/shard_map/ppermute | solution.py:631
  93.5 2.3 %collective-permute-start.33 = (bf16[320,128]{1,0:T(8,128)(2,1)S(1)}, bf16[320,128]{1,0:T(8,128)(2,1)S(1)}, u32[]{:S(2)}, u32[]{:S(2)}) collective-permute-start(bf16[320,128]{1,0:T(8,128)(2,1)S(1)} %get-tuple-element.34), channel_id=1, source_target_pairs={{0,6},{1,7},{2,0},{3,1},{4,2},{5,3},{6,4},{7,5},{8,14},{9,15},{10,... | collective-permute-start | bytes 245768 | tf_op jit(solution)/shard_map/ppermute | solution.py:631
  95.8 1.9 %own_attention.1.refs_0_ = bf16[320,128]{1,0:T(8,128)(2,1)S(1)} custom-call(bf16[960,1024]{1,0:T(8,128)(2,1)S(1)} %get-tuple-element.30.made_ref, bf16[5,1024,64]{2,1,0:T(8,128)(2,1)S(1)} %get-tuple-element.31.key_ref), custom_call_target="tpu_custom_call" | custom-call | flops 167772160 | bytes 2621440 | tf_op jit(solution)/shard_map/own_attention/pallas_call | solution.py:632
  98.4 2.8 %collective-permute-done.32.refs_2_ = bf16[320,128]{1,0:T(8,128)(2,1)S(1)} collective-permute-done((bf16[320,128]{1,0:T(8,128)(2,1)S(1)}, bf16[320,128]{1,0:T(8,128)(2,1)S(1)}, u32[]{:S(2)}, u32[]{:S(2)}) %collective-permute-start.32) | collective-permute-done | bytes 81952 | tf_op jit(solution)/shard_map/ppermute | solution.py:631
  101.2 2.1 %project.1 = bf16[128,1280]{1,0:T(8,128)(2,1)} custom-call(bf16[320,128]{1,0:T(8,128)(2,1)S(1)} %own_attention.1.refs_0_, bf16[320,128]{1,0:T(8,128)(2,1)S(1)} %collective-permute-done.31.refs_1_, bf16[320,128]{1,0:T(8,128)(2,1)S(1)} %collective-permute-done.32.refs_2_, bf16[320,128]{1,0:T(8,128)(2,1)S(1)} %collective-permute-done.33.refs_3_, ...), custom_call_target="tpu_custom_call" | custom-call | flops 419430400 | bytes 4259840 | tf_op jit(solution)/shard_map/project/pallas_call | solution.py:649
  (82 shorter events, 21.1 us)
Async XLA Ops:
  1.0 8.1 %collective-permute-start = (bf16[64,1280]{1,0:T(8,128)(2,1)S(1)}, bf16[64,1280]{1,0:T(8,128)(2,1)S(1)}, u32[]{:S(2)}, u32[]{:S(2)}) collective-permute-start(bf16[64,1280]{1,0:T(8,128)(2,1)S(1)} %get-tuple-element.40.refs_0_), channel_id=1, source_target_pairs={{0,1},{1,3},{3,5},{5,7},{7,6},{6,4},{4,2},{2,0},{8,9},{9,11},{11,1... | collective-permute-start | bytes 491528 | tf_op jit(solution)/shard_map/ppermute | solution.py:407
  4.0 11.2 %collective-permute-start.2 = (bf16[64,1280]{1,0:T(8,128)(2,1)S(1)}, bf16[64,1280]{1,0:T(8,128)(2,1)S(1)}, u32[]{:S(2)}, u32[]{:S(2)}) collective-permute-start(bf16[64,1280]{1,0:T(8,128)(2,1)S(1)} %get-tuple-element.40.refs_0_), channel_id=1, source_target_pairs={{1,0},{3,1},{5,3},{7,5},{6,7},{4,6},{2,4},{0,2},{9,8},{11,9},{13,1... | collective-permute-start | bytes 491528 | tf_op jit(solution)/shard_map/ppermute | solution.py:407
  4.2 9.5 %collective-permute-start.1 = (bf16[64,1280]{1,0:T(8,128)(2,1)S(1)}, bf16[64,1280]{1,0:T(8,128)(2,1)S(1)}, u32[]{:S(2)}, u32[]{:S(2)}) collective-permute-start(bf16[64,1280]{1,0:T(8,128)(2,1)S(1)} %get-tuple-element.39.refs_1_), channel_id=1, source_target_pairs={{0,1},{1,3},{3,5},{5,7},{7,6},{6,4},{4,2},{2,0},{8,9},{9,11},{11,1... | collective-permute-start | bytes 491528 | tf_op jit(solution)/shard_map/ppermute | solution.py:407
  6.1 7.1 %collective-permute-start.3 = (bf16[64,1280]{1,0:T(8,128)(2,1)S(1)}, bf16[64,1280]{1,0:T(8,128)(2,1)S(1)}, u32[]{:S(2)}, u32[]{:S(2)}) collective-permute-start(bf16[64,1280]{1,0:T(8,128)(2,1)S(1)} %get-tuple-element.39.refs_1_), channel_id=1, source_target_pairs={{1,0},{3,1},{5,3},{7,5},{6,7},{4,6},{2,4},{0,2},{9,8},{11,9},{13,1... | collective-permute-start | bytes 491528 | tf_op jit(solution)/shard_map/ppermute | solution.py:407
  13.6 7.1 %collective-permute-start.5 = (bf16[64,1280]{1,0:T(8,128)(2,1)S(1)}, bf16[64,1280]{1,0:T(8,128)(2,1)S(1)}, u32[]{:S(2)}, u32[]{:S(2)}) collective-permute-start(bf16[64,1280]{1,0:T(8,128)(2,1)S(1)} %collective-permute-done.1.refs_3_), channel_id=1, source_target_pairs={{0,1},{1,3},{3,5},{5,7},{7,6},{6,4},{4,2},{2,0},{8,9},{9,11},{11,1... | collective-permute-start | bytes 491528 | tf_op jit(solution)/shard_map/ppermute | solution.py:407
  15.2 8.6 %collective-permute-start.6 = (bf16[64,1280]{1,0:T(8,128)(2,1)S(1)}, bf16[64,1280]{1,0:T(8,128)(2,1)S(1)}, u32[]{:S(2)}, u32[]{:S(2)}) collective-permute-start(bf16[64,1280]{1,0:T(8,128)(2,1)S(1)} %collective-permute-done.2.refs_4_), channel_id=1, source_target_pairs={{1,0},{3,1},{5,3},{7,5},{6,7},{4,6},{2,4},{0,2},{9,8},{11,9},{13,1... | collective-permute-start | bytes 491528 | tf_op jit(solution)/shard_map/ppermute | solution.py:407
  15.7 9.4 %collective-permute-start.8 = (bf16[64,1280]{1,0:T(8,128)(2,1)S(1)}, bf16[64,1280]{1,0:T(8,128)(2,1)S(1)}, u32[]{:S(2)}, u32[]{:S(2)}) collective-permute-start(bf16[64,1280]{1,0:T(8,128)(2,1)S(1)} %collective-permute-done.4.refs_6_.refs_1_), channel_id=1, source_target_pairs={{0,1},{1,3},{3,5},{5,7},{7,6},{6,4},{4,2},{2,0},{8,9},{9,11},{11,1... | collective-permute-start | bytes 491528 | tf_op jit(solution)/shard_map/ppermute | solution.py:407
  20.3 7.1 %collective-permute-start.11 = (bf16[64,1280]{1,0:T(8,128)(2,1)S(1)}, bf16[64,1280]{1,0:T(8,128)(2,1)S(1)}, u32[]{:S(2)}, u32[]{:S(2)}) collective-permute-start(bf16[64,1280]{1,0:T(8,128)(2,1)S(1)} %collective-permute-done.7.refs_9_.refs_4_), channel_id=1, source_target_pairs={{1,0},{3,1},{5,3},{7,5},{6,7},{4,6},{2,4},{0,2},{9,8},{11,9},{13,1... | collective-permute-start | bytes 491528 | tf_op jit(solution)/shard_map/ppermute | solution.py:407
  20.8 8.8 %collective-permute-start.9 = (bf16[64,1280]{1,0:T(8,128)(2,1)S(1)}, bf16[64,1280]{1,0:T(8,128)(2,1)S(1)}, u32[]{:S(2)}, u32[]{:S(2)}) collective-permute-start(bf16[64,1280]{1,0:T(8,128)(2,1)S(1)} %collective-permute-done.5.refs_7_.refs_2_), channel_id=1, source_target_pairs={{0,1},{1,3},{3,5},{5,7},{7,6},{6,4},{4,2},{2,0},{8,9},{9,11},{11,1... | collective-permute-start | bytes 491528 | tf_op jit(solution)/shard_map/ppermute | solution.py:407
  24.6 7.2 %collective-permute-start.10 = (bf16[64,1280]{1,0:T(8,128)(2,1)S(1)}, bf16[64,1280]{1,0:T(8,128)(2,1)S(1)}, u32[]{:S(2)}, u32[]{:S(2)}) collective-permute-start(bf16[64,1280]{1,0:T(8,128)(2,1)S(1)} %collective-permute-done.6.refs_8_.refs_3_), channel_id=1, source_target_pairs={{1,0},{3,1},{5,3},{7,5},{6,7},{4,6},{2,4},{0,2},{9,8},{11,9},{13,1... | collective-permute-start | bytes 491528 | tf_op jit(solution)/shard_map/ppermute | solution.py:407
  27.5 7.8 %collective-permute-start.13 = (bf16[64,1280]{1,0:T(8,128)(2,1)S(1)}, bf16[64,1280]{1,0:T(8,128)(2,1)S(1)}, u32[]{:S(2)}, u32[]{:S(2)}) collective-permute-start(bf16[64,1280]{1,0:T(8,128)(2,1)S(1)} %collective-permute-done.11.refs_13_.refs_4_), channel_id=1, source_target_pairs={{1,0},{3,1},{5,3},{7,5},{6,7},{4,6},{2,4},{0,2},{9,8},{11,9},{13,1... | collective-permute-start | bytes 491528 | tf_op jit(solution)/shard_map/ppermute | solution.py:407
  27.9 22.4 %collective-permute-start.26 = (bf16[240,1280]{1,0:T(8,128)(2,1)S(1)}, bf16[240,1280]{1,0:T(8,128)(2,1)S(1)}, u32[]{:S(2)}, u32[]{:S(2)}) collective-permute-start(bf16[240,1280]{1,0:T(8,128)(2,1)S(1)} %after.11), channel_id=1, source_target_pairs={{0,1},{1,0},{2,3},{3,2},{4,5},{5,4},{6,7},{7,6},{8,9},{9,8},{10,11... | collective-permute-start | bytes 1843208 | tf_op jit(solution)/shard_map/ppermute | solution.py:429
  31.8 18.5 %collective-permute-start.27 = (bf16[160,1280]{1,0:T(8,128)(2,1)S(1)}, bf16[160,1280]{1,0:T(8,128)(2,1)S(1)}, u32[]{:S(2)}, u32[]{:S(2)}) collective-permute-start(bf16[160,1280]{1,0:T(8,128)(2,1)S(1)} %after.12), channel_id=1, source_target_pairs={{0,2},{1,3},{2,4},{3,5},{4,6},{5,7},{6,0},{7,1},{8,14},{9,15},{10,... | collective-permute-start | bytes 1228808 | tf_op jit(solution)/shard_map/ppermute | solution.py:429
  46.6 9.1 %collective-permute-start.19 = (bf16[160,512]{1,0:T(8,128)(2,1)S(1)}, bf16[160,512]{1,0:T(8,128)(2,1)S(1)}, u32[]{:S(2)}, u32[]{:S(2)}) collective-permute-start(bf16[160,512]{1,0:T(8,128)(2,1)S(1)} %second_conv.1.refs_1_), channel_id=1, source_target_pairs={{1,0},{3,1},{5,3},{7,5},{6,7},{4,6},{2,4},{0,2},{9,8},{11,9},{13,1... | collective-permute-start | bytes 491528 | tf_op jit(solution)/shard_map/ppermute | solution.py:407
  47.0 10.6 %collective-permute-start.18 = (bf16[160,512]{1,0:T(8,128)(2,1)S(1)}, bf16[160,512]{1,0:T(8,128)(2,1)S(1)}, u32[]{:S(2)}, u32[]{:S(2)}) collective-permute-start(bf16[160,512]{1,0:T(8,128)(2,1)S(1)} %get-tuple-element.22.refs_0_), channel_id=1, source_target_pairs={{1,0},{3,1},{5,3},{7,5},{6,7},{4,6},{2,4},{0,2},{9,8},{11,9},{13,1... | collective-permute-start | bytes 491528 | tf_op jit(solution)/shard_map/ppermute | solution.py:407
  50.3 23.0 %collective-permute-start.34 = (bf16[160,1280]{1,0:T(8,128)(2,1)S(1)}, bf16[160,1280]{1,0:T(8,128)(2,1)S(1)}, u32[]{:S(2)}, u32[]{:S(2)}) collective-permute-start(bf16[160,1280]{1,0:T(8,128)(2,1)S(1)} %get-tuple-element.36.refs_0_), channel_id=1, source_target_pairs={{0,16},{8,24},{16,0},{24,8},{1,17},{9,25},{17,1},{25,9},{2,18},{10... | collective-permute-start | bytes 1228808 | tf_op jit(solution)/shard_map/ppermute | solution.py:434
  55.7 7.8 %collective-permute-start.20 = (bf16[160,512]{1,0:T(8,128)(2,1)S(1)}, bf16[160,512]{1,0:T(8,128)(2,1)S(1)}, u32[]{:S(2)}, u32[]{:S(2)}) collective-permute-start(bf16[160,512]{1,0:T(8,128)(2,1)S(1)} %collective-permute-done.17.refs_3_), channel_id=1, source_target_pairs={{0,1},{1,3},{3,5},{5,7},{7,6},{6,4},{4,2},{2,0},{8,9},{9,11},{11,1... | collective-permute-start | bytes 491528 | tf_op jit(solution)/shard_map/ppermute | solution.py:407
  57.7 8.4 %collective-permute-start.21 = (bf16[160,512]{1,0:T(8,128)(2,1)S(1)}, bf16[160,512]{1,0:T(8,128)(2,1)S(1)}, u32[]{:S(2)}, u32[]{:S(2)}) collective-permute-start(bf16[160,512]{1,0:T(8,128)(2,1)S(1)} %collective-permute-done.18.refs_4_), channel_id=1, source_target_pairs={{1,0},{3,1},{5,3},{7,5},{6,7},{4,6},{2,4},{0,2},{9,8},{11,9},{13,1... | collective-permute-start | bytes 491528 | tf_op jit(solution)/shard_map/ppermute | solution.py:407
  60.0 8.6 %collective-permute-start.16 = (bf16[160,512]{1,0:T(8,128)(2,1)}, bf16[160,512]{1,0:T(8,128)(2,1)S(1)}, u32[]{:S(2)}, u32[]{:S(2)}) collective-permute-start(bf16[160,512]{1,0:T(8,128)(2,1)} %collective-permute-done.15.refs_6_), channel_id=1, source_target_pairs={{0,1},{1,3},{3,5},{5,7},{7,6},{6,4},{4,2},{2,0},{8,9},{9,11},{11,1... | collective-permute-start | bytes 491528 | tf_op jit(solution)/shard_map/ppermute | solution.py:407
  62.6 7.3 %collective-permute-start.24 = (bf16[160,512]{1,0:T(8,128)(2,1)S(1)}, bf16[160,512]{1,0:T(8,128)(2,1)}, u32[]{:S(2)}, u32[]{:S(2)}) collective-permute-start(bf16[160,512]{1,0:T(8,128)(2,1)S(1)} %collective-permute-done.22.refs_9_), channel_id=1, source_target_pairs={{1,0},{3,1},{5,3},{7,5},{6,7},{4,6},{2,4},{0,2},{9,8},{11,9},{13,1... | collective-permute-start | bytes 491528 | tf_op jit(solution)/shard_map/ppermute | solution.py:407
  63.4 7.4 %collective-permute-start.29 = (bf16[160,512]{1,0:T(8,128)(2,1)S(1)}, bf16[160,512]{1,0:T(8,128)(2,1)}, u32[]{:S(2)}, u32[]{:S(2)}) collective-permute-start(bf16[160,512]{1,0:T(8,128)(2,1)S(1)} %collective-permute-done.20.refs_7_), channel_id=1, source_target_pairs={{0,1},{1,3},{3,5},{5,7},{7,6},{6,4},{4,2},{2,0},{8,9},{9,11},{11,1... | collective-permute-start | bytes 491528 | tf_op jit(solution)/shard_map/ppermute | solution.py:407
  66.1 7.3 %collective-permute-start.30 = (bf16[160,512]{1,0:T(8,128)(2,1)S(1)}, bf16[160,512]{1,0:T(8,128)(2,1)}, u32[]{:S(2)}, u32[]{:S(2)}) collective-permute-start(bf16[160,512]{1,0:T(8,128)(2,1)S(1)} %collective-permute-done.21.refs_8_), channel_id=1, source_target_pairs={{1,0},{3,1},{5,3},{7,5},{6,7},{4,6},{2,4},{0,2},{9,8},{11,9},{13,1... | collective-permute-start | bytes 491528 | tf_op jit(solution)/shard_map/ppermute | solution.py:407
  68.6 9.2 %collective-permute-start.28 = (bf16[240,1280]{1,0:T(8,128)(2,1)S(1)}, bf16[240,1280]{1,0:T(8,128)(2,1)S(1)}, u32[]{:S(2)}, u32[]{:S(2)}) collective-permute-start(bf16[240,1280]{1,0:T(8,128)(2,1)S(1)} %get-tuple-element.26.refs_9_.refs_5_), channel_id=1, source_target_pairs={{0,8},{8,0},{16,24},{24,16},{1,9},{9,1},{17,25},{25,17},{2,10},{10... | collective-permute-start | bytes 1843208 | tf_op jit(solution)/shard_map/ppermute | solution.py:434
  69.9 12.8 %collective-permute-start.23 = (bf16[160,512]{1,0:T(8,128)(2,1)S(1)}, bf16[160,512]{1,0:T(8,128)(2,1)S(1)}, u32[]{:S(2)}, u32[]{:S(2)}) collective-permute-start(bf16[160,512]{1,0:T(8,128)(2,1)S(1)} %after.10.refs_2_), channel_id=1, source_target_pairs={{0,1},{1,3},{3,5},{5,7},{7,6},{6,4},{4,2},{2,0},{8,9},{9,11},{11,1... | collective-permute-start | bytes 491528 | tf_op jit(solution)/shard_map/ppermute | solution.py:407
  70.8 11.8 %collective-permute-start.25 = (bf16[160,512]{1,0:T(8,128)(2,1)}, bf16[160,512]{1,0:T(8,128)(2,1)S(1)}, u32[]{:S(2)}, u32[]{:S(2)}) collective-permute-start(bf16[160,512]{1,0:T(8,128)(2,1)} %collective-permute-done.24.refs_5_), channel_id=1, source_target_pairs={{1,0},{3,1},{5,3},{7,5},{6,7},{4,6},{2,4},{0,2},{9,8},{11,9},{13,1... | collective-permute-start | bytes 491528 | tf_op jit(solution)/shard_map/ppermute | solution.py:407
  73.4 15.4 %collective-permute-start.37 = (bf16[160,1280]{1,0:T(8,128)(2,1)S(1)}, bf16[160,1280]{1,0:T(8,128)(2,1)S(1)}, u32[]{:S(2)}, u32[]{:S(2)}) collective-permute-start(bf16[160,1280]{1,0:T(8,128)(2,1)S(1)} %get-tuple-element.38.refs_7_), channel_id=1, source_target_pairs={{0,1},{1,0},{2,3},{3,2},{4,5},{5,4},{6,7},{7,6},{16,17},{17,16},{1... | collective-permute-start | bytes 1228808 | tf_op jit(solution)/shard_map/ppermute | solution.py:429
  75.7 15.4 %collective-permute-start.36 = (bf16[160,1280]{1,0:T(8,128)(2,1)S(1)}, bf16[160,1280]{1,0:T(8,128)(2,1)S(1)}, u32[]{:S(2)}, u32[]{:S(2)}) collective-permute-start(bf16[160,1280]{1,0:T(8,128)(2,1)S(1)} %broadcast_select_fusion), channel_id=1, source_target_pairs={{0,1},{1,0},{2,3},{3,2},{4,5},{5,4},{6,7},{7,6},{8,9},{9,8},{10,11... | collective-permute-start | bytes 1228808 | tf_op jit(solution)/shard_map/ppermute | solution.py:429
  77.8 23.4 %collective-permute-start.35 = (bf16[320,1280]{1,0:T(8,128)(2,1)S(1)}, bf16[320,1280]{1,0:T(8,128)(2,1)S(1)}, u32[]{:S(2)}, u32[]{:S(2)}) collective-permute-start(bf16[320,1280]{1,0:T(8,128)(2,1)S(1)} %pad_maximum_fusion), channel_id=1, source_target_pairs={{0,8},{8,0},{16,24},{24,16},{1,9},{9,1},{17,25},{25,17},{2,10},{10... | collective-permute-start | bytes 2457608 | tf_op jit(solution)/shard_map/ppermute | solution.py:434
  91.2 10.1 %collective-permute-start.38 = (bf16[320,1280]{1,0:T(8,128)(2,1)S(1)}, bf16[320,1280]{1,0:T(8,128)(2,1)S(1)}, u32[]{:S(2)}, u32[]{:S(2)}) collective-permute-start(bf16[320,1280]{1,0:T(8,128)(2,1)S(1)} %after.15.refs_9_), channel_id=1, source_target_pairs={{0,8},{8,0},{16,24},{24,16},{1,9},{9,1},{17,25},{25,17},{2,10},{10... | collective-permute-start | bytes 2457608 | tf_op jit(solution)/shard_map/ppermute | solution.py:434
  91.2 7.2 %collective-permute-start.31 = (bf16[320,128]{1,0:T(8,128)(2,1)S(1)}, bf16[320,128]{1,0:T(8,128)(2,1)S(1)}, u32[]{:S(2)}, u32[]{:S(2)}) collective-permute-start(bf16[320,128]{1,0:T(8,128)(2,1)S(1)} %get-tuple-element.32.refs_1_), channel_id=1, source_target_pairs={{0,2},{1,3},{2,4},{3,5},{4,6},{5,7},{6,0},{7,1},{8,10},{9,11},{10,... | collective-permute-start | bytes 245768 | tf_op jit(solution)/shard_map/ppermute | solution.py:631
  91.5 9.7 %collective-permute-start.32 = (bf16[320,128]{1,0:T(8,128)(2,1)S(1)}, bf16[320,128]{1,0:T(8,128)(2,1)S(1)}, u32[]{:S(2)}, u32[]{:S(2)}) collective-permute-start(bf16[320,128]{1,0:T(8,128)(2,1)S(1)} %get-tuple-element.33), channel_id=1, source_target_pairs={{0,4},{1,5},{2,6},{3,7},{4,0},{5,1},{6,2},{7,3},{8,12},{9,13},{10,... | collective-permute-start | bytes 245768 | tf_op jit(solution)/shard_map/ppermute | solution.py:631
  93.5 7.7 %collective-permute-start.33 = (bf16[320,128]{1,0:T(8,128)(2,1)S(1)}, bf16[320,128]{1,0:T(8,128)(2,1)S(1)}, u32[]{:S(2)}, u32[]{:S(2)}) collective-permute-start(bf16[320,128]{1,0:T(8,128)(2,1)S(1)} %get-tuple-element.34), channel_id=1, source_target_pairs={{0,6},{1,7},{2,0},{3,1},{4,2},{5,3},{6,4},{7,5},{8,14},{9,15},{10,... | collective-permute-start | bytes 245768 | tf_op jit(solution)/shard_map/ppermute | solution.py:631
  (14 other events, 110.7 us)

commit v15 on v14

--- a/solution.py
+++ b/solution.py
@@ -574,7 +574,7 @@
 
     hidden_pieces = gather((first_hidden, second_hidden), n, beside_second)
     if inner == 2:
-        chosen, far = after([chosen, far], hidden_pieces[2:4])
+        chosen, far = after([chosen, far], [second_hidden])
         near = [chosen]
         near.append(swap(near[0], 1))
         weights = [w_query, w_key, w_value] + near

time: 104 us -> 108 us (1.038)
  waiting for transfers between devices: 28.5 us -> 34.5 us
  starting transfers between devices: 45.8 us -> 43.9 us
    ppermute x28, waiting for transfers between devices: 22.7 us -> 28 us  [gather(): lax.ppermute(found[half, sign * (step - 1)], 'patch', pairs)]
    ppermute x28, starting transfers between devices: 32.1 us -> 29.9 us  [gather(): lax.ppermute(found[half, sign * (step - 1)], 'patch', pairs)]
  transfers between devices with their start and end apart: 39 -> 39, of which waited for: 19 -> 15; matrix products, arithmetic and copies ran while one was open for 2% -> 2% of each run, Pallas kernels for 23% -> 22%
where the time goes in v15:
time: 108 us
  starting transfers between devices  43.9 us (41%)
  waiting for transfers between devices  34.5 us (32%)
  Pallas kernels  26.1 us (24%)
  other arithmetic  1.72 us (2%)
  local copies, waits for them, and re-layouts  1.08 us (1%)
    ppermute x28, starting transfers between devices, gather(): lax.ppermute(found[half, sign * (step - 1)], 'patch', pairs)  29.9 us
    ppermute x28, waiting for transfers between devices, gather(): lax.ppermute(found[half, sign * (step - 1)], 'patch', pairs)  28 us
    pallas_call x1, Pallas kernels, on_device(): pl.pallas_call(functools.partial(attention_kernel, 2 * n, inner), out_sha...  6.14 us
    ppermute x4, starting transfers between devices, send(): return lax.ppermute(block, ('batch', 'patch'), pairs)  5.94 us
    pallas_call x1, Pallas kernels, on_device(): pl.pallas_call(functools.partial(conv_kernel, columns), out_shape=[half_h...  5.78 us
    pallas_call x1, Pallas kernels, on_device(): pl.pallas_call(functools.partial(project_kernel, 2 * n), out_shape=[jax.S...  4.68 us
    ppermute x4, starting transfers between devices, swap(): return lax.ppermute(block, 'batch', pairs)  4.21 us
    ppermute x3, waiting for transfers between devices, on_device(): received.append(lax.ppermute(sent_block, 'patch', pairs))  3.98 us
  transfers between devices with their start and end apart: 39, of which 15 were waited for; matrix products, arithmetic and copies ran while one was open for 2% of the time, Pallas kernels for 22%

profile of v15, /device:TPU:0, one launch (start us, length us, event | category | flops | bytes accessed | tf_op | source)
XLA Modules:
  0.0 107.6 jit_solution(17181577808114464429)
XLA Ops:
  1.0 3.0 %collective-permute-start = (bf16[64,1280]{1,0:T(8,128)(2,1)S(1)}, bf16[64,1280]{1,0:T(8,128)(2,1)S(1)}, u32[]{:S(2)}, u32[]{:S(2)}) collective-permute-start(bf16[64,1280]{1,0:T(8,128)(2,1)S(1)} %get-tuple-element.40.refs_0_), channel_id=1, source_target_pairs={{0,1},{1,3},{3,5},{5,7},{7,6},{6,4},{4,2},{2,0},{8,9},{9,11},{11,1... | collective-permute-start | bytes 491528 | tf_op jit(solution)/shard_map/ppermute | solution.py:407
  4.2 1.9 %collective-permute-start.1 = (bf16[64,1280]{1,0:T(8,128)(2,1)S(1)}, bf16[64,1280]{1,0:T(8,128)(2,1)S(1)}, u32[]{:S(2)}, u32[]{:S(2)}) collective-permute-start(bf16[64,1280]{1,0:T(8,128)(2,1)S(1)} %get-tuple-element.39.refs_1_), channel_id=1, source_target_pairs={{0,1},{1,3},{3,5},{5,7},{7,6},{6,4},{4,2},{2,0},{8,9},{9,11},{11,1... | collective-permute-start | bytes 491528 | tf_op jit(solution)/shard_map/ppermute | solution.py:407
  6.2 1.6 %fusion.1.refs_1_.refs_0_ = bf16[240,1280]{1,0:T(8,128)(2,1)S(1)} fusion(s32[]{:T(128)S(6)} %select_n.11, bf16[160,1280]{1,0:T(8,128)(2,1)} %refs_2_.1, bf16[160,1280]{1,0:T(8,128)(2,1)} %refs_3_.1, bf16[160,1280]{1,0:T(8,128)(2,1)} %refs_4_.1), kind=kLoop, calls=%fused_computation.6 | loop fusion | flops 1843200 | bytes 1843204 | tf_op jit(solution)/shard_map/concatenate | solution.py:479
  9.1 2.0 %collective-permute-start.4 = (bf16[64,1280]{1,0:T(8,128)(2,1)S(1)}, bf16[64,1280]{1,0:T(8,128)(2,1)S(1)}, u32[]{:S(2)}, u32[]{:S(2)}) collective-permute-start(bf16[64,1280]{1,0:T(8,128)(2,1)S(1)} %after.8.refs_2_), channel_id=1, source_target_pairs={{0,1},{1,3},{3,5},{5,7},{7,6},{6,4},{4,2},{2,0},{8,9},{9,11},{11,1... | collective-permute-start | bytes 491528 | tf_op jit(solution)/shard_map/ppermute | solution.py:407
  11.1 2.1 %collective-permute-done.3.refs_5_ = bf16[64,1280]{1,0:T(8,128)(2,1)S(1)} collective-permute-done((bf16[64,1280]{1,0:T(8,128)(2,1)S(1)}, bf16[64,1280]{1,0:T(8,128)(2,1)S(1)}, u32[]{:S(2)}, u32[]{:S(2)}) %collective-permute-start.3) | collective-permute-done | bytes 163872 | tf_op jit(solution)/shard_map/ppermute | solution.py:407
  13.6 1.6 %collective-permute-start.5 = (bf16[64,1280]{1,0:T(8,128)(2,1)S(1)}, bf16[64,1280]{1,0:T(8,128)(2,1)S(1)}, u32[]{:S(2)}, u32[]{:S(2)}) collective-permute-start(bf16[64,1280]{1,0:T(8,128)(2,1)S(1)} %collective-permute-done.1.refs_3_), channel_id=1, source_target_pairs={{0,1},{1,3},{3,5},{5,7},{7,6},{6,4},{4,2},{2,0},{8,9},{9,11},{11,1... | collective-permute-start | bytes 491528 | tf_op jit(solution)/shard_map/ppermute | solution.py:407
  15.7 2.1 %collective-permute-start.8 = (bf16[64,1280]{1,0:T(8,128)(2,1)S(1)}, bf16[64,1280]{1,0:T(8,128)(2,1)S(1)}, u32[]{:S(2)}, u32[]{:S(2)}) collective-permute-start(bf16[64,1280]{1,0:T(8,128)(2,1)S(1)} %collective-permute-done.4.refs_6_.refs_1_), channel_id=1, source_target_pairs={{0,1},{1,3},{3,5},{5,7},{7,6},{6,4},{4,2},{2,0},{8,9},{9,11},{11,1... | collective-permute-start | bytes 491528 | tf_op jit(solution)/shard_map/ppermute | solution.py:407
  17.7 2.6 %collective-permute-done.7.refs_9_.refs_4_ = bf16[64,1280]{1,0:T(8,128)(2,1)S(1)} collective-permute-done((bf16[64,1280]{1,0:T(8,128)(2,1)S(1)}, bf16[64,1280]{1,0:T(8,128)(2,1)S(1)}, u32[]{:S(2)}, u32[]{:S(2)}) %collective-permute-start.7) | collective-permute-done | bytes 163872 | tf_op jit(solution)/shard_map/ppermute | solution.py:407
  20.8 1.6 %collective-permute-start.9 = (bf16[64,1280]{1,0:T(8,128)(2,1)S(1)}, bf16[64,1280]{1,0:T(8,128)(2,1)S(1)}, u32[]{:S(2)}, u32[]{:S(2)}) collective-permute-start(bf16[64,1280]{1,0:T(8,128)(2,1)S(1)} %collective-permute-done.5.refs_7_.refs_2_), channel_id=1, source_target_pairs={{0,1},{1,3},{3,5},{5,7},{7,6},{6,4},{4,2},{2,0},{8,9},{9,11},{11,1... | collective-permute-start | bytes 491528 | tf_op jit(solution)/shard_map/ppermute | solution.py:407
  24.3 1.6 %collective-permute-start.26 = (bf16[240,1280]{1,0:T(8,128)(2,1)S(1)}, bf16[240,1280]{1,0:T(8,128)(2,1)S(1)}, u32[]{:S(2)}, u32[]{:S(2)}) collective-permute-start(bf16[240,1280]{1,0:T(8,128)(2,1)S(1)} %after.11), channel_id=1, source_target_pairs={{0,1},{1,0},{2,3},{3,2},{4,5},{5,4},{6,7},{7,6},{8,9},{9,8},{10,11... | collective-permute-start | bytes 1843208 | tf_op jit(solution)/shard_map/ppermute | solution.py:429
  28.8 2.2 %collective-permute-done.10.refs_12_.refs_3_ = bf16[64,1280]{1,0:T(8,128)(2,1)S(1)} collective-permute-done((bf16[64,1280]{1,0:T(8,128)(2,1)S(1)}, bf16[64,1280]{1,0:T(8,128)(2,1)S(1)}, u32[]{:S(2)}, u32[]{:S(2)}) %collective-permute-start.10) | collective-permute-done | bytes 163872 | tf_op jit(solution)/shard_map/ppermute | solution.py:407
  31.0 10.7 %collective-permute-done.12.refs_14_ = bf16[64,1280]{1,0:T(8,128)(2,1)S(1)} collective-permute-done((bf16[64,1280]{1,0:T(8,128)(2,1)S(1)}, bf16[64,1280]{1,0:T(8,128)(2,1)S(1)}, u32[]{:S(2)}, u32[]{:S(2)}) %collective-permute-start.12) | collective-permute-done | bytes 163872 | tf_op jit(solution)/shard_map/ppermute | solution.py:407
  41.7 3.4 %collective-permute-done.13.refs_15_ = bf16[64,1280]{1,0:T(8,128)(2,1)S(1)} collective-permute-done((bf16[64,1280]{1,0:T(8,128)(2,1)S(1)}, bf16[64,1280]{1,0:T(8,128)(2,1)S(1)}, u32[]{:S(2)}, u32[]{:S(2)}) %collective-permute-start.13) | collective-permute-done | bytes 163872 | tf_op jit(solution)/shard_map/ppermute | solution.py:407
  45.2 5.8 %norm_conv.1 = (bf16[160,512]{1,0:T(8,128)(2,1)S(1)}, bf16[1152,1280]{1,0:T(8,128)(2,1)S(1)}, f32[160,1024]{1,0:T(8,128)S(1)}) custom-call(s32[128]{0:T(128)S(1)} %copy-done.6, bf16[64,1280]{1,0:T(8,128)(2,1)S(1)} %get-tuple-element.40.refs_0_, bf16[64,1280]{1,0:T(8,128)(2,1)S(1)} %get-tuple-element.39.refs_1_, bf16[64,1280]{1,0:T(8,128)(2,1)S(1)} %after.8.refs_2_, ...), custom_call_target="tpu_custom_call" | custom-call | flops 1887436800 | bytes 6307840 | tf_op jit(solution)/shard_map/norm_conv/pallas_call | solution.py:524
  51.0 2.2 %second_conv.1.refs_1_.refs_2_ = bf16[160,512]{1,0:T(8,128)(2,1)S(1)} custom-call(bf16[1152,1280]{1,0:T(8,128)(2,1)S(1)} %get-tuple-element.23.act_ref, f32[160,1024]{1,0:T(8,128)S(1)} %get-tuple-element.24.kept_ref, bf16[3,480,1280]{2,1,0:T(8,128)(2,1)S(1)} %bitcast.8, f32[1,160]{1,0:T(1,128)S(1)} %bitcast.10), custom_call_target="tpu_custom_call" | custom-call | flops 1887436800 | bytes 1887436 | tf_op jit(solution)/shard_map/second_conv/pallas_call | solution.py:541
  53.3 2.1 %collective-permute-start.19 = (bf16[160,512]{1,0:T(8,128)(2,1)S(1)}, bf16[160,512]{1,0:T(8,128)(2,1)S(1)}, u32[]{:S(2)}, u32[]{:S(2)}) collective-permute-start(bf16[160,512]{1,0:T(8,128)(2,1)S(1)} %second_conv.1.refs_1_.refs_2_), channel_id=1, source_target_pairs={{1,0},{3,1},{5,3},{7,5},{6,7},{4,6},{2,4},{0,2},{9,8},{11,9},{13,1... | collective-permute-start | bytes 491528 | tf_op jit(solution)/shard_map/ppermute | solution.py:407
  55.3 2.0 %collective-permute-start.18 = (bf16[160,512]{1,0:T(8,128)(2,1)S(1)}, bf16[160,512]{1,0:T(8,128)(2,1)S(1)}, u32[]{:S(2)}, u32[]{:S(2)}) collective-permute-start(bf16[160,512]{1,0:T(8,128)(2,1)S(1)} %get-tuple-element.22.refs_0_), channel_id=1, source_target_pairs={{1,0},{3,1},{5,3},{7,5},{6,7},{4,6},{2,4},{0,2},{9,8},{11,9},{13,1... | collective-permute-start | bytes 491528 | tf_op jit(solution)/shard_map/ppermute | solution.py:407
  57.4 4.0 %collective-permute-start.34 = (bf16[160,1280]{1,0:T(8,128)(2,1)S(1)}, bf16[160,1280]{1,0:T(8,128)(2,1)S(1)}, u32[]{:S(2)}, u32[]{:S(2)}) collective-permute-start(bf16[160,1280]{1,0:T(8,128)(2,1)S(1)} %get-tuple-element.36.refs_0_), channel_id=1, source_target_pairs={{0,16},{8,24},{16,0},{24,8},{1,17},{9,25},{17,1},{25,9},{2,18},{10... | collective-permute-start | bytes 1228808 | tf_op jit(solution)/shard_map/ppermute | solution.py:434
  61.4 2.0 %collective-permute-start.22 = (bf16[160,512]{1,0:T(8,128)(2,1)S(1)}, bf16[160,512]{1,0:T(8,128)(2,1)S(1)}, u32[]{:S(2)}, u32[]{:S(2)}) collective-permute-start(bf16[160,512]{1,0:T(8,128)(2,1)S(1)} %collective-permute-done.19.refs_5_), channel_id=1, source_target_pairs={{1,0},{3,1},{5,3},{7,5},{6,7},{4,6},{2,4},{0,2},{9,8},{11,9},{13,1... | collective-permute-start | bytes 491528 | tf_op jit(solution)/shard_map/ppermute | solution.py:407
  63.4 2.0 %collective-permute-start.21 = (bf16[160,512]{1,0:T(8,128)(2,1)S(1)}, bf16[160,512]{1,0:T(8,128)(2,1)S(1)}, u32[]{:S(2)}, u32[]{:S(2)}) collective-permute-start(bf16[160,512]{1,0:T(8,128)(2,1)S(1)} %collective-permute-done.18.refs_4_), channel_id=1, source_target_pairs={{1,0},{3,1},{5,3},{7,5},{6,7},{4,6},{2,4},{0,2},{9,8},{11,9},{13,1... | collective-permute-start | bytes 491528 | tf_op jit(solution)/shard_map/ppermute | solution.py:407
  65.4 2.9 %collective-permute-done.15.refs_6_ = bf16[160,512]{1,0:T(8,128)(2,1)} collective-permute-done((bf16[160,512]{1,0:T(8,128)(2,1)S(1)}, bf16[160,512]{1,0:T(8,128)(2,1)}, u32[]{:S(2)}, u32[]{:S(2)}) %collective-permute-start.15) | collective-permute-done | bytes 163872 | tf_op jit(solution)/shard_map/ppermute | solution.py:407
  68.5 1.9 %collective-permute-start.24 = (bf16[160,512]{1,0:T(8,128)(2,1)S(1)}, bf16[160,512]{1,0:T(8,128)(2,1)}, u32[]{:S(2)}, u32[]{:S(2)}) collective-permute-start(bf16[160,512]{1,0:T(8,128)(2,1)S(1)} %collective-permute-done.22.refs_9_), channel_id=1, source_target_pairs={{1,0},{3,1},{5,3},{7,5},{6,7},{4,6},{2,4},{0,2},{9,8},{11,9},{13,1... | collective-permute-start | bytes 491528 | tf_op jit(solution)/shard_map/ppermute | solution.py:407
  71.2 1.7 %collective-permute-start.30 = (bf16[160,512]{1,0:T(8,128)(2,1)S(1)}, bf16[160,512]{1,0:T(8,128)(2,1)}, u32[]{:S(2)}, u32[]{:S(2)}) collective-permute-start(bf16[160,512]{1,0:T(8,128)(2,1)S(1)} %collective-permute-done.21.refs_8_), channel_id=1, source_target_pairs={{1,0},{3,1},{5,3},{7,5},{6,7},{4,6},{2,4},{0,2},{9,8},{11,9},{13,1... | collective-permute-start | bytes 491528 | tf_op jit(solution)/shard_map/ppermute | solution.py:407
  72.9 2.5 %early_norm.1 = (bf16[800,1024]{1,0:T(8,128)(2,1)S(1)}, bf16[800,128]{1,0:T(8,128)(2,1)S(1)}) custom-call(bf16[160,512]{1,0:T(8,128)(2,1)S(1)} %get-tuple-element.22.refs_0_, bf16[160,512]{1,0:T(8,128)(2,1)S(1)} %second_conv.1.refs_1_.refs_2_, bf16[160,512]{1,0:T(8,128)(2,1)S(1)} %collective-permute-done.14.refs_2_, ...), custom_call_target="tpu_custom_call" | custom-call | flops 10485760 | bytes 5242880 | tf_op jit(solution)/shard_map/early_norm/pallas_call | solution.py:556
  77.6 2.9 %collective-permute-start.37 = (bf16[160,1280]{1,0:T(8,128)(2,1)S(1)}, bf16[160,1280]{1,0:T(8,128)(2,1)S(1)}, u32[]{:S(2)}, u32[]{:S(2)}) collective-permute-start(bf16[160,1280]{1,0:T(8,128)(2,1)S(1)} %get-tuple-element.38.refs_7_), channel_id=1, source_target_pairs={{0,1},{1,0},{2,3},{3,2},{4,5},{5,4},{6,7},{7,6},{16,17},{17,16},{1... | collective-permute-start | bytes 1228808 | tf_op jit(solution)/shard_map/ppermute | solution.py:429
  82.2 4.7 %norm_project.1 = (f32[960,1024]{1,0:T(8,128)S(1)}, bf16[1280,128]{1,0:T(8,128)(2,1)S(1)}) custom-call(s32[128]{0:T(128)S(1)} %copy-done.6, bf16[800,1024]{1,0:T(8,128)(2,1)S(1)} %get-tuple-element.25.refs_1_.refs_0_, bf16[800,128]{1,0:T(8,128)(2,1)S(1)} %get-tuple-element.27.refs_1_, bf16[160,512]{1,0:T(8,128)(2,1)S(1)} %after.10.refs_2_, ...), custom_call_target="tpu_custom_call" | custom-call | flops 2516582400 | bytes 5079040 | tf_op jit(solution)/shard_map/norm_project/pallas_call | solution.py:584
  86.9 6.1 %attention.1 = (bf16[320,128]{1,0:T(8,128)(2,1)S(1)}, bf16[320,128]{1,0:T(8,128)(2,1)S(1)}, bf16[320,128]{1,0:T(8,128)(2,1)S(1)}, bf16[1280,128]{1,0:T(8,128)(2,...) custom-call(s32[128]{0:T(128)S(1)} %copy-done.6, ...), custom_call_target="tpu_custom_call" | custom-call | flops 1258291200 | bytes 5898240 | tf_op jit(solution)/shard_map/attention/pallas_call | solution.py:608
  93.0 2.5 %collective-permute-done.36 = bf16[160,1280]{1,0:T(8,128)(2,1)S(1)} collective-permute-done((bf16[160,1280]{1,0:T(8,128)(2,1)S(1)}, bf16[160,1280]{1,0:T(8,128)(2,1)S(1)}, u32[]{:S(2)}, u32[]{:S(2)}) %collective-permute-start.36) | collective-permute-done | bytes 409632 | tf_op jit(solution)/shard_map/ppermute | solution.py:429
  95.7 2.7 %collective-permute-start.32 = (bf16[320,128]{1,0:T(8,128)(2,1)S(1)}, bf16[320,128]{1,0:T(8,128)(2,1)S(1)}, u32[]{:S(2)}, u32[]{:S(2)}) collective-permute-start(bf16[320,128]{1,0:T(8,128)(2,1)S(1)} %get-tuple-element.33), channel_id=1, source_target_pairs={{0,4},{1,5},{2,6},{3,7},{4,0},{5,1},{6,2},{7,3},{8,12},{9,13},{10,... | collective-permute-start | bytes 245768 | tf_op jit(solution)/shard_map/ppermute | solution.py:631
  99.6 1.9 %own_attention.1.refs_0_ = bf16[320,128]{1,0:T(8,128)(2,1)S(1)} custom-call(bf16[960,1024]{1,0:T(8,128)(2,1)S(1)} %get-tuple-element.30.made_ref, bf16[5,1024,64]{2,1,0:T(8,128)(2,1)S(1)} %get-tuple-element.31.key_ref), custom_call_target="tpu_custom_call" | custom-call | flops 167772160 | bytes 2621440 | tf_op jit(solution)/shard_map/own_attention/pallas_call | solution.py:632
  102.9 2.6 %collective-permute-done.32.refs_2_ = bf16[320,128]{1,0:T(8,128)(2,1)S(1)} collective-permute-done((bf16[320,128]{1,0:T(8,128)(2,1)S(1)}, bf16[320,128]{1,0:T(8,128)(2,1)S(1)}, u32[]{:S(2)}, u32[]{:S(2)}) %collective-permute-start.32) | collective-permute-done | bytes 81952 | tf_op jit(solution)/shard_map/ppermute | solution.py:631
  105.5 2.1 %project.1 = bf16[128,1280]{1,0:T(8,128)(2,1)} custom-call(bf16[320,128]{1,0:T(8,128)(2,1)S(1)} %own_attention.1.refs_0_, bf16[320,128]{1,0:T(8,128)(2,1)S(1)} %collective-permute-done.31.refs_1_, bf16[320,128]{1,0:T(8,128)(2,1)S(1)} %collective-permute-done.32.refs_2_, bf16[320,128]{1,0:T(8,128)(2,1)S(1)} %collective-permute-done.33.refs_3_, ...), custom_call_target="tpu_custom_call" | custom-call | flops 419430400 | bytes 4259840 | tf_op jit(solution)/shard_map/project/pallas_call | solution.py:649
  (82 shorter events, 16.2 us)
Async XLA Ops:
  1.0 8.1 %collective-permute-start = (bf16[64,1280]{1,0:T(8,128)(2,1)S(1)}, bf16[64,1280]{1,0:T(8,128)(2,1)S(1)}, u32[]{:S(2)}, u32[]{:S(2)}) collective-permute-start(bf16[64,1280]{1,0:T(8,128)(2,1)S(1)} %get-tuple-element.40.refs_0_), channel_id=1, source_target_pairs={{0,1},{1,3},{3,5},{5,7},{7,6},{6,4},{4,2},{2,0},{8,9},{9,11},{11,1... | collective-permute-start | bytes 491528 | tf_op jit(solution)/shard_map/ppermute | solution.py:407
  4.0 11.2 %collective-permute-start.2 = (bf16[64,1280]{1,0:T(8,128)(2,1)S(1)}, bf16[64,1280]{1,0:T(8,128)(2,1)S(1)}, u32[]{:S(2)}, u32[]{:S(2)}) collective-permute-start(bf16[64,1280]{1,0:T(8,128)(2,1)S(1)} %get-tuple-element.40.refs_0_), channel_id=1, source_target_pairs={{1,0},{3,1},{5,3},{7,5},{6,7},{4,6},{2,4},{0,2},{9,8},{11,9},{13,1... | collective-permute-start | bytes 491528 | tf_op jit(solution)/shard_map/ppermute | solution.py:407
  4.2 9.5 %collective-permute-start.1 = (bf16[64,1280]{1,0:T(8,128)(2,1)S(1)}, bf16[64,1280]{1,0:T(8,128)(2,1)S(1)}, u32[]{:S(2)}, u32[]{:S(2)}) collective-permute-start(bf16[64,1280]{1,0:T(8,128)(2,1)S(1)} %get-tuple-element.39.refs_1_), channel_id=1, source_target_pairs={{0,1},{1,3},{3,5},{5,7},{7,6},{6,4},{4,2},{2,0},{8,9},{9,11},{11,1... | collective-permute-start | bytes 491528 | tf_op jit(solution)/shard_map/ppermute | solution.py:407
  6.1 7.1 %collective-permute-start.3 = (bf16[64,1280]{1,0:T(8,128)(2,1)S(1)}, bf16[64,1280]{1,0:T(8,128)(2,1)S(1)}, u32[]{:S(2)}, u32[]{:S(2)}) collective-permute-start(bf16[64,1280]{1,0:T(8,128)(2,1)S(1)} %get-tuple-element.39.refs_1_), channel_id=1, source_target_pairs={{1,0},{3,1},{5,3},{7,5},{6,7},{4,6},{2,4},{0,2},{9,8},{11,9},{13,1... | collective-permute-start | bytes 491528 | tf_op jit(solution)/shard_map/ppermute | solution.py:407
  13.2 7.1 %collective-permute-start.7 = (bf16[64,1280]{1,0:T(8,128)(2,1)S(1)}, bf16[64,1280]{1,0:T(8,128)(2,1)S(1)}, u32[]{:S(2)}, u32[]{:S(2)}) collective-permute-start(bf16[64,1280]{1,0:T(8,128)(2,1)S(1)} %collective-permute-done.3.refs_5_), channel_id=1, source_target_pairs={{1,0},{3,1},{5,3},{7,5},{6,7},{4,6},{2,4},{0,2},{9,8},{11,9},{13,1... | collective-permute-start | bytes 491528 | tf_op jit(solution)/shard_map/ppermute | solution.py:407
  13.6 7.1 %collective-permute-start.5 = (bf16[64,1280]{1,0:T(8,128)(2,1)S(1)}, bf16[64,1280]{1,0:T(8,128)(2,1)S(1)}, u32[]{:S(2)}, u32[]{:S(2)}) collective-permute-start(bf16[64,1280]{1,0:T(8,128)(2,1)S(1)} %collective-permute-done.1.refs_3_), channel_id=1, source_target_pairs={{0,1},{1,3},{3,5},{5,7},{7,6},{6,4},{4,2},{2,0},{8,9},{9,11},{11,1... | collective-permute-start | bytes 491528 | tf_op jit(solution)/shard_map/ppermute | solution.py:407
  15.2 8.6 %collective-permute-start.6 = (bf16[64,1280]{1,0:T(8,128)(2,1)S(1)}, bf16[64,1280]{1,0:T(8,128)(2,1)S(1)}, u32[]{:S(2)}, u32[]{:S(2)}) collective-permute-start(bf16[64,1280]{1,0:T(8,128)(2,1)S(1)} %collective-permute-done.2.refs_4_), channel_id=1, source_target_pairs={{1,0},{3,1},{5,3},{7,5},{6,7},{4,6},{2,4},{0,2},{9,8},{11,9},{13,1... | collective-permute-start | bytes 491528 | tf_op jit(solution)/shard_map/ppermute | solution.py:407
  15.7 11.0 %collective-permute-start.8 = (bf16[64,1280]{1,0:T(8,128)(2,1)S(1)}, bf16[64,1280]{1,0:T(8,128)(2,1)S(1)}, u32[]{:S(2)}, u32[]{:S(2)}) collective-permute-start(bf16[64,1280]{1,0:T(8,128)(2,1)S(1)} %collective-permute-done.4.refs_6_.refs_1_), channel_id=1, source_target_pairs={{0,1},{1,3},{3,5},{5,7},{7,6},{6,4},{4,2},{2,0},{8,9},{9,11},{11,1... | collective-permute-start | bytes 491528 | tf_op jit(solution)/shard_map/ppermute | solution.py:407
  20.3 7.1 %collective-permute-start.11 = (bf16[64,1280]{1,0:T(8,128)(2,1)S(1)}, bf16[64,1280]{1,0:T(8,128)(2,1)S(1)}, u32[]{:S(2)}, u32[]{:S(2)}) collective-permute-start(bf16[64,1280]{1,0:T(8,128)(2,1)S(1)} %collective-permute-done.7.refs_9_.refs_4_), channel_id=1, source_target_pairs={{1,0},{3,1},{5,3},{7,5},{6,7},{4,6},{2,4},{0,2},{9,8},{11,9},{13,1... | collective-permute-start | bytes 491528 | tf_op jit(solution)/shard_map/ppermute | solution.py:407
  20.8 8.0 %collective-permute-start.9 = (bf16[64,1280]{1,0:T(8,128)(2,1)S(1)}, bf16[64,1280]{1,0:T(8,128)(2,1)S(1)}, u32[]{:S(2)}, u32[]{:S(2)}) collective-permute-start(bf16[64,1280]{1,0:T(8,128)(2,1)S(1)} %collective-permute-done.5.refs_7_.refs_2_), channel_id=1, source_target_pairs={{0,1},{1,3},{3,5},{5,7},{7,6},{6,4},{4,2},{2,0},{8,9},{9,11},{11,1... | collective-permute-start | bytes 491528 | tf_op jit(solution)/shard_map/ppermute | solution.py:407
  23.9 7.1 %collective-permute-start.10 = (bf16[64,1280]{1,0:T(8,128)(2,1)S(1)}, bf16[64,1280]{1,0:T(8,128)(2,1)S(1)}, u32[]{:S(2)}, u32[]{:S(2)}) collective-permute-start(bf16[64,1280]{1,0:T(8,128)(2,1)S(1)} %collective-permute-done.6.refs_8_.refs_3_), channel_id=1, source_target_pairs={{1,0},{3,1},{5,3},{7,5},{6,7},{4,6},{2,4},{0,2},{9,8},{11,9},{13,1... | collective-permute-start | bytes 491528 | tf_op jit(solution)/shard_map/ppermute | solution.py:407
  24.3 33.1 %collective-permute-start.26 = (bf16[240,1280]{1,0:T(8,128)(2,1)S(1)}, bf16[240,1280]{1,0:T(8,128)(2,1)S(1)}, u32[]{:S(2)}, u32[]{:S(2)}) collective-permute-start(bf16[240,1280]{1,0:T(8,128)(2,1)S(1)} %after.11), channel_id=1, source_target_pairs={{0,1},{1,0},{2,3},{3,2},{4,5},{5,4},{6,7},{7,6},{8,9},{9,8},{10,11... | collective-permute-start | bytes 1843208 | tf_op jit(solution)/shard_map/ppermute | solution.py:429
  26.7 15.1 %collective-permute-start.12 = (bf16[64,1280]{1,0:T(8,128)(2,1)S(1)}, bf16[64,1280]{1,0:T(8,128)(2,1)S(1)}, u32[]{:S(2)}, u32[]{:S(2)}) collective-permute-start(bf16[64,1280]{1,0:T(8,128)(2,1)S(1)} %after.9.refs_10_.refs_1_), channel_id=1, source_target_pairs={{0,1},{1,3},{3,5},{5,7},{7,6},{6,4},{4,2},{2,0},{8,9},{9,11},{11,1... | collective-permute-start | bytes 491528 | tf_op jit(solution)/shard_map/ppermute | solution.py:407
  27.5 17.7 %collective-permute-start.13 = (bf16[64,1280]{1,0:T(8,128)(2,1)S(1)}, bf16[64,1280]{1,0:T(8,128)(2,1)S(1)}, u32[]{:S(2)}, u32[]{:S(2)}) collective-permute-start(bf16[64,1280]{1,0:T(8,128)(2,1)S(1)} %collective-permute-done.11.refs_13_.refs_4_), channel_id=1, source_target_pairs={{1,0},{3,1},{5,3},{7,5},{6,7},{4,6},{2,4},{0,2},{9,8},{11,9},{13,1... | collective-permute-start | bytes 491528 | tf_op jit(solution)/shard_map/ppermute | solution.py:407
  31.0 24.3 %collective-permute-start.27 = (bf16[160,1280]{1,0:T(8,128)(2,1)S(1)}, bf16[160,1280]{1,0:T(8,128)(2,1)S(1)}, u32[]{:S(2)}, u32[]{:S(2)}) collective-permute-start(bf16[160,1280]{1,0:T(8,128)(2,1)S(1)} %after.12), channel_id=1, source_target_pairs={{0,2},{1,3},{2,4},{3,5},{4,6},{5,7},{6,0},{7,1},{8,14},{9,15},{10,... | collective-permute-start | bytes 1228808 | tf_op jit(solution)/shard_map/ppermute | solution.py:429
  51.0 10.4 %collective-permute-start.14 = (bf16[160,512]{1,0:T(8,128)(2,1)S(1)}, bf16[160,512]{1,0:T(8,128)(2,1)S(1)}, u32[]{:S(2)}, u32[]{:S(2)}) collective-permute-start(bf16[160,512]{1,0:T(8,128)(2,1)S(1)} %get-tuple-element.22.refs_0_), channel_id=1, source_target_pairs={{0,1},{1,3},{3,5},{5,7},{7,6},{6,4},{4,2},{2,0},{8,9},{9,11},{11,1... | collective-permute-start | bytes 491528 | tf_op jit(solution)/shard_map/ppermute | solution.py:407
  53.3 8.1 %collective-permute-start.19 = (bf16[160,512]{1,0:T(8,128)(2,1)S(1)}, bf16[160,512]{1,0:T(8,128)(2,1)S(1)}, u32[]{:S(2)}, u32[]{:S(2)}) collective-permute-start(bf16[160,512]{1,0:T(8,128)(2,1)S(1)} %second_conv.1.refs_1_.refs_2_), channel_id=1, source_target_pairs={{1,0},{3,1},{5,3},{7,5},{6,7},{4,6},{2,4},{0,2},{9,8},{11,9},{13,1... | collective-permute-start | bytes 491528 | tf_op jit(solution)/shard_map/ppermute | solution.py:407
  55.3 8.1 %collective-permute-start.17 = (bf16[160,512]{1,0:T(8,128)(2,1)S(1)}, bf16[160,512]{1,0:T(8,128)(2,1)S(1)}, u32[]{:S(2)}, u32[]{:S(2)}) collective-permute-start(bf16[160,512]{1,0:T(8,128)(2,1)S(1)} %second_conv.1.refs_1_.refs_2_), channel_id=1, source_target_pairs={{0,1},{1,3},{3,5},{5,7},{7,6},{6,4},{4,2},{2,0},{8,9},{9,11},{11,1... | collective-permute-start | bytes 491528 | tf_op jit(solution)/shard_map/ppermute | solution.py:407
  55.3 8.1 %collective-permute-start.18 = (bf16[160,512]{1,0:T(8,128)(2,1)S(1)}, bf16[160,512]{1,0:T(8,128)(2,1)S(1)}, u32[]{:S(2)}, u32[]{:S(2)}) collective-permute-start(bf16[160,512]{1,0:T(8,128)(2,1)S(1)} %get-tuple-element.22.refs_0_), channel_id=1, source_target_pairs={{1,0},{3,1},{5,3},{7,5},{6,7},{4,6},{2,4},{0,2},{9,8},{11,9},{13,1... | collective-permute-start | bytes 491528 | tf_op jit(solution)/shard_map/ppermute | solution.py:407
  57.4 20.2 %collective-permute-start.34 = (bf16[160,1280]{1,0:T(8,128)(2,1)S(1)}, bf16[160,1280]{1,0:T(8,128)(2,1)S(1)}, u32[]{:S(2)}, u32[]{:S(2)}) collective-permute-start(bf16[160,1280]{1,0:T(8,128)(2,1)S(1)} %get-tuple-element.36.refs_0_), channel_id=1, source_target_pairs={{0,16},{8,24},{16,0},{24,8},{1,17},{9,25},{17,1},{25,9},{2,18},{10... | collective-permute-start | bytes 1228808 | tf_op jit(solution)/shard_map/ppermute | solution.py:434
  61.4 7.2 %collective-permute-start.22 = (bf16[160,512]{1,0:T(8,128)(2,1)S(1)}, bf16[160,512]{1,0:T(8,128)(2,1)S(1)}, u32[]{:S(2)}, u32[]{:S(2)}) collective-permute-start(bf16[160,512]{1,0:T(8,128)(2,1)S(1)} %collective-permute-done.19.refs_5_), channel_id=1, source_target_pairs={{1,0},{3,1},{5,3},{7,5},{6,7},{4,6},{2,4},{0,2},{9,8},{11,9},{13,1... | collective-permute-start | bytes 491528 | tf_op jit(solution)/shard_map/ppermute | solution.py:407
  63.4 7.3 %collective-permute-start.20 = (bf16[160,512]{1,0:T(8,128)(2,1)S(1)}, bf16[160,512]{1,0:T(8,128)(2,1)S(1)}, u32[]{:S(2)}, u32[]{:S(2)}) collective-permute-start(bf16[160,512]{1,0:T(8,128)(2,1)S(1)} %collective-permute-done.17.refs_3_), channel_id=1, source_target_pairs={{0,1},{1,3},{3,5},{5,7},{7,6},{6,4},{4,2},{2,0},{8,9},{9,11},{11,1... | collective-permute-start | bytes 491528 | tf_op jit(solution)/shard_map/ppermute | solution.py:407
  63.4 7.8 %collective-permute-start.21 = (bf16[160,512]{1,0:T(8,128)(2,1)S(1)}, bf16[160,512]{1,0:T(8,128)(2,1)S(1)}, u32[]{:S(2)}, u32[]{:S(2)}) collective-permute-start(bf16[160,512]{1,0:T(8,128)(2,1)S(1)} %collective-permute-done.18.refs_4_), channel_id=1, source_target_pairs={{1,0},{3,1},{5,3},{7,5},{6,7},{4,6},{2,4},{0,2},{9,8},{11,9},{13,1... | collective-permute-start | bytes 491528 | tf_op jit(solution)/shard_map/ppermute | solution.py:407
  75.5 11.4 %collective-permute-start.23 = (bf16[160,512]{1,0:T(8,128)(2,1)S(1)}, bf16[160,512]{1,0:T(8,128)(2,1)S(1)}, u32[]{:S(2)}, u32[]{:S(2)}) collective-permute-start(bf16[160,512]{1,0:T(8,128)(2,1)S(1)} %after.10.refs_2_), channel_id=1, source_target_pairs={{0,1},{1,3},{3,5},{5,7},{7,6},{6,4},{4,2},{2,0},{8,9},{9,11},{11,1... | collective-permute-start | bytes 491528 | tf_op jit(solution)/shard_map/ppermute | solution.py:407
  76.1 10.8 %collective-permute-start.25 = (bf16[160,512]{1,0:T(8,128)(2,1)}, bf16[160,512]{1,0:T(8,128)(2,1)S(1)}, u32[]{:S(2)}, u32[]{:S(2)}) collective-permute-start(bf16[160,512]{1,0:T(8,128)(2,1)} %collective-permute-done.24.refs_5_), channel_id=1, source_target_pairs={{1,0},{3,1},{5,3},{7,5},{6,7},{4,6},{2,4},{0,2},{9,8},{11,9},{13,1... | collective-permute-start | bytes 491528 | tf_op jit(solution)/shard_map/ppermute | solution.py:407
  77.6 15.4 %collective-permute-start.37 = (bf16[160,1280]{1,0:T(8,128)(2,1)S(1)}, bf16[160,1280]{1,0:T(8,128)(2,1)S(1)}, u32[]{:S(2)}, u32[]{:S(2)}) collective-permute-start(bf16[160,1280]{1,0:T(8,128)(2,1)S(1)} %get-tuple-element.38.refs_7_), channel_id=1, source_target_pairs={{0,1},{1,0},{2,3},{3,2},{4,5},{5,4},{6,7},{7,6},{16,17},{17,16},{1... | collective-permute-start | bytes 1228808 | tf_op jit(solution)/shard_map/ppermute | solution.py:429
  80.6 14.9 %collective-permute-start.36 = (bf16[160,1280]{1,0:T(8,128)(2,1)S(1)}, bf16[160,1280]{1,0:T(8,128)(2,1)S(1)}, u32[]{:S(2)}, u32[]{:S(2)}) collective-permute-start(bf16[160,1280]{1,0:T(8,128)(2,1)S(1)} %broadcast_select_fusion), channel_id=1, source_target_pairs={{0,1},{1,0},{2,3},{3,2},{4,5},{5,4},{6,7},{7,6},{8,9},{9,8},{10,11... | collective-permute-start | bytes 1228808 | tf_op jit(solution)/shard_map/ppermute | solution.py:429
  82.1 23.4 %collective-permute-start.35 = (bf16[320,1280]{1,0:T(8,128)(2,1)S(1)}, bf16[320,1280]{1,0:T(8,128)(2,1)S(1)}, u32[]{:S(2)}, u32[]{:S(2)}) collective-permute-start(bf16[320,1280]{1,0:T(8,128)(2,1)S(1)} %pad_maximum_fusion), channel_id=1, source_target_pairs={{0,8},{8,0},{16,24},{24,16},{1,9},{9,1},{17,25},{25,17},{2,10},{10... | collective-permute-start | bytes 2457608 | tf_op jit(solution)/shard_map/ppermute | solution.py:434
  95.6 9.9 %collective-permute-start.38 = (bf16[320,1280]{1,0:T(8,128)(2,1)S(1)}, bf16[320,1280]{1,0:T(8,128)(2,1)S(1)}, u32[]{:S(2)}, u32[]{:S(2)}) collective-permute-start(bf16[320,1280]{1,0:T(8,128)(2,1)S(1)} %after.15.refs_9_), channel_id=1, source_target_pairs={{0,8},{8,0},{16,24},{24,16},{1,9},{9,1},{17,25},{25,17},{2,10},{10... | collective-permute-start | bytes 2457608 | tf_op jit(solution)/shard_map/ppermute | solution.py:434
  95.7 7.2 %collective-permute-start.31 = (bf16[320,128]{1,0:T(8,128)(2,1)S(1)}, bf16[320,128]{1,0:T(8,128)(2,1)S(1)}, u32[]{:S(2)}, u32[]{:S(2)}) collective-permute-start(bf16[320,128]{1,0:T(8,128)(2,1)S(1)} %get-tuple-element.32.refs_1_), channel_id=1, source_target_pairs={{0,2},{1,3},{2,4},{3,5},{4,6},{5,7},{6,0},{7,1},{8,10},{9,11},{10,... | collective-permute-start | bytes 245768 | tf_op jit(solution)/shard_map/ppermute | solution.py:631
  95.7 9.8 %collective-permute-start.32 = (bf16[320,128]{1,0:T(8,128)(2,1)S(1)}, bf16[320,128]{1,0:T(8,128)(2,1)S(1)}, u32[]{:S(2)}, u32[]{:S(2)}) collective-permute-start(bf16[320,128]{1,0:T(8,128)(2,1)S(1)} %get-tuple-element.33), channel_id=1, source_target_pairs={{0,4},{1,5},{2,6},{3,7},{4,0},{5,1},{6,2},{7,3},{8,12},{9,13},{10,... | collective-permute-start | bytes 245768 | tf_op jit(solution)/shard_map/ppermute | solution.py:631
  98.4 7.1 %collective-permute-start.33 = (bf16[320,128]{1,0:T(8,128)(2,1)S(1)}, bf16[320,128]{1,0:T(8,128)(2,1)S(1)}, u32[]{:S(2)}, u32[]{:S(2)}) collective-permute-start(bf16[320,128]{1,0:T(8,128)(2,1)S(1)} %get-tuple-element.34), channel_id=1, source_target_pairs={{0,6},{1,7},{2,0},{3,1},{4,2},{5,3},{6,4},{7,5},{8,14},{9,15},{10,... | collective-permute-start | bytes 245768 | tf_op jit(solution)/shard_map/ppermute | solution.py:631
  (14 other events, 135.7 us)

commit v16 on v15

--- a/solution.py
+++ b/solution.py
@@ -506,8 +506,7 @@
     pieces = gather(halves, n, beside_first)
     stats = made_beside[0]
     if inner == 2:
-        (chosen,) = after(chosen, pieces[6:10])
-        (out_own,) = after([w_out], pieces[-6:-2])
+        chosen, out_own = after(chosen + [w_out], pieces[-5:])
         chosen = send(chosen, [(0, 1)])
         far = send(out_own, FAR)
     else:

time: 108 us -> 101 us (0.935)
  waiting for transfers between devices: 34.5 us -> 25.2 us
  starting transfers between devices: 43.9 us -> 46.4 us
    ppermute x28, waiting for transfers between devices: 28 us -> 20.4 us  [gather(): lax.ppermute(found[half, sign * (step - 1)], 'patch', pairs)]
    ppermute x4, starting transfers between devices: 5.94 us -> 7.46 us  [send(): return lax.ppermute(block, ('batch', 'patch'), pairs)]
    ppermute x4, waiting for transfers between devices: 2.5 us -> 1.31 us  [send(): return lax.ppermute(block, ('batch', 'patch'), pairs)]
  transfers between devices with their start and end apart: 39 -> 39, of which waited for: 15 -> 16; matrix products, arithmetic and copies ran while one was open for 2% -> 2% of each run, Pallas kernels for 22% -> 24%
where the time goes in v16:
time: 101 us
  starting transfers between devices  46.4 us (46%)
  Pallas kernels  26.1 us (26%)
  waiting for transfers between devices  25.2 us (25%)
  other arithmetic  1.72 us (2%)
  local copies, waits for them, and re-layouts  1.08 us (1%)
    ppermute x28, starting transfers between devices, gather(): lax.ppermute(found[half, sign * (step - 1)], 'patch', pairs)  30.3 us
    ppermute x28, waiting for transfers between devices, gather(): lax.ppermute(found[half, sign * (step - 1)], 'patch', pairs)  20.4 us
    ppermute x4, starting transfers between devices, send(): return lax.ppermute(block, ('batch', 'patch'), pairs)  7.46 us
    pallas_call x1, Pallas kernels, on_device(): pl.pallas_call(functools.partial(attention_kernel, 2 * n, inner), out_sha...  6.14 us
    pallas_call x1, Pallas kernels, on_device(): pl.pallas_call(functools.partial(conv_kernel, columns), out_shape=[half_h...  5.78 us
    ppermute x3, starting transfers between devices, on_device(): received.append(lax.ppermute(sent_block, 'patch', pairs))  4.75 us
    pallas_call x1, Pallas kernels, on_device(): pl.pallas_call(functools.partial(project_kernel, 2 * n), out_shape=[jax.S...  4.68 us
    ppermute x4, starting transfers between devices, swap(): return lax.ppermute(block, 'batch', pairs)  3.84 us
  transfers between devices with their start and end apart: 39, of which 16 were waited for; matrix products, arithmetic and copies ran while one was open for 2% of the time, Pallas kernels for 24%

profile of v16, /device:TPU:0, one launch (start us, length us, event | category | flops | bytes accessed | tf_op | source)
XLA Modules:
  0.0 100.7 jit_solution(2094960346511572717)
XLA Ops:
  1.0 3.0 %collective-permute-start = (bf16[64,1280]{1,0:T(8,128)(2,1)S(1)}, bf16[64,1280]{1,0:T(8,128)(2,1)S(1)}, u32[]{:S(2)}, u32[]{:S(2)}) collective-permute-start(bf16[64,1280]{1,0:T(8,128)(2,1)S(1)} %get-tuple-element.44.refs_0_), channel_id=1, source_target_pairs={{0,1},{1,3},{3,5},{5,7},{7,6},{6,4},{4,2},{2,0},{8,9},{9,11},{11,1... | collective-permute-start | bytes 491528 | tf_op jit(solution)/shard_map/ppermute | solution.py:407
  4.2 1.9 %collective-permute-start.1 = (bf16[64,1280]{1,0:T(8,128)(2,1)S(1)}, bf16[64,1280]{1,0:T(8,128)(2,1)S(1)}, u32[]{:S(2)}, u32[]{:S(2)}) collective-permute-start(bf16[64,1280]{1,0:T(8,128)(2,1)S(1)} %get-tuple-element.43.refs_1_), channel_id=1, source_target_pairs={{0,1},{1,3},{3,5},{5,7},{7,6},{6,4},{4,2},{2,0},{8,9},{9,11},{11,1... | collective-permute-start | bytes 491528 | tf_op jit(solution)/shard_map/ppermute | solution.py:407
  9.1 2.0 %collective-permute-start.4 = (bf16[64,1280]{1,0:T(8,128)(2,1)S(1)}, bf16[64,1280]{1,0:T(8,128)(2,1)S(1)}, u32[]{:S(2)}, u32[]{:S(2)}) collective-permute-start(bf16[64,1280]{1,0:T(8,128)(2,1)S(1)} %after.7.refs_2_), channel_id=1, source_target_pairs={{0,1},{1,3},{3,5},{5,7},{7,6},{6,4},{4,2},{2,0},{8,9},{9,11},{11,1... | collective-permute-start | bytes 491528 | tf_op jit(solution)/shard_map/ppermute | solution.py:407
  11.1 2.1 %collective-permute-done.3.refs_5_ = bf16[64,1280]{1,0:T(8,128)(2,1)S(1)} collective-permute-done((bf16[64,1280]{1,0:T(8,128)(2,1)S(1)}, bf16[64,1280]{1,0:T(8,128)(2,1)S(1)}, u32[]{:S(2)}, u32[]{:S(2)}) %collective-permute-start.3) | collective-permute-done | bytes 163872 | tf_op jit(solution)/shard_map/ppermute | solution.py:407
  13.6 1.6 %collective-permute-start.5 = (bf16[64,1280]{1,0:T(8,128)(2,1)S(1)}, bf16[64,1280]{1,0:T(8,128)(2,1)S(1)}, u32[]{:S(2)}, u32[]{:S(2)}) collective-permute-start(bf16[64,1280]{1,0:T(8,128)(2,1)S(1)} %collective-permute-done.1.refs_3_), channel_id=1, source_target_pairs={{0,1},{1,3},{3,5},{5,7},{7,6},{6,4},{4,2},{2,0},{8,9},{9,11},{11,1... | collective-permute-start | bytes 491528 | tf_op jit(solution)/shard_map/ppermute | solution.py:407
  15.7 2.1 %collective-permute-start.8 = (bf16[64,1280]{1,0:T(8,128)(2,1)S(1)}, bf16[64,1280]{1,0:T(8,128)(2,1)S(1)}, u32[]{:S(2)}, u32[]{:S(2)}) collective-permute-start(bf16[64,1280]{1,0:T(8,128)(2,1)S(1)} %collective-permute-done.4.refs_6_), channel_id=1, source_target_pairs={{0,1},{1,3},{3,5},{5,7},{7,6},{6,4},{4,2},{2,0},{8,9},{9,11},{11,1... | collective-permute-start | bytes 491528 | tf_op jit(solution)/shard_map/ppermute | solution.py:407
  17.7 2.6 %collective-permute-done.7.refs_9_ = bf16[64,1280]{1,0:T(8,128)(2,1)S(1)} collective-permute-done((bf16[64,1280]{1,0:T(8,128)(2,1)S(1)}, bf16[64,1280]{1,0:T(8,128)(2,1)S(1)}, u32[]{:S(2)}, u32[]{:S(2)}) %collective-permute-start.7) | collective-permute-done | bytes 163872 | tf_op jit(solution)/shard_map/ppermute | solution.py:407
  20.8 1.6 %collective-permute-start.9 = (bf16[64,1280]{1,0:T(8,128)(2,1)S(1)}, bf16[64,1280]{1,0:T(8,128)(2,1)S(1)}, u32[]{:S(2)}, u32[]{:S(2)}) collective-permute-start(bf16[64,1280]{1,0:T(8,128)(2,1)S(1)} %collective-permute-done.5.refs_7_), channel_id=1, source_target_pairs={{0,1},{1,3},{3,5},{5,7},{7,6},{6,4},{4,2},{2,0},{8,9},{9,11},{11,1... | collective-permute-start | bytes 491528 | tf_op jit(solution)/shard_map/ppermute | solution.py:407
  25.1 1.7 %collective-permute-start.12 = (bf16[64,1280]{1,0:T(8,128)(2,1)S(1)}, bf16[64,1280]{1,0:T(8,128)(2,1)S(1)}, u32[]{:S(2)}, u32[]{:S(2)}) collective-permute-start(bf16[64,1280]{1,0:T(8,128)(2,1)S(1)} %after.8.refs_10_), channel_id=1, source_target_pairs={{0,1},{1,3},{3,5},{5,7},{7,6},{6,4},{4,2},{2,0},{8,9},{9,11},{11,1... | collective-permute-start | bytes 491528 | tf_op jit(solution)/shard_map/ppermute | solution.py:407
  27.9 2.3 %collective-permute-done.10.refs_12_.refs_3_ = bf16[64,1280]{1,0:T(8,128)(2,1)S(1)} collective-permute-done((bf16[64,1280]{1,0:T(8,128)(2,1)S(1)}, bf16[64,1280]{1,0:T(8,128)(2,1)S(1)}, u32[]{:S(2)}, u32[]{:S(2)}) %collective-permute-start.10) | collective-permute-done | bytes 163872 | tf_op jit(solution)/shard_map/ppermute | solution.py:407
  30.4 2.9 %collective-permute-done.13.refs_15_.refs_6_ = bf16[64,1280]{1,0:T(8,128)(2,1)S(1)} collective-permute-done((bf16[64,1280]{1,0:T(8,128)(2,1)S(1)}, bf16[64,1280]{1,0:T(8,128)(2,1)S(1)}, u32[]{:S(2)}, u32[]{:S(2)}) %collective-permute-start.13) | collective-permute-done | bytes 163872 | tf_op jit(solution)/shard_map/ppermute | solution.py:407
  34.8 1.8 %collective-permute-start.27 = (bf16[160,1280]{1,0:T(8,128)(2,1)S(1)}, bf16[160,1280]{1,0:T(8,128)(2,1)S(1)}, u32[]{:S(2)}, u32[]{:S(2)}) collective-permute-start(bf16[160,1280]{1,0:T(8,128)(2,1)S(1)} %get-tuple-element.29), channel_id=1, source_target_pairs={{0,2},{1,3},{2,4},{3,5},{4,6},{5,7},{6,0},{7,1},{8,14},{9,15},{10,... | collective-permute-start | bytes 1228808 | tf_op jit(solution)/shard_map/ppermute | solution.py:429
  36.5 5.8 %norm_conv.1 = (bf16[160,512]{1,0:T(8,128)(2,1)S(1)}, bf16[1152,1280]{1,0:T(8,128)(2,1)S(1)}, f32[160,1024]{1,0:T(8,128)S(1)}) custom-call(s32[128]{0:T(128)S(1)} %copy-done.6, bf16[64,1280]{1,0:T(8,128)(2,1)S(1)} %get-tuple-element.44.refs_0_, bf16[64,1280]{1,0:T(8,128)(2,1)S(1)} %get-tuple-element.43.refs_1_, bf16[64,1280]{1,0:T(8,128)(2,1)S(1)} %after.7.refs_2_, ...), custom_call_target="tpu_custom_call" | custom-call | flops 1887436800 | bytes 6307840 | tf_op jit(solution)/shard_map/norm_conv/pallas_call | solution.py:523
  42.4 2.2 %second_conv.1.refs_1_.refs_2_ = bf16[160,512]{1,0:T(8,128)(2,1)S(1)} custom-call(bf16[1152,1280]{1,0:T(8,128)(2,1)S(1)} %get-tuple-element.25.act_ref, f32[160,1024]{1,0:T(8,128)S(1)} %get-tuple-element.26.kept_ref, bf16[3,480,1280]{2,1,0:T(8,128)(2,1)S(1)} %bitcast.8, f32[1,160]{1,0:T(1,128)S(1)} %bitcast.10), custom_call_target="tpu_custom_call" | custom-call | flops 1887436800 | bytes 1887436 | tf_op jit(solution)/shard_map/second_conv/pallas_call | solution.py:540
  44.6 2.1 %collective-permute-start.19 = (bf16[160,512]{1,0:T(8,128)(2,1)S(1)}, bf16[160,512]{1,0:T(8,128)(2,1)S(1)}, u32[]{:S(2)}, u32[]{:S(2)}) collective-permute-start(bf16[160,512]{1,0:T(8,128)(2,1)S(1)} %second_conv.1.refs_1_.refs_2_), channel_id=1, source_target_pairs={{1,0},{3,1},{5,3},{7,5},{6,7},{4,6},{2,4},{0,2},{9,8},{11,9},{13,1... | collective-permute-start | bytes 491528 | tf_op jit(solution)/shard_map/ppermute | solution.py:407
  48.7 3.7 %collective-permute-start.34 = (bf16[160,1280]{1,0:T(8,128)(2,1)S(1)}, bf16[160,1280]{1,0:T(8,128)(2,1)S(1)}, u32[]{:S(2)}, u32[]{:S(2)}) collective-permute-start(bf16[160,1280]{1,0:T(8,128)(2,1)S(1)} %get-tuple-element.40.refs_0_), channel_id=1, source_target_pairs={{0,16},{8,24},{16,0},{24,8},{1,17},{9,25},{17,1},{25,9},{2,18},{10... | collective-permute-start | bytes 1228808 | tf_op jit(solution)/shard_map/ppermute | solution.py:434
  52.4 2.0 %collective-permute-start.15 = (bf16[160,512]{1,0:T(8,128)(2,1)S(1)}, bf16[160,512]{1,0:T(8,128)(2,1)}, u32[]{:S(2)}, u32[]{:S(2)}) collective-permute-start(bf16[160,512]{1,0:T(8,128)(2,1)S(1)} %collective-permute-done.14.refs_2_), channel_id=1, source_target_pairs={{0,1},{1,3},{3,5},{5,7},{7,6},{6,4},{4,2},{2,0},{8,9},{9,11},{11,1... | collective-permute-start | bytes 491528 | tf_op jit(solution)/shard_map/ppermute | solution.py:407
  54.4 2.0 %collective-permute-start.20 = (bf16[160,512]{1,0:T(8,128)(2,1)S(1)}, bf16[160,512]{1,0:T(8,128)(2,1)S(1)}, u32[]{:S(2)}, u32[]{:S(2)}) collective-permute-start(bf16[160,512]{1,0:T(8,128)(2,1)S(1)} %collective-permute-done.17.refs_3_), channel_id=1, source_target_pairs={{0,1},{1,3},{3,5},{5,7},{7,6},{6,4},{4,2},{2,0},{8,9},{9,11},{11,1... | collective-permute-start | bytes 491528 | tf_op jit(solution)/shard_map/ppermute | solution.py:407
  56.5 3.1 %collective-permute-done.15.refs_6_ = bf16[160,512]{1,0:T(8,128)(2,1)} collective-permute-done((bf16[160,512]{1,0:T(8,128)(2,1)S(1)}, bf16[160,512]{1,0:T(8,128)(2,1)}, u32[]{:S(2)}, u32[]{:S(2)}) %collective-permute-start.15) | collective-permute-done | bytes 163872 | tf_op jit(solution)/shard_map/ppermute | solution.py:407
  59.6 2.0 %collective-permute-start.16 = (bf16[160,512]{1,0:T(8,128)(2,1)}, bf16[160,512]{1,0:T(8,128)(2,1)S(1)}, u32[]{:S(2)}, u32[]{:S(2)}) collective-permute-start(bf16[160,512]{1,0:T(8,128)(2,1)} %collective-permute-done.15.refs_6_), channel_id=1, source_target_pairs={{0,1},{1,3},{3,5},{5,7},{7,6},{6,4},{4,2},{2,0},{8,9},{9,11},{11,1... | collective-permute-start | bytes 491528 | tf_op jit(solution)/shard_map/ppermute | solution.py:407
  62.7 2.3 %collective-permute-start.29 = (bf16[160,512]{1,0:T(8,128)(2,1)S(1)}, bf16[160,512]{1,0:T(8,128)(2,1)}, u32[]{:S(2)}, u32[]{:S(2)}) collective-permute-start(bf16[160,512]{1,0:T(8,128)(2,1)S(1)} %collective-permute-done.20.refs_7_), channel_id=1, source_target_pairs={{0,1},{1,3},{3,5},{5,7},{7,6},{6,4},{4,2},{2,0},{8,9},{9,11},{11,1... | collective-permute-start | bytes 491528 | tf_op jit(solution)/shard_map/ppermute | solution.py:407
  65.0 2.5 %early_norm.1 = (bf16[800,1024]{1,0:T(8,128)(2,1)S(1)}, bf16[800,128]{1,0:T(8,128)(2,1)S(1)}) custom-call(bf16[160,512]{1,0:T(8,128)(2,1)S(1)} %get-tuple-element.24.refs_0_, bf16[160,512]{1,0:T(8,128)(2,1)S(1)} %second_conv.1.refs_1_.refs_2_, bf16[160,512]{1,0:T(8,128)(2,1)S(1)} %collective-permute-done.14.refs_2_, ...), custom_call_target="tpu_custom_call" | custom-call | flops 10485760 | bytes 5242880 | tf_op jit(solution)/shard_map/early_norm/pallas_call | solution.py:555
  67.5 2.1 %collective-permute-start.23 = (bf16[160,512]{1,0:T(8,128)(2,1)S(1)}, bf16[160,512]{1,0:T(8,128)(2,1)S(1)}, u32[]{:S(2)}, u32[]{:S(2)}) collective-permute-start(bf16[160,512]{1,0:T(8,128)(2,1)S(1)} %after.9.refs_2_), channel_id=1, source_target_pairs={{0,1},{1,3},{3,5},{5,7},{7,6},{6,4},{4,2},{2,0},{8,9},{9,11},{11,1... | collective-permute-start | bytes 491528 | tf_op jit(solution)/shard_map/ppermute | solution.py:407
  69.7 2.4 %collective-permute-done.30.refs_4_ = bf16[160,512]{1,0:T(8,128)(2,1)} collective-permute-done((bf16[160,512]{1,0:T(8,128)(2,1)S(1)}, bf16[160,512]{1,0:T(8,128)(2,1)}, u32[]{:S(2)}, u32[]{:S(2)}) %collective-permute-start.30) | collective-permute-done | bytes 163872 | tf_op jit(solution)/shard_map/ppermute | solution.py:407
  72.1 2.4 %collective-permute-start.37 = (bf16[160,1280]{1,0:T(8,128)(2,1)S(1)}, bf16[160,1280]{1,0:T(8,128)(2,1)S(1)}, u32[]{:S(2)}, u32[]{:S(2)}) collective-permute-start(bf16[160,1280]{1,0:T(8,128)(2,1)S(1)} %get-tuple-element.42.refs_7_), channel_id=1, source_target_pairs={{0,1},{1,0},{2,3},{3,2},{4,5},{5,4},{6,7},{7,6},{16,17},{17,16},{1... | collective-permute-start | bytes 1228808 | tf_op jit(solution)/shard_map/ppermute | solution.py:429
  74.5 2.0 %collective-permute-start.36 = (bf16[160,1280]{1,0:T(8,128)(2,1)S(1)}, bf16[160,1280]{1,0:T(8,128)(2,1)S(1)}, u32[]{:S(2)}, u32[]{:S(2)}) collective-permute-start(bf16[160,1280]{1,0:T(8,128)(2,1)S(1)} %broadcast_select_fusion), channel_id=1, source_target_pairs={{0,1},{1,0},{2,3},{3,2},{4,5},{5,4},{6,7},{7,6},{8,9},{9,8},{10,11... | collective-permute-start | bytes 1228808 | tf_op jit(solution)/shard_map/ppermute | solution.py:429
  76.6 4.7 %norm_project.1 = (f32[960,1024]{1,0:T(8,128)S(1)}, bf16[1280,128]{1,0:T(8,128)(2,1)S(1)}) custom-call(s32[128]{0:T(128)S(1)} %copy-done.6, bf16[800,1024]{1,0:T(8,128)(2,1)S(1)} %get-tuple-element.27.refs_1_.refs_0_, bf16[800,128]{1,0:T(8,128)(2,1)S(1)} %get-tuple-element.31.refs_1_, bf16[160,512]{1,0:T(8,128)(2,1)S(1)} %after.9.refs_2_, ...), custom_call_target="tpu_custom_call" | custom-call | flops 2516582400 | bytes 5079040 | tf_op jit(solution)/shard_map/norm_project/pallas_call | solution.py:583
  81.3 6.1 %attention.1 = (bf16[320,128]{1,0:T(8,128)(2,1)S(1)}, bf16[320,128]{1,0:T(8,128)(2,1)S(1)}, bf16[320,128]{1,0:T(8,128)(2,1)S(1)}, bf16[1280,128]{1,0:T(8,128)(2,...) custom-call(s32[128]{0:T(128)S(1)} %copy-done.6, ...), custom_call_target="tpu_custom_call" | custom-call | flops 1258291200 | bytes 5898240 | tf_op jit(solution)/shard_map/attention/pallas_call | solution.py:607
  88.7 3.3 %collective-permute-start.32 = (bf16[320,128]{1,0:T(8,128)(2,1)S(1)}, bf16[320,128]{1,0:T(8,128)(2,1)S(1)}, u32[]{:S(2)}, u32[]{:S(2)}) collective-permute-start(bf16[320,128]{1,0:T(8,128)(2,1)S(1)} %get-tuple-element.37), channel_id=1, source_target_pairs={{0,4},{1,5},{2,6},{3,7},{4,0},{5,1},{6,2},{7,3},{8,12},{9,13},{10,... | collective-permute-start | bytes 245768 | tf_op jit(solution)/shard_map/ppermute | solution.py:630
  93.2 1.9 %own_attention.1.refs_0_ = bf16[320,128]{1,0:T(8,128)(2,1)S(1)} custom-call(bf16[960,1024]{1,0:T(8,128)(2,1)S(1)} %get-tuple-element.34.made_ref, bf16[5,1024,64]{2,1,0:T(8,128)(2,1)S(1)} %get-tuple-element.35.key_ref), custom_call_target="tpu_custom_call" | custom-call | flops 167772160 | bytes 2621440 | tf_op jit(solution)/shard_map/own_attention/pallas_call | solution.py:631
  95.6 3.0 %collective-permute-done.32.refs_2_ = bf16[320,128]{1,0:T(8,128)(2,1)S(1)} collective-permute-done((bf16[320,128]{1,0:T(8,128)(2,1)S(1)}, bf16[320,128]{1,0:T(8,128)(2,1)S(1)}, u32[]{:S(2)}, u32[]{:S(2)}) %collective-permute-start.32) | collective-permute-done | bytes 81952 | tf_op jit(solution)/shard_map/ppermute | solution.py:630
  98.6 2.1 %project.1 = bf16[128,1280]{1,0:T(8,128)(2,1)} custom-call(bf16[320,128]{1,0:T(8,128)(2,1)S(1)} %own_attention.1.refs_0_, bf16[320,128]{1,0:T(8,128)(2,1)S(1)} %collective-permute-done.31.refs_1_, bf16[320,128]{1,0:T(8,128)(2,1)S(1)} %collective-permute-done.32.refs_2_, bf16[320,128]{1,0:T(8,128)(2,1)S(1)} %collective-permute-done.33.refs_3_, ...), custom_call_target="tpu_custom_call" | custom-call | flops 419430400 | bytes 4259840 | tf_op jit(solution)/shard_map/project/pallas_call | solution.py:648
  (81 shorter events, 17.3 us)
Async XLA Ops:
  1.0 8.1 %collective-permute-start = (bf16[64,1280]{1,0:T(8,128)(2,1)S(1)}, bf16[64,1280]{1,0:T(8,128)(2,1)S(1)}, u32[]{:S(2)}, u32[]{:S(2)}) collective-permute-start(bf16[64,1280]{1,0:T(8,128)(2,1)S(1)} %get-tuple-element.44.refs_0_), channel_id=1, source_target_pairs={{0,1},{1,3},{3,5},{5,7},{7,6},{6,4},{4,2},{2,0},{8,9},{9,11},{11,1... | collective-permute-start | bytes 491528 | tf_op jit(solution)/shard_map/ppermute | solution.py:407
  4.0 11.2 %collective-permute-start.2 = (bf16[64,1280]{1,0:T(8,128)(2,1)S(1)}, bf16[64,1280]{1,0:T(8,128)(2,1)S(1)}, u32[]{:S(2)}, u32[]{:S(2)}) collective-permute-start(bf16[64,1280]{1,0:T(8,128)(2,1)S(1)} %get-tuple-element.44.refs_0_), channel_id=1, source_target_pairs={{1,0},{3,1},{5,3},{7,5},{6,7},{4,6},{2,4},{0,2},{9,8},{11,9},{13,1... | collective-permute-start | bytes 491528 | tf_op jit(solution)/shard_map/ppermute | solution.py:407
  4.2 9.5 %collective-permute-start.1 = (bf16[64,1280]{1,0:T(8,128)(2,1)S(1)}, bf16[64,1280]{1,0:T(8,128)(2,1)S(1)}, u32[]{:S(2)}, u32[]{:S(2)}) collective-permute-start(bf16[64,1280]{1,0:T(8,128)(2,1)S(1)} %get-tuple-element.43.refs_1_), channel_id=1, source_target_pairs={{0,1},{1,3},{3,5},{5,7},{7,6},{6,4},{4,2},{2,0},{8,9},{9,11},{11,1... | collective-permute-start | bytes 491528 | tf_op jit(solution)/shard_map/ppermute | solution.py:407
  6.1 7.1 %collective-permute-start.3 = (bf16[64,1280]{1,0:T(8,128)(2,1)S(1)}, bf16[64,1280]{1,0:T(8,128)(2,1)S(1)}, u32[]{:S(2)}, u32[]{:S(2)}) collective-permute-start(bf16[64,1280]{1,0:T(8,128)(2,1)S(1)} %get-tuple-element.43.refs_1_), channel_id=1, source_target_pairs={{1,0},{3,1},{5,3},{7,5},{6,7},{4,6},{2,4},{0,2},{9,8},{11,9},{13,1... | collective-permute-start | bytes 491528 | tf_op jit(solution)/shard_map/ppermute | solution.py:407
  13.2 7.1 %collective-permute-start.7 = (bf16[64,1280]{1,0:T(8,128)(2,1)S(1)}, bf16[64,1280]{1,0:T(8,128)(2,1)S(1)}, u32[]{:S(2)}, u32[]{:S(2)}) collective-permute-start(bf16[64,1280]{1,0:T(8,128)(2,1)S(1)} %collective-permute-done.3.refs_5_), channel_id=1, source_target_pairs={{1,0},{3,1},{5,3},{7,5},{6,7},{4,6},{2,4},{0,2},{9,8},{11,9},{13,1... | collective-permute-start | bytes 491528 | tf_op jit(solution)/shard_map/ppermute | solution.py:407
  13.6 7.1 %collective-permute-start.5 = (bf16[64,1280]{1,0:T(8,128)(2,1)S(1)}, bf16[64,1280]{1,0:T(8,128)(2,1)S(1)}, u32[]{:S(2)}, u32[]{:S(2)}) collective-permute-start(bf16[64,1280]{1,0:T(8,128)(2,1)S(1)} %collective-permute-done.1.refs_3_), channel_id=1, source_target_pairs={{0,1},{1,3},{3,5},{5,7},{7,6},{6,4},{4,2},{2,0},{8,9},{9,11},{11,1... | collective-permute-start | bytes 491528 | tf_op jit(solution)/shard_map/ppermute | solution.py:407
  15.2 8.6 %collective-permute-start.6 = (bf16[64,1280]{1,0:T(8,128)(2,1)S(1)}, bf16[64,1280]{1,0:T(8,128)(2,1)S(1)}, u32[]{:S(2)}, u32[]{:S(2)}) collective-permute-start(bf16[64,1280]{1,0:T(8,128)(2,1)S(1)} %collective-permute-done.2.refs_4_), channel_id=1, source_target_pairs={{1,0},{3,1},{5,3},{7,5},{6,7},{4,6},{2,4},{0,2},{9,8},{11,9},{13,1... | collective-permute-start | bytes 491528 | tf_op jit(solution)/shard_map/ppermute | solution.py:407
  15.7 9.4 %collective-permute-start.8 = (bf16[64,1280]{1,0:T(8,128)(2,1)S(1)}, bf16[64,1280]{1,0:T(8,128)(2,1)S(1)}, u32[]{:S(2)}, u32[]{:S(2)}) collective-permute-start(bf16[64,1280]{1,0:T(8,128)(2,1)S(1)} %collective-permute-done.4.refs_6_), channel_id=1, source_target_pairs={{0,1},{1,3},{3,5},{5,7},{7,6},{6,4},{4,2},{2,0},{8,9},{9,11},{11,1... | collective-permute-start | bytes 491528 | tf_op jit(solution)/shard_map/ppermute | solution.py:407
  20.3 7.1 %collective-permute-start.11 = (bf16[64,1280]{1,0:T(8,128)(2,1)S(1)}, bf16[64,1280]{1,0:T(8,128)(2,1)S(1)}, u32[]{:S(2)}, u32[]{:S(2)}) collective-permute-start(bf16[64,1280]{1,0:T(8,128)(2,1)S(1)} %collective-permute-done.7.refs_9_), channel_id=1, source_target_pairs={{1,0},{3,1},{5,3},{7,5},{6,7},{4,6},{2,4},{0,2},{9,8},{11,9},{13,1... | collective-permute-start | bytes 491528 | tf_op jit(solution)/shard_map/ppermute | solution.py:407
  20.8 7.2 %collective-permute-start.9 = (bf16[64,1280]{1,0:T(8,128)(2,1)S(1)}, bf16[64,1280]{1,0:T(8,128)(2,1)S(1)}, u32[]{:S(2)}, u32[]{:S(2)}) collective-permute-start(bf16[64,1280]{1,0:T(8,128)(2,1)S(1)} %collective-permute-done.5.refs_7_), channel_id=1, source_target_pairs={{0,1},{1,3},{3,5},{5,7},{7,6},{6,4},{4,2},{2,0},{8,9},{9,11},{11,1... | collective-permute-start | bytes 491528 | tf_op jit(solution)/shard_map/ppermute | solution.py:407
  33.4 15.3 %collective-permute-start.26 = (bf16[240,1280]{1,0:T(8,128)(2,1)S(1)}, bf16[240,1280]{1,0:T(8,128)(2,1)S(1)}, u32[]{:S(2)}, u32[]{:S(2)}) collective-permute-start(bf16[240,1280]{1,0:T(8,128)(2,1)S(1)} %get-tuple-element.28), channel_id=1, source_target_pairs={{0,1},{1,0},{2,3},{3,2},{4,5},{5,4},{6,7},{7,6},{8,9},{9,8},{10,11... | collective-permute-start | bytes 1843208 | tf_op jit(solution)/shard_map/ppermute | solution.py:429
  34.8 12.4 %collective-permute-start.27 = (bf16[160,1280]{1,0:T(8,128)(2,1)S(1)}, bf16[160,1280]{1,0:T(8,128)(2,1)S(1)}, u32[]{:S(2)}, u32[]{:S(2)}) collective-permute-start(bf16[160,1280]{1,0:T(8,128)(2,1)S(1)} %get-tuple-element.29), channel_id=1, source_target_pairs={{0,2},{1,3},{2,4},{3,5},{4,6},{5,7},{6,0},{7,1},{8,14},{9,15},{10,... | collective-permute-start | bytes 1228808 | tf_op jit(solution)/shard_map/ppermute | solution.py:429
  42.3 10.1 %collective-permute-start.14 = (bf16[160,512]{1,0:T(8,128)(2,1)S(1)}, bf16[160,512]{1,0:T(8,128)(2,1)S(1)}, u32[]{:S(2)}, u32[]{:S(2)}) collective-permute-start(bf16[160,512]{1,0:T(8,128)(2,1)S(1)} %get-tuple-element.24.refs_0_), channel_id=1, source_target_pairs={{0,1},{1,3},{3,5},{5,7},{7,6},{6,4},{4,2},{2,0},{8,9},{9,11},{11,1... | collective-permute-start | bytes 491528 | tf_op jit(solution)/shard_map/ppermute | solution.py:407
  44.6 9.8 %collective-permute-start.19 = (bf16[160,512]{1,0:T(8,128)(2,1)S(1)}, bf16[160,512]{1,0:T(8,128)(2,1)S(1)}, u32[]{:S(2)}, u32[]{:S(2)}) collective-permute-start(bf16[160,512]{1,0:T(8,128)(2,1)S(1)} %second_conv.1.refs_1_.refs_2_), channel_id=1, source_target_pairs={{1,0},{3,1},{5,3},{7,5},{6,7},{4,6},{2,4},{0,2},{9,8},{11,9},{13,1... | collective-permute-start | bytes 491528 | tf_op jit(solution)/shard_map/ppermute | solution.py:407
  46.7 7.7 %collective-permute-start.17 = (bf16[160,512]{1,0:T(8,128)(2,1)S(1)}, bf16[160,512]{1,0:T(8,128)(2,1)S(1)}, u32[]{:S(2)}, u32[]{:S(2)}) collective-permute-start(bf16[160,512]{1,0:T(8,128)(2,1)S(1)} %second_conv.1.refs_1_.refs_2_), channel_id=1, source_target_pairs={{0,1},{1,3},{3,5},{5,7},{7,6},{6,4},{4,2},{2,0},{8,9},{9,11},{11,1... | collective-permute-start | bytes 491528 | tf_op jit(solution)/shard_map/ppermute | solution.py:407
  47.2 9.2 %collective-permute-start.18 = (bf16[160,512]{1,0:T(8,128)(2,1)S(1)}, bf16[160,512]{1,0:T(8,128)(2,1)S(1)}, u32[]{:S(2)}, u32[]{:S(2)}) collective-permute-start(bf16[160,512]{1,0:T(8,128)(2,1)S(1)} %get-tuple-element.24.refs_0_), channel_id=1, source_target_pairs={{1,0},{3,1},{5,3},{7,5},{6,7},{4,6},{2,4},{0,2},{9,8},{11,9},{13,1... | collective-permute-start | bytes 491528 | tf_op jit(solution)/shard_map/ppermute | solution.py:407
  48.7 23.3 %collective-permute-start.34 = (bf16[160,1280]{1,0:T(8,128)(2,1)S(1)}, bf16[160,1280]{1,0:T(8,128)(2,1)S(1)}, u32[]{:S(2)}, u32[]{:S(2)}) collective-permute-start(bf16[160,1280]{1,0:T(8,128)(2,1)S(1)} %get-tuple-element.40.refs_0_), channel_id=1, source_target_pairs={{0,16},{8,24},{16,0},{24,8},{1,17},{9,25},{17,1},{25,9},{2,18},{10... | collective-permute-start | bytes 1228808 | tf_op jit(solution)/shard_map/ppermute | solution.py:434
  52.4 7.2 %collective-permute-start.15 = (bf16[160,512]{1,0:T(8,128)(2,1)S(1)}, bf16[160,512]{1,0:T(8,128)(2,1)}, u32[]{:S(2)}, u32[]{:S(2)}) collective-permute-start(bf16[160,512]{1,0:T(8,128)(2,1)S(1)} %collective-permute-done.14.refs_2_), channel_id=1, source_target_pairs={{0,1},{1,3},{3,5},{5,7},{7,6},{6,4},{4,2},{2,0},{8,9},{9,11},{11,1... | collective-permute-start | bytes 491528 | tf_op jit(solution)/shard_map/ppermute | solution.py:407
  54.4 7.2 %collective-permute-start.22 = (bf16[160,512]{1,0:T(8,128)(2,1)S(1)}, bf16[160,512]{1,0:T(8,128)(2,1)S(1)}, u32[]{:S(2)}, u32[]{:S(2)}) collective-permute-start(bf16[160,512]{1,0:T(8,128)(2,1)S(1)} %collective-permute-done.19.refs_5_), channel_id=1, source_target_pairs={{1,0},{3,1},{5,3},{7,5},{6,7},{4,6},{2,4},{0,2},{9,8},{11,9},{13,1... | collective-permute-start | bytes 491528 | tf_op jit(solution)/shard_map/ppermute | solution.py:407
  54.4 8.3 %collective-permute-start.20 = (bf16[160,512]{1,0:T(8,128)(2,1)S(1)}, bf16[160,512]{1,0:T(8,128)(2,1)S(1)}, u32[]{:S(2)}, u32[]{:S(2)}) collective-permute-start(bf16[160,512]{1,0:T(8,128)(2,1)S(1)} %collective-permute-done.17.refs_3_), channel_id=1, source_target_pairs={{0,1},{1,3},{3,5},{5,7},{7,6},{6,4},{4,2},{2,0},{8,9},{9,11},{11,1... | collective-permute-start | bytes 491528 | tf_op jit(solution)/shard_map/ppermute | solution.py:407
  56.4 8.6 %collective-permute-start.21 = (bf16[160,512]{1,0:T(8,128)(2,1)S(1)}, bf16[160,512]{1,0:T(8,128)(2,1)S(1)}, u32[]{:S(2)}, u32[]{:S(2)}) collective-permute-start(bf16[160,512]{1,0:T(8,128)(2,1)S(1)} %collective-permute-done.18.refs_4_), channel_id=1, source_target_pairs={{1,0},{3,1},{5,3},{7,5},{6,7},{4,6},{2,4},{0,2},{9,8},{11,9},{13,1... | collective-permute-start | bytes 491528 | tf_op jit(solution)/shard_map/ppermute | solution.py:407
  59.6 7.9 %collective-permute-start.16 = (bf16[160,512]{1,0:T(8,128)(2,1)}, bf16[160,512]{1,0:T(8,128)(2,1)S(1)}, u32[]{:S(2)}, u32[]{:S(2)}) collective-permute-start(bf16[160,512]{1,0:T(8,128)(2,1)} %collective-permute-done.15.refs_6_), channel_id=1, source_target_pairs={{0,1},{1,3},{3,5},{5,7},{7,6},{6,4},{4,2},{2,0},{8,9},{9,11},{11,1... | collective-permute-start | bytes 491528 | tf_op jit(solution)/shard_map/ppermute | solution.py:407
  61.6 8.0 %collective-permute-start.24 = (bf16[160,512]{1,0:T(8,128)(2,1)S(1)}, bf16[160,512]{1,0:T(8,128)(2,1)}, u32[]{:S(2)}, u32[]{:S(2)}) collective-permute-start(bf16[160,512]{1,0:T(8,128)(2,1)S(1)} %collective-permute-done.22.refs_9_), channel_id=1, source_target_pairs={{1,0},{3,1},{5,3},{7,5},{6,7},{4,6},{2,4},{0,2},{9,8},{11,9},{13,1... | collective-permute-start | bytes 491528 | tf_op jit(solution)/shard_map/ppermute | solution.py:407
  65.0 7.0 %collective-permute-start.30 = (bf16[160,512]{1,0:T(8,128)(2,1)S(1)}, bf16[160,512]{1,0:T(8,128)(2,1)}, u32[]{:S(2)}, u32[]{:S(2)}) collective-permute-start(bf16[160,512]{1,0:T(8,128)(2,1)S(1)} %collective-permute-done.21.refs_8_), channel_id=1, source_target_pairs={{1,0},{3,1},{5,3},{7,5},{6,7},{4,6},{2,4},{0,2},{9,8},{11,9},{13,1... | collective-permute-start | bytes 491528 | tf_op jit(solution)/shard_map/ppermute | solution.py:407
  67.5 13.8 %collective-permute-start.23 = (bf16[160,512]{1,0:T(8,128)(2,1)S(1)}, bf16[160,512]{1,0:T(8,128)(2,1)S(1)}, u32[]{:S(2)}, u32[]{:S(2)}) collective-permute-start(bf16[160,512]{1,0:T(8,128)(2,1)S(1)} %after.9.refs_2_), channel_id=1, source_target_pairs={{0,1},{1,3},{3,5},{5,7},{7,6},{6,4},{4,2},{2,0},{8,9},{9,11},{11,1... | collective-permute-start | bytes 491528 | tf_op jit(solution)/shard_map/ppermute | solution.py:407
  69.6 11.7 %collective-permute-start.25 = (bf16[160,512]{1,0:T(8,128)(2,1)}, bf16[160,512]{1,0:T(8,128)(2,1)S(1)}, u32[]{:S(2)}, u32[]{:S(2)}) collective-permute-start(bf16[160,512]{1,0:T(8,128)(2,1)} %collective-permute-done.24.refs_5_), channel_id=1, source_target_pairs={{1,0},{3,1},{5,3},{7,5},{6,7},{4,6},{2,4},{0,2},{9,8},{11,9},{13,1... | collective-permute-start | bytes 491528 | tf_op jit(solution)/shard_map/ppermute | solution.py:407
  72.1 15.4 %collective-permute-start.37 = (bf16[160,1280]{1,0:T(8,128)(2,1)S(1)}, bf16[160,1280]{1,0:T(8,128)(2,1)S(1)}, u32[]{:S(2)}, u32[]{:S(2)}) collective-permute-start(bf16[160,1280]{1,0:T(8,128)(2,1)S(1)} %get-tuple-element.42.refs_7_), channel_id=1, source_target_pairs={{0,1},{1,0},{2,3},{3,2},{4,5},{5,4},{6,7},{7,6},{16,17},{17,16},{1... | collective-permute-start | bytes 1228808 | tf_op jit(solution)/shard_map/ppermute | solution.py:429
  74.5 13.8 %collective-permute-start.36 = (bf16[160,1280]{1,0:T(8,128)(2,1)S(1)}, bf16[160,1280]{1,0:T(8,128)(2,1)S(1)}, u32[]{:S(2)}, u32[]{:S(2)}) collective-permute-start(bf16[160,1280]{1,0:T(8,128)(2,1)S(1)} %broadcast_select_fusion), channel_id=1, source_target_pairs={{0,1},{1,0},{2,3},{3,2},{4,5},{5,4},{6,7},{7,6},{8,9},{9,8},{10,11... | collective-permute-start | bytes 1228808 | tf_op jit(solution)/shard_map/ppermute | solution.py:429
  76.5 22.1 %collective-permute-start.35 = (bf16[320,1280]{1,0:T(8,128)(2,1)S(1)}, bf16[320,1280]{1,0:T(8,128)(2,1)S(1)}, u32[]{:S(2)}, u32[]{:S(2)}) collective-permute-start(bf16[320,1280]{1,0:T(8,128)(2,1)S(1)} %pad_maximum_fusion), channel_id=1, source_target_pairs={{0,8},{8,0},{16,24},{24,16},{1,9},{9,1},{17,25},{25,17},{2,10},{10... | collective-permute-start | bytes 2457608 | tf_op jit(solution)/shard_map/ppermute | solution.py:434
  88.3 10.3 %collective-permute-start.38 = (bf16[320,1280]{1,0:T(8,128)(2,1)S(1)}, bf16[320,1280]{1,0:T(8,128)(2,1)S(1)}, u32[]{:S(2)}, u32[]{:S(2)}) collective-permute-start(bf16[320,1280]{1,0:T(8,128)(2,1)S(1)} %after.13.refs_9_), channel_id=1, source_target_pairs={{0,8},{8,0},{16,24},{24,16},{1,9},{9,1},{17,25},{25,17},{2,10},{10... | collective-permute-start | bytes 2457608 | tf_op jit(solution)/shard_map/ppermute | solution.py:434
  88.4 7.2 %collective-permute-start.31 = (bf16[320,128]{1,0:T(8,128)(2,1)S(1)}, bf16[320,128]{1,0:T(8,128)(2,1)S(1)}, u32[]{:S(2)}, u32[]{:S(2)}) collective-permute-start(bf16[320,128]{1,0:T(8,128)(2,1)S(1)} %get-tuple-element.36.refs_1_), channel_id=1, source_target_pairs={{0,2},{1,3},{2,4},{3,5},{4,6},{5,7},{6,0},{7,1},{8,10},{9,11},{10,... | collective-permute-start | bytes 245768 | tf_op jit(solution)/shard_map/ppermute | solution.py:630
  88.7 9.9 %collective-permute-start.32 = (bf16[320,128]{1,0:T(8,128)(2,1)S(1)}, bf16[320,128]{1,0:T(8,128)(2,1)S(1)}, u32[]{:S(2)}, u32[]{:S(2)}) collective-permute-start(bf16[320,128]{1,0:T(8,128)(2,1)S(1)} %get-tuple-element.37), channel_id=1, source_target_pairs={{0,4},{1,5},{2,6},{3,7},{4,0},{5,1},{6,2},{7,3},{8,12},{9,13},{10,... | collective-permute-start | bytes 245768 | tf_op jit(solution)/shard_map/ppermute | solution.py:630
  (14 other events, 113.7 us)

commit v17 on v16

--- a/solution.py
+++ b/solution.py
@@ -642,7 +642,7 @@
         name="own_attention",
     )(made, key)
     if inner == 2:
-        (relayed,) = after([jnp.concatenate(relayed, axis=0)], sent[:1])
+        (relayed,) = after([jnp.concatenate(relayed, axis=0)], received[1:2])
         out_weights = [w_out] + far + [relayed, swap(relayed, 1)]
 
     output = pl.pallas_call(

time: 101 us -> 103 us (1.020)
  waiting for transfers between devices: 25.2 us -> 31.3 us
  starting transfers between devices: 46.4 us -> 42.4 us
    ppermute x3, waiting for transfers between devices: 3.47 us -> 9.6 us  [on_device(): received.append(lax.ppermute(sent_block, 'patch', pairs))]
    ppermute x3, starting transfers between devices: 4.75 us -> 0.91 us  [on_device(): received.append(lax.ppermute(sent_block, 'patch', pairs))]
  transfers between devices with their start and end apart: 39 -> 39, of which waited for: 16 -> 17; matrix products, arithmetic and copies ran while one was open for 2% -> 2% of each run, Pallas kernels for 24% -> 23%
where the time goes in v17:
time: 103 us
  starting transfers between devices  42.4 us (41%)
  waiting for transfers between devices  31.3 us (30%)
  Pallas kernels  26.1 us (25%)
  other arithmetic  1.72 us (2%)
  local copies, waits for them, and re-layouts  1.08 us (1%)
    ppermute x28, starting transfers between devices, gather(): lax.ppermute(found[half, sign * (step - 1)], 'patch', pairs)  30.3 us
    ppermute x28, waiting for transfers between devices, gather(): lax.ppermute(found[half, sign * (step - 1)], 'patch', pairs)  20.4 us
    ppermute x3, waiting for transfers between devices, on_device(): received.append(lax.ppermute(sent_block, 'patch', pairs))  9.6 us
    ppermute x4, starting transfers between devices, send(): return lax.ppermute(block, ('batch', 'patch'), pairs)  7.46 us
    pallas_call x1, Pallas kernels, on_device(): pl.pallas_call(functools.partial(attention_kernel, 2 * n, inner), out_sha...  6.14 us
    pallas_call x1, Pallas kernels, on_device(): pl.pallas_call(functools.partial(conv_kernel, columns), out_shape=[half_h...  5.78 us
    pallas_call x1, Pallas kernels, on_device(): pl.pallas_call(functools.partial(project_kernel, 2 * n), out_shape=[jax.S...  4.68 us
    ppermute x4, starting transfers between devices, swap(): return lax.ppermute(block, 'batch', pairs)  3.77 us
  transfers between devices with their start and end apart: 39, of which 17 were waited for; matrix products, arithmetic and copies ran while one was open for 2% of the time, Pallas kernels for 23%

profile of v17, /device:TPU:0, one launch (start us, length us, event | category | flops | bytes accessed | tf_op | source)
XLA Modules:
  0.0 102.9 jit_solution(14471973561878561425)
XLA Ops:
  1.0 3.0 %collective-permute-start = (bf16[64,1280]{1,0:T(8,128)(2,1)S(1)}, bf16[64,1280]{1,0:T(8,128)(2,1)S(1)}, u32[]{:S(2)}, u32[]{:S(2)}) collective-permute-start(bf16[64,1280]{1,0:T(8,128)(2,1)S(1)} %get-tuple-element.44.refs_0_), channel_id=1, source_target_pairs={{0,1},{1,3},{3,5},{5,7},{7,6},{6,4},{4,2},{2,0},{8,9},{9,11},{11,1... | collective-permute-start | bytes 491528 | tf_op jit(solution)/shard_map/ppermute | solution.py:407
  4.2 1.9 %collective-permute-start.1 = (bf16[64,1280]{1,0:T(8,128)(2,1)S(1)}, bf16[64,1280]{1,0:T(8,128)(2,1)S(1)}, u32[]{:S(2)}, u32[]{:S(2)}) collective-permute-start(bf16[64,1280]{1,0:T(8,128)(2,1)S(1)} %get-tuple-element.43.refs_1_), channel_id=1, source_target_pairs={{0,1},{1,3},{3,5},{5,7},{7,6},{6,4},{4,2},{2,0},{8,9},{9,11},{11,1... | collective-permute-start | bytes 491528 | tf_op jit(solution)/shard_map/ppermute | solution.py:407
  9.1 2.0 %collective-permute-start.4 = (bf16[64,1280]{1,0:T(8,128)(2,1)S(1)}, bf16[64,1280]{1,0:T(8,128)(2,1)S(1)}, u32[]{:S(2)}, u32[]{:S(2)}) collective-permute-start(bf16[64,1280]{1,0:T(8,128)(2,1)S(1)} %after.7.refs_2_), channel_id=1, source_target_pairs={{0,1},{1,3},{3,5},{5,7},{7,6},{6,4},{4,2},{2,0},{8,9},{9,11},{11,1... | collective-permute-start | bytes 491528 | tf_op jit(solution)/shard_map/ppermute | solution.py:407
  11.1 2.1 %collective-permute-done.3.refs_5_ = bf16[64,1280]{1,0:T(8,128)(2,1)S(1)} collective-permute-done((bf16[64,1280]{1,0:T(8,128)(2,1)S(1)}, bf16[64,1280]{1,0:T(8,128)(2,1)S(1)}, u32[]{:S(2)}, u32[]{:S(2)}) %collective-permute-start.3) | collective-permute-done | bytes 163872 | tf_op jit(solution)/shard_map/ppermute | solution.py:407
  13.6 1.6 %collective-permute-start.5 = (bf16[64,1280]{1,0:T(8,128)(2,1)S(1)}, bf16[64,1280]{1,0:T(8,128)(2,1)S(1)}, u32[]{:S(2)}, u32[]{:S(2)}) collective-permute-start(bf16[64,1280]{1,0:T(8,128)(2,1)S(1)} %collective-permute-done.1.refs_3_), channel_id=1, source_target_pairs={{0,1},{1,3},{3,5},{5,7},{7,6},{6,4},{4,2},{2,0},{8,9},{9,11},{11,1... | collective-permute-start | bytes 491528 | tf_op jit(solution)/shard_map/ppermute | solution.py:407
  15.7 2.1 %collective-permute-start.8 = (bf16[64,1280]{1,0:T(8,128)(2,1)S(1)}, bf16[64,1280]{1,0:T(8,128)(2,1)S(1)}, u32[]{:S(2)}, u32[]{:S(2)}) collective-permute-start(bf16[64,1280]{1,0:T(8,128)(2,1)S(1)} %collective-permute-done.4.refs_6_), channel_id=1, source_target_pairs={{0,1},{1,3},{3,5},{5,7},{7,6},{6,4},{4,2},{2,0},{8,9},{9,11},{11,1... | collective-permute-start | bytes 491528 | tf_op jit(solution)/shard_map/ppermute | solution.py:407
  17.7 2.6 %collective-permute-done.7.refs_9_ = bf16[64,1280]{1,0:T(8,128)(2,1)S(1)} collective-permute-done((bf16[64,1280]{1,0:T(8,128)(2,1)S(1)}, bf16[64,1280]{1,0:T(8,128)(2,1)S(1)}, u32[]{:S(2)}, u32[]{:S(2)}) %collective-permute-start.7) | collective-permute-done | bytes 163872 | tf_op jit(solution)/shard_map/ppermute | solution.py:407
  20.8 1.6 %collective-permute-start.9 = (bf16[64,1280]{1,0:T(8,128)(2,1)S(1)}, bf16[64,1280]{1,0:T(8,128)(2,1)S(1)}, u32[]{:S(2)}, u32[]{:S(2)}) collective-permute-start(bf16[64,1280]{1,0:T(8,128)(2,1)S(1)} %collective-permute-done.5.refs_7_), channel_id=1, source_target_pairs={{0,1},{1,3},{3,5},{5,7},{7,6},{6,4},{4,2},{2,0},{8,9},{9,11},{11,1... | collective-permute-start | bytes 491528 | tf_op jit(solution)/shard_map/ppermute | solution.py:407
  25.1 1.7 %collective-permute-start.12 = (bf16[64,1280]{1,0:T(8,128)(2,1)S(1)}, bf16[64,1280]{1,0:T(8,128)(2,1)S(1)}, u32[]{:S(2)}, u32[]{:S(2)}) collective-permute-start(bf16[64,1280]{1,0:T(8,128)(2,1)S(1)} %after.8.refs_10_), channel_id=1, source_target_pairs={{0,1},{1,3},{3,5},{5,7},{7,6},{6,4},{4,2},{2,0},{8,9},{9,11},{11,1... | collective-permute-start | bytes 491528 | tf_op jit(solution)/shard_map/ppermute | solution.py:407
  27.9 2.3 %collective-permute-done.10.refs_12_.refs_3_ = bf16[64,1280]{1,0:T(8,128)(2,1)S(1)} collective-permute-done((bf16[64,1280]{1,0:T(8,128)(2,1)S(1)}, bf16[64,1280]{1,0:T(8,128)(2,1)S(1)}, u32[]{:S(2)}, u32[]{:S(2)}) %collective-permute-start.10) | collective-permute-done | bytes 163872 | tf_op jit(solution)/shard_map/ppermute | solution.py:407
  30.4 2.9 %collective-permute-done.13.refs_15_.refs_6_ = bf16[64,1280]{1,0:T(8,128)(2,1)S(1)} collective-permute-done((bf16[64,1280]{1,0:T(8,128)(2,1)S(1)}, bf16[64,1280]{1,0:T(8,128)(2,1)S(1)}, u32[]{:S(2)}, u32[]{:S(2)}) %collective-permute-start.13) | collective-permute-done | bytes 163872 | tf_op jit(solution)/shard_map/ppermute | solution.py:407
  34.8 1.8 %collective-permute-start.27 = (bf16[160,1280]{1,0:T(8,128)(2,1)S(1)}, bf16[160,1280]{1,0:T(8,128)(2,1)S(1)}, u32[]{:S(2)}, u32[]{:S(2)}) collective-permute-start(bf16[160,1280]{1,0:T(8,128)(2,1)S(1)} %get-tuple-element.29), channel_id=1, source_target_pairs={{0,2},{1,3},{2,4},{3,5},{4,6},{5,7},{6,0},{7,1},{8,14},{9,15},{10,... | collective-permute-start | bytes 1228808 | tf_op jit(solution)/shard_map/ppermute | solution.py:429
  36.5 5.8 %norm_conv.1 = (bf16[160,512]{1,0:T(8,128)(2,1)S(1)}, bf16[1152,1280]{1,0:T(8,128)(2,1)S(1)}, f32[160,1024]{1,0:T(8,128)S(1)}) custom-call(s32[128]{0:T(128)S(1)} %copy-done.6, bf16[64,1280]{1,0:T(8,128)(2,1)S(1)} %get-tuple-element.44.refs_0_, bf16[64,1280]{1,0:T(8,128)(2,1)S(1)} %get-tuple-element.43.refs_1_, bf16[64,1280]{1,0:T(8,128)(2,1)S(1)} %after.7.refs_2_, ...), custom_call_target="tpu_custom_call" | custom-call | flops 1887436800 | bytes 6307840 | tf_op jit(solution)/shard_map/norm_conv/pallas_call | solution.py:523
  42.4 2.2 %second_conv.1.refs_1_.refs_2_ = bf16[160,512]{1,0:T(8,128)(2,1)S(1)} custom-call(bf16[1152,1280]{1,0:T(8,128)(2,1)S(1)} %get-tuple-element.25.act_ref, f32[160,1024]{1,0:T(8,128)S(1)} %get-tuple-element.26.kept_ref, bf16[3,480,1280]{2,1,0:T(8,128)(2,1)S(1)} %bitcast.8, f32[1,160]{1,0:T(1,128)S(1)} %bitcast.10), custom_call_target="tpu_custom_call" | custom-call | flops 1887436800 | bytes 1887436 | tf_op jit(solution)/shard_map/second_conv/pallas_call | solution.py:540
  44.6 2.1 %collective-permute-start.19 = (bf16[160,512]{1,0:T(8,128)(2,1)S(1)}, bf16[160,512]{1,0:T(8,128)(2,1)S(1)}, u32[]{:S(2)}, u32[]{:S(2)}) collective-permute-start(bf16[160,512]{1,0:T(8,128)(2,1)S(1)} %second_conv.1.refs_1_.refs_2_), channel_id=1, source_target_pairs={{1,0},{3,1},{5,3},{7,5},{6,7},{4,6},{2,4},{0,2},{9,8},{11,9},{13,1... | collective-permute-start | bytes 491528 | tf_op jit(solution)/shard_map/ppermute | solution.py:407
  48.7 3.7 %collective-permute-start.34 = (bf16[160,1280]{1,0:T(8,128)(2,1)S(1)}, bf16[160,1280]{1,0:T(8,128)(2,1)S(1)}, u32[]{:S(2)}, u32[]{:S(2)}) collective-permute-start(bf16[160,1280]{1,0:T(8,128)(2,1)S(1)} %get-tuple-element.40.refs_0_), channel_id=1, source_target_pairs={{0,16},{8,24},{16,0},{24,8},{1,17},{9,25},{17,1},{25,9},{2,18},{10... | collective-permute-start | bytes 1228808 | tf_op jit(solution)/shard_map/ppermute | solution.py:434
  52.4 2.0 %collective-permute-start.15 = (bf16[160,512]{1,0:T(8,128)(2,1)S(1)}, bf16[160,512]{1,0:T(8,128)(2,1)}, u32[]{:S(2)}, u32[]{:S(2)}) collective-permute-start(bf16[160,512]{1,0:T(8,128)(2,1)S(1)} %collective-permute-done.14.refs_2_), channel_id=1, source_target_pairs={{0,1},{1,3},{3,5},{5,7},{7,6},{6,4},{4,2},{2,0},{8,9},{9,11},{11,1... | collective-permute-start | bytes 491528 | tf_op jit(solution)/shard_map/ppermute | solution.py:407
  54.4 2.0 %collective-permute-start.20 = (bf16[160,512]{1,0:T(8,128)(2,1)S(1)}, bf16[160,512]{1,0:T(8,128)(2,1)S(1)}, u32[]{:S(2)}, u32[]{:S(2)}) collective-permute-start(bf16[160,512]{1,0:T(8,128)(2,1)S(1)} %collective-permute-done.17.refs_3_), channel_id=1, source_target_pairs={{0,1},{1,3},{3,5},{5,7},{7,6},{6,4},{4,2},{2,0},{8,9},{9,11},{11,1... | collective-permute-start | bytes 491528 | tf_op jit(solution)/shard_map/ppermute | solution.py:407
  56.5 3.1 %collective-permute-done.15.refs_6_ = bf16[160,512]{1,0:T(8,128)(2,1)} collective-permute-done((bf16[160,512]{1,0:T(8,128)(2,1)S(1)}, bf16[160,512]{1,0:T(8,128)(2,1)}, u32[]{:S(2)}, u32[]{:S(2)}) %collective-permute-start.15) | collective-permute-done | bytes 163872 | tf_op jit(solution)/shard_map/ppermute | solution.py:407
  59.6 2.0 %collective-permute-start.16 = (bf16[160,512]{1,0:T(8,128)(2,1)}, bf16[160,512]{1,0:T(8,128)(2,1)S(1)}, u32[]{:S(2)}, u32[]{:S(2)}) collective-permute-start(bf16[160,512]{1,0:T(8,128)(2,1)} %collective-permute-done.15.refs_6_), channel_id=1, source_target_pairs={{0,1},{1,3},{3,5},{5,7},{7,6},{6,4},{4,2},{2,0},{8,9},{9,11},{11,1... | collective-permute-start | bytes 491528 | tf_op jit(solution)/shard_map/ppermute | solution.py:407
  62.7 2.3 %collective-permute-start.29 = (bf16[160,512]{1,0:T(8,128)(2,1)S(1)}, bf16[160,512]{1,0:T(8,128)(2,1)}, u32[]{:S(2)}, u32[]{:S(2)}) collective-permute-start(bf16[160,512]{1,0:T(8,128)(2,1)S(1)} %collective-permute-done.20.refs_7_), channel_id=1, source_target_pairs={{0,1},{1,3},{3,5},{5,7},{7,6},{6,4},{4,2},{2,0},{8,9},{9,11},{11,1... | collective-permute-start | bytes 491528 | tf_op jit(solution)/shard_map/ppermute | solution.py:407
  65.0 2.5 %early_norm.1 = (bf16[800,1024]{1,0:T(8,128)(2,1)S(1)}, bf16[800,128]{1,0:T(8,128)(2,1)S(1)}) custom-call(bf16[160,512]{1,0:T(8,128)(2,1)S(1)} %get-tuple-element.24.refs_0_, bf16[160,512]{1,0:T(8,128)(2,1)S(1)} %second_conv.1.refs_1_.refs_2_, bf16[160,512]{1,0:T(8,128)(2,1)S(1)} %collective-permute-done.14.refs_2_, ...), custom_call_target="tpu_custom_call" | custom-call | flops 10485760 | bytes 5242880 | tf_op jit(solution)/shard_map/early_norm/pallas_call | solution.py:555
  67.5 2.1 %collective-permute-start.23 = (bf16[160,512]{1,0:T(8,128)(2,1)S(1)}, bf16[160,512]{1,0:T(8,128)(2,1)S(1)}, u32[]{:S(2)}, u32[]{:S(2)}) collective-permute-start(bf16[160,512]{1,0:T(8,128)(2,1)S(1)} %after.9.refs_2_), channel_id=1, source_target_pairs={{0,1},{1,3},{3,5},{5,7},{7,6},{6,4},{4,2},{2,0},{8,9},{9,11},{11,1... | collective-permute-start | bytes 491528 | tf_op jit(solution)/shard_map/ppermute | solution.py:407
  69.7 2.4 %collective-permute-done.30.refs_4_ = bf16[160,512]{1,0:T(8,128)(2,1)} collective-permute-done((bf16[160,512]{1,0:T(8,128)(2,1)S(1)}, bf16[160,512]{1,0:T(8,128)(2,1)}, u32[]{:S(2)}, u32[]{:S(2)}) %collective-permute-start.30) | collective-permute-done | bytes 163872 | tf_op jit(solution)/shard_map/ppermute | solution.py:407
  72.1 2.4 %collective-permute-start.37 = (bf16[160,1280]{1,0:T(8,128)(2,1)S(1)}, bf16[160,1280]{1,0:T(8,128)(2,1)S(1)}, u32[]{:S(2)}, u32[]{:S(2)}) collective-permute-start(bf16[160,1280]{1,0:T(8,128)(2,1)S(1)} %get-tuple-element.42.refs_7_), channel_id=1, source_target_pairs={{0,1},{1,0},{2,3},{3,2},{4,5},{5,4},{6,7},{7,6},{16,17},{17,16},{1... | collective-permute-start | bytes 1228808 | tf_op jit(solution)/shard_map/ppermute | solution.py:429
  74.5 2.0 %collective-permute-start.36 = (bf16[160,1280]{1,0:T(8,128)(2,1)S(1)}, bf16[160,1280]{1,0:T(8,128)(2,1)S(1)}, u32[]{:S(2)}, u32[]{:S(2)}) collective-permute-start(bf16[160,1280]{1,0:T(8,128)(2,1)S(1)} %broadcast_select_fusion), channel_id=1, source_target_pairs={{0,1},{1,0},{2,3},{3,2},{4,5},{5,4},{6,7},{7,6},{8,9},{9,8},{10,11... | collective-permute-start | bytes 1228808 | tf_op jit(solution)/shard_map/ppermute | solution.py:429
  76.6 4.7 %norm_project.1 = (f32[960,1024]{1,0:T(8,128)S(1)}, bf16[1280,128]{1,0:T(8,128)(2,1)S(1)}) custom-call(s32[128]{0:T(128)S(1)} %copy-done.6, bf16[800,1024]{1,0:T(8,128)(2,1)S(1)} %get-tuple-element.27.refs_1_.refs_0_, bf16[800,128]{1,0:T(8,128)(2,1)S(1)} %get-tuple-element.31.refs_1_, bf16[160,512]{1,0:T(8,128)(2,1)S(1)} %after.9.refs_2_, ...), custom_call_target="tpu_custom_call" | custom-call | flops 2516582400 | bytes 5079040 | tf_op jit(solution)/shard_map/norm_project/pallas_call | solution.py:583
  81.3 6.1 %attention.1 = (bf16[320,128]{1,0:T(8,128)(2,1)S(1)}, bf16[320,128]{1,0:T(8,128)(2,1)S(1)}, bf16[320,128]{1,0:T(8,128)(2,1)S(1)}, bf16[1280,128]{1,0:T(8,128)(2,...) custom-call(s32[128]{0:T(128)S(1)} %copy-done.6, ...), custom_call_target="tpu_custom_call" | custom-call | flops 1258291200 | bytes 5898240 | tf_op jit(solution)/shard_map/attention/pallas_call | solution.py:607
  88.3 5.8 %collective-permute-done.31.refs_1_ = bf16[320,128]{1,0:T(8,128)(2,1)S(1)} collective-permute-done((bf16[320,128]{1,0:T(8,128)(2,1)S(1)}, bf16[320,128]{1,0:T(8,128)(2,1)S(1)}, u32[]{:S(2)}, u32[]{:S(2)}) %collective-permute-start.31) | collective-permute-done | bytes 81952 | tf_op jit(solution)/shard_map/ppermute | solution.py:630
  95.0 1.9 %own_attention.1.refs_0_ = bf16[320,128]{1,0:T(8,128)(2,1)S(1)} custom-call(bf16[960,1024]{1,0:T(8,128)(2,1)S(1)} %get-tuple-element.34.made_ref, bf16[5,1024,64]{2,1,0:T(8,128)(2,1)S(1)} %get-tuple-element.35.key_ref), custom_call_target="tpu_custom_call" | custom-call | flops 167772160 | bytes 2621440 | tf_op jit(solution)/shard_map/own_attention/pallas_call | solution.py:631
  96.9 3.4 %collective-permute-done.32.refs_2_ = bf16[320,128]{1,0:T(8,128)(2,1)S(1)} collective-permute-done((bf16[320,128]{1,0:T(8,128)(2,1)S(1)}, bf16[320,128]{1,0:T(8,128)(2,1)S(1)}, u32[]{:S(2)}, u32[]{:S(2)}) %collective-permute-start.32) | collective-permute-done | bytes 81952 | tf_op jit(solution)/shard_map/ppermute | solution.py:630
  100.8 2.1 %project.1 = bf16[128,1280]{1,0:T(8,128)(2,1)} custom-call(bf16[320,128]{1,0:T(8,128)(2,1)S(1)} %own_attention.1.refs_0_, bf16[320,128]{1,0:T(8,128)(2,1)S(1)} %collective-permute-done.31.refs_1_, bf16[320,128]{1,0:T(8,128)(2,1)S(1)} %collective-permute-done.32.refs_2_, bf16[320,128]{1,0:T(8,128)(2,1)S(1)} %collective-permute-done.33.refs_3_, ...), custom_call_target="tpu_custom_call" | custom-call | flops 419430400 | bytes 4259840 | tf_op jit(solution)/shard_map/project/pallas_call | solution.py:648
  (81 shorter events, 16.6 us)
Async XLA Ops:
  1.0 8.1 %collective-permute-start = (bf16[64,1280]{1,0:T(8,128)(2,1)S(1)}, bf16[64,1280]{1,0:T(8,128)(2,1)S(1)}, u32[]{:S(2)}, u32[]{:S(2)}) collective-permute-start(bf16[64,1280]{1,0:T(8,128)(2,1)S(1)} %get-tuple-element.44.refs_0_), channel_id=1, source_target_pairs={{0,1},{1,3},{3,5},{5,7},{7,6},{6,4},{4,2},{2,0},{8,9},{9,11},{11,1... | collective-permute-start | bytes 491528 | tf_op jit(solution)/shard_map/ppermute | solution.py:407
  4.0 11.2 %collective-permute-start.2 = (bf16[64,1280]{1,0:T(8,128)(2,1)S(1)}, bf16[64,1280]{1,0:T(8,128)(2,1)S(1)}, u32[]{:S(2)}, u32[]{:S(2)}) collective-permute-start(bf16[64,1280]{1,0:T(8,128)(2,1)S(1)} %get-tuple-element.44.refs_0_), channel_id=1, source_target_pairs={{1,0},{3,1},{5,3},{7,5},{6,7},{4,6},{2,4},{0,2},{9,8},{11,9},{13,1... | collective-permute-start | bytes 491528 | tf_op jit(solution)/shard_map/ppermute | solution.py:407
  4.2 9.5 %collective-permute-start.1 = (bf16[64,1280]{1,0:T(8,128)(2,1)S(1)}, bf16[64,1280]{1,0:T(8,128)(2,1)S(1)}, u32[]{:S(2)}, u32[]{:S(2)}) collective-permute-start(bf16[64,1280]{1,0:T(8,128)(2,1)S(1)} %get-tuple-element.43.refs_1_), channel_id=1, source_target_pairs={{0,1},{1,3},{3,5},{5,7},{7,6},{6,4},{4,2},{2,0},{8,9},{9,11},{11,1... | collective-permute-start | bytes 491528 | tf_op jit(solution)/shard_map/ppermute | solution.py:407
  6.1 7.1 %collective-permute-start.3 = (bf16[64,1280]{1,0:T(8,128)(2,1)S(1)}, bf16[64,1280]{1,0:T(8,128)(2,1)S(1)}, u32[]{:S(2)}, u32[]{:S(2)}) collective-permute-start(bf16[64,1280]{1,0:T(8,128)(2,1)S(1)} %get-tuple-element.43.refs_1_), channel_id=1, source_target_pairs={{1,0},{3,1},{5,3},{7,5},{6,7},{4,6},{2,4},{0,2},{9,8},{11,9},{13,1... | collective-permute-start | bytes 491528 | tf_op jit(solution)/shard_map/ppermute | solution.py:407
  13.2 7.1 %collective-permute-start.7 = (bf16[64,1280]{1,0:T(8,128)(2,1)S(1)}, bf16[64,1280]{1,0:T(8,128)(2,1)S(1)}, u32[]{:S(2)}, u32[]{:S(2)}) collective-permute-start(bf16[64,1280]{1,0:T(8,128)(2,1)S(1)} %collective-permute-done.3.refs_5_), channel_id=1, source_target_pairs={{1,0},{3,1},{5,3},{7,5},{6,7},{4,6},{2,4},{0,2},{9,8},{11,9},{13,1... | collective-permute-start | bytes 491528 | tf_op jit(solution)/shard_map/ppermute | solution.py:407
  13.6 7.1 %collective-permute-start.5 = (bf16[64,1280]{1,0:T(8,128)(2,1)S(1)}, bf16[64,1280]{1,0:T(8,128)(2,1)S(1)}, u32[]{:S(2)}, u32[]{:S(2)}) collective-permute-start(bf16[64,1280]{1,0:T(8,128)(2,1)S(1)} %collective-permute-done.1.refs_3_), channel_id=1, source_target_pairs={{0,1},{1,3},{3,5},{5,7},{7,6},{6,4},{4,2},{2,0},{8,9},{9,11},{11,1... | collective-permute-start | bytes 491528 | tf_op jit(solution)/shard_map/ppermute | solution.py:407
  15.2 8.6 %collective-permute-start.6 = (bf16[64,1280]{1,0:T(8,128)(2,1)S(1)}, bf16[64,1280]{1,0:T(8,128)(2,1)S(1)}, u32[]{:S(2)}, u32[]{:S(2)}) collective-permute-start(bf16[64,1280]{1,0:T(8,128)(2,1)S(1)} %collective-permute-done.2.refs_4_), channel_id=1, source_target_pairs={{1,0},{3,1},{5,3},{7,5},{6,7},{4,6},{2,4},{0,2},{9,8},{11,9},{13,1... | collective-permute-start | bytes 491528 | tf_op jit(solution)/shard_map/ppermute | solution.py:407
  15.7 9.4 %collective-permute-start.8 = (bf16[64,1280]{1,0:T(8,128)(2,1)S(1)}, bf16[64,1280]{1,0:T(8,128)(2,1)S(1)}, u32[]{:S(2)}, u32[]{:S(2)}) collective-permute-start(bf16[64,1280]{1,0:T(8,128)(2,1)S(1)} %collective-permute-done.4.refs_6_), channel_id=1, source_target_pairs={{0,1},{1,3},{3,5},{5,7},{7,6},{6,4},{4,2},{2,0},{8,9},{9,11},{11,1... | collective-permute-start | bytes 491528 | tf_op jit(solution)/shard_map/ppermute | solution.py:407
  20.3 7.1 %collective-permute-start.11 = (bf16[64,1280]{1,0:T(8,128)(2,1)S(1)}, bf16[64,1280]{1,0:T(8,128)(2,1)S(1)}, u32[]{:S(2)}, u32[]{:S(2)}) collective-permute-start(bf16[64,1280]{1,0:T(8,128)(2,1)S(1)} %collective-permute-done.7.refs_9_), channel_id=1, source_target_pairs={{1,0},{3,1},{5,3},{7,5},{6,7},{4,6},{2,4},{0,2},{9,8},{11,9},{13,1... | collective-permute-start | bytes 491528 | tf_op jit(solution)/shard_map/ppermute | solution.py:407
  20.8 7.2 %collective-permute-start.9 = (bf16[64,1280]{1,0:T(8,128)(2,1)S(1)}, bf16[64,1280]{1,0:T(8,128)(2,1)S(1)}, u32[]{:S(2)}, u32[]{:S(2)}) collective-permute-start(bf16[64,1280]{1,0:T(8,128)(2,1)S(1)} %collective-permute-done.5.refs_7_), channel_id=1, source_target_pairs={{0,1},{1,3},{3,5},{5,7},{7,6},{6,4},{4,2},{2,0},{8,9},{9,11},{11,1... | collective-permute-start | bytes 491528 | tf_op jit(solution)/shard_map/ppermute | solution.py:407
  33.4 15.3 %collective-permute-start.26 = (bf16[240,1280]{1,0:T(8,128)(2,1)S(1)}, bf16[240,1280]{1,0:T(8,128)(2,1)S(1)}, u32[]{:S(2)}, u32[]{:S(2)}) collective-permute-start(bf16[240,1280]{1,0:T(8,128)(2,1)S(1)} %get-tuple-element.28), channel_id=1, source_target_pairs={{0,1},{1,0},{2,3},{3,2},{4,5},{5,4},{6,7},{7,6},{8,9},{9,8},{10,11... | collective-permute-start | bytes 1843208 | tf_op jit(solution)/shard_map/ppermute | solution.py:429
  34.8 12.4 %collective-permute-start.27 = (bf16[160,1280]{1,0:T(8,128)(2,1)S(1)}, bf16[160,1280]{1,0:T(8,128)(2,1)S(1)}, u32[]{:S(2)}, u32[]{:S(2)}) collective-permute-start(bf16[160,1280]{1,0:T(8,128)(2,1)S(1)} %get-tuple-element.29), channel_id=1, source_target_pairs={{0,2},{1,3},{2,4},{3,5},{4,6},{5,7},{6,0},{7,1},{8,14},{9,15},{10,... | collective-permute-start | bytes 1228808 | tf_op jit(solution)/shard_map/ppermute | solution.py:429
  42.3 10.1 %collective-permute-start.14 = (bf16[160,512]{1,0:T(8,128)(2,1)S(1)}, bf16[160,512]{1,0:T(8,128)(2,1)S(1)}, u32[]{:S(2)}, u32[]{:S(2)}) collective-permute-start(bf16[160,512]{1,0:T(8,128)(2,1)S(1)} %get-tuple-element.24.refs_0_), channel_id=1, source_target_pairs={{0,1},{1,3},{3,5},{5,7},{7,6},{6,4},{4,2},{2,0},{8,9},{9,11},{11,1... | collective-permute-start | bytes 491528 | tf_op jit(solution)/shard_map/ppermute | solution.py:407
  44.6 9.8 %collective-permute-start.19 = (bf16[160,512]{1,0:T(8,128)(2,1)S(1)}, bf16[160,512]{1,0:T(8,128)(2,1)S(1)}, u32[]{:S(2)}, u32[]{:S(2)}) collective-permute-start(bf16[160,512]{1,0:T(8,128)(2,1)S(1)} %second_conv.1.refs_1_.refs_2_), channel_id=1, source_target_pairs={{1,0},{3,1},{5,3},{7,5},{6,7},{4,6},{2,4},{0,2},{9,8},{11,9},{13,1... | collective-permute-start | bytes 491528 | tf_op jit(solution)/shard_map/ppermute | solution.py:407
  46.7 7.7 %collective-permute-start.17 = (bf16[160,512]{1,0:T(8,128)(2,1)S(1)}, bf16[160,512]{1,0:T(8,128)(2,1)S(1)}, u32[]{:S(2)}, u32[]{:S(2)}) collective-permute-start(bf16[160,512]{1,0:T(8,128)(2,1)S(1)} %second_conv.1.refs_1_.refs_2_), channel_id=1, source_target_pairs={{0,1},{1,3},{3,5},{5,7},{7,6},{6,4},{4,2},{2,0},{8,9},{9,11},{11,1... | collective-permute-start | bytes 491528 | tf_op jit(solution)/shard_map/ppermute | solution.py:407
  47.2 9.2 %collective-permute-start.18 = (bf16[160,512]{1,0:T(8,128)(2,1)S(1)}, bf16[160,512]{1,0:T(8,128)(2,1)S(1)}, u32[]{:S(2)}, u32[]{:S(2)}) collective-permute-start(bf16[160,512]{1,0:T(8,128)(2,1)S(1)} %get-tuple-element.24.refs_0_), channel_id=1, source_target_pairs={{1,0},{3,1},{5,3},{7,5},{6,7},{4,6},{2,4},{0,2},{9,8},{11,9},{13,1... | collective-permute-start | bytes 491528 | tf_op jit(solution)/shard_map/ppermute | solution.py:407
  48.7 23.3 %collective-permute-start.34 = (bf16[160,1280]{1,0:T(8,128)(2,1)S(1)}, bf16[160,1280]{1,0:T(8,128)(2,1)S(1)}, u32[]{:S(2)}, u32[]{:S(2)}) collective-permute-start(bf16[160,1280]{1,0:T(8,128)(2,1)S(1)} %get-tuple-element.40.refs_0_), channel_id=1, source_target_pairs={{0,16},{8,24},{16,0},{24,8},{1,17},{9,25},{17,1},{25,9},{2,18},{10... | collective-permute-start | bytes 1228808 | tf_op jit(solution)/shard_map/ppermute | solution.py:434
  52.4 7.2 %collective-permute-start.15 = (bf16[160,512]{1,0:T(8,128)(2,1)S(1)}, bf16[160,512]{1,0:T(8,128)(2,1)}, u32[]{:S(2)}, u32[]{:S(2)}) collective-permute-start(bf16[160,512]{1,0:T(8,128)(2,1)S(1)} %collective-permute-done.14.refs_2_), channel_id=1, source_target_pairs={{0,1},{1,3},{3,5},{5,7},{7,6},{6,4},{4,2},{2,0},{8,9},{9,11},{11,1... | collective-permute-start | bytes 491528 | tf_op jit(solution)/shard_map/ppermute | solution.py:407
  54.4 7.2 %collective-permute-start.22 = (bf16[160,512]{1,0:T(8,128)(2,1)S(1)}, bf16[160,512]{1,0:T(8,128)(2,1)S(1)}, u32[]{:S(2)}, u32[]{:S(2)}) collective-permute-start(bf16[160,512]{1,0:T(8,128)(2,1)S(1)} %collective-permute-done.19.refs_5_), channel_id=1, source_target_pairs={{1,0},{3,1},{5,3},{7,5},{6,7},{4,6},{2,4},{0,2},{9,8},{11,9},{13,1... | collective-permute-start | bytes 491528 | tf_op jit(solution)/shard_map/ppermute | solution.py:407
  54.4 8.3 %collective-permute-start.20 = (bf16[160,512]{1,0:T(8,128)(2,1)S(1)}, bf16[160,512]{1,0:T(8,128)(2,1)S(1)}, u32[]{:S(2)}, u32[]{:S(2)}) collective-permute-start(bf16[160,512]{1,0:T(8,128)(2,1)S(1)} %collective-permute-done.17.refs_3_), channel_id=1, source_target_pairs={{0,1},{1,3},{3,5},{5,7},{7,6},{6,4},{4,2},{2,0},{8,9},{9,11},{11,1... | collective-permute-start | bytes 491528 | tf_op jit(solution)/shard_map/ppermute | solution.py:407
  56.4 8.6 %collective-permute-start.21 = (bf16[160,512]{1,0:T(8,128)(2,1)S(1)}, bf16[160,512]{1,0:T(8,128)(2,1)S(1)}, u32[]{:S(2)}, u32[]{:S(2)}) collective-permute-start(bf16[160,512]{1,0:T(8,128)(2,1)S(1)} %collective-permute-done.18.refs_4_), channel_id=1, source_target_pairs={{1,0},{3,1},{5,3},{7,5},{6,7},{4,6},{2,4},{0,2},{9,8},{11,9},{13,1... | collective-permute-start | bytes 491528 | tf_op jit(solution)/shard_map/ppermute | solution.py:407
  59.6 7.9 %collective-permute-start.16 = (bf16[160,512]{1,0:T(8,128)(2,1)}, bf16[160,512]{1,0:T(8,128)(2,1)S(1)}, u32[]{:S(2)}, u32[]{:S(2)}) collective-permute-start(bf16[160,512]{1,0:T(8,128)(2,1)} %collective-permute-done.15.refs_6_), channel_id=1, source_target_pairs={{0,1},{1,3},{3,5},{5,7},{7,6},{6,4},{4,2},{2,0},{8,9},{9,11},{11,1... | collective-permute-start | bytes 491528 | tf_op jit(solution)/shard_map/ppermute | solution.py:407
  61.6 8.0 %collective-permute-start.24 = (bf16[160,512]{1,0:T(8,128)(2,1)S(1)}, bf16[160,512]{1,0:T(8,128)(2,1)}, u32[]{:S(2)}, u32[]{:S(2)}) collective-permute-start(bf16[160,512]{1,0:T(8,128)(2,1)S(1)} %collective-permute-done.22.refs_9_), channel_id=1, source_target_pairs={{1,0},{3,1},{5,3},{7,5},{6,7},{4,6},{2,4},{0,2},{9,8},{11,9},{13,1... | collective-permute-start | bytes 491528 | tf_op jit(solution)/shard_map/ppermute | solution.py:407
  62.7 6.9 %collective-permute-start.29 = (bf16[160,512]{1,0:T(8,128)(2,1)S(1)}, bf16[160,512]{1,0:T(8,128)(2,1)}, u32[]{:S(2)}, u32[]{:S(2)}) collective-permute-start(bf16[160,512]{1,0:T(8,128)(2,1)S(1)} %collective-permute-done.20.refs_7_), channel_id=1, source_target_pairs={{0,1},{1,3},{3,5},{5,7},{7,6},{6,4},{4,2},{2,0},{8,9},{9,11},{11,1... | collective-permute-start | bytes 491528 | tf_op jit(solution)/shard_map/ppermute | solution.py:407
  65.0 7.0 %collective-permute-start.30 = (bf16[160,512]{1,0:T(8,128)(2,1)S(1)}, bf16[160,512]{1,0:T(8,128)(2,1)}, u32[]{:S(2)}, u32[]{:S(2)}) collective-permute-start(bf16[160,512]{1,0:T(8,128)(2,1)S(1)} %collective-permute-done.21.refs_8_), channel_id=1, source_target_pairs={{1,0},{3,1},{5,3},{7,5},{6,7},{4,6},{2,4},{0,2},{9,8},{11,9},{13,1... | collective-permute-start | bytes 491528 | tf_op jit(solution)/shard_map/ppermute | solution.py:407
  67.5 13.8 %collective-permute-start.23 = (bf16[160,512]{1,0:T(8,128)(2,1)S(1)}, bf16[160,512]{1,0:T(8,128)(2,1)S(1)}, u32[]{:S(2)}, u32[]{:S(2)}) collective-permute-start(bf16[160,512]{1,0:T(8,128)(2,1)S(1)} %after.9.refs_2_), channel_id=1, source_target_pairs={{0,1},{1,3},{3,5},{5,7},{7,6},{6,4},{4,2},{2,0},{8,9},{9,11},{11,1... | collective-permute-start | bytes 491528 | tf_op jit(solution)/shard_map/ppermute | solution.py:407
  69.6 11.7 %collective-permute-start.25 = (bf16[160,512]{1,0:T(8,128)(2,1)}, bf16[160,512]{1,0:T(8,128)(2,1)S(1)}, u32[]{:S(2)}, u32[]{:S(2)}) collective-permute-start(bf16[160,512]{1,0:T(8,128)(2,1)} %collective-permute-done.24.refs_5_), channel_id=1, source_target_pairs={{1,0},{3,1},{5,3},{7,5},{6,7},{4,6},{2,4},{0,2},{9,8},{11,9},{13,1... | collective-permute-start | bytes 491528 | tf_op jit(solution)/shard_map/ppermute | solution.py:407
  69.6 6.9 %collective-permute-start.28 = (bf16[240,1280]{1,0:T(8,128)(2,1)S(1)}, bf16[240,1280]{1,0:T(8,128)(2,1)S(1)}, u32[]{:S(2)}, u32[]{:S(2)}) collective-permute-start(bf16[240,1280]{1,0:T(8,128)(2,1)S(1)} %get-tuple-element.30.refs_9_.refs_5_), channel_id=1, source_target_pairs={{0,8},{8,0},{16,24},{24,16},{1,9},{9,1},{17,25},{25,17},{2,10},{10... | collective-permute-start | bytes 1843208 | tf_op jit(solution)/shard_map/ppermute | solution.py:434
  72.1 15.5 %collective-permute-start.37 = (bf16[160,1280]{1,0:T(8,128)(2,1)S(1)}, bf16[160,1280]{1,0:T(8,128)(2,1)S(1)}, u32[]{:S(2)}, u32[]{:S(2)}) collective-permute-start(bf16[160,1280]{1,0:T(8,128)(2,1)S(1)} %get-tuple-element.42.refs_7_), channel_id=1, source_target_pairs={{0,1},{1,0},{2,3},{3,2},{4,5},{5,4},{6,7},{7,6},{16,17},{17,16},{1... | collective-permute-start | bytes 1228808 | tf_op jit(solution)/shard_map/ppermute | solution.py:429
  74.5 13.8 %collective-permute-start.36 = (bf16[160,1280]{1,0:T(8,128)(2,1)S(1)}, bf16[160,1280]{1,0:T(8,128)(2,1)S(1)}, u32[]{:S(2)}, u32[]{:S(2)}) collective-permute-start(bf16[160,1280]{1,0:T(8,128)(2,1)S(1)} %broadcast_select_fusion), channel_id=1, source_target_pairs={{0,1},{1,0},{2,3},{3,2},{4,5},{5,4},{6,7},{7,6},{8,9},{9,8},{10,11... | collective-permute-start | bytes 1228808 | tf_op jit(solution)/shard_map/ppermute | solution.py:429
  76.5 24.2 %collective-permute-start.35 = (bf16[320,1280]{1,0:T(8,128)(2,1)S(1)}, bf16[320,1280]{1,0:T(8,128)(2,1)S(1)}, u32[]{:S(2)}, u32[]{:S(2)}) collective-permute-start(bf16[320,1280]{1,0:T(8,128)(2,1)S(1)} %pad_maximum_fusion), channel_id=1, source_target_pairs={{0,8},{8,0},{16,24},{24,16},{1,9},{9,1},{17,25},{25,17},{2,10},{10... | collective-permute-start | bytes 2457608 | tf_op jit(solution)/shard_map/ppermute | solution.py:434
  87.5 6.7 %collective-permute-start.31 = (bf16[320,128]{1,0:T(8,128)(2,1)S(1)}, bf16[320,128]{1,0:T(8,128)(2,1)S(1)}, u32[]{:S(2)}, u32[]{:S(2)}) collective-permute-start(bf16[320,128]{1,0:T(8,128)(2,1)S(1)} %get-tuple-element.36), channel_id=1, source_target_pairs={{0,2},{1,3},{2,4},{3,5},{4,6},{5,7},{6,0},{7,1},{8,10},{9,11},{10,... | collective-permute-start | bytes 245768 | tf_op jit(solution)/shard_map/ppermute | solution.py:630
  (14 other events, 112.7 us)

commit v18 on v16

--- a/solution.py
+++ b/solution.py
@@ -19,7 +19,7 @@
 HANDED = (0, 2, 1, 3)
 FAR = ((1, 0), (3, 0), (2, 0), (0, 1))
 SOONER = tuple(range(1, OUTER))
-WIDE = 256
+WIDE = 512
 EPSILON = 1e-05
 LATE = 6
 CHUNK = 16

time: 101 us -> 101 us (level)
  no operation moved by 1% of the time
where the time goes in v18:
time: 101 us
  starting transfers between devices  46.4 us (46%)
  Pallas kernels  25.9 us (26%)
  waiting for transfers between devices  25.4 us (25%)
  other arithmetic  1.72 us (2%)
  local copies, waits for them, and re-layouts  1.08 us (1%)
    ppermute x28, starting transfers between devices, gather(): lax.ppermute(found[half, sign * (step - 1)], 'patch', pairs)  30.3 us
    ppermute x28, waiting for transfers between devices, gather(): lax.ppermute(found[half, sign * (step - 1)], 'patch', pairs)  20.4 us
    ppermute x4, starting transfers between devices, send(): return lax.ppermute(block, ('batch', 'patch'), pairs)  7.46 us
    pallas_call x1, Pallas kernels, on_device(): pl.pallas_call(functools.partial(attention_kernel, 2 * n, inner), out_sha...  5.96 us
    pallas_call x1, Pallas kernels, on_device(): pl.pallas_call(functools.partial(conv_kernel, columns), out_shape=[half_h...  5.79 us
    ppermute x3, starting transfers between devices, on_device(): received.append(lax.ppermute(sent_block, 'patch', pairs))  4.75 us
    pallas_call x1, Pallas kernels, on_device(): pl.pallas_call(functools.partial(project_kernel, 2 * n), out_shape=[jax.S...  4.68 us
    ppermute x4, starting transfers between devices, swap(): return lax.ppermute(block, 'batch', pairs)  3.82 us
  transfers between devices with their start and end apart: 39, of which 16 were waited for; matrix products, arithmetic and copies ran while one was open for 2% of the time, Pallas kernels for 24%

profile of v18, /device:TPU:0, one launch (start us, length us, event | category | flops | bytes accessed | tf_op | source)
XLA Modules:
  0.0 100.7 jit_solution(18203934282179364946)
XLA Ops:
  1.0 3.0 %collective-permute-start = (bf16[64,1280]{1,0:T(8,128)(2,1)S(1)}, bf16[64,1280]{1,0:T(8,128)(2,1)S(1)}, u32[]{:S(2)}, u32[]{:S(2)}) collective-permute-start(bf16[64,1280]{1,0:T(8,128)(2,1)S(1)} %get-tuple-element.44.refs_0_), channel_id=1, source_target_pairs={{0,1},{1,3},{3,5},{5,7},{7,6},{6,4},{4,2},{2,0},{8,9},{9,11},{11,1... | collective-permute-start | bytes 491528 | tf_op jit(solution)/shard_map/ppermute | solution.py:407
  4.2 1.9 %collective-permute-start.1 = (bf16[64,1280]{1,0:T(8,128)(2,1)S(1)}, bf16[64,1280]{1,0:T(8,128)(2,1)S(1)}, u32[]{:S(2)}, u32[]{:S(2)}) collective-permute-start(bf16[64,1280]{1,0:T(8,128)(2,1)S(1)} %get-tuple-element.43.refs_1_), channel_id=1, source_target_pairs={{0,1},{1,3},{3,5},{5,7},{7,6},{6,4},{4,2},{2,0},{8,9},{9,11},{11,1... | collective-permute-start | bytes 491528 | tf_op jit(solution)/shard_map/ppermute | solution.py:407
  9.1 2.0 %collective-permute-start.4 = (bf16[64,1280]{1,0:T(8,128)(2,1)S(1)}, bf16[64,1280]{1,0:T(8,128)(2,1)S(1)}, u32[]{:S(2)}, u32[]{:S(2)}) collective-permute-start(bf16[64,1280]{1,0:T(8,128)(2,1)S(1)} %after.7.refs_2_), channel_id=1, source_target_pairs={{0,1},{1,3},{3,5},{5,7},{7,6},{6,4},{4,2},{2,0},{8,9},{9,11},{11,1... | collective-permute-start | bytes 491528 | tf_op jit(solution)/shard_map/ppermute | solution.py:407
  11.1 2.1 %collective-permute-done.3.refs_5_ = bf16[64,1280]{1,0:T(8,128)(2,1)S(1)} collective-permute-done((bf16[64,1280]{1,0:T(8,128)(2,1)S(1)}, bf16[64,1280]{1,0:T(8,128)(2,1)S(1)}, u32[]{:S(2)}, u32[]{:S(2)}) %collective-permute-start.3) | collective-permute-done | bytes 163872 | tf_op jit(solution)/shard_map/ppermute | solution.py:407
  13.6 1.6 %collective-permute-start.5 = (bf16[64,1280]{1,0:T(8,128)(2,1)S(1)}, bf16[64,1280]{1,0:T(8,128)(2,1)S(1)}, u32[]{:S(2)}, u32[]{:S(2)}) collective-permute-start(bf16[64,1280]{1,0:T(8,128)(2,1)S(1)} %collective-permute-done.1.refs_3_), channel_id=1, source_target_pairs={{0,1},{1,3},{3,5},{5,7},{7,6},{6,4},{4,2},{2,0},{8,9},{9,11},{11,1... | collective-permute-start | bytes 491528 | tf_op jit(solution)/shard_map/ppermute | solution.py:407
  15.7 2.1 %collective-permute-start.8 = (bf16[64,1280]{1,0:T(8,128)(2,1)S(1)}, bf16[64,1280]{1,0:T(8,128)(2,1)S(1)}, u32[]{:S(2)}, u32[]{:S(2)}) collective-permute-start(bf16[64,1280]{1,0:T(8,128)(2,1)S(1)} %collective-permute-done.4.refs_6_), channel_id=1, source_target_pairs={{0,1},{1,3},{3,5},{5,7},{7,6},{6,4},{4,2},{2,0},{8,9},{9,11},{11,1... | collective-permute-start | bytes 491528 | tf_op jit(solution)/shard_map/ppermute | solution.py:407
  17.7 2.6 %collective-permute-done.7.refs_9_ = bf16[64,1280]{1,0:T(8,128)(2,1)S(1)} collective-permute-done((bf16[64,1280]{1,0:T(8,128)(2,1)S(1)}, bf16[64,1280]{1,0:T(8,128)(2,1)S(1)}, u32[]{:S(2)}, u32[]{:S(2)}) %collective-permute-start.7) | collective-permute-done | bytes 163872 | tf_op jit(solution)/shard_map/ppermute | solution.py:407
  20.8 1.6 %collective-permute-start.9 = (bf16[64,1280]{1,0:T(8,128)(2,1)S(1)}, bf16[64,1280]{1,0:T(8,128)(2,1)S(1)}, u32[]{:S(2)}, u32[]{:S(2)}) collective-permute-start(bf16[64,1280]{1,0:T(8,128)(2,1)S(1)} %collective-permute-done.5.refs_7_), channel_id=1, source_target_pairs={{0,1},{1,3},{3,5},{5,7},{7,6},{6,4},{4,2},{2,0},{8,9},{9,11},{11,1... | collective-permute-start | bytes 491528 | tf_op jit(solution)/shard_map/ppermute | solution.py:407
  25.1 1.7 %collective-permute-start.12 = (bf16[64,1280]{1,0:T(8,128)(2,1)S(1)}, bf16[64,1280]{1,0:T(8,128)(2,1)S(1)}, u32[]{:S(2)}, u32[]{:S(2)}) collective-permute-start(bf16[64,1280]{1,0:T(8,128)(2,1)S(1)} %after.8.refs_10_), channel_id=1, source_target_pairs={{0,1},{1,3},{3,5},{5,7},{7,6},{6,4},{4,2},{2,0},{8,9},{9,11},{11,1... | collective-permute-start | bytes 491528 | tf_op jit(solution)/shard_map/ppermute | solution.py:407
  27.9 2.3 %collective-permute-done.10.refs_12_.refs_3_ = bf16[64,1280]{1,0:T(8,128)(2,1)S(1)} collective-permute-done((bf16[64,1280]{1,0:T(8,128)(2,1)S(1)}, bf16[64,1280]{1,0:T(8,128)(2,1)S(1)}, u32[]{:S(2)}, u32[]{:S(2)}) %collective-permute-start.10) | collective-permute-done | bytes 163872 | tf_op jit(solution)/shard_map/ppermute | solution.py:407
  30.4 2.9 %collective-permute-done.13.refs_15_.refs_6_ = bf16[64,1280]{1,0:T(8,128)(2,1)S(1)} collective-permute-done((bf16[64,1280]{1,0:T(8,128)(2,1)S(1)}, bf16[64,1280]{1,0:T(8,128)(2,1)S(1)}, u32[]{:S(2)}, u32[]{:S(2)}) %collective-permute-start.13) | collective-permute-done | bytes 163872 | tf_op jit(solution)/shard_map/ppermute | solution.py:407
  34.8 1.8 %collective-permute-start.27 = (bf16[160,1280]{1,0:T(8,128)(2,1)S(1)}, bf16[160,1280]{1,0:T(8,128)(2,1)S(1)}, u32[]{:S(2)}, u32[]{:S(2)}) collective-permute-start(bf16[160,1280]{1,0:T(8,128)(2,1)S(1)} %get-tuple-element.29), channel_id=1, source_target_pairs={{0,2},{1,3},{2,4},{3,5},{4,6},{5,7},{6,0},{7,1},{8,14},{9,15},{10,... | collective-permute-start | bytes 1228808 | tf_op jit(solution)/shard_map/ppermute | solution.py:429
  36.5 5.8 %norm_conv.1 = (bf16[160,512]{1,0:T(8,128)(2,1)S(1)}, bf16[1152,1280]{1,0:T(8,128)(2,1)S(1)}, f32[160,1024]{1,0:T(8,128)S(1)}) custom-call(s32[128]{0:T(128)S(1)} %copy-done.6, bf16[64,1280]{1,0:T(8,128)(2,1)S(1)} %get-tuple-element.44.refs_0_, bf16[64,1280]{1,0:T(8,128)(2,1)S(1)} %get-tuple-element.43.refs_1_, bf16[64,1280]{1,0:T(8,128)(2,1)S(1)} %after.7.refs_2_, ...), custom_call_target="tpu_custom_call" | custom-call | flops 1887436800 | bytes 6307840 | tf_op jit(solution)/shard_map/norm_conv/pallas_call | solution.py:523
  42.4 2.2 %second_conv.1.refs_1_.refs_2_ = bf16[160,512]{1,0:T(8,128)(2,1)S(1)} custom-call(bf16[1152,1280]{1,0:T(8,128)(2,1)S(1)} %get-tuple-element.25.act_ref, f32[160,1024]{1,0:T(8,128)S(1)} %get-tuple-element.26.kept_ref, bf16[3,480,1280]{2,1,0:T(8,128)(2,1)S(1)} %bitcast.8, f32[1,160]{1,0:T(1,128)S(1)} %bitcast.10), custom_call_target="tpu_custom_call" | custom-call | flops 1887436800 | bytes 1887436 | tf_op jit(solution)/shard_map/second_conv/pallas_call | solution.py:540
  44.6 2.1 %collective-permute-start.19 = (bf16[160,512]{1,0:T(8,128)(2,1)S(1)}, bf16[160,512]{1,0:T(8,128)(2,1)S(1)}, u32[]{:S(2)}, u32[]{:S(2)}) collective-permute-start(bf16[160,512]{1,0:T(8,128)(2,1)S(1)} %second_conv.1.refs_1_.refs_2_), channel_id=1, source_target_pairs={{1,0},{3,1},{5,3},{7,5},{6,7},{4,6},{2,4},{0,2},{9,8},{11,9},{13,1... | collective-permute-start | bytes 491528 | tf_op jit(solution)/shard_map/ppermute | solution.py:407
  48.7 3.7 %collective-permute-start.34 = (bf16[160,1280]{1,0:T(8,128)(2,1)S(1)}, bf16[160,1280]{1,0:T(8,128)(2,1)S(1)}, u32[]{:S(2)}, u32[]{:S(2)}) collective-permute-start(bf16[160,1280]{1,0:T(8,128)(2,1)S(1)} %get-tuple-element.40.refs_0_), channel_id=1, source_target_pairs={{0,16},{8,24},{16,0},{24,8},{1,17},{9,25},{17,1},{25,9},{2,18},{10... | collective-permute-start | bytes 1228808 | tf_op jit(solution)/shard_map/ppermute | solution.py:434
  52.4 2.0 %collective-permute-start.15 = (bf16[160,512]{1,0:T(8,128)(2,1)S(1)}, bf16[160,512]{1,0:T(8,128)(2,1)}, u32[]{:S(2)}, u32[]{:S(2)}) collective-permute-start(bf16[160,512]{1,0:T(8,128)(2,1)S(1)} %collective-permute-done.14.refs_2_), channel_id=1, source_target_pairs={{0,1},{1,3},{3,5},{5,7},{7,6},{6,4},{4,2},{2,0},{8,9},{9,11},{11,1... | collective-permute-start | bytes 491528 | tf_op jit(solution)/shard_map/ppermute | solution.py:407
  54.4 2.0 %collective-permute-start.20 = (bf16[160,512]{1,0:T(8,128)(2,1)S(1)}, bf16[160,512]{1,0:T(8,128)(2,1)S(1)}, u32[]{:S(2)}, u32[]{:S(2)}) collective-permute-start(bf16[160,512]{1,0:T(8,128)(2,1)S(1)} %collective-permute-done.17.refs_3_), channel_id=1, source_target_pairs={{0,1},{1,3},{3,5},{5,7},{7,6},{6,4},{4,2},{2,0},{8,9},{9,11},{11,1... | collective-permute-start | bytes 491528 | tf_op jit(solution)/shard_map/ppermute | solution.py:407
  56.5 3.1 %collective-permute-done.15.refs_6_ = bf16[160,512]{1,0:T(8,128)(2,1)} collective-permute-done((bf16[160,512]{1,0:T(8,128)(2,1)S(1)}, bf16[160,512]{1,0:T(8,128)(2,1)}, u32[]{:S(2)}, u32[]{:S(2)}) %collective-permute-start.15) | collective-permute-done | bytes 163872 | tf_op jit(solution)/shard_map/ppermute | solution.py:407
  59.6 2.0 %collective-permute-start.16 = (bf16[160,512]{1,0:T(8,128)(2,1)}, bf16[160,512]{1,0:T(8,128)(2,1)S(1)}, u32[]{:S(2)}, u32[]{:S(2)}) collective-permute-start(bf16[160,512]{1,0:T(8,128)(2,1)} %collective-permute-done.15.refs_6_), channel_id=1, source_target_pairs={{0,1},{1,3},{3,5},{5,7},{7,6},{6,4},{4,2},{2,0},{8,9},{9,11},{11,1... | collective-permute-start | bytes 491528 | tf_op jit(solution)/shard_map/ppermute | solution.py:407
  62.7 2.3 %collective-permute-start.29 = (bf16[160,512]{1,0:T(8,128)(2,1)S(1)}, bf16[160,512]{1,0:T(8,128)(2,1)}, u32[]{:S(2)}, u32[]{:S(2)}) collective-permute-start(bf16[160,512]{1,0:T(8,128)(2,1)S(1)} %collective-permute-done.20.refs_7_), channel_id=1, source_target_pairs={{0,1},{1,3},{3,5},{5,7},{7,6},{6,4},{4,2},{2,0},{8,9},{9,11},{11,1... | collective-permute-start | bytes 491528 | tf_op jit(solution)/shard_map/ppermute | solution.py:407
  65.0 2.5 %early_norm.1 = (bf16[800,1024]{1,0:T(8,128)(2,1)S(1)}, bf16[800,128]{1,0:T(8,128)(2,1)S(1)}) custom-call(bf16[160,512]{1,0:T(8,128)(2,1)S(1)} %get-tuple-element.24.refs_0_, bf16[160,512]{1,0:T(8,128)(2,1)S(1)} %second_conv.1.refs_1_.refs_2_, bf16[160,512]{1,0:T(8,128)(2,1)S(1)} %collective-permute-done.14.refs_2_, ...), custom_call_target="tpu_custom_call" | custom-call | flops 10485760 | bytes 5242880 | tf_op jit(solution)/shard_map/early_norm/pallas_call | solution.py:555
  67.5 2.1 %collective-permute-start.23 = (bf16[160,512]{1,0:T(8,128)(2,1)S(1)}, bf16[160,512]{1,0:T(8,128)(2,1)S(1)}, u32[]{:S(2)}, u32[]{:S(2)}) collective-permute-start(bf16[160,512]{1,0:T(8,128)(2,1)S(1)} %after.9.refs_2_), channel_id=1, source_target_pairs={{0,1},{1,3},{3,5},{5,7},{7,6},{6,4},{4,2},{2,0},{8,9},{9,11},{11,1... | collective-permute-start | bytes 491528 | tf_op jit(solution)/shard_map/ppermute | solution.py:407
  69.7 2.4 %collective-permute-done.30.refs_4_ = bf16[160,512]{1,0:T(8,128)(2,1)} collective-permute-done((bf16[160,512]{1,0:T(8,128)(2,1)S(1)}, bf16[160,512]{1,0:T(8,128)(2,1)}, u32[]{:S(2)}, u32[]{:S(2)}) %collective-permute-start.30) | collective-permute-done | bytes 163872 | tf_op jit(solution)/shard_map/ppermute | solution.py:407
  72.1 2.4 %collective-permute-start.37 = (bf16[160,1280]{1,0:T(8,128)(2,1)S(1)}, bf16[160,1280]{1,0:T(8,128)(2,1)S(1)}, u32[]{:S(2)}, u32[]{:S(2)}) collective-permute-start(bf16[160,1280]{1,0:T(8,128)(2,1)S(1)} %get-tuple-element.42.refs_7_), channel_id=1, source_target_pairs={{0,1},{1,0},{2,3},{3,2},{4,5},{5,4},{6,7},{7,6},{16,17},{17,16},{1... | collective-permute-start | bytes 1228808 | tf_op jit(solution)/shard_map/ppermute | solution.py:429
  74.5 2.0 %collective-permute-start.36 = (bf16[160,1280]{1,0:T(8,128)(2,1)S(1)}, bf16[160,1280]{1,0:T(8,128)(2,1)S(1)}, u32[]{:S(2)}, u32[]{:S(2)}) collective-permute-start(bf16[160,1280]{1,0:T(8,128)(2,1)S(1)} %broadcast_select_fusion), channel_id=1, source_target_pairs={{0,1},{1,0},{2,3},{3,2},{4,5},{5,4},{6,7},{7,6},{8,9},{9,8},{10,11... | collective-permute-start | bytes 1228808 | tf_op jit(solution)/shard_map/ppermute | solution.py:429
  76.6 4.7 %norm_project.1 = (f32[960,1024]{1,0:T(8,128)S(1)}, bf16[1280,128]{1,0:T(8,128)(2,1)S(1)}) custom-call(s32[128]{0:T(128)S(1)} %copy-done.6, bf16[800,1024]{1,0:T(8,128)(2,1)S(1)} %get-tuple-element.27.refs_1_.refs_0_, bf16[800,128]{1,0:T(8,128)(2,1)S(1)} %get-tuple-element.31.refs_1_, bf16[160,512]{1,0:T(8,128)(2,1)S(1)} %after.9.refs_2_, ...), custom_call_target="tpu_custom_call" | custom-call | flops 2516582400 | bytes 5079040 | tf_op jit(solution)/shard_map/norm_project/pallas_call | solution.py:583
  81.3 6.0 %attention.1 = (bf16[320,128]{1,0:T(8,128)(2,1)S(1)}, bf16[320,128]{1,0:T(8,128)(2,1)S(1)}, bf16[320,128]{1,0:T(8,128)(2,1)S(1)}, bf16[1280,128]{1,0:T(8,128)(2,...) custom-call(s32[128]{0:T(128)S(1)} %copy-done.6, ...), custom_call_target="tpu_custom_call" | custom-call | flops 1258291200 | bytes 5898240 | tf_op jit(solution)/shard_map/attention/pallas_call | solution.py:607
  88.7 3.3 %collective-permute-start.32 = (bf16[320,128]{1,0:T(8,128)(2,1)S(1)}, bf16[320,128]{1,0:T(8,128)(2,1)S(1)}, u32[]{:S(2)}, u32[]{:S(2)}) collective-permute-start(bf16[320,128]{1,0:T(8,128)(2,1)S(1)} %get-tuple-element.37), channel_id=1, source_target_pairs={{0,4},{1,5},{2,6},{3,7},{4,0},{5,1},{6,2},{7,3},{8,12},{9,13},{10,... | collective-permute-start | bytes 245768 | tf_op jit(solution)/shard_map/ppermute | solution.py:630
  93.2 1.9 %own_attention.1.refs_0_ = bf16[320,128]{1,0:T(8,128)(2,1)S(1)} custom-call(bf16[960,1024]{1,0:T(8,128)(2,1)S(1)} %get-tuple-element.34.made_ref, bf16[5,1024,64]{2,1,0:T(8,128)(2,1)S(1)} %get-tuple-element.35.key_ref), custom_call_target="tpu_custom_call" | custom-call | flops 167772160 | bytes 2621440 | tf_op jit(solution)/shard_map/own_attention/pallas_call | solution.py:631
  95.6 3.0 %collective-permute-done.32.refs_2_ = bf16[320,128]{1,0:T(8,128)(2,1)S(1)} collective-permute-done((bf16[320,128]{1,0:T(8,128)(2,1)S(1)}, bf16[320,128]{1,0:T(8,128)(2,1)S(1)}, u32[]{:S(2)}, u32[]{:S(2)}) %collective-permute-start.32) | collective-permute-done | bytes 81952 | tf_op jit(solution)/shard_map/ppermute | solution.py:630
  98.6 2.1 %project.1 = bf16[128,1280]{1,0:T(8,128)(2,1)} custom-call(bf16[320,128]{1,0:T(8,128)(2,1)S(1)} %own_attention.1.refs_0_, bf16[320,128]{1,0:T(8,128)(2,1)S(1)} %collective-permute-done.31.refs_1_, bf16[320,128]{1,0:T(8,128)(2,1)S(1)} %collective-permute-done.32.refs_2_, bf16[320,128]{1,0:T(8,128)(2,1)S(1)} %collective-permute-done.33.refs_3_, ...), custom_call_target="tpu_custom_call" | custom-call | flops 419430400 | bytes 4259840 | tf_op jit(solution)/shard_map/project/pallas_call | solution.py:648
  (81 shorter events, 17.5 us)
Async XLA Ops:
  1.0 8.1 %collective-permute-start = (bf16[64,1280]{1,0:T(8,128)(2,1)S(1)}, bf16[64,1280]{1,0:T(8,128)(2,1)S(1)}, u32[]{:S(2)}, u32[]{:S(2)}) collective-permute-start(bf16[64,1280]{1,0:T(8,128)(2,1)S(1)} %get-tuple-element.44.refs_0_), channel_id=1, source_target_pairs={{0,1},{1,3},{3,5},{5,7},{7,6},{6,4},{4,2},{2,0},{8,9},{9,11},{11,1... | collective-permute-start | bytes 491528 | tf_op jit(solution)/shard_map/ppermute | solution.py:407
  4.0 11.2 %collective-permute-start.2 = (bf16[64,1280]{1,0:T(8,128)(2,1)S(1)}, bf16[64,1280]{1,0:T(8,128)(2,1)S(1)}, u32[]{:S(2)}, u32[]{:S(2)}) collective-permute-start(bf16[64,1280]{1,0:T(8,128)(2,1)S(1)} %get-tuple-element.44.refs_0_), channel_id=1, source_target_pairs={{1,0},{3,1},{5,3},{7,5},{6,7},{4,6},{2,4},{0,2},{9,8},{11,9},{13,1... | collective-permute-start | bytes 491528 | tf_op jit(solution)/shard_map/ppermute | solution.py:407
  4.2 9.5 %collective-permute-start.1 = (bf16[64,1280]{1,0:T(8,128)(2,1)S(1)}, bf16[64,1280]{1,0:T(8,128)(2,1)S(1)}, u32[]{:S(2)}, u32[]{:S(2)}) collective-permute-start(bf16[64,1280]{1,0:T(8,128)(2,1)S(1)} %get-tuple-element.43.refs_1_), channel_id=1, source_target_pairs={{0,1},{1,3},{3,5},{5,7},{7,6},{6,4},{4,2},{2,0},{8,9},{9,11},{11,1... | collective-permute-start | bytes 491528 | tf_op jit(solution)/shard_map/ppermute | solution.py:407
  6.1 7.1 %collective-permute-start.3 = (bf16[64,1280]{1,0:T(8,128)(2,1)S(1)}, bf16[64,1280]{1,0:T(8,128)(2,1)S(1)}, u32[]{:S(2)}, u32[]{:S(2)}) collective-permute-start(bf16[64,1280]{1,0:T(8,128)(2,1)S(1)} %get-tuple-element.43.refs_1_), channel_id=1, source_target_pairs={{1,0},{3,1},{5,3},{7,5},{6,7},{4,6},{2,4},{0,2},{9,8},{11,9},{13,1... | collective-permute-start | bytes 491528 | tf_op jit(solution)/shard_map/ppermute | solution.py:407
  13.2 7.1 %collective-permute-start.7 = (bf16[64,1280]{1,0:T(8,128)(2,1)S(1)}, bf16[64,1280]{1,0:T(8,128)(2,1)S(1)}, u32[]{:S(2)}, u32[]{:S(2)}) collective-permute-start(bf16[64,1280]{1,0:T(8,128)(2,1)S(1)} %collective-permute-done.3.refs_5_), channel_id=1, source_target_pairs={{1,0},{3,1},{5,3},{7,5},{6,7},{4,6},{2,4},{0,2},{9,8},{11,9},{13,1... | collective-permute-start | bytes 491528 | tf_op jit(solution)/shard_map/ppermute | solution.py:407
  13.6 7.1 %collective-permute-start.5 = (bf16[64,1280]{1,0:T(8,128)(2,1)S(1)}, bf16[64,1280]{1,0:T(8,128)(2,1)S(1)}, u32[]{:S(2)}, u32[]{:S(2)}) collective-permute-start(bf16[64,1280]{1,0:T(8,128)(2,1)S(1)} %collective-permute-done.1.refs_3_), channel_id=1, source_target_pairs={{0,1},{1,3},{3,5},{5,7},{7,6},{6,4},{4,2},{2,0},{8,9},{9,11},{11,1... | collective-permute-start | bytes 491528 | tf_op jit(solution)/shard_map/ppermute | solution.py:407
  15.2 8.6 %collective-permute-start.6 = (bf16[64,1280]{1,0:T(8,128)(2,1)S(1)}, bf16[64,1280]{1,0:T(8,128)(2,1)S(1)}, u32[]{:S(2)}, u32[]{:S(2)}) collective-permute-start(bf16[64,1280]{1,0:T(8,128)(2,1)S(1)} %collective-permute-done.2.refs_4_), channel_id=1, source_target_pairs={{1,0},{3,1},{5,3},{7,5},{6,7},{4,6},{2,4},{0,2},{9,8},{11,9},{13,1... | collective-permute-start | bytes 491528 | tf_op jit(solution)/shard_map/ppermute | solution.py:407
  15.7 9.4 %collective-permute-start.8 = (bf16[64,1280]{1,0:T(8,128)(2,1)S(1)}, bf16[64,1280]{1,0:T(8,128)(2,1)S(1)}, u32[]{:S(2)}, u32[]{:S(2)}) collective-permute-start(bf16[64,1280]{1,0:T(8,128)(2,1)S(1)} %collective-permute-done.4.refs_6_), channel_id=1, source_target_pairs={{0,1},{1,3},{3,5},{5,7},{7,6},{6,4},{4,2},{2,0},{8,9},{9,11},{11,1... | collective-permute-start | bytes 491528 | tf_op jit(solution)/shard_map/ppermute | solution.py:407
  20.3 7.1 %collective-permute-start.11 = (bf16[64,1280]{1,0:T(8,128)(2,1)S(1)}, bf16[64,1280]{1,0:T(8,128)(2,1)S(1)}, u32[]{:S(2)}, u32[]{:S(2)}) collective-permute-start(bf16[64,1280]{1,0:T(8,128)(2,1)S(1)} %collective-permute-done.7.refs_9_), channel_id=1, source_target_pairs={{1,0},{3,1},{5,3},{7,5},{6,7},{4,6},{2,4},{0,2},{9,8},{11,9},{13,1... | collective-permute-start | bytes 491528 | tf_op jit(solution)/shard_map/ppermute | solution.py:407
  20.8 7.2 %collective-permute-start.9 = (bf16[64,1280]{1,0:T(8,128)(2,1)S(1)}, bf16[64,1280]{1,0:T(8,128)(2,1)S(1)}, u32[]{:S(2)}, u32[]{:S(2)}) collective-permute-start(bf16[64,1280]{1,0:T(8,128)(2,1)S(1)} %collective-permute-done.5.refs_7_), channel_id=1, source_target_pairs={{0,1},{1,3},{3,5},{5,7},{7,6},{6,4},{4,2},{2,0},{8,9},{9,11},{11,1... | collective-permute-start | bytes 491528 | tf_op jit(solution)/shard_map/ppermute | solution.py:407
  33.4 15.4 %collective-permute-start.26 = (bf16[240,1280]{1,0:T(8,128)(2,1)S(1)}, bf16[240,1280]{1,0:T(8,128)(2,1)S(1)}, u32[]{:S(2)}, u32[]{:S(2)}) collective-permute-start(bf16[240,1280]{1,0:T(8,128)(2,1)S(1)} %get-tuple-element.28), channel_id=1, source_target_pairs={{0,1},{1,0},{2,3},{3,2},{4,5},{5,4},{6,7},{7,6},{8,9},{9,8},{10,11... | collective-permute-start | bytes 1843208 | tf_op jit(solution)/shard_map/ppermute | solution.py:429
  34.8 12.4 %collective-permute-start.27 = (bf16[160,1280]{1,0:T(8,128)(2,1)S(1)}, bf16[160,1280]{1,0:T(8,128)(2,1)S(1)}, u32[]{:S(2)}, u32[]{:S(2)}) collective-permute-start(bf16[160,1280]{1,0:T(8,128)(2,1)S(1)} %get-tuple-element.29), channel_id=1, source_target_pairs={{0,2},{1,3},{2,4},{3,5},{4,6},{5,7},{6,0},{7,1},{8,14},{9,15},{10,... | collective-permute-start | bytes 1228808 | tf_op jit(solution)/shard_map/ppermute | solution.py:429
  42.3 10.1 %collective-permute-start.14 = (bf16[160,512]{1,0:T(8,128)(2,1)S(1)}, bf16[160,512]{1,0:T(8,128)(2,1)S(1)}, u32[]{:S(2)}, u32[]{:S(2)}) collective-permute-start(bf16[160,512]{1,0:T(8,128)(2,1)S(1)} %get-tuple-element.24.refs_0_), channel_id=1, source_target_pairs={{0,1},{1,3},{3,5},{5,7},{7,6},{6,4},{4,2},{2,0},{8,9},{9,11},{11,1... | collective-permute-start | bytes 491528 | tf_op jit(solution)/shard_map/ppermute | solution.py:407
  44.6 9.7 %collective-permute-start.19 = (bf16[160,512]{1,0:T(8,128)(2,1)S(1)}, bf16[160,512]{1,0:T(8,128)(2,1)S(1)}, u32[]{:S(2)}, u32[]{:S(2)}) collective-permute-start(bf16[160,512]{1,0:T(8,128)(2,1)S(1)} %second_conv.1.refs_1_.refs_2_), channel_id=1, source_target_pairs={{1,0},{3,1},{5,3},{7,5},{6,7},{4,6},{2,4},{0,2},{9,8},{11,9},{13,1... | collective-permute-start | bytes 491528 | tf_op jit(solution)/shard_map/ppermute | solution.py:407
  46.7 7.7 %collective-permute-start.17 = (bf16[160,512]{1,0:T(8,128)(2,1)S(1)}, bf16[160,512]{1,0:T(8,128)(2,1)S(1)}, u32[]{:S(2)}, u32[]{:S(2)}) collective-permute-start(bf16[160,512]{1,0:T(8,128)(2,1)S(1)} %second_conv.1.refs_1_.refs_2_), channel_id=1, source_target_pairs={{0,1},{1,3},{3,5},{5,7},{7,6},{6,4},{4,2},{2,0},{8,9},{9,11},{11,1... | collective-permute-start | bytes 491528 | tf_op jit(solution)/shard_map/ppermute | solution.py:407
  47.2 9.2 %collective-permute-start.18 = (bf16[160,512]{1,0:T(8,128)(2,1)S(1)}, bf16[160,512]{1,0:T(8,128)(2,1)S(1)}, u32[]{:S(2)}, u32[]{:S(2)}) collective-permute-start(bf16[160,512]{1,0:T(8,128)(2,1)S(1)} %get-tuple-element.24.refs_0_), channel_id=1, source_target_pairs={{1,0},{3,1},{5,3},{7,5},{6,7},{4,6},{2,4},{0,2},{9,8},{11,9},{13,1... | collective-permute-start | bytes 491528 | tf_op jit(solution)/shard_map/ppermute | solution.py:407
  48.7 23.3 %collective-permute-start.34 = (bf16[160,1280]{1,0:T(8,128)(2,1)S(1)}, bf16[160,1280]{1,0:T(8,128)(2,1)S(1)}, u32[]{:S(2)}, u32[]{:S(2)}) collective-permute-start(bf16[160,1280]{1,0:T(8,128)(2,1)S(1)} %get-tuple-element.40.refs_0_), channel_id=1, source_target_pairs={{0,16},{8,24},{16,0},{24,8},{1,17},{9,25},{17,1},{25,9},{2,18},{10... | collective-permute-start | bytes 1228808 | tf_op jit(solution)/shard_map/ppermute | solution.py:434
  52.4 7.2 %collective-permute-start.15 = (bf16[160,512]{1,0:T(8,128)(2,1)S(1)}, bf16[160,512]{1,0:T(8,128)(2,1)}, u32[]{:S(2)}, u32[]{:S(2)}) collective-permute-start(bf16[160,512]{1,0:T(8,128)(2,1)S(1)} %collective-permute-done.14.refs_2_), channel_id=1, source_target_pairs={{0,1},{1,3},{3,5},{5,7},{7,6},{6,4},{4,2},{2,0},{8,9},{9,11},{11,1... | collective-permute-start | bytes 491528 | tf_op jit(solution)/shard_map/ppermute | solution.py:407
  54.4 7.2 %collective-permute-start.22 = (bf16[160,512]{1,0:T(8,128)(2,1)S(1)}, bf16[160,512]{1,0:T(8,128)(2,1)S(1)}, u32[]{:S(2)}, u32[]{:S(2)}) collective-permute-start(bf16[160,512]{1,0:T(8,128)(2,1)S(1)} %collective-permute-done.19.refs_5_), channel_id=1, source_target_pairs={{1,0},{3,1},{5,3},{7,5},{6,7},{4,6},{2,4},{0,2},{9,8},{11,9},{13,1... | collective-permute-start | bytes 491528 | tf_op jit(solution)/shard_map/ppermute | solution.py:407
  54.4 8.3 %collective-permute-start.20 = (bf16[160,512]{1,0:T(8,128)(2,1)S(1)}, bf16[160,512]{1,0:T(8,128)(2,1)S(1)}, u32[]{:S(2)}, u32[]{:S(2)}) collective-permute-start(bf16[160,512]{1,0:T(8,128)(2,1)S(1)} %collective-permute-done.17.refs_3_), channel_id=1, source_target_pairs={{0,1},{1,3},{3,5},{5,7},{7,6},{6,4},{4,2},{2,0},{8,9},{9,11},{11,1... | collective-permute-start | bytes 491528 | tf_op jit(solution)/shard_map/ppermute | solution.py:407
  56.4 8.6 %collective-permute-start.21 = (bf16[160,512]{1,0:T(8,128)(2,1)S(1)}, bf16[160,512]{1,0:T(8,128)(2,1)S(1)}, u32[]{:S(2)}, u32[]{:S(2)}) collective-permute-start(bf16[160,512]{1,0:T(8,128)(2,1)S(1)} %collective-permute-done.18.refs_4_), channel_id=1, source_target_pairs={{1,0},{3,1},{5,3},{7,5},{6,7},{4,6},{2,4},{0,2},{9,8},{11,9},{13,1... | collective-permute-start | bytes 491528 | tf_op jit(solution)/shard_map/ppermute | solution.py:407
  59.6 7.9 %collective-permute-start.16 = (bf16[160,512]{1,0:T(8,128)(2,1)}, bf16[160,512]{1,0:T(8,128)(2,1)S(1)}, u32[]{:S(2)}, u32[]{:S(2)}) collective-permute-start(bf16[160,512]{1,0:T(8,128)(2,1)} %collective-permute-done.15.refs_6_), channel_id=1, source_target_pairs={{0,1},{1,3},{3,5},{5,7},{7,6},{6,4},{4,2},{2,0},{8,9},{9,11},{11,1... | collective-permute-start | bytes 491528 | tf_op jit(solution)/shard_map/ppermute | solution.py:407
  61.6 8.0 %collective-permute-start.24 = (bf16[160,512]{1,0:T(8,128)(2,1)S(1)}, bf16[160,512]{1,0:T(8,128)(2,1)}, u32[]{:S(2)}, u32[]{:S(2)}) collective-permute-start(bf16[160,512]{1,0:T(8,128)(2,1)S(1)} %collective-permute-done.22.refs_9_), channel_id=1, source_target_pairs={{1,0},{3,1},{5,3},{7,5},{6,7},{4,6},{2,4},{0,2},{9,8},{11,9},{13,1... | collective-permute-start | bytes 491528 | tf_op jit(solution)/shard_map/ppermute | solution.py:407
  65.0 7.0 %collective-permute-start.30 = (bf16[160,512]{1,0:T(8,128)(2,1)S(1)}, bf16[160,512]{1,0:T(8,128)(2,1)}, u32[]{:S(2)}, u32[]{:S(2)}) collective-permute-start(bf16[160,512]{1,0:T(8,128)(2,1)S(1)} %collective-permute-done.21.refs_8_), channel_id=1, source_target_pairs={{1,0},{3,1},{5,3},{7,5},{6,7},{4,6},{2,4},{0,2},{9,8},{11,9},{13,1... | collective-permute-start | bytes 491528 | tf_op jit(solution)/shard_map/ppermute | solution.py:407
  67.5 13.8 %collective-permute-start.23 = (bf16[160,512]{1,0:T(8,128)(2,1)S(1)}, bf16[160,512]{1,0:T(8,128)(2,1)S(1)}, u32[]{:S(2)}, u32[]{:S(2)}) collective-permute-start(bf16[160,512]{1,0:T(8,128)(2,1)S(1)} %after.9.refs_2_), channel_id=1, source_target_pairs={{0,1},{1,3},{3,5},{5,7},{7,6},{6,4},{4,2},{2,0},{8,9},{9,11},{11,1... | collective-permute-start | bytes 491528 | tf_op jit(solution)/shard_map/ppermute | solution.py:407
  69.6 11.7 %collective-permute-start.25 = (bf16[160,512]{1,0:T(8,128)(2,1)}, bf16[160,512]{1,0:T(8,128)(2,1)S(1)}, u32[]{:S(2)}, u32[]{:S(2)}) collective-permute-start(bf16[160,512]{1,0:T(8,128)(2,1)} %collective-permute-done.24.refs_5_), channel_id=1, source_target_pairs={{1,0},{3,1},{5,3},{7,5},{6,7},{4,6},{2,4},{0,2},{9,8},{11,9},{13,1... | collective-permute-start | bytes 491528 | tf_op jit(solution)/shard_map/ppermute | solution.py:407
  72.1 15.2 %collective-permute-start.37 = (bf16[160,1280]{1,0:T(8,128)(2,1)S(1)}, bf16[160,1280]{1,0:T(8,128)(2,1)S(1)}, u32[]{:S(2)}, u32[]{:S(2)}) collective-permute-start(bf16[160,1280]{1,0:T(8,128)(2,1)S(1)} %get-tuple-element.42.refs_7_), channel_id=1, source_target_pairs={{0,1},{1,0},{2,3},{3,2},{4,5},{5,4},{6,7},{7,6},{16,17},{17,16},{1... | collective-permute-start | bytes 1228808 | tf_op jit(solution)/shard_map/ppermute | solution.py:429
  74.5 13.8 %collective-permute-start.36 = (bf16[160,1280]{1,0:T(8,128)(2,1)S(1)}, bf16[160,1280]{1,0:T(8,128)(2,1)S(1)}, u32[]{:S(2)}, u32[]{:S(2)}) collective-permute-start(bf16[160,1280]{1,0:T(8,128)(2,1)S(1)} %broadcast_select_fusion), channel_id=1, source_target_pairs={{0,1},{1,0},{2,3},{3,2},{4,5},{5,4},{6,7},{7,6},{8,9},{9,8},{10,11... | collective-permute-start | bytes 1228808 | tf_op jit(solution)/shard_map/ppermute | solution.py:429
  76.5 22.1 %collective-permute-start.35 = (bf16[320,1280]{1,0:T(8,128)(2,1)S(1)}, bf16[320,1280]{1,0:T(8,128)(2,1)S(1)}, u32[]{:S(2)}, u32[]{:S(2)}) collective-permute-start(bf16[320,1280]{1,0:T(8,128)(2,1)S(1)} %pad_maximum_fusion), channel_id=1, source_target_pairs={{0,8},{8,0},{16,24},{24,16},{1,9},{9,1},{17,25},{25,17},{2,10},{10... | collective-permute-start | bytes 2457608 | tf_op jit(solution)/shard_map/ppermute | solution.py:434
  88.3 10.3 %collective-permute-start.38 = (bf16[320,1280]{1,0:T(8,128)(2,1)S(1)}, bf16[320,1280]{1,0:T(8,128)(2,1)S(1)}, u32[]{:S(2)}, u32[]{:S(2)}) collective-permute-start(bf16[320,1280]{1,0:T(8,128)(2,1)S(1)} %after.13.refs_9_), channel_id=1, source_target_pairs={{0,8},{8,0},{16,24},{24,16},{1,9},{9,1},{17,25},{25,17},{2,10},{10... | collective-permute-start | bytes 2457608 | tf_op jit(solution)/shard_map/ppermute | solution.py:434
  88.4 7.2 %collective-permute-start.31 = (bf16[320,128]{1,0:T(8,128)(2,1)S(1)}, bf16[320,128]{1,0:T(8,128)(2,1)S(1)}, u32[]{:S(2)}, u32[]{:S(2)}) collective-permute-start(bf16[320,128]{1,0:T(8,128)(2,1)S(1)} %get-tuple-element.36.refs_1_), channel_id=1, source_target_pairs={{0,2},{1,3},{2,4},{3,5},{4,6},{5,7},{6,0},{7,1},{8,10},{9,11},{10,... | collective-permute-start | bytes 245768 | tf_op jit(solution)/shard_map/ppermute | solution.py:630
  88.7 9.9 %collective-permute-start.32 = (bf16[320,128]{1,0:T(8,128)(2,1)S(1)}, bf16[320,128]{1,0:T(8,128)(2,1)S(1)}, u32[]{:S(2)}, u32[]{:S(2)}) collective-permute-start(bf16[320,128]{1,0:T(8,128)(2,1)S(1)} %get-tuple-element.37), channel_id=1, source_target_pairs={{0,4},{1,5},{2,6},{3,7},{4,0},{5,1},{6,2},{7,3},{8,12},{9,13},{10,... | collective-permute-start | bytes 245768 | tf_op jit(solution)/shard_map/ppermute | solution.py:630
  (14 other events, 113.7 us)
